TPU v7x, 32 devices: a whole 2x2x4 slice. The times are simulated.
32 devices in a mesh: group: 2 (over y), expert: 4 (over z), etp: 4 (over x, core).
Axes of the slice: x: 2, y: 2, z: 4, core: 2. Of those that a mesh axis runs over, the one named last changes fastest.
Arguments:
- tokens: bfloat16 [128, 4096], P(('group', 'expert')), parts along dimension 0, may hold values from -6 to 6
- expert_ids: int32 [128, 2], P(('group', 'expert')), parts along dimension 0, may hold values from 0 to 3, all different within a row; in each aligned block of 4 rows (0 to 3, 4 to 7, ...) at most 4 rows name the same one
- route_weights: float32 [128, 2], P(('group', 'expert', 'etp')), parts along dimension 0, may hold values from 0.05 to 1
- w_gate: bfloat16 [4, 1536, 4096], P('expert', 'etp'), may hold values from -0.09375 to 0.09375
- w_up: bfloat16 [4, 1536, 4096], P('expert', 'etp'), may hold values from -0.09375 to 0.09375
- w_down: bfloat16 [4, 1536, 4096], P('expert', 'etp'), may hold values from -0.15625 to 0.15625
Outputs:
- mixed: bfloat16 [128, 4096], P(('group', 'expert', 'etp')), parts along dimension 0
There are 2 independent parts, one for each index of `group`. A program takes and returns all parts, laid end to end along the dimension named above; an argument that names none is the same for every part. Nothing has to cross between parts.
Inputs may be any that keep to these rules, and one draw needn't show every extreme that they name: `expert_ids`: each row names 2 different experts; in each aligned block of 4 rows no expert is named by more than 4 rows, a bound that some block reaches.
All inputs are finite; a program needn't handle non-finite values.
Results may differ from a plain program's by a relative error of at most 0.015.
Values may be sent and summed in bfloat16 or wider, within the bound.
No kernel may reach another device: no remote copies, remote signals or barrier semaphores. Data moves between devices by JAX's collectives and lax.ppermute only.
A program may use at most 64 MiB of HBM per device.

v0:
```python
import jax
import jax.numpy as jnp
from jax import lax
from jax.sharding import PartitionSpec as P


def slot_layout(expert_ids, experts, rows_dev, n_blocks):
    flat = expert_ids.reshape(-1)
    count = flat.shape[0]
    top = expert_ids.shape[1]
    row = jnp.arange(count, dtype=jnp.int32) // top
    block = row // rows_dev
    by_block = expert_ids.reshape(n_blocks, rows_dev * top)
    onehot = (by_block[:, :, None] == jnp.arange(experts, dtype=jnp.int32)[None, None, :]).astype(
        jnp.int32
    )
    ranks = jnp.cumsum(onehot, axis=1) - onehot
    slot = jnp.sum(ranks * onehot, axis=2).reshape(-1)
    return (flat, block, slot)


def on_device(tokens, expert_ids, route_weights, w_gate, w_up, w_down):
    n_expert = lax.axis_size("expert")
    n_etp = lax.axis_size("etp")
    exp_dev = w_gate.shape[0]
    width = tokens.shape[1]
    experts = n_expert * exp_dev
    tok_dev, top = expert_ids.shape
    rows_dev = tok_dev // n_etp
    capsub = max(2, 2 * rows_dev * top // experts)
    flat, block, slot = slot_layout(expert_ids, experts, rows_dev, n_etp)
    dest = (flat * n_etp + block) * capsub + slot
    repeated = jnp.repeat(tokens, top, axis=0)
    send = jnp.zeros((experts * n_etp * capsub, width), jnp.bfloat16).at[dest].set(repeated)
    send = send.reshape(n_expert, exp_dev, n_etp, capsub, width)
    received = lax.all_to_all(send, "expert", split_axis=0, concat_axis=0, tiled=True)
    gate = jnp.einsum("sepcd,efd->sepcf", received, w_gate, preferred_element_type=jnp.float32)
    upper = jnp.einsum("sepcd,efd->sepcf", received, w_up, preferred_element_type=jnp.float32)
    hidden = (jax.nn.silu(gate) * upper).astype(jnp.bfloat16)
    partial_out = jnp.einsum("sepcf,efd->sepcd", hidden, w_down, preferred_element_type=jnp.float32)
    summed = lax.psum_scatter(
        partial_out.astype(jnp.bfloat16), "etp", scatter_dimension=2, tiled=True
    )
    back = lax.all_to_all(summed, "expert", split_axis=0, concat_axis=0, tiled=True)
    results = back.reshape(experts * capsub, width)
    own_count = rows_dev * top
    own_start = lax.axis_index("etp") * own_count
    own_expert = lax.dynamic_slice_in_dim(flat, own_start, own_count, 0)
    own_slot = lax.dynamic_slice_in_dim(slot, own_start, own_count, 0)
    index = own_expert * capsub + own_slot
    picked = results[index].astype(jnp.float32).reshape(rows_dev, top, width)
    combine = route_weights / jnp.sum(route_weights, axis=1, keepdims=True)
    return jnp.sum(picked * combine[:, :, None], axis=1).astype(jnp.bfloat16)


def solution(mesh):
    in_specs = (
        P(("group", "expert"), None),
        P(("group", "expert"), None),
        P(("group", "expert", "etp"), None),
        P("expert", "etp", None),
        P("expert", "etp", None),
        P("expert", "etp", None),
    )
    out_specs = P(("group", "expert", "etp"), None)
    return jax.shard_map(
        on_device, mesh=mesh, in_specs=in_specs, out_specs=out_specs, check_vma=False
    )
```

profile of v0, /device:TPU:0, one launch (start us, length us, event | category | flops | bytes accessed | tf_op | source)
XLA Modules:
  0.0 96.1 jit_solution(16440530250967646768)
XLA Ops:
  6.5 0.8 broadcast_multiply_fusion
  7.4 0.9 copy.21
  8.3 0.1 copy.20
  8.3 0.1 mul.48
  8.5 0.7 reduce_window_sum.11
  9.3 0.1 reshape.160
  9.3 1.1 %broadcast_in_dim.14 = bf16[16,2,4096]{2,1,0:T(2,128)(2,1)S(1)} broadcast(bf16[16,4096]{1,0:T(8,128)(2,1)} %param.6), dimensions={0,2} | broadcast | bytes 393216 | tf_op jit(solution)/shard_map/broadcast_in_dim | solution.py:33
  10.4 0.8 reshape.184
  11.3 2.2 %scatter_custom_fusion = bf16[64,4096]{1,0:T(8,128)(2,1)} fusion(s32[32]{0:T(128)S(1)} %fusion.26, bf16[32,4096]{1,0:T(8,128)(2,1)} %reshape.184, bf16[]{:T(256)} %constant.42.clone.1), kind=kCustom, calls=%fused_computation.16 | custom fusion | bytes 524800 | tf_op jit(solution)/shard_map/scatter | solution.py:34
  13.5 2.0 %reshape.162 = bf16[4,1,4,4,4096]{4,3,2,1,0:T(4,128)(2,1)} reshape(bf16[64,4096]{1,0:T(8,128)(2,1)} %scatter_custom_fusion) | data formatting | bytes 1048576 | tf_op jit(solution)/shard_map/reshape | solution.py:35
  15.5 20.8 %all_to_all.10 = bf16[4,1,4,4,4096]{4,3,2,1,0:T(4,128)(2,1)S(1)} all-to-all(bf16[4,1,4,4,4096]{4,3,2,1,0:T(4,128)(2,1)} %reshape.162), channel_id=1, replica_groups=mesh['group'=2,'expert'=4,'etp'=4] {'expert'}, dimensions={0} | all-to-all | bytes 1048576 | tf_op jit(solution)/shard_map/all_to_all | solution.py:36
  36.3 3.2 %fusion.6 = f32[4,1,4,4,384]{4,3,2,0,1:T(4,128)S(1)} fusion(bf16[1,384,4096]{2,1,0:T(8,128)(2,1)} %param.9, bf16[4,1,4,4,4096]{4,3,2,1,0:T(4,128)(2,1)S(1)} %all_to_all.10), kind=kOutput, calls=%fused_computation.9 | convolution fusion | flops 201326592 | bytes 3768320 | tf_op jit(solution)/shard_map/sepcd,efd->sepcf/dot_general | solution.py:37
  39.6 1.2 %fusion.18 = bf16[4,4,4,384]{3,2,1,0:T(4,128)(2,1)S(1)} fusion(bf16[1,384,4096]{2,1,0:T(8,128)(2,1)S(1)} %copy-done.2, bf16[4,1,4,4,4096]{4,3,2,1,0:T(4,128)(2,1)S(1)} %all_to_all.10, f32[4,1,4,4,384]{4,3,2,0,1:T(4,128)S(1)} %fusion.6), kind=kOutput, calls=%fused_computation.13 | convolution fusion | flops 201474048 | bytes 3817472 | tf_op jit(solution)/shard_map/sepcd,efd->sepcf/dot_general | solution.py:38
  40.9 1.5 %fusion = bf16[4,1,4,4,4096]{4,3,2,0,1:T(4,128)(2,1)} fusion(bf16[4,4,4,384]{3,2,1,0:T(4,128)(2,1)S(1)} %fusion.18, bf16[1,384,4096]{2,1,0:T(8,128)(2,1)S(1)} %copy-done), kind=kOutput, calls=%fused_computation.3 | convolution fusion | flops 201588736 | bytes 3719168 | tf_op jit(solution)/shard_map/sepcf,efd->sepcd/dot_general | solution.py:40
  42.4 0.1 reshape.169
  42.6 0.1 copy.24
  42.7 0.6 dynamic-slice
  43.3 31.6 %all-reduce.3.cloned.1.call-done = bf16[4,1,4,4,4096]{4,3,2,0,1:T(4,128)(2,1)} async-done(((bf16[4,1,4,4,4096]{4,3,2,0,1:T(4,128)(2,1)}), bf16[4,1,4,4,4096]{4,3,2,0,1:T(4,128)(2,1)}) %all-reduce.3.cloned.1.call-update) | async-done | bytes 524304
  74.9 2.2 %dynamic-slice_bitcast_fusion = bf16[4,1,1,4,4096]{4,3,2,1,0:T(4,128)(2,1)} fusion(bf16[4,1,4,4,4096]{4,3,2,0,1:T(4,128)(2,1)} %all-reduce.3.cloned.1.call-done, u32[]{:T(128)} %bitcast.38), kind=kLoop, calls=%fused_computation.18 | loop fusion | bytes 262148 | tf_op jit(solution)/shard_map/reduce_scatter | solution.py:41
  77.1 4.6 %all-to-all-start.1 = ((bf16[4,1,1,4,4096]{4,3,2,1,0:T(4,128)(2,1)}), bf16[4,1,1,4,4096]{4,3,2,1,0:T(4,128)(2,1)S(1)}, u32[]{:S(2)}, u32[]{:S(2)}) async-start(bf16[4,1,1,4,4096]{4,3,2,1,0:T(4,128)(2,1)} %dynamic-slice_bitcast_fusion), calls=%async_computation.1 | async-start | bytes 262144 | tf_op jit(solution)/shard_map/all_to_all | solution.py:44
  81.8 5.8 %all-to-all-done.1 = bf16[4,1,1,4,4096]{4,3,2,1,0:T(4,128)(2,1)S(1)} async-done(((bf16[4,1,1,4,4096]{4,3,2,1,0:T(4,128)(2,1)}), bf16[4,1,1,4,4096]{4,3,2,1,0:T(4,128)(2,1)S(1)}, u32[]{:S(2)}, u32[]{:S(2)}) %all-to-all-start.1) | async-done | bytes 131104 | tf_op jit(solution)/shard_map/all_to_all | solution.py:44
  87.7 0.6 gather_fusion
  88.3 0.1 reshape.171
  88.4 0.9 multiply_reduce_fusion
  (20 shorter events, 0.4 us)
Async XLA Ops:
  6.5 34.3 %copy-start = (bf16[1,384,4096]{2,1,0:T(8,128)(2,1)S(1)}, bf16[1,384,4096]{2,1,0:T(8,128)(2,1)}, u32[]{:S(2)}) copy-start(bf16[1,384,4096]{2,1,0:T(8,128)(2,1)} %param.11) | copy-start | bytes 9437188
  6.5 68.3 %all-reduce.3.cloned.1.call-start = ((), (), s32[]{:S(2)}) async-start(), calls=%async_computation.2 | async-start | bytes 1048576
  36.3 3.3 %copy-start.2 = (bf16[1,384,4096]{2,1,0:T(8,128)(2,1)S(1)}, bf16[1,384,4096]{2,1,0:T(8,128)(2,1)}, u32[]{:S(2)}) copy-start(bf16[1,384,4096]{2,1,0:T(8,128)(2,1)} %param.10) | copy-start | bytes 9437188
  40.8 1.7 %copy-start.1 = (f32[4,2]{0,1:T(2,128)S(1)}, f32[4,2]{0,1:T(2,128)}, u32[]{:S(2)}) copy-start(f32[4,2]{0,1:T(2,128)} %param.8) | copy-start | bytes 100
  40.9 1.8 %copy-start.3 = (u32[32]{0:T(128)S(1)}, u32[32]{0:T(128)}, u32[]{:S(2)}) copy-start(u32[32]{0:T(128)} %constant.62) | copy-start | bytes 388
  77.1 10.5 %all-to-all-start.1 = ((bf16[4,1,1,4,4096]{4,3,2,1,0:T(4,128)(2,1)}), bf16[4,1,1,4,4096]{4,3,2,1,0:T(4,128)(2,1)S(1)}, u32[]{:S(2)}, u32[]{:S(2)}) async-start(bf16[4,1,1,4,4096]{4,3,2,1,0:T(4,128)(2,1)} %dynamic-slice_bitcast_fusion), calls=%async_computation.1 | async-start | bytes 262144 | tf_op jit(solution)/shard_map/all_to_all | solution.py:44
Sparse Core Ops, SparseCore 0:
  42.5 32.3 all-reduce.2
where the time goes:
time: 96.4 us; the launch traced here: 96.1 us
  waiting for transfers between devices  37.4 us (39%)
  blocking collectives  20.8 us (22%)
  between operations  13.5 us (14%)
  local copies, waits for them, and re-layouts  11.2 us (12%)
  matrix products  5.98 us (6%)
  starting transfers between devices  4.6 us (5%)
  other arithmetic  2.56 us (3%)
    unnamed x2, waiting for transfers between devices  31.6 us
    all_to_all x1, blocking collectives, on_device(): lax.all_to_all(send, 'expert', split_axis=0, concat_axis=0, tiled=True)  20.8 us
    all_to_all x1, waiting for transfers between devices, on_device(): lax.all_to_all(summed, 'expert', split_axis=0, concat_axis=0, tiled=True)  5.83 us
    all_to_all x1, starting transfers between devices, on_device(): lax.all_to_all(summed, 'expert', split_axis=0, concat_axis=0, tiled=True)  4.6 us
    dot_general x1, matrix products, on_device(): jnp.einsum('sepcd,efd->sepcf', received, w_gate, preferred_element_type=j...  3.25 us
    reduce_scatter x1, local copies, waits for them, and re-layouts, on_device(): lax.psum_scatter(partial_out.astype(jnp.bfloat16), 'etp', scatter_dimensi...  2.25 us
    scatter x1, local copies, waits for them, and re-layouts, on_device(): jnp.zeros((experts * n_etp * capsub, width), jnp.bfloat16).at[dest]  2.19 us
    reshape x1, local copies, waits for them, and re-layouts, on_device(): send = send.reshape(n_expert, exp_dev, n_etp, capsub, width)  2.05 us
  transfers between devices with their start and end apart: 2, of which 2 were waited for; matrix products, arithmetic and copies ran while one was open for 1% of the time, Pallas kernels for 0%

commit v1 on v0

v1 whole, which is shorter than its diff:
```python
import functools

import jax
import jax.numpy as jnp
from jax import lax
from jax.experimental import pallas as pl
from jax.experimental.pallas import tpu as pltpu
from jax.sharding import PartitionSpec as P

VMEM = pl.BlockSpec(memory_space=pltpu.VMEM)
HBM = pl.BlockSpec(memory_space=pl.ANY)


def order_matrix(n_expert, pairs, rows, me):
    total = n_expert * pairs * 2 * rows
    core, pair = lax.rem(me, 2), lax.div(me, 2)
    place = lax.broadcasted_iota(jnp.int32, (total, total), 0)
    source = lax.broadcasted_iota(jnp.int32, (total, total), 1)
    row = lax.rem(place, rows)
    h = lax.rem(lax.div(place, rows), pairs)
    k = lax.rem(lax.div(place, rows * pairs), n_expert)
    sent = lax.div(place, rows * pairs * n_expert)
    block = 2 * lax.rem(pair + h, pairs) + lax.rem(core + sent, 2)
    wanted = (k * pairs * 2 + block) * rows + row
    return jnp.where(source == wanted, 1.0, 0.0).astype(jnp.bfloat16)


def ffn_kernel(n_expert, n_etp, rows, parts, own, *refs):
    near = refs[: n_expert - 1]
    far = refs[n_expert - 1 : 2 * n_expert - 2]
    w_gate, w_up, w_down, kept, sent, x, gate_v, up_v, down_v, sems = refs[2 * n_expert - 2 :]
    me = lax.axis_index("etp")
    core = lax.rem(me, 2)
    width = own.shape[1]
    half = width // 2
    step = width // parts
    copies = []
    for i, (src, dst) in enumerate(((w_gate, gate_v), (w_up, up_v), (w_down, down_v))):
        group = []
        for c in range(parts):
            cols = pl.ds(c * step, step)
            copy = pltpu.make_async_copy(src.at[0, :, cols], dst.at[:, cols], sems.at[i, c])
            copy.start()
            group.append(copy)
        copies.append(group)
    tok = own.shape[0]
    x[0:tok, :] = own[...]
    mine = pl.ds(pl.multiple_of(core * half, half), half)
    other = pl.ds(pl.multiple_of((1 - core) * half, half), half)
    for k in range(1, n_expert):
        x[k * tok : (k + 1) * tok, mine] = near[k - 1][...]
        x[k * tok : (k + 1) * tok, other] = far[k - 1][...]
    contract = (((1,), (1,)), ((), ()))
    sums = []
    for group, w in ((copies[0], gate_v), (copies[1], up_v)):
        total = None
        for c in range(parts):
            group[c].wait()
            cols = slice(c * step, (c + 1) * step)
            part = lax.dot_general(
                x[:, cols], w[:, cols], contract, preferred_element_type=jnp.float32
            )
            total = part if total is None else total + part
        sums.append(total)
    gate, upper = sums
    hidden = (gate / (1.0 + jnp.exp(-gate)) * upper).astype(jnp.bfloat16)
    order = order_matrix(n_expert, n_etp // 2, rows, me)
    hidden = jnp.dot(order, hidden, preferred_element_type=jnp.float32).astype(jnp.bfloat16)
    side = kept.shape[0]
    for c in range(parts):
        copies[2][c].wait()
        cols = slice(c * step, (c + 1) * step)
        out = jnp.dot(hidden, down_v[:, cols], preferred_element_type=jnp.float32)
        kept[:, cols] = out[:side]
        sent[:, cols] = out[side:].astype(jnp.bfloat16)


def add_kernel(rows, kept, arrived, *pieces):
    for i, piece in enumerate(pieces):
        span = slice(i * rows, (i + 1) * rows)
        piece[...] = (kept[span, :] + arrived[span, :].astype(jnp.float32)).astype(jnp.bfloat16)


def mix_kernel(n_expert, pairs, ids, weights, *refs):
    pieces, out = refs[:-1], refs[-1]
    rows = out.shape[0]
    me, expert = lax.axis_index("etp"), lax.axis_index("expert")
    own_ids = ids[pl.ds(me * rows, rows), :]
    scale = weights[...]
    scale = scale / jnp.sum(scale, axis=1, keepdims=True)
    total = None
    for k in range(n_expert):
        owner = lax.rem(expert + k, n_expert)
        factor = jnp.sum(jnp.where(own_ids == owner, scale, 0.0), axis=1, keepdims=True)
        summed = None
        for h in range(pairs):
            piece = pieces[k * pairs + h][...].astype(jnp.float32)
            summed = piece if summed is None else summed + piece
        term = summed * factor
        total = term if total is None else total + term
    out[...] = total.astype(out.dtype)


def on_device(n_expert, n_etp, tokens, expert_ids, route_weights, w_gate, w_up, w_down):
    tok, width = tokens.shape
    hidden = w_gate.shape[1]
    rows = tok // n_etp
    pairs = n_etp // 2
    side = n_expert * tok // 2
    half = width // 2
    me = lax.axis_index("etp")
    core = lax.rem(me, 2)

    own_half = lax.dynamic_slice_in_dim(tokens, core * half, half, 1)
    near, far = [], []
    swap = [(i, i ^ 1) for i in range(n_etp)]
    for k in range(1, n_expert):
        hop = [(i, (i + k) % n_expert) for i in range(n_expert)]
        near.append(lax.ppermute(own_half, "expert", hop))
    for block in near:
        far.append(lax.ppermute(block, "etp", swap))

    parts = 4
    kept, sent = pl.pallas_call(
        functools.partial(ffn_kernel, n_expert, n_etp, rows, parts),
        out_shape=(
            jax.ShapeDtypeStruct((side, width), jnp.float32),
            jax.ShapeDtypeStruct((side, width), jnp.bfloat16),
        ),
        in_specs=[VMEM] * (2 * n_expert - 1) + [HBM] * 3,
        out_specs=(VMEM, VMEM),
        scratch_shapes=[
            pltpu.VMEM((n_expert * tok, width), jnp.bfloat16),
            pltpu.VMEM((hidden, width), jnp.bfloat16),
            pltpu.VMEM((hidden, width), jnp.bfloat16),
            pltpu.VMEM((hidden, width), jnp.bfloat16),
            pltpu.SemaphoreType.DMA((3, parts)),
        ],
        compiler_params=pltpu.CompilerParams(vmem_limit_bytes=56 * 1024 * 1024),
        name="ffn",
    )(tokens, *near, *far, w_gate, w_up, w_down)

    arrived = lax.ppermute(sent, "etp", swap)
    count = n_expert * pairs
    pieces = pl.pallas_call(
        functools.partial(add_kernel, rows),
        out_shape=[jax.ShapeDtypeStruct((rows, width), jnp.bfloat16)] * count,
        in_specs=[VMEM] * 2,
        out_specs=[VMEM] * count,
        compiler_params=pltpu.CompilerParams(vmem_limit_bytes=56 * 1024 * 1024),
        name="add",
    )(kept, arrived)

    landed = []
    for i, piece in enumerate(pieces):
        k, h = divmod(i, pairs)
        route = []
        for e in range(n_expert):
            for t in range(n_etp):
                to_e, to_t = (e - k) % n_expert, 2 * ((t // 2 + h) % pairs) + t % 2
                route.append((e * n_etp + t, to_e * n_etp + to_t))
        landed.append(lax.ppermute(piece, ("expert", "etp"), route) if i else piece)

    return pl.pallas_call(
        functools.partial(mix_kernel, n_expert, pairs),
        out_shape=jax.ShapeDtypeStruct((rows, width), jnp.bfloat16),
        in_specs=[VMEM] * (2 + count),
        out_specs=VMEM,
        compiler_params=pltpu.CompilerParams(vmem_limit_bytes=56 * 1024 * 1024),
        name="mix",
    )(expert_ids, route_weights, *landed)


def solution(mesh):
    in_specs = (
        P(("group", "expert"), None),
        P(("group", "expert"), None),
        P(("group", "expert", "etp"), None),
        P("expert", "etp", None),
        P("expert", "etp", None),
        P("expert", "etp", None),
    )
    out_specs = P(("group", "expert", "etp"), None)
    return jax.shard_map(
        functools.partial(on_device, mesh.shape["expert"], mesh.shape["etp"]),
        mesh=mesh,
        in_specs=in_specs,
        out_specs=out_specs,
        check_vma=False,
    )
```

time: 96.4 us -> 44 us (0.46)
  waiting for transfers between devices: 37.4 us -> 8.77 us
  blocking collectives: 20.8 us -> 0 us
  starting transfers between devices: 4.6 us -> 18.7 us
  between operations: 13.5 us -> 0.12 us
  Pallas kernels: 0 us -> 11.7 us
  local copies, waits for them, and re-layouts: 11.2 us -> 4.49 us
  matrix products: 5.98 us -> 0 us
  other arithmetic: 2.56 us -> 0 us
    unnamed x2 -> x0, waiting for transfers between devices: 31.6 us -> none
    all_to_all x1 -> x0, blocking collectives: 20.8 us -> none  [on_device(): lax.all_to_all(send, 'expert', split_axis=0, concat_axis=0, tiled=True)]
    ppermute x0 -> x14, starting transfers between devices: none -> 18.7 us  [the longest x7 11.1 us: on_device(): landed.append(lax.ppermute(piece, ('expert', 'etp'), route) if i else piece)]
    pallas_call x0 -> x3, Pallas kernels: none -> 11.7 us  [the longest x1 8.15 us: on_device(): pl.pallas_call(functools.partial(ffn_kernel, n_expert, n_etp, rows, parts...]
    ppermute x0 -> x14, waiting for transfers between devices: none -> 8.77 us  [the longest x3 3.35 us: on_device(): near.append(lax.ppermute(own_half, 'expert', hop))]
    dot_general x3 -> x0, matrix products: 5.98 us -> none  [the longest x1 3.25 us: on_device(): jnp.einsum('sepcd,efd->sepcf', received, w_gate, preferred_element_type=j...]
    all_to_all x1 -> x0, waiting for transfers between devices: 5.83 us -> none  [on_device(): lax.all_to_all(summed, 'expert', split_axis=0, concat_axis=0, tiled=True)]
    all_to_all x1 -> x0, starting transfers between devices: 4.6 us -> none  [on_device(): lax.all_to_all(summed, 'expert', split_axis=0, concat_axis=0, tiled=True)]
  transfers between devices with their start and end apart: 2 -> 14, of which waited for: 2 -> 7; matrix products, arithmetic and copies ran while one was open for 1% -> 3% of each run, Pallas kernels for 0% -> 0%
where the time goes in v1:
time: 44 us; the launch traced here: 43.7 us
  starting transfers between devices  18.7 us (42%)
  Pallas kernels  11.7 us (27%)
  waiting for transfers between devices  8.77 us (20%)
  local copies, waits for them, and re-layouts  4.49 us (10%)
    ppermute x7, starting transfers between devices, on_device(): landed.append(lax.ppermute(piece, ('expert', 'etp'), route) if i else piece)  11.1 us
    pallas_call x1, Pallas kernels, on_device(): pl.pallas_call(functools.partial(ffn_kernel, n_expert, n_etp, rows, parts...  8.15 us
    ppermute x3, starting transfers between devices, on_device(): near.append(lax.ppermute(own_half, 'expert', hop))  7.01 us
    unnamed x34, local copies, waits for them, and re-layouts  3.65 us
    ppermute x3, waiting for transfers between devices, on_device(): near.append(lax.ppermute(own_half, 'expert', hop))  3.35 us
    ppermute x7, waiting for transfers between devices, on_device(): landed.append(lax.ppermute(piece, ('expert', 'etp'), route) if i else piece)  2.86 us
    pallas_call x1, Pallas kernels, on_device(): pl.pallas_call(functools.partial(add_kernel, rows), out_shape=[jax.ShapeD...  1.83 us
    pallas_call x1, Pallas kernels, on_device(): pl.pallas_call(functools.partial(mix_kernel, n_expert, pairs), out_shape=...  1.69 us
  transfers between devices with their start and end apart: 14, of which 7 were waited for; matrix products, arithmetic and copies ran while one was open for 3% of the time, Pallas kernels for 0%

profile of v1, /device:TPU:0, one launch (start us, length us, event | category | flops | bytes accessed | tf_op | source)
XLA Modules:
  0.0 43.7 jit_solution(2030132454539982939)
XLA Ops:
  0.0 0.8 %constant_dynamic-slice_fusion = bf16[16,2048]{1,0:T(8,128)(2,1)S(1)} fusion(bf16[16,4096]{1,0:T(8,128)(2,1)} %own.1, s32[]{:T(128)S(6)} %select_n.3), kind=kLoop, calls=%fused_computation | loop fusion | bytes 131076 | tf_op jit(solution)/shard_map/dynamic_slice | solution.py:114
  0.9 3.1 %collective-permute-start = (bf16[16,2048]{1,0:T(8,128)(2,1)S(1)}, bf16[16,2048]{1,0:T(8,128)(2,1)S(1)}, u32[]{:S(2)}, u32[]{:S(2)}) collective-permute-start(bf16[16,2048]{1,0:T(8,128)(2,1)S(1)} %constant_dynamic-slice_fusion), channel_id=1, source_target_pairs={{0,4},{4,8},{8,12},{12,0},{1,5},{5,9},{9,13},{13,1},{2,6},{6,10},{... | collective-permute-start | bytes 196616 | tf_op jit(solution)/shard_map/ppermute | solution.py:119
  3.9 2.6 %collective-permute-start.1 = (bf16[16,2048]{1,0:T(8,128)(2,1)S(1)}, bf16[16,2048]{1,0:T(8,128)(2,1)S(1)}, u32[]{:S(2)}, u32[]{:S(2)}) collective-permute-start(bf16[16,2048]{1,0:T(8,128)(2,1)S(1)} %constant_dynamic-slice_fusion), channel_id=1, source_target_pairs={{0,8},{4,12},{8,0},{12,4},{1,9},{5,13},{9,1},{13,5},{2,10},{6,14},... | collective-permute-start | bytes 196616 | tf_op jit(solution)/shard_map/ppermute | solution.py:119
  6.5 1.3 %collective-permute-start.2 = (bf16[16,2048]{1,0:T(8,128)(2,1)S(1)}, bf16[16,2048]{1,0:T(8,128)(2,1)S(1)}, u32[]{:S(2)}, u32[]{:S(2)}) collective-permute-start(bf16[16,2048]{1,0:T(8,128)(2,1)S(1)} %constant_dynamic-slice_fusion), channel_id=1, source_target_pairs={{0,12},{4,0},{8,4},{12,8},{1,13},{5,1},{9,5},{13,9},{2,14},{6,2},{... | collective-permute-start | bytes 196616 | tf_op jit(solution)/shard_map/ppermute | solution.py:119
  7.9 0.6 %collective-permute-done.refs_0_ = bf16[16,2048]{1,0:T(8,128)(2,1)S(1)} collective-permute-done((bf16[16,2048]{1,0:T(8,128)(2,1)S(1)}, bf16[16,2048]{1,0:T(8,128)(2,1)S(1)}, u32[]{:S(2)}, u32[]{:S(2)}) %collective-permute-start) | collective-permute-done | bytes 65568 | tf_op jit(solution)/shard_map/ppermute | solution.py:119
  8.5 2.5 %collective-permute-done.1.refs_1_ = bf16[16,2048]{1,0:T(8,128)(2,1)S(1)} collective-permute-done((bf16[16,2048]{1,0:T(8,128)(2,1)S(1)}, bf16[16,2048]{1,0:T(8,128)(2,1)S(1)}, u32[]{:S(2)}, u32[]{:S(2)}) %collective-permute-start.1) | collective-permute-done | bytes 65568 | tf_op jit(solution)/shard_map/ppermute | solution.py:119
  11.5 0.7 %collective-permute-done.4.refs_4_ = bf16[16,2048]{1,0:T(8,128)(2,1)S(1)} collective-permute-done((bf16[16,2048]{1,0:T(8,128)(2,1)S(1)}, bf16[16,2048]{1,0:T(8,128)(2,1)S(1)}, u32[]{:S(2)}, u32[]{:S(2)}) %collective-permute-start.4) | collective-permute-done | bytes 65568 | tf_op jit(solution)/shard_map/ppermute | solution.py:121
  12.5 0.4 copy-done.5
  12.9 0.6 %copy-done.6 = bf16[16,2048]{1,0:T(8,128)(2,1)} copy-done((bf16[16,2048]{1,0:T(8,128)(2,1)}, bf16[16,2048]{1,0:T(8,128)(2,1)S(1)}, u32[]{:S(2)}) %copy-start.6) | copy-done | bytes 65560
  13.5 8.1 %ffn.1 = (f32[32,4096]{1,0:T(8,128)}, bf16[32,4096]{1,0:T(8,128)(2,1)}) custom-call(bf16[16,4096]{1,0:T(8,128)(2,1)} %own.1, bf16[16,2048]{1,0:T(8,128)(2,1)} %copy-done.1, bf16[16,2048]{1,0:T(8,128)(2,1)} %copy-done.2, bf16[16,2048]{1,0:T(8,128)(2,1)} %copy-done.3, bf16[16,2048]{1,0:T(8,128)(2,1)} %copy-done.4, bf16[16,2048]{1,0:T(8,128)(2,1)} %copy-done.5, ...), custom_call_target="tpu_custom_call" | custom-call | tf_op jit(solution)/shard_map/ffn/pallas_call | solution.py:124
  21.9 1.6 %collective-permute-done.6.arrived = bf16[32,4096]{1,0:T(8,128)(2,1)S(1)} collective-permute-done((bf16[32,4096]{1,0:T(8,128)(2,1)}, bf16[32,4096]{1,0:T(8,128)(2,1)S(1)}, u32[]{:S(2)}, u32[]{:S(2)}) %collective-permute-start.6) | collective-permute-done | bytes 262176 | tf_op jit(solution)/shard_map/ppermute | solution.py:143
  23.5 0.7 %copy-done = bf16[32,4096]{1,0:T(8,128)(2,1)} copy-done((bf16[32,4096]{1,0:T(8,128)(2,1)}, bf16[32,4096]{1,0:T(8,128)(2,1)S(1)}, u32[]{:S(2)}) %copy-start) | copy-done | bytes 262168
  24.2 1.8 %add.5 = (bf16[4,4096]{1,0:T(4,128)(2,1)}, bf16[4,4096]{1,0:T(4,128)(2,1)}, bf16[4,4096]{1,0:T(4,128)(2,1)}, bf16[4,4096]{1,0:T(4,128)(2,1)}, bf16[4,4096]{1,0:T...) custom-call(f32[32,4096]{1,0:T(8,128)} %get-tuple-element.15.kept, ...), custom_call_target="tpu_custom_call" | custom-call | tf_op jit(solution)/shard_map/add/pallas_call | solution.py:145
  26.0 1.0 %collective-permute-start.10 = (bf16[4,4096]{1,0:T(4,128)(2,1)}, bf16[4,4096]{1,0:T(4,128)(2,1)S(1)}, u32[]{:S(2)}, u32[]{:S(2)}) collective-permute-start(bf16[4,4096]{1,0:T(4,128)(2,1)} %get-tuple-element.21), channel_id=1, source_target_pairs={{0,8},{1,9},{2,10},{3,11},{4,12},{5,13},{6,14},{7,15},{8,0},{9,1},... | collective-permute-start | bytes 98312 | tf_op jit(solution)/shard_map/ppermute | solution.py:162
  27.0 3.1 %collective-permute-start.11 = (bf16[4,4096]{1,0:T(4,128)(2,1)}, bf16[4,4096]{1,0:T(4,128)(2,1)S(1)}, u32[]{:S(2)}, u32[]{:S(2)}) collective-permute-start(bf16[4,4096]{1,0:T(4,128)(2,1)} %get-tuple-element.22), channel_id=1, source_target_pairs={{0,10},{1,11},{2,8},{3,9},{4,14},{5,15},{6,12},{7,13},{8,2},{9,3},... | collective-permute-start | bytes 98312 | tf_op jit(solution)/shard_map/ppermute | solution.py:162
  30.1 1.0 %collective-permute-start.12 = (bf16[4,4096]{1,0:T(4,128)(2,1)}, bf16[4,4096]{1,0:T(4,128)(2,1)S(1)}, u32[]{:S(2)}, u32[]{:S(2)}) collective-permute-start(bf16[4,4096]{1,0:T(4,128)(2,1)} %get-tuple-element.23), channel_id=1, source_target_pairs={{0,4},{1,5},{2,6},{3,7},{4,8},{5,9},{6,10},{7,11},{8,12},{9,13},{1... | collective-permute-start | bytes 98312 | tf_op jit(solution)/shard_map/ppermute | solution.py:162
  31.4 1.5 %collective-permute-start.7 = (bf16[4,4096]{1,0:T(4,128)(2,1)}, bf16[4,4096]{1,0:T(4,128)(2,1)S(1)}, u32[]{:S(2)}, u32[]{:S(2)}) collective-permute-start(bf16[4,4096]{1,0:T(4,128)(2,1)} %get-tuple-element.18), channel_id=1, source_target_pairs={{0,2},{1,3},{2,0},{3,1},{4,6},{5,7},{6,4},{7,5},{8,10},{9,11},{10,... | collective-permute-start | bytes 98312 | tf_op jit(solution)/shard_map/ppermute | solution.py:162
  32.9 3.5 %collective-permute-start.8 = (bf16[4,4096]{1,0:T(4,128)(2,1)}, bf16[4,4096]{1,0:T(4,128)(2,1)S(1)}, u32[]{:S(2)}, u32[]{:S(2)}) collective-permute-start(bf16[4,4096]{1,0:T(4,128)(2,1)} %get-tuple-element.19), channel_id=1, source_target_pairs={{0,12},{1,13},{2,14},{3,15},{4,0},{5,1},{6,2},{7,3},{8,4},{9,5},{1... | collective-permute-start | bytes 98312 | tf_op jit(solution)/shard_map/ppermute | solution.py:162
  36.4 0.8 %collective-permute-start.9 = (bf16[4,4096]{1,0:T(4,128)(2,1)}, bf16[4,4096]{1,0:T(4,128)(2,1)S(1)}, u32[]{:S(2)}, u32[]{:S(2)}) collective-permute-start(bf16[4,4096]{1,0:T(4,128)(2,1)} %get-tuple-element.20), channel_id=1, source_target_pairs={{0,14},{1,15},{2,12},{3,13},{4,2},{5,3},{6,0},{7,1},{8,6},{9,7},{1... | collective-permute-start | bytes 98312 | tf_op jit(solution)/shard_map/ppermute | solution.py:162
  37.2 0.7 %copy.7.ids = s32[16,2]{1,0:T(8,128)} copy(s32[16,2]{0,1:T(2,128)S(1)} %copy-done.14) | data formatting | bytes 256 | tf_op args[1]
  37.8 0.7 %copy.8.weights = f32[4,2]{1,0:T(4,128)} copy(f32[4,2]{0,1:T(2,128)S(1)} %copy-done.15) | data formatting | bytes 64 | tf_op args[2]
  38.6 2.8 %collective-permute-done.9.refs_3_ = bf16[4,4096]{1,0:T(4,128)(2,1)S(1)} collective-permute-done((bf16[4,4096]{1,0:T(4,128)(2,1)}, bf16[4,4096]{1,0:T(4,128)(2,1)S(1)}, u32[]{:S(2)}, u32[]{:S(2)}) %collective-permute-start.9) | collective-permute-done | bytes 32800 | tf_op jit(solution)/shard_map/ppermute | solution.py:162
  41.5 0.6 %copy-done.13 = bf16[4,4096]{1,0:T(4,128)(2,1)} copy-done((bf16[4,4096]{1,0:T(4,128)(2,1)}, bf16[4,4096]{1,0:T(4,128)(2,1)S(1)}, u32[]{:S(2)}) %copy-start.13) | copy-done | bytes 32792
  42.0 1.7 %mix.1 = bf16[4,4096]{1,0:T(4,128)(2,1)} custom-call(s32[16,2]{1,0:T(8,128)} %copy.7.ids, f32[4,2]{1,0:T(4,128)} %copy.8.weights, bf16[4,4096]{1,0:T(4,128)(2,1)} %get-tuple-element.17.refs_0_, bf16[4,4096]{1,0:T(4,128)(2,1)} %copy-done.11, bf16[4,4096]{1,0:T(4,128)(2,1)} %copy-done.12, bf16[4,4096]{1,0:T(4,128)(2,1)} %copy-done.13, ...), custom_call_target="tpu_custom_call" | custom-call | tf_op jit(solution)/shard_map/mix/pallas_call | solution.py:164
  (42 shorter events, 1.4 us)
Async XLA Ops:
  0.8 36.3 %copy-start.14 = (s32[16,2]{0,1:T(2,128)S(1)}, s32[16,2]{0,1:T(2,128)}, u32[]{:S(2)}) copy-start(s32[16,2]{0,1:T(2,128)} %param.7) | copy-start | bytes 388
  0.8 37.0 %copy-start.15 = (f32[4,2]{0,1:T(2,128)S(1)}, f32[4,2]{0,1:T(2,128)}, u32[]{:S(2)}) copy-start(f32[4,2]{0,1:T(2,128)} %param.8) | copy-start | bytes 100
  0.9 7.6 %collective-permute-start = (bf16[16,2048]{1,0:T(8,128)(2,1)S(1)}, bf16[16,2048]{1,0:T(8,128)(2,1)S(1)}, u32[]{:S(2)}, u32[]{:S(2)}) collective-permute-start(bf16[16,2048]{1,0:T(8,128)(2,1)S(1)} %constant_dynamic-slice_fusion), channel_id=1, source_target_pairs={{0,4},{4,8},{8,12},{12,0},{1,5},{5,9},{9,13},{13,1},{2,6},{6,10},{... | collective-permute-start | bytes 196616 | tf_op jit(solution)/shard_map/ppermute | solution.py:119
  3.9 7.1 %collective-permute-start.1 = (bf16[16,2048]{1,0:T(8,128)(2,1)S(1)}, bf16[16,2048]{1,0:T(8,128)(2,1)S(1)}, u32[]{:S(2)}, u32[]{:S(2)}) collective-permute-start(bf16[16,2048]{1,0:T(8,128)(2,1)S(1)} %constant_dynamic-slice_fusion), channel_id=1, source_target_pairs={{0,8},{4,12},{8,0},{12,4},{1,9},{5,13},{9,1},{13,5},{2,10},{6,14},... | collective-permute-start | bytes 196616 | tf_op jit(solution)/shard_map/ppermute | solution.py:119
  6.5 4.7 %collective-permute-start.2 = (bf16[16,2048]{1,0:T(8,128)(2,1)S(1)}, bf16[16,2048]{1,0:T(8,128)(2,1)S(1)}, u32[]{:S(2)}, u32[]{:S(2)}) collective-permute-start(bf16[16,2048]{1,0:T(8,128)(2,1)S(1)} %constant_dynamic-slice_fusion), channel_id=1, source_target_pairs={{0,12},{4,0},{8,4},{12,8},{1,13},{5,1},{9,5},{13,9},{2,14},{6,2},{... | collective-permute-start | bytes 196616 | tf_op jit(solution)/shard_map/ppermute | solution.py:119
  8.5 4.0 %copy-start.1 = (bf16[16,2048]{1,0:T(8,128)(2,1)}, bf16[16,2048]{1,0:T(8,128)(2,1)S(1)}, u32[]{:S(2)}) copy-start(bf16[16,2048]{1,0:T(8,128)(2,1)S(1)} %collective-permute-done.refs_0_) | copy-start | bytes 196612
  8.5 3.0 %collective-permute-start.3 = (bf16[16,2048]{1,0:T(8,128)(2,1)S(1)}, bf16[16,2048]{1,0:T(8,128)(2,1)S(1)}, u32[]{:S(2)}, u32[]{:S(2)}) collective-permute-start(bf16[16,2048]{1,0:T(8,128)(2,1)S(1)} %collective-permute-done.refs_0_), channel_id=1, source_target_pairs={{0,1},{1,0},{2,3},{3,2},{4,5},{5,4},{6,7},{7,6},{8,9},{9,8},{10,11... | collective-permute-start | bytes 196616 | tf_op jit(solution)/shard_map/ppermute | solution.py:121
  11.0 1.5 %copy-start.2 = (bf16[16,2048]{1,0:T(8,128)(2,1)}, bf16[16,2048]{1,0:T(8,128)(2,1)S(1)}, u32[]{:S(2)}) copy-start(bf16[16,2048]{1,0:T(8,128)(2,1)S(1)} %collective-permute-done.1.refs_1_) | copy-start | bytes 196612
  11.0 1.3 %collective-permute-start.4 = (bf16[16,2048]{1,0:T(8,128)(2,1)S(1)}, bf16[16,2048]{1,0:T(8,128)(2,1)S(1)}, u32[]{:S(2)}, u32[]{:S(2)}) collective-permute-start(bf16[16,2048]{1,0:T(8,128)(2,1)S(1)} %collective-permute-done.1.refs_1_), channel_id=1, source_target_pairs={{0,1},{1,0},{2,3},{3,2},{4,5},{5,4},{6,7},{7,6},{8,9},{9,8},{10,11... | collective-permute-start | bytes 196616 | tf_op jit(solution)/shard_map/ppermute | solution.py:121
  11.2 1.3 %collective-permute-start.5 = (bf16[16,2048]{1,0:T(8,128)(2,1)S(1)}, bf16[16,2048]{1,0:T(8,128)(2,1)S(1)}, u32[]{:S(2)}, u32[]{:S(2)}) collective-permute-start(bf16[16,2048]{1,0:T(8,128)(2,1)S(1)} %collective-permute-done.2.refs_2_), channel_id=1, source_target_pairs={{0,1},{1,0},{2,3},{3,2},{4,5},{5,4},{6,7},{7,6},{8,9},{9,8},{10,11... | collective-permute-start | bytes 196616 | tf_op jit(solution)/shard_map/ppermute | solution.py:121
  21.7 1.8 %collective-permute-start.6 = (bf16[32,4096]{1,0:T(8,128)(2,1)}, bf16[32,4096]{1,0:T(8,128)(2,1)S(1)}, u32[]{:S(2)}, u32[]{:S(2)}) collective-permute-start(bf16[32,4096]{1,0:T(8,128)(2,1)} %get-tuple-element.16), channel_id=1, source_target_pairs={{0,1},{1,0},{2,3},{3,2},{4,5},{5,4},{6,7},{7,6},{8,9},{9,8},{10,11... | collective-permute-start | bytes 786440 | tf_op jit(solution)/shard_map/ppermute | solution.py:143
  26.0 6.9 %collective-permute-start.10 = (bf16[4,4096]{1,0:T(4,128)(2,1)}, bf16[4,4096]{1,0:T(4,128)(2,1)S(1)}, u32[]{:S(2)}, u32[]{:S(2)}) collective-permute-start(bf16[4,4096]{1,0:T(4,128)(2,1)} %get-tuple-element.21), channel_id=1, source_target_pairs={{0,8},{1,9},{2,10},{3,11},{4,12},{5,13},{6,14},{7,15},{8,0},{9,1},... | collective-permute-start | bytes 98312 | tf_op jit(solution)/shard_map/ppermute | solution.py:162
  27.0 9.3 %collective-permute-start.11 = (bf16[4,4096]{1,0:T(4,128)(2,1)}, bf16[4,4096]{1,0:T(4,128)(2,1)S(1)}, u32[]{:S(2)}, u32[]{:S(2)}) collective-permute-start(bf16[4,4096]{1,0:T(4,128)(2,1)} %get-tuple-element.22), channel_id=1, source_target_pairs={{0,10},{1,11},{2,8},{3,9},{4,14},{5,15},{6,12},{7,13},{8,2},{9,3},... | collective-permute-start | bytes 98312 | tf_op jit(solution)/shard_map/ppermute | solution.py:162
  30.1 8.4 %collective-permute-start.12 = (bf16[4,4096]{1,0:T(4,128)(2,1)}, bf16[4,4096]{1,0:T(4,128)(2,1)S(1)}, u32[]{:S(2)}, u32[]{:S(2)}) collective-permute-start(bf16[4,4096]{1,0:T(4,128)(2,1)} %get-tuple-element.23), channel_id=1, source_target_pairs={{0,4},{1,5},{2,6},{3,7},{4,8},{5,9},{6,10},{7,11},{8,12},{9,13},{1... | collective-permute-start | bytes 98312 | tf_op jit(solution)/shard_map/ppermute | solution.py:162
  31.1 7.4 %collective-permute-start.13 = (bf16[4,4096]{1,0:T(4,128)(2,1)}, bf16[4,4096]{1,0:T(4,128)(2,1)S(1)}, u32[]{:S(2)}, u32[]{:S(2)}) collective-permute-start(bf16[4,4096]{1,0:T(4,128)(2,1)} %get-tuple-element.24), channel_id=1, source_target_pairs={{0,6},{1,7},{2,4},{3,5},{4,10},{5,11},{6,8},{7,9},{8,14},{9,15},{1... | collective-permute-start | bytes 98312 | tf_op jit(solution)/shard_map/ppermute | solution.py:162
  31.4 7.1 %collective-permute-start.7 = (bf16[4,4096]{1,0:T(4,128)(2,1)}, bf16[4,4096]{1,0:T(4,128)(2,1)S(1)}, u32[]{:S(2)}, u32[]{:S(2)}) collective-permute-start(bf16[4,4096]{1,0:T(4,128)(2,1)} %get-tuple-element.18), channel_id=1, source_target_pairs={{0,2},{1,3},{2,0},{3,1},{4,6},{5,7},{6,4},{7,5},{8,10},{9,11},{10,... | collective-permute-start | bytes 98312 | tf_op jit(solution)/shard_map/ppermute | solution.py:162
  32.9 8.5 %copy-start.7 = (bf16[4,4096]{1,0:T(4,128)(2,1)}, bf16[4,4096]{1,0:T(4,128)(2,1)S(1)}, u32[]{:S(2)}) copy-start(bf16[4,4096]{1,0:T(4,128)(2,1)S(1)} %collective-permute-done.10.refs_4_) | copy-start | bytes 98308
  32.9 5.6 %collective-permute-start.8 = (bf16[4,4096]{1,0:T(4,128)(2,1)}, bf16[4,4096]{1,0:T(4,128)(2,1)S(1)}, u32[]{:S(2)}, u32[]{:S(2)}) collective-permute-start(bf16[4,4096]{1,0:T(4,128)(2,1)} %get-tuple-element.19), channel_id=1, source_target_pairs={{0,12},{1,13},{2,14},{3,15},{4,0},{5,1},{6,2},{7,3},{8,4},{9,5},{1... | collective-permute-start | bytes 98312 | tf_op jit(solution)/shard_map/ppermute | solution.py:162
  36.4 5.0 %copy-start.8 = (bf16[4,4096]{1,0:T(4,128)(2,1)}, bf16[4,4096]{1,0:T(4,128)(2,1)S(1)}, u32[]{:S(2)}) copy-start(bf16[4,4096]{1,0:T(4,128)(2,1)S(1)} %collective-permute-done.11.refs_5_) | copy-start | bytes 98308
  36.4 5.0 %collective-permute-start.9 = (bf16[4,4096]{1,0:T(4,128)(2,1)}, bf16[4,4096]{1,0:T(4,128)(2,1)S(1)}, u32[]{:S(2)}, u32[]{:S(2)}) collective-permute-start(bf16[4,4096]{1,0:T(4,128)(2,1)} %get-tuple-element.20), channel_id=1, source_target_pairs={{0,14},{1,15},{2,12},{3,13},{4,2},{5,3},{6,0},{7,1},{8,6},{9,7},{1... | collective-permute-start | bytes 98312 | tf_op jit(solution)/shard_map/ppermute | solution.py:162
  38.5 2.9 %copy-start.9 = (bf16[4,4096]{1,0:T(4,128)(2,1)}, bf16[4,4096]{1,0:T(4,128)(2,1)S(1)}, u32[]{:S(2)}) copy-start(bf16[4,4096]{1,0:T(4,128)(2,1)S(1)} %collective-permute-done.12.refs_6_) | copy-start | bytes 98308
  38.5 2.9 %copy-start.10 = (bf16[4,4096]{1,0:T(4,128)(2,1)}, bf16[4,4096]{1,0:T(4,128)(2,1)S(1)}, u32[]{:S(2)}) copy-start(bf16[4,4096]{1,0:T(4,128)(2,1)S(1)} %collective-permute-done.13.refs_7_) | copy-start | bytes 98308
  38.5 2.9 %copy-start.11 = (bf16[4,4096]{1,0:T(4,128)(2,1)}, bf16[4,4096]{1,0:T(4,128)(2,1)S(1)}, u32[]{:S(2)}) copy-start(bf16[4,4096]{1,0:T(4,128)(2,1)S(1)} %collective-permute-done.7.refs_1_) | copy-start | bytes 98308
  38.6 2.9 %copy-start.12 = (bf16[4,4096]{1,0:T(4,128)(2,1)}, bf16[4,4096]{1,0:T(4,128)(2,1)S(1)}, u32[]{:S(2)}) copy-start(bf16[4,4096]{1,0:T(4,128)(2,1)S(1)} %collective-permute-done.8.refs_2_) | copy-start | bytes 98308
  (6 other events, 4.8 us)

commit v2 on v1

--- a/solution.py
+++ b/solution.py
@@ -8,7 +8,7 @@
 from jax.sharding import PartitionSpec as P
 
 VMEM = pl.BlockSpec(memory_space=pltpu.VMEM)
-HBM = pl.BlockSpec(memory_space=pl.ANY)
+HBM = pl.BlockSpec(memory_space=pltpu.HBM)
 
 
 def order_matrix(n_expert, pairs, rows, me):
@@ -25,25 +25,27 @@
     return jnp.where(source == wanted, 1.0, 0.0).astype(jnp.bfloat16)
 
 
+def load_kernel(count, *refs):
+    sources, targets, sems = refs[:count], refs[count : 2 * count], refs[-1]
+    copies = [
+        pltpu.make_async_copy(source, target, sems.at[i])
+        for i, (source, target) in enumerate(zip(sources, targets))
+    ]
+    for copy in copies:
+        copy.start()
+    for copy in copies:
+        copy.wait()
+
+
 def ffn_kernel(n_expert, n_etp, rows, parts, own, *refs):
     near = refs[: n_expert - 1]
     far = refs[n_expert - 1 : 2 * n_expert - 2]
-    w_gate, w_up, w_down, kept, sent, x, gate_v, up_v, down_v, sems = refs[2 * n_expert - 2 :]
+    w_gate, w_up, w_down, kept, sent, x = refs[2 * n_expert - 2 :]
     me = lax.axis_index("etp")
     core = lax.rem(me, 2)
-    width = own.shape[1]
+    tok, width = own.shape
     half = width // 2
     step = width // parts
-    copies = []
-    for i, (src, dst) in enumerate(((w_gate, gate_v), (w_up, up_v), (w_down, down_v))):
-        group = []
-        for c in range(parts):
-            cols = pl.ds(c * step, step)
-            copy = pltpu.make_async_copy(src.at[0, :, cols], dst.at[:, cols], sems.at[i, c])
-            copy.start()
-            group.append(copy)
-        copies.append(group)
-    tok = own.shape[0]
     x[0:tok, :] = own[...]
     mine = pl.ds(pl.multiple_of(core * half, half), half)
     other = pl.ds(pl.multiple_of((1 - core) * half, half), half)
@@ -51,26 +53,16 @@
         x[k * tok : (k + 1) * tok, mine] = near[k - 1][...]
         x[k * tok : (k + 1) * tok, other] = far[k - 1][...]
     contract = (((1,), (1,)), ((), ()))
-    sums = []
-    for group, w in ((copies[0], gate_v), (copies[1], up_v)):
-        total = None
-        for c in range(parts):
-            group[c].wait()
-            cols = slice(c * step, (c + 1) * step)
-            part = lax.dot_general(
-                x[:, cols], w[:, cols], contract, preferred_element_type=jnp.float32
-            )
-            total = part if total is None else total + part
-        sums.append(total)
-    gate, upper = sums
+    gate = lax.dot_general(w_gate[0], x[...], contract, preferred_element_type=jnp.float32)
+    upper = lax.dot_general(w_up[0], x[...], contract, preferred_element_type=jnp.float32)
     hidden = (gate / (1.0 + jnp.exp(-gate)) * upper).astype(jnp.bfloat16)
     order = order_matrix(n_expert, n_etp // 2, rows, me)
-    hidden = jnp.dot(order, hidden, preferred_element_type=jnp.float32).astype(jnp.bfloat16)
+    hidden = lax.dot_general(order, hidden, contract, preferred_element_type=jnp.float32)
+    hidden = hidden.astype(jnp.bfloat16)
     side = kept.shape[0]
     for c in range(parts):
-        copies[2][c].wait()
         cols = slice(c * step, (c + 1) * step)
-        out = jnp.dot(hidden, down_v[:, cols], preferred_element_type=jnp.float32)
+        out = jnp.dot(hidden, w_down[0, :, cols], preferred_element_type=jnp.float32)
         kept[:, cols] = out[:side]
         sent[:, cols] = out[side:].astype(jnp.bfloat16)
 
@@ -85,13 +77,21 @@
     pieces, out = refs[:-1], refs[-1]
     rows = out.shape[0]
     me, expert = lax.axis_index("etp"), lax.axis_index("expert")
-    own_ids = ids[pl.ds(me * rows, rows), :]
-    scale = weights[...]
-    scale = scale / jnp.sum(scale, axis=1, keepdims=True)
+    top, tok = ids.shape
+
+    def column(ref, start, i):
+        lane = lax.broadcasted_iota(jnp.int32, (rows, ref.shape[1]), 1)
+        row = lax.broadcasted_iota(jnp.int32, (rows, ref.shape[1]), 0)
+        values = jnp.where(lane == start + row, ref[i : i + 1, :], 0)
+        return jnp.sum(values, axis=1, keepdims=True)
+
+    own_ids = [column(ids, me * rows, i) for i in range(top)]
+    own_weights = [column(weights, 0, i) for i in range(top)]
+    scale = sum(own_weights)
     total = None
     for k in range(n_expert):
         owner = lax.rem(expert + k, n_expert)
-        factor = jnp.sum(jnp.where(own_ids == owner, scale, 0.0), axis=1, keepdims=True)
+        factor = sum(jnp.where(own_ids[i] == owner, own_weights[i], 0.0) for i in range(top)) / scale
         summed = None
         for h in range(pairs):
             piece = pieces[k * pairs + h][...].astype(jnp.float32)
@@ -103,7 +103,6 @@
 
 def on_device(n_expert, n_etp, tokens, expert_ids, route_weights, w_gate, w_up, w_down):
     tok, width = tokens.shape
-    hidden = w_gate.shape[1]
     rows = tok // n_etp
     pairs = n_etp // 2
     side = n_expert * tok // 2
@@ -120,6 +119,18 @@
     for block in near:
         far.append(lax.ppermute(block, "etp", swap))
 
+    weights = (w_gate, w_up, w_down)
+    size = sum(w.size * 2 for w in weights)
+    weights = pl.pallas_call(
+        functools.partial(load_kernel, len(weights)),
+        out_shape=[jax.ShapeDtypeStruct(w.shape, w.dtype) for w in weights],
+        in_specs=[HBM] * len(weights),
+        out_specs=[VMEM] * len(weights),
+        scratch_shapes=[pltpu.SemaphoreType.DMA((len(weights),))],
+        cost_estimate=pl.CostEstimate(flops=0, bytes_accessed=2 * size, transcendentals=0),
+        name="load",
+    )(*(pltpu.with_memory_space_constraint(w, pltpu.HBM) for w in weights))
+
     parts = 4
     kept, sent = pl.pallas_call(
         functools.partial(ffn_kernel, n_expert, n_etp, rows, parts),
@@ -127,18 +138,14 @@
             jax.ShapeDtypeStruct((side, width), jnp.float32),
             jax.ShapeDtypeStruct((side, width), jnp.bfloat16),
         ),
-        in_specs=[VMEM] * (2 * n_expert - 1) + [HBM] * 3,
+        in_specs=[VMEM] * (2 * n_expert + 2),
         out_specs=(VMEM, VMEM),
         scratch_shapes=[
             pltpu.VMEM((n_expert * tok, width), jnp.bfloat16),
-            pltpu.VMEM((hidden, width), jnp.bfloat16),
-            pltpu.VMEM((hidden, width), jnp.bfloat16),
-            pltpu.VMEM((hidden, width), jnp.bfloat16),
-            pltpu.SemaphoreType.DMA((3, parts)),
         ],
-        compiler_params=pltpu.CompilerParams(vmem_limit_bytes=56 * 1024 * 1024),
+        compiler_params=pltpu.CompilerParams(vmem_limit_bytes=16 * 1024 * 1024),
         name="ffn",
-    )(tokens, *near, *far, w_gate, w_up, w_down)
+    )(tokens, *near, *far, *weights)
 
     arrived = lax.ppermute(sent, "etp", swap)
     count = n_expert * pairs
@@ -147,7 +154,6 @@
         out_shape=[jax.ShapeDtypeStruct((rows, width), jnp.bfloat16)] * count,
         in_specs=[VMEM] * 2,
         out_specs=[VMEM] * count,
-        compiler_params=pltpu.CompilerParams(vmem_limit_bytes=56 * 1024 * 1024),
         name="add",
     )(kept, arrived)
 
@@ -166,9 +172,8 @@
         out_shape=jax.ShapeDtypeStruct((rows, width), jnp.bfloat16),
         in_specs=[VMEM] * (2 + count),
         out_specs=VMEM,
-        compiler_params=pltpu.CompilerParams(vmem_limit_bytes=56 * 1024 * 1024),
         name="mix",
-    )(expert_ids, route_weights, *landed)
+    )(expert_ids.T, route_weights.T, *landed)
 
 
 def solution(mesh):

time: 44 us -> 52.1 us (1.18)
  waiting for transfers between devices: 8.77 us -> 13.7 us
  local copies, waits for them, and re-layouts: 4.49 us -> 8.61 us
  starting transfers between devices: 18.7 us -> 15.9 us
  Pallas kernels: 11.7 us -> 13.4 us
    pallas_call x0 -> x1, Pallas kernels: none -> 7.37 us  [on_device(): pl.pallas_call(functools.partial(load_kernel, len(weights)), out_shape=[j...]
    pallas_call x1, Pallas kernels: 8.15 us -> 2.54 us  [on_device(): pl.pallas_call(functools.partial(ffn_kernel, n_expert, n_etp, rows, parts...]
    unnamed x34 -> x26, local copies, waits for them, and re-layouts: 3.65 us -> 7.76 us
    ppermute x7, waiting for transfers between devices: 2.86 us -> 6.71 us  [on_device(): landed.append(lax.ppermute(piece, ('expert', 'etp'), route) if i else piece)]
    ppermute x3, waiting for transfers between devices: 3.35 us -> 5.45 us  [on_device(): near.append(lax.ppermute(own_half, 'expert', hop))]
    ppermute x7, starting transfers between devices: 11.1 us -> 9.34 us  [on_device(): landed.append(lax.ppermute(piece, ('expert', 'etp'), route) if i else piece)]
    ppermute x3, waiting for transfers between devices: 0.96 us -> 0.01 us  [on_device(): far.append(lax.ppermute(block, 'etp', swap))]
    ppermute x3, starting transfers between devices: 7.01 us -> 6.06 us  [on_device(): near.append(lax.ppermute(own_half, 'expert', hop))]
  transfers between devices with their start and end apart: 14 -> 14, of which waited for: 7 -> 7; matrix products, arithmetic and copies ran while one was open for 3% -> 0% of each run, Pallas kernels for 0% -> 14%
where the time goes in v2:
time: 52.1 us; the launch traced here: 51.7 us
  starting transfers between devices  15.9 us (31%)
  waiting for transfers between devices  13.7 us (26%)
  Pallas kernels  13.4 us (26%)
  local copies, waits for them, and re-layouts  8.61 us (17%)
    ppermute x7, starting transfers between devices, on_device(): landed.append(lax.ppermute(piece, ('expert', 'etp'), route) if i else piece)  9.34 us
    unnamed x26, local copies, waits for them, and re-layouts  7.76 us
    pallas_call x1, Pallas kernels, on_device(): pl.pallas_call(functools.partial(load_kernel, len(weights)), out_shape=[j...  7.37 us
    ppermute x7, waiting for transfers between devices, on_device(): landed.append(lax.ppermute(piece, ('expert', 'etp'), route) if i else piece)  6.71 us
    ppermute x3, starting transfers between devices, on_device(): near.append(lax.ppermute(own_half, 'expert', hop))  6.06 us
    ppermute x3, waiting for transfers between devices, on_device(): near.append(lax.ppermute(own_half, 'expert', hop))  5.45 us
    pallas_call x1, Pallas kernels, on_device(): pl.pallas_call(functools.partial(ffn_kernel, n_expert, n_etp, rows, parts...  2.54 us
    pallas_call x1, Pallas kernels, on_device(): pl.pallas_call(functools.partial(add_kernel, rows), out_shape=[jax.ShapeD...  1.83 us
  transfers between devices with their start and end apart: 14, of which 7 were waited for; matrix products, arithmetic and copies ran while one was open for 0% of the time, Pallas kernels for 14%

profile of v2, /device:TPU:0, one launch (start us, length us, event | category | flops | bytes accessed | tf_op | source)
XLA Modules:
  0.0 51.7 jit_solution(15786755850057782653)
XLA Ops:
  0.0 0.8 %constant_dynamic-slice_fusion = bf16[16,2048]{1,0:T(8,128)(2,1)S(1)} fusion(bf16[16,4096]{1,0:T(8,128)(2,1)} %own.1, s32[]{:T(128)S(6)} %select_n.3), kind=kLoop, calls=%fused_computation | loop fusion | bytes 131076 | tf_op jit(solution)/shard_map/dynamic_slice | solution.py:113
  0.8 5.0 %collective-permute-start.2 = (bf16[16,2048]{1,0:T(8,128)(2,1)S(1)}, bf16[16,2048]{1,0:T(8,128)(2,1)S(1)}, u32[]{:S(2)}, u32[]{:S(2)}) collective-permute-start(bf16[16,2048]{1,0:T(8,128)(2,1)S(1)} %constant_dynamic-slice_fusion), channel_id=1, source_target_pairs={{0,12},{4,0},{8,4},{12,8},{1,13},{5,1},{9,5},{13,9},{2,14},{6,2},{... | collective-permute-start | bytes 196616 | tf_op jit(solution)/shard_map/ppermute | solution.py:118
  5.9 1.0 %collective-permute-start = (bf16[16,2048]{1,0:T(8,128)(2,1)S(1)}, bf16[16,2048]{1,0:T(8,128)(2,1)S(1)}, u32[]{:S(2)}, u32[]{:S(2)}) collective-permute-start(bf16[16,2048]{1,0:T(8,128)(2,1)S(1)} %constant_dynamic-slice_fusion), channel_id=1, source_target_pairs={{0,4},{4,8},{8,12},{12,0},{1,5},{5,9},{9,13},{13,1},{2,6},{6,10},{... | collective-permute-start | bytes 196616 | tf_op jit(solution)/shard_map/ppermute | solution.py:118
  6.9 1.5 %collective-permute-done.2.refs_2_ = bf16[16,2048]{1,0:T(8,128)(2,1)S(1)} collective-permute-done((bf16[16,2048]{1,0:T(8,128)(2,1)S(1)}, bf16[16,2048]{1,0:T(8,128)(2,1)S(1)}, u32[]{:S(2)}, u32[]{:S(2)}) %collective-permute-start.2) | collective-permute-done | bytes 65568 | tf_op jit(solution)/shard_map/ppermute | solution.py:118
  8.4 4.0 %collective-permute-done.1.refs_1_ = bf16[16,2048]{1,0:T(8,128)(2,1)S(1)} collective-permute-done((bf16[16,2048]{1,0:T(8,128)(2,1)S(1)}, bf16[16,2048]{1,0:T(8,128)(2,1)S(1)}, u32[]{:S(2)}, u32[]{:S(2)}) %collective-permute-start.1) | collective-permute-done | bytes 65568 | tf_op jit(solution)/shard_map/ppermute | solution.py:118
  12.9 7.4 %load.1 = (bf16[1,384,4096]{2,1,0:T(8,128)(2,1)}, bf16[1,384,4096]{2,1,0:T(8,128)(2,1)}, bf16[1,384,4096]{2,1,0:T(8,128)(2,1)}) custom-call(bf16[1,384,4096]{2,1,0:T(8,128)(2,1)} %refs_0_.1, bf16[1,384,4096]{2,1,0:T(8,128)(2,1)} %refs_1_.1, bf16[1,384,4096]{2,1,0:T(8,128)(2,1)} %refs_2_.1), custom_call_target="tpu_custom_call" | custom-call | bytes 18874368 | tf_op jit(solution)/shard_map/load/pallas_call | solution.py:124
  20.3 1.9 %copy-done = bf16[1,384,4096]{2,1,0:T(8,128)(2,1)S(1)} copy-done((bf16[1,384,4096]{2,1,0:T(8,128)(2,1)S(1)}, bf16[1,384,4096]{2,1,0:T(8,128)(2,1)}, u32[]{:S(2)}) %copy-start) | copy-done | bytes 3145752
  22.2 1.9 %copy-done.1 = bf16[1,384,4096]{2,1,0:T(8,128)(2,1)S(1)} copy-done((bf16[1,384,4096]{2,1,0:T(8,128)(2,1)S(1)}, bf16[1,384,4096]{2,1,0:T(8,128)(2,1)}, u32[]{:S(2)}) %copy-start.1) | copy-done | bytes 3145752
  24.1 1.9 %copy-done.2 = bf16[1,384,4096]{2,1,0:T(8,128)(2,1)S(1)} copy-done((bf16[1,384,4096]{2,1,0:T(8,128)(2,1)S(1)}, bf16[1,384,4096]{2,1,0:T(8,128)(2,1)}, u32[]{:S(2)}) %copy-start.2) | copy-done | bytes 3145752
  26.0 2.5 %ffn.1 = (f32[32,4096]{1,0:T(8,128)S(1)}, bf16[32,4096]{1,0:T(8,128)(2,1)S(1)}) custom-call(bf16[16,4096]{1,0:T(8,128)(2,1)S(1)} %copy-done.4, bf16[16,2048]{1,0:T(8,128)(2,1)S(1)} %collective-permute-done.refs_0_, bf16[16,2048]{1,0:T(8,128)(2,1)S(1)} %collective-permute-done.1.refs_1_, bf16[16,2048]{1,0:T(8,128)(2,1)S(1)} %collective-permute-done.2.refs_2_, ...), custom_call_target="tpu_custom_call" | custom-call | tf_op jit(solution)/shard_map/ffn/pallas_call | solution.py:135
  28.5 0.8 %copy-done.3 = f32[32,4096]{1,0:T(8,128)} copy-done((f32[32,4096]{1,0:T(8,128)}, f32[32,4096]{1,0:T(8,128)S(1)}, u32[]{:S(2)}) %copy-start.3) | copy-done | bytes 524312
  29.4 1.5 %collective-permute-done.6.arrived = bf16[32,4096]{1,0:T(8,128)(2,1)S(1)} collective-permute-done((bf16[32,4096]{1,0:T(8,128)(2,1)S(1)}, bf16[32,4096]{1,0:T(8,128)(2,1)S(1)}, u32[]{:S(2)}, u32[]{:S(2)}) %collective-permute-start.6) | collective-permute-done | bytes 262176 | tf_op jit(solution)/shard_map/ppermute | solution.py:150
  30.9 0.7 %copy-done.5 = bf16[32,4096]{1,0:T(8,128)(2,1)} copy-done((bf16[32,4096]{1,0:T(8,128)(2,1)}, bf16[32,4096]{1,0:T(8,128)(2,1)S(1)}, u32[]{:S(2)}) %copy-start.5) | copy-done | bytes 262168
  31.6 1.8 %add.5 = (bf16[4,4096]{1,0:T(4,128)(2,1)}, bf16[4,4096]{1,0:T(4,128)(2,1)}, bf16[4,4096]{1,0:T(4,128)(2,1)}, bf16[4,4096]{1,0:T(4,128)(2,1)}, bf16[4,4096]{1,0:T...) custom-call(f32[32,4096]{1,0:T(8,128)} %copy-done.3, ...), custom_call_target="tpu_custom_call" | custom-call | tf_op jit(solution)/shard_map/add/pallas_call | solution.py:152
  33.4 1.5 %collective-permute-start.7 = (bf16[4,4096]{1,0:T(4,128)(2,1)}, bf16[4,4096]{1,0:T(4,128)(2,1)S(1)}, u32[]{:S(2)}, u32[]{:S(2)}) collective-permute-start(bf16[4,4096]{1,0:T(4,128)(2,1)} %get-tuple-element.24), channel_id=1, source_target_pairs={{0,2},{1,3},{2,0},{3,1},{4,6},{5,7},{6,4},{7,5},{8,10},{9,11},{10,... | collective-permute-start | bytes 98312 | tf_op jit(solution)/shard_map/ppermute | solution.py:168
  34.9 1.9 %collective-permute-start.8 = (bf16[4,4096]{1,0:T(4,128)(2,1)}, bf16[4,4096]{1,0:T(4,128)(2,1)S(1)}, u32[]{:S(2)}, u32[]{:S(2)}) collective-permute-start(bf16[4,4096]{1,0:T(4,128)(2,1)} %get-tuple-element.25), channel_id=1, source_target_pairs={{0,12},{1,13},{2,14},{3,15},{4,0},{5,1},{6,2},{7,3},{8,4},{9,5},{1... | collective-permute-start | bytes 98312 | tf_op jit(solution)/shard_map/ppermute | solution.py:168
  36.8 1.0 %collective-permute-start.9 = (bf16[4,4096]{1,0:T(4,128)(2,1)}, bf16[4,4096]{1,0:T(4,128)(2,1)S(1)}, u32[]{:S(2)}, u32[]{:S(2)}) collective-permute-start(bf16[4,4096]{1,0:T(4,128)(2,1)} %get-tuple-element.26), channel_id=1, source_target_pairs={{0,14},{1,15},{2,12},{3,13},{4,2},{5,3},{6,0},{7,1},{8,6},{9,7},{1... | collective-permute-start | bytes 98312 | tf_op jit(solution)/shard_map/ppermute | solution.py:168
  38.4 3.3 %collective-permute-start.11 = (bf16[4,4096]{1,0:T(4,128)(2,1)}, bf16[4,4096]{1,0:T(4,128)(2,1)S(1)}, u32[]{:S(2)}, u32[]{:S(2)}) collective-permute-start(bf16[4,4096]{1,0:T(4,128)(2,1)} %get-tuple-element.28), channel_id=1, source_target_pairs={{0,10},{1,11},{2,8},{3,9},{4,14},{5,15},{6,12},{7,13},{8,2},{9,3},... | collective-permute-start | bytes 98312 | tf_op jit(solution)/shard_map/ppermute | solution.py:168
  41.6 1.0 %collective-permute-start.12 = (bf16[4,4096]{1,0:T(4,128)(2,1)}, bf16[4,4096]{1,0:T(4,128)(2,1)S(1)}, u32[]{:S(2)}, u32[]{:S(2)}) collective-permute-start(bf16[4,4096]{1,0:T(4,128)(2,1)} %get-tuple-element.29), channel_id=1, source_target_pairs={{0,4},{1,5},{2,6},{3,7},{4,8},{5,9},{6,10},{7,11},{8,12},{9,13},{1... | collective-permute-start | bytes 98312 | tf_op jit(solution)/shard_map/ppermute | solution.py:168
  42.8 0.6 %collective-permute-done.10.refs_4_ = bf16[4,4096]{1,0:T(4,128)(2,1)S(1)} collective-permute-done((bf16[4,4096]{1,0:T(4,128)(2,1)}, bf16[4,4096]{1,0:T(4,128)(2,1)S(1)}, u32[]{:S(2)}, u32[]{:S(2)}) %collective-permute-start.10) | collective-permute-done | bytes 32800 | tf_op jit(solution)/shard_map/ppermute | solution.py:168
  43.4 1.5 %collective-permute-done.11.refs_5_ = bf16[4,4096]{1,0:T(4,128)(2,1)S(1)} collective-permute-done((bf16[4,4096]{1,0:T(4,128)(2,1)}, bf16[4,4096]{1,0:T(4,128)(2,1)S(1)}, u32[]{:S(2)}, u32[]{:S(2)}) %collective-permute-start.11) | collective-permute-done | bytes 32800 | tf_op jit(solution)/shard_map/ppermute | solution.py:168
  44.9 2.7 %collective-permute-done.12.refs_6_ = bf16[4,4096]{1,0:T(4,128)(2,1)S(1)} collective-permute-done((bf16[4,4096]{1,0:T(4,128)(2,1)}, bf16[4,4096]{1,0:T(4,128)(2,1)S(1)}, u32[]{:S(2)}, u32[]{:S(2)}) %collective-permute-start.12) | collective-permute-done | bytes 32800 | tf_op jit(solution)/shard_map/ppermute | solution.py:168
  47.5 1.9 %collective-permute-done.13.refs_7_ = bf16[4,4096]{1,0:T(4,128)(2,1)S(1)} collective-permute-done((bf16[4,4096]{1,0:T(4,128)(2,1)}, bf16[4,4096]{1,0:T(4,128)(2,1)S(1)}, u32[]{:S(2)}, u32[]{:S(2)}) %collective-permute-start.13) | collective-permute-done | bytes 32800 | tf_op jit(solution)/shard_map/ppermute | solution.py:168
  50.1 1.6 %mix.1 = bf16[4,4096]{1,0:T(4,128)(2,1)} custom-call(s32[2,16]{1,0:T(2,128)} %bitcast.2, f32[2,4]{1,0:T(2,128)} %bitcast.3, bf16[4,4096]{1,0:T(4,128)(2,1)} %get-tuple-element.23.refs_0_, bf16[4,4096]{1,0:T(4,128)(2,1)} %copy-done.6, bf16[4,4096]{1,0:T(4,128)(2,1)} %copy-done.7, bf16[4,4096]{1,0:T(4,128)(2,1)} %copy-done.8, bf16[4,4096]{1,0:T(4,128)(2,1)} %copy-done.9, ...), custom_call_target="tpu_custom_call" | custom-call | tf_op jit(solution)/shard_map/mix/pallas_call | solution.py:170
  (35 shorter events, 1.9 us)
Async XLA Ops:
  0.8 19.5 %copy-start.4 = (bf16[16,4096]{1,0:T(8,128)(2,1)S(1)}, bf16[16,4096]{1,0:T(8,128)(2,1)}, u32[]{:S(2)}) copy-start(bf16[16,4096]{1,0:T(8,128)(2,1)} %own.1) | copy-start | bytes 393220
  0.8 7.5 %collective-permute-start.2 = (bf16[16,2048]{1,0:T(8,128)(2,1)S(1)}, bf16[16,2048]{1,0:T(8,128)(2,1)S(1)}, u32[]{:S(2)}, u32[]{:S(2)}) collective-permute-start(bf16[16,2048]{1,0:T(8,128)(2,1)S(1)} %constant_dynamic-slice_fusion), channel_id=1, source_target_pairs={{0,12},{4,0},{8,4},{12,8},{1,13},{5,1},{9,5},{13,9},{2,14},{6,2},{... | collective-permute-start | bytes 196616 | tf_op jit(solution)/shard_map/ppermute | solution.py:118
  5.9 6.5 %collective-permute-start.1 = (bf16[16,2048]{1,0:T(8,128)(2,1)S(1)}, bf16[16,2048]{1,0:T(8,128)(2,1)S(1)}, u32[]{:S(2)}, u32[]{:S(2)}) collective-permute-start(bf16[16,2048]{1,0:T(8,128)(2,1)S(1)} %constant_dynamic-slice_fusion), channel_id=1, source_target_pairs={{0,8},{4,12},{8,0},{12,4},{1,9},{5,13},{9,1},{13,5},{2,10},{6,14},... | collective-permute-start | bytes 196616 | tf_op jit(solution)/shard_map/ppermute | solution.py:118
  5.9 6.5 %collective-permute-start = (bf16[16,2048]{1,0:T(8,128)(2,1)S(1)}, bf16[16,2048]{1,0:T(8,128)(2,1)S(1)}, u32[]{:S(2)}, u32[]{:S(2)}) collective-permute-start(bf16[16,2048]{1,0:T(8,128)(2,1)S(1)} %constant_dynamic-slice_fusion), channel_id=1, source_target_pairs={{0,4},{4,8},{8,12},{12,0},{1,5},{5,9},{9,13},{13,1},{2,6},{6,10},{... | collective-permute-start | bytes 196616 | tf_op jit(solution)/shard_map/ppermute | solution.py:118
  8.4 11.9 %collective-permute-start.5 = (bf16[16,2048]{1,0:T(8,128)(2,1)S(1)}, bf16[16,2048]{1,0:T(8,128)(2,1)S(1)}, u32[]{:S(2)}, u32[]{:S(2)}) collective-permute-start(bf16[16,2048]{1,0:T(8,128)(2,1)S(1)} %collective-permute-done.2.refs_2_), channel_id=1, source_target_pairs={{0,1},{1,0},{2,3},{3,2},{4,5},{5,4},{6,7},{7,6},{8,9},{9,8},{10,11... | collective-permute-start | bytes 196616 | tf_op jit(solution)/shard_map/ppermute | solution.py:120
  12.4 7.9 %collective-permute-start.4 = (bf16[16,2048]{1,0:T(8,128)(2,1)S(1)}, bf16[16,2048]{1,0:T(8,128)(2,1)S(1)}, u32[]{:S(2)}, u32[]{:S(2)}) collective-permute-start(bf16[16,2048]{1,0:T(8,128)(2,1)S(1)} %collective-permute-done.1.refs_1_), channel_id=1, source_target_pairs={{0,1},{1,0},{2,3},{3,2},{4,5},{5,4},{6,7},{7,6},{8,9},{9,8},{10,11... | collective-permute-start | bytes 196616 | tf_op jit(solution)/shard_map/ppermute | solution.py:120
  12.4 7.9 %collective-permute-start.3 = (bf16[16,2048]{1,0:T(8,128)(2,1)S(1)}, bf16[16,2048]{1,0:T(8,128)(2,1)S(1)}, u32[]{:S(2)}, u32[]{:S(2)}) collective-permute-start(bf16[16,2048]{1,0:T(8,128)(2,1)S(1)} %collective-permute-done.refs_0_), channel_id=1, source_target_pairs={{0,1},{1,0},{2,3},{3,2},{4,5},{5,4},{6,7},{7,6},{8,9},{9,8},{10,11... | collective-permute-start | bytes 196616 | tf_op jit(solution)/shard_map/ppermute | solution.py:120
  20.3 1.9 %copy-start = (bf16[1,384,4096]{2,1,0:T(8,128)(2,1)S(1)}, bf16[1,384,4096]{2,1,0:T(8,128)(2,1)}, u32[]{:S(2)}) copy-start(bf16[1,384,4096]{2,1,0:T(8,128)(2,1)} %get-tuple-element.18.refs_6_) | copy-start | bytes 9437188
  22.2 1.9 %copy-start.1 = (bf16[1,384,4096]{2,1,0:T(8,128)(2,1)S(1)}, bf16[1,384,4096]{2,1,0:T(8,128)(2,1)}, u32[]{:S(2)}) copy-start(bf16[1,384,4096]{2,1,0:T(8,128)(2,1)} %get-tuple-element.19.refs_7_) | copy-start | bytes 9437188
  24.1 1.9 %copy-start.2 = (bf16[1,384,4096]{2,1,0:T(8,128)(2,1)S(1)}, bf16[1,384,4096]{2,1,0:T(8,128)(2,1)}, u32[]{:S(2)}) copy-start(bf16[1,384,4096]{2,1,0:T(8,128)(2,1)} %get-tuple-element.20.refs_8_) | copy-start | bytes 9437188
  29.3 1.5 %collective-permute-start.6 = (bf16[32,4096]{1,0:T(8,128)(2,1)S(1)}, bf16[32,4096]{1,0:T(8,128)(2,1)S(1)}, u32[]{:S(2)}, u32[]{:S(2)}) collective-permute-start(bf16[32,4096]{1,0:T(8,128)(2,1)S(1)} %get-tuple-element.22), channel_id=1, source_target_pairs={{0,1},{1,0},{2,3},{3,2},{4,5},{5,4},{6,7},{7,6},{8,9},{9,8},{10,11... | collective-permute-start | bytes 786440 | tf_op jit(solution)/shard_map/ppermute | solution.py:150
  33.4 8.2 %collective-permute-start.7 = (bf16[4,4096]{1,0:T(4,128)(2,1)}, bf16[4,4096]{1,0:T(4,128)(2,1)S(1)}, u32[]{:S(2)}, u32[]{:S(2)}) collective-permute-start(bf16[4,4096]{1,0:T(4,128)(2,1)} %get-tuple-element.24), channel_id=1, source_target_pairs={{0,2},{1,3},{2,0},{3,1},{4,6},{5,7},{6,4},{7,5},{8,10},{9,11},{10,... | collective-permute-start | bytes 98312 | tf_op jit(solution)/shard_map/ppermute | solution.py:168
  34.9 7.8 %collective-permute-start.8 = (bf16[4,4096]{1,0:T(4,128)(2,1)}, bf16[4,4096]{1,0:T(4,128)(2,1)S(1)}, u32[]{:S(2)}, u32[]{:S(2)}) collective-permute-start(bf16[4,4096]{1,0:T(4,128)(2,1)} %get-tuple-element.25), channel_id=1, source_target_pairs={{0,12},{1,13},{2,14},{3,15},{4,0},{5,1},{6,2},{7,3},{8,4},{9,5},{1... | collective-permute-start | bytes 98312 | tf_op jit(solution)/shard_map/ppermute | solution.py:168
  36.8 6.0 %collective-permute-start.9 = (bf16[4,4096]{1,0:T(4,128)(2,1)}, bf16[4,4096]{1,0:T(4,128)(2,1)S(1)}, u32[]{:S(2)}, u32[]{:S(2)}) collective-permute-start(bf16[4,4096]{1,0:T(4,128)(2,1)} %get-tuple-element.26), channel_id=1, source_target_pairs={{0,14},{1,15},{2,12},{3,13},{4,2},{5,3},{6,0},{7,1},{8,6},{9,7},{1... | collective-permute-start | bytes 98312 | tf_op jit(solution)/shard_map/ppermute | solution.py:168
  37.8 5.7 %collective-permute-start.10 = (bf16[4,4096]{1,0:T(4,128)(2,1)}, bf16[4,4096]{1,0:T(4,128)(2,1)S(1)}, u32[]{:S(2)}, u32[]{:S(2)}) collective-permute-start(bf16[4,4096]{1,0:T(4,128)(2,1)} %get-tuple-element.27), channel_id=1, source_target_pairs={{0,8},{1,9},{2,10},{3,11},{4,12},{5,13},{6,14},{7,15},{8,0},{9,1},... | collective-permute-start | bytes 98312 | tf_op jit(solution)/shard_map/ppermute | solution.py:168
  38.4 6.5 %collective-permute-start.11 = (bf16[4,4096]{1,0:T(4,128)(2,1)}, bf16[4,4096]{1,0:T(4,128)(2,1)S(1)}, u32[]{:S(2)}, u32[]{:S(2)}) collective-permute-start(bf16[4,4096]{1,0:T(4,128)(2,1)} %get-tuple-element.28), channel_id=1, source_target_pairs={{0,10},{1,11},{2,8},{3,9},{4,14},{5,15},{6,12},{7,13},{8,2},{9,3},... | collective-permute-start | bytes 98312 | tf_op jit(solution)/shard_map/ppermute | solution.py:168
  41.6 7.9 %copy-start.6 = (bf16[4,4096]{1,0:T(4,128)(2,1)}, bf16[4,4096]{1,0:T(4,128)(2,1)S(1)}, u32[]{:S(2)}) copy-start(bf16[4,4096]{1,0:T(4,128)(2,1)S(1)} %collective-permute-done.7.refs_1_) | copy-start | bytes 98308
  41.6 5.9 %collective-permute-start.12 = (bf16[4,4096]{1,0:T(4,128)(2,1)}, bf16[4,4096]{1,0:T(4,128)(2,1)S(1)}, u32[]{:S(2)}, u32[]{:S(2)}) collective-permute-start(bf16[4,4096]{1,0:T(4,128)(2,1)} %get-tuple-element.29), channel_id=1, source_target_pairs={{0,4},{1,5},{2,6},{3,7},{4,8},{5,9},{6,10},{7,11},{8,12},{9,13},{1... | collective-permute-start | bytes 98312 | tf_op jit(solution)/shard_map/ppermute | solution.py:168
  42.6 6.8 %copy-start.7 = (bf16[4,4096]{1,0:T(4,128)(2,1)}, bf16[4,4096]{1,0:T(4,128)(2,1)S(1)}, u32[]{:S(2)}) copy-start(bf16[4,4096]{1,0:T(4,128)(2,1)S(1)} %collective-permute-done.8.refs_2_) | copy-start | bytes 98308
  42.7 6.8 %collective-permute-start.13 = (bf16[4,4096]{1,0:T(4,128)(2,1)}, bf16[4,4096]{1,0:T(4,128)(2,1)S(1)}, u32[]{:S(2)}, u32[]{:S(2)}) collective-permute-start(bf16[4,4096]{1,0:T(4,128)(2,1)} %get-tuple-element.30), channel_id=1, source_target_pairs={{0,6},{1,7},{2,4},{3,5},{4,10},{5,11},{6,8},{7,9},{8,14},{9,15},{1... | collective-permute-start | bytes 98312 | tf_op jit(solution)/shard_map/ppermute | solution.py:168
  42.8 6.7 %copy-start.8 = (bf16[4,4096]{1,0:T(4,128)(2,1)}, bf16[4,4096]{1,0:T(4,128)(2,1)S(1)}, u32[]{:S(2)}) copy-start(bf16[4,4096]{1,0:T(4,128)(2,1)S(1)} %collective-permute-done.9.refs_3_) | copy-start | bytes 98308
  43.4 6.1 %copy-start.9 = (bf16[4,4096]{1,0:T(4,128)(2,1)}, bf16[4,4096]{1,0:T(4,128)(2,1)S(1)}, u32[]{:S(2)}) copy-start(bf16[4,4096]{1,0:T(4,128)(2,1)S(1)} %collective-permute-done.10.refs_4_) | copy-start | bytes 98308
  44.9 4.6 %copy-start.10 = (bf16[4,4096]{1,0:T(4,128)(2,1)}, bf16[4,4096]{1,0:T(4,128)(2,1)S(1)}, u32[]{:S(2)}) copy-start(bf16[4,4096]{1,0:T(4,128)(2,1)S(1)} %collective-permute-done.11.refs_5_) | copy-start | bytes 98308
  47.5 2.0 %copy-start.11 = (bf16[4,4096]{1,0:T(4,128)(2,1)}, bf16[4,4096]{1,0:T(4,128)(2,1)S(1)}, u32[]{:S(2)}) copy-start(bf16[4,4096]{1,0:T(4,128)(2,1)S(1)} %collective-permute-done.12.refs_6_) | copy-start | bytes 98308
  (3 other events, 2.1 us)

commit v3 on v2

--- a/solution.py
+++ b/solution.py
@@ -8,6 +8,7 @@
 from jax.sharding import PartitionSpec as P
 
 VMEM = pl.BlockSpec(memory_space=pltpu.VMEM)
+GRANT = pltpu.CompilerParams(vmem_limit_bytes=16 * 1024 * 1024)
 HBM = pl.BlockSpec(memory_space=pltpu.HBM)
 
 
@@ -25,12 +26,16 @@
     return jnp.where(source == wanted, 1.0, 0.0).astype(jnp.bfloat16)
 
 
-def load_kernel(count, *refs):
+def load_kernel(count, parts, *refs):
     sources, targets, sems = refs[:count], refs[count : 2 * count], refs[-1]
-    copies = [
-        pltpu.make_async_copy(source, target, sems.at[i])
-        for i, (source, target) in enumerate(zip(sources, targets))
-    ]
+    copies = []
+    for i, (source, target) in enumerate(zip(sources, targets)):
+        step = source.shape[1] // parts
+        for c in range(parts):
+            span = pl.ds(c * step, step)
+            copies.append(
+                pltpu.make_async_copy(source.at[:, span], target.at[:, span], sems.at[i, c])
+            )
     for copy in copies:
         copy.start()
     for copy in copies:
@@ -119,19 +124,20 @@
     for block in near:
         far.append(lax.ppermute(block, "etp", swap))
 
+    parts = 4
     weights = (w_gate, w_up, w_down)
     size = sum(w.size * 2 for w in weights)
     weights = pl.pallas_call(
-        functools.partial(load_kernel, len(weights)),
+        functools.partial(load_kernel, len(weights), parts),
         out_shape=[jax.ShapeDtypeStruct(w.shape, w.dtype) for w in weights],
         in_specs=[HBM] * len(weights),
         out_specs=[VMEM] * len(weights),
-        scratch_shapes=[pltpu.SemaphoreType.DMA((len(weights),))],
+        scratch_shapes=[pltpu.SemaphoreType.DMA((len(weights), parts))],
         cost_estimate=pl.CostEstimate(flops=0, bytes_accessed=2 * size, transcendentals=0),
+        compiler_params=GRANT,
         name="load",
     )(*(pltpu.with_memory_space_constraint(w, pltpu.HBM) for w in weights))
 
-    parts = 4
     kept, sent = pl.pallas_call(
         functools.partial(ffn_kernel, n_expert, n_etp, rows, parts),
         out_shape=(
@@ -143,7 +149,7 @@
         scratch_shapes=[
             pltpu.VMEM((n_expert * tok, width), jnp.bfloat16),
         ],
-        compiler_params=pltpu.CompilerParams(vmem_limit_bytes=16 * 1024 * 1024),
+        compiler_params=GRANT,
         name="ffn",
     )(tokens, *near, *far, *weights)
 
@@ -154,6 +160,7 @@
         out_shape=[jax.ShapeDtypeStruct((rows, width), jnp.bfloat16)] * count,
         in_specs=[VMEM] * 2,
         out_specs=[VMEM] * count,
+        compiler_params=GRANT,
         name="add",
     )(kept, arrived)
 
@@ -172,6 +179,7 @@
         out_shape=jax.ShapeDtypeStruct((rows, width), jnp.bfloat16),
         in_specs=[VMEM] * (2 + count),
         out_specs=VMEM,
+        compiler_params=GRANT,
         name="mix",
     )(expert_ids.T, route_weights.T, *landed)
 

time: 52.1 us -> 37.8 us (0.73)
  local copies, waits for them, and re-layouts: 8.61 us -> 0.86 us
  Pallas kernels: 13.4 us -> 7.19 us
    unnamed x26 -> x6, local copies, waits for them, and re-layouts: 7.76 us -> 0.02 us
    pallas_call x1, Pallas kernels: 7.37 us -> 3.79 us  [on_device(): pl.pallas_call(functools.partial(load_kernel, len(weights), parts), out_s...]
    pallas_call x1, Pallas kernels: 1.83 us -> 0.12 us  [on_device(): pl.pallas_call(functools.partial(add_kernel, rows), out_shape=[jax.ShapeD...]
    pallas_call x1, Pallas kernels: 1.64 us -> 0.74 us  [on_device(): pl.pallas_call(functools.partial(mix_kernel, n_expert, pairs), out_shape=...]
  transfers between devices with their start and end apart: 14 -> 14, of which waited for: 7 -> 7; matrix products, arithmetic and copies ran while one was open for 0% -> 0% of each run, Pallas kernels for 14% -> 10%
where the time goes in v3:
time: 37.8 us; the launch traced here: 37.7 us
  starting transfers between devices  16.1 us (43%)
  waiting for transfers between devices  13.5 us (36%)
  Pallas kernels  7.19 us (19%)
  local copies, waits for them, and re-layouts  0.86 us (2%)
    ppermute x7, starting transfers between devices, on_device(): landed.append(lax.ppermute(piece, ('expert', 'etp'), route) if i else piece)  9.4 us
    ppermute x7, waiting for transfers between devices, on_device(): landed.append(lax.ppermute(piece, ('expert', 'etp'), route) if i else piece)  6.51 us
    ppermute x3, starting transfers between devices, on_device(): near.append(lax.ppermute(own_half, 'expert', hop))  6.06 us
    ppermute x3, waiting for transfers between devices, on_device(): near.append(lax.ppermute(own_half, 'expert', hop))  5.45 us
    pallas_call x1, Pallas kernels, on_device(): pl.pallas_call(functools.partial(load_kernel, len(weights), parts), out_s...  3.79 us
    pallas_call x1, Pallas kernels, on_device(): pl.pallas_call(functools.partial(ffn_kernel, n_expert, n_etp, rows, parts...  2.54 us
    ppermute x1, waiting for transfers between devices, on_device(): arrived = lax.ppermute(sent, 'etp', swap)  1.52 us
    dynamic_slice x1, local copies, waits for them, and re-layouts, on_device(): own_half = lax.dynamic_slice_in_dim(tokens, core * half, half, 1)  0.84 us
  transfers between devices with their start and end apart: 14, of which 7 were waited for; matrix products, arithmetic and copies ran while one was open for 0% of the time, Pallas kernels for 10%

profile of v3, /device:TPU:0, one launch (start us, length us, event | category | flops | bytes accessed | tf_op | source)
XLA Modules:
  0.0 37.7 jit_solution(14205342088448723763)
XLA Ops:
  0.0 0.8 %constant_dynamic-slice_fusion = bf16[16,2048]{1,0:T(8,128)(2,1)S(1)} fusion(bf16[16,4096]{1,0:T(8,128)(2,1)} %own.1, s32[]{:T(128)S(6)} %select_n.3), kind=kLoop, calls=%fused_computation | loop fusion | bytes 131076 | tf_op jit(solution)/shard_map/dynamic_slice | solution.py:118
  0.8 5.0 %collective-permute-start.2 = (bf16[16,2048]{1,0:T(8,128)(2,1)S(1)}, bf16[16,2048]{1,0:T(8,128)(2,1)S(1)}, u32[]{:S(2)}, u32[]{:S(2)}) collective-permute-start(bf16[16,2048]{1,0:T(8,128)(2,1)S(1)} %constant_dynamic-slice_fusion), channel_id=1, source_target_pairs={{0,12},{4,0},{8,4},{12,8},{1,13},{5,1},{9,5},{13,9},{2,14},{6,2},{... | collective-permute-start | bytes 196616 | tf_op jit(solution)/shard_map/ppermute | solution.py:123
  5.9 1.0 %collective-permute-start = (bf16[16,2048]{1,0:T(8,128)(2,1)S(1)}, bf16[16,2048]{1,0:T(8,128)(2,1)S(1)}, u32[]{:S(2)}, u32[]{:S(2)}) collective-permute-start(bf16[16,2048]{1,0:T(8,128)(2,1)S(1)} %constant_dynamic-slice_fusion), channel_id=1, source_target_pairs={{0,4},{4,8},{8,12},{12,0},{1,5},{5,9},{9,13},{13,1},{2,6},{6,10},{... | collective-permute-start | bytes 196616 | tf_op jit(solution)/shard_map/ppermute | solution.py:123
  6.9 1.5 %collective-permute-done.2.refs_2_ = bf16[16,2048]{1,0:T(8,128)(2,1)S(1)} collective-permute-done((bf16[16,2048]{1,0:T(8,128)(2,1)S(1)}, bf16[16,2048]{1,0:T(8,128)(2,1)S(1)}, u32[]{:S(2)}, u32[]{:S(2)}) %collective-permute-start.2) | collective-permute-done | bytes 65568 | tf_op jit(solution)/shard_map/ppermute | solution.py:123
  8.4 4.0 %collective-permute-done.1.refs_1_ = bf16[16,2048]{1,0:T(8,128)(2,1)S(1)} collective-permute-done((bf16[16,2048]{1,0:T(8,128)(2,1)S(1)}, bf16[16,2048]{1,0:T(8,128)(2,1)S(1)}, u32[]{:S(2)}, u32[]{:S(2)}) %collective-permute-start.1) | collective-permute-done | bytes 65568 | tf_op jit(solution)/shard_map/ppermute | solution.py:123
  12.4 0.5 %collective-permute-start.3 = (bf16[16,2048]{1,0:T(8,128)(2,1)S(1)}, bf16[16,2048]{1,0:T(8,128)(2,1)S(1)}, u32[]{:S(2)}, u32[]{:S(2)}) collective-permute-start(bf16[16,2048]{1,0:T(8,128)(2,1)S(1)} %collective-permute-done.refs_0_), channel_id=1, source_target_pairs={{0,1},{1,0},{2,3},{3,2},{4,5},{5,4},{6,7},{7,6},{8,9},{9,8},{10,11... | collective-permute-start | bytes 196616 | tf_op jit(solution)/shard_map/ppermute | solution.py:125
  12.9 3.8 %load.1 = (bf16[1,384,4096]{2,1,0:T(8,128)(2,1)S(1)}, bf16[1,384,4096]{2,1,0:T(8,128)(2,1)S(1)}, bf16[1,384,4096]{2,1,0:T(8,128)(2,1)S(1)}) custom-call(bf16[1,384,4096]{2,1,0:T(8,128)(2,1)} %refs_0_.1, bf16[1,384,4096]{2,1,0:T(8,128)(2,1)} %refs_1_.1, bf16[1,384,4096]{2,1,0:T(8,128)(2,1)} %refs_2_.1), custom_call_target="tpu_custom_call" | custom-call | bytes 18874368 | tf_op jit(solution)/shard_map/load/pallas_call | solution.py:130
  16.7 0.0 copy-start.1
  16.7 2.5 %ffn.1 = (f32[32,4096]{1,0:T(8,128)S(1)}, bf16[32,4096]{1,0:T(8,128)(2,1)S(1)}) custom-call(bf16[16,4096]{1,0:T(8,128)(2,1)S(1)} %copy-done, bf16[16,2048]{1,0:T(8,128)(2,1)S(1)} %collective-permute-done.refs_0_, bf16[16,2048]{1,0:T(8,128)(2,1)S(1)} %collective-permute-done.1.refs_1_, bf16[16,2048]{1,0:T(8,128)(2,1)S(1)} %collective-permute-done.2.refs_2_, ...), custom_call_target="tpu_custom_call" | custom-call | tf_op jit(solution)/shard_map/ffn/pallas_call | solution.py:141
  19.3 0.1 collective-permute-start.6
  19.4 1.5 %collective-permute-done.6.arrived = bf16[32,4096]{1,0:T(8,128)(2,1)S(1)} collective-permute-done((bf16[32,4096]{1,0:T(8,128)(2,1)S(1)}, bf16[32,4096]{1,0:T(8,128)(2,1)S(1)}, u32[]{:S(2)}, u32[]{:S(2)}) %collective-permute-start.6) | collective-permute-done | bytes 262176 | tf_op jit(solution)/shard_map/ppermute | solution.py:156
  20.9 0.1 add.5
  21.0 1.6 %collective-permute-start.7 = (bf16[4,4096]{1,0:T(4,128)(2,1)S(1)}, bf16[4,4096]{1,0:T(4,128)(2,1)S(1)}, u32[]{:S(2)}, u32[]{:S(2)}) collective-permute-start(bf16[4,4096]{1,0:T(4,128)(2,1)S(1)} %get-tuple-element.24), channel_id=1, source_target_pairs={{0,2},{1,3},{2,0},{3,1},{4,6},{5,7},{6,4},{7,5},{8,10},{9,11},{10,... | collective-permute-start | bytes 98312 | tf_op jit(solution)/shard_map/ppermute | solution.py:175
  22.6 1.9 %collective-permute-start.8 = (bf16[4,4096]{1,0:T(4,128)(2,1)S(1)}, bf16[4,4096]{1,0:T(4,128)(2,1)S(1)}, u32[]{:S(2)}, u32[]{:S(2)}) collective-permute-start(bf16[4,4096]{1,0:T(4,128)(2,1)S(1)} %get-tuple-element.25), channel_id=1, source_target_pairs={{0,12},{1,13},{2,14},{3,15},{4,0},{5,1},{6,2},{7,3},{8,4},{9,5},{1... | collective-permute-start | bytes 98312 | tf_op jit(solution)/shard_map/ppermute | solution.py:175
  24.5 1.0 %collective-permute-start.9 = (bf16[4,4096]{1,0:T(4,128)(2,1)S(1)}, bf16[4,4096]{1,0:T(4,128)(2,1)S(1)}, u32[]{:S(2)}, u32[]{:S(2)}) collective-permute-start(bf16[4,4096]{1,0:T(4,128)(2,1)S(1)} %get-tuple-element.26), channel_id=1, source_target_pairs={{0,14},{1,15},{2,12},{3,13},{4,2},{5,3},{6,0},{7,1},{8,6},{9,7},{1... | collective-permute-start | bytes 98312 | tf_op jit(solution)/shard_map/ppermute | solution.py:175
  25.4 0.6 %collective-permute-start.10 = (bf16[4,4096]{1,0:T(4,128)(2,1)S(1)}, bf16[4,4096]{1,0:T(4,128)(2,1)S(1)}, u32[]{:S(2)}, u32[]{:S(2)}) collective-permute-start(bf16[4,4096]{1,0:T(4,128)(2,1)S(1)} %get-tuple-element.27), channel_id=1, source_target_pairs={{0,8},{1,9},{2,10},{3,11},{4,12},{5,13},{6,14},{7,15},{8,0},{9,1},... | collective-permute-start | bytes 98312 | tf_op jit(solution)/shard_map/ppermute | solution.py:175
  26.0 3.3 %collective-permute-start.11 = (bf16[4,4096]{1,0:T(4,128)(2,1)S(1)}, bf16[4,4096]{1,0:T(4,128)(2,1)S(1)}, u32[]{:S(2)}, u32[]{:S(2)}) collective-permute-start(bf16[4,4096]{1,0:T(4,128)(2,1)S(1)} %get-tuple-element.28), channel_id=1, source_target_pairs={{0,10},{1,11},{2,8},{3,9},{4,14},{5,15},{6,12},{7,13},{8,2},{9,3},... | collective-permute-start | bytes 98312 | tf_op jit(solution)/shard_map/ppermute | solution.py:175
  29.3 1.0 %collective-permute-start.12 = (bf16[4,4096]{1,0:T(4,128)(2,1)S(1)}, bf16[4,4096]{1,0:T(4,128)(2,1)S(1)}, u32[]{:S(2)}, u32[]{:S(2)}) collective-permute-start(bf16[4,4096]{1,0:T(4,128)(2,1)S(1)} %get-tuple-element.29), channel_id=1, source_target_pairs={{0,4},{1,5},{2,6},{3,7},{4,8},{5,9},{6,10},{7,11},{8,12},{9,13},{1... | collective-permute-start | bytes 98312 | tf_op jit(solution)/shard_map/ppermute | solution.py:175
  30.3 0.1 collective-permute-start.13
  30.4 0.4 %collective-permute-done.10.refs_4_ = bf16[4,4096]{1,0:T(4,128)(2,1)S(1)} collective-permute-done((bf16[4,4096]{1,0:T(4,128)(2,1)S(1)}, bf16[4,4096]{1,0:T(4,128)(2,1)S(1)}, u32[]{:S(2)}, u32[]{:S(2)}) %collective-permute-start.10) | collective-permute-done | bytes 32800 | tf_op jit(solution)/shard_map/ppermute | solution.py:175
  30.9 1.5 %collective-permute-done.11.refs_5_ = bf16[4,4096]{1,0:T(4,128)(2,1)S(1)} collective-permute-done((bf16[4,4096]{1,0:T(4,128)(2,1)S(1)}, bf16[4,4096]{1,0:T(4,128)(2,1)S(1)}, u32[]{:S(2)}, u32[]{:S(2)}) %collective-permute-start.11) | collective-permute-done | bytes 32800 | tf_op jit(solution)/shard_map/ppermute | solution.py:175
  32.3 2.7 %collective-permute-done.12.refs_6_ = bf16[4,4096]{1,0:T(4,128)(2,1)S(1)} collective-permute-done((bf16[4,4096]{1,0:T(4,128)(2,1)S(1)}, bf16[4,4096]{1,0:T(4,128)(2,1)S(1)}, u32[]{:S(2)}, u32[]{:S(2)}) %collective-permute-start.12) | collective-permute-done | bytes 32800 | tf_op jit(solution)/shard_map/ppermute | solution.py:175
  35.0 1.9 %collective-permute-done.13.refs_7_ = bf16[4,4096]{1,0:T(4,128)(2,1)S(1)} collective-permute-done((bf16[4,4096]{1,0:T(4,128)(2,1)S(1)}, bf16[4,4096]{1,0:T(4,128)(2,1)S(1)}, u32[]{:S(2)}, u32[]{:S(2)}) %collective-permute-start.13) | collective-permute-done | bytes 32800 | tf_op jit(solution)/shard_map/ppermute | solution.py:175
  36.9 0.7 %mix.1 = bf16[4,4096]{1,0:T(4,128)(2,1)} custom-call(s32[2,16]{1,0:T(2,128)S(1)} %bitcast.2, f32[2,4]{1,0:T(2,128)S(1)} %bitcast.3, bf16[4,4096]{1,0:T(4,128)(2,1)S(1)} %get-tuple-element.23.refs_0_, bf16[4,4096]{1,0:T(4,128)(2,1)S(1)} %collective-permute-done.7.refs_1_, bf16[4,4096]{1,0:T(4,128)(2,1)S(1)} %collective-permute-done.8.refs_2_, ...), custom_call_target="tpu_custom_call" | custom-call | tf_op jit(solution)/shard_map/mix/pallas_call | solution.py:177
  (15 shorter events, 0.0 us)
Async XLA Ops:
  0.8 15.9 %copy-start = (bf16[16,4096]{1,0:T(8,128)(2,1)S(1)}, bf16[16,4096]{1,0:T(8,128)(2,1)}, u32[]{:S(2)}) copy-start(bf16[16,4096]{1,0:T(8,128)(2,1)} %own.1) | copy-start | bytes 393220
  0.8 7.5 %collective-permute-start.2 = (bf16[16,2048]{1,0:T(8,128)(2,1)S(1)}, bf16[16,2048]{1,0:T(8,128)(2,1)S(1)}, u32[]{:S(2)}, u32[]{:S(2)}) collective-permute-start(bf16[16,2048]{1,0:T(8,128)(2,1)S(1)} %constant_dynamic-slice_fusion), channel_id=1, source_target_pairs={{0,12},{4,0},{8,4},{12,8},{1,13},{5,1},{9,5},{13,9},{2,14},{6,2},{... | collective-permute-start | bytes 196616 | tf_op jit(solution)/shard_map/ppermute | solution.py:123
  5.9 6.5 %collective-permute-start.1 = (bf16[16,2048]{1,0:T(8,128)(2,1)S(1)}, bf16[16,2048]{1,0:T(8,128)(2,1)S(1)}, u32[]{:S(2)}, u32[]{:S(2)}) collective-permute-start(bf16[16,2048]{1,0:T(8,128)(2,1)S(1)} %constant_dynamic-slice_fusion), channel_id=1, source_target_pairs={{0,8},{4,12},{8,0},{12,4},{1,9},{5,13},{9,1},{13,5},{2,10},{6,14},... | collective-permute-start | bytes 196616 | tf_op jit(solution)/shard_map/ppermute | solution.py:123
  5.9 6.5 %collective-permute-start = (bf16[16,2048]{1,0:T(8,128)(2,1)S(1)}, bf16[16,2048]{1,0:T(8,128)(2,1)S(1)}, u32[]{:S(2)}, u32[]{:S(2)}) collective-permute-start(bf16[16,2048]{1,0:T(8,128)(2,1)S(1)} %constant_dynamic-slice_fusion), channel_id=1, source_target_pairs={{0,4},{4,8},{8,12},{12,0},{1,5},{5,9},{9,13},{13,1},{2,6},{6,10},{... | collective-permute-start | bytes 196616 | tf_op jit(solution)/shard_map/ppermute | solution.py:123
  8.4 8.3 %collective-permute-start.5 = (bf16[16,2048]{1,0:T(8,128)(2,1)S(1)}, bf16[16,2048]{1,0:T(8,128)(2,1)S(1)}, u32[]{:S(2)}, u32[]{:S(2)}) collective-permute-start(bf16[16,2048]{1,0:T(8,128)(2,1)S(1)} %collective-permute-done.2.refs_2_), channel_id=1, source_target_pairs={{0,1},{1,0},{2,3},{3,2},{4,5},{5,4},{6,7},{7,6},{8,9},{9,8},{10,11... | collective-permute-start | bytes 196616 | tf_op jit(solution)/shard_map/ppermute | solution.py:125
  12.4 4.3 %collective-permute-start.4 = (bf16[16,2048]{1,0:T(8,128)(2,1)S(1)}, bf16[16,2048]{1,0:T(8,128)(2,1)S(1)}, u32[]{:S(2)}, u32[]{:S(2)}) collective-permute-start(bf16[16,2048]{1,0:T(8,128)(2,1)S(1)} %collective-permute-done.1.refs_1_), channel_id=1, source_target_pairs={{0,1},{1,0},{2,3},{3,2},{4,5},{5,4},{6,7},{7,6},{8,9},{9,8},{10,11... | collective-permute-start | bytes 196616 | tf_op jit(solution)/shard_map/ppermute | solution.py:125
  12.4 4.3 %collective-permute-start.3 = (bf16[16,2048]{1,0:T(8,128)(2,1)S(1)}, bf16[16,2048]{1,0:T(8,128)(2,1)S(1)}, u32[]{:S(2)}, u32[]{:S(2)}) collective-permute-start(bf16[16,2048]{1,0:T(8,128)(2,1)S(1)} %collective-permute-done.refs_0_), channel_id=1, source_target_pairs={{0,1},{1,0},{2,3},{3,2},{4,5},{5,4},{6,7},{7,6},{8,9},{9,8},{10,11... | collective-permute-start | bytes 196616 | tf_op jit(solution)/shard_map/ppermute | solution.py:125
  16.7 20.2 %copy-start.1 = (s32[16,2]{0,1:T(2,128)S(1)}, s32[16,2]{0,1:T(2,128)}, u32[]{:S(2)}) copy-start(s32[16,2]{0,1:T(2,128)} %param.7) | copy-start | bytes 388
  16.7 20.2 %copy-start.2 = (f32[4,2]{0,1:T(2,128)S(1)}, f32[4,2]{0,1:T(2,128)}, u32[]{:S(2)}) copy-start(f32[4,2]{0,1:T(2,128)} %param.8) | copy-start | bytes 100
  19.3 1.6 %collective-permute-start.6 = (bf16[32,4096]{1,0:T(8,128)(2,1)S(1)}, bf16[32,4096]{1,0:T(8,128)(2,1)S(1)}, u32[]{:S(2)}, u32[]{:S(2)}) collective-permute-start(bf16[32,4096]{1,0:T(8,128)(2,1)S(1)} %get-tuple-element.22), channel_id=1, source_target_pairs={{0,1},{1,0},{2,3},{3,2},{4,5},{5,4},{6,7},{7,6},{8,9},{9,8},{10,11... | collective-permute-start | bytes 786440 | tf_op jit(solution)/shard_map/ppermute | solution.py:156
  21.0 8.3 %collective-permute-start.7 = (bf16[4,4096]{1,0:T(4,128)(2,1)S(1)}, bf16[4,4096]{1,0:T(4,128)(2,1)S(1)}, u32[]{:S(2)}, u32[]{:S(2)}) collective-permute-start(bf16[4,4096]{1,0:T(4,128)(2,1)S(1)} %get-tuple-element.24), channel_id=1, source_target_pairs={{0,2},{1,3},{2,0},{3,1},{4,6},{5,7},{6,4},{7,5},{8,10},{9,11},{10,... | collective-permute-start | bytes 98312 | tf_op jit(solution)/shard_map/ppermute | solution.py:175
  22.6 7.7 %collective-permute-start.8 = (bf16[4,4096]{1,0:T(4,128)(2,1)S(1)}, bf16[4,4096]{1,0:T(4,128)(2,1)S(1)}, u32[]{:S(2)}, u32[]{:S(2)}) collective-permute-start(bf16[4,4096]{1,0:T(4,128)(2,1)S(1)} %get-tuple-element.25), channel_id=1, source_target_pairs={{0,12},{1,13},{2,14},{3,15},{4,0},{5,1},{6,2},{7,3},{8,4},{9,5},{1... | collective-permute-start | bytes 98312 | tf_op jit(solution)/shard_map/ppermute | solution.py:175
  24.5 6.0 %collective-permute-start.9 = (bf16[4,4096]{1,0:T(4,128)(2,1)S(1)}, bf16[4,4096]{1,0:T(4,128)(2,1)S(1)}, u32[]{:S(2)}, u32[]{:S(2)}) collective-permute-start(bf16[4,4096]{1,0:T(4,128)(2,1)S(1)} %get-tuple-element.26), channel_id=1, source_target_pairs={{0,14},{1,15},{2,12},{3,13},{4,2},{5,3},{6,0},{7,1},{8,6},{9,7},{1... | collective-permute-start | bytes 98312 | tf_op jit(solution)/shard_map/ppermute | solution.py:175
  25.4 5.5 %collective-permute-start.10 = (bf16[4,4096]{1,0:T(4,128)(2,1)S(1)}, bf16[4,4096]{1,0:T(4,128)(2,1)S(1)}, u32[]{:S(2)}, u32[]{:S(2)}) collective-permute-start(bf16[4,4096]{1,0:T(4,128)(2,1)S(1)} %get-tuple-element.27), channel_id=1, source_target_pairs={{0,8},{1,9},{2,10},{3,11},{4,12},{5,13},{6,14},{7,15},{8,0},{9,1},... | collective-permute-start | bytes 98312 | tf_op jit(solution)/shard_map/ppermute | solution.py:175
  26.0 6.3 %collective-permute-start.11 = (bf16[4,4096]{1,0:T(4,128)(2,1)S(1)}, bf16[4,4096]{1,0:T(4,128)(2,1)S(1)}, u32[]{:S(2)}, u32[]{:S(2)}) collective-permute-start(bf16[4,4096]{1,0:T(4,128)(2,1)S(1)} %get-tuple-element.28), channel_id=1, source_target_pairs={{0,10},{1,11},{2,8},{3,9},{4,14},{5,15},{6,12},{7,13},{8,2},{9,3},... | collective-permute-start | bytes 98312 | tf_op jit(solution)/shard_map/ppermute | solution.py:175
  29.3 5.7 %collective-permute-start.12 = (bf16[4,4096]{1,0:T(4,128)(2,1)S(1)}, bf16[4,4096]{1,0:T(4,128)(2,1)S(1)}, u32[]{:S(2)}, u32[]{:S(2)}) collective-permute-start(bf16[4,4096]{1,0:T(4,128)(2,1)S(1)} %get-tuple-element.29), channel_id=1, source_target_pairs={{0,4},{1,5},{2,6},{3,7},{4,8},{5,9},{6,10},{7,11},{8,12},{9,13},{1... | collective-permute-start | bytes 98312 | tf_op jit(solution)/shard_map/ppermute | solution.py:175
  30.3 6.6 %collective-permute-start.13 = (bf16[4,4096]{1,0:T(4,128)(2,1)S(1)}, bf16[4,4096]{1,0:T(4,128)(2,1)S(1)}, u32[]{:S(2)}, u32[]{:S(2)}) collective-permute-start(bf16[4,4096]{1,0:T(4,128)(2,1)S(1)} %get-tuple-element.30), channel_id=1, source_target_pairs={{0,6},{1,7},{2,4},{3,5},{4,10},{5,11},{6,8},{7,9},{8,14},{9,15},{1... | collective-permute-start | bytes 98312 | tf_op jit(solution)/shard_map/ppermute | solution.py:175

commit v4 on v3

--- a/solution.py
+++ b/solution.py
@@ -18,8 +18,8 @@
     place = lax.broadcasted_iota(jnp.int32, (total, total), 0)
     source = lax.broadcasted_iota(jnp.int32, (total, total), 1)
     row = lax.rem(place, rows)
-    h = lax.rem(lax.div(place, rows), pairs)
-    k = lax.rem(lax.div(place, rows * pairs), n_expert)
+    k = lax.rem(lax.div(place, rows), n_expert)
+    h = lax.rem(lax.div(place, rows * n_expert), pairs)
     sent = lax.div(place, rows * pairs * n_expert)
     block = 2 * lax.rem(pair + h, pairs) + lax.rem(core + sent, 2)
     wanted = (k * pairs * 2 + block) * rows + row
@@ -72,13 +72,25 @@
         sent[:, cols] = out[side:].astype(jnp.bfloat16)
 
 
-def add_kernel(rows, kept, arrived, *pieces):
+def add_kernel(kept, arrived, own, *pieces):
+    span = own.shape[0]
+    own[...] = kept[:span, :] + arrived[:span, :].astype(jnp.float32)
     for i, piece in enumerate(pieces):
-        span = slice(i * rows, (i + 1) * rows)
-        piece[...] = (kept[span, :] + arrived[span, :].astype(jnp.float32)).astype(jnp.bfloat16)
-
-
-def mix_kernel(n_expert, pairs, ids, weights, *refs):
+        at = slice((i + 1) * span, (i + 2) * span)
+        piece[...] = (kept[at, :] + arrived[at, :].astype(jnp.float32)).astype(jnp.bfloat16)
+
+
+def fold_kernel(pairs, own, *refs):
+    arrived, pieces = refs[: pairs - 1], refs[pairs - 1 :]
+    total = own[...]
+    for block in arrived:
+        total = total + block[...].astype(jnp.float32)
+    rows = pieces[0].shape[0]
+    for k, piece in enumerate(pieces):
+        piece[...] = total[k * rows : (k + 1) * rows].astype(piece.dtype)
+
+
+def mix_kernel(n_expert, ids, weights, *refs):
     pieces, out = refs[:-1], refs[-1]
     rows = out.shape[0]
     me, expert = lax.axis_index("etp"), lax.axis_index("expert")
@@ -97,11 +109,7 @@
     for k in range(n_expert):
         owner = lax.rem(expert + k, n_expert)
         factor = sum(jnp.where(own_ids[i] == owner, own_weights[i], 0.0) for i in range(top)) / scale
-        summed = None
-        for h in range(pairs):
-            piece = pieces[k * pairs + h][...].astype(jnp.float32)
-            summed = piece if summed is None else summed + piece
-        term = summed * factor
+        term = pieces[k][...].astype(jnp.float32) * factor
         total = term if total is None else total + term
     out[...] = total.astype(out.dtype)
 
@@ -154,30 +162,38 @@
     )(tokens, *near, *far, *weights)
 
     arrived = lax.ppermute(sent, "etp", swap)
-    count = n_expert * pairs
-    pieces = pl.pallas_call(
-        functools.partial(add_kernel, rows),
-        out_shape=[jax.ShapeDtypeStruct((rows, width), jnp.bfloat16)] * count,
+    block = n_expert * rows
+    own, *pieces = pl.pallas_call(
+        add_kernel,
+        out_shape=[jax.ShapeDtypeStruct((block, width), jnp.float32)]
+        + [jax.ShapeDtypeStruct((block, width), jnp.bfloat16)] * (pairs - 1),
         in_specs=[VMEM] * 2,
-        out_specs=[VMEM] * count,
+        out_specs=[VMEM] * pairs,
         compiler_params=GRANT,
         name="add",
     )(kept, arrived)
-
     landed = []
-    for i, piece in enumerate(pieces):
-        k, h = divmod(i, pairs)
-        route = []
-        for e in range(n_expert):
-            for t in range(n_etp):
-                to_e, to_t = (e - k) % n_expert, 2 * ((t // 2 + h) % pairs) + t % 2
-                route.append((e * n_etp + t, to_e * n_etp + to_t))
-        landed.append(lax.ppermute(piece, ("expert", "etp"), route) if i else piece)
+    for h, piece in enumerate(pieces, 1):
+        route = [(t, 2 * ((t // 2 + h) % pairs) + t % 2) for t in range(n_etp)]
+        landed.append(lax.ppermute(piece, "etp", route))
+    own, *pieces = pl.pallas_call(
+        functools.partial(fold_kernel, pairs),
+        out_shape=[jax.ShapeDtypeStruct((rows, width), jnp.float32)]
+        + [jax.ShapeDtypeStruct((rows, width), jnp.bfloat16)] * (n_expert - 1),
+        in_specs=[VMEM] * pairs,
+        out_specs=[VMEM] * n_expert,
+        compiler_params=GRANT,
+        name="fold",
+    )(own, *landed)
+    landed = [own]
+    for k, piece in enumerate(pieces, 1):
+        route = [(e, (e - k) % n_expert) for e in range(n_expert)]
+        landed.append(lax.ppermute(piece, "expert", route))
 
     return pl.pallas_call(
-        functools.partial(mix_kernel, n_expert, pairs),
+        functools.partial(mix_kernel, n_expert),
         out_shape=jax.ShapeDtypeStruct((rows, width), jnp.bfloat16),
-        in_specs=[VMEM] * (2 + count),
+        in_specs=[VMEM] * (2 + n_expert),
         out_specs=VMEM,
         compiler_params=GRANT,
         name="mix",

time: 37.8 us -> 35.2 us (0.931)
  starting transfers between devices: 16.1 us -> 11.9 us
  waiting for transfers between devices: 13.5 us -> 15 us
    ppermute x7 -> x4, starting transfers between devices: 9.4 us -> 5.27 us  [the longest x3 3.72 us: on_device(): landed.append(lax.ppermute(piece, 'expert', route))]
    ppermute x7 -> x4, waiting for transfers between devices: 6.51 us -> 8 us  [the longest x1 4.05 us: on_device(): landed.append(lax.ppermute(piece, 'etp', route))]
    pallas_call x2 -> x3, Pallas kernels: 0.86 us -> 0.83 us  [the longest x1 0.74 us: on_device(): pl.pallas_call(functools.partial(mix_kernel, n_expert), out_shape=jax.Sha...]
  transfers between devices with their start and end apart: 14 -> 11, of which waited for: 7 -> 7; matrix products, arithmetic and copies ran while one was open for 0% -> 0% of each run, Pallas kernels for 10% -> 11%
where the time goes in v4:
time: 35.2 us; the launch traced here: 35 us
  waiting for transfers between devices  15 us (43%)
  starting transfers between devices  11.9 us (34%)
  Pallas kernels  7.17 us (20%)
  local copies, waits for them, and re-layouts  0.86 us (2%)
    ppermute x3, starting transfers between devices, on_device(): near.append(lax.ppermute(own_half, 'expert', hop))  6.06 us
    ppermute x3, waiting for transfers between devices, on_device(): near.append(lax.ppermute(own_half, 'expert', hop))  5.45 us
    ppermute x1, waiting for transfers between devices, on_device(): landed.append(lax.ppermute(piece, 'etp', route))  4.05 us
    ppermute x3, waiting for transfers between devices, on_device(): landed.append(lax.ppermute(piece, 'expert', route))  3.95 us
    pallas_call x1, Pallas kernels, on_device(): pl.pallas_call(functools.partial(load_kernel, len(weights), parts), out_s...  3.79 us
    ppermute x3, starting transfers between devices, on_device(): landed.append(lax.ppermute(piece, 'expert', route))  3.72 us
    pallas_call x1, Pallas kernels, on_device(): pl.pallas_call(functools.partial(ffn_kernel, n_expert, n_etp, rows, parts...  2.55 us
    ppermute x1, starting transfers between devices, on_device(): landed.append(lax.ppermute(piece, 'etp', route))  1.55 us
  transfers between devices with their start and end apart: 11, of which 7 were waited for; matrix products, arithmetic and copies ran while one was open for 0% of the time, Pallas kernels for 11%

profile of v4, /device:TPU:0, one launch (start us, length us, event | category | flops | bytes accessed | tf_op | source)
XLA Modules:
  0.0 35.0 jit_solution(4534022205804764003)
XLA Ops:
  0.0 0.8 %constant_dynamic-slice_fusion = bf16[16,2048]{1,0:T(8,128)(2,1)S(1)} fusion(bf16[16,4096]{1,0:T(8,128)(2,1)} %own.1, s32[]{:T(128)S(6)} %select_n.3), kind=kLoop, calls=%fused_computation | loop fusion | bytes 131076 | tf_op jit(solution)/shard_map/dynamic_slice | solution.py:126
  0.8 5.0 %collective-permute-start.2 = (bf16[16,2048]{1,0:T(8,128)(2,1)S(1)}, bf16[16,2048]{1,0:T(8,128)(2,1)S(1)}, u32[]{:S(2)}, u32[]{:S(2)}) collective-permute-start(bf16[16,2048]{1,0:T(8,128)(2,1)S(1)} %constant_dynamic-slice_fusion), channel_id=1, source_target_pairs={{0,12},{4,0},{8,4},{12,8},{1,13},{5,1},{9,5},{13,9},{2,14},{6,2},{... | collective-permute-start | bytes 196616 | tf_op jit(solution)/shard_map/ppermute | solution.py:131
  5.9 1.0 %collective-permute-start = (bf16[16,2048]{1,0:T(8,128)(2,1)S(1)}, bf16[16,2048]{1,0:T(8,128)(2,1)S(1)}, u32[]{:S(2)}, u32[]{:S(2)}) collective-permute-start(bf16[16,2048]{1,0:T(8,128)(2,1)S(1)} %constant_dynamic-slice_fusion), channel_id=1, source_target_pairs={{0,4},{4,8},{8,12},{12,0},{1,5},{5,9},{9,13},{13,1},{2,6},{6,10},{... | collective-permute-start | bytes 196616 | tf_op jit(solution)/shard_map/ppermute | solution.py:131
  6.9 1.5 %collective-permute-done.2.refs_2_ = bf16[16,2048]{1,0:T(8,128)(2,1)S(1)} collective-permute-done((bf16[16,2048]{1,0:T(8,128)(2,1)S(1)}, bf16[16,2048]{1,0:T(8,128)(2,1)S(1)}, u32[]{:S(2)}, u32[]{:S(2)}) %collective-permute-start.2) | collective-permute-done | bytes 65568 | tf_op jit(solution)/shard_map/ppermute | solution.py:131
  8.4 0.0 collective-permute-start.5
  8.4 4.0 %collective-permute-done.1.refs_1_ = bf16[16,2048]{1,0:T(8,128)(2,1)S(1)} collective-permute-done((bf16[16,2048]{1,0:T(8,128)(2,1)S(1)}, bf16[16,2048]{1,0:T(8,128)(2,1)S(1)}, u32[]{:S(2)}, u32[]{:S(2)}) %collective-permute-start.1) | collective-permute-done | bytes 65568 | tf_op jit(solution)/shard_map/ppermute | solution.py:131
  12.4 0.0 collective-permute-start.4
  12.4 0.0 collective-permute-done.refs_0_
  12.4 0.5 %collective-permute-start.3 = (bf16[16,2048]{1,0:T(8,128)(2,1)S(1)}, bf16[16,2048]{1,0:T(8,128)(2,1)S(1)}, u32[]{:S(2)}, u32[]{:S(2)}) collective-permute-start(bf16[16,2048]{1,0:T(8,128)(2,1)S(1)} %collective-permute-done.refs_0_), channel_id=1, source_target_pairs={{0,1},{1,0},{2,3},{3,2},{4,5},{5,4},{6,7},{7,6},{8,9},{9,8},{10,11... | collective-permute-start | bytes 196616 | tf_op jit(solution)/shard_map/ppermute | solution.py:133
  12.9 3.8 %load.1 = (bf16[1,384,4096]{2,1,0:T(8,128)(2,1)S(1)}, bf16[1,384,4096]{2,1,0:T(8,128)(2,1)S(1)}, bf16[1,384,4096]{2,1,0:T(8,128)(2,1)S(1)}) custom-call(bf16[1,384,4096]{2,1,0:T(8,128)(2,1)} %refs_0_.1, bf16[1,384,4096]{2,1,0:T(8,128)(2,1)} %refs_1_.1, bf16[1,384,4096]{2,1,0:T(8,128)(2,1)} %refs_2_.1), custom_call_target="tpu_custom_call" | custom-call | bytes 18874368 | tf_op jit(solution)/shard_map/load/pallas_call | solution.py:138
  16.7 0.0 collective-permute-done.5.refs_5_
  16.7 0.0 copy-start.1
  16.7 0.0 copy-start.2
  16.7 2.5 %ffn.1 = (f32[32,4096]{1,0:T(8,128)S(1)}, bf16[32,4096]{1,0:T(8,128)(2,1)S(1)}) custom-call(bf16[16,4096]{1,0:T(8,128)(2,1)S(1)} %copy-done, bf16[16,2048]{1,0:T(8,128)(2,1)S(1)} %collective-permute-done.refs_0_, bf16[16,2048]{1,0:T(8,128)(2,1)S(1)} %collective-permute-done.1.refs_1_, bf16[16,2048]{1,0:T(8,128)(2,1)S(1)} %collective-permute-done.2.refs_2_, ...), custom_call_target="tpu_custom_call" | custom-call | tf_op jit(solution)/shard_map/ffn/pallas_call | solution.py:149
  19.3 0.1 collective-permute-start.6
  19.4 1.5 %collective-permute-done.6.arrived = bf16[32,4096]{1,0:T(8,128)(2,1)S(1)} collective-permute-done((bf16[32,4096]{1,0:T(8,128)(2,1)S(1)}, bf16[32,4096]{1,0:T(8,128)(2,1)S(1)}, u32[]{:S(2)}, u32[]{:S(2)}) %collective-permute-start.6) | collective-permute-done | bytes 262176 | tf_op jit(solution)/shard_map/ppermute | solution.py:164
  21.0 1.6 %collective-permute-start.7 = (bf16[16,4096]{1,0:T(8,128)(2,1)S(1)}, bf16[16,4096]{1,0:T(8,128)(2,1)S(1)}, u32[]{:S(2)}, u32[]{:S(2)}) collective-permute-start(bf16[16,4096]{1,0:T(8,128)(2,1)S(1)} %get-tuple-element.22), channel_id=1, source_target_pairs={{0,2},{1,3},{2,0},{3,1},{4,6},{5,7},{6,4},{7,5},{8,10},{9,11},{10,... | collective-permute-start | bytes 393224 | tf_op jit(solution)/shard_map/ppermute | solution.py:178
  22.5 4.0 %collective-permute-done.7.refs_0_ = bf16[16,4096]{1,0:T(8,128)(2,1)S(1)} collective-permute-done((bf16[16,4096]{1,0:T(8,128)(2,1)S(1)}, bf16[16,4096]{1,0:T(8,128)(2,1)S(1)}, u32[]{:S(2)}, u32[]{:S(2)}) %collective-permute-start.7) | collective-permute-done | bytes 131104 | tf_op jit(solution)/shard_map/ppermute | solution.py:178
  26.6 1.9 %collective-permute-start.8 = (bf16[4,4096]{1,0:T(4,128)(2,1)S(1)}, bf16[4,4096]{1,0:T(4,128)(2,1)S(1)}, u32[]{:S(2)}, u32[]{:S(2)}) collective-permute-start(bf16[4,4096]{1,0:T(4,128)(2,1)S(1)} %get-tuple-element.24), channel_id=1, source_target_pairs={{0,12},{4,0},{8,4},{12,8},{1,13},{5,1},{9,5},{13,9},{2,14},{6,2},{... | collective-permute-start | bytes 98312 | tf_op jit(solution)/shard_map/ppermute | solution.py:191
  28.5 1.8 %collective-permute-start.10 = (bf16[4,4096]{1,0:T(4,128)(2,1)S(1)}, bf16[4,4096]{1,0:T(4,128)(2,1)S(1)}, u32[]{:S(2)}, u32[]{:S(2)}) collective-permute-start(bf16[4,4096]{1,0:T(4,128)(2,1)S(1)} %get-tuple-element.26), channel_id=1, source_target_pairs={{0,4},{4,8},{8,12},{12,0},{1,5},{5,9},{9,13},{13,1},{2,6},{6,10},{... | collective-permute-start | bytes 98312 | tf_op jit(solution)/shard_map/ppermute | solution.py:191
  30.3 0.2 collective-permute-done.8.refs_1_
  30.6 2.8 %collective-permute-done.9.refs_2_ = bf16[4,4096]{1,0:T(4,128)(2,1)S(1)} collective-permute-done((bf16[4,4096]{1,0:T(4,128)(2,1)S(1)}, bf16[4,4096]{1,0:T(4,128)(2,1)S(1)}, u32[]{:S(2)}, u32[]{:S(2)}) %collective-permute-start.9) | collective-permute-done | bytes 32800 | tf_op jit(solution)/shard_map/ppermute | solution.py:191
  33.4 0.9 %collective-permute-done.10.refs_3_ = bf16[4,4096]{1,0:T(4,128)(2,1)S(1)} collective-permute-done((bf16[4,4096]{1,0:T(4,128)(2,1)S(1)}, bf16[4,4096]{1,0:T(4,128)(2,1)S(1)}, u32[]{:S(2)}, u32[]{:S(2)}) %collective-permute-start.10) | collective-permute-done | bytes 32800 | tf_op jit(solution)/shard_map/ppermute | solution.py:191
  34.3 0.7 %mix.1 = bf16[4,4096]{1,0:T(4,128)(2,1)} custom-call(s32[2,16]{1,0:T(2,128)S(1)} %bitcast.2, f32[2,4]{1,0:T(2,128)S(1)} %bitcast.3, f32[4,4096]{1,0:T(4,128)S(1)} %get-tuple-element.23.refs_0_, bf16[4,4096]{1,0:T(4,128)(2,1)S(1)} %collective-permute-done.8.refs_1_, bf16[4,4096]{1,0:T(4,128)(2,1)S(1)} %collective-permute-done.9.refs_2_, ...), custom_call_target="tpu_custom_call" | custom-call | tf_op jit(solution)/shard_map/mix/pallas_call | solution.py:193
  (10 shorter events, 0.1 us)
Async XLA Ops:
  0.8 15.9 %copy-start = (bf16[16,4096]{1,0:T(8,128)(2,1)S(1)}, bf16[16,4096]{1,0:T(8,128)(2,1)}, u32[]{:S(2)}) copy-start(bf16[16,4096]{1,0:T(8,128)(2,1)} %own.1) | copy-start | bytes 393220
  0.8 7.5 %collective-permute-start.2 = (bf16[16,2048]{1,0:T(8,128)(2,1)S(1)}, bf16[16,2048]{1,0:T(8,128)(2,1)S(1)}, u32[]{:S(2)}, u32[]{:S(2)}) collective-permute-start(bf16[16,2048]{1,0:T(8,128)(2,1)S(1)} %constant_dynamic-slice_fusion), channel_id=1, source_target_pairs={{0,12},{4,0},{8,4},{12,8},{1,13},{5,1},{9,5},{13,9},{2,14},{6,2},{... | collective-permute-start | bytes 196616 | tf_op jit(solution)/shard_map/ppermute | solution.py:131
  5.9 6.5 %collective-permute-start.1 = (bf16[16,2048]{1,0:T(8,128)(2,1)S(1)}, bf16[16,2048]{1,0:T(8,128)(2,1)S(1)}, u32[]{:S(2)}, u32[]{:S(2)}) collective-permute-start(bf16[16,2048]{1,0:T(8,128)(2,1)S(1)} %constant_dynamic-slice_fusion), channel_id=1, source_target_pairs={{0,8},{4,12},{8,0},{12,4},{1,9},{5,13},{9,1},{13,5},{2,10},{6,14},... | collective-permute-start | bytes 196616 | tf_op jit(solution)/shard_map/ppermute | solution.py:131
  5.9 6.5 %collective-permute-start = (bf16[16,2048]{1,0:T(8,128)(2,1)S(1)}, bf16[16,2048]{1,0:T(8,128)(2,1)S(1)}, u32[]{:S(2)}, u32[]{:S(2)}) collective-permute-start(bf16[16,2048]{1,0:T(8,128)(2,1)S(1)} %constant_dynamic-slice_fusion), channel_id=1, source_target_pairs={{0,4},{4,8},{8,12},{12,0},{1,5},{5,9},{9,13},{13,1},{2,6},{6,10},{... | collective-permute-start | bytes 196616 | tf_op jit(solution)/shard_map/ppermute | solution.py:131
  8.4 8.3 %collective-permute-start.5 = (bf16[16,2048]{1,0:T(8,128)(2,1)S(1)}, bf16[16,2048]{1,0:T(8,128)(2,1)S(1)}, u32[]{:S(2)}, u32[]{:S(2)}) collective-permute-start(bf16[16,2048]{1,0:T(8,128)(2,1)S(1)} %collective-permute-done.2.refs_2_), channel_id=1, source_target_pairs={{0,1},{1,0},{2,3},{3,2},{4,5},{5,4},{6,7},{7,6},{8,9},{9,8},{10,11... | collective-permute-start | bytes 196616 | tf_op jit(solution)/shard_map/ppermute | solution.py:133
  12.4 4.3 %collective-permute-start.4 = (bf16[16,2048]{1,0:T(8,128)(2,1)S(1)}, bf16[16,2048]{1,0:T(8,128)(2,1)S(1)}, u32[]{:S(2)}, u32[]{:S(2)}) collective-permute-start(bf16[16,2048]{1,0:T(8,128)(2,1)S(1)} %collective-permute-done.1.refs_1_), channel_id=1, source_target_pairs={{0,1},{1,0},{2,3},{3,2},{4,5},{5,4},{6,7},{7,6},{8,9},{9,8},{10,11... | collective-permute-start | bytes 196616 | tf_op jit(solution)/shard_map/ppermute | solution.py:133
  12.4 4.3 %collective-permute-start.3 = (bf16[16,2048]{1,0:T(8,128)(2,1)S(1)}, bf16[16,2048]{1,0:T(8,128)(2,1)S(1)}, u32[]{:S(2)}, u32[]{:S(2)}) collective-permute-start(bf16[16,2048]{1,0:T(8,128)(2,1)S(1)} %collective-permute-done.refs_0_), channel_id=1, source_target_pairs={{0,1},{1,0},{2,3},{3,2},{4,5},{5,4},{6,7},{7,6},{8,9},{9,8},{10,11... | collective-permute-start | bytes 196616 | tf_op jit(solution)/shard_map/ppermute | solution.py:133
  16.7 17.5 %copy-start.1 = (s32[16,2]{0,1:T(2,128)S(1)}, s32[16,2]{0,1:T(2,128)}, u32[]{:S(2)}) copy-start(s32[16,2]{0,1:T(2,128)} %param.7) | copy-start | bytes 388
  16.7 17.5 %copy-start.2 = (f32[4,2]{0,1:T(2,128)S(1)}, f32[4,2]{0,1:T(2,128)}, u32[]{:S(2)}) copy-start(f32[4,2]{0,1:T(2,128)} %param.8) | copy-start | bytes 100
  19.3 1.6 %collective-permute-start.6 = (bf16[32,4096]{1,0:T(8,128)(2,1)S(1)}, bf16[32,4096]{1,0:T(8,128)(2,1)S(1)}, u32[]{:S(2)}, u32[]{:S(2)}) collective-permute-start(bf16[32,4096]{1,0:T(8,128)(2,1)S(1)} %get-tuple-element.20), channel_id=1, source_target_pairs={{0,1},{1,0},{2,3},{3,2},{4,5},{5,4},{6,7},{7,6},{8,9},{9,8},{10,11... | collective-permute-start | bytes 786440 | tf_op jit(solution)/shard_map/ppermute | solution.py:164
  21.0 5.6 %collective-permute-start.7 = (bf16[16,4096]{1,0:T(8,128)(2,1)S(1)}, bf16[16,4096]{1,0:T(8,128)(2,1)S(1)}, u32[]{:S(2)}, u32[]{:S(2)}) collective-permute-start(bf16[16,4096]{1,0:T(8,128)(2,1)S(1)} %get-tuple-element.22), channel_id=1, source_target_pairs={{0,2},{1,3},{2,0},{3,1},{4,6},{5,7},{6,4},{7,5},{8,10},{9,11},{10,... | collective-permute-start | bytes 393224 | tf_op jit(solution)/shard_map/ppermute | solution.py:178
  26.6 4.0 %collective-permute-start.8 = (bf16[4,4096]{1,0:T(4,128)(2,1)S(1)}, bf16[4,4096]{1,0:T(4,128)(2,1)S(1)}, u32[]{:S(2)}, u32[]{:S(2)}) collective-permute-start(bf16[4,4096]{1,0:T(4,128)(2,1)S(1)} %get-tuple-element.24), channel_id=1, source_target_pairs={{0,12},{4,0},{8,4},{12,8},{1,13},{5,1},{9,5},{13,9},{2,14},{6,2},{... | collective-permute-start | bytes 98312 | tf_op jit(solution)/shard_map/ppermute | solution.py:191
  28.5 4.8 %collective-permute-start.9 = (bf16[4,4096]{1,0:T(4,128)(2,1)S(1)}, bf16[4,4096]{1,0:T(4,128)(2,1)S(1)}, u32[]{:S(2)}, u32[]{:S(2)}) collective-permute-start(bf16[4,4096]{1,0:T(4,128)(2,1)S(1)} %get-tuple-element.25), channel_id=1, source_target_pairs={{0,8},{4,12},{8,0},{12,4},{1,9},{5,13},{9,1},{13,5},{2,10},{6,14},... | collective-permute-start | bytes 98312 | tf_op jit(solution)/shard_map/ppermute | solution.py:191
  28.5 5.7 %collective-permute-start.10 = (bf16[4,4096]{1,0:T(4,128)(2,1)S(1)}, bf16[4,4096]{1,0:T(4,128)(2,1)S(1)}, u32[]{:S(2)}, u32[]{:S(2)}) collective-permute-start(bf16[4,4096]{1,0:T(4,128)(2,1)S(1)} %get-tuple-element.26), channel_id=1, source_target_pairs={{0,4},{4,8},{8,12},{12,0},{1,5},{5,9},{9,13},{13,1},{2,6},{6,10},{... | collective-permute-start | bytes 98312 | tf_op jit(solution)/shard_map/ppermute | solution.py:191

commit v5 on v4

--- a/solution.py
+++ b/solution.py
@@ -9,6 +9,7 @@
 
 VMEM = pl.BlockSpec(memory_space=pltpu.VMEM)
 GRANT = pltpu.CompilerParams(vmem_limit_bytes=16 * 1024 * 1024)
+AHEAD = pl.CostEstimate(flops=10**10, bytes_accessed=0, transcendentals=0)
 HBM = pl.BlockSpec(memory_space=pltpu.HBM)
 
 
@@ -26,20 +27,13 @@
     return jnp.where(source == wanted, 1.0, 0.0).astype(jnp.bfloat16)
 
 
-def load_kernel(count, parts, *refs):
-    sources, targets, sems = refs[:count], refs[count : 2 * count], refs[-1]
-    copies = []
-    for i, (source, target) in enumerate(zip(sources, targets)):
-        step = source.shape[1] // parts
-        for c in range(parts):
-            span = pl.ds(c * step, step)
-            copies.append(
-                pltpu.make_async_copy(source.at[:, span], target.at[:, span], sems.at[i, c])
-            )
-    for copy in copies:
-        copy.start()
-    for copy in copies:
-        copy.wait()
+def half_kernel(tokens, out, sem):
+    half = out.shape[1]
+    core = lax.rem(lax.axis_index("etp"), 2)
+    cols = pl.ds(pl.multiple_of(core * half, half), half)
+    copy = pltpu.make_async_copy(tokens.at[:, cols], out, sem)
+    copy.start()
+    copy.wait()
 
 
 def ffn_kernel(n_expert, n_etp, rows, parts, own, *refs):
@@ -120,10 +114,17 @@
     pairs = n_etp // 2
     side = n_expert * tok // 2
     half = width // 2
-    me = lax.axis_index("etp")
-    core = lax.rem(me, 2)
-
-    own_half = lax.dynamic_slice_in_dim(tokens, core * half, half, 1)
+
+    own_half = pl.pallas_call(
+        half_kernel,
+        out_shape=jax.ShapeDtypeStruct((tok, half), tokens.dtype),
+        in_specs=[HBM],
+        out_specs=VMEM,
+        scratch_shapes=[pltpu.SemaphoreType.DMA],
+        cost_estimate=AHEAD,
+        compiler_params=GRANT,
+        name="half",
+    )(pltpu.with_memory_space_constraint(tokens, pltpu.HBM))
     near, far = [], []
     swap = [(i, i ^ 1) for i in range(n_etp)]
     for k in range(1, n_expert):
@@ -133,19 +134,6 @@
         far.append(lax.ppermute(block, "etp", swap))
 
     parts = 4
-    weights = (w_gate, w_up, w_down)
-    size = sum(w.size * 2 for w in weights)
-    weights = pl.pallas_call(
-        functools.partial(load_kernel, len(weights), parts),
-        out_shape=[jax.ShapeDtypeStruct(w.shape, w.dtype) for w in weights],
-        in_specs=[HBM] * len(weights),
-        out_specs=[VMEM] * len(weights),
-        scratch_shapes=[pltpu.SemaphoreType.DMA((len(weights), parts))],
-        cost_estimate=pl.CostEstimate(flops=0, bytes_accessed=2 * size, transcendentals=0),
-        compiler_params=GRANT,
-        name="load",
-    )(*(pltpu.with_memory_space_constraint(w, pltpu.HBM) for w in weights))
-
     kept, sent = pl.pallas_call(
         functools.partial(ffn_kernel, n_expert, n_etp, rows, parts),
         out_shape=(
@@ -159,7 +147,7 @@
         ],
         compiler_params=GRANT,
         name="ffn",
-    )(tokens, *near, *far, *weights)
+    )(tokens, *near, *far, w_gate, w_up, w_down)
 
     arrived = lax.ppermute(sent, "etp", swap)
     block = n_expert * rows

time: 35.2 us -> 32.7 us (0.929)
  Pallas kernels: 7.17 us -> 4.38 us
  waiting for transfers between devices: 15 us -> 16 us
  local copies, waits for them, and re-layouts: 0.86 us -> 0.03 us
    pallas_call x1, Pallas kernels: 3.79 us -> 1 us  [on_device(): pl.pallas_call(half_kernel, out_shape=jax.ShapeDtypeStruct((tok, half), t...]
    ppermute x3, waiting for transfers between devices: 0.01 us -> 0.9 us  [on_device(): far.append(lax.ppermute(block, 'etp', swap))]
    dynamic_slice x1 -> x0, local copies, waits for them, and re-layouts: 0.84 us -> none  [on_device(): own_half = lax.dynamic_slice_in_dim(tokens, core * half, half, 1)]
    ppermute x1, starting transfers between devices: 0.09 us -> 0.45 us  [on_device(): arrived = lax.ppermute(sent, 'etp', swap)]
  transfers between devices with their start and end apart: 11 -> 11, of which waited for: 7 -> 9; matrix products, arithmetic and copies ran while one was open for 0% -> 0% of each run, Pallas kernels for 11% -> 0%
where the time goes in v5:
time: 32.7 us; the launch traced here: 32.6 us
  waiting for transfers between devices  16 us (49%)
  starting transfers between devices  12.1 us (37%)
  Pallas kernels  4.38 us (13%)
    ppermute x3, starting transfers between devices, on_device(): near.append(lax.ppermute(own_half, 'expert', hop))  6.13 us
    ppermute x3, waiting for transfers between devices, on_device(): near.append(lax.ppermute(own_half, 'expert', hop))  5.45 us
    ppermute x1, waiting for transfers between devices, on_device(): landed.append(lax.ppermute(piece, 'etp', route))  4.27 us
    ppermute x3, waiting for transfers between devices, on_device(): landed.append(lax.ppermute(piece, 'expert', route))  4.17 us
    ppermute x3, starting transfers between devices, on_device(): landed.append(lax.ppermute(piece, 'expert', route))  3.48 us
    pallas_call x1, Pallas kernels, on_device(): pl.pallas_call(functools.partial(ffn_kernel, n_expert, n_etp, rows, parts...  2.55 us
    ppermute x1, starting transfers between devices, on_device(): landed.append(lax.ppermute(piece, 'etp', route))  1.57 us
    ppermute x1, waiting for transfers between devices, on_device(): arrived = lax.ppermute(sent, 'etp', swap)  1.16 us
  transfers between devices with their start and end apart: 11, of which 9 were waited for; matrix products, arithmetic and copies ran while one was open for 0% of the time, Pallas kernels for 0%

profile of v5, /device:TPU:0, one launch (start us, length us, event | category | flops | bytes accessed | tf_op | source)
XLA Modules:
  0.0 32.6 jit_solution(577707199138372690)
XLA Ops:
  0.0 1.0 %half.1 = bf16[16,2048]{1,0:T(8,128)(2,1)S(1)} custom-call(bf16[16,4096]{1,0:T(8,128)(2,1)} %own.1), custom_call_target="tpu_custom_call" | custom-call | flops 10000000000 | tf_op jit(solution)/shard_map/half/pallas_call | solution.py:118
  1.0 0.0 copy-start.4
  1.0 0.0 copy-start.5
  1.0 5.1 %collective-permute-start.2 = (bf16[16,2048]{1,0:T(8,128)(2,1)S(1)}, bf16[16,2048]{1,0:T(8,128)(2,1)S(1)}, u32[]{:S(2)}, u32[]{:S(2)}) collective-permute-start(bf16[16,2048]{1,0:T(8,128)(2,1)S(1)} %half.1), channel_id=1, source_target_pairs={{0,12},{4,0},{8,4},{12,8},{1,13},{5,1},{9,5},{13,9},{2,14},{6,2},{... | collective-permute-start | bytes 196616 | tf_op jit(solution)/shard_map/ppermute | solution.py:132
  6.2 1.0 %collective-permute-start = (bf16[16,2048]{1,0:T(8,128)(2,1)S(1)}, bf16[16,2048]{1,0:T(8,128)(2,1)S(1)}, u32[]{:S(2)}, u32[]{:S(2)}) collective-permute-start(bf16[16,2048]{1,0:T(8,128)(2,1)S(1)} %half.1), channel_id=1, source_target_pairs={{0,4},{4,8},{8,12},{12,0},{1,5},{5,9},{9,13},{13,1},{2,6},{6,10},{... | collective-permute-start | bytes 196616 | tf_op jit(solution)/shard_map/ppermute | solution.py:132
  7.2 1.5 %collective-permute-done.2.refs_2_ = bf16[16,2048]{1,0:T(8,128)(2,1)S(1)} collective-permute-done((bf16[16,2048]{1,0:T(8,128)(2,1)S(1)}, bf16[16,2048]{1,0:T(8,128)(2,1)S(1)}, u32[]{:S(2)}, u32[]{:S(2)}) %collective-permute-start.2) | collective-permute-done | bytes 65568 | tf_op jit(solution)/shard_map/ppermute | solution.py:132
  8.7 0.0 collective-permute-start.5
  8.7 4.0 %collective-permute-done.1.refs_1_ = bf16[16,2048]{1,0:T(8,128)(2,1)S(1)} collective-permute-done((bf16[16,2048]{1,0:T(8,128)(2,1)S(1)}, bf16[16,2048]{1,0:T(8,128)(2,1)S(1)}, u32[]{:S(2)}, u32[]{:S(2)}) %collective-permute-start.1) | collective-permute-done | bytes 65568 | tf_op jit(solution)/shard_map/ppermute | solution.py:132
  12.6 0.0 collective-permute-start.4
  12.6 0.0 collective-permute-done.refs_0_
  12.6 0.5 %collective-permute-start.3 = (bf16[16,2048]{1,0:T(8,128)(2,1)S(1)}, bf16[16,2048]{1,0:T(8,128)(2,1)S(1)}, u32[]{:S(2)}, u32[]{:S(2)}) collective-permute-start(bf16[16,2048]{1,0:T(8,128)(2,1)S(1)} %collective-permute-done.refs_0_), channel_id=1, source_target_pairs={{0,1},{1,0},{2,3},{3,2},{4,5},{5,4},{6,7},{7,6},{8,9},{9,8},{10,11... | collective-permute-start | bytes 196616 | tf_op jit(solution)/shard_map/ppermute | solution.py:134
  13.2 0.7 %collective-permute-done.4.refs_4_ = bf16[16,2048]{1,0:T(8,128)(2,1)S(1)} collective-permute-done((bf16[16,2048]{1,0:T(8,128)(2,1)S(1)}, bf16[16,2048]{1,0:T(8,128)(2,1)S(1)}, u32[]{:S(2)}, u32[]{:S(2)}) %collective-permute-start.4) | collective-permute-done | bytes 65568 | tf_op jit(solution)/shard_map/ppermute | solution.py:134
  13.9 0.2 collective-permute-done.3.refs_3_
  14.1 2.5 %ffn.1 = (f32[32,4096]{1,0:T(8,128)S(1)}, bf16[32,4096]{1,0:T(8,128)(2,1)S(1)}) custom-call(bf16[16,4096]{1,0:T(8,128)(2,1)S(1)} %copy-done.3, bf16[16,2048]{1,0:T(8,128)(2,1)S(1)} %collective-permute-done.refs_0_, bf16[16,2048]{1,0:T(8,128)(2,1)S(1)} %collective-permute-done.1.refs_1_, bf16[16,2048]{1,0:T(8,128)(2,1)S(1)} %collective-permute-done.2.refs_2_, ...), custom_call_target="tpu_custom_call" | custom-call | tf_op jit(solution)/shard_map/ffn/pallas_call | solution.py:137
  16.6 0.4 %collective-permute-start.6 = (bf16[32,4096]{1,0:T(8,128)(2,1)S(1)}, bf16[32,4096]{1,0:T(8,128)(2,1)S(1)}, u32[]{:S(2)}, u32[]{:S(2)}) collective-permute-start(bf16[32,4096]{1,0:T(8,128)(2,1)S(1)} %get-tuple-element.14), channel_id=1, source_target_pairs={{0,1},{1,0},{2,3},{3,2},{4,5},{5,4},{6,7},{7,6},{8,9},{9,8},{10,11... | collective-permute-start | bytes 786440 | tf_op jit(solution)/shard_map/ppermute | solution.py:152
  17.1 1.2 %collective-permute-done.6.arrived = bf16[32,4096]{1,0:T(8,128)(2,1)S(1)} collective-permute-done((bf16[32,4096]{1,0:T(8,128)(2,1)S(1)}, bf16[32,4096]{1,0:T(8,128)(2,1)S(1)}, u32[]{:S(2)}, u32[]{:S(2)}) %collective-permute-start.6) | collective-permute-done | bytes 262176 | tf_op jit(solution)/shard_map/ppermute | solution.py:152
  18.3 1.6 %collective-permute-start.7 = (bf16[16,4096]{1,0:T(8,128)(2,1)S(1)}, bf16[16,4096]{1,0:T(8,128)(2,1)S(1)}, u32[]{:S(2)}, u32[]{:S(2)}) collective-permute-start(bf16[16,4096]{1,0:T(8,128)(2,1)S(1)} %get-tuple-element.16), channel_id=1, source_target_pairs={{0,2},{1,3},{2,0},{3,1},{4,6},{5,7},{6,4},{7,5},{8,10},{9,11},{10,... | collective-permute-start | bytes 393224 | tf_op jit(solution)/shard_map/ppermute | solution.py:166
  19.8 4.3 %collective-permute-done.7.refs_0_ = bf16[16,4096]{1,0:T(8,128)(2,1)S(1)} collective-permute-done((bf16[16,4096]{1,0:T(8,128)(2,1)S(1)}, bf16[16,4096]{1,0:T(8,128)(2,1)S(1)}, u32[]{:S(2)}, u32[]{:S(2)}) %collective-permute-start.7) | collective-permute-done | bytes 131104 | tf_op jit(solution)/shard_map/ppermute | solution.py:166
  24.2 1.9 %collective-permute-start.8 = (bf16[4,4096]{1,0:T(4,128)(2,1)S(1)}, bf16[4,4096]{1,0:T(4,128)(2,1)S(1)}, u32[]{:S(2)}, u32[]{:S(2)}) collective-permute-start(bf16[4,4096]{1,0:T(4,128)(2,1)S(1)} %get-tuple-element.18), channel_id=1, source_target_pairs={{0,12},{4,0},{8,4},{12,8},{1,13},{5,1},{9,5},{13,9},{2,14},{6,2},{... | collective-permute-start | bytes 98312 | tf_op jit(solution)/shard_map/ppermute | solution.py:179
  26.1 1.5 %collective-permute-start.10 = (bf16[4,4096]{1,0:T(4,128)(2,1)S(1)}, bf16[4,4096]{1,0:T(4,128)(2,1)S(1)}, u32[]{:S(2)}, u32[]{:S(2)}) collective-permute-start(bf16[4,4096]{1,0:T(4,128)(2,1)S(1)} %get-tuple-element.20), channel_id=1, source_target_pairs={{0,4},{4,8},{8,12},{12,0},{1,5},{5,9},{9,13},{13,1},{2,6},{6,10},{... | collective-permute-start | bytes 98312 | tf_op jit(solution)/shard_map/ppermute | solution.py:179
  27.6 0.5 %collective-permute-done.8.refs_1_ = bf16[4,4096]{1,0:T(4,128)(2,1)S(1)} collective-permute-done((bf16[4,4096]{1,0:T(4,128)(2,1)S(1)}, bf16[4,4096]{1,0:T(4,128)(2,1)S(1)}, u32[]{:S(2)}, u32[]{:S(2)}) %collective-permute-start.8) | collective-permute-done | bytes 32800 | tf_op jit(solution)/shard_map/ppermute | solution.py:179
  28.1 2.8 %collective-permute-done.9.refs_2_ = bf16[4,4096]{1,0:T(4,128)(2,1)S(1)} collective-permute-done((bf16[4,4096]{1,0:T(4,128)(2,1)S(1)}, bf16[4,4096]{1,0:T(4,128)(2,1)S(1)}, u32[]{:S(2)}, u32[]{:S(2)}) %collective-permute-start.9) | collective-permute-done | bytes 32800 | tf_op jit(solution)/shard_map/ppermute | solution.py:179
  30.9 0.9 %collective-permute-done.10.refs_3_ = bf16[4,4096]{1,0:T(4,128)(2,1)S(1)} collective-permute-done((bf16[4,4096]{1,0:T(4,128)(2,1)S(1)}, bf16[4,4096]{1,0:T(4,128)(2,1)S(1)}, u32[]{:S(2)}, u32[]{:S(2)}) %collective-permute-start.10) | collective-permute-done | bytes 32800 | tf_op jit(solution)/shard_map/ppermute | solution.py:179
  31.8 0.7 %mix.1 = bf16[4,4096]{1,0:T(4,128)(2,1)} custom-call(s32[2,16]{1,0:T(2,128)S(1)} %bitcast.2, f32[2,4]{1,0:T(2,128)S(1)} %bitcast.3, f32[4,4096]{1,0:T(4,128)S(1)} %get-tuple-element.17.refs_0_, bf16[4,4096]{1,0:T(4,128)(2,1)S(1)} %collective-permute-done.8.refs_1_, bf16[4,4096]{1,0:T(4,128)(2,1)S(1)} %collective-permute-done.9.refs_2_, ...), custom_call_target="tpu_custom_call" | custom-call | tf_op jit(solution)/shard_map/mix/pallas_call | solution.py:181
  (15 shorter events, 0.1 us)
Async XLA Ops:
  0.0 14.1 %copy-start.3 = (bf16[16,4096]{1,0:T(8,128)(2,1)S(1)}, bf16[16,4096]{1,0:T(8,128)(2,1)}, u32[]{:S(2)}) copy-start(bf16[16,4096]{1,0:T(8,128)(2,1)} %own.1) | copy-start | bytes 393220
  0.0 14.1 %copy-start.2 = (bf16[1,384,4096]{2,1,0:T(8,128)(2,1)S(1)}, bf16[1,384,4096]{2,1,0:T(8,128)(2,1)}, u32[]{:S(2)}) copy-start(bf16[1,384,4096]{2,1,0:T(8,128)(2,1)} %refs_8_.1) | copy-start | bytes 9437188
  0.0 14.1 %copy-start.1 = (bf16[1,384,4096]{2,1,0:T(8,128)(2,1)S(1)}, bf16[1,384,4096]{2,1,0:T(8,128)(2,1)}, u32[]{:S(2)}) copy-start(bf16[1,384,4096]{2,1,0:T(8,128)(2,1)} %refs_7_.1) | copy-start | bytes 9437188
  0.0 14.1 %copy-start = (bf16[1,384,4096]{2,1,0:T(8,128)(2,1)S(1)}, bf16[1,384,4096]{2,1,0:T(8,128)(2,1)}, u32[]{:S(2)}) copy-start(bf16[1,384,4096]{2,1,0:T(8,128)(2,1)} %refs_6_.1) | copy-start | bytes 9437188
  1.0 30.8 %copy-start.4 = (s32[16,2]{0,1:T(2,128)S(1)}, s32[16,2]{0,1:T(2,128)}, u32[]{:S(2)}) copy-start(s32[16,2]{0,1:T(2,128)} %param.7) | copy-start | bytes 388
  1.0 30.8 %copy-start.5 = (f32[4,2]{0,1:T(2,128)S(1)}, f32[4,2]{0,1:T(2,128)}, u32[]{:S(2)}) copy-start(f32[4,2]{0,1:T(2,128)} %param.8) | copy-start | bytes 100
  1.0 7.6 %collective-permute-start.2 = (bf16[16,2048]{1,0:T(8,128)(2,1)S(1)}, bf16[16,2048]{1,0:T(8,128)(2,1)S(1)}, u32[]{:S(2)}, u32[]{:S(2)}) collective-permute-start(bf16[16,2048]{1,0:T(8,128)(2,1)S(1)} %half.1), channel_id=1, source_target_pairs={{0,12},{4,0},{8,4},{12,8},{1,13},{5,1},{9,5},{13,9},{2,14},{6,2},{... | collective-permute-start | bytes 196616 | tf_op jit(solution)/shard_map/ppermute | solution.py:132
  6.2 6.5 %collective-permute-start.1 = (bf16[16,2048]{1,0:T(8,128)(2,1)S(1)}, bf16[16,2048]{1,0:T(8,128)(2,1)S(1)}, u32[]{:S(2)}, u32[]{:S(2)}) collective-permute-start(bf16[16,2048]{1,0:T(8,128)(2,1)S(1)} %half.1), channel_id=1, source_target_pairs={{0,8},{4,12},{8,0},{12,4},{1,9},{5,13},{9,1},{13,5},{2,10},{6,14},... | collective-permute-start | bytes 196616 | tf_op jit(solution)/shard_map/ppermute | solution.py:132
  6.2 6.5 %collective-permute-start = (bf16[16,2048]{1,0:T(8,128)(2,1)S(1)}, bf16[16,2048]{1,0:T(8,128)(2,1)S(1)}, u32[]{:S(2)}, u32[]{:S(2)}) collective-permute-start(bf16[16,2048]{1,0:T(8,128)(2,1)S(1)} %half.1), channel_id=1, source_target_pairs={{0,4},{4,8},{8,12},{12,0},{1,5},{5,9},{9,13},{13,1},{2,6},{6,10},{... | collective-permute-start | bytes 196616 | tf_op jit(solution)/shard_map/ppermute | solution.py:132
  8.7 4.5 %collective-permute-start.5 = (bf16[16,2048]{1,0:T(8,128)(2,1)S(1)}, bf16[16,2048]{1,0:T(8,128)(2,1)S(1)}, u32[]{:S(2)}, u32[]{:S(2)}) collective-permute-start(bf16[16,2048]{1,0:T(8,128)(2,1)S(1)} %collective-permute-done.2.refs_2_), channel_id=1, source_target_pairs={{0,1},{1,0},{2,3},{3,2},{4,5},{5,4},{6,7},{7,6},{8,9},{9,8},{10,11... | collective-permute-start | bytes 196616 | tf_op jit(solution)/shard_map/ppermute | solution.py:134
  12.6 1.3 %collective-permute-start.4 = (bf16[16,2048]{1,0:T(8,128)(2,1)S(1)}, bf16[16,2048]{1,0:T(8,128)(2,1)S(1)}, u32[]{:S(2)}, u32[]{:S(2)}) collective-permute-start(bf16[16,2048]{1,0:T(8,128)(2,1)S(1)} %collective-permute-done.1.refs_1_), channel_id=1, source_target_pairs={{0,1},{1,0},{2,3},{3,2},{4,5},{5,4},{6,7},{7,6},{8,9},{9,8},{10,11... | collective-permute-start | bytes 196616 | tf_op jit(solution)/shard_map/ppermute | solution.py:134
  12.6 1.4 %collective-permute-start.3 = (bf16[16,2048]{1,0:T(8,128)(2,1)S(1)}, bf16[16,2048]{1,0:T(8,128)(2,1)S(1)}, u32[]{:S(2)}, u32[]{:S(2)}) collective-permute-start(bf16[16,2048]{1,0:T(8,128)(2,1)S(1)} %collective-permute-done.refs_0_), channel_id=1, source_target_pairs={{0,1},{1,0},{2,3},{3,2},{4,5},{5,4},{6,7},{7,6},{8,9},{9,8},{10,11... | collective-permute-start | bytes 196616 | tf_op jit(solution)/shard_map/ppermute | solution.py:134
  16.6 1.6 %collective-permute-start.6 = (bf16[32,4096]{1,0:T(8,128)(2,1)S(1)}, bf16[32,4096]{1,0:T(8,128)(2,1)S(1)}, u32[]{:S(2)}, u32[]{:S(2)}) collective-permute-start(bf16[32,4096]{1,0:T(8,128)(2,1)S(1)} %get-tuple-element.14), channel_id=1, source_target_pairs={{0,1},{1,0},{2,3},{3,2},{4,5},{5,4},{6,7},{7,6},{8,9},{9,8},{10,11... | collective-permute-start | bytes 786440 | tf_op jit(solution)/shard_map/ppermute | solution.py:152
  18.3 5.8 %collective-permute-start.7 = (bf16[16,4096]{1,0:T(8,128)(2,1)S(1)}, bf16[16,4096]{1,0:T(8,128)(2,1)S(1)}, u32[]{:S(2)}, u32[]{:S(2)}) collective-permute-start(bf16[16,4096]{1,0:T(8,128)(2,1)S(1)} %get-tuple-element.16), channel_id=1, source_target_pairs={{0,2},{1,3},{2,0},{3,1},{4,6},{5,7},{6,4},{7,5},{8,10},{9,11},{10,... | collective-permute-start | bytes 393224 | tf_op jit(solution)/shard_map/ppermute | solution.py:166
  24.2 4.0 %collective-permute-start.8 = (bf16[4,4096]{1,0:T(4,128)(2,1)S(1)}, bf16[4,4096]{1,0:T(4,128)(2,1)S(1)}, u32[]{:S(2)}, u32[]{:S(2)}) collective-permute-start(bf16[4,4096]{1,0:T(4,128)(2,1)S(1)} %get-tuple-element.18), channel_id=1, source_target_pairs={{0,12},{4,0},{8,4},{12,8},{1,13},{5,1},{9,5},{13,9},{2,14},{6,2},{... | collective-permute-start | bytes 98312 | tf_op jit(solution)/shard_map/ppermute | solution.py:179
  26.1 4.8 %collective-permute-start.9 = (bf16[4,4096]{1,0:T(4,128)(2,1)S(1)}, bf16[4,4096]{1,0:T(4,128)(2,1)S(1)}, u32[]{:S(2)}, u32[]{:S(2)}) collective-permute-start(bf16[4,4096]{1,0:T(4,128)(2,1)S(1)} %get-tuple-element.19), channel_id=1, source_target_pairs={{0,8},{4,12},{8,0},{12,4},{1,9},{5,13},{9,1},{13,5},{2,10},{6,14},... | collective-permute-start | bytes 98312 | tf_op jit(solution)/shard_map/ppermute | solution.py:179
  26.1 5.7 %collective-permute-start.10 = (bf16[4,4096]{1,0:T(4,128)(2,1)S(1)}, bf16[4,4096]{1,0:T(4,128)(2,1)S(1)}, u32[]{:S(2)}, u32[]{:S(2)}) collective-permute-start(bf16[4,4096]{1,0:T(4,128)(2,1)S(1)} %get-tuple-element.20), channel_id=1, source_target_pairs={{0,4},{4,8},{8,12},{12,0},{1,5},{5,9},{9,13},{13,1},{2,6},{6,10},{... | collective-permute-start | bytes 98312 | tf_op jit(solution)/shard_map/ppermute | solution.py:179

commit v6 on v5

--- a/solution.py
+++ b/solution.py
@@ -13,8 +13,9 @@
 HBM = pl.BlockSpec(memory_space=pltpu.HBM)
 
 
-def order_matrix(n_expert, pairs, rows, me):
-    total = n_expert * pairs * 2 * rows
+def order_kernel(n_expert, pairs, rows, out):
+    total = out.shape[0]
+    me = lax.axis_index("etp")
     core, pair = lax.rem(me, 2), lax.div(me, 2)
     place = lax.broadcasted_iota(jnp.int32, (total, total), 0)
     source = lax.broadcasted_iota(jnp.int32, (total, total), 1)
@@ -24,39 +25,25 @@
     sent = lax.div(place, rows * pairs * n_expert)
     block = 2 * lax.rem(pair + h, pairs) + lax.rem(core + sent, 2)
     wanted = (k * pairs * 2 + block) * rows + row
-    return jnp.where(source == wanted, 1.0, 0.0).astype(jnp.bfloat16)
+    out[...] = jnp.where(source == wanted, 1.0, 0.0).astype(jnp.bfloat16)
 
 
-def half_kernel(tokens, out, sem):
-    half = out.shape[1]
+def ffn_kernel(n_expert, parts, own, next_block, order, *refs):
+    far = refs[: n_expert - 2]
+    w_gate, w_up, w_down, kept, sent, x = refs[n_expert - 2 :]
     core = lax.rem(lax.axis_index("etp"), 2)
-    cols = pl.ds(pl.multiple_of(core * half, half), half)
-    copy = pltpu.make_async_copy(tokens.at[:, cols], out, sem)
-    copy.start()
-    copy.wait()
-
-
-def ffn_kernel(n_expert, n_etp, rows, parts, own, *refs):
-    near = refs[: n_expert - 1]
-    far = refs[n_expert - 1 : 2 * n_expert - 2]
-    w_gate, w_up, w_down, kept, sent, x = refs[2 * n_expert - 2 :]
-    me = lax.axis_index("etp")
-    core = lax.rem(me, 2)
     tok, width = own.shape
-    half = width // 2
     step = width // parts
     x[0:tok, :] = own[...]
-    mine = pl.ds(pl.multiple_of(core * half, half), half)
-    other = pl.ds(pl.multiple_of((1 - core) * half, half), half)
-    for k in range(1, n_expert):
-        x[k * tok : (k + 1) * tok, mine] = near[k - 1][...]
-        x[k * tok : (k + 1) * tok, other] = far[k - 1][...]
+    x[tok : 2 * tok, :] = next_block[...]
+    for i in range(0, n_expert - 2, 2):
+        for block, k in ((far[i], i + 2 + core), (far[i + 1], i + 3 - core)):
+            x[pl.ds(pl.multiple_of(k * tok, tok), tok), :] = block[...]
     contract = (((1,), (1,)), ((), ()))
     gate = lax.dot_general(w_gate[0], x[...], contract, preferred_element_type=jnp.float32)
     upper = lax.dot_general(w_up[0], x[...], contract, preferred_element_type=jnp.float32)
     hidden = (gate / (1.0 + jnp.exp(-gate)) * upper).astype(jnp.bfloat16)
-    order = order_matrix(n_expert, n_etp // 2, rows, me)
-    hidden = lax.dot_general(order, hidden, contract, preferred_element_type=jnp.float32)
+    hidden = lax.dot_general(order[...], hidden, contract, preferred_element_type=jnp.float32)
     hidden = hidden.astype(jnp.bfloat16)
     side = kept.shape[0]
     for c in range(parts):
@@ -101,7 +88,7 @@
     scale = sum(own_weights)
     total = None
     for k in range(n_expert):
-        owner = lax.rem(expert + k, n_expert)
+        owner = lax.bitwise_xor(expert, k)
         factor = sum(jnp.where(own_ids[i] == owner, own_weights[i], 0.0) for i in range(top)) / scale
         term = pieces[k][...].astype(jnp.float32) * factor
         total = term if total is None else total + term
@@ -113,41 +100,44 @@
     rows = tok // n_etp
     pairs = n_etp // 2
     side = n_expert * tok // 2
-    half = width // 2
 
-    own_half = pl.pallas_call(
-        half_kernel,
-        out_shape=jax.ShapeDtypeStruct((tok, half), tokens.dtype),
-        in_specs=[HBM],
+    order = pl.pallas_call(
+        functools.partial(order_kernel, n_expert, pairs, rows),
+        out_shape=jax.ShapeDtypeStruct((2 * side, 2 * side), jnp.bfloat16),
         out_specs=VMEM,
-        scratch_shapes=[pltpu.SemaphoreType.DMA],
         cost_estimate=AHEAD,
         compiler_params=GRANT,
-        name="half",
-    )(pltpu.with_memory_space_constraint(tokens, pltpu.HBM))
-    near, far = [], []
-    swap = [(i, i ^ 1) for i in range(n_etp)]
-    for k in range(1, n_expert):
-        hop = [(i, (i + k) % n_expert) for i in range(n_expert)]
-        near.append(lax.ppermute(own_half, "expert", hop))
-    for block in near:
-        far.append(lax.ppermute(block, "etp", swap))
+        name="order",
+    )()
+    tokens, order = lax.optimization_barrier((tokens, order))
+
+    swap = [(t, t ^ 1) for t in range(n_etp)]
+    far = []
+    for k in range(2, n_expert, 2):
+        route = [
+            (e * n_etp + t, (e ^ (k + t % 2)) * n_etp + t)
+            for e in range(n_expert)
+            for t in range(n_etp)
+        ]
+        far.append(lax.ppermute(tokens, ("expert", "etp"), route))
+    next_block = lax.ppermute(tokens, "expert", [(e, e ^ 1) for e in range(n_expert)])
+    far = [b for block in far for b in (block, lax.ppermute(block, "etp", swap))]
 
     parts = 4
     kept, sent = pl.pallas_call(
-        functools.partial(ffn_kernel, n_expert, n_etp, rows, parts),
+        functools.partial(ffn_kernel, n_expert, parts),
         out_shape=(
             jax.ShapeDtypeStruct((side, width), jnp.float32),
             jax.ShapeDtypeStruct((side, width), jnp.bfloat16),
         ),
-        in_specs=[VMEM] * (2 * n_expert + 2),
+        in_specs=[VMEM] * (n_expert + 4),
         out_specs=(VMEM, VMEM),
         scratch_shapes=[
             pltpu.VMEM((n_expert * tok, width), jnp.bfloat16),
         ],
         compiler_params=GRANT,
         name="ffn",
-    )(tokens, *near, *far, w_gate, w_up, w_down)
+    )(tokens, next_block, order, *far, w_gate, w_up, w_down)
 
     arrived = lax.ppermute(sent, "etp", swap)
     block = n_expert * rows
@@ -175,7 +165,7 @@
     )(own, *landed)
     landed = [own]
     for k, piece in enumerate(pieces, 1):
-        route = [(e, (e - k) % n_expert) for e in range(n_expert)]
+        route = [(e, e ^ k) for e in range(n_expert)]
         landed.append(lax.ppermute(piece, "expert", route))
 
     return pl.pallas_call(

time: 32.7 us -> 32.9 us (level)
  Pallas kernels: 4.38 us -> 3.4 us
  local copies, waits for them, and re-layouts: 0.03 us -> 0.87 us
  waiting for transfers between devices: 16 us -> 16.6 us
    ppermute x6 -> x3, starting transfers between devices: 6.64 us -> 5.62 us  [the longest x1 4.04 us: on_device(): far.append(lax.ppermute(tokens, ('expert', 'etp'), route))]
    pallas_call x2, Pallas kernels: 3.55 us -> 2.57 us  [the longest x1 2.53 us: on_device(): pl.pallas_call(functools.partial(ffn_kernel, n_expert, parts), out_shape=...]
    ppermute x3, starting transfers between devices: 3.48 us -> 4.45 us  [on_device(): landed.append(lax.ppermute(piece, 'expert', route))]
    unnamed x12, local copies, waits for them, and re-layouts: 0.03 us -> 0.87 us
    ppermute x3, waiting for transfers between devices: 4.17 us -> 4.77 us  [on_device(): landed.append(lax.ppermute(piece, 'expert', route))]
    ppermute x6 -> x3, waiting for transfers between devices: 6.35 us -> 6.34 us  [the longest x1 5 us: on_device(): far.append(lax.ppermute(tokens, ('expert', 'etp'), route))]
  transfers between devices with their start and end apart: 11 -> 8, of which waited for: 9 -> 7; matrix products, arithmetic and copies ran while one was open for 0% -> 0% of each run, Pallas kernels for 0% -> 0%
where the time goes in v6:
time: 32.9 us; the launch traced here: 32.7 us
  waiting for transfers between devices  16.6 us (50%)
  starting transfers between devices  11.9 us (36%)
  Pallas kernels  3.4 us (10%)
  local copies, waits for them, and re-layouts  0.87 us (3%)
    ppermute x1, waiting for transfers between devices, on_device(): far.append(lax.ppermute(tokens, ('expert', 'etp'), route))  5 us
    ppermute x3, waiting for transfers between devices, on_device(): landed.append(lax.ppermute(piece, 'expert', route))  4.77 us
    ppermute x3, starting transfers between devices, on_device(): landed.append(lax.ppermute(piece, 'expert', route))  4.45 us
    ppermute x1, waiting for transfers between devices, on_device(): landed.append(lax.ppermute(piece, 'etp', route))  4.06 us
    ppermute x1, starting transfers between devices, on_device(): far.append(lax.ppermute(tokens, ('expert', 'etp'), route))  4.04 us
    pallas_call x1, Pallas kernels, on_device(): pl.pallas_call(functools.partial(ffn_kernel, n_expert, parts), out_shape=...  2.53 us
    ppermute x1, starting transfers between devices, on_device(): lax.ppermute(tokens, 'expert', [(e, e ^ 1) for e in range(n_expert)])  1.58 us
    ppermute x1, starting transfers between devices, on_device(): landed.append(lax.ppermute(piece, 'etp', route))  1.56 us
  transfers between devices with their start and end apart: 8, of which 7 were waited for; matrix products, arithmetic and copies ran while one was open for 0% of the time, Pallas kernels for 0%

profile of v6, /device:TPU:0, one launch (start us, length us, event | category | flops | bytes accessed | tf_op | source)
XLA Modules:
  0.0 32.7 jit_solution(5522964585484367571)
XLA Ops:
  0.1 0.9 %copy-done.3 = bf16[16,4096]{1,0:T(8,128)(2,1)S(1)} copy-done((bf16[16,4096]{1,0:T(8,128)(2,1)S(1)}, bf16[16,4096]{1,0:T(8,128)(2,1)}, u32[]{:S(2)}) %copy-start.3) | copy-done | bytes 131096
  0.9 4.0 %collective-permute-start.1 = (bf16[16,4096]{1,0:T(8,128)(2,1)S(1)}, bf16[16,4096]{1,0:T(8,128)(2,1)S(1)}, u32[]{:S(2)}, u32[]{:S(2)}) collective-permute-start(bf16[16,4096]{1,0:T(8,128)(2,1)S(1)} %copy-done.3), channel_id=1, source_target_pairs={{0,8},{1,13},{2,10},{3,15},{4,12},{5,9},{6,14},{7,11},{8,0},{9,5},... | collective-permute-start | bytes 393224 | tf_op jit(solution)/shard_map/ppermute | solution.py:122
  4.9 1.6 %collective-permute-start = (bf16[16,4096]{1,0:T(8,128)(2,1)S(1)}, bf16[16,4096]{1,0:T(8,128)(2,1)S(1)}, u32[]{:S(2)}, u32[]{:S(2)}) collective-permute-start(bf16[16,4096]{1,0:T(8,128)(2,1)S(1)} %copy-done.3), channel_id=1, source_target_pairs={{0,4},{4,0},{8,12},{12,8},{1,5},{5,1},{9,13},{13,9},{2,6},{6,2},{1... | collective-permute-start | bytes 393224 | tf_op jit(solution)/shard_map/ppermute | solution.py:123
  6.5 5.0 %collective-permute-done.1.refs_0_ = bf16[16,4096]{1,0:T(8,128)(2,1)S(1)} collective-permute-done((bf16[16,4096]{1,0:T(8,128)(2,1)S(1)}, bf16[16,4096]{1,0:T(8,128)(2,1)S(1)}, u32[]{:S(2)}, u32[]{:S(2)}) %collective-permute-start.1) | collective-permute-done | bytes 131104 | tf_op jit(solution)/shard_map/ppermute | solution.py:122
  11.5 0.0 collective-permute-start.2
  11.5 0.8 %collective-permute-done.next_block = bf16[16,4096]{1,0:T(8,128)(2,1)S(1)} collective-permute-done((bf16[16,4096]{1,0:T(8,128)(2,1)S(1)}, bf16[16,4096]{1,0:T(8,128)(2,1)S(1)}, u32[]{:S(2)}, u32[]{:S(2)}) %collective-permute-start) | collective-permute-done | bytes 131104 | tf_op jit(solution)/shard_map/ppermute | solution.py:123
  12.3 0.6 %collective-permute-done.2.refs_1_ = bf16[16,4096]{1,0:T(8,128)(2,1)S(1)} collective-permute-done((bf16[16,4096]{1,0:T(8,128)(2,1)S(1)}, bf16[16,4096]{1,0:T(8,128)(2,1)S(1)}, u32[]{:S(2)}, u32[]{:S(2)}) %collective-permute-start.2) | collective-permute-done | bytes 131104 | tf_op jit(solution)/shard_map/ppermute | solution.py:124
  12.9 0.0 copy-done.2
  12.9 0.0 copy-done.1
  12.9 0.0 copy-done
  12.9 2.5 %ffn.1 = (f32[32,4096]{1,0:T(8,128)S(1)}, bf16[32,4096]{1,0:T(8,128)(2,1)S(1)}) custom-call(bf16[16,4096]{1,0:T(8,128)(2,1)S(1)} %copy-done.3, bf16[16,4096]{1,0:T(8,128)(2,1)S(1)} %collective-permute-done.next_block, bf16[64,64]{1,0:T(8,128)(2,1)S(1)} %order.1, bf16[16,4096]{1,0:T(8,128)(2,1)S(1)} %collective-permute-done.1.refs_0_, ...), custom_call_target="tpu_custom_call" | custom-call | tf_op jit(solution)/shard_map/ffn/pallas_call | solution.py:127
  15.4 0.2 collective-permute-start.3
  15.6 1.4 %collective-permute-done.3.arrived = bf16[32,4096]{1,0:T(8,128)(2,1)S(1)} collective-permute-done((bf16[32,4096]{1,0:T(8,128)(2,1)S(1)}, bf16[32,4096]{1,0:T(8,128)(2,1)S(1)}, u32[]{:S(2)}, u32[]{:S(2)}) %collective-permute-start.3) | collective-permute-done | bytes 262176 | tf_op jit(solution)/shard_map/ppermute | solution.py:142
  17.1 1.6 %collective-permute-start.4 = (bf16[16,4096]{1,0:T(8,128)(2,1)S(1)}, bf16[16,4096]{1,0:T(8,128)(2,1)S(1)}, u32[]{:S(2)}, u32[]{:S(2)}) collective-permute-start(bf16[16,4096]{1,0:T(8,128)(2,1)S(1)} %get-tuple-element.20), channel_id=1, source_target_pairs={{0,2},{1,3},{2,0},{3,1},{4,6},{5,7},{6,4},{7,5},{8,10},{9,11},{10,... | collective-permute-start | bytes 393224 | tf_op jit(solution)/shard_map/ppermute | solution.py:156
  18.6 4.1 %collective-permute-done.4.refs_0_ = bf16[16,4096]{1,0:T(8,128)(2,1)S(1)} collective-permute-done((bf16[16,4096]{1,0:T(8,128)(2,1)S(1)}, bf16[16,4096]{1,0:T(8,128)(2,1)S(1)}, u32[]{:S(2)}, u32[]{:S(2)}) %collective-permute-start.4) | collective-permute-done | bytes 131104 | tf_op jit(solution)/shard_map/ppermute | solution.py:156
  22.7 1.2 %collective-permute-start.5 = (bf16[4,4096]{1,0:T(4,128)(2,1)S(1)}, bf16[4,4096]{1,0:T(4,128)(2,1)S(1)}, u32[]{:S(2)}, u32[]{:S(2)}) collective-permute-start(bf16[4,4096]{1,0:T(4,128)(2,1)S(1)} %get-tuple-element.22), channel_id=1, source_target_pairs={{0,4},{4,0},{8,12},{12,8},{1,5},{5,1},{9,13},{13,9},{2,6},{6,2},{1... | collective-permute-start | bytes 98312 | tf_op jit(solution)/shard_map/ppermute | solution.py:169
  24.0 2.3 %collective-permute-start.6 = (bf16[4,4096]{1,0:T(4,128)(2,1)S(1)}, bf16[4,4096]{1,0:T(4,128)(2,1)S(1)}, u32[]{:S(2)}, u32[]{:S(2)}) collective-permute-start(bf16[4,4096]{1,0:T(4,128)(2,1)S(1)} %get-tuple-element.23), channel_id=1, source_target_pairs={{0,8},{4,12},{8,0},{12,4},{1,9},{5,13},{9,1},{13,5},{2,10},{6,14},... | collective-permute-start | bytes 98312 | tf_op jit(solution)/shard_map/ppermute | solution.py:169
  26.2 0.9 %collective-permute-start.7 = (bf16[4,4096]{1,0:T(4,128)(2,1)S(1)}, bf16[4,4096]{1,0:T(4,128)(2,1)S(1)}, u32[]{:S(2)}, u32[]{:S(2)}) collective-permute-start(bf16[4,4096]{1,0:T(4,128)(2,1)S(1)} %get-tuple-element.24), channel_id=1, source_target_pairs={{0,12},{4,8},{8,4},{12,0},{1,13},{5,9},{9,5},{13,1},{2,14},{6,10},... | collective-permute-start | bytes 98312 | tf_op jit(solution)/shard_map/ppermute | solution.py:169
  27.2 0.0 collective-permute-done.5.refs_1_
  27.2 1.6 %collective-permute-done.6.refs_2_ = bf16[4,4096]{1,0:T(4,128)(2,1)S(1)} collective-permute-done((bf16[4,4096]{1,0:T(4,128)(2,1)S(1)}, bf16[4,4096]{1,0:T(4,128)(2,1)S(1)}, u32[]{:S(2)}, u32[]{:S(2)}) %collective-permute-start.6) | collective-permute-done | bytes 32800 | tf_op jit(solution)/shard_map/ppermute | solution.py:169
  28.8 3.2 %collective-permute-done.7.refs_3_ = bf16[4,4096]{1,0:T(4,128)(2,1)S(1)} collective-permute-done((bf16[4,4096]{1,0:T(4,128)(2,1)S(1)}, bf16[4,4096]{1,0:T(4,128)(2,1)S(1)}, u32[]{:S(2)}, u32[]{:S(2)}) %collective-permute-start.7) | collective-permute-done | bytes 32800 | tf_op jit(solution)/shard_map/ppermute | solution.py:169
  32.0 0.0 copy-done.4
  32.0 0.0 copy-done.5
  32.0 0.7 %mix.1 = bf16[4,4096]{1,0:T(4,128)(2,1)} custom-call(s32[2,16]{1,0:T(2,128)S(1)} %bitcast.2, f32[2,4]{1,0:T(2,128)S(1)} %bitcast.3, f32[4,4096]{1,0:T(4,128)S(1)} %get-tuple-element.21.refs_0_, bf16[4,4096]{1,0:T(4,128)(2,1)S(1)} %collective-permute-done.5.refs_1_, bf16[4,4096]{1,0:T(4,128)(2,1)S(1)} %collective-permute-done.6.refs_2_, ...), custom_call_target="tpu_custom_call" | custom-call | tf_op jit(solution)/shard_map/mix/pallas_call | solution.py:171
  (9 shorter events, 0.1 us)
Async XLA Ops:
  0.0 0.9 %copy-start.3 = (bf16[16,4096]{1,0:T(8,128)(2,1)S(1)}, bf16[16,4096]{1,0:T(8,128)(2,1)}, u32[]{:S(2)}) copy-start(bf16[16,4096]{1,0:T(8,128)(2,1)} %own) | copy-start | bytes 393220
  0.0 12.9 %copy-start.2 = (bf16[1,384,4096]{2,1,0:T(8,128)(2,1)S(1)}, bf16[1,384,4096]{2,1,0:T(8,128)(2,1)}, u32[]{:S(2)}) copy-start(bf16[1,384,4096]{2,1,0:T(8,128)(2,1)} %refs_4_.1) | copy-start | bytes 9437188
  0.0 12.9 %copy-start.1 = (bf16[1,384,4096]{2,1,0:T(8,128)(2,1)S(1)}, bf16[1,384,4096]{2,1,0:T(8,128)(2,1)}, u32[]{:S(2)}) copy-start(bf16[1,384,4096]{2,1,0:T(8,128)(2,1)} %refs_3_.1) | copy-start | bytes 9437188
  0.0 12.9 %copy-start = (bf16[1,384,4096]{2,1,0:T(8,128)(2,1)S(1)}, bf16[1,384,4096]{2,1,0:T(8,128)(2,1)}, u32[]{:S(2)}) copy-start(bf16[1,384,4096]{2,1,0:T(8,128)(2,1)} %refs_2_.1) | copy-start | bytes 9437188
  0.9 31.1 %copy-start.4 = (s32[16,2]{0,1:T(2,128)S(1)}, s32[16,2]{0,1:T(2,128)}, u32[]{:S(2)}) copy-start(s32[16,2]{0,1:T(2,128)} %param.7) | copy-start | bytes 388
  0.9 31.1 %copy-start.5 = (f32[4,2]{0,1:T(2,128)S(1)}, f32[4,2]{0,1:T(2,128)}, u32[]{:S(2)}) copy-start(f32[4,2]{0,1:T(2,128)} %param.8) | copy-start | bytes 100
  0.9 10.6 %collective-permute-start.1 = (bf16[16,4096]{1,0:T(8,128)(2,1)S(1)}, bf16[16,4096]{1,0:T(8,128)(2,1)S(1)}, u32[]{:S(2)}, u32[]{:S(2)}) collective-permute-start(bf16[16,4096]{1,0:T(8,128)(2,1)S(1)} %copy-done.3), channel_id=1, source_target_pairs={{0,8},{1,13},{2,10},{3,15},{4,12},{5,9},{6,14},{7,11},{8,0},{9,5},... | collective-permute-start | bytes 393224 | tf_op jit(solution)/shard_map/ppermute | solution.py:122
  4.9 7.4 %collective-permute-start = (bf16[16,4096]{1,0:T(8,128)(2,1)S(1)}, bf16[16,4096]{1,0:T(8,128)(2,1)S(1)}, u32[]{:S(2)}, u32[]{:S(2)}) collective-permute-start(bf16[16,4096]{1,0:T(8,128)(2,1)S(1)} %copy-done.3), channel_id=1, source_target_pairs={{0,4},{4,0},{8,12},{12,8},{1,5},{5,1},{9,13},{13,9},{2,6},{6,2},{1... | collective-permute-start | bytes 393224 | tf_op jit(solution)/shard_map/ppermute | solution.py:123
  11.5 1.3 %collective-permute-start.2 = (bf16[16,4096]{1,0:T(8,128)(2,1)S(1)}, bf16[16,4096]{1,0:T(8,128)(2,1)S(1)}, u32[]{:S(2)}, u32[]{:S(2)}) collective-permute-start(bf16[16,4096]{1,0:T(8,128)(2,1)S(1)} %collective-permute-done.1.refs_0_), channel_id=1, source_target_pairs={{0,1},{1,0},{2,3},{3,2},{4,5},{5,4},{6,7},{7,6},{8,9},{9,8},{10,11... | collective-permute-start | bytes 393224 | tf_op jit(solution)/shard_map/ppermute | solution.py:124
  15.4 1.6 %collective-permute-start.3 = (bf16[32,4096]{1,0:T(8,128)(2,1)S(1)}, bf16[32,4096]{1,0:T(8,128)(2,1)S(1)}, u32[]{:S(2)}, u32[]{:S(2)}) collective-permute-start(bf16[32,4096]{1,0:T(8,128)(2,1)S(1)} %get-tuple-element.18), channel_id=1, source_target_pairs={{0,1},{1,0},{2,3},{3,2},{4,5},{5,4},{6,7},{7,6},{8,9},{9,8},{10,11... | collective-permute-start | bytes 786440 | tf_op jit(solution)/shard_map/ppermute | solution.py:142
  17.1 5.6 %collective-permute-start.4 = (bf16[16,4096]{1,0:T(8,128)(2,1)S(1)}, bf16[16,4096]{1,0:T(8,128)(2,1)S(1)}, u32[]{:S(2)}, u32[]{:S(2)}) collective-permute-start(bf16[16,4096]{1,0:T(8,128)(2,1)S(1)} %get-tuple-element.20), channel_id=1, source_target_pairs={{0,2},{1,3},{2,0},{3,1},{4,6},{5,7},{6,4},{7,5},{8,10},{9,11},{10,... | collective-permute-start | bytes 393224 | tf_op jit(solution)/shard_map/ppermute | solution.py:156
  22.7 4.5 %collective-permute-start.5 = (bf16[4,4096]{1,0:T(4,128)(2,1)S(1)}, bf16[4,4096]{1,0:T(4,128)(2,1)S(1)}, u32[]{:S(2)}, u32[]{:S(2)}) collective-permute-start(bf16[4,4096]{1,0:T(4,128)(2,1)S(1)} %get-tuple-element.22), channel_id=1, source_target_pairs={{0,4},{4,0},{8,12},{12,8},{1,5},{5,1},{9,13},{13,9},{2,6},{6,2},{1... | collective-permute-start | bytes 98312 | tf_op jit(solution)/shard_map/ppermute | solution.py:169
  24.0 4.8 %collective-permute-start.6 = (bf16[4,4096]{1,0:T(4,128)(2,1)S(1)}, bf16[4,4096]{1,0:T(4,128)(2,1)S(1)}, u32[]{:S(2)}, u32[]{:S(2)}) collective-permute-start(bf16[4,4096]{1,0:T(4,128)(2,1)S(1)} %get-tuple-element.23), channel_id=1, source_target_pairs={{0,8},{4,12},{8,0},{12,4},{1,9},{5,13},{9,1},{13,5},{2,10},{6,14},... | collective-permute-start | bytes 98312 | tf_op jit(solution)/shard_map/ppermute | solution.py:169
  26.2 5.7 %collective-permute-start.7 = (bf16[4,4096]{1,0:T(4,128)(2,1)S(1)}, bf16[4,4096]{1,0:T(4,128)(2,1)S(1)}, u32[]{:S(2)}, u32[]{:S(2)}) collective-permute-start(bf16[4,4096]{1,0:T(4,128)(2,1)S(1)} %get-tuple-element.24), channel_id=1, source_target_pairs={{0,12},{4,8},{8,4},{12,0},{1,13},{5,9},{9,5},{13,1},{2,14},{6,10},... | collective-permute-start | bytes 98312 | tf_op jit(solution)/shard_map/ppermute | solution.py:169

commit v7 on v6

--- a/solution.py
+++ b/solution.py
@@ -19,10 +19,12 @@
     core, pair = lax.rem(me, 2), lax.div(me, 2)
     place = lax.broadcasted_iota(jnp.int32, (total, total), 0)
     source = lax.broadcasted_iota(jnp.int32, (total, total), 1)
+    half = n_expert // 2
     row = lax.rem(place, rows)
-    k = lax.rem(lax.div(place, rows), n_expert)
-    h = lax.rem(lax.div(place, rows * n_expert), pairs)
-    sent = lax.div(place, rows * pairs * n_expert)
+    k = lax.rem(lax.div(place, rows), half)
+    h = lax.rem(lax.div(place, rows * half), pairs)
+    sent = lax.rem(lax.div(place, rows * half * pairs), 2)
+    k = k + half * (1 - lax.div(place, rows * half * pairs * 2))
     block = 2 * lax.rem(pair + h, pairs) + lax.rem(core + sent, 2)
     wanted = (k * pairs * 2 + block) * rows + row
     out[...] = jnp.where(source == wanted, 1.0, 0.0).astype(jnp.bfloat16)
@@ -30,10 +32,9 @@
 
 def ffn_kernel(n_expert, parts, own, next_block, order, *refs):
     far = refs[: n_expert - 2]
-    w_gate, w_up, w_down, kept, sent, x = refs[n_expert - 2 :]
+    w_gate, w_up, w_down, kept, sent, rest, x = refs[n_expert - 2 :]
     core = lax.rem(lax.axis_index("etp"), 2)
-    tok, width = own.shape
-    step = width // parts
+    tok = own.shape[0]
     x[0:tok, :] = own[...]
     x[tok : 2 * tok, :] = next_block[...]
     for i in range(0, n_expert - 2, 2):
@@ -45,12 +46,23 @@
     hidden = (gate / (1.0 + jnp.exp(-gate)) * upper).astype(jnp.bfloat16)
     hidden = lax.dot_general(order[...], hidden, contract, preferred_element_type=jnp.float32)
     hidden = hidden.astype(jnp.bfloat16)
-    side = kept.shape[0]
+    now = rest.shape[0]
+    rest[...] = hidden[now:]
+    down(parts, hidden[:now], w_down, kept, sent)
+
+
+def down(parts, hidden, w_down, kept, sent):
+    side, width = kept.shape
+    step = width // parts
     for c in range(parts):
         cols = slice(c * step, (c + 1) * step)
         out = jnp.dot(hidden, w_down[0, :, cols], preferred_element_type=jnp.float32)
         kept[:, cols] = out[:side]
         sent[:, cols] = out[side:].astype(jnp.bfloat16)
+
+
+def down_kernel(parts, hidden, w_down, kept, sent):
+    down(parts, hidden[...], w_down, kept, sent)
 
 
 def add_kernel(kept, arrived, own, *pieces):
@@ -124,49 +136,58 @@
     far = [b for block in far for b in (block, lax.ppermute(block, "etp", swap))]
 
     parts = 4
-    kept, sent = pl.pallas_call(
+    halves = [
+        jax.ShapeDtypeStruct((side // 2, width), jnp.float32),
+        jax.ShapeDtypeStruct((side // 2, width), jnp.bfloat16),
+    ]
+    far_kept, far_sent, rest = pl.pallas_call(
         functools.partial(ffn_kernel, n_expert, parts),
-        out_shape=(
-            jax.ShapeDtypeStruct((side, width), jnp.float32),
-            jax.ShapeDtypeStruct((side, width), jnp.bfloat16),
-        ),
+        out_shape=halves + [jax.ShapeDtypeStruct((side, w_gate.shape[1]), jnp.bfloat16)],
         in_specs=[VMEM] * (n_expert + 4),
-        out_specs=(VMEM, VMEM),
-        scratch_shapes=[
-            pltpu.VMEM((n_expert * tok, width), jnp.bfloat16),
-        ],
+        out_specs=[VMEM] * 3,
+        scratch_shapes=[pltpu.VMEM((n_expert * tok, width), jnp.bfloat16)],
         compiler_params=GRANT,
         name="ffn",
     )(tokens, next_block, order, *far, w_gate, w_up, w_down)
-
-    arrived = lax.ppermute(sent, "etp", swap)
-    block = n_expert * rows
-    own, *pieces = pl.pallas_call(
-        add_kernel,
-        out_shape=[jax.ShapeDtypeStruct((block, width), jnp.float32)]
-        + [jax.ShapeDtypeStruct((block, width), jnp.bfloat16)] * (pairs - 1),
+    near_kept, near_sent = pl.pallas_call(
+        functools.partial(down_kernel, parts),
+        out_shape=halves,
         in_specs=[VMEM] * 2,
-        out_specs=[VMEM] * pairs,
-        compiler_params=GRANT,
-        name="add",
-    )(kept, arrived)
+        out_specs=[VMEM] * 2,
+        compiler_params=GRANT,
+        name="down",
+    )(rest, w_down)
+
+    block = n_expert // 2 * rows
+    pieces = []
+    for kept, sent in ((far_kept, far_sent), (near_kept, near_sent)):
+        arrived = lax.ppermute(sent, "etp", swap)
+        own, *others = pl.pallas_call(
+            add_kernel,
+            out_shape=[jax.ShapeDtypeStruct((block, width), jnp.float32)]
+            + [jax.ShapeDtypeStruct((block, width), jnp.bfloat16)] * (pairs - 1),
+            in_specs=[VMEM] * 2,
+            out_specs=[VMEM] * pairs,
+            compiler_params=GRANT,
+            name="add",
+        )(kept, arrived)
+        landed = []
+        for h, piece in enumerate(others, 1):
+            route = [(t, 2 * ((t // 2 + h) % pairs) + t % 2) for t in range(n_etp)]
+            landed.append(lax.ppermute(piece, "etp", route))
+        folded = pl.pallas_call(
+            functools.partial(fold_kernel, pairs),
+            out_shape=[jax.ShapeDtypeStruct((rows, width), jnp.bfloat16)] * (n_expert // 2),
+            in_specs=[VMEM] * pairs,
+            out_specs=[VMEM] * (n_expert // 2),
+            compiler_params=GRANT,
+            name="fold",
+        )(own, *landed)
+        pieces = list(folded) + pieces
     landed = []
-    for h, piece in enumerate(pieces, 1):
-        route = [(t, 2 * ((t // 2 + h) % pairs) + t % 2) for t in range(n_etp)]
-        landed.append(lax.ppermute(piece, "etp", route))
-    own, *pieces = pl.pallas_call(
-        functools.partial(fold_kernel, pairs),
-        out_shape=[jax.ShapeDtypeStruct((rows, width), jnp.float32)]
-        + [jax.ShapeDtypeStruct((rows, width), jnp.bfloat16)] * (n_expert - 1),
-        in_specs=[VMEM] * pairs,
-        out_specs=[VMEM] * n_expert,
-        compiler_params=GRANT,
-        name="fold",
-    )(own, *landed)
-    landed = [own]
-    for k, piece in enumerate(pieces, 1):
-        route = [(e, e ^ k) for e in range(n_expert)]
-        landed.append(lax.ppermute(piece, "expert", route))
+    for k in range(n_expert - 1, 0, -1):
+        landed.insert(0, lax.ppermute(pieces[k], "expert", [(e, e ^ k) for e in range(n_expert)]))
+    landed.insert(0, pieces[0])
 
     return pl.pallas_call(
         functools.partial(mix_kernel, n_expert),

time: 32.9 us -> 30 us (0.912)
  waiting for transfers between devices: 16.6 us -> 12.6 us
  Pallas kernels: 3.4 us -> 4.06 us
  starting transfers between devices: 11.9 us -> 12.3 us
    ppermute x1 -> x2, waiting for transfers between devices: 4.06 us -> 2.2 us  [on_device(): landed.append(lax.ppermute(piece, 'etp', route))]
    ppermute x1 -> x2, waiting for transfers between devices: 1.38 us -> 0.17 us  [on_device(): arrived = lax.ppermute(sent, 'etp', swap)]
    ppermute x3, waiting for transfers between devices: 4.77 us -> 3.9 us  [on_device(): lax.ppermute(pieces[k], 'expert', [(e, e ^ k) for e in range(n_expert)])]
    ppermute x1 -> x2, starting transfers between devices: 1.56 us -> 2.35 us  [on_device(): landed.append(lax.ppermute(piece, 'etp', route))]
    ppermute x3, starting transfers between devices: 4.45 us -> 3.7 us  [on_device(): lax.ppermute(pieces[k], 'expert', [(e, e ^ k) for e in range(n_expert)])]
    pallas_call x0 -> x1, Pallas kernels: none -> 0.64 us  [on_device(): pl.pallas_call(functools.partial(down_kernel, parts), out_shape=halves, i...]
    ppermute x1 -> x2, starting transfers between devices: 0.22 us -> 0.6 us  [on_device(): arrived = lax.ppermute(sent, 'etp', swap)]
  transfers between devices with their start and end apart: 8 -> 10, of which waited for: 7 -> 8; matrix products, arithmetic and copies ran while one was open for 0% -> 0% of each run, Pallas kernels for 0% -> 2%
where the time goes in v7:
time: 30 us; the launch traced here: 29.9 us
  waiting for transfers between devices  12.6 us (42%)
  starting transfers between devices  12.3 us (41%)
  Pallas kernels  4.06 us (14%)
  local copies, waits for them, and re-layouts  0.87 us (3%)
    ppermute x1, waiting for transfers between devices, on_device(): far.append(lax.ppermute(tokens, ('expert', 'etp'), route))  5 us
    ppermute x1, starting transfers between devices, on_device(): far.append(lax.ppermute(tokens, ('expert', 'etp'), route))  4.04 us
    ppermute x3, waiting for transfers between devices, on_device(): lax.ppermute(pieces[k], 'expert', [(e, e ^ k) for e in range(n_expert)])  3.9 us
    ppermute x3, starting transfers between devices, on_device(): lax.ppermute(pieces[k], 'expert', [(e, e ^ k) for e in range(n_expert)])  3.7 us
    pallas_call x1, Pallas kernels, on_device(): pl.pallas_call(functools.partial(ffn_kernel, n_expert, parts), out_shape=...  2.52 us
    ppermute x2, starting transfers between devices, on_device(): landed.append(lax.ppermute(piece, 'etp', route))  2.35 us
    ppermute x2, waiting for transfers between devices, on_device(): landed.append(lax.ppermute(piece, 'etp', route))  2.2 us
    ppermute x1, starting transfers between devices, on_device(): lax.ppermute(tokens, 'expert', [(e, e ^ 1) for e in range(n_expert)])  1.58 us
  transfers between devices with their start and end apart: 10, of which 8 were waited for; matrix products, arithmetic and copies ran while one was open for 0% of the time, Pallas kernels for 2%

profile of v7, /device:TPU:0, one launch (start us, length us, event | category | flops | bytes accessed | tf_op | source)
XLA Modules:
  0.0 29.9 jit_solution(9927357242806628182)
XLA Ops:
  0.1 0.8 %copy-done.3 = bf16[16,4096]{1,0:T(8,128)(2,1)S(1)} copy-done((bf16[16,4096]{1,0:T(8,128)(2,1)S(1)}, bf16[16,4096]{1,0:T(8,128)(2,1)}, u32[]{:S(2)}) %copy-start.3) | copy-done | bytes 131096
  0.9 4.0 %collective-permute-start.1 = (bf16[16,4096]{1,0:T(8,128)(2,1)S(1)}, bf16[16,4096]{1,0:T(8,128)(2,1)S(1)}, u32[]{:S(2)}, u32[]{:S(2)}) collective-permute-start(bf16[16,4096]{1,0:T(8,128)(2,1)S(1)} %copy-done.3), channel_id=1, source_target_pairs={{0,8},{1,13},{2,10},{3,15},{4,12},{5,9},{6,14},{7,11},{8,0},{9,5},... | collective-permute-start | bytes 393224 | tf_op jit(solution)/shard_map/ppermute | solution.py:134
  4.9 1.6 %collective-permute-start = (bf16[16,4096]{1,0:T(8,128)(2,1)S(1)}, bf16[16,4096]{1,0:T(8,128)(2,1)S(1)}, u32[]{:S(2)}, u32[]{:S(2)}) collective-permute-start(bf16[16,4096]{1,0:T(8,128)(2,1)S(1)} %copy-done.3), channel_id=1, source_target_pairs={{0,4},{4,0},{8,12},{12,8},{1,5},{5,1},{9,13},{13,9},{2,6},{6,2},{1... | collective-permute-start | bytes 393224 | tf_op jit(solution)/shard_map/ppermute | solution.py:135
  6.5 5.0 %collective-permute-done.1.refs_0_ = bf16[16,4096]{1,0:T(8,128)(2,1)S(1)} collective-permute-done((bf16[16,4096]{1,0:T(8,128)(2,1)S(1)}, bf16[16,4096]{1,0:T(8,128)(2,1)S(1)}, u32[]{:S(2)}, u32[]{:S(2)}) %collective-permute-start.1) | collective-permute-done | bytes 131104 | tf_op jit(solution)/shard_map/ppermute | solution.py:134
  11.5 0.0 collective-permute-start.2
  11.5 0.8 %collective-permute-done.next_block = bf16[16,4096]{1,0:T(8,128)(2,1)S(1)} collective-permute-done((bf16[16,4096]{1,0:T(8,128)(2,1)S(1)}, bf16[16,4096]{1,0:T(8,128)(2,1)S(1)}, u32[]{:S(2)}, u32[]{:S(2)}) %collective-permute-start) | collective-permute-done | bytes 131104 | tf_op jit(solution)/shard_map/ppermute | solution.py:135
  12.3 0.6 %collective-permute-done.2.refs_1_ = bf16[16,4096]{1,0:T(8,128)(2,1)S(1)} collective-permute-done((bf16[16,4096]{1,0:T(8,128)(2,1)S(1)}, bf16[16,4096]{1,0:T(8,128)(2,1)S(1)}, u32[]{:S(2)}, u32[]{:S(2)}) %collective-permute-start.2) | collective-permute-done | bytes 131104 | tf_op jit(solution)/shard_map/ppermute | solution.py:136
  12.9 2.5 %ffn.1 = (f32[16,4096]{1,0:T(8,128)S(1)}, bf16[16,4096]{1,0:T(8,128)(2,1)S(1)}, bf16[32,384]{1,0:T(8,128)(2,1)S(1)}) custom-call(bf16[16,4096]{1,0:T(8,128)(2,1)S(1)} %copy-done.3, bf16[16,4096]{1,0:T(8,128)(2,1)S(1)} %collective-permute-done.next_block, bf16[64,64]{1,0:T(8,128)(2,1)S(1)} %order.1, bf16[16,4096]{1,0:T(8,128)(2,1)S(1)} %collective-permute-done.1.refs_0_, ...), custom_call_target="tpu_custom_call" | custom-call | tf_op jit(solution)/shard_map/ffn/pallas_call | solution.py:143
  15.4 0.0 copy-start.5
  15.4 0.2 collective-permute-start.6
  15.6 0.6 %down.1 = (f32[16,4096]{1,0:T(8,128)S(1)}, bf16[16,4096]{1,0:T(8,128)(2,1)S(1)}) custom-call(bf16[32,384]{1,0:T(8,128)(2,1)S(1)} %get-tuple-element.22.hidden, bf16[1,384,4096]{2,1,0:T(8,128)(2,1)S(1)} %copy-done), custom_call_target="tpu_custom_call" | custom-call | tf_op jit(solution)/shard_map/down/pallas_call | solution.py:152
  16.3 0.4 %collective-permute-start.3 = (bf16[16,4096]{1,0:T(8,128)(2,1)S(1)}, bf16[16,4096]{1,0:T(8,128)(2,1)S(1)}, u32[]{:S(2)}, u32[]{:S(2)}) collective-permute-start(bf16[16,4096]{1,0:T(8,128)(2,1)S(1)} %get-tuple-element.24), channel_id=1, source_target_pairs={{0,1},{1,0},{2,3},{3,2},{4,5},{5,4},{6,7},{7,6},{8,9},{9,8},{10,11... | collective-permute-start | bytes 393224 | tf_op jit(solution)/shard_map/ppermute | solution.py:164
  16.7 0.2 collective-permute-done.6.arrived
  16.9 1.6 %collective-permute-start.7 = (bf16[8,4096]{1,0:T(8,128)(2,1)S(1)}, bf16[8,4096]{1,0:T(8,128)(2,1)S(1)}, u32[]{:S(2)}, u32[]{:S(2)}) collective-permute-start(bf16[8,4096]{1,0:T(8,128)(2,1)S(1)} %get-tuple-element.32), channel_id=1, source_target_pairs={{0,2},{1,3},{2,0},{3,1},{4,6},{5,7},{6,4},{7,5},{8,10},{9,11},{10,... | collective-permute-start | bytes 196616 | tf_op jit(solution)/shard_map/ppermute | solution.py:177
  18.4 0.0 collective-permute-done.3.arrived
  18.5 0.8 %collective-permute-start.4 = (bf16[8,4096]{1,0:T(8,128)(2,1)S(1)}, bf16[8,4096]{1,0:T(8,128)(2,1)S(1)}, u32[]{:S(2)}, u32[]{:S(2)}) collective-permute-start(bf16[8,4096]{1,0:T(8,128)(2,1)S(1)} %get-tuple-element.26), channel_id=1, source_target_pairs={{0,2},{1,3},{2,0},{3,1},{4,6},{5,7},{6,4},{7,5},{8,10},{9,11},{10,... | collective-permute-start | bytes 196616 | tf_op jit(solution)/shard_map/ppermute | solution.py:177
  19.2 2.2 %collective-permute-done.7.refs_0_ = bf16[8,4096]{1,0:T(8,128)(2,1)S(1)} collective-permute-done((bf16[8,4096]{1,0:T(8,128)(2,1)S(1)}, bf16[8,4096]{1,0:T(8,128)(2,1)S(1)}, u32[]{:S(2)}, u32[]{:S(2)}) %collective-permute-start.7) | collective-permute-done | bytes 65568 | tf_op jit(solution)/shard_map/ppermute | solution.py:177
  21.5 0.8 %collective-permute-start.8 = (bf16[4,4096]{1,0:T(4,128)(2,1)S(1)}, bf16[4,4096]{1,0:T(4,128)(2,1)S(1)}, u32[]{:S(2)}, u32[]{:S(2)}) collective-permute-start(bf16[4,4096]{1,0:T(4,128)(2,1)S(1)} %get-tuple-element.33), channel_id=1, source_target_pairs={{0,8},{4,12},{8,0},{12,4},{1,9},{5,13},{9,1},{13,5},{2,10},{6,14},... | collective-permute-start | bytes 98312 | tf_op jit(solution)/shard_map/ppermute | solution.py:189
  22.3 2.8 %collective-permute-start.9 = (bf16[4,4096]{1,0:T(4,128)(2,1)S(1)}, bf16[4,4096]{1,0:T(4,128)(2,1)S(1)}, u32[]{:S(2)}, u32[]{:S(2)}) collective-permute-start(bf16[4,4096]{1,0:T(4,128)(2,1)S(1)} %get-tuple-element.34), channel_id=1, source_target_pairs={{0,12},{4,8},{8,4},{12,0},{1,13},{5,9},{9,5},{13,1},{2,14},{6,10},... | collective-permute-start | bytes 98312 | tf_op jit(solution)/shard_map/ppermute | solution.py:189
  25.1 0.1 collective-permute-start.5
  25.2 1.3 %collective-permute-done.8.refs_2_ = bf16[4,4096]{1,0:T(4,128)(2,1)S(1)} collective-permute-done((bf16[4,4096]{1,0:T(4,128)(2,1)S(1)}, bf16[4,4096]{1,0:T(4,128)(2,1)S(1)}, u32[]{:S(2)}, u32[]{:S(2)}) %collective-permute-start.8) | collective-permute-done | bytes 32800 | tf_op jit(solution)/shard_map/ppermute | solution.py:189
  26.5 1.5 %collective-permute-done.9.refs_3_ = bf16[4,4096]{1,0:T(4,128)(2,1)S(1)} collective-permute-done((bf16[4,4096]{1,0:T(4,128)(2,1)S(1)}, bf16[4,4096]{1,0:T(4,128)(2,1)S(1)}, u32[]{:S(2)}, u32[]{:S(2)}) %collective-permute-start.9) | collective-permute-done | bytes 32800 | tf_op jit(solution)/shard_map/ppermute | solution.py:189
  28.0 1.1 %collective-permute-done.5.refs_1_ = bf16[4,4096]{1,0:T(4,128)(2,1)S(1)} collective-permute-done((bf16[4,4096]{1,0:T(4,128)(2,1)S(1)}, bf16[4,4096]{1,0:T(4,128)(2,1)S(1)}, u32[]{:S(2)}, u32[]{:S(2)}) %collective-permute-start.5) | collective-permute-done | bytes 32800 | tf_op jit(solution)/shard_map/ppermute | solution.py:189
  29.1 0.7 %mix.1 = bf16[4,4096]{1,0:T(4,128)(2,1)} custom-call(s32[2,16]{1,0:T(2,128)S(1)} %bitcast.2, f32[2,4]{1,0:T(2,128)S(1)} %bitcast.3, bf16[4,4096]{1,0:T(4,128)(2,1)S(1)} %get-tuple-element.27.refs_0_, bf16[4,4096]{1,0:T(4,128)(2,1)S(1)} %collective-permute-done.5.refs_1_, bf16[4,4096]{1,0:T(4,128)(2,1)S(1)} %collective-permute-done.8.refs_2_, ...), custom_call_target="tpu_custom_call" | custom-call | tf_op jit(solution)/shard_map/mix/pallas_call | solution.py:192
  (16 shorter events, 0.2 us)
Async XLA Ops:
  0.0 0.9 %copy-start.3 = (bf16[16,4096]{1,0:T(8,128)(2,1)S(1)}, bf16[16,4096]{1,0:T(8,128)(2,1)}, u32[]{:S(2)}) copy-start(bf16[16,4096]{1,0:T(8,128)(2,1)} %own) | copy-start | bytes 393220
  0.0 12.9 %copy-start = (bf16[1,384,4096]{2,1,0:T(8,128)(2,1)S(1)}, bf16[1,384,4096]{2,1,0:T(8,128)(2,1)}, u32[]{:S(2)}) copy-start(bf16[1,384,4096]{2,1,0:T(8,128)(2,1)} %w_down.1) | copy-start | bytes 9437188
  0.0 12.9 %copy-start.2 = (bf16[1,384,4096]{2,1,0:T(8,128)(2,1)S(1)}, bf16[1,384,4096]{2,1,0:T(8,128)(2,1)}, u32[]{:S(2)}) copy-start(bf16[1,384,4096]{2,1,0:T(8,128)(2,1)} %refs_3_.1) | copy-start | bytes 9437188
  0.0 12.9 %copy-start.1 = (bf16[1,384,4096]{2,1,0:T(8,128)(2,1)S(1)}, bf16[1,384,4096]{2,1,0:T(8,128)(2,1)}, u32[]{:S(2)}) copy-start(bf16[1,384,4096]{2,1,0:T(8,128)(2,1)} %refs_2_.1) | copy-start | bytes 9437188
  0.9 10.6 %collective-permute-start.1 = (bf16[16,4096]{1,0:T(8,128)(2,1)S(1)}, bf16[16,4096]{1,0:T(8,128)(2,1)S(1)}, u32[]{:S(2)}, u32[]{:S(2)}) collective-permute-start(bf16[16,4096]{1,0:T(8,128)(2,1)S(1)} %copy-done.3), channel_id=1, source_target_pairs={{0,8},{1,13},{2,10},{3,15},{4,12},{5,9},{6,14},{7,11},{8,0},{9,5},... | collective-permute-start | bytes 393224 | tf_op jit(solution)/shard_map/ppermute | solution.py:134
  4.9 7.4 %collective-permute-start = (bf16[16,4096]{1,0:T(8,128)(2,1)S(1)}, bf16[16,4096]{1,0:T(8,128)(2,1)S(1)}, u32[]{:S(2)}, u32[]{:S(2)}) collective-permute-start(bf16[16,4096]{1,0:T(8,128)(2,1)S(1)} %copy-done.3), channel_id=1, source_target_pairs={{0,4},{4,0},{8,12},{12,8},{1,5},{5,1},{9,13},{13,9},{2,6},{6,2},{1... | collective-permute-start | bytes 393224 | tf_op jit(solution)/shard_map/ppermute | solution.py:135
  11.5 1.3 %collective-permute-start.2 = (bf16[16,4096]{1,0:T(8,128)(2,1)S(1)}, bf16[16,4096]{1,0:T(8,128)(2,1)S(1)}, u32[]{:S(2)}, u32[]{:S(2)}) collective-permute-start(bf16[16,4096]{1,0:T(8,128)(2,1)S(1)} %collective-permute-done.1.refs_0_), channel_id=1, source_target_pairs={{0,1},{1,0},{2,3},{3,2},{4,5},{5,4},{6,7},{7,6},{8,9},{9,8},{10,11... | collective-permute-start | bytes 393224 | tf_op jit(solution)/shard_map/ppermute | solution.py:136
  15.4 13.7 %copy-start.4 = (s32[16,2]{0,1:T(2,128)S(1)}, s32[16,2]{0,1:T(2,128)}, u32[]{:S(2)}) copy-start(s32[16,2]{0,1:T(2,128)} %param.7) | copy-start | bytes 388
  15.4 13.7 %copy-start.5 = (f32[4,2]{0,1:T(2,128)S(1)}, f32[4,2]{0,1:T(2,128)}, u32[]{:S(2)}) copy-start(f32[4,2]{0,1:T(2,128)} %param.8) | copy-start | bytes 100
  15.4 1.4 %collective-permute-start.6 = (bf16[16,4096]{1,0:T(8,128)(2,1)S(1)}, bf16[16,4096]{1,0:T(8,128)(2,1)S(1)}, u32[]{:S(2)}, u32[]{:S(2)}) collective-permute-start(bf16[16,4096]{1,0:T(8,128)(2,1)S(1)} %get-tuple-element.30), channel_id=1, source_target_pairs={{0,1},{1,0},{2,3},{3,2},{4,5},{5,4},{6,7},{7,6},{8,9},{9,8},{10,11... | collective-permute-start | bytes 393224 | tf_op jit(solution)/shard_map/ppermute | solution.py:164
  16.3 2.1 %collective-permute-start.3 = (bf16[16,4096]{1,0:T(8,128)(2,1)S(1)}, bf16[16,4096]{1,0:T(8,128)(2,1)S(1)}, u32[]{:S(2)}, u32[]{:S(2)}) collective-permute-start(bf16[16,4096]{1,0:T(8,128)(2,1)S(1)} %get-tuple-element.24), channel_id=1, source_target_pairs={{0,1},{1,0},{2,3},{3,2},{4,5},{5,4},{6,7},{7,6},{8,9},{9,8},{10,11... | collective-permute-start | bytes 393224 | tf_op jit(solution)/shard_map/ppermute | solution.py:164
  16.9 4.6 %collective-permute-start.7 = (bf16[8,4096]{1,0:T(8,128)(2,1)S(1)}, bf16[8,4096]{1,0:T(8,128)(2,1)S(1)}, u32[]{:S(2)}, u32[]{:S(2)}) collective-permute-start(bf16[8,4096]{1,0:T(8,128)(2,1)S(1)} %get-tuple-element.32), channel_id=1, source_target_pairs={{0,2},{1,3},{2,0},{3,1},{4,6},{5,7},{6,4},{7,5},{8,10},{9,11},{10,... | collective-permute-start | bytes 196616 | tf_op jit(solution)/shard_map/ppermute | solution.py:177
  18.5 6.7 %collective-permute-start.4 = (bf16[8,4096]{1,0:T(8,128)(2,1)S(1)}, bf16[8,4096]{1,0:T(8,128)(2,1)S(1)}, u32[]{:S(2)}, u32[]{:S(2)}) collective-permute-start(bf16[8,4096]{1,0:T(8,128)(2,1)S(1)} %get-tuple-element.26), channel_id=1, source_target_pairs={{0,2},{1,3},{2,0},{3,1},{4,6},{5,7},{6,4},{7,5},{8,10},{9,11},{10,... | collective-permute-start | bytes 196616 | tf_op jit(solution)/shard_map/ppermute | solution.py:177
  21.5 5.0 %collective-permute-start.8 = (bf16[4,4096]{1,0:T(4,128)(2,1)S(1)}, bf16[4,4096]{1,0:T(4,128)(2,1)S(1)}, u32[]{:S(2)}, u32[]{:S(2)}) collective-permute-start(bf16[4,4096]{1,0:T(4,128)(2,1)S(1)} %get-tuple-element.33), channel_id=1, source_target_pairs={{0,8},{4,12},{8,0},{12,4},{1,9},{5,13},{9,1},{13,5},{2,10},{6,14},... | collective-permute-start | bytes 98312 | tf_op jit(solution)/shard_map/ppermute | solution.py:189
  22.3 5.7 %collective-permute-start.9 = (bf16[4,4096]{1,0:T(4,128)(2,1)S(1)}, bf16[4,4096]{1,0:T(4,128)(2,1)S(1)}, u32[]{:S(2)}, u32[]{:S(2)}) collective-permute-start(bf16[4,4096]{1,0:T(4,128)(2,1)S(1)} %get-tuple-element.34), channel_id=1, source_target_pairs={{0,12},{4,8},{8,4},{12,0},{1,13},{5,9},{9,5},{13,1},{2,14},{6,10},... | collective-permute-start | bytes 98312 | tf_op jit(solution)/shard_map/ppermute | solution.py:189
  25.1 4.0 %collective-permute-start.5 = (bf16[4,4096]{1,0:T(4,128)(2,1)S(1)}, bf16[4,4096]{1,0:T(4,128)(2,1)S(1)}, u32[]{:S(2)}, u32[]{:S(2)}) collective-permute-start(bf16[4,4096]{1,0:T(4,128)(2,1)S(1)} %get-tuple-element.28), channel_id=1, source_target_pairs={{0,4},{4,0},{8,12},{12,8},{1,5},{5,1},{9,13},{13,9},{2,6},{6,2},{1... | collective-permute-start | bytes 98312 | tf_op jit(solution)/shard_map/ppermute | solution.py:189

commit v8 on v7

--- a/solution.py
+++ b/solution.py
@@ -19,7 +19,7 @@
     core, pair = lax.rem(me, 2), lax.div(me, 2)
     place = lax.broadcasted_iota(jnp.int32, (total, total), 0)
     source = lax.broadcasted_iota(jnp.int32, (total, total), 1)
-    half = n_expert // 2
+    half, split = n_expert // 2, 2
     row = lax.rem(place, rows)
     k = lax.rem(lax.div(place, rows), half)
     h = lax.rem(lax.div(place, rows * half), pairs)
@@ -65,12 +65,15 @@
     down(parts, hidden[...], w_down, kept, sent)
 
 
-def add_kernel(kept, arrived, own, *pieces):
-    span = own.shape[0]
-    own[...] = kept[:span, :] + arrived[:span, :].astype(jnp.float32)
-    for i, piece in enumerate(pieces):
-        at = slice((i + 1) * span, (i + 2) * span)
-        piece[...] = (kept[at, :] + arrived[at, :].astype(jnp.float32)).astype(jnp.bfloat16)
+def add_kernel(parts, pairs, rows, kept, arrived, *refs):
+    count = kept.shape[0] // (pairs * rows)
+    take = count // parts
+    for h in range(pairs):
+        at = slice(h * count * rows, (h + 1) * count * rows)
+        total = kept[at, :] + arrived[at, :].astype(jnp.float32)
+        for i in range(parts):
+            out = refs[i * pairs + h]
+            out[...] = total[i * take * rows : (i + 1) * take * rows].astype(out.dtype)
 
 
 def fold_kernel(pairs, own, *refs):
@@ -158,32 +161,43 @@
         name="down",
     )(rest, w_down)
 
-    block = n_expert // 2 * rows
     pieces = []
-    for kept, sent in ((far_kept, far_sent), (near_kept, near_sent)):
+    half, split = n_expert // 2, 2
+    for far, sent in ((True, far_sent), (False, near_sent)):
         arrived = lax.ppermute(sent, "etp", swap)
-        own, *others = pl.pallas_call(
-            add_kernel,
-            out_shape=[jax.ShapeDtypeStruct((block, width), jnp.float32)]
-            + [jax.ShapeDtypeStruct((block, width), jnp.bfloat16)] * (pairs - 1),
+        kept = far_kept if far else near_kept
+        take = half // split
+        shape = (take * rows, width)
+        sums = pl.pallas_call(
+            functools.partial(add_kernel, split, pairs, rows),
+            out_shape=(
+                [jax.ShapeDtypeStruct(shape, jnp.float32)]
+                + [jax.ShapeDtypeStruct(shape, jnp.bfloat16)] * (pairs - 1)
+            )
+            * split,
             in_specs=[VMEM] * 2,
-            out_specs=[VMEM] * pairs,
+            out_specs=[VMEM] * (pairs * split),
             compiler_params=GRANT,
             name="add",
         )(kept, arrived)
-        landed = []
-        for h, piece in enumerate(others, 1):
-            route = [(t, 2 * ((t // 2 + h) % pairs) + t % 2) for t in range(n_etp)]
-            landed.append(lax.ppermute(piece, "etp", route))
-        folded = pl.pallas_call(
-            functools.partial(fold_kernel, pairs),
-            out_shape=[jax.ShapeDtypeStruct((rows, width), jnp.bfloat16)] * (n_expert // 2),
-            in_specs=[VMEM] * pairs,
-            out_specs=[VMEM] * (n_expert // 2),
-            compiler_params=GRANT,
-            name="fold",
-        )(own, *landed)
-        pieces = list(folded) + pieces
+        if far:
+            near_kept, sums = lax.optimization_barrier((near_kept, sums))
+        folded = []
+        for i in range(split):
+            own, *others = sums[i * pairs : (i + 1) * pairs]
+            landed = []
+            for h, piece in enumerate(others, 1):
+                route = [(t, 2 * ((t // 2 + h) % pairs) + t % 2) for t in range(n_etp)]
+                landed.append(lax.ppermute(piece, "etp", route))
+            folded += pl.pallas_call(
+                functools.partial(fold_kernel, pairs),
+                out_shape=[jax.ShapeDtypeStruct((rows, width), jnp.bfloat16)] * take,
+                in_specs=[VMEM] * pairs,
+                out_specs=[VMEM] * take,
+                compiler_params=GRANT,
+                name="fold",
+            )(own, *landed)
+        pieces = folded + pieces
     landed = []
     for k in range(n_expert - 1, 0, -1):
         landed.insert(0, lax.ppermute(pieces[k], "expert", [(e, e ^ k) for e in range(n_expert)]))

time: 30 us -> 30.2 us (level)
  starting transfers between devices: 12.3 us -> 14.2 us
  waiting for transfers between devices: 12.6 us -> 10.8 us
    ppermute x2 -> x4, starting transfers between devices: 2.35 us -> 4.18 us  [on_device(): landed.append(lax.ppermute(piece, 'etp', route))]
    ppermute x2 -> x4, waiting for transfers between devices: 2.2 us -> 0.42 us  [on_device(): landed.append(lax.ppermute(piece, 'etp', route))]
  transfers between devices with their start and end apart: 10 -> 12, of which waited for: 8 -> 8; matrix products, arithmetic and copies ran while one was open for 0% -> 0% of each run, Pallas kernels for 2% -> 3%
where the time goes in v8:
time: 30.2 us; the launch traced here: 30.1 us
  starting transfers between devices  14.2 us (47%)
  waiting for transfers between devices  10.8 us (36%)
  Pallas kernels  4.1 us (14%)
  local copies, waits for them, and re-layouts  0.87 us (3%)
    ppermute x1, waiting for transfers between devices, on_device(): far.append(lax.ppermute(tokens, ('expert', 'etp'), route))  5 us
    ppermute x4, starting transfers between devices, on_device(): landed.append(lax.ppermute(piece, 'etp', route))  4.18 us
    ppermute x1, starting transfers between devices, on_device(): far.append(lax.ppermute(tokens, ('expert', 'etp'), route))  4.04 us
    ppermute x3, waiting for transfers between devices, on_device(): lax.ppermute(pieces[k], 'expert', [(e, e ^ k) for e in range(n_expert)])  3.86 us
    ppermute x3, starting transfers between devices, on_device(): lax.ppermute(pieces[k], 'expert', [(e, e ^ k) for e in range(n_expert)])  3.82 us
    pallas_call x1, Pallas kernels, on_device(): pl.pallas_call(functools.partial(ffn_kernel, n_expert, parts), out_shape=...  2.52 us
    ppermute x1, starting transfers between devices, on_device(): lax.ppermute(tokens, 'expert', [(e, e ^ 1) for e in range(n_expert)])  1.58 us
    unnamed x12, local copies, waits for them, and re-layouts  0.87 us
  transfers between devices with their start and end apart: 12, of which 8 were waited for; matrix products, arithmetic and copies ran while one was open for 0% of the time, Pallas kernels for 3%

profile of v8, /device:TPU:0, one launch (start us, length us, event | category | flops | bytes accessed | tf_op | source)
XLA Modules:
  0.0 30.1 jit_solution(13148315848245694618)
XLA Ops:
  0.1 0.8 %copy-done.3 = bf16[16,4096]{1,0:T(8,128)(2,1)S(1)} copy-done((bf16[16,4096]{1,0:T(8,128)(2,1)S(1)}, bf16[16,4096]{1,0:T(8,128)(2,1)}, u32[]{:S(2)}) %copy-start.3) | copy-done | bytes 131096
  0.9 4.0 %collective-permute-start.1 = (bf16[16,4096]{1,0:T(8,128)(2,1)S(1)}, bf16[16,4096]{1,0:T(8,128)(2,1)S(1)}, u32[]{:S(2)}, u32[]{:S(2)}) collective-permute-start(bf16[16,4096]{1,0:T(8,128)(2,1)S(1)} %copy-done.3), channel_id=1, source_target_pairs={{0,8},{1,13},{2,10},{3,15},{4,12},{5,9},{6,14},{7,11},{8,0},{9,5},... | collective-permute-start | bytes 393224 | tf_op jit(solution)/shard_map/ppermute | solution.py:137
  4.9 1.6 %collective-permute-start = (bf16[16,4096]{1,0:T(8,128)(2,1)S(1)}, bf16[16,4096]{1,0:T(8,128)(2,1)S(1)}, u32[]{:S(2)}, u32[]{:S(2)}) collective-permute-start(bf16[16,4096]{1,0:T(8,128)(2,1)S(1)} %copy-done.3), channel_id=1, source_target_pairs={{0,4},{4,0},{8,12},{12,8},{1,5},{5,1},{9,13},{13,9},{2,6},{6,2},{1... | collective-permute-start | bytes 393224 | tf_op jit(solution)/shard_map/ppermute | solution.py:138
  6.5 5.0 %collective-permute-done.1.refs_0_ = bf16[16,4096]{1,0:T(8,128)(2,1)S(1)} collective-permute-done((bf16[16,4096]{1,0:T(8,128)(2,1)S(1)}, bf16[16,4096]{1,0:T(8,128)(2,1)S(1)}, u32[]{:S(2)}, u32[]{:S(2)}) %collective-permute-start.1) | collective-permute-done | bytes 131104 | tf_op jit(solution)/shard_map/ppermute | solution.py:137
  11.5 0.8 %collective-permute-done.next_block = bf16[16,4096]{1,0:T(8,128)(2,1)S(1)} collective-permute-done((bf16[16,4096]{1,0:T(8,128)(2,1)S(1)}, bf16[16,4096]{1,0:T(8,128)(2,1)S(1)}, u32[]{:S(2)}, u32[]{:S(2)}) %collective-permute-start) | collective-permute-done | bytes 131104 | tf_op jit(solution)/shard_map/ppermute | solution.py:138
  12.3 0.6 %collective-permute-done.2.refs_1_ = bf16[16,4096]{1,0:T(8,128)(2,1)S(1)} collective-permute-done((bf16[16,4096]{1,0:T(8,128)(2,1)S(1)}, bf16[16,4096]{1,0:T(8,128)(2,1)S(1)}, u32[]{:S(2)}, u32[]{:S(2)}) %collective-permute-start.2) | collective-permute-done | bytes 131104 | tf_op jit(solution)/shard_map/ppermute | solution.py:139
  12.9 2.5 %ffn.1 = (f32[16,4096]{1,0:T(8,128)S(1)}, bf16[16,4096]{1,0:T(8,128)(2,1)S(1)}, bf16[32,384]{1,0:T(8,128)(2,1)S(1)}) custom-call(bf16[16,4096]{1,0:T(8,128)(2,1)S(1)} %copy-done.3, bf16[16,4096]{1,0:T(8,128)(2,1)S(1)} %collective-permute-done.next_block, bf16[64,64]{1,0:T(8,128)(2,1)S(1)} %order.1, bf16[16,4096]{1,0:T(8,128)(2,1)S(1)} %collective-permute-done.1.refs_0_, ...), custom_call_target="tpu_custom_call" | custom-call | tf_op jit(solution)/shard_map/ffn/pallas_call | solution.py:146
  15.4 0.0 copy-start.5
  15.4 0.2 collective-permute-start.3
  15.6 0.6 %down.1 = (f32[16,4096]{1,0:T(8,128)S(1)}, bf16[16,4096]{1,0:T(8,128)(2,1)S(1)}) custom-call(bf16[32,384]{1,0:T(8,128)(2,1)S(1)} %get-tuple-element.27.hidden, bf16[1,384,4096]{2,1,0:T(8,128)(2,1)S(1)} %copy-done), custom_call_target="tpu_custom_call" | custom-call | tf_op jit(solution)/shard_map/down/pallas_call | solution.py:155
  16.3 0.4 %collective-permute-start.4 = (bf16[16,4096]{1,0:T(8,128)(2,1)S(1)}, bf16[16,4096]{1,0:T(8,128)(2,1)S(1)}, u32[]{:S(2)}, u32[]{:S(2)}) collective-permute-start(bf16[16,4096]{1,0:T(8,128)(2,1)S(1)} %get-tuple-element.36), channel_id=1, source_target_pairs={{0,1},{1,0},{2,3},{3,2},{4,5},{5,4},{6,7},{7,6},{8,9},{9,8},{10,11... | collective-permute-start | bytes 393224 | tf_op jit(solution)/shard_map/ppermute | solution.py:167
  16.7 0.2 collective-permute-done.3.arrived
  16.9 1.6 %collective-permute-start.8 = (bf16[4,4096]{1,0:T(4,128)(2,1)S(1)}, bf16[4,4096]{1,0:T(4,128)(2,1)S(1)}, u32[]{:S(2)}, u32[]{:S(2)}) collective-permute-start(bf16[4,4096]{1,0:T(4,128)(2,1)S(1)} %get-tuple-element.42), channel_id=1, source_target_pairs={{0,2},{1,3},{2,0},{3,1},{4,6},{5,7},{6,4},{7,5},{8,10},{9,11},{10,... | collective-permute-start | bytes 98312 | tf_op jit(solution)/shard_map/ppermute | solution.py:191
  18.4 0.5 %collective-permute-start.10 = (bf16[4,4096]{1,0:T(4,128)(2,1)S(1)}, bf16[4,4096]{1,0:T(4,128)(2,1)S(1)}, u32[]{:S(2)}, u32[]{:S(2)}) collective-permute-start(bf16[4,4096]{1,0:T(4,128)(2,1)S(1)} %get-tuple-element.44), channel_id=1, source_target_pairs={{0,2},{1,3},{2,0},{3,1},{4,6},{5,7},{6,4},{7,5},{8,10},{9,11},{10,... | collective-permute-start | bytes 98312 | tf_op jit(solution)/shard_map/ppermute | solution.py:191
  19.0 1.6 %collective-permute-start.6 = (bf16[4,4096]{1,0:T(4,128)(2,1)S(1)}, bf16[4,4096]{1,0:T(4,128)(2,1)S(1)}, u32[]{:S(2)}, u32[]{:S(2)}) collective-permute-start(bf16[4,4096]{1,0:T(4,128)(2,1)S(1)} %get-tuple-element.40), channel_id=1, source_target_pairs={{0,2},{1,3},{2,0},{3,1},{4,6},{5,7},{6,4},{7,5},{8,10},{9,11},{10,... | collective-permute-start | bytes 98312 | tf_op jit(solution)/shard_map/ppermute | solution.py:191
  20.6 0.5 %collective-permute-start.5 = (bf16[4,4096]{1,0:T(4,128)(2,1)S(1)}, bf16[4,4096]{1,0:T(4,128)(2,1)S(1)}, u32[]{:S(2)}, u32[]{:S(2)}) collective-permute-start(bf16[4,4096]{1,0:T(4,128)(2,1)S(1)} %get-tuple-element.38), channel_id=1, source_target_pairs={{0,2},{1,3},{2,0},{3,1},{4,6},{5,7},{6,4},{7,5},{8,10},{9,11},{10,... | collective-permute-start | bytes 98312 | tf_op jit(solution)/shard_map/ppermute | solution.py:191
  21.1 0.8 %collective-permute-start.9 = (bf16[4,4096]{1,0:T(4,128)(2,1)S(1)}, bf16[4,4096]{1,0:T(4,128)(2,1)S(1)}, u32[]{:S(2)}, u32[]{:S(2)}) collective-permute-start(bf16[4,4096]{1,0:T(4,128)(2,1)S(1)} %fold.6), channel_id=1, source_target_pairs={{0,8},{4,12},{8,0},{12,4},{1,9},{5,13},{9,1},{13,5},{2,10},{6,14},... | collective-permute-start | bytes 98312 | tf_op jit(solution)/shard_map/ppermute | solution.py:203
  21.9 0.4 %collective-permute-done.10.refs_0_ = bf16[4,4096]{1,0:T(4,128)(2,1)S(1)} collective-permute-done((bf16[4,4096]{1,0:T(4,128)(2,1)S(1)}, bf16[4,4096]{1,0:T(4,128)(2,1)S(1)}, u32[]{:S(2)}, u32[]{:S(2)}) %collective-permute-start.10) | collective-permute-done | bytes 32800 | tf_op jit(solution)/shard_map/ppermute | solution.py:191
  22.4 2.9 %collective-permute-start.11 = (bf16[4,4096]{1,0:T(4,128)(2,1)S(1)}, bf16[4,4096]{1,0:T(4,128)(2,1)S(1)}, u32[]{:S(2)}, u32[]{:S(2)}) collective-permute-start(bf16[4,4096]{1,0:T(4,128)(2,1)S(1)} %fold.7), channel_id=1, source_target_pairs={{0,12},{4,8},{8,4},{12,0},{1,13},{5,9},{9,5},{13,1},{2,14},{6,10},... | collective-permute-start | bytes 98312 | tf_op jit(solution)/shard_map/ppermute | solution.py:203
  25.3 0.1 collective-permute-start.7
  25.4 1.6 %collective-permute-done.9.refs_2_ = bf16[4,4096]{1,0:T(4,128)(2,1)S(1)} collective-permute-done((bf16[4,4096]{1,0:T(4,128)(2,1)S(1)}, bf16[4,4096]{1,0:T(4,128)(2,1)S(1)}, u32[]{:S(2)}, u32[]{:S(2)}) %collective-permute-start.9) | collective-permute-done | bytes 32800 | tf_op jit(solution)/shard_map/ppermute | solution.py:203
  27.0 1.2 %collective-permute-done.11.refs_3_ = bf16[4,4096]{1,0:T(4,128)(2,1)S(1)} collective-permute-done((bf16[4,4096]{1,0:T(4,128)(2,1)S(1)}, bf16[4,4096]{1,0:T(4,128)(2,1)S(1)}, u32[]{:S(2)}, u32[]{:S(2)}) %collective-permute-start.11) | collective-permute-done | bytes 32800 | tf_op jit(solution)/shard_map/ppermute | solution.py:203
  28.2 1.1 %collective-permute-done.7.refs_1_ = bf16[4,4096]{1,0:T(4,128)(2,1)S(1)} collective-permute-done((bf16[4,4096]{1,0:T(4,128)(2,1)S(1)}, bf16[4,4096]{1,0:T(4,128)(2,1)S(1)}, u32[]{:S(2)}, u32[]{:S(2)}) %collective-permute-start.7) | collective-permute-done | bytes 32800 | tf_op jit(solution)/shard_map/ppermute | solution.py:203
  29.3 0.7 %mix.1 = bf16[4,4096]{1,0:T(4,128)(2,1)} custom-call(s32[2,16]{1,0:T(2,128)S(1)} %bitcast.2, f32[2,4]{1,0:T(2,128)S(1)} %bitcast.3, bf16[4,4096]{1,0:T(4,128)(2,1)S(1)} %fold.4.refs_0_, bf16[4,4096]{1,0:T(4,128)(2,1)S(1)} %collective-permute-done.7.refs_1_, bf16[4,4096]{1,0:T(4,128)(2,1)S(1)} %collective-permute-done.9.refs_2_, ...), custom_call_target="tpu_custom_call" | custom-call | tf_op jit(solution)/shard_map/mix/pallas_call | solution.py:206
  (22 shorter events, 0.2 us)
Async XLA Ops:
  0.0 0.9 %copy-start.3 = (bf16[16,4096]{1,0:T(8,128)(2,1)S(1)}, bf16[16,4096]{1,0:T(8,128)(2,1)}, u32[]{:S(2)}) copy-start(bf16[16,4096]{1,0:T(8,128)(2,1)} %own) | copy-start | bytes 393220
  0.0 12.9 %copy-start = (bf16[1,384,4096]{2,1,0:T(8,128)(2,1)S(1)}, bf16[1,384,4096]{2,1,0:T(8,128)(2,1)}, u32[]{:S(2)}) copy-start(bf16[1,384,4096]{2,1,0:T(8,128)(2,1)} %w_down.1) | copy-start | bytes 9437188
  0.0 12.9 %copy-start.2 = (bf16[1,384,4096]{2,1,0:T(8,128)(2,1)S(1)}, bf16[1,384,4096]{2,1,0:T(8,128)(2,1)}, u32[]{:S(2)}) copy-start(bf16[1,384,4096]{2,1,0:T(8,128)(2,1)} %refs_3_.1) | copy-start | bytes 9437188
  0.0 12.9 %copy-start.1 = (bf16[1,384,4096]{2,1,0:T(8,128)(2,1)S(1)}, bf16[1,384,4096]{2,1,0:T(8,128)(2,1)}, u32[]{:S(2)}) copy-start(bf16[1,384,4096]{2,1,0:T(8,128)(2,1)} %refs_2_.1) | copy-start | bytes 9437188
  0.9 10.6 %collective-permute-start.1 = (bf16[16,4096]{1,0:T(8,128)(2,1)S(1)}, bf16[16,4096]{1,0:T(8,128)(2,1)S(1)}, u32[]{:S(2)}, u32[]{:S(2)}) collective-permute-start(bf16[16,4096]{1,0:T(8,128)(2,1)S(1)} %copy-done.3), channel_id=1, source_target_pairs={{0,8},{1,13},{2,10},{3,15},{4,12},{5,9},{6,14},{7,11},{8,0},{9,5},... | collective-permute-start | bytes 393224 | tf_op jit(solution)/shard_map/ppermute | solution.py:137
  4.9 7.4 %collective-permute-start = (bf16[16,4096]{1,0:T(8,128)(2,1)S(1)}, bf16[16,4096]{1,0:T(8,128)(2,1)S(1)}, u32[]{:S(2)}, u32[]{:S(2)}) collective-permute-start(bf16[16,4096]{1,0:T(8,128)(2,1)S(1)} %copy-done.3), channel_id=1, source_target_pairs={{0,4},{4,0},{8,12},{12,8},{1,5},{5,1},{9,13},{13,9},{2,6},{6,2},{1... | collective-permute-start | bytes 393224 | tf_op jit(solution)/shard_map/ppermute | solution.py:138
  11.5 1.3 %collective-permute-start.2 = (bf16[16,4096]{1,0:T(8,128)(2,1)S(1)}, bf16[16,4096]{1,0:T(8,128)(2,1)S(1)}, u32[]{:S(2)}, u32[]{:S(2)}) collective-permute-start(bf16[16,4096]{1,0:T(8,128)(2,1)S(1)} %collective-permute-done.1.refs_0_), channel_id=1, source_target_pairs={{0,1},{1,0},{2,3},{3,2},{4,5},{5,4},{6,7},{7,6},{8,9},{9,8},{10,11... | collective-permute-start | bytes 393224 | tf_op jit(solution)/shard_map/ppermute | solution.py:139
  15.4 13.9 %copy-start.4 = (s32[16,2]{0,1:T(2,128)S(1)}, s32[16,2]{0,1:T(2,128)}, u32[]{:S(2)}) copy-start(s32[16,2]{0,1:T(2,128)} %param.7) | copy-start | bytes 388
  15.4 13.9 %copy-start.5 = (f32[4,2]{0,1:T(2,128)S(1)}, f32[4,2]{0,1:T(2,128)}, u32[]{:S(2)}) copy-start(f32[4,2]{0,1:T(2,128)} %param.8) | copy-start | bytes 100
  15.4 1.4 %collective-permute-start.3 = (bf16[16,4096]{1,0:T(8,128)(2,1)S(1)}, bf16[16,4096]{1,0:T(8,128)(2,1)S(1)}, u32[]{:S(2)}, u32[]{:S(2)}) collective-permute-start(bf16[16,4096]{1,0:T(8,128)(2,1)S(1)} %get-tuple-element.30), channel_id=1, source_target_pairs={{0,1},{1,0},{2,3},{3,2},{4,5},{5,4},{6,7},{7,6},{8,9},{9,8},{10,11... | collective-permute-start | bytes 393224 | tf_op jit(solution)/shard_map/ppermute | solution.py:167
  16.3 2.7 %collective-permute-start.4 = (bf16[16,4096]{1,0:T(8,128)(2,1)S(1)}, bf16[16,4096]{1,0:T(8,128)(2,1)S(1)}, u32[]{:S(2)}, u32[]{:S(2)}) collective-permute-start(bf16[16,4096]{1,0:T(8,128)(2,1)S(1)} %get-tuple-element.36), channel_id=1, source_target_pairs={{0,1},{1,0},{2,3},{3,2},{4,5},{5,4},{6,7},{7,6},{8,9},{9,8},{10,11... | collective-permute-start | bytes 393224 | tf_op jit(solution)/shard_map/ppermute | solution.py:167
  16.9 4.2 %collective-permute-start.8 = (bf16[4,4096]{1,0:T(4,128)(2,1)S(1)}, bf16[4,4096]{1,0:T(4,128)(2,1)S(1)}, u32[]{:S(2)}, u32[]{:S(2)}) collective-permute-start(bf16[4,4096]{1,0:T(4,128)(2,1)S(1)} %get-tuple-element.42), channel_id=1, source_target_pairs={{0,2},{1,3},{2,0},{3,1},{4,6},{5,7},{6,4},{7,5},{8,10},{9,11},{10,... | collective-permute-start | bytes 98312 | tf_op jit(solution)/shard_map/ppermute | solution.py:191
  18.4 3.9 %collective-permute-start.10 = (bf16[4,4096]{1,0:T(4,128)(2,1)S(1)}, bf16[4,4096]{1,0:T(4,128)(2,1)S(1)}, u32[]{:S(2)}, u32[]{:S(2)}) collective-permute-start(bf16[4,4096]{1,0:T(4,128)(2,1)S(1)} %get-tuple-element.44), channel_id=1, source_target_pairs={{0,2},{1,3},{2,0},{3,1},{4,6},{5,7},{6,4},{7,5},{8,10},{9,11},{10,... | collective-permute-start | bytes 98312 | tf_op jit(solution)/shard_map/ppermute | solution.py:191
  19.0 6.3 %collective-permute-start.6 = (bf16[4,4096]{1,0:T(4,128)(2,1)S(1)}, bf16[4,4096]{1,0:T(4,128)(2,1)S(1)}, u32[]{:S(2)}, u32[]{:S(2)}) collective-permute-start(bf16[4,4096]{1,0:T(4,128)(2,1)S(1)} %get-tuple-element.40), channel_id=1, source_target_pairs={{0,2},{1,3},{2,0},{3,1},{4,6},{5,7},{6,4},{7,5},{8,10},{9,11},{10,... | collective-permute-start | bytes 98312 | tf_op jit(solution)/shard_map/ppermute | solution.py:191
  20.6 4.8 %collective-permute-start.5 = (bf16[4,4096]{1,0:T(4,128)(2,1)S(1)}, bf16[4,4096]{1,0:T(4,128)(2,1)S(1)}, u32[]{:S(2)}, u32[]{:S(2)}) collective-permute-start(bf16[4,4096]{1,0:T(4,128)(2,1)S(1)} %get-tuple-element.38), channel_id=1, source_target_pairs={{0,2},{1,3},{2,0},{3,1},{4,6},{5,7},{6,4},{7,5},{8,10},{9,11},{10,... | collective-permute-start | bytes 98312 | tf_op jit(solution)/shard_map/ppermute | solution.py:191
  21.1 5.9 %collective-permute-start.9 = (bf16[4,4096]{1,0:T(4,128)(2,1)S(1)}, bf16[4,4096]{1,0:T(4,128)(2,1)S(1)}, u32[]{:S(2)}, u32[]{:S(2)}) collective-permute-start(bf16[4,4096]{1,0:T(4,128)(2,1)S(1)} %fold.6), channel_id=1, source_target_pairs={{0,8},{4,12},{8,0},{12,4},{1,9},{5,13},{9,1},{13,5},{2,10},{6,14},... | collective-permute-start | bytes 98312 | tf_op jit(solution)/shard_map/ppermute | solution.py:203
  22.4 5.9 %collective-permute-start.11 = (bf16[4,4096]{1,0:T(4,128)(2,1)S(1)}, bf16[4,4096]{1,0:T(4,128)(2,1)S(1)}, u32[]{:S(2)}, u32[]{:S(2)}) collective-permute-start(bf16[4,4096]{1,0:T(4,128)(2,1)S(1)} %fold.7), channel_id=1, source_target_pairs={{0,12},{4,8},{8,4},{12,0},{1,13},{5,9},{9,5},{13,1},{2,14},{6,10},... | collective-permute-start | bytes 98312 | tf_op jit(solution)/shard_map/ppermute | solution.py:203
  25.3 4.0 %collective-permute-start.7 = (bf16[4,4096]{1,0:T(4,128)(2,1)S(1)}, bf16[4,4096]{1,0:T(4,128)(2,1)S(1)}, u32[]{:S(2)}, u32[]{:S(2)}) collective-permute-start(bf16[4,4096]{1,0:T(4,128)(2,1)S(1)} %fold.5), channel_id=1, source_target_pairs={{0,4},{4,0},{8,12},{12,8},{1,5},{5,1},{9,13},{13,9},{2,6},{6,2},{1... | collective-permute-start | bytes 98312 | tf_op jit(solution)/shard_map/ppermute | solution.py:203

commit v9 on v7

--- a/solution.py
+++ b/solution.py
@@ -13,7 +13,22 @@
 HBM = pl.BlockSpec(memory_space=pltpu.HBM)
 
 
-def order_kernel(n_expert, pairs, rows, out):
+def fetch_kernel(tokens, first, second, mine, sems):
+    half = first.shape[1]
+    core = lax.rem(lax.axis_index("etp"), 2)
+    starts = (0, half, pl.multiple_of(core * half, half))
+    copies = [
+        pltpu.make_async_copy(tokens.at[:, pl.ds(start, half)], out, sems.at[i])
+        for i, (start, out) in enumerate(zip(starts, (first, second, mine)))
+    ]
+    for copy in copies:
+        copy.start()
+    for copy in copies:
+        copy.wait()
+
+
+def order_kernel(n_expert, pairs, rows, first, out):
+    del first
     total = out.shape[0]
     me = lax.axis_index("etp")
     core, pair = lax.rem(me, 2), lax.div(me, 2)
@@ -30,21 +45,39 @@
     out[...] = jnp.where(source == wanted, 1.0, 0.0).astype(jnp.bfloat16)
 
 
-def ffn_kernel(n_expert, parts, own, next_block, order, *refs):
-    far = refs[: n_expert - 2]
-    w_gate, w_up, w_down, kept, sent, rest, x = refs[n_expert - 2 :]
+CONTRACT = (((1,), (1,)), ((), ()))
+
+
+def gate_up(part, own, next_block, next_swapped, far, w_gate, w_up, x):
     core = lax.rem(lax.axis_index("etp"), 2)
-    tok = own.shape[0]
+    tok, half = own.shape
     x[0:tok, :] = own[...]
-    x[tok : 2 * tok, :] = next_block[...]
-    for i in range(0, n_expert - 2, 2):
+    x[tok : 2 * tok, :] = jnp.where(core == part, next_block[...], next_swapped[...])
+    for i in range(0, len(far), 2):
         for block, k in ((far[i], i + 2 + core), (far[i + 1], i + 3 - core)):
             x[pl.ds(pl.multiple_of(k * tok, tok), tok), :] = block[...]
-    contract = (((1,), (1,)), ((), ()))
-    gate = lax.dot_general(w_gate[0], x[...], contract, preferred_element_type=jnp.float32)
-    upper = lax.dot_general(w_up[0], x[...], contract, preferred_element_type=jnp.float32)
+    cols = slice(part * half, (part + 1) * half)
+    return [
+        lax.dot_general(w[0, :, cols], x[...], CONTRACT, preferred_element_type=jnp.float32)
+        for w in (w_gate, w_up)
+    ]
+
+
+def first_kernel(own, next_block, next_swapped, *refs):
+    far, (w_gate, w_up, gate, upper, x) = refs[:-5], refs[-5:]
+    gate[...], upper[...] = gate_up(
+        0, own, next_block, next_swapped, far, w_gate, w_up, x
+    )
+
+
+def second_kernel(parts, own, next_block, next_swapped, *refs):
+    far, refs = refs[:-10], refs[-10:]
+    w_gate, w_up, gate, upper, order, w_down, kept, sent, rest, x = refs
+    more_gate, more_upper = gate_up(1, own, next_block, next_swapped, far, w_gate, w_up, x)
+    gate = gate[...] + more_gate
+    upper = upper[...] + more_upper
     hidden = (gate / (1.0 + jnp.exp(-gate)) * upper).astype(jnp.bfloat16)
-    hidden = lax.dot_general(order[...], hidden, contract, preferred_element_type=jnp.float32)
+    hidden = lax.dot_general(order[...], hidden, CONTRACT, preferred_element_type=jnp.float32)
     hidden = hidden.astype(jnp.bfloat16)
     now = rest.shape[0]
     rest[...] = hidden[now:]
@@ -113,42 +146,70 @@
     pairs = n_etp // 2
     side = n_expert * tok // 2
 
+    column_half = jax.ShapeDtypeStruct((tok, width // 2), tokens.dtype)
+    first, second, mine = pl.pallas_call(
+        fetch_kernel,
+        out_shape=[column_half] * 3,
+        in_specs=[HBM],
+        out_specs=[VMEM] * 3,
+        scratch_shapes=[pltpu.SemaphoreType.DMA((3,))],
+        compiler_params=GRANT,
+        name="fetch",
+    )(pltpu.with_memory_space_constraint(tokens, pltpu.HBM))
     order = pl.pallas_call(
         functools.partial(order_kernel, n_expert, pairs, rows),
         out_shape=jax.ShapeDtypeStruct((2 * side, 2 * side), jnp.bfloat16),
+        in_specs=[VMEM],
         out_specs=VMEM,
         cost_estimate=AHEAD,
         compiler_params=GRANT,
         name="order",
-    )()
-    tokens, order = lax.optimization_barrier((tokens, order))
+    )(first)
+    first, second, mine, order = lax.optimization_barrier((first, second, mine, order))
 
     swap = [(t, t ^ 1) for t in range(n_etp)]
-    far = []
-    for k in range(2, n_expert, 2):
-        route = [
+    routes = [
+        [
             (e * n_etp + t, (e ^ (k + t % 2)) * n_etp + t)
             for e in range(n_expert)
             for t in range(n_etp)
         ]
-        far.append(lax.ppermute(tokens, ("expert", "etp"), route))
-    next_block = lax.ppermute(tokens, "expert", [(e, e ^ 1) for e in range(n_expert)])
-    far = [b for block in far for b in (block, lax.ppermute(block, "etp", swap))]
+        for k in range(2, n_expert, 2)
+    ]
+
+    def exchange(block, axes, route):
+        block = lax.ppermute(block, axes, route)
+        return [block, lax.ppermute(block, "etp", swap)]
+
+    far_first = [b for route in routes for b in exchange(first, ("expert", "etp"), route)]
+    near = exchange(mine, "expert", [(e, e ^ 1) for e in range(n_expert)])
+    far_second = [b for route in routes for b in exchange(second, ("expert", "etp"), route)]
 
     parts = 4
+    hidden = w_gate.shape[1]
+    scratch = [pltpu.VMEM((n_expert * tok, width // 2), jnp.bfloat16)]
+    gate, upper = pl.pallas_call(
+        first_kernel,
+        out_shape=[jax.ShapeDtypeStruct((hidden, n_expert * tok), jnp.float32)] * 2,
+        in_specs=[VMEM] * (n_expert + 3),
+        out_specs=[VMEM] * 2,
+        scratch_shapes=scratch,
+        compiler_params=GRANT,
+        name="first",
+    )(first, *near, *far_first, w_gate, w_up)
     halves = [
         jax.ShapeDtypeStruct((side // 2, width), jnp.float32),
         jax.ShapeDtypeStruct((side // 2, width), jnp.bfloat16),
     ]
     far_kept, far_sent, rest = pl.pallas_call(
-        functools.partial(ffn_kernel, n_expert, parts),
-        out_shape=halves + [jax.ShapeDtypeStruct((side, w_gate.shape[1]), jnp.bfloat16)],
-        in_specs=[VMEM] * (n_expert + 4),
+        functools.partial(second_kernel, parts),
+        out_shape=halves + [jax.ShapeDtypeStruct((side, hidden), jnp.bfloat16)],
+        in_specs=[VMEM] * (n_expert + 7),
         out_specs=[VMEM] * 3,
-        scratch_shapes=[pltpu.VMEM((n_expert * tok, width), jnp.bfloat16)],
-        compiler_params=GRANT,
-        name="ffn",
-    )(tokens, next_block, order, *far, w_gate, w_up, w_down)
+        scratch_shapes=scratch,
+        compiler_params=GRANT,
+        name="second",
+    )(second, *near, *far_second, w_gate, w_up, gate, upper, order, w_down)
     near_kept, near_sent = pl.pallas_call(
         functools.partial(down_kernel, parts),
         out_shape=halves,

time: 30 us -> 29.8 us (level)
  Pallas kernels: 4.06 us -> 5.17 us
  local copies, waits for them, and re-layouts: 0.87 us -> 0.03 us
  waiting for transfers between devices: 12.6 us -> 11.8 us
    ppermute x3, waiting for transfers between devices: 3.9 us -> 2.67 us  [on_device(): lax.ppermute(pieces[k], 'expert', [(e, e ^ k) for e in range(n_expert)])]
    pallas_call x1 -> x3, Pallas kernels: 2.52 us -> 3.63 us  [the longest x1 1.73 us: on_device(): pl.pallas_call(functools.partial(second_kernel, parts), out_shape=halves...]
    unnamed x12 -> x10, local copies, waits for them, and re-layouts: 0.87 us -> 0.03 us
    ppermute x3 -> x6, starting transfers between devices: 5.62 us -> 6.02 us  [the longest x3 6.01 us: exchange(): block = lax.ppermute(block, axes, route)]
    ppermute x3 -> x6, waiting for transfers between devices: 6.34 us -> 6.71 us  [the longest x3 6.15 us: exchange(): block = lax.ppermute(block, axes, route)]
  transfers between devices with their start and end apart: 10 -> 13, of which waited for: 8 -> 8; matrix products, arithmetic and copies ran while one was open for 0% -> 0% of each run, Pallas kernels for 2% -> 6%
where the time goes in v9:
time: 29.8 us; the launch traced here: 29.7 us
  starting transfers between devices  12.6 us (42%)
  waiting for transfers between devices  11.8 us (40%)
  Pallas kernels  5.17 us (17%)
    ppermute x3, waiting for transfers between devices, exchange(): block = lax.ppermute(block, axes, route)  6.15 us
    ppermute x3, starting transfers between devices, exchange(): block = lax.ppermute(block, axes, route)  6.01 us
    ppermute x3, starting transfers between devices, on_device(): lax.ppermute(pieces[k], 'expert', [(e, e ^ k) for e in range(n_expert)])  3.61 us
    ppermute x3, waiting for transfers between devices, on_device(): lax.ppermute(pieces[k], 'expert', [(e, e ^ k) for e in range(n_expert)])  2.67 us
    ppermute x2, starting transfers between devices, on_device(): landed.append(lax.ppermute(piece, 'etp', route))  2.34 us
    ppermute x2, waiting for transfers between devices, on_device(): landed.append(lax.ppermute(piece, 'etp', route))  2.23 us
    pallas_call x1, Pallas kernels, on_device(): pl.pallas_call(functools.partial(second_kernel, parts), out_shape=halves...  1.73 us
    pallas_call x1, Pallas kernels, on_device(): pl.pallas_call(first_kernel, out_shape=[jax.ShapeDtypeStruct((hidden, n_e...  0.97 us
  transfers between devices with their start and end apart: 13, of which 8 were waited for; matrix products, arithmetic and copies ran while one was open for 0% of the time, Pallas kernels for 6%

profile of v9, /device:TPU:0, one launch (start us, length us, event | category | flops | bytes accessed | tf_op | source)
XLA Modules:
  0.0 29.7 jit_solution(12394985065181204814)
XLA Ops:
  0.0 0.9 %fetch.1 = (bf16[16,2048]{1,0:T(8,128)(2,1)S(1)}, bf16[16,2048]{1,0:T(8,128)(2,1)S(1)}, bf16[16,2048]{1,0:T(8,128)(2,1)S(1)}) custom-call(bf16[16,4096]{1,0:T(8,128)(2,1)} %tokens.1), custom_call_target="tpu_custom_call" | custom-call | tf_op jit(solution)/shard_map/fetch/pallas_call | solution.py:150
  1.0 3.1 %collective-permute-start = (bf16[16,2048]{1,0:T(8,128)(2,1)S(1)}, bf16[16,2048]{1,0:T(8,128)(2,1)S(1)}, u32[]{:S(2)}, u32[]{:S(2)}) collective-permute-start(bf16[16,2048]{1,0:T(8,128)(2,1)S(1)} %get-tuple-element.31), channel_id=1, source_target_pairs={{0,4},{4,0},{8,12},{12,8},{1,5},{5,1},{9,13},{13,9},{2,6},{6,2},{1... | collective-permute-start | bytes 196616 | tf_op jit(solution)/shard_map/ppermute | solution.py:181
  4.1 2.6 %collective-permute-start.4 = (bf16[16,2048]{1,0:T(8,128)(2,1)S(1)}, bf16[16,2048]{1,0:T(8,128)(2,1)S(1)}, u32[]{:S(2)}, u32[]{:S(2)}) collective-permute-start(bf16[16,2048]{1,0:T(8,128)(2,1)S(1)} %get-tuple-element.32.first.own), channel_id=1, source_target_pairs={{0,8},{1,13},{2,10},{3,15},{4,12},{5,9},{6,14},{7,11},{8,0},{9,5},... | collective-permute-start | bytes 196616 | tf_op jit(solution)/shard_map/ppermute | solution.py:181
  6.7 0.3 %collective-permute-start.2 = (bf16[16,2048]{1,0:T(8,128)(2,1)S(1)}, bf16[16,2048]{1,0:T(8,128)(2,1)S(1)}, u32[]{:S(2)}, u32[]{:S(2)}) collective-permute-start(bf16[16,2048]{1,0:T(8,128)(2,1)S(1)} %get-tuple-element.30.own), channel_id=1, source_target_pairs={{0,8},{1,13},{2,10},{3,15},{4,12},{5,9},{6,14},{7,11},{8,0},{9,5},... | collective-permute-start | bytes 196616 | tf_op jit(solution)/shard_map/ppermute | solution.py:181
  7.1 5.5 %collective-permute-done.4.refs_0_ = bf16[16,2048]{1,0:T(8,128)(2,1)S(1)} collective-permute-done((bf16[16,2048]{1,0:T(8,128)(2,1)S(1)}, bf16[16,2048]{1,0:T(8,128)(2,1)S(1)}, u32[]{:S(2)}, u32[]{:S(2)}) %collective-permute-start.4) | collective-permute-done | bytes 65568 | tf_op jit(solution)/shard_map/ppermute | solution.py:181
  12.5 0.7 %collective-permute-done.2.refs_0_ = bf16[16,2048]{1,0:T(8,128)(2,1)S(1)} collective-permute-done((bf16[16,2048]{1,0:T(8,128)(2,1)S(1)}, bf16[16,2048]{1,0:T(8,128)(2,1)S(1)}, u32[]{:S(2)}, u32[]{:S(2)}) %collective-permute-start.2) | collective-permute-done | bytes 65568 | tf_op jit(solution)/shard_map/ppermute | solution.py:181
  13.2 0.5 %collective-permute-done.5.refs_1_ = bf16[16,2048]{1,0:T(8,128)(2,1)S(1)} collective-permute-done((bf16[16,2048]{1,0:T(8,128)(2,1)S(1)}, bf16[16,2048]{1,0:T(8,128)(2,1)S(1)}, u32[]{:S(2)}, u32[]{:S(2)}) %collective-permute-start.5) | collective-permute-done | bytes 65568 | tf_op jit(solution)/shard_map/ppermute | solution.py:182
  13.8 1.0 %first.1 = (f32[384,64]{1,0:T(8,128)S(1)}, f32[384,64]{1,0:T(8,128)S(1)}) custom-call(bf16[16,2048]{1,0:T(8,128)(2,1)S(1)} %get-tuple-element.32.first.own, bf16[16,2048]{1,0:T(8,128)(2,1)S(1)} %collective-permute-done.next_block, bf16[16,2048]{1,0:T(8,128)(2,1)S(1)} %collective-permute-done.1.next_swapped, ...), custom_call_target="tpu_custom_call" | custom-call | tf_op jit(solution)/shard_map/first/pallas_call | solution.py:191
  14.8 1.7 %second.1 = (f32[16,4096]{1,0:T(8,128)S(1)}, bf16[16,4096]{1,0:T(8,128)(2,1)S(1)}, bf16[32,384]{1,0:T(8,128)(2,1)S(1)}) custom-call(bf16[16,2048]{1,0:T(8,128)(2,1)S(1)} %get-tuple-element.30.own, bf16[16,2048]{1,0:T(8,128)(2,1)S(1)} %collective-permute-done.next_block, bf16[16,2048]{1,0:T(8,128)(2,1)S(1)} %collective-permute-done.1.next_swapped, ...), custom_call_target="tpu_custom_call" | custom-call | tf_op jit(solution)/shard_map/second/pallas_call | solution.py:204
  16.5 0.0 copy-start.4
  16.5 0.2 collective-permute-start.9
  16.7 0.6 %down.1 = (f32[16,4096]{1,0:T(8,128)S(1)}, bf16[16,4096]{1,0:T(8,128)(2,1)S(1)}) custom-call(bf16[32,384]{1,0:T(8,128)(2,1)S(1)} %get-tuple-element.36.hidden, bf16[1,384,4096]{2,1,0:T(8,128)(2,1)S(1)} %copy-done.2), custom_call_target="tpu_custom_call" | custom-call | tf_op jit(solution)/shard_map/down/pallas_call | solution.py:213
  17.4 0.4 %collective-permute-start.6 = (bf16[16,4096]{1,0:T(8,128)(2,1)S(1)}, bf16[16,4096]{1,0:T(8,128)(2,1)S(1)}, u32[]{:S(2)}, u32[]{:S(2)}) collective-permute-start(bf16[16,4096]{1,0:T(8,128)(2,1)S(1)} %get-tuple-element.38), channel_id=1, source_target_pairs={{0,1},{1,0},{2,3},{3,2},{4,5},{5,4},{6,7},{7,6},{8,9},{9,8},{10,11... | collective-permute-start | bytes 393224 | tf_op jit(solution)/shard_map/ppermute | solution.py:225
  17.8 0.2 collective-permute-done.9.arrived
  18.0 1.6 %collective-permute-start.10 = (bf16[8,4096]{1,0:T(8,128)(2,1)S(1)}, bf16[8,4096]{1,0:T(8,128)(2,1)S(1)}, u32[]{:S(2)}, u32[]{:S(2)}) collective-permute-start(bf16[8,4096]{1,0:T(8,128)(2,1)S(1)} %get-tuple-element.46), channel_id=1, source_target_pairs={{0,2},{1,3},{2,0},{3,1},{4,6},{5,7},{6,4},{7,5},{8,10},{9,11},{10,... | collective-permute-start | bytes 196616 | tf_op jit(solution)/shard_map/ppermute | solution.py:238
  19.6 0.8 %collective-permute-start.7 = (bf16[8,4096]{1,0:T(8,128)(2,1)S(1)}, bf16[8,4096]{1,0:T(8,128)(2,1)S(1)}, u32[]{:S(2)}, u32[]{:S(2)}) collective-permute-start(bf16[8,4096]{1,0:T(8,128)(2,1)S(1)} %get-tuple-element.40), channel_id=1, source_target_pairs={{0,2},{1,3},{2,0},{3,1},{4,6},{5,7},{6,4},{7,5},{8,10},{9,11},{10,... | collective-permute-start | bytes 196616 | tf_op jit(solution)/shard_map/ppermute | solution.py:238
  20.3 2.2 %collective-permute-done.10.refs_0_ = bf16[8,4096]{1,0:T(8,128)(2,1)S(1)} collective-permute-done((bf16[8,4096]{1,0:T(8,128)(2,1)S(1)}, bf16[8,4096]{1,0:T(8,128)(2,1)S(1)}, u32[]{:S(2)}, u32[]{:S(2)}) %collective-permute-start.10) | collective-permute-done | bytes 65568 | tf_op jit(solution)/shard_map/ppermute | solution.py:238
  22.6 0.1 collective-permute-start.11
  22.7 2.2 %collective-permute-start.12 = (bf16[4,4096]{1,0:T(4,128)(2,1)S(1)}, bf16[4,4096]{1,0:T(4,128)(2,1)S(1)}, u32[]{:S(2)}, u32[]{:S(2)}) collective-permute-start(bf16[4,4096]{1,0:T(4,128)(2,1)S(1)} %get-tuple-element.48), channel_id=1, source_target_pairs={{0,12},{4,8},{8,4},{12,0},{1,13},{5,9},{9,5},{13,1},{2,14},{6,10},... | collective-permute-start | bytes 98312 | tf_op jit(solution)/shard_map/ppermute | solution.py:250
  24.9 1.3 %collective-permute-start.8 = (bf16[4,4096]{1,0:T(4,128)(2,1)S(1)}, bf16[4,4096]{1,0:T(4,128)(2,1)S(1)}, u32[]{:S(2)}, u32[]{:S(2)}) collective-permute-start(bf16[4,4096]{1,0:T(4,128)(2,1)S(1)} %get-tuple-element.42), channel_id=1, source_target_pairs={{0,4},{4,0},{8,12},{12,8},{1,5},{5,1},{9,13},{13,9},{2,6},{6,2},{1... | collective-permute-start | bytes 98312 | tf_op jit(solution)/shard_map/ppermute | solution.py:250
  26.2 1.2 %collective-permute-done.11.refs_2_ = bf16[4,4096]{1,0:T(4,128)(2,1)S(1)} collective-permute-done((bf16[4,4096]{1,0:T(4,128)(2,1)S(1)}, bf16[4,4096]{1,0:T(4,128)(2,1)S(1)}, u32[]{:S(2)}, u32[]{:S(2)}) %collective-permute-start.11) | collective-permute-done | bytes 32800 | tf_op jit(solution)/shard_map/ppermute | solution.py:250
  27.5 1.0 %collective-permute-done.12.refs_3_ = bf16[4,4096]{1,0:T(4,128)(2,1)S(1)} collective-permute-done((bf16[4,4096]{1,0:T(4,128)(2,1)S(1)}, bf16[4,4096]{1,0:T(4,128)(2,1)S(1)}, u32[]{:S(2)}, u32[]{:S(2)}) %collective-permute-start.12) | collective-permute-done | bytes 32800 | tf_op jit(solution)/shard_map/ppermute | solution.py:250
  28.4 0.5 %collective-permute-done.8.refs_1_ = bf16[4,4096]{1,0:T(4,128)(2,1)S(1)} collective-permute-done((bf16[4,4096]{1,0:T(4,128)(2,1)S(1)}, bf16[4,4096]{1,0:T(4,128)(2,1)S(1)}, u32[]{:S(2)}, u32[]{:S(2)}) %collective-permute-start.8) | collective-permute-done | bytes 32800 | tf_op jit(solution)/shard_map/ppermute | solution.py:250
  28.9 0.7 %mix.1 = bf16[4,4096]{1,0:T(4,128)(2,1)} custom-call(s32[2,16]{1,0:T(2,128)S(1)} %bitcast.2, f32[2,4]{1,0:T(2,128)S(1)} %bitcast.3, bf16[4,4096]{1,0:T(4,128)(2,1)S(1)} %get-tuple-element.41.refs_0_, bf16[4,4096]{1,0:T(4,128)(2,1)S(1)} %collective-permute-done.8.refs_1_, bf16[4,4096]{1,0:T(4,128)(2,1)S(1)} %collective-permute-done.11.refs_2_, ...), custom_call_target="tpu_custom_call" | custom-call | tf_op jit(solution)/shard_map/mix/pallas_call | solution.py:253
  (22 shorter events, 0.2 us)
Async XLA Ops:
  0.9 12.8 %copy-start = (bf16[1,384,4096]{2,1,0:T(8,128)(2,1)S(1)}, bf16[1,384,4096]{2,1,0:T(8,128)(2,1)}, u32[]{:S(2)}) copy-start(bf16[1,384,4096]{2,1,0:T(8,128)(2,1)} %refs_2_.3) | copy-start | bytes 9437188
  1.0 12.8 %copy-start.1 = (bf16[1,384,4096]{2,1,0:T(8,128)(2,1)S(1)}, bf16[1,384,4096]{2,1,0:T(8,128)(2,1)}, u32[]{:S(2)}) copy-start(bf16[1,384,4096]{2,1,0:T(8,128)(2,1)} %refs_3_.3) | copy-start | bytes 9437188
  1.0 13.7 %copy-start.2 = (bf16[1,384,4096]{2,1,0:T(8,128)(2,1)S(1)}, bf16[1,384,4096]{2,1,0:T(8,128)(2,1)}, u32[]{:S(2)}) copy-start(bf16[1,384,4096]{2,1,0:T(8,128)(2,1)} %w_down.1) | copy-start | bytes 9437188
  1.0 6.0 %collective-permute-start = (bf16[16,2048]{1,0:T(8,128)(2,1)S(1)}, bf16[16,2048]{1,0:T(8,128)(2,1)S(1)}, u32[]{:S(2)}, u32[]{:S(2)}) collective-permute-start(bf16[16,2048]{1,0:T(8,128)(2,1)S(1)} %get-tuple-element.31), channel_id=1, source_target_pairs={{0,4},{4,0},{8,12},{12,8},{1,5},{5,1},{9,13},{13,9},{2,6},{6,2},{1... | collective-permute-start | bytes 196616 | tf_op jit(solution)/shard_map/ppermute | solution.py:181
  4.1 8.4 %collective-permute-start.4 = (bf16[16,2048]{1,0:T(8,128)(2,1)S(1)}, bf16[16,2048]{1,0:T(8,128)(2,1)S(1)}, u32[]{:S(2)}, u32[]{:S(2)}) collective-permute-start(bf16[16,2048]{1,0:T(8,128)(2,1)S(1)} %get-tuple-element.32.first.own), channel_id=1, source_target_pairs={{0,8},{1,13},{2,10},{3,15},{4,12},{5,9},{6,14},{7,11},{8,0},{9,5},... | collective-permute-start | bytes 196616 | tf_op jit(solution)/shard_map/ppermute | solution.py:181
  6.7 6.5 %collective-permute-start.2 = (bf16[16,2048]{1,0:T(8,128)(2,1)S(1)}, bf16[16,2048]{1,0:T(8,128)(2,1)S(1)}, u32[]{:S(2)}, u32[]{:S(2)}) collective-permute-start(bf16[16,2048]{1,0:T(8,128)(2,1)S(1)} %get-tuple-element.30.own), channel_id=1, source_target_pairs={{0,8},{1,13},{2,10},{3,15},{4,12},{5,9},{6,14},{7,11},{8,0},{9,5},... | collective-permute-start | bytes 196616 | tf_op jit(solution)/shard_map/ppermute | solution.py:181
  7.1 6.2 %collective-permute-start.1 = (bf16[16,2048]{1,0:T(8,128)(2,1)S(1)}, bf16[16,2048]{1,0:T(8,128)(2,1)S(1)}, u32[]{:S(2)}, u32[]{:S(2)}) collective-permute-start(bf16[16,2048]{1,0:T(8,128)(2,1)S(1)} %collective-permute-done.next_block), channel_id=1, source_target_pairs={{0,1},{1,0},{2,3},{3,2},{4,5},{5,4},{6,7},{7,6},{8,9},{9,8},{10,11... | collective-permute-start | bytes 196616 | tf_op jit(solution)/shard_map/ppermute | solution.py:182
  12.5 1.3 %collective-permute-start.5 = (bf16[16,2048]{1,0:T(8,128)(2,1)S(1)}, bf16[16,2048]{1,0:T(8,128)(2,1)S(1)}, u32[]{:S(2)}, u32[]{:S(2)}) collective-permute-start(bf16[16,2048]{1,0:T(8,128)(2,1)S(1)} %collective-permute-done.4.refs_0_), channel_id=1, source_target_pairs={{0,1},{1,0},{2,3},{3,2},{4,5},{5,4},{6,7},{7,6},{8,9},{9,8},{10,11... | collective-permute-start | bytes 196616 | tf_op jit(solution)/shard_map/ppermute | solution.py:182
  13.2 1.5 %collective-permute-start.3 = (bf16[16,2048]{1,0:T(8,128)(2,1)S(1)}, bf16[16,2048]{1,0:T(8,128)(2,1)S(1)}, u32[]{:S(2)}, u32[]{:S(2)}) collective-permute-start(bf16[16,2048]{1,0:T(8,128)(2,1)S(1)} %collective-permute-done.2.refs_0_), channel_id=1, source_target_pairs={{0,1},{1,0},{2,3},{3,2},{4,5},{5,4},{6,7},{7,6},{8,9},{9,8},{10,11... | collective-permute-start | bytes 196616 | tf_op jit(solution)/shard_map/ppermute | solution.py:182
  16.5 12.4 %copy-start.3 = (s32[16,2]{0,1:T(2,128)S(1)}, s32[16,2]{0,1:T(2,128)}, u32[]{:S(2)}) copy-start(s32[16,2]{0,1:T(2,128)} %param.7) | copy-start | bytes 388
  16.5 12.4 %copy-start.4 = (f32[4,2]{0,1:T(2,128)S(1)}, f32[4,2]{0,1:T(2,128)}, u32[]{:S(2)}) copy-start(f32[4,2]{0,1:T(2,128)} %param.8) | copy-start | bytes 100
  16.5 1.4 %collective-permute-start.9 = (bf16[16,4096]{1,0:T(8,128)(2,1)S(1)}, bf16[16,4096]{1,0:T(8,128)(2,1)S(1)}, u32[]{:S(2)}, u32[]{:S(2)}) collective-permute-start(bf16[16,4096]{1,0:T(8,128)(2,1)S(1)} %get-tuple-element.44), channel_id=1, source_target_pairs={{0,1},{1,0},{2,3},{3,2},{4,5},{5,4},{6,7},{7,6},{8,9},{9,8},{10,11... | collective-permute-start | bytes 393224 | tf_op jit(solution)/shard_map/ppermute | solution.py:225
  17.4 2.1 %collective-permute-start.6 = (bf16[16,4096]{1,0:T(8,128)(2,1)S(1)}, bf16[16,4096]{1,0:T(8,128)(2,1)S(1)}, u32[]{:S(2)}, u32[]{:S(2)}) collective-permute-start(bf16[16,4096]{1,0:T(8,128)(2,1)S(1)} %get-tuple-element.38), channel_id=1, source_target_pairs={{0,1},{1,0},{2,3},{3,2},{4,5},{5,4},{6,7},{7,6},{8,9},{9,8},{10,11... | collective-permute-start | bytes 393224 | tf_op jit(solution)/shard_map/ppermute | solution.py:225
  18.0 4.6 %collective-permute-start.10 = (bf16[8,4096]{1,0:T(8,128)(2,1)S(1)}, bf16[8,4096]{1,0:T(8,128)(2,1)S(1)}, u32[]{:S(2)}, u32[]{:S(2)}) collective-permute-start(bf16[8,4096]{1,0:T(8,128)(2,1)S(1)} %get-tuple-element.46), channel_id=1, source_target_pairs={{0,2},{1,3},{2,0},{3,1},{4,6},{5,7},{6,4},{7,5},{8,10},{9,11},{10,... | collective-permute-start | bytes 196616 | tf_op jit(solution)/shard_map/ppermute | solution.py:238
  19.6 5.4 %collective-permute-start.7 = (bf16[8,4096]{1,0:T(8,128)(2,1)S(1)}, bf16[8,4096]{1,0:T(8,128)(2,1)S(1)}, u32[]{:S(2)}, u32[]{:S(2)}) collective-permute-start(bf16[8,4096]{1,0:T(8,128)(2,1)S(1)} %get-tuple-element.40), channel_id=1, source_target_pairs={{0,2},{1,3},{2,0},{3,1},{4,6},{5,7},{6,4},{7,5},{8,10},{9,11},{10,... | collective-permute-start | bytes 196616 | tf_op jit(solution)/shard_map/ppermute | solution.py:238
  22.6 4.9 %collective-permute-start.11 = (bf16[4,4096]{1,0:T(4,128)(2,1)S(1)}, bf16[4,4096]{1,0:T(4,128)(2,1)S(1)}, u32[]{:S(2)}, u32[]{:S(2)}) collective-permute-start(bf16[4,4096]{1,0:T(4,128)(2,1)S(1)} %get-tuple-element.47), channel_id=1, source_target_pairs={{0,8},{4,12},{8,0},{12,4},{1,9},{5,13},{9,1},{13,5},{2,10},{6,14},... | collective-permute-start | bytes 98312 | tf_op jit(solution)/shard_map/ppermute | solution.py:250
  22.7 5.8 %collective-permute-start.12 = (bf16[4,4096]{1,0:T(4,128)(2,1)S(1)}, bf16[4,4096]{1,0:T(4,128)(2,1)S(1)}, u32[]{:S(2)}, u32[]{:S(2)}) collective-permute-start(bf16[4,4096]{1,0:T(4,128)(2,1)S(1)} %get-tuple-element.48), channel_id=1, source_target_pairs={{0,12},{4,8},{8,4},{12,0},{1,13},{5,9},{9,5},{13,1},{2,14},{6,10},... | collective-permute-start | bytes 98312 | tf_op jit(solution)/shard_map/ppermute | solution.py:250
  24.9 4.0 %collective-permute-start.8 = (bf16[4,4096]{1,0:T(4,128)(2,1)S(1)}, bf16[4,4096]{1,0:T(4,128)(2,1)S(1)}, u32[]{:S(2)}, u32[]{:S(2)}) collective-permute-start(bf16[4,4096]{1,0:T(4,128)(2,1)S(1)} %get-tuple-element.42), channel_id=1, source_target_pairs={{0,4},{4,0},{8,12},{12,8},{1,5},{5,1},{9,13},{13,9},{2,6},{6,2},{1... | collective-permute-start | bytes 98312 | tf_op jit(solution)/shard_map/ppermute | solution.py:250

commit v10 on v7

--- a/solution.py
+++ b/solution.py
@@ -13,7 +13,22 @@
 HBM = pl.BlockSpec(memory_space=pltpu.HBM)
 
 
-def order_kernel(n_expert, pairs, rows, out):
+def fetch_kernel(tokens, own, mine, sems):
+    half = mine.shape[1]
+    core = lax.rem(lax.axis_index("etp"), 2)
+    cols = pl.ds(pl.multiple_of(core * half, half), half)
+    copies = [
+        pltpu.make_async_copy(tokens.at[:, cols], mine, sems.at[0]),
+        pltpu.make_async_copy(tokens, own, sems.at[1]),
+    ]
+    for copy in copies:
+        copy.start()
+    for copy in copies:
+        copy.wait()
+
+
+def order_kernel(n_expert, pairs, rows, mine, out):
+    del mine
     total = out.shape[0]
     me = lax.axis_index("etp")
     core, pair = lax.rem(me, 2), lax.div(me, 2)
@@ -30,13 +45,15 @@
     out[...] = jnp.where(source == wanted, 1.0, 0.0).astype(jnp.bfloat16)
 
 
-def ffn_kernel(n_expert, parts, own, next_block, order, *refs):
+def ffn_kernel(n_expert, parts, own, next_block, next_swapped, order, *refs):
     far = refs[: n_expert - 2]
     w_gate, w_up, w_down, kept, sent, rest, x = refs[n_expert - 2 :]
     core = lax.rem(lax.axis_index("etp"), 2)
     tok = own.shape[0]
     x[0:tok, :] = own[...]
-    x[tok : 2 * tok, :] = next_block[...]
+    half = next_block.shape[1]
+    for block, side in ((next_block, core), (next_swapped, 1 - core)):
+        x[tok : 2 * tok, pl.ds(pl.multiple_of(side * half, half), half)] = block[...]
     for i in range(0, n_expert - 2, 2):
         for block, k in ((far[i], i + 2 + core), (far[i + 1], i + 3 - core)):
             x[pl.ds(pl.multiple_of(k * tok, tok), tok), :] = block[...]
@@ -113,15 +130,28 @@
     pairs = n_etp // 2
     side = n_expert * tok // 2
 
+    own, mine = pl.pallas_call(
+        fetch_kernel,
+        out_shape=[
+            jax.ShapeDtypeStruct((tok, width), tokens.dtype),
+            jax.ShapeDtypeStruct((tok, width // 2), tokens.dtype),
+        ],
+        in_specs=[HBM],
+        out_specs=[VMEM] * 2,
+        scratch_shapes=[pltpu.SemaphoreType.DMA((2,))],
+        compiler_params=GRANT,
+        name="fetch",
+    )(pltpu.with_memory_space_constraint(tokens, pltpu.HBM))
     order = pl.pallas_call(
         functools.partial(order_kernel, n_expert, pairs, rows),
         out_shape=jax.ShapeDtypeStruct((2 * side, 2 * side), jnp.bfloat16),
+        in_specs=[VMEM],
         out_specs=VMEM,
         cost_estimate=AHEAD,
         compiler_params=GRANT,
         name="order",
-    )()
-    tokens, order = lax.optimization_barrier((tokens, order))
+    )(mine)
+    mine, order = lax.optimization_barrier((mine, order))
 
     swap = [(t, t ^ 1) for t in range(n_etp)]
     far = []
@@ -132,7 +162,8 @@
             for t in range(n_etp)
         ]
         far.append(lax.ppermute(tokens, ("expert", "etp"), route))
-    next_block = lax.ppermute(tokens, "expert", [(e, e ^ 1) for e in range(n_expert)])
+    next_block = lax.ppermute(mine, "expert", [(e, e ^ 1) for e in range(n_expert)])
+    near = [next_block, lax.ppermute(next_block, "etp", swap)]
     far = [b for block in far for b in (block, lax.ppermute(block, "etp", swap))]
 
     parts = 4
@@ -143,12 +174,12 @@
     far_kept, far_sent, rest = pl.pallas_call(
         functools.partial(ffn_kernel, n_expert, parts),
         out_shape=halves + [jax.ShapeDtypeStruct((side, w_gate.shape[1]), jnp.bfloat16)],
-        in_specs=[VMEM] * (n_expert + 4),
+        in_specs=[VMEM] * (n_expert + 5),
         out_specs=[VMEM] * 3,
         scratch_shapes=[pltpu.VMEM((n_expert * tok, width), jnp.bfloat16)],
         compiler_params=GRANT,
         name="ffn",
-    )(tokens, next_block, order, *far, w_gate, w_up, w_down)
+    )(own, *near, order, *far, w_gate, w_up, w_down)
     near_kept, near_sent = pl.pallas_call(
         functools.partial(down_kernel, parts),
         out_shape=halves,

time: 30 us -> 29.2 us (0.973)
  waiting for transfers between devices: 12.6 us -> 10.9 us
  Pallas kernels: 4.06 us -> 5.06 us
  local copies, waits for them, and re-layouts: 0.87 us -> 0.03 us
  starting transfers between devices: 12.3 us -> 12.9 us
    pallas_call x0 -> x1, Pallas kernels: none -> 0.99 us  [on_device(): pl.pallas_call(fetch_kernel, out_shape=[jax.ShapeDtypeStruct((tok, width)...]
    ppermute x1, waiting for transfers between devices: 5 us -> 4.05 us  [on_device(): far.append(lax.ppermute(tokens, ('expert', 'etp'), route))]
    unnamed x12 -> x10, local copies, waits for them, and re-layouts: 0.87 us -> 0.03 us
    ppermute x1, waiting for transfers between devices: 0.56 us -> 0.01 us  [on_device(): lax.ppermute(block, 'etp', swap)]
    ppermute x1 -> x2, starting transfers between devices: 1.58 us -> 2.12 us  [the longest x1 1.64 us: on_device(): lax.ppermute(mine, 'expert', [(e, e ^ 1) for e in range(n_expert)])]
    ppermute x1 -> x2, waiting for transfers between devices: 0.79 us -> 0.96 us  [the longest x1 0.93 us: on_device(): near = [next_block, lax.ppermute(next_block, 'etp', swap)]]
  transfers between devices with their start and end apart: 10 -> 11, of which waited for: 8 -> 7; matrix products, arithmetic and copies ran while one was open for 0% -> 0% of each run, Pallas kernels for 2% -> 6%
where the time goes in v10:
time: 29.2 us; the launch traced here: 29 us
  starting transfers between devices  12.9 us (44%)
  waiting for transfers between devices  10.9 us (37%)
  Pallas kernels  5.06 us (17%)
    ppermute x1, waiting for transfers between devices, on_device(): far.append(lax.ppermute(tokens, ('expert', 'etp'), route))  4.05 us
    ppermute x1, starting transfers between devices, on_device(): far.append(lax.ppermute(tokens, ('expert', 'etp'), route))  4.04 us
    ppermute x3, waiting for transfers between devices, on_device(): lax.ppermute(pieces[k], 'expert', [(e, e ^ k) for e in range(n_expert)])  3.8 us
    ppermute x3, starting transfers between devices, on_device(): lax.ppermute(pieces[k], 'expert', [(e, e ^ k) for e in range(n_expert)])  3.62 us
    pallas_call x1, Pallas kernels, on_device(): pl.pallas_call(functools.partial(ffn_kernel, n_expert, parts), out_shape=...  2.53 us
    ppermute x2, starting transfers between devices, on_device(): landed.append(lax.ppermute(piece, 'etp', route))  2.52 us
    ppermute x2, waiting for transfers between devices, on_device(): landed.append(lax.ppermute(piece, 'etp', route))  1.96 us
    ppermute x1, starting transfers between devices, on_device(): lax.ppermute(mine, 'expert', [(e, e ^ 1) for e in range(n_expert)])  1.64 us
  transfers between devices with their start and end apart: 11, of which 7 were waited for; matrix products, arithmetic and copies ran while one was open for 0% of the time, Pallas kernels for 6%

profile of v10, /device:TPU:0, one launch (start us, length us, event | category | flops | bytes accessed | tf_op | source)
XLA Modules:
  0.0 29.0 jit_solution(14103967359105003720)
XLA Ops:
  0.0 4.0 %collective-permute-start.2 = (bf16[16,4096]{1,0:T(8,128)(2,1)}, bf16[16,4096]{1,0:T(8,128)(2,1)S(1)}, u32[]{:S(2)}, u32[]{:S(2)}) collective-permute-start(bf16[16,4096]{1,0:T(8,128)(2,1)} %tokens.1), channel_id=1, source_target_pairs={{0,8},{1,13},{2,10},{3,15},{4,12},{5,9},{6,14},{7,11},{8,0},{9,5},... | collective-permute-start | bytes 393224 | tf_op jit(solution)/shard_map/ppermute | solution.py:164
  4.0 1.0 %fetch.1 = (bf16[16,4096]{1,0:T(8,128)(2,1)S(1)}, bf16[16,2048]{1,0:T(8,128)(2,1)S(1)}) custom-call(bf16[16,4096]{1,0:T(8,128)(2,1)} %tokens.1), custom_call_target="tpu_custom_call" | custom-call | tf_op jit(solution)/shard_map/fetch/pallas_call | solution.py:133
  5.0 0.0 copy-start
  5.1 1.6 %collective-permute-start = (bf16[16,2048]{1,0:T(8,128)(2,1)S(1)}, bf16[16,2048]{1,0:T(8,128)(2,1)S(1)}, u32[]{:S(2)}, u32[]{:S(2)}) collective-permute-start(bf16[16,2048]{1,0:T(8,128)(2,1)S(1)} %get-tuple-element.24.mine), channel_id=1, source_target_pairs={{0,4},{4,0},{8,12},{12,8},{1,5},{5,1},{9,13},{13,9},{2,6},{6,2},{1... | collective-permute-start | bytes 196616 | tf_op jit(solution)/shard_map/ppermute | solution.py:165
  6.8 4.1 %collective-permute-done.2.refs_0_ = bf16[16,4096]{1,0:T(8,128)(2,1)S(1)} collective-permute-done((bf16[16,4096]{1,0:T(8,128)(2,1)}, bf16[16,4096]{1,0:T(8,128)(2,1)S(1)}, u32[]{:S(2)}, u32[]{:S(2)}) %collective-permute-start.2) | collective-permute-done | bytes 131104 | tf_op jit(solution)/shard_map/ppermute | solution.py:164
  10.8 0.0 collective-permute-done.next_block
  10.9 0.5 %collective-permute-start.1 = (bf16[16,2048]{1,0:T(8,128)(2,1)S(1)}, bf16[16,2048]{1,0:T(8,128)(2,1)S(1)}, u32[]{:S(2)}, u32[]{:S(2)}) collective-permute-start(bf16[16,2048]{1,0:T(8,128)(2,1)S(1)} %collective-permute-done.next_block), channel_id=1, source_target_pairs={{0,1},{1,0},{2,3},{3,2},{4,5},{5,4},{6,7},{7,6},{8,9},{9,8},{10,11... | collective-permute-start | bytes 196616 | tf_op jit(solution)/shard_map/ppermute | solution.py:166
  11.3 0.9 %collective-permute-done.1.next_swapped = bf16[16,2048]{1,0:T(8,128)(2,1)S(1)} collective-permute-done((bf16[16,2048]{1,0:T(8,128)(2,1)S(1)}, bf16[16,2048]{1,0:T(8,128)(2,1)S(1)}, u32[]{:S(2)}, u32[]{:S(2)}) %collective-permute-start.1) | collective-permute-done | bytes 65568 | tf_op jit(solution)/shard_map/ppermute | solution.py:166
  12.3 2.5 %ffn.1 = (f32[16,4096]{1,0:T(8,128)S(1)}, bf16[16,4096]{1,0:T(8,128)(2,1)S(1)}, bf16[32,384]{1,0:T(8,128)(2,1)S(1)}) custom-call(bf16[16,4096]{1,0:T(8,128)(2,1)S(1)} %get-tuple-element.22.own, bf16[16,2048]{1,0:T(8,128)(2,1)S(1)} %collective-permute-done.next_block, bf16[16,2048]{1,0:T(8,128)(2,1)S(1)} %collective-permute-done.1.next_swapped, ...), custom_call_target="tpu_custom_call" | custom-call | tf_op jit(solution)/shard_map/ffn/pallas_call | solution.py:174
  14.8 0.0 copy-start.4
  14.8 0.4 %collective-permute-start.7 = (bf16[16,4096]{1,0:T(8,128)(2,1)S(1)}, bf16[16,4096]{1,0:T(8,128)(2,1)S(1)}, u32[]{:S(2)}, u32[]{:S(2)}) collective-permute-start(bf16[16,4096]{1,0:T(8,128)(2,1)S(1)} %get-tuple-element.34), channel_id=1, source_target_pairs={{0,1},{1,0},{2,3},{3,2},{4,5},{5,4},{6,7},{7,6},{8,9},{9,8},{10,11... | collective-permute-start | bytes 393224 | tf_op jit(solution)/shard_map/ppermute | solution.py:195
  15.2 0.6 %down.1 = (f32[16,4096]{1,0:T(8,128)S(1)}, bf16[16,4096]{1,0:T(8,128)(2,1)S(1)}) custom-call(bf16[32,384]{1,0:T(8,128)(2,1)S(1)} %get-tuple-element.26.hidden, bf16[1,384,4096]{2,1,0:T(8,128)(2,1)S(1)} %copy-done), custom_call_target="tpu_custom_call" | custom-call | tf_op jit(solution)/shard_map/down/pallas_call | solution.py:183
  15.9 0.2 collective-permute-start.4
  16.1 0.2 collective-permute-done.7.arrived
  16.3 1.6 %collective-permute-start.8 = (bf16[8,4096]{1,0:T(8,128)(2,1)S(1)}, bf16[8,4096]{1,0:T(8,128)(2,1)S(1)}, u32[]{:S(2)}, u32[]{:S(2)}) collective-permute-start(bf16[8,4096]{1,0:T(8,128)(2,1)S(1)} %get-tuple-element.36), channel_id=1, source_target_pairs={{0,2},{1,3},{2,0},{3,1},{4,6},{5,7},{6,4},{7,5},{8,10},{9,11},{10,... | collective-permute-start | bytes 196616 | tf_op jit(solution)/shard_map/ppermute | solution.py:208
  17.9 1.0 %collective-permute-start.5 = (bf16[8,4096]{1,0:T(8,128)(2,1)S(1)}, bf16[8,4096]{1,0:T(8,128)(2,1)S(1)}, u32[]{:S(2)}, u32[]{:S(2)}) collective-permute-start(bf16[8,4096]{1,0:T(8,128)(2,1)S(1)} %get-tuple-element.30), channel_id=1, source_target_pairs={{0,2},{1,3},{2,0},{3,1},{4,6},{5,7},{6,4},{7,5},{8,10},{9,11},{10,... | collective-permute-start | bytes 196616 | tf_op jit(solution)/shard_map/ppermute | solution.py:208
  18.8 2.0 %collective-permute-done.8.refs_0_ = bf16[8,4096]{1,0:T(8,128)(2,1)S(1)} collective-permute-done((bf16[8,4096]{1,0:T(8,128)(2,1)S(1)}, bf16[8,4096]{1,0:T(8,128)(2,1)S(1)}, u32[]{:S(2)}, u32[]{:S(2)}) %collective-permute-start.8) | collective-permute-done | bytes 65568 | tf_op jit(solution)/shard_map/ppermute | solution.py:208
  20.8 0.8 %collective-permute-start.9 = (bf16[4,4096]{1,0:T(4,128)(2,1)S(1)}, bf16[4,4096]{1,0:T(4,128)(2,1)S(1)}, u32[]{:S(2)}, u32[]{:S(2)}) collective-permute-start(bf16[4,4096]{1,0:T(4,128)(2,1)S(1)} %get-tuple-element.37), channel_id=1, source_target_pairs={{0,8},{4,12},{8,0},{12,4},{1,9},{5,13},{9,1},{13,5},{2,10},{6,14},... | collective-permute-start | bytes 98312 | tf_op jit(solution)/shard_map/ppermute | solution.py:220
  21.6 2.6 %collective-permute-start.10 = (bf16[4,4096]{1,0:T(4,128)(2,1)S(1)}, bf16[4,4096]{1,0:T(4,128)(2,1)S(1)}, u32[]{:S(2)}, u32[]{:S(2)}) collective-permute-start(bf16[4,4096]{1,0:T(4,128)(2,1)S(1)} %get-tuple-element.38), channel_id=1, source_target_pairs={{0,12},{4,8},{8,4},{12,0},{1,13},{5,9},{9,5},{13,1},{2,14},{6,10},... | collective-permute-start | bytes 98312 | tf_op jit(solution)/shard_map/ppermute | solution.py:220
  24.3 0.2 collective-permute-start.6
  24.5 2.0 %collective-permute-done.9.refs_2_ = bf16[4,4096]{1,0:T(4,128)(2,1)S(1)} collective-permute-done((bf16[4,4096]{1,0:T(4,128)(2,1)S(1)}, bf16[4,4096]{1,0:T(4,128)(2,1)S(1)}, u32[]{:S(2)}, u32[]{:S(2)}) %collective-permute-start.9) | collective-permute-done | bytes 32800 | tf_op jit(solution)/shard_map/ppermute | solution.py:220
  26.5 1.0 %collective-permute-done.10.refs_3_ = bf16[4,4096]{1,0:T(4,128)(2,1)S(1)} collective-permute-done((bf16[4,4096]{1,0:T(4,128)(2,1)S(1)}, bf16[4,4096]{1,0:T(4,128)(2,1)S(1)}, u32[]{:S(2)}, u32[]{:S(2)}) %collective-permute-start.10) | collective-permute-done | bytes 32800 | tf_op jit(solution)/shard_map/ppermute | solution.py:220
  27.5 0.8 %collective-permute-done.6.refs_1_ = bf16[4,4096]{1,0:T(4,128)(2,1)S(1)} collective-permute-done((bf16[4,4096]{1,0:T(4,128)(2,1)S(1)}, bf16[4,4096]{1,0:T(4,128)(2,1)S(1)}, u32[]{:S(2)}, u32[]{:S(2)}) %collective-permute-start.6) | collective-permute-done | bytes 32800 | tf_op jit(solution)/shard_map/ppermute | solution.py:220
  28.3 0.7 %mix.1 = bf16[4,4096]{1,0:T(4,128)(2,1)} custom-call(s32[2,16]{1,0:T(2,128)S(1)} %bitcast.2, f32[2,4]{1,0:T(2,128)S(1)} %bitcast.3, bf16[4,4096]{1,0:T(4,128)(2,1)S(1)} %get-tuple-element.31.refs_0_, bf16[4,4096]{1,0:T(4,128)(2,1)S(1)} %collective-permute-done.6.refs_1_, bf16[4,4096]{1,0:T(4,128)(2,1)S(1)} %collective-permute-done.9.refs_2_, ...), custom_call_target="tpu_custom_call" | custom-call | tf_op jit(solution)/shard_map/mix/pallas_call | solution.py:223
  (17 shorter events, 0.2 us)
Async XLA Ops:
  0.0 10.8 %collective-permute-start.2 = (bf16[16,4096]{1,0:T(8,128)(2,1)}, bf16[16,4096]{1,0:T(8,128)(2,1)S(1)}, u32[]{:S(2)}, u32[]{:S(2)}) collective-permute-start(bf16[16,4096]{1,0:T(8,128)(2,1)} %tokens.1), channel_id=1, source_target_pairs={{0,8},{1,13},{2,10},{3,15},{4,12},{5,9},{6,14},{7,11},{8,0},{9,5},... | collective-permute-start | bytes 393224 | tf_op jit(solution)/shard_map/ppermute | solution.py:164
  5.0 7.2 %copy-start = (bf16[1,384,4096]{2,1,0:T(8,128)(2,1)S(1)}, bf16[1,384,4096]{2,1,0:T(8,128)(2,1)}, u32[]{:S(2)}) copy-start(bf16[1,384,4096]{2,1,0:T(8,128)(2,1)} %w_down.1) | copy-start | bytes 9437188
  5.0 7.2 %copy-start.1 = (bf16[1,384,4096]{2,1,0:T(8,128)(2,1)S(1)}, bf16[1,384,4096]{2,1,0:T(8,128)(2,1)}, u32[]{:S(2)}) copy-start(bf16[1,384,4096]{2,1,0:T(8,128)(2,1)} %refs_2_.1) | copy-start | bytes 9437188
  5.1 7.2 %copy-start.2 = (bf16[1,384,4096]{2,1,0:T(8,128)(2,1)S(1)}, bf16[1,384,4096]{2,1,0:T(8,128)(2,1)}, u32[]{:S(2)}) copy-start(bf16[1,384,4096]{2,1,0:T(8,128)(2,1)} %refs_3_.1) | copy-start | bytes 9437188
  5.1 5.7 %collective-permute-start = (bf16[16,2048]{1,0:T(8,128)(2,1)S(1)}, bf16[16,2048]{1,0:T(8,128)(2,1)S(1)}, u32[]{:S(2)}, u32[]{:S(2)}) collective-permute-start(bf16[16,2048]{1,0:T(8,128)(2,1)S(1)} %get-tuple-element.24.mine), channel_id=1, source_target_pairs={{0,4},{4,0},{8,12},{12,8},{1,5},{5,1},{9,13},{13,9},{2,6},{6,2},{1... | collective-permute-start | bytes 196616 | tf_op jit(solution)/shard_map/ppermute | solution.py:165
  10.8 1.4 %collective-permute-start.3 = (bf16[16,4096]{1,0:T(8,128)(2,1)S(1)}, bf16[16,4096]{1,0:T(8,128)(2,1)S(1)}, u32[]{:S(2)}, u32[]{:S(2)}) collective-permute-start(bf16[16,4096]{1,0:T(8,128)(2,1)S(1)} %collective-permute-done.2.refs_0_), channel_id=1, source_target_pairs={{0,1},{1,0},{2,3},{3,2},{4,5},{5,4},{6,7},{7,6},{8,9},{9,8},{10,11... | collective-permute-start | bytes 393224 | tf_op jit(solution)/shard_map/ppermute | solution.py:167
  10.9 1.4 %collective-permute-start.1 = (bf16[16,2048]{1,0:T(8,128)(2,1)S(1)}, bf16[16,2048]{1,0:T(8,128)(2,1)S(1)}, u32[]{:S(2)}, u32[]{:S(2)}) collective-permute-start(bf16[16,2048]{1,0:T(8,128)(2,1)S(1)} %collective-permute-done.next_block), channel_id=1, source_target_pairs={{0,1},{1,0},{2,3},{3,2},{4,5},{5,4},{6,7},{7,6},{8,9},{9,8},{10,11... | collective-permute-start | bytes 196616 | tf_op jit(solution)/shard_map/ppermute | solution.py:166
  14.8 13.5 %copy-start.3 = (s32[16,2]{0,1:T(2,128)S(1)}, s32[16,2]{0,1:T(2,128)}, u32[]{:S(2)}) copy-start(s32[16,2]{0,1:T(2,128)} %param.7) | copy-start | bytes 388
  14.8 13.5 %copy-start.4 = (f32[4,2]{0,1:T(2,128)S(1)}, f32[4,2]{0,1:T(2,128)}, u32[]{:S(2)}) copy-start(f32[4,2]{0,1:T(2,128)} %param.8) | copy-start | bytes 100
  14.8 1.4 %collective-permute-start.7 = (bf16[16,4096]{1,0:T(8,128)(2,1)S(1)}, bf16[16,4096]{1,0:T(8,128)(2,1)S(1)}, u32[]{:S(2)}, u32[]{:S(2)}) collective-permute-start(bf16[16,4096]{1,0:T(8,128)(2,1)S(1)} %get-tuple-element.34), channel_id=1, source_target_pairs={{0,1},{1,0},{2,3},{3,2},{4,5},{5,4},{6,7},{7,6},{8,9},{9,8},{10,11... | collective-permute-start | bytes 393224 | tf_op jit(solution)/shard_map/ppermute | solution.py:195
  15.9 2.0 %collective-permute-start.4 = (bf16[16,4096]{1,0:T(8,128)(2,1)S(1)}, bf16[16,4096]{1,0:T(8,128)(2,1)S(1)}, u32[]{:S(2)}, u32[]{:S(2)}) collective-permute-start(bf16[16,4096]{1,0:T(8,128)(2,1)S(1)} %get-tuple-element.28), channel_id=1, source_target_pairs={{0,1},{1,0},{2,3},{3,2},{4,5},{5,4},{6,7},{7,6},{8,9},{9,8},{10,11... | collective-permute-start | bytes 393224 | tf_op jit(solution)/shard_map/ppermute | solution.py:195
  16.3 4.5 %collective-permute-start.8 = (bf16[8,4096]{1,0:T(8,128)(2,1)S(1)}, bf16[8,4096]{1,0:T(8,128)(2,1)S(1)}, u32[]{:S(2)}, u32[]{:S(2)}) collective-permute-start(bf16[8,4096]{1,0:T(8,128)(2,1)S(1)} %get-tuple-element.36), channel_id=1, source_target_pairs={{0,2},{1,3},{2,0},{3,1},{4,6},{5,7},{6,4},{7,5},{8,10},{9,11},{10,... | collective-permute-start | bytes 196616 | tf_op jit(solution)/shard_map/ppermute | solution.py:208
  17.9 6.4 %collective-permute-start.5 = (bf16[8,4096]{1,0:T(8,128)(2,1)S(1)}, bf16[8,4096]{1,0:T(8,128)(2,1)S(1)}, u32[]{:S(2)}, u32[]{:S(2)}) collective-permute-start(bf16[8,4096]{1,0:T(8,128)(2,1)S(1)} %get-tuple-element.30), channel_id=1, source_target_pairs={{0,2},{1,3},{2,0},{3,1},{4,6},{5,7},{6,4},{7,5},{8,10},{9,11},{10,... | collective-permute-start | bytes 196616 | tf_op jit(solution)/shard_map/ppermute | solution.py:208
  20.8 5.7 %collective-permute-start.9 = (bf16[4,4096]{1,0:T(4,128)(2,1)S(1)}, bf16[4,4096]{1,0:T(4,128)(2,1)S(1)}, u32[]{:S(2)}, u32[]{:S(2)}) collective-permute-start(bf16[4,4096]{1,0:T(4,128)(2,1)S(1)} %get-tuple-element.37), channel_id=1, source_target_pairs={{0,8},{4,12},{8,0},{12,4},{1,9},{5,13},{9,1},{13,5},{2,10},{6,14},... | collective-permute-start | bytes 98312 | tf_op jit(solution)/shard_map/ppermute | solution.py:220
  21.6 5.8 %collective-permute-start.10 = (bf16[4,4096]{1,0:T(4,128)(2,1)S(1)}, bf16[4,4096]{1,0:T(4,128)(2,1)S(1)}, u32[]{:S(2)}, u32[]{:S(2)}) collective-permute-start(bf16[4,4096]{1,0:T(4,128)(2,1)S(1)} %get-tuple-element.38), channel_id=1, source_target_pairs={{0,12},{4,8},{8,4},{12,0},{1,13},{5,9},{9,5},{13,1},{2,14},{6,10},... | collective-permute-start | bytes 98312 | tf_op jit(solution)/shard_map/ppermute | solution.py:220
  24.3 4.0 %collective-permute-start.6 = (bf16[4,4096]{1,0:T(4,128)(2,1)S(1)}, bf16[4,4096]{1,0:T(4,128)(2,1)S(1)}, u32[]{:S(2)}, u32[]{:S(2)}) collective-permute-start(bf16[4,4096]{1,0:T(4,128)(2,1)S(1)} %get-tuple-element.32), channel_id=1, source_target_pairs={{0,4},{4,0},{8,12},{12,8},{1,5},{5,1},{9,13},{13,9},{2,6},{6,2},{1... | collective-permute-start | bytes 98312 | tf_op jit(solution)/shard_map/ppermute | solution.py:220

commit v11 on v9

--- a/solution.py
+++ b/solution.py
@@ -13,13 +13,22 @@
 HBM = pl.BlockSpec(memory_space=pltpu.HBM)
 
 
-def fetch_kernel(tokens, first, second, mine, sems):
-    half = first.shape[1]
-    core = lax.rem(lax.axis_index("etp"), 2)
-    starts = (0, half, pl.multiple_of(core * half, half))
+def fetch_kernel(tokens, share, first, *refs):
+    quarters, sems = refs[:4], refs[4]
+    half, part, wide = first.shape[1], share.shape[1], quarters[0].shape[1]
+    me = lax.axis_index("etp")
+    core, pair = lax.rem(me, 2), lax.div(me, 2)
+    moves = [
+        (share, pl.multiple_of(pair * part, part)),
+        (quarters[0], half),
+        (quarters[1], half + wide),
+        (quarters[2], pl.multiple_of(core * half, wide)),
+        (quarters[3], pl.multiple_of(core * half + wide, wide)),
+        (first, 0),
+    ]
     copies = [
-        pltpu.make_async_copy(tokens.at[:, pl.ds(start, half)], out, sems.at[i])
-        for i, (start, out) in enumerate(zip(starts, (first, second, mine)))
+        pltpu.make_async_copy(tokens.at[:, pl.ds(start, out.shape[1])], out, sems.at[i])
+        for i, (out, start) in enumerate(moves)
     ]
     for copy in copies:
         copy.start()
@@ -48,14 +57,22 @@
 CONTRACT = (((1,), (1,)), ((), ()))
 
 
-def gate_up(part, own, next_block, next_swapped, far, w_gate, w_up, x):
+def gate_up(part, own, near, far, w_gate, w_up, x):
     core = lax.rem(lax.axis_index("etp"), 2)
-    tok, half = own.shape
-    x[0:tok, :] = own[...]
-    x[tok : 2 * tok, :] = jnp.where(core == part, next_block[...], next_swapped[...])
-    for i in range(0, len(far), 2):
-        for block, k in ((far[i], i + 2 + core), (far[i + 1], i + 3 - core)):
-            x[pl.ds(pl.multiple_of(k * tok, tok), tok), :] = block[...]
+    tok, half = own[0].shape[0], x.shape[1]
+    for i, block in enumerate(own):
+        wide = block.shape[1]
+        x[0:tok, i * wide : (i + 1) * wide] = block[...]
+    wide = near[0].shape[1]
+    for i in range(2):
+        x[tok : 2 * tok, i * wide : (i + 1) * wide] = jnp.where(
+            core == part, near[i][...], near[2 + i][...]
+        )
+    for block, swapped, two, start in far:
+        wide = block.shape[1]
+        cols = pl.ds(start if isinstance(start, int) else pl.multiple_of(start, wide), wide)
+        for ref, k in ((block, 2 * two + 2 + core), (swapped, 2 * two + 3 - core)):
+            x[pl.ds(pl.multiple_of(k * tok, tok), tok), cols] = ref[...]
     cols = slice(part * half, (part + 1) * half)
     return [
         lax.dot_general(w[0, :, cols], x[...], CONTRACT, preferred_element_type=jnp.float32)
@@ -63,17 +80,23 @@
     ]
 
 
-def first_kernel(own, next_block, next_swapped, *refs):
-    far, (w_gate, w_up, gate, upper, x) = refs[:-5], refs[-5:]
-    gate[...], upper[...] = gate_up(
-        0, own, next_block, next_swapped, far, w_gate, w_up, x
-    )
-
-
-def second_kernel(parts, own, next_block, next_swapped, *refs):
-    far, refs = refs[:-10], refs[-10:]
+def first_kernel(pairs, own, *refs):
+    near, far, (w_gate, w_up, gate, upper, x) = refs[:4], refs[4:-5], refs[-5:]
+    pair = lax.div(lax.axis_index("etp"), 2)
+    wide = far[0].shape[1]
+    placed = []
+    for i in range(0, len(far), 2):
+        two, h = divmod(i // 2, pairs)
+        placed.append((far[i], far[i + 1], two, lax.rem(pair - h + pairs, pairs) * wide))
+    gate[...], upper[...] = gate_up(0, [own], near, placed, w_gate, w_up, x)
+
+
+def second_kernel(parts, *refs):
+    own, near, far, refs = refs[:2], refs[2:6], refs[6:-10], refs[-10:]
     w_gate, w_up, gate, upper, order, w_down, kept, sent, rest, x = refs
-    more_gate, more_upper = gate_up(1, own, next_block, next_swapped, far, w_gate, w_up, x)
+    wide = far[0].shape[1]
+    placed = [(far[i], far[i + 1], i // 4, i // 2 % 2 * wide) for i in range(0, len(far), 2)]
+    more_gate, more_upper = gate_up(1, own, near, placed, w_gate, w_up, x)
     gate = gate[...] + more_gate
     upper = upper[...] + more_upper
     hidden = (gate / (1.0 + jnp.exp(-gate)) * upper).astype(jnp.bfloat16)
@@ -146,13 +169,16 @@
     pairs = n_etp // 2
     side = n_expert * tok // 2
 
-    column_half = jax.ShapeDtypeStruct((tok, width // 2), tokens.dtype)
-    first, second, mine = pl.pallas_call(
+    def columns(count):
+        return jax.ShapeDtypeStruct((tok, count), tokens.dtype)
+
+    half, quarter = width // 2, width // 4
+    share, first, *quarters = pl.pallas_call(
         fetch_kernel,
-        out_shape=[column_half] * 3,
+        out_shape=[columns(half // pairs), columns(half)] + [columns(quarter)] * 4,
         in_specs=[HBM],
-        out_specs=[VMEM] * 3,
-        scratch_shapes=[pltpu.SemaphoreType.DMA((3,))],
+        out_specs=[VMEM] * 6,
+        scratch_shapes=[pltpu.SemaphoreType.DMA((6,))],
         compiler_params=GRANT,
         name="fetch",
     )(pltpu.with_memory_space_constraint(tokens, pltpu.HBM))
@@ -165,7 +191,7 @@
         compiler_params=GRANT,
         name="order",
     )(first)
-    first, second, mine, order = lax.optimization_barrier((first, second, mine, order))
+    quarters, order = lax.optimization_barrier((quarters, order))
 
     swap = [(t, t ^ 1) for t in range(n_etp)]
     routes = [
@@ -181,17 +207,27 @@
         block = lax.ppermute(block, axes, route)
         return [block, lax.ppermute(block, "etp", swap)]
 
-    far_first = [b for route in routes for b in exchange(first, ("expert", "etp"), route)]
-    near = exchange(mine, "expert", [(e, e ^ 1) for e in range(n_expert)])
-    far_second = [b for route in routes for b in exchange(second, ("expert", "etp"), route)]
+    turns = [
+        [(t, 2 * ((t // 2 + h) % pairs) + t % 2) for t in range(n_etp)] for h in range(1, pairs)
+    ]
+    far_first, far_second = [], []
+    for route in routes:
+        block = lax.ppermute(share, ("expert", "etp"), route)
+        for piece in [block] + [lax.ppermute(block, "etp", turn) for turn in turns]:
+            far_first += [piece, lax.ppermute(piece, "etp", swap)]
+        for piece in quarters[:2]:
+            far_second += exchange(piece, ("expert", "etp"), route)
+    next_route = [(e, e ^ 1) for e in range(n_expert)]
+    near = [exchange(piece, "expert", next_route) for piece in quarters[2:]]
+    near = [near[0][0], near[1][0], near[0][1], near[1][1]]
 
     parts = 4
     hidden = w_gate.shape[1]
     scratch = [pltpu.VMEM((n_expert * tok, width // 2), jnp.bfloat16)]
     gate, upper = pl.pallas_call(
-        first_kernel,
+        functools.partial(first_kernel, pairs),
         out_shape=[jax.ShapeDtypeStruct((hidden, n_expert * tok), jnp.float32)] * 2,
-        in_specs=[VMEM] * (n_expert + 3),
+        in_specs=[VMEM] * (7 + len(far_first)),
         out_specs=[VMEM] * 2,
         scratch_shapes=scratch,
         compiler_params=GRANT,
@@ -204,12 +240,12 @@
     far_kept, far_sent, rest = pl.pallas_call(
         functools.partial(second_kernel, parts),
         out_shape=halves + [jax.ShapeDtypeStruct((side, hidden), jnp.bfloat16)],
-        in_specs=[VMEM] * (n_expert + 7),
+        in_specs=[VMEM] * (12 + len(far_second)),
         out_specs=[VMEM] * 3,
         scratch_shapes=scratch,
         compiler_params=GRANT,
         name="second",
-    )(second, *near, *far_second, w_gate, w_up, gate, upper, order, w_down)
+    )(*quarters[:2], *near, *far_second, w_gate, w_up, gate, upper, order, w_down)
     near_kept, near_sent = pl.pallas_call(
         functools.partial(down_kernel, parts),
         out_shape=halves,
@@ -232,10 +268,7 @@
             compiler_params=GRANT,
             name="add",
         )(kept, arrived)
-        landed = []
-        for h, piece in enumerate(others, 1):
-            route = [(t, 2 * ((t // 2 + h) % pairs) + t % 2) for t in range(n_etp)]
-            landed.append(lax.ppermute(piece, "etp", route))
+        landed = [lax.ppermute(piece, "etp", turn) for piece, turn in zip(others, turns)]
         folded = pl.pallas_call(
             functools.partial(fold_kernel, pairs),
             out_shape=[jax.ShapeDtypeStruct((rows, width), jnp.bfloat16)] * (n_expert // 2),

time: 29.8 us -> 33 us (1.11)
  starting transfers between devices: 12.6 us -> 19.7 us
  waiting for transfers between devices: 11.8 us -> 7.74 us
    ppermute x2 -> x6, starting transfers between devices: 2.34 us -> 8.96 us  [the longest x1 4.1 us: on_device(): block = lax.ppermute(share, ('expert', 'etp'), route)]
    ppermute x3 -> x4, waiting for transfers between devices: 6.15 us -> 1.12 us  [exchange(): block = lax.ppermute(block, axes, route)]
    ppermute x3 -> x4, starting transfers between devices: 6.01 us -> 4.79 us  [exchange(): block = lax.ppermute(block, axes, route)]
    ppermute x3, starting transfers between devices: 3.61 us -> 4.78 us  [on_device(): lax.ppermute(pieces[k], 'expert', [(e, e ^ k) for e in range(n_expert)])]
    ppermute x3, waiting for transfers between devices: 2.67 us -> 3.78 us  [on_device(): lax.ppermute(pieces[k], 'expert', [(e, e ^ k) for e in range(n_expert)])]
    ppermute x3 -> x4, starting transfers between devices: 0.01 us -> 0.57 us  [exchange(): return [block, lax.ppermute(block, 'etp', swap)]]
    ppermute x3 -> x4, waiting for transfers between devices: 0.55 us -> 0.01 us  [exchange(): return [block, lax.ppermute(block, 'etp', swap)]]
    ppermute x2 -> x6, waiting for transfers between devices: 2.23 us -> 2.66 us  [the longest x2 2.6 us: on_device(): lax.ppermute(piece, 'etp', turn)]
  transfers between devices with their start and end apart: 13 -> 19, of which waited for: 8 -> 5; matrix products, arithmetic and copies ran while one was open for 0% -> 0% of each run, Pallas kernels for 6% -> 5%
where the time goes in v11:
time: 33 us; the launch traced here: 32.9 us
  starting transfers between devices  19.7 us (60%)
  waiting for transfers between devices  7.74 us (23%)
  Pallas kernels  5.31 us (16%)
    ppermute x4, starting transfers between devices, exchange(): block = lax.ppermute(block, axes, route)  4.79 us
    ppermute x3, starting transfers between devices, on_device(): lax.ppermute(pieces[k], 'expert', [(e, e ^ k) for e in range(n_expert)])  4.78 us
    ppermute x1, starting transfers between devices, on_device(): block = lax.ppermute(share, ('expert', 'etp'), route)  4.1 us
    ppermute x3, waiting for transfers between devices, on_device(): lax.ppermute(pieces[k], 'expert', [(e, e ^ k) for e in range(n_expert)])  3.78 us
    ppermute x2, waiting for transfers between devices, on_device(): lax.ppermute(piece, 'etp', turn)  2.6 us
    ppermute x2, starting transfers between devices, on_device(): lax.ppermute(piece, 'etp', turn)  2.16 us
    ppermute x1, starting transfers between devices, on_device(): lax.ppermute(block, 'etp', turn)  1.75 us
    pallas_call x1, Pallas kernels, on_device(): pl.pallas_call(functools.partial(second_kernel, parts), out_shape=halves...  1.73 us
  transfers between devices with their start and end apart: 19, of which 5 were waited for; matrix products, arithmetic and copies ran while one was open for 0% of the time, Pallas kernels for 5%

profile of v11, /device:TPU:0, one launch (start us, length us, event | category | flops | bytes accessed | tf_op | source)
XLA Modules:
  0.0 32.9 jit_solution(14103181273469588765)
XLA Ops:
  0.0 1.1 %fetch.1 = (bf16[16,1024]{1,0:T(8,128)(2,1)S(1)}, bf16[16,2048]{1,0:T(8,128)(2,1)S(1)}, bf16[16,1024]{1,0:T(8,128)(2,1)S(1)}, bf16[16,1024]{1,0:T(8,128)(2,1)S(1...) custom-call(bf16[16,4096]{1,0:T(8,128)(2,1)} %tokens.1), custom_call_target="tpu_custom_call" | custom-call | tf_op jit(solution)/shard_map/fetch/pallas_call | solution.py:176
  1.1 4.1 %collective-permute-start.8 = (bf16[16,1024]{1,0:T(8,128)(2,1)S(1)}, bf16[16,1024]{1,0:T(8,128)(2,1)S(1)}, u32[]{:S(2)}, u32[]{:S(2)}) collective-permute-start(bf16[16,1024]{1,0:T(8,128)(2,1)S(1)} %get-tuple-element.40), channel_id=1, source_target_pairs={{0,8},{1,13},{2,10},{3,15},{4,12},{5,9},{6,14},{7,11},{8,0},{9,5},... | collective-permute-start | bytes 98312 | tf_op jit(solution)/shard_map/ppermute | solution.py:215
  5.2 1.6 %collective-permute-start = (bf16[16,1024]{1,0:T(8,128)(2,1)S(1)}, bf16[16,1024]{1,0:T(8,128)(2,1)S(1)}, u32[]{:S(2)}, u32[]{:S(2)}) collective-permute-start(bf16[16,1024]{1,0:T(8,128)(2,1)S(1)} %get-tuple-element.38), channel_id=1, source_target_pairs={{0,4},{4,0},{8,12},{12,8},{1,5},{5,1},{9,13},{13,9},{2,6},{6,2},{1... | collective-permute-start | bytes 98312 | tf_op jit(solution)/shard_map/ppermute | solution.py:207
  6.9 0.4 %collective-permute-start.1 = (bf16[16,1024]{1,0:T(8,128)(2,1)S(1)}, bf16[16,1024]{1,0:T(8,128)(2,1)S(1)}, u32[]{:S(2)}, u32[]{:S(2)}) collective-permute-start(bf16[16,1024]{1,0:T(8,128)(2,1)S(1)} %get-tuple-element.39), channel_id=1, source_target_pairs={{0,4},{4,0},{8,12},{12,8},{1,5},{5,1},{9,13},{13,9},{2,6},{6,2},{1... | collective-permute-start | bytes 98312 | tf_op jit(solution)/shard_map/ppermute | solution.py:207
  7.4 1.7 %collective-permute-start.10 = (bf16[16,1024]{1,0:T(8,128)(2,1)S(1)}, bf16[16,1024]{1,0:T(8,128)(2,1)S(1)}, u32[]{:S(2)}, u32[]{:S(2)}) collective-permute-start(bf16[16,1024]{1,0:T(8,128)(2,1)S(1)} %collective-permute-done.8.refs_4_), channel_id=1, source_target_pairs={{0,2},{1,3},{2,0},{3,1},{4,6},{5,7},{6,4},{7,5},{8,10},{9,11},{10,... | collective-permute-start | bytes 98312 | tf_op jit(solution)/shard_map/ppermute | solution.py:216
  9.2 2.7 %collective-permute-start.6 = (bf16[16,1024]{1,0:T(8,128)(2,1)S(1)}, bf16[16,1024]{1,0:T(8,128)(2,1)S(1)}, u32[]{:S(2)}, u32[]{:S(2)}) collective-permute-start(bf16[16,1024]{1,0:T(8,128)(2,1)S(1)} %get-tuple-element.37.refs_1_), channel_id=1, source_target_pairs={{0,8},{1,13},{2,10},{3,15},{4,12},{5,9},{6,14},{7,11},{8,0},{9,5},... | collective-permute-start | bytes 98312 | tf_op jit(solution)/shard_map/ppermute | solution.py:207
  11.8 0.5 %collective-permute-start.9 = (bf16[16,1024]{1,0:T(8,128)(2,1)S(1)}, bf16[16,1024]{1,0:T(8,128)(2,1)S(1)}, u32[]{:S(2)}, u32[]{:S(2)}) collective-permute-start(bf16[16,1024]{1,0:T(8,128)(2,1)S(1)} %collective-permute-done.8.refs_4_), channel_id=1, source_target_pairs={{0,1},{1,0},{2,3},{3,2},{4,5},{5,4},{6,7},{7,6},{8,9},{9,8},{10,11... | collective-permute-start | bytes 98312 | tf_op jit(solution)/shard_map/ppermute | solution.py:217
  12.4 0.5 %collective-permute-start.11 = (bf16[16,1024]{1,0:T(8,128)(2,1)S(1)}, bf16[16,1024]{1,0:T(8,128)(2,1)S(1)}, u32[]{:S(2)}, u32[]{:S(2)}) collective-permute-start(bf16[16,1024]{1,0:T(8,128)(2,1)S(1)} %collective-permute-done.10.refs_6_), channel_id=1, source_target_pairs={{0,1},{1,0},{2,3},{3,2},{4,5},{5,4},{6,7},{7,6},{8,9},{9,8},{10,11... | collective-permute-start | bytes 98312 | tf_op jit(solution)/shard_map/ppermute | solution.py:217
  12.9 1.1 %collective-permute-done.6.refs_8_ = bf16[16,1024]{1,0:T(8,128)(2,1)S(1)} collective-permute-done((bf16[16,1024]{1,0:T(8,128)(2,1)S(1)}, bf16[16,1024]{1,0:T(8,128)(2,1)S(1)}, u32[]{:S(2)}, u32[]{:S(2)}) %collective-permute-start.6) | collective-permute-done | bytes 32800 | tf_op jit(solution)/shard_map/ppermute | solution.py:207
  14.0 0.5 %collective-permute-start.7 = (bf16[16,1024]{1,0:T(8,128)(2,1)S(1)}, bf16[16,1024]{1,0:T(8,128)(2,1)S(1)}, u32[]{:S(2)}, u32[]{:S(2)}) collective-permute-start(bf16[16,1024]{1,0:T(8,128)(2,1)S(1)} %collective-permute-done.6.refs_8_), channel_id=1, source_target_pairs={{0,1},{1,0},{2,3},{3,2},{4,5},{5,4},{6,7},{7,6},{8,9},{9,8},{10,11... | collective-permute-start | bytes 98312 | tf_op jit(solution)/shard_map/ppermute | solution.py:208
  14.5 1.0 %first.1 = (f32[384,64]{1,0:T(8,128)S(1)}, f32[384,64]{1,0:T(8,128)S(1)}) custom-call(bf16[16,2048]{1,0:T(8,128)(2,1)S(1)} %get-tuple-element.35.first.own, bf16[16,1024]{1,0:T(8,128)(2,1)S(1)} %collective-permute-done.refs_0_.refs_2_, bf16[16,1024]{1,0:T(8,128)(2,1)S(1)} %collective-permute-done.1.refs_1_.refs_3_, ...), custom_call_target="tpu_custom_call" | custom-call | tf_op jit(solution)/shard_map/first/pallas_call | solution.py:227
  15.5 1.7 %second.1 = (f32[16,4096]{1,0:T(8,128)S(1)}, bf16[16,4096]{1,0:T(8,128)(2,1)S(1)}, bf16[32,384]{1,0:T(8,128)(2,1)S(1)}) custom-call(bf16[16,1024]{1,0:T(8,128)(2,1)S(1)} %get-tuple-element.36.refs_0_, bf16[16,1024]{1,0:T(8,128)(2,1)S(1)} %get-tuple-element.37.refs_1_, bf16[16,1024]{1,0:T(8,128)(2,1)S(1)} %collective-permute-done.refs_0_.refs_2_, ...), custom_call_target="tpu_custom_call" | custom-call | tf_op jit(solution)/shard_map/second/pallas_call | solution.py:240
  17.3 0.2 collective-permute-start.15
  17.5 0.6 %down.1 = (f32[16,4096]{1,0:T(8,128)S(1)}, bf16[16,4096]{1,0:T(8,128)(2,1)S(1)}) custom-call(bf16[32,384]{1,0:T(8,128)(2,1)S(1)} %get-tuple-element.44.hidden, bf16[1,384,4096]{2,1,0:T(8,128)(2,1)S(1)} %copy-done.2), custom_call_target="tpu_custom_call" | custom-call | tf_op jit(solution)/shard_map/down/pallas_call | solution.py:249
  18.1 0.4 %collective-permute-start.12 = (bf16[16,4096]{1,0:T(8,128)(2,1)S(1)}, bf16[16,4096]{1,0:T(8,128)(2,1)S(1)}, u32[]{:S(2)}, u32[]{:S(2)}) collective-permute-start(bf16[16,4096]{1,0:T(8,128)(2,1)S(1)} %get-tuple-element.46), channel_id=1, source_target_pairs={{0,1},{1,0},{2,3},{3,2},{4,5},{5,4},{6,7},{7,6},{8,9},{9,8},{10,11... | collective-permute-start | bytes 393224 | tf_op jit(solution)/shard_map/ppermute | solution.py:261
  18.5 0.2 collective-permute-done.15.arrived
  18.7 1.1 %collective-permute-start.16 = (bf16[8,4096]{1,0:T(8,128)(2,1)S(1)}, bf16[8,4096]{1,0:T(8,128)(2,1)S(1)}, u32[]{:S(2)}, u32[]{:S(2)}) collective-permute-start(bf16[8,4096]{1,0:T(8,128)(2,1)S(1)} %get-tuple-element.54), channel_id=1, source_target_pairs={{0,2},{1,3},{2,0},{3,1},{4,6},{5,7},{6,4},{7,5},{8,10},{9,11},{10,... | collective-permute-start | bytes 196616 | tf_op jit(solution)/shard_map/ppermute | solution.py:271
  19.9 1.0 %collective-permute-start.13 = (bf16[8,4096]{1,0:T(8,128)(2,1)S(1)}, bf16[8,4096]{1,0:T(8,128)(2,1)S(1)}, u32[]{:S(2)}, u32[]{:S(2)}) collective-permute-start(bf16[8,4096]{1,0:T(8,128)(2,1)S(1)} %get-tuple-element.48), channel_id=1, source_target_pairs={{0,2},{1,3},{2,0},{3,1},{4,6},{5,7},{6,4},{7,5},{8,10},{9,11},{10,... | collective-permute-start | bytes 196616 | tf_op jit(solution)/shard_map/ppermute | solution.py:271
  20.9 2.6 %collective-permute-done.16.refs_0_ = bf16[8,4096]{1,0:T(8,128)(2,1)S(1)} collective-permute-done((bf16[8,4096]{1,0:T(8,128)(2,1)S(1)}, bf16[8,4096]{1,0:T(8,128)(2,1)S(1)}, u32[]{:S(2)}, u32[]{:S(2)}) %collective-permute-start.16) | collective-permute-done | bytes 65568 | tf_op jit(solution)/shard_map/ppermute | solution.py:271
  23.6 2.8 %collective-permute-start.17 = (bf16[4,4096]{1,0:T(4,128)(2,1)S(1)}, bf16[4,4096]{1,0:T(4,128)(2,1)S(1)}, u32[]{:S(2)}, u32[]{:S(2)}) collective-permute-start(bf16[4,4096]{1,0:T(4,128)(2,1)S(1)} %get-tuple-element.55), channel_id=1, source_target_pairs={{0,8},{4,12},{8,0},{12,4},{1,9},{5,13},{9,1},{13,5},{2,10},{6,14},... | collective-permute-start | bytes 98312 | tf_op jit(solution)/shard_map/ppermute | solution.py:283
  26.3 1.5 %collective-permute-start.18 = (bf16[4,4096]{1,0:T(4,128)(2,1)S(1)}, bf16[4,4096]{1,0:T(4,128)(2,1)S(1)}, u32[]{:S(2)}, u32[]{:S(2)}) collective-permute-start(bf16[4,4096]{1,0:T(4,128)(2,1)S(1)} %get-tuple-element.56), channel_id=1, source_target_pairs={{0,12},{4,8},{8,4},{12,0},{1,13},{5,9},{9,5},{13,1},{2,14},{6,10},... | collective-permute-start | bytes 98312 | tf_op jit(solution)/shard_map/ppermute | solution.py:283
  27.8 0.6 %collective-permute-start.14 = (bf16[4,4096]{1,0:T(4,128)(2,1)S(1)}, bf16[4,4096]{1,0:T(4,128)(2,1)S(1)}, u32[]{:S(2)}, u32[]{:S(2)}) collective-permute-start(bf16[4,4096]{1,0:T(4,128)(2,1)S(1)} %get-tuple-element.50), channel_id=1, source_target_pairs={{0,4},{4,0},{8,12},{12,8},{1,5},{5,1},{9,13},{13,9},{2,6},{6,2},{1... | collective-permute-start | bytes 98312 | tf_op jit(solution)/shard_map/ppermute | solution.py:283
  28.4 3.7 %collective-permute-done.18.refs_3_ = bf16[4,4096]{1,0:T(4,128)(2,1)S(1)} collective-permute-done((bf16[4,4096]{1,0:T(4,128)(2,1)S(1)}, bf16[4,4096]{1,0:T(4,128)(2,1)S(1)}, u32[]{:S(2)}, u32[]{:S(2)}) %collective-permute-start.18) | collective-permute-done | bytes 32800 | tf_op jit(solution)/shard_map/ppermute | solution.py:283
  32.1 0.7 %mix.1 = bf16[4,4096]{1,0:T(4,128)(2,1)} custom-call(s32[2,16]{1,0:T(2,128)S(1)} %bitcast.2, f32[2,4]{1,0:T(2,128)S(1)} %bitcast.3, bf16[4,4096]{1,0:T(4,128)(2,1)S(1)} %get-tuple-element.49.refs_0_, bf16[4,4096]{1,0:T(4,128)(2,1)S(1)} %collective-permute-done.14.refs_1_, bf16[4,4096]{1,0:T(4,128)(2,1)S(1)} %collective-permute-done.17.refs_2_, ...), custom_call_target="tpu_custom_call" | custom-call | tf_op jit(solution)/shard_map/mix/pallas_call | solution.py:286
  (34 shorter events, 0.5 us)
Async XLA Ops:
  1.1 6.3 %collective-permute-start.8 = (bf16[16,1024]{1,0:T(8,128)(2,1)S(1)}, bf16[16,1024]{1,0:T(8,128)(2,1)S(1)}, u32[]{:S(2)}, u32[]{:S(2)}) collective-permute-start(bf16[16,1024]{1,0:T(8,128)(2,1)S(1)} %get-tuple-element.40), channel_id=1, source_target_pairs={{0,8},{1,13},{2,10},{3,15},{4,12},{5,9},{6,14},{7,11},{8,0},{9,5},... | collective-permute-start | bytes 98312 | tf_op jit(solution)/shard_map/ppermute | solution.py:215
  5.2 9.3 %copy-start = (bf16[1,384,4096]{2,1,0:T(8,128)(2,1)S(1)}, bf16[1,384,4096]{2,1,0:T(8,128)(2,1)}, u32[]{:S(2)}) copy-start(bf16[1,384,4096]{2,1,0:T(8,128)(2,1)} %refs_10_.1) | copy-start | bytes 9437188
  5.2 9.3 %copy-start.1 = (bf16[1,384,4096]{2,1,0:T(8,128)(2,1)S(1)}, bf16[1,384,4096]{2,1,0:T(8,128)(2,1)}, u32[]{:S(2)}) copy-start(bf16[1,384,4096]{2,1,0:T(8,128)(2,1)} %refs_11_.1) | copy-start | bytes 9437188
  5.2 10.3 %copy-start.2 = (bf16[1,384,4096]{2,1,0:T(8,128)(2,1)S(1)}, bf16[1,384,4096]{2,1,0:T(8,128)(2,1)}, u32[]{:S(2)}) copy-start(bf16[1,384,4096]{2,1,0:T(8,128)(2,1)} %w_down.1) | copy-start | bytes 9437188
  5.2 6.6 %collective-permute-start = (bf16[16,1024]{1,0:T(8,128)(2,1)S(1)}, bf16[16,1024]{1,0:T(8,128)(2,1)S(1)}, u32[]{:S(2)}, u32[]{:S(2)}) collective-permute-start(bf16[16,1024]{1,0:T(8,128)(2,1)S(1)} %get-tuple-element.38), channel_id=1, source_target_pairs={{0,4},{4,0},{8,12},{12,8},{1,5},{5,1},{9,13},{13,9},{2,6},{6,2},{1... | collective-permute-start | bytes 98312 | tf_op jit(solution)/shard_map/ppermute | solution.py:207
  6.9 5.0 %collective-permute-start.1 = (bf16[16,1024]{1,0:T(8,128)(2,1)S(1)}, bf16[16,1024]{1,0:T(8,128)(2,1)S(1)}, u32[]{:S(2)}, u32[]{:S(2)}) collective-permute-start(bf16[16,1024]{1,0:T(8,128)(2,1)S(1)} %get-tuple-element.39), channel_id=1, source_target_pairs={{0,4},{4,0},{8,12},{12,8},{1,5},{5,1},{9,13},{13,9},{2,6},{6,2},{1... | collective-permute-start | bytes 98312 | tf_op jit(solution)/shard_map/ppermute | solution.py:207
  7.3 5.0 %collective-permute-start.4 = (bf16[16,1024]{1,0:T(8,128)(2,1)S(1)}, bf16[16,1024]{1,0:T(8,128)(2,1)S(1)}, u32[]{:S(2)}, u32[]{:S(2)}) collective-permute-start(bf16[16,1024]{1,0:T(8,128)(2,1)S(1)} %get-tuple-element.36.refs_0_), channel_id=1, source_target_pairs={{0,8},{1,13},{2,10},{3,15},{4,12},{5,9},{6,14},{7,11},{8,0},{9,5},... | collective-permute-start | bytes 98312 | tf_op jit(solution)/shard_map/ppermute | solution.py:207
  7.4 5.0 %collective-permute-start.10 = (bf16[16,1024]{1,0:T(8,128)(2,1)S(1)}, bf16[16,1024]{1,0:T(8,128)(2,1)S(1)}, u32[]{:S(2)}, u32[]{:S(2)}) collective-permute-start(bf16[16,1024]{1,0:T(8,128)(2,1)S(1)} %collective-permute-done.8.refs_4_), channel_id=1, source_target_pairs={{0,2},{1,3},{2,0},{3,1},{4,6},{5,7},{6,4},{7,5},{8,10},{9,11},{10,... | collective-permute-start | bytes 98312 | tf_op jit(solution)/shard_map/ppermute | solution.py:216
  9.2 4.8 %collective-permute-start.6 = (bf16[16,1024]{1,0:T(8,128)(2,1)S(1)}, bf16[16,1024]{1,0:T(8,128)(2,1)S(1)}, u32[]{:S(2)}, u32[]{:S(2)}) collective-permute-start(bf16[16,1024]{1,0:T(8,128)(2,1)S(1)} %get-tuple-element.37.refs_1_), channel_id=1, source_target_pairs={{0,8},{1,13},{2,10},{3,15},{4,12},{5,9},{6,14},{7,11},{8,0},{9,5},... | collective-permute-start | bytes 98312 | tf_op jit(solution)/shard_map/ppermute | solution.py:207
  11.8 2.2 %collective-permute-start.2 = (bf16[16,1024]{1,0:T(8,128)(2,1)S(1)}, bf16[16,1024]{1,0:T(8,128)(2,1)S(1)}, u32[]{:S(2)}, u32[]{:S(2)}) collective-permute-start(bf16[16,1024]{1,0:T(8,128)(2,1)S(1)} %collective-permute-done.refs_0_.refs_2_), channel_id=1, source_target_pairs={{0,1},{1,0},{2,3},{3,2},{4,5},{5,4},{6,7},{7,6},{8,9},{9,8},{10,11... | collective-permute-start | bytes 98312 | tf_op jit(solution)/shard_map/ppermute | solution.py:208
  11.8 2.7 %collective-permute-start.9 = (bf16[16,1024]{1,0:T(8,128)(2,1)S(1)}, bf16[16,1024]{1,0:T(8,128)(2,1)S(1)}, u32[]{:S(2)}, u32[]{:S(2)}) collective-permute-start(bf16[16,1024]{1,0:T(8,128)(2,1)S(1)} %collective-permute-done.8.refs_4_), channel_id=1, source_target_pairs={{0,1},{1,0},{2,3},{3,2},{4,5},{5,4},{6,7},{7,6},{8,9},{9,8},{10,11... | collective-permute-start | bytes 98312 | tf_op jit(solution)/shard_map/ppermute | solution.py:217
  12.4 2.1 %collective-permute-start.3 = (bf16[16,1024]{1,0:T(8,128)(2,1)S(1)}, bf16[16,1024]{1,0:T(8,128)(2,1)S(1)}, u32[]{:S(2)}, u32[]{:S(2)}) collective-permute-start(bf16[16,1024]{1,0:T(8,128)(2,1)S(1)} %collective-permute-done.1.refs_1_.refs_3_), channel_id=1, source_target_pairs={{0,1},{1,0},{2,3},{3,2},{4,5},{5,4},{6,7},{7,6},{8,9},{9,8},{10,11... | collective-permute-start | bytes 98312 | tf_op jit(solution)/shard_map/ppermute | solution.py:208
  12.4 2.1 %collective-permute-start.11 = (bf16[16,1024]{1,0:T(8,128)(2,1)S(1)}, bf16[16,1024]{1,0:T(8,128)(2,1)S(1)}, u32[]{:S(2)}, u32[]{:S(2)}) collective-permute-start(bf16[16,1024]{1,0:T(8,128)(2,1)S(1)} %collective-permute-done.10.refs_6_), channel_id=1, source_target_pairs={{0,1},{1,0},{2,3},{3,2},{4,5},{5,4},{6,7},{7,6},{8,9},{9,8},{10,11... | collective-permute-start | bytes 98312 | tf_op jit(solution)/shard_map/ppermute | solution.py:217
  14.0 1.6 %collective-permute-start.5 = (bf16[16,1024]{1,0:T(8,128)(2,1)S(1)}, bf16[16,1024]{1,0:T(8,128)(2,1)S(1)}, u32[]{:S(2)}, u32[]{:S(2)}) collective-permute-start(bf16[16,1024]{1,0:T(8,128)(2,1)S(1)} %collective-permute-done.4.refs_6_), channel_id=1, source_target_pairs={{0,1},{1,0},{2,3},{3,2},{4,5},{5,4},{6,7},{7,6},{8,9},{9,8},{10,11... | collective-permute-start | bytes 98312 | tf_op jit(solution)/shard_map/ppermute | solution.py:208
  14.0 1.6 %collective-permute-start.7 = (bf16[16,1024]{1,0:T(8,128)(2,1)S(1)}, bf16[16,1024]{1,0:T(8,128)(2,1)S(1)}, u32[]{:S(2)}, u32[]{:S(2)}) collective-permute-start(bf16[16,1024]{1,0:T(8,128)(2,1)S(1)} %collective-permute-done.6.refs_8_), channel_id=1, source_target_pairs={{0,1},{1,0},{2,3},{3,2},{4,5},{5,4},{6,7},{7,6},{8,9},{9,8},{10,11... | collective-permute-start | bytes 98312 | tf_op jit(solution)/shard_map/ppermute | solution.py:208
  17.3 14.9 %copy-start.3 = (s32[16,2]{0,1:T(2,128)S(1)}, s32[16,2]{0,1:T(2,128)}, u32[]{:S(2)}) copy-start(s32[16,2]{0,1:T(2,128)} %param.7) | copy-start | bytes 388
  17.3 14.9 %copy-start.4 = (f32[4,2]{0,1:T(2,128)S(1)}, f32[4,2]{0,1:T(2,128)}, u32[]{:S(2)}) copy-start(f32[4,2]{0,1:T(2,128)} %param.8) | copy-start | bytes 100
  17.3 1.4 %collective-permute-start.15 = (bf16[16,4096]{1,0:T(8,128)(2,1)S(1)}, bf16[16,4096]{1,0:T(8,128)(2,1)S(1)}, u32[]{:S(2)}, u32[]{:S(2)}) collective-permute-start(bf16[16,4096]{1,0:T(8,128)(2,1)S(1)} %get-tuple-element.52), channel_id=1, source_target_pairs={{0,1},{1,0},{2,3},{3,2},{4,5},{5,4},{6,7},{7,6},{8,9},{9,8},{10,11... | collective-permute-start | bytes 393224 | tf_op jit(solution)/shard_map/ppermute | solution.py:261
  18.1 1.7 %collective-permute-start.12 = (bf16[16,4096]{1,0:T(8,128)(2,1)S(1)}, bf16[16,4096]{1,0:T(8,128)(2,1)S(1)}, u32[]{:S(2)}, u32[]{:S(2)}) collective-permute-start(bf16[16,4096]{1,0:T(8,128)(2,1)S(1)} %get-tuple-element.46), channel_id=1, source_target_pairs={{0,1},{1,0},{2,3},{3,2},{4,5},{5,4},{6,7},{7,6},{8,9},{9,8},{10,11... | collective-permute-start | bytes 393224 | tf_op jit(solution)/shard_map/ppermute | solution.py:261
  18.7 4.8 %collective-permute-start.16 = (bf16[8,4096]{1,0:T(8,128)(2,1)S(1)}, bf16[8,4096]{1,0:T(8,128)(2,1)S(1)}, u32[]{:S(2)}, u32[]{:S(2)}) collective-permute-start(bf16[8,4096]{1,0:T(8,128)(2,1)S(1)} %get-tuple-element.54), channel_id=1, source_target_pairs={{0,2},{1,3},{2,0},{3,1},{4,6},{5,7},{6,4},{7,5},{8,10},{9,11},{10,... | collective-permute-start | bytes 196616 | tf_op jit(solution)/shard_map/ppermute | solution.py:271
  19.9 7.9 %collective-permute-start.13 = (bf16[8,4096]{1,0:T(8,128)(2,1)S(1)}, bf16[8,4096]{1,0:T(8,128)(2,1)S(1)}, u32[]{:S(2)}, u32[]{:S(2)}) collective-permute-start(bf16[8,4096]{1,0:T(8,128)(2,1)S(1)} %get-tuple-element.48), channel_id=1, source_target_pairs={{0,2},{1,3},{2,0},{3,1},{4,6},{5,7},{6,4},{7,5},{8,10},{9,11},{10,... | collective-permute-start | bytes 196616 | tf_op jit(solution)/shard_map/ppermute | solution.py:271
  23.6 4.9 %collective-permute-start.17 = (bf16[4,4096]{1,0:T(4,128)(2,1)S(1)}, bf16[4,4096]{1,0:T(4,128)(2,1)S(1)}, u32[]{:S(2)}, u32[]{:S(2)}) collective-permute-start(bf16[4,4096]{1,0:T(4,128)(2,1)S(1)} %get-tuple-element.55), channel_id=1, source_target_pairs={{0,8},{4,12},{8,0},{12,4},{1,9},{5,13},{9,1},{13,5},{2,10},{6,14},... | collective-permute-start | bytes 98312 | tf_op jit(solution)/shard_map/ppermute | solution.py:283
  26.3 5.8 %collective-permute-start.18 = (bf16[4,4096]{1,0:T(4,128)(2,1)S(1)}, bf16[4,4096]{1,0:T(4,128)(2,1)S(1)}, u32[]{:S(2)}, u32[]{:S(2)}) collective-permute-start(bf16[4,4096]{1,0:T(4,128)(2,1)S(1)} %get-tuple-element.56), channel_id=1, source_target_pairs={{0,12},{4,8},{8,4},{12,0},{1,13},{5,9},{9,5},{13,1},{2,14},{6,10},... | collective-permute-start | bytes 98312 | tf_op jit(solution)/shard_map/ppermute | solution.py:283
  27.8 4.3 %collective-permute-start.14 = (bf16[4,4096]{1,0:T(4,128)(2,1)S(1)}, bf16[4,4096]{1,0:T(4,128)(2,1)S(1)}, u32[]{:S(2)}, u32[]{:S(2)}) collective-permute-start(bf16[4,4096]{1,0:T(4,128)(2,1)S(1)} %get-tuple-element.50), channel_id=1, source_target_pairs={{0,4},{4,0},{8,12},{12,8},{1,5},{5,1},{9,13},{13,9},{2,6},{6,2},{1... | collective-permute-start | bytes 98312 | tf_op jit(solution)/shard_map/ppermute | solution.py:283

commit v12 on v10

--- a/solution.py
+++ b/solution.py
@@ -34,13 +34,17 @@
     core, pair = lax.rem(me, 2), lax.div(me, 2)
     place = lax.broadcasted_iota(jnp.int32, (total, total), 0)
     source = lax.broadcasted_iota(jnp.int32, (total, total), 1)
-    half = n_expert // 2
+    far = total - 4 * pairs * rows
+    is_near = place >= far
+    place = jnp.where(is_near, place - far, place)
+    count = jnp.where(is_near, 1, n_expert // 2 - 1)
     row = lax.rem(place, rows)
-    k = lax.rem(lax.div(place, rows), half)
-    h = lax.rem(lax.div(place, rows * half), pairs)
-    sent = lax.rem(lax.div(place, rows * half * pairs), 2)
-    k = k + half * (1 - lax.div(place, rows * half * pairs * 2))
-    block = 2 * lax.rem(pair + h, pairs) + lax.rem(core + sent, 2)
+    side = lax.rem(lax.div(place, rows), 2)
+    two = lax.rem(lax.div(place, rows * 2), count)
+    h = lax.rem(lax.div(place, rows * 2 * count), pairs)
+    sent = lax.div(place, rows * 2 * count * pairs)
+    k = jnp.where(is_near, 0, 2 * two + 2) + lax.rem(core + sent, 2)
+    block = 2 * lax.rem(pair + h, pairs) + lax.rem(core + sent + side, 2)
     wanted = (k * pairs * 2 + block) * rows + row
     out[...] = jnp.where(source == wanted, 1.0, 0.0).astype(jnp.bfloat16)
 
@@ -63,7 +67,7 @@
     hidden = (gate / (1.0 + jnp.exp(-gate)) * upper).astype(jnp.bfloat16)
     hidden = lax.dot_general(order[...], hidden, contract, preferred_element_type=jnp.float32)
     hidden = hidden.astype(jnp.bfloat16)
-    now = rest.shape[0]
+    now = hidden.shape[0] - rest.shape[0]
     rest[...] = hidden[now:]
     down(parts, hidden[:now], w_down, kept, sent)
 
@@ -100,10 +104,20 @@
         piece[...] = total[k * rows : (k + 1) * rows].astype(piece.dtype)
 
 
-def mix_kernel(n_expert, ids, weights, *refs):
-    pieces, out = refs[:-1], refs[-1]
+def pack_kernel(near_kept, near_landed, *refs):
+    far, out = refs[:-1], refs[-1]
+    rows = near_kept.shape[0] // 2
+    core = lax.rem(lax.axis_index("etp"), 2)
+    out[:rows] = jnp.where(core == 0, near_kept[rows:], near_landed[rows:])
+    for i, piece in enumerate(far, 1):
+        out[i * rows : (i + 1) * rows] = piece[rows:]
+
+
+def mix_kernel(ids, weights, swapped, near_kept, near_landed, *refs):
+    far, out = refs[:-1], refs[-1]
     rows = out.shape[0]
     me, expert = lax.axis_index("etp"), lax.axis_index("expert")
+    core = lax.rem(me, 2)
     top, tok = ids.shape
 
     def column(ref, start, i):
@@ -116,11 +130,18 @@
     own_weights = [column(weights, 0, i) for i in range(top)]
     scale = sum(own_weights)
     total = None
-    for k in range(n_expert):
-        owner = lax.bitwise_xor(expert, k)
-        factor = sum(jnp.where(own_ids[i] == owner, own_weights[i], 0.0) for i in range(top)) / scale
-        term = pieces[k][...].astype(jnp.float32) * factor
-        total = term if total is None else total + term
+    for i in range(len(far) + 1):
+        if i == 0:
+            mine = jnp.where(core == 0, near_kept[:rows], near_landed[:rows])
+        else:
+            mine = far[i - 1][:rows]
+        for part, k in ((mine, 2 * i + core), (swapped[i * rows : (i + 1) * rows], 2 * i + 1 - core)):
+            owner = lax.bitwise_xor(expert, k)
+            factor = (
+                sum(jnp.where(own_ids[j] == owner, own_weights[j], 0.0) for j in range(top)) / scale
+            )
+            term = part.astype(jnp.float32) * factor
+            total = term if total is None else total + term
     out[...] = total.astype(out.dtype)
 
 
@@ -154,26 +175,28 @@
     mine, order = lax.optimization_barrier((mine, order))
 
     swap = [(t, t ^ 1) for t in range(n_etp)]
-    far = []
-    for k in range(2, n_expert, 2):
-        route = [
+    routes = [
+        [
             (e * n_etp + t, (e ^ (k + t % 2)) * n_etp + t)
             for e in range(n_expert)
             for t in range(n_etp)
         ]
-        far.append(lax.ppermute(tokens, ("expert", "etp"), route))
+        for k in range(2, n_expert, 2)
+    ]
+    far = [lax.ppermute(tokens, ("expert", "etp"), route) for route in routes]
     next_block = lax.ppermute(mine, "expert", [(e, e ^ 1) for e in range(n_expert)])
     near = [next_block, lax.ppermute(next_block, "etp", swap)]
     far = [b for block in far for b in (block, lax.ppermute(block, "etp", swap))]
 
     parts = 4
-    halves = [
-        jax.ShapeDtypeStruct((side // 2, width), jnp.float32),
-        jax.ShapeDtypeStruct((side // 2, width), jnp.bfloat16),
-    ]
+    def halves(experts):
+        shape = (experts * tok // 2, width)
+        return [jax.ShapeDtypeStruct(shape, dtype) for dtype in (jnp.float32, jnp.bfloat16)]
+
     far_kept, far_sent, rest = pl.pallas_call(
         functools.partial(ffn_kernel, n_expert, parts),
-        out_shape=halves + [jax.ShapeDtypeStruct((side, w_gate.shape[1]), jnp.bfloat16)],
+        out_shape=halves(n_expert - 2)
+        + [jax.ShapeDtypeStruct((2 * tok, w_gate.shape[1]), jnp.bfloat16)],
         in_specs=[VMEM] * (n_expert + 5),
         out_specs=[VMEM] * 3,
         scratch_shapes=[pltpu.VMEM((n_expert * tok, width), jnp.bfloat16)],
@@ -182,52 +205,66 @@
     )(own, *near, order, *far, w_gate, w_up, w_down)
     near_kept, near_sent = pl.pallas_call(
         functools.partial(down_kernel, parts),
-        out_shape=halves,
+        out_shape=halves(2),
         in_specs=[VMEM] * 2,
         out_specs=[VMEM] * 2,
         compiler_params=GRANT,
         name="down",
     )(rest, w_down)
 
-    block = n_expert // 2 * rows
-    pieces = []
-    for kept, sent in ((far_kept, far_sent), (near_kept, near_sent)):
-        arrived = lax.ppermute(sent, "etp", swap)
+    turns = [
+        [(t, 2 * ((t // 2 + h) % pairs) + t % 2) for t in range(n_etp)] for h in range(1, pairs)
+    ]
+
+    def over_etp(kept, sent, twos):
+        block = (kept.shape[0] // pairs, width)
         own, *others = pl.pallas_call(
             add_kernel,
-            out_shape=[jax.ShapeDtypeStruct((block, width), jnp.float32)]
-            + [jax.ShapeDtypeStruct((block, width), jnp.bfloat16)] * (pairs - 1),
+            out_shape=[jax.ShapeDtypeStruct(block, jnp.float32)]
+            + [jax.ShapeDtypeStruct(block, jnp.bfloat16)] * (pairs - 1),
             in_specs=[VMEM] * 2,
             out_specs=[VMEM] * pairs,
             compiler_params=GRANT,
             name="add",
-        )(kept, arrived)
-        landed = []
-        for h, piece in enumerate(others, 1):
-            route = [(t, 2 * ((t // 2 + h) % pairs) + t % 2) for t in range(n_etp)]
-            landed.append(lax.ppermute(piece, "etp", route))
-        folded = pl.pallas_call(
+        )(kept, lax.ppermute(sent, "etp", swap))
+        landed = [lax.ppermute(piece, "etp", turn) for piece, turn in zip(others, turns)]
+        return pl.pallas_call(
             functools.partial(fold_kernel, pairs),
-            out_shape=[jax.ShapeDtypeStruct((rows, width), jnp.bfloat16)] * (n_expert // 2),
+            out_shape=[jax.ShapeDtypeStruct((2 * rows, width), jnp.bfloat16)] * twos,
             in_specs=[VMEM] * pairs,
-            out_specs=[VMEM] * (n_expert // 2),
+            out_specs=[VMEM] * twos,
             compiler_params=GRANT,
             name="fold",
         )(own, *landed)
-        pieces = list(folded) + pieces
-    landed = []
-    for k in range(n_expert - 1, 0, -1):
-        landed.insert(0, lax.ppermute(pieces[k], "expert", [(e, e ^ k) for e in range(n_expert)]))
-    landed.insert(0, pieces[0])
+
+    twos = n_expert // 2
+    far = [
+        lax.ppermute(piece, ("expert", "etp"), route)
+        for piece, route in zip(over_etp(far_kept, far_sent, twos - 1), routes)
+    ]
+    (near_kept,) = over_etp(near_kept, near_sent, 1)
+    odd = [
+        (e * n_etp + t, (e ^ 1) * n_etp + t) for e in range(n_expert) for t in range(1, n_etp, 2)
+    ]
+    near_landed = lax.ppermute(near_kept, ("expert", "etp"), odd)
+    packed = pl.pallas_call(
+        pack_kernel,
+        out_shape=jax.ShapeDtypeStruct((twos * rows, width), jnp.bfloat16),
+        in_specs=[VMEM] * (twos + 1),
+        out_specs=VMEM,
+        compiler_params=GRANT,
+        name="pack",
+    )(near_kept, near_landed, *far)
+    swapped = lax.ppermute(packed, "etp", swap)
 
     return pl.pallas_call(
-        functools.partial(mix_kernel, n_expert),
+        mix_kernel,
         out_shape=jax.ShapeDtypeStruct((rows, width), jnp.bfloat16),
-        in_specs=[VMEM] * (2 + n_expert),
+        in_specs=[VMEM] * (twos + 4),
         out_specs=VMEM,
         compiler_params=GRANT,
         name="mix",
-    )(expert_ids.T, route_weights.T, *landed)
+    )(expert_ids.T, route_weights.T, swapped, near_kept, near_landed, *far)
 
 
 def solution(mesh):

time: 29.2 us -> 29.8 us (1.021)
  waiting for transfers between devices: 10.9 us -> 12.5 us
  starting transfers between devices: 12.9 us -> 12 us
    ppermute x8, waiting for transfers between devices: 9.99 us -> 11.5 us  [the longest x1 4.05 us: on_device(): far = [lax.ppermute(tokens, ('expert', 'etp'), route) for route in routes]]
    ppermute x8, starting transfers between devices: 10.8 us -> 9.84 us  [the longest x1 4.04 us: on_device(): far = [lax.ppermute(tokens, ('expert', 'etp'), route) for route in routes]]
    pallas_call x6 -> x7, Pallas kernels: 1.49 us -> 1.52 us  [the longest x1 0.77 us: on_device(): pl.pallas_call(mix_kernel, out_shape=jax.ShapeDtypeStruct((rows, width),...]
where the time goes in v12:
time: 29.8 us; the launch traced here: 29.7 us
  waiting for transfers between devices  12.5 us (42%)
  starting transfers between devices  12 us (40%)
  Pallas kernels  5.1 us (17%)
    ppermute x1, waiting for transfers between devices, on_device(): far = [lax.ppermute(tokens, ('expert', 'etp'), route) for route in routes]  4.05 us
    ppermute x1, starting transfers between devices, on_device(): far = [lax.ppermute(tokens, ('expert', 'etp'), route) for route in routes]  4.04 us
    ppermute x1, waiting for transfers between devices, on_device(): lax.ppermute(piece, ('expert', 'etp'), route)  3.87 us
    ppermute x2, waiting for transfers between devices, over_etp(): lax.ppermute(piece, 'etp', turn)  2.55 us
    pallas_call x1, Pallas kernels, on_device(): pl.pallas_call(functools.partial(ffn_kernel, n_expert, parts), out_shape=...  2.54 us
    ppermute x2, starting transfers between devices, over_etp(): lax.ppermute(piece, 'etp', turn)  2.52 us
    ppermute x1, starting transfers between devices, on_device(): lax.ppermute(mine, 'expert', [(e, e ^ 1) for e in range(n_expert)])  1.64 us
    ppermute x1, starting transfers between devices, on_device(): swapped = lax.ppermute(packed, 'etp', swap)  1.21 us
  transfers between devices with their start and end apart: 11, of which 7 were waited for; matrix products, arithmetic and copies ran while one was open for 0% of the time, Pallas kernels for 6%

profile of v12, /device:TPU:0, one launch (start us, length us, event | category | flops | bytes accessed | tf_op | source)
XLA Modules:
  0.0 29.7 jit_solution(17947292850038373626)
XLA Ops:
  0.0 4.0 %collective-permute-start.2 = (bf16[16,4096]{1,0:T(8,128)(2,1)}, bf16[16,4096]{1,0:T(8,128)(2,1)S(1)}, u32[]{:S(2)}, u32[]{:S(2)}) collective-permute-start(bf16[16,4096]{1,0:T(8,128)(2,1)} %tokens.1), channel_id=1, source_target_pairs={{0,8},{1,13},{2,10},{3,15},{4,12},{5,9},{6,14},{7,11},{8,0},{9,5},... | collective-permute-start | bytes 393224 | tf_op jit(solution)/shard_map/ppermute | solution.py:186
  4.0 1.0 %fetch.1 = (bf16[16,4096]{1,0:T(8,128)(2,1)S(1)}, bf16[16,2048]{1,0:T(8,128)(2,1)S(1)}) custom-call(bf16[16,4096]{1,0:T(8,128)(2,1)} %tokens.1), custom_call_target="tpu_custom_call" | custom-call | tf_op jit(solution)/shard_map/fetch/pallas_call | solution.py:154
  5.1 0.0 copy-start.2
  5.1 1.6 %collective-permute-start = (bf16[16,2048]{1,0:T(8,128)(2,1)S(1)}, bf16[16,2048]{1,0:T(8,128)(2,1)S(1)}, u32[]{:S(2)}, u32[]{:S(2)}) collective-permute-start(bf16[16,2048]{1,0:T(8,128)(2,1)S(1)} %get-tuple-element.20.mine), channel_id=1, source_target_pairs={{0,4},{4,0},{8,12},{12,8},{1,5},{5,1},{9,13},{13,9},{2,6},{6,2},{1... | collective-permute-start | bytes 196616 | tf_op jit(solution)/shard_map/ppermute | solution.py:187
  6.8 4.1 %collective-permute-done.2.refs_0_ = bf16[16,4096]{1,0:T(8,128)(2,1)S(1)} collective-permute-done((bf16[16,4096]{1,0:T(8,128)(2,1)}, bf16[16,4096]{1,0:T(8,128)(2,1)S(1)}, u32[]{:S(2)}, u32[]{:S(2)}) %collective-permute-start.2) | collective-permute-done | bytes 131104 | tf_op jit(solution)/shard_map/ppermute | solution.py:186
  10.8 0.0 collective-permute-done.next_block
  10.9 0.5 %collective-permute-start.1 = (bf16[16,2048]{1,0:T(8,128)(2,1)S(1)}, bf16[16,2048]{1,0:T(8,128)(2,1)S(1)}, u32[]{:S(2)}, u32[]{:S(2)}) collective-permute-start(bf16[16,2048]{1,0:T(8,128)(2,1)S(1)} %collective-permute-done.next_block), channel_id=1, source_target_pairs={{0,1},{1,0},{2,3},{3,2},{4,5},{5,4},{6,7},{7,6},{8,9},{9,8},{10,11... | collective-permute-start | bytes 196616 | tf_op jit(solution)/shard_map/ppermute | solution.py:188
  11.3 0.9 %collective-permute-done.1.next_swapped = bf16[16,2048]{1,0:T(8,128)(2,1)S(1)} collective-permute-done((bf16[16,2048]{1,0:T(8,128)(2,1)S(1)}, bf16[16,2048]{1,0:T(8,128)(2,1)S(1)}, u32[]{:S(2)}, u32[]{:S(2)}) %collective-permute-start.1) | collective-permute-done | bytes 65568 | tf_op jit(solution)/shard_map/ppermute | solution.py:188
  12.3 2.5 %ffn.1 = (f32[16,4096]{1,0:T(8,128)S(1)}, bf16[16,4096]{1,0:T(8,128)(2,1)S(1)}, bf16[32,384]{1,0:T(8,128)(2,1)S(1)}) custom-call(bf16[16,4096]{1,0:T(8,128)(2,1)S(1)} %get-tuple-element.18.own, bf16[16,2048]{1,0:T(8,128)(2,1)S(1)} %collective-permute-done.next_block, bf16[16,2048]{1,0:T(8,128)(2,1)S(1)} %collective-permute-done.1.next_swapped, ...), custom_call_target="tpu_custom_call" | custom-call | tf_op jit(solution)/shard_map/ffn/pallas_call | solution.py:196
  14.8 0.0 copy-start.4
  14.8 0.4 %collective-permute-start.7 = (bf16[16,4096]{1,0:T(8,128)(2,1)S(1)}, bf16[16,4096]{1,0:T(8,128)(2,1)S(1)}, u32[]{:S(2)}, u32[]{:S(2)}) collective-permute-start(bf16[16,4096]{1,0:T(8,128)(2,1)S(1)} %get-tuple-element.28), channel_id=1, source_target_pairs={{0,1},{1,0},{2,3},{3,2},{4,5},{5,4},{6,7},{7,6},{8,9},{9,8},{10,11... | collective-permute-start | bytes 393224 | tf_op jit(solution)/shard_map/ppermute | solution.py:229
  15.2 0.6 %down.1 = (f32[16,4096]{1,0:T(8,128)S(1)}, bf16[16,4096]{1,0:T(8,128)(2,1)S(1)}) custom-call(bf16[32,384]{1,0:T(8,128)(2,1)S(1)} %get-tuple-element.22.hidden, bf16[1,384,4096]{2,1,0:T(8,128)(2,1)S(1)} %copy-done), custom_call_target="tpu_custom_call" | custom-call | tf_op jit(solution)/shard_map/down/pallas_call | solution.py:206
  15.9 0.2 collective-permute-start.4
  16.1 0.2 collective-permute-done.7.arrived
  16.3 1.6 %collective-permute-start.8 = (bf16[8,4096]{1,0:T(8,128)(2,1)S(1)}, bf16[8,4096]{1,0:T(8,128)(2,1)S(1)}, u32[]{:S(2)}, u32[]{:S(2)}) collective-permute-start(bf16[8,4096]{1,0:T(8,128)(2,1)S(1)} %get-tuple-element.30), channel_id=1, source_target_pairs={{0,2},{1,3},{2,0},{3,1},{4,6},{5,7},{6,4},{7,5},{8,10},{9,11},{10,... | collective-permute-start | bytes 196616 | tf_op jit(solution)/shard_map/ppermute | solution.py:230
  17.9 1.0 %collective-permute-start.5 = (bf16[8,4096]{1,0:T(8,128)(2,1)S(1)}, bf16[8,4096]{1,0:T(8,128)(2,1)S(1)}, u32[]{:S(2)}, u32[]{:S(2)}) collective-permute-start(bf16[8,4096]{1,0:T(8,128)(2,1)S(1)} %get-tuple-element.26), channel_id=1, source_target_pairs={{0,2},{1,3},{2,0},{3,1},{4,6},{5,7},{6,4},{7,5},{8,10},{9,11},{10,... | collective-permute-start | bytes 196616 | tf_op jit(solution)/shard_map/ppermute | solution.py:230
  18.8 2.0 %collective-permute-done.8.refs_0_ = bf16[8,4096]{1,0:T(8,128)(2,1)S(1)} collective-permute-done((bf16[8,4096]{1,0:T(8,128)(2,1)S(1)}, bf16[8,4096]{1,0:T(8,128)(2,1)S(1)}, u32[]{:S(2)}, u32[]{:S(2)}) %collective-permute-start.8) | collective-permute-done | bytes 65568 | tf_op jit(solution)/shard_map/ppermute | solution.py:230
  20.8 0.8 %collective-permute-start.9 = (bf16[8,4096]{1,0:T(8,128)(2,1)S(1)}, bf16[8,4096]{1,0:T(8,128)(2,1)S(1)}, u32[]{:S(2)}, u32[]{:S(2)}) collective-permute-start(bf16[8,4096]{1,0:T(8,128)(2,1)S(1)} %fold.3), channel_id=1, source_target_pairs={{0,8},{1,13},{2,10},{3,15},{4,12},{5,9},{6,14},{7,11},{8,0},{9,5},... | collective-permute-start | bytes 196616 | tf_op jit(solution)/shard_map/ppermute | solution.py:242
  21.6 0.6 %collective-permute-done.5.refs_0_ = bf16[8,4096]{1,0:T(8,128)(2,1)S(1)} collective-permute-done((bf16[8,4096]{1,0:T(8,128)(2,1)S(1)}, bf16[8,4096]{1,0:T(8,128)(2,1)S(1)}, u32[]{:S(2)}, u32[]{:S(2)}) %collective-permute-start.5) | collective-permute-done | bytes 65568 | tf_op jit(solution)/shard_map/ppermute | solution.py:230
  22.2 0.7 %collective-permute-start.6 = (bf16[8,4096]{1,0:T(8,128)(2,1)S(1)}, bf16[8,4096]{1,0:T(8,128)(2,1)S(1)}, u32[]{:S(2)}, u32[]{:S(2)}) collective-permute-start(bf16[8,4096]{1,0:T(8,128)(2,1)S(1)} %fold.2.near_kept), channel_id=1, source_target_pairs={{1,5},{3,7},{5,1},{7,3},{9,13},{11,15},{13,9},{15,11},{17,21},{19,... | collective-permute-start | bytes 196616 | tf_op jit(solution)/shard_map/ppermute | solution.py:249
  22.9 3.9 %collective-permute-done.9.refs_0_ = bf16[8,4096]{1,0:T(8,128)(2,1)S(1)} collective-permute-done((bf16[8,4096]{1,0:T(8,128)(2,1)S(1)}, bf16[8,4096]{1,0:T(8,128)(2,1)S(1)}, u32[]{:S(2)}, u32[]{:S(2)}) %collective-permute-start.9) | collective-permute-done | bytes 65568 | tf_op jit(solution)/shard_map/ppermute | solution.py:242
  26.8 1.2 %collective-permute-start.10 = (bf16[8,4096]{1,0:T(8,128)(2,1)S(1)}, bf16[8,4096]{1,0:T(8,128)(2,1)S(1)}, u32[]{:S(2)}, u32[]{:S(2)}) collective-permute-start(bf16[8,4096]{1,0:T(8,128)(2,1)S(1)} %pack.1), channel_id=1, source_target_pairs={{0,1},{1,0},{2,3},{3,2},{4,5},{5,4},{6,7},{7,6},{8,9},{9,8},{10,11... | collective-permute-start | bytes 196616 | tf_op jit(solution)/shard_map/ppermute | solution.py:258
  28.0 0.9 %collective-permute-done.10.swapped = bf16[8,4096]{1,0:T(8,128)(2,1)S(1)} collective-permute-done((bf16[8,4096]{1,0:T(8,128)(2,1)S(1)}, bf16[8,4096]{1,0:T(8,128)(2,1)S(1)}, u32[]{:S(2)}, u32[]{:S(2)}) %collective-permute-start.10) | collective-permute-done | bytes 65568 | tf_op jit(solution)/shard_map/ppermute | solution.py:258
  28.9 0.8 %mix.1 = bf16[4,4096]{1,0:T(4,128)(2,1)} custom-call(s32[2,16]{1,0:T(2,128)S(1)} %bitcast.2, f32[2,4]{1,0:T(2,128)S(1)} %bitcast.3, bf16[8,4096]{1,0:T(8,128)(2,1)S(1)} %collective-permute-done.10.swapped, bf16[8,4096]{1,0:T(8,128)(2,1)S(1)} %fold.2.near_kept, bf16[8,4096]{1,0:T(8,128)(2,1)S(1)} %collective-permute-done.6.near_landed, ...), custom_call_target="tpu_custom_call" | custom-call | tf_op jit(solution)/shard_map/mix/pallas_call | solution.py:260
  (18 shorter events, 0.2 us)
Async XLA Ops:
  0.0 10.8 %collective-permute-start.2 = (bf16[16,4096]{1,0:T(8,128)(2,1)}, bf16[16,4096]{1,0:T(8,128)(2,1)S(1)}, u32[]{:S(2)}, u32[]{:S(2)}) collective-permute-start(bf16[16,4096]{1,0:T(8,128)(2,1)} %tokens.1), channel_id=1, source_target_pairs={{0,8},{1,13},{2,10},{3,15},{4,12},{5,9},{6,14},{7,11},{8,0},{9,5},... | collective-permute-start | bytes 393224 | tf_op jit(solution)/shard_map/ppermute | solution.py:186
  5.0 7.2 %copy-start = (bf16[1,384,4096]{2,1,0:T(8,128)(2,1)S(1)}, bf16[1,384,4096]{2,1,0:T(8,128)(2,1)}, u32[]{:S(2)}) copy-start(bf16[1,384,4096]{2,1,0:T(8,128)(2,1)} %w_down.1) | copy-start | bytes 9437188
  5.0 7.2 %copy-start.1 = (bf16[1,384,4096]{2,1,0:T(8,128)(2,1)S(1)}, bf16[1,384,4096]{2,1,0:T(8,128)(2,1)}, u32[]{:S(2)}) copy-start(bf16[1,384,4096]{2,1,0:T(8,128)(2,1)} %refs_2_.1) | copy-start | bytes 9437188
  5.1 7.2 %copy-start.2 = (bf16[1,384,4096]{2,1,0:T(8,128)(2,1)S(1)}, bf16[1,384,4096]{2,1,0:T(8,128)(2,1)}, u32[]{:S(2)}) copy-start(bf16[1,384,4096]{2,1,0:T(8,128)(2,1)} %refs_3_.1) | copy-start | bytes 9437188
  5.1 5.7 %collective-permute-start = (bf16[16,2048]{1,0:T(8,128)(2,1)S(1)}, bf16[16,2048]{1,0:T(8,128)(2,1)S(1)}, u32[]{:S(2)}, u32[]{:S(2)}) collective-permute-start(bf16[16,2048]{1,0:T(8,128)(2,1)S(1)} %get-tuple-element.20.mine), channel_id=1, source_target_pairs={{0,4},{4,0},{8,12},{12,8},{1,5},{5,1},{9,13},{13,9},{2,6},{6,2},{1... | collective-permute-start | bytes 196616 | tf_op jit(solution)/shard_map/ppermute | solution.py:187
  10.8 1.4 %collective-permute-start.3 = (bf16[16,4096]{1,0:T(8,128)(2,1)S(1)}, bf16[16,4096]{1,0:T(8,128)(2,1)S(1)}, u32[]{:S(2)}, u32[]{:S(2)}) collective-permute-start(bf16[16,4096]{1,0:T(8,128)(2,1)S(1)} %collective-permute-done.2.refs_0_), channel_id=1, source_target_pairs={{0,1},{1,0},{2,3},{3,2},{4,5},{5,4},{6,7},{7,6},{8,9},{9,8},{10,11... | collective-permute-start | bytes 393224 | tf_op jit(solution)/shard_map/ppermute | solution.py:189
  10.9 1.4 %collective-permute-start.1 = (bf16[16,2048]{1,0:T(8,128)(2,1)S(1)}, bf16[16,2048]{1,0:T(8,128)(2,1)S(1)}, u32[]{:S(2)}, u32[]{:S(2)}) collective-permute-start(bf16[16,2048]{1,0:T(8,128)(2,1)S(1)} %collective-permute-done.next_block), channel_id=1, source_target_pairs={{0,1},{1,0},{2,3},{3,2},{4,5},{5,4},{6,7},{7,6},{8,9},{9,8},{10,11... | collective-permute-start | bytes 196616 | tf_op jit(solution)/shard_map/ppermute | solution.py:188
  14.8 14.1 %copy-start.3 = (s32[16,2]{0,1:T(2,128)S(1)}, s32[16,2]{0,1:T(2,128)}, u32[]{:S(2)}) copy-start(s32[16,2]{0,1:T(2,128)} %param.7) | copy-start | bytes 388
  14.8 14.1 %copy-start.4 = (f32[4,2]{0,1:T(2,128)S(1)}, f32[4,2]{0,1:T(2,128)}, u32[]{:S(2)}) copy-start(f32[4,2]{0,1:T(2,128)} %param.8) | copy-start | bytes 100
  14.8 1.4 %collective-permute-start.7 = (bf16[16,4096]{1,0:T(8,128)(2,1)S(1)}, bf16[16,4096]{1,0:T(8,128)(2,1)S(1)}, u32[]{:S(2)}, u32[]{:S(2)}) collective-permute-start(bf16[16,4096]{1,0:T(8,128)(2,1)S(1)} %get-tuple-element.28), channel_id=1, source_target_pairs={{0,1},{1,0},{2,3},{3,2},{4,5},{5,4},{6,7},{7,6},{8,9},{9,8},{10,11... | collective-permute-start | bytes 393224 | tf_op jit(solution)/shard_map/ppermute | solution.py:229
  15.9 2.0 %collective-permute-start.4 = (bf16[16,4096]{1,0:T(8,128)(2,1)S(1)}, bf16[16,4096]{1,0:T(8,128)(2,1)S(1)}, u32[]{:S(2)}, u32[]{:S(2)}) collective-permute-start(bf16[16,4096]{1,0:T(8,128)(2,1)S(1)} %get-tuple-element.24), channel_id=1, source_target_pairs={{0,1},{1,0},{2,3},{3,2},{4,5},{5,4},{6,7},{7,6},{8,9},{9,8},{10,11... | collective-permute-start | bytes 393224 | tf_op jit(solution)/shard_map/ppermute | solution.py:229
  16.3 4.5 %collective-permute-start.8 = (bf16[8,4096]{1,0:T(8,128)(2,1)S(1)}, bf16[8,4096]{1,0:T(8,128)(2,1)S(1)}, u32[]{:S(2)}, u32[]{:S(2)}) collective-permute-start(bf16[8,4096]{1,0:T(8,128)(2,1)S(1)} %get-tuple-element.30), channel_id=1, source_target_pairs={{0,2},{1,3},{2,0},{3,1},{4,6},{5,7},{6,4},{7,5},{8,10},{9,11},{10,... | collective-permute-start | bytes 196616 | tf_op jit(solution)/shard_map/ppermute | solution.py:230
  17.9 4.3 %collective-permute-start.5 = (bf16[8,4096]{1,0:T(8,128)(2,1)S(1)}, bf16[8,4096]{1,0:T(8,128)(2,1)S(1)}, u32[]{:S(2)}, u32[]{:S(2)}) collective-permute-start(bf16[8,4096]{1,0:T(8,128)(2,1)S(1)} %get-tuple-element.26), channel_id=1, source_target_pairs={{0,2},{1,3},{2,0},{3,1},{4,6},{5,7},{6,4},{7,5},{8,10},{9,11},{10,... | collective-permute-start | bytes 196616 | tf_op jit(solution)/shard_map/ppermute | solution.py:230
  20.8 5.9 %collective-permute-start.9 = (bf16[8,4096]{1,0:T(8,128)(2,1)S(1)}, bf16[8,4096]{1,0:T(8,128)(2,1)S(1)}, u32[]{:S(2)}, u32[]{:S(2)}) collective-permute-start(bf16[8,4096]{1,0:T(8,128)(2,1)S(1)} %fold.3), channel_id=1, source_target_pairs={{0,8},{1,13},{2,10},{3,15},{4,12},{5,9},{6,14},{7,11},{8,0},{9,5},... | collective-permute-start | bytes 196616 | tf_op jit(solution)/shard_map/ppermute | solution.py:242
  22.2 4.5 %collective-permute-start.6 = (bf16[8,4096]{1,0:T(8,128)(2,1)S(1)}, bf16[8,4096]{1,0:T(8,128)(2,1)S(1)}, u32[]{:S(2)}, u32[]{:S(2)}) collective-permute-start(bf16[8,4096]{1,0:T(8,128)(2,1)S(1)} %fold.2.near_kept), channel_id=1, source_target_pairs={{1,5},{3,7},{5,1},{7,3},{9,13},{11,15},{13,9},{15,11},{17,21},{19,... | collective-permute-start | bytes 196616 | tf_op jit(solution)/shard_map/ppermute | solution.py:249
  26.8 2.1 %collective-permute-start.10 = (bf16[8,4096]{1,0:T(8,128)(2,1)S(1)}, bf16[8,4096]{1,0:T(8,128)(2,1)S(1)}, u32[]{:S(2)}, u32[]{:S(2)}) collective-permute-start(bf16[8,4096]{1,0:T(8,128)(2,1)S(1)} %pack.1), channel_id=1, source_target_pairs={{0,1},{1,0},{2,3},{3,2},{4,5},{5,4},{6,7},{7,6},{8,9},{9,8},{10,11... | collective-permute-start | bytes 196616 | tf_op jit(solution)/shard_map/ppermute | solution.py:258

commit v13 on v7

--- a/solution.py
+++ b/solution.py
@@ -13,7 +13,14 @@
 HBM = pl.BlockSpec(memory_space=pltpu.HBM)
 
 
-def order_kernel(n_expert, pairs, rows, out):
+def fetch_kernel(tokens, own, sem):
+    copy = pltpu.make_async_copy(tokens, own, sem)
+    copy.start()
+    copy.wait()
+
+
+def order_kernel(n_expert, pairs, rows, own, out):
+    del own
     total = out.shape[0]
     me = lax.axis_index("etp")
     core, pair = lax.rem(me, 2), lax.div(me, 2)
@@ -113,15 +120,25 @@
     pairs = n_etp // 2
     side = n_expert * tok // 2
 
+    own = pl.pallas_call(
+        fetch_kernel,
+        out_shape=jax.ShapeDtypeStruct((tok, width), tokens.dtype),
+        in_specs=[HBM],
+        out_specs=VMEM,
+        scratch_shapes=[pltpu.SemaphoreType.DMA],
+        compiler_params=GRANT,
+        name="fetch",
+    )(pltpu.with_memory_space_constraint(tokens, pltpu.HBM))
     order = pl.pallas_call(
         functools.partial(order_kernel, n_expert, pairs, rows),
         out_shape=jax.ShapeDtypeStruct((2 * side, 2 * side), jnp.bfloat16),
+        in_specs=[VMEM],
         out_specs=VMEM,
         cost_estimate=AHEAD,
         compiler_params=GRANT,
         name="order",
-    )()
-    tokens, order = lax.optimization_barrier((tokens, order))
+    )(own)
+    own, order = lax.optimization_barrier((own, order))
 
     swap = [(t, t ^ 1) for t in range(n_etp)]
     far = []
@@ -132,7 +149,7 @@
             for t in range(n_etp)
         ]
         far.append(lax.ppermute(tokens, ("expert", "etp"), route))
-    next_block = lax.ppermute(tokens, "expert", [(e, e ^ 1) for e in range(n_expert)])
+    next_block = lax.ppermute(own, "expert", [(e, e ^ 1) for e in range(n_expert)])
     far = [b for block in far for b in (block, lax.ppermute(block, "etp", swap))]
 
     parts = 4
@@ -148,7 +165,7 @@
         scratch_shapes=[pltpu.VMEM((n_expert * tok, width), jnp.bfloat16)],
         compiler_params=GRANT,
         name="ffn",
-    )(tokens, next_block, order, *far, w_gate, w_up, w_down)
+    )(own, next_block, order, *far, w_gate, w_up, w_down)
     near_kept, near_sent = pl.pallas_call(
         functools.partial(down_kernel, parts),
         out_shape=halves,

time: 30 us -> 29.3 us (0.977)
  waiting for transfers between devices: 12.6 us -> 11.5 us
  Pallas kernels: 4.06 us -> 5 us
  local copies, waits for them, and re-layouts: 0.87 us -> 0.03 us
    pallas_call x0 -> x1, Pallas kernels: none -> 0.95 us  [on_device(): pl.pallas_call(fetch_kernel, out_shape=jax.ShapeDtypeStruct((tok, width),...]
    ppermute x1, waiting for transfers between devices: 5 us -> 4.1 us  [on_device(): far.append(lax.ppermute(tokens, ('expert', 'etp'), route))]
    unnamed x12 -> x10, local copies, waits for them, and re-layouts: 0.87 us -> 0.03 us
    ppermute x1, waiting for transfers between devices: 0.79 us -> 1.41 us  [on_device(): lax.ppermute(own, 'expert', [(e, e ^ 1) for e in range(n_expert)])]
    ppermute x1, waiting for transfers between devices: 0.56 us -> 0.01 us  [on_device(): lax.ppermute(block, 'etp', swap)]
    ppermute x2, waiting for transfers between devices: 2.2 us -> 1.89 us  [on_device(): landed.append(lax.ppermute(piece, 'etp', route))]
  transfers between devices with their start and end apart: 10 -> 10, of which waited for: 8 -> 7; matrix products, arithmetic and copies ran while one was open for 0% -> 0% of each run, Pallas kernels for 2% -> 6%
where the time goes in v13:
time: 29.3 us; the launch traced here: 29.2 us
  starting transfers between devices  12.6 us (43%)
  waiting for transfers between devices  11.5 us (39%)
  Pallas kernels  5 us (17%)
    ppermute x1, waiting for transfers between devices, on_device(): far.append(lax.ppermute(tokens, ('expert', 'etp'), route))  4.1 us
    ppermute x1, starting transfers between devices, on_device(): far.append(lax.ppermute(tokens, ('expert', 'etp'), route))  4.04 us
    ppermute x3, waiting for transfers between devices, on_device(): lax.ppermute(pieces[k], 'expert', [(e, e ^ k) for e in range(n_expert)])  3.9 us
    ppermute x3, starting transfers between devices, on_device(): lax.ppermute(pieces[k], 'expert', [(e, e ^ k) for e in range(n_expert)])  3.78 us
    pallas_call x1, Pallas kernels, on_device(): pl.pallas_call(functools.partial(ffn_kernel, n_expert, parts), out_shape=...  2.52 us
    ppermute x2, starting transfers between devices, on_device(): landed.append(lax.ppermute(piece, 'etp', route))  2.5 us
    ppermute x2, waiting for transfers between devices, on_device(): landed.append(lax.ppermute(piece, 'etp', route))  1.89 us
    ppermute x1, starting transfers between devices, on_device(): lax.ppermute(own, 'expert', [(e, e ^ 1) for e in range(n_expert)])  1.64 us
  transfers between devices with their start and end apart: 10, of which 7 were waited for; matrix products, arithmetic and copies ran while one was open for 0% of the time, Pallas kernels for 6%

profile of v13, /device:TPU:0, one launch (start us, length us, event | category | flops | bytes accessed | tf_op | source)
XLA Modules:
  0.0 29.2 jit_solution(10118419662661784279)
XLA Ops:
  0.0 4.0 %collective-permute-start.1 = (bf16[16,4096]{1,0:T(8,128)(2,1)}, bf16[16,4096]{1,0:T(8,128)(2,1)S(1)}, u32[]{:S(2)}, u32[]{:S(2)}) collective-permute-start(bf16[16,4096]{1,0:T(8,128)(2,1)} %tokens.1), channel_id=1, source_target_pairs={{0,8},{1,13},{2,10},{3,15},{4,12},{5,9},{6,14},{7,11},{8,0},{9,5},... | collective-permute-start | bytes 393224 | tf_op jit(solution)/shard_map/ppermute | solution.py:151
  4.0 0.9 %fetch.1.own = bf16[16,4096]{1,0:T(8,128)(2,1)S(1)} custom-call(bf16[16,4096]{1,0:T(8,128)(2,1)} %tokens.1), custom_call_target="tpu_custom_call" | custom-call | tf_op jit(solution)/shard_map/fetch/pallas_call | solution.py:123
  5.0 0.0 copy-start
  5.0 0.0 copy-start.1
  5.0 0.0 copy-start.2
  5.1 1.6 %collective-permute-start = (bf16[16,4096]{1,0:T(8,128)(2,1)S(1)}, bf16[16,4096]{1,0:T(8,128)(2,1)S(1)}, u32[]{:S(2)}, u32[]{:S(2)}) collective-permute-start(bf16[16,4096]{1,0:T(8,128)(2,1)S(1)} %fetch.1.own), channel_id=1, source_target_pairs={{0,4},{4,0},{8,12},{12,8},{1,5},{5,1},{9,13},{13,9},{2,6},{6,2},{1... | collective-permute-start | bytes 393224 | tf_op jit(solution)/shard_map/ppermute | solution.py:152
  6.7 4.1 %collective-permute-done.1.refs_0_ = bf16[16,4096]{1,0:T(8,128)(2,1)S(1)} collective-permute-done((bf16[16,4096]{1,0:T(8,128)(2,1)}, bf16[16,4096]{1,0:T(8,128)(2,1)S(1)}, u32[]{:S(2)}, u32[]{:S(2)}) %collective-permute-start.1) | collective-permute-done | bytes 131104 | tf_op jit(solution)/shard_map/ppermute | solution.py:151
  10.8 1.4 %collective-permute-done.next_block = bf16[16,4096]{1,0:T(8,128)(2,1)S(1)} collective-permute-done((bf16[16,4096]{1,0:T(8,128)(2,1)S(1)}, bf16[16,4096]{1,0:T(8,128)(2,1)S(1)}, u32[]{:S(2)}, u32[]{:S(2)}) %collective-permute-start) | collective-permute-done | bytes 131104 | tf_op jit(solution)/shard_map/ppermute | solution.py:152
  12.3 2.5 %ffn.1 = (f32[16,4096]{1,0:T(8,128)S(1)}, bf16[16,4096]{1,0:T(8,128)(2,1)S(1)}, bf16[32,384]{1,0:T(8,128)(2,1)S(1)}) custom-call(bf16[16,4096]{1,0:T(8,128)(2,1)S(1)} %fetch.1.own, bf16[16,4096]{1,0:T(8,128)(2,1)S(1)} %collective-permute-done.next_block, bf16[64,64]{1,0:T(8,128)(2,1)S(1)} %order.1, bf16[16,4096]{1,0:T(8,128)(2,1)S(1)} %collective-permute-done.1.refs_0_, ...), custom_call_target="tpu_custom_call" | custom-call | tf_op jit(solution)/shard_map/ffn/pallas_call | solution.py:160
  14.8 0.0 copy-start.4
  14.8 0.1 collective-permute-start.6
  14.9 0.6 %down.1 = (f32[16,4096]{1,0:T(8,128)S(1)}, bf16[16,4096]{1,0:T(8,128)(2,1)S(1)}) custom-call(bf16[32,384]{1,0:T(8,128)(2,1)S(1)} %get-tuple-element.22.hidden, bf16[1,384,4096]{2,1,0:T(8,128)(2,1)S(1)} %copy-done), custom_call_target="tpu_custom_call" | custom-call | tf_op jit(solution)/shard_map/down/pallas_call | solution.py:169
  15.6 0.5 %collective-permute-start.3 = (bf16[16,4096]{1,0:T(8,128)(2,1)S(1)}, bf16[16,4096]{1,0:T(8,128)(2,1)S(1)}, u32[]{:S(2)}, u32[]{:S(2)}) collective-permute-start(bf16[16,4096]{1,0:T(8,128)(2,1)S(1)} %get-tuple-element.24), channel_id=1, source_target_pairs={{0,1},{1,0},{2,3},{3,2},{4,5},{5,4},{6,7},{7,6},{8,9},{9,8},{10,11... | collective-permute-start | bytes 393224 | tf_op jit(solution)/shard_map/ppermute | solution.py:181
  16.0 0.2 collective-permute-done.6.arrived
  16.2 1.7 %collective-permute-start.7 = (bf16[8,4096]{1,0:T(8,128)(2,1)S(1)}, bf16[8,4096]{1,0:T(8,128)(2,1)S(1)}, u32[]{:S(2)}, u32[]{:S(2)}) collective-permute-start(bf16[8,4096]{1,0:T(8,128)(2,1)S(1)} %get-tuple-element.32), channel_id=1, source_target_pairs={{0,2},{1,3},{2,0},{3,1},{4,6},{5,7},{6,4},{7,5},{8,10},{9,11},{10,... | collective-permute-start | bytes 196616 | tf_op jit(solution)/shard_map/ppermute | solution.py:194
  18.0 0.8 %collective-permute-start.4 = (bf16[8,4096]{1,0:T(8,128)(2,1)S(1)}, bf16[8,4096]{1,0:T(8,128)(2,1)S(1)}, u32[]{:S(2)}, u32[]{:S(2)}) collective-permute-start(bf16[8,4096]{1,0:T(8,128)(2,1)S(1)} %get-tuple-element.26), channel_id=1, source_target_pairs={{0,2},{1,3},{2,0},{3,1},{4,6},{5,7},{6,4},{7,5},{8,10},{9,11},{10,... | collective-permute-start | bytes 196616 | tf_op jit(solution)/shard_map/ppermute | solution.py:194
  18.8 1.9 %collective-permute-done.7.refs_0_ = bf16[8,4096]{1,0:T(8,128)(2,1)S(1)} collective-permute-done((bf16[8,4096]{1,0:T(8,128)(2,1)S(1)}, bf16[8,4096]{1,0:T(8,128)(2,1)S(1)}, u32[]{:S(2)}, u32[]{:S(2)}) %collective-permute-start.7) | collective-permute-done | bytes 65568 | tf_op jit(solution)/shard_map/ppermute | solution.py:194
  20.7 0.9 %collective-permute-start.8 = (bf16[4,4096]{1,0:T(4,128)(2,1)S(1)}, bf16[4,4096]{1,0:T(4,128)(2,1)S(1)}, u32[]{:S(2)}, u32[]{:S(2)}) collective-permute-start(bf16[4,4096]{1,0:T(4,128)(2,1)S(1)} %get-tuple-element.33), channel_id=1, source_target_pairs={{0,8},{4,12},{8,0},{12,4},{1,9},{5,13},{9,1},{13,5},{2,10},{6,14},... | collective-permute-start | bytes 98312 | tf_op jit(solution)/shard_map/ppermute | solution.py:206
  21.6 2.8 %collective-permute-start.9 = (bf16[4,4096]{1,0:T(4,128)(2,1)S(1)}, bf16[4,4096]{1,0:T(4,128)(2,1)S(1)}, u32[]{:S(2)}, u32[]{:S(2)}) collective-permute-start(bf16[4,4096]{1,0:T(4,128)(2,1)S(1)} %get-tuple-element.34), channel_id=1, source_target_pairs={{0,12},{4,8},{8,4},{12,0},{1,13},{5,9},{9,5},{13,1},{2,14},{6,10},... | collective-permute-start | bytes 98312 | tf_op jit(solution)/shard_map/ppermute | solution.py:206
  24.4 0.1 collective-permute-start.5
  24.5 1.1 %collective-permute-done.8.refs_2_ = bf16[4,4096]{1,0:T(4,128)(2,1)S(1)} collective-permute-done((bf16[4,4096]{1,0:T(4,128)(2,1)S(1)}, bf16[4,4096]{1,0:T(4,128)(2,1)S(1)}, u32[]{:S(2)}, u32[]{:S(2)}) %collective-permute-start.8) | collective-permute-done | bytes 32800 | tf_op jit(solution)/shard_map/ppermute | solution.py:206
  25.6 1.7 %collective-permute-done.9.refs_3_ = bf16[4,4096]{1,0:T(4,128)(2,1)S(1)} collective-permute-done((bf16[4,4096]{1,0:T(4,128)(2,1)S(1)}, bf16[4,4096]{1,0:T(4,128)(2,1)S(1)}, u32[]{:S(2)}, u32[]{:S(2)}) %collective-permute-start.9) | collective-permute-done | bytes 32800 | tf_op jit(solution)/shard_map/ppermute | solution.py:206
  27.3 1.1 %collective-permute-done.5.refs_1_ = bf16[4,4096]{1,0:T(4,128)(2,1)S(1)} collective-permute-done((bf16[4,4096]{1,0:T(4,128)(2,1)S(1)}, bf16[4,4096]{1,0:T(4,128)(2,1)S(1)}, u32[]{:S(2)}, u32[]{:S(2)}) %collective-permute-start.5) | collective-permute-done | bytes 32800 | tf_op jit(solution)/shard_map/ppermute | solution.py:206
  28.4 0.7 %mix.1 = bf16[4,4096]{1,0:T(4,128)(2,1)} custom-call(s32[2,16]{1,0:T(2,128)S(1)} %bitcast.2, f32[2,4]{1,0:T(2,128)S(1)} %bitcast.3, bf16[4,4096]{1,0:T(4,128)(2,1)S(1)} %get-tuple-element.27.refs_0_, bf16[4,4096]{1,0:T(4,128)(2,1)S(1)} %collective-permute-done.5.refs_1_, bf16[4,4096]{1,0:T(4,128)(2,1)S(1)} %collective-permute-done.8.refs_2_, ...), custom_call_target="tpu_custom_call" | custom-call | tf_op jit(solution)/shard_map/mix/pallas_call | solution.py:209
  (15 shorter events, 0.2 us)
Async XLA Ops:
  0.0 10.8 %collective-permute-start.1 = (bf16[16,4096]{1,0:T(8,128)(2,1)}, bf16[16,4096]{1,0:T(8,128)(2,1)S(1)}, u32[]{:S(2)}, u32[]{:S(2)}) collective-permute-start(bf16[16,4096]{1,0:T(8,128)(2,1)} %tokens.1), channel_id=1, source_target_pairs={{0,8},{1,13},{2,10},{3,15},{4,12},{5,9},{6,14},{7,11},{8,0},{9,5},... | collective-permute-start | bytes 393224 | tf_op jit(solution)/shard_map/ppermute | solution.py:151
  5.0 7.2 %copy-start = (bf16[1,384,4096]{2,1,0:T(8,128)(2,1)S(1)}, bf16[1,384,4096]{2,1,0:T(8,128)(2,1)}, u32[]{:S(2)}) copy-start(bf16[1,384,4096]{2,1,0:T(8,128)(2,1)} %w_down.1) | copy-start | bytes 9437188
  5.0 7.2 %copy-start.1 = (bf16[1,384,4096]{2,1,0:T(8,128)(2,1)S(1)}, bf16[1,384,4096]{2,1,0:T(8,128)(2,1)}, u32[]{:S(2)}) copy-start(bf16[1,384,4096]{2,1,0:T(8,128)(2,1)} %refs_2_.1) | copy-start | bytes 9437188
  5.0 7.2 %copy-start.2 = (bf16[1,384,4096]{2,1,0:T(8,128)(2,1)S(1)}, bf16[1,384,4096]{2,1,0:T(8,128)(2,1)}, u32[]{:S(2)}) copy-start(bf16[1,384,4096]{2,1,0:T(8,128)(2,1)} %refs_3_.1) | copy-start | bytes 9437188
  5.1 7.1 %collective-permute-start = (bf16[16,4096]{1,0:T(8,128)(2,1)S(1)}, bf16[16,4096]{1,0:T(8,128)(2,1)S(1)}, u32[]{:S(2)}, u32[]{:S(2)}) collective-permute-start(bf16[16,4096]{1,0:T(8,128)(2,1)S(1)} %fetch.1.own), channel_id=1, source_target_pairs={{0,4},{4,0},{8,12},{12,8},{1,5},{5,1},{9,13},{13,9},{2,6},{6,2},{1... | collective-permute-start | bytes 393224 | tf_op jit(solution)/shard_map/ppermute | solution.py:152
  10.8 1.4 %collective-permute-start.2 = (bf16[16,4096]{1,0:T(8,128)(2,1)S(1)}, bf16[16,4096]{1,0:T(8,128)(2,1)S(1)}, u32[]{:S(2)}, u32[]{:S(2)}) collective-permute-start(bf16[16,4096]{1,0:T(8,128)(2,1)S(1)} %collective-permute-done.1.refs_0_), channel_id=1, source_target_pairs={{0,1},{1,0},{2,3},{3,2},{4,5},{5,4},{6,7},{7,6},{8,9},{9,8},{10,11... | collective-permute-start | bytes 393224 | tf_op jit(solution)/shard_map/ppermute | solution.py:153
  14.8 13.6 %copy-start.3 = (s32[16,2]{0,1:T(2,128)S(1)}, s32[16,2]{0,1:T(2,128)}, u32[]{:S(2)}) copy-start(s32[16,2]{0,1:T(2,128)} %param.7) | copy-start | bytes 388
  14.8 13.6 %copy-start.4 = (f32[4,2]{0,1:T(2,128)S(1)}, f32[4,2]{0,1:T(2,128)}, u32[]{:S(2)}) copy-start(f32[4,2]{0,1:T(2,128)} %param.8) | copy-start | bytes 100
  14.8 1.4 %collective-permute-start.6 = (bf16[16,4096]{1,0:T(8,128)(2,1)S(1)}, bf16[16,4096]{1,0:T(8,128)(2,1)S(1)}, u32[]{:S(2)}, u32[]{:S(2)}) collective-permute-start(bf16[16,4096]{1,0:T(8,128)(2,1)S(1)} %get-tuple-element.30), channel_id=1, source_target_pairs={{0,1},{1,0},{2,3},{3,2},{4,5},{5,4},{6,7},{7,6},{8,9},{9,8},{10,11... | collective-permute-start | bytes 393224 | tf_op jit(solution)/shard_map/ppermute | solution.py:181
  15.6 2.4 %collective-permute-start.3 = (bf16[16,4096]{1,0:T(8,128)(2,1)S(1)}, bf16[16,4096]{1,0:T(8,128)(2,1)S(1)}, u32[]{:S(2)}, u32[]{:S(2)}) collective-permute-start(bf16[16,4096]{1,0:T(8,128)(2,1)S(1)} %get-tuple-element.24), channel_id=1, source_target_pairs={{0,1},{1,0},{2,3},{3,2},{4,5},{5,4},{6,7},{7,6},{8,9},{9,8},{10,11... | collective-permute-start | bytes 393224 | tf_op jit(solution)/shard_map/ppermute | solution.py:181
  16.2 4.4 %collective-permute-start.7 = (bf16[8,4096]{1,0:T(8,128)(2,1)S(1)}, bf16[8,4096]{1,0:T(8,128)(2,1)S(1)}, u32[]{:S(2)}, u32[]{:S(2)}) collective-permute-start(bf16[8,4096]{1,0:T(8,128)(2,1)S(1)} %get-tuple-element.32), channel_id=1, source_target_pairs={{0,2},{1,3},{2,0},{3,1},{4,6},{5,7},{6,4},{7,5},{8,10},{9,11},{10,... | collective-permute-start | bytes 196616 | tf_op jit(solution)/shard_map/ppermute | solution.py:194
  18.0 6.4 %collective-permute-start.4 = (bf16[8,4096]{1,0:T(8,128)(2,1)S(1)}, bf16[8,4096]{1,0:T(8,128)(2,1)S(1)}, u32[]{:S(2)}, u32[]{:S(2)}) collective-permute-start(bf16[8,4096]{1,0:T(8,128)(2,1)S(1)} %get-tuple-element.26), channel_id=1, source_target_pairs={{0,2},{1,3},{2,0},{3,1},{4,6},{5,7},{6,4},{7,5},{8,10},{9,11},{10,... | collective-permute-start | bytes 196616 | tf_op jit(solution)/shard_map/ppermute | solution.py:194
  20.7 4.9 %collective-permute-start.8 = (bf16[4,4096]{1,0:T(4,128)(2,1)S(1)}, bf16[4,4096]{1,0:T(4,128)(2,1)S(1)}, u32[]{:S(2)}, u32[]{:S(2)}) collective-permute-start(bf16[4,4096]{1,0:T(4,128)(2,1)S(1)} %get-tuple-element.33), channel_id=1, source_target_pairs={{0,8},{4,12},{8,0},{12,4},{1,9},{5,13},{9,1},{13,5},{2,10},{6,14},... | collective-permute-start | bytes 98312 | tf_op jit(solution)/shard_map/ppermute | solution.py:206
  21.6 5.7 %collective-permute-start.9 = (bf16[4,4096]{1,0:T(4,128)(2,1)S(1)}, bf16[4,4096]{1,0:T(4,128)(2,1)S(1)}, u32[]{:S(2)}, u32[]{:S(2)}) collective-permute-start(bf16[4,4096]{1,0:T(4,128)(2,1)S(1)} %get-tuple-element.34), channel_id=1, source_target_pairs={{0,12},{4,8},{8,4},{12,0},{1,13},{5,9},{9,5},{13,1},{2,14},{6,10},... | collective-permute-start | bytes 98312 | tf_op jit(solution)/shard_map/ppermute | solution.py:206
  24.4 4.0 %collective-permute-start.5 = (bf16[4,4096]{1,0:T(4,128)(2,1)S(1)}, bf16[4,4096]{1,0:T(4,128)(2,1)S(1)}, u32[]{:S(2)}, u32[]{:S(2)}) collective-permute-start(bf16[4,4096]{1,0:T(4,128)(2,1)S(1)} %get-tuple-element.28), channel_id=1, source_target_pairs={{0,4},{4,0},{8,12},{12,8},{1,5},{5,1},{9,13},{13,9},{2,6},{6,2},{1... | collective-permute-start | bytes 98312 | tf_op jit(solution)/shard_map/ppermute | solution.py:206

commit v14 on v13

--- a/solution.py
+++ b/solution.py
@@ -85,9 +85,11 @@
     total = own[...]
     for block in arrived:
         total = total + block[...].astype(jnp.float32)
-    rows = pieces[0].shape[0]
+    rows, half = pieces[0].shape[0] // 2, pieces[0].shape[1]
     for k, piece in enumerate(pieces):
-        piece[...] = total[k * rows : (k + 1) * rows].astype(piece.dtype)
+        block = total[k * rows : (k + 1) * rows].astype(piece.dtype)
+        piece[:rows] = block[:, :half]
+        piece[rows:] = block[:, half:]
 
 
 def mix_kernel(n_expert, ids, weights, *refs):
@@ -105,13 +107,17 @@
     own_ids = [column(ids, me * rows, i) for i in range(top)]
     own_weights = [column(weights, 0, i) for i in range(top)]
     scale = sum(own_weights)
-    total = None
+    left, right = None, None
     for k in range(n_expert):
         owner = lax.bitwise_xor(expert, k)
         factor = sum(jnp.where(own_ids[i] == owner, own_weights[i], 0.0) for i in range(top)) / scale
-        term = pieces[k][...].astype(jnp.float32) * factor
-        total = term if total is None else total + term
-    out[...] = total.astype(out.dtype)
+        term = pieces[k][:rows].astype(jnp.float32) * factor
+        left = term if left is None else left + term
+        term = pieces[k][rows:].astype(jnp.float32) * factor
+        right = term if right is None else right + term
+    half = out.shape[1] // 2
+    out[:, :half] = left.astype(out.dtype)
+    out[:, half:] = right.astype(out.dtype)
 
 
 def on_device(n_expert, n_etp, tokens, expert_ids, route_weights, w_gate, w_up, w_down):
@@ -194,7 +200,8 @@
             landed.append(lax.ppermute(piece, "etp", route))
         folded = pl.pallas_call(
             functools.partial(fold_kernel, pairs),
-            out_shape=[jax.ShapeDtypeStruct((rows, width), jnp.bfloat16)] * (n_expert // 2),
+            out_shape=[jax.ShapeDtypeStruct((2 * rows, width // 2), jnp.bfloat16)]
+            * (n_expert // 2),
             in_specs=[VMEM] * pairs,
             out_specs=[VMEM] * (n_expert // 2),
             compiler_params=GRANT,

time: 29.3 us -> 29.3 us (level)
  no operation moved by 1% of the time
where the time goes in v14:
time: 29.3 us; the launch traced here: 29.2 us
  starting transfers between devices  12.6 us (43%)
  waiting for transfers between devices  11.5 us (39%)
  Pallas kernels  5.02 us (17%)
    ppermute x1, waiting for transfers between devices, on_device(): far.append(lax.ppermute(tokens, ('expert', 'etp'), route))  4.1 us
    ppermute x1, starting transfers between devices, on_device(): far.append(lax.ppermute(tokens, ('expert', 'etp'), route))  4.04 us
    ppermute x3, waiting for transfers between devices, on_device(): lax.ppermute(pieces[k], 'expert', [(e, e ^ k) for e in range(n_expert)])  3.9 us
    ppermute x3, starting transfers between devices, on_device(): lax.ppermute(pieces[k], 'expert', [(e, e ^ k) for e in range(n_expert)])  3.78 us
    pallas_call x1, Pallas kernels, on_device(): pl.pallas_call(functools.partial(ffn_kernel, n_expert, parts), out_shape=...  2.52 us
    ppermute x2, starting transfers between devices, on_device(): landed.append(lax.ppermute(piece, 'etp', route))  2.5 us
    ppermute x2, waiting for transfers between devices, on_device(): landed.append(lax.ppermute(piece, 'etp', route))  1.89 us
    ppermute x1, starting transfers between devices, on_device(): lax.ppermute(own, 'expert', [(e, e ^ 1) for e in range(n_expert)])  1.64 us
  transfers between devices with their start and end apart: 10, of which 7 were waited for; matrix products, arithmetic and copies ran while one was open for 0% of the time, Pallas kernels for 6%

profile of v14, /device:TPU:0, one launch (start us, length us, event | category | flops | bytes accessed | tf_op | source)
XLA Modules:
  0.0 29.2 jit_solution(67731464091555675)
XLA Ops:
  0.0 4.0 %collective-permute-start.1 = (bf16[16,4096]{1,0:T(8,128)(2,1)}, bf16[16,4096]{1,0:T(8,128)(2,1)S(1)}, u32[]{:S(2)}, u32[]{:S(2)}) collective-permute-start(bf16[16,4096]{1,0:T(8,128)(2,1)} %tokens.1), channel_id=1, source_target_pairs={{0,8},{1,13},{2,10},{3,15},{4,12},{5,9},{6,14},{7,11},{8,0},{9,5},... | collective-permute-start | bytes 393224 | tf_op jit(solution)/shard_map/ppermute | solution.py:157
  4.0 0.9 %fetch.1.own = bf16[16,4096]{1,0:T(8,128)(2,1)S(1)} custom-call(bf16[16,4096]{1,0:T(8,128)(2,1)} %tokens.1), custom_call_target="tpu_custom_call" | custom-call | tf_op jit(solution)/shard_map/fetch/pallas_call | solution.py:129
  5.0 0.0 copy-start
  5.0 0.0 copy-start.1
  5.0 0.0 copy-start.2
  5.1 1.6 %collective-permute-start = (bf16[16,4096]{1,0:T(8,128)(2,1)S(1)}, bf16[16,4096]{1,0:T(8,128)(2,1)S(1)}, u32[]{:S(2)}, u32[]{:S(2)}) collective-permute-start(bf16[16,4096]{1,0:T(8,128)(2,1)S(1)} %fetch.1.own), channel_id=1, source_target_pairs={{0,4},{4,0},{8,12},{12,8},{1,5},{5,1},{9,13},{13,9},{2,6},{6,2},{1... | collective-permute-start | bytes 393224 | tf_op jit(solution)/shard_map/ppermute | solution.py:158
  6.7 4.1 %collective-permute-done.1.refs_0_ = bf16[16,4096]{1,0:T(8,128)(2,1)S(1)} collective-permute-done((bf16[16,4096]{1,0:T(8,128)(2,1)}, bf16[16,4096]{1,0:T(8,128)(2,1)S(1)}, u32[]{:S(2)}, u32[]{:S(2)}) %collective-permute-start.1) | collective-permute-done | bytes 131104 | tf_op jit(solution)/shard_map/ppermute | solution.py:157
  10.8 1.4 %collective-permute-done.next_block = bf16[16,4096]{1,0:T(8,128)(2,1)S(1)} collective-permute-done((bf16[16,4096]{1,0:T(8,128)(2,1)S(1)}, bf16[16,4096]{1,0:T(8,128)(2,1)S(1)}, u32[]{:S(2)}, u32[]{:S(2)}) %collective-permute-start) | collective-permute-done | bytes 131104 | tf_op jit(solution)/shard_map/ppermute | solution.py:158
  12.3 2.5 %ffn.1 = (f32[16,4096]{1,0:T(8,128)S(1)}, bf16[16,4096]{1,0:T(8,128)(2,1)S(1)}, bf16[32,384]{1,0:T(8,128)(2,1)S(1)}) custom-call(bf16[16,4096]{1,0:T(8,128)(2,1)S(1)} %fetch.1.own, bf16[16,4096]{1,0:T(8,128)(2,1)S(1)} %collective-permute-done.next_block, bf16[64,64]{1,0:T(8,128)(2,1)S(1)} %order.1, bf16[16,4096]{1,0:T(8,128)(2,1)S(1)} %collective-permute-done.1.refs_0_, ...), custom_call_target="tpu_custom_call" | custom-call | tf_op jit(solution)/shard_map/ffn/pallas_call | solution.py:166
  14.8 0.0 copy-start.4
  14.8 0.1 collective-permute-start.6
  14.9 0.6 %down.1 = (f32[16,4096]{1,0:T(8,128)S(1)}, bf16[16,4096]{1,0:T(8,128)(2,1)S(1)}) custom-call(bf16[32,384]{1,0:T(8,128)(2,1)S(1)} %get-tuple-element.22.hidden, bf16[1,384,4096]{2,1,0:T(8,128)(2,1)S(1)} %copy-done), custom_call_target="tpu_custom_call" | custom-call | tf_op jit(solution)/shard_map/down/pallas_call | solution.py:175
  15.6 0.5 %collective-permute-start.3 = (bf16[16,4096]{1,0:T(8,128)(2,1)S(1)}, bf16[16,4096]{1,0:T(8,128)(2,1)S(1)}, u32[]{:S(2)}, u32[]{:S(2)}) collective-permute-start(bf16[16,4096]{1,0:T(8,128)(2,1)S(1)} %get-tuple-element.24), channel_id=1, source_target_pairs={{0,1},{1,0},{2,3},{3,2},{4,5},{5,4},{6,7},{7,6},{8,9},{9,8},{10,11... | collective-permute-start | bytes 393224 | tf_op jit(solution)/shard_map/ppermute | solution.py:187
  16.0 0.2 collective-permute-done.6.arrived
  16.2 1.7 %collective-permute-start.7 = (bf16[8,4096]{1,0:T(8,128)(2,1)S(1)}, bf16[8,4096]{1,0:T(8,128)(2,1)S(1)}, u32[]{:S(2)}, u32[]{:S(2)}) collective-permute-start(bf16[8,4096]{1,0:T(8,128)(2,1)S(1)} %get-tuple-element.32), channel_id=1, source_target_pairs={{0,2},{1,3},{2,0},{3,1},{4,6},{5,7},{6,4},{7,5},{8,10},{9,11},{10,... | collective-permute-start | bytes 196616 | tf_op jit(solution)/shard_map/ppermute | solution.py:200
  18.0 0.8 %collective-permute-start.4 = (bf16[8,4096]{1,0:T(8,128)(2,1)S(1)}, bf16[8,4096]{1,0:T(8,128)(2,1)S(1)}, u32[]{:S(2)}, u32[]{:S(2)}) collective-permute-start(bf16[8,4096]{1,0:T(8,128)(2,1)S(1)} %get-tuple-element.26), channel_id=1, source_target_pairs={{0,2},{1,3},{2,0},{3,1},{4,6},{5,7},{6,4},{7,5},{8,10},{9,11},{10,... | collective-permute-start | bytes 196616 | tf_op jit(solution)/shard_map/ppermute | solution.py:200
  18.8 1.9 %collective-permute-done.7.refs_0_ = bf16[8,4096]{1,0:T(8,128)(2,1)S(1)} collective-permute-done((bf16[8,4096]{1,0:T(8,128)(2,1)S(1)}, bf16[8,4096]{1,0:T(8,128)(2,1)S(1)}, u32[]{:S(2)}, u32[]{:S(2)}) %collective-permute-start.7) | collective-permute-done | bytes 65568 | tf_op jit(solution)/shard_map/ppermute | solution.py:200
  20.7 0.9 %collective-permute-start.8 = (bf16[8,2048]{1,0:T(8,128)(2,1)S(1)}, bf16[8,2048]{1,0:T(8,128)(2,1)S(1)}, u32[]{:S(2)}, u32[]{:S(2)}) collective-permute-start(bf16[8,2048]{1,0:T(8,128)(2,1)S(1)} %get-tuple-element.33), channel_id=1, source_target_pairs={{0,8},{4,12},{8,0},{12,4},{1,9},{5,13},{9,1},{13,5},{2,10},{6,14},... | collective-permute-start | bytes 98312 | tf_op jit(solution)/shard_map/ppermute | solution.py:213
  21.6 2.8 %collective-permute-start.9 = (bf16[8,2048]{1,0:T(8,128)(2,1)S(1)}, bf16[8,2048]{1,0:T(8,128)(2,1)S(1)}, u32[]{:S(2)}, u32[]{:S(2)}) collective-permute-start(bf16[8,2048]{1,0:T(8,128)(2,1)S(1)} %get-tuple-element.34), channel_id=1, source_target_pairs={{0,12},{4,8},{8,4},{12,0},{1,13},{5,9},{9,5},{13,1},{2,14},{6,10},... | collective-permute-start | bytes 98312 | tf_op jit(solution)/shard_map/ppermute | solution.py:213
  24.4 0.1 collective-permute-start.5
  24.5 1.1 %collective-permute-done.8.refs_2_ = bf16[8,2048]{1,0:T(8,128)(2,1)S(1)} collective-permute-done((bf16[8,2048]{1,0:T(8,128)(2,1)S(1)}, bf16[8,2048]{1,0:T(8,128)(2,1)S(1)}, u32[]{:S(2)}, u32[]{:S(2)}) %collective-permute-start.8) | collective-permute-done | bytes 32800 | tf_op jit(solution)/shard_map/ppermute | solution.py:213
  25.6 1.7 %collective-permute-done.9.refs_3_ = bf16[8,2048]{1,0:T(8,128)(2,1)S(1)} collective-permute-done((bf16[8,2048]{1,0:T(8,128)(2,1)S(1)}, bf16[8,2048]{1,0:T(8,128)(2,1)S(1)}, u32[]{:S(2)}, u32[]{:S(2)}) %collective-permute-start.9) | collective-permute-done | bytes 32800 | tf_op jit(solution)/shard_map/ppermute | solution.py:213
  27.3 1.1 %collective-permute-done.5.refs_1_ = bf16[8,2048]{1,0:T(8,128)(2,1)S(1)} collective-permute-done((bf16[8,2048]{1,0:T(8,128)(2,1)S(1)}, bf16[8,2048]{1,0:T(8,128)(2,1)S(1)}, u32[]{:S(2)}, u32[]{:S(2)}) %collective-permute-start.5) | collective-permute-done | bytes 32800 | tf_op jit(solution)/shard_map/ppermute | solution.py:213
  28.4 0.8 %mix.1 = bf16[4,4096]{1,0:T(4,128)(2,1)} custom-call(s32[2,16]{1,0:T(2,128)S(1)} %bitcast.2, f32[2,4]{1,0:T(2,128)S(1)} %bitcast.3, bf16[8,2048]{1,0:T(8,128)(2,1)S(1)} %get-tuple-element.27.refs_0_, bf16[8,2048]{1,0:T(8,128)(2,1)S(1)} %collective-permute-done.5.refs_1_, bf16[8,2048]{1,0:T(8,128)(2,1)S(1)} %collective-permute-done.8.refs_2_, ...), custom_call_target="tpu_custom_call" | custom-call | tf_op jit(solution)/shard_map/mix/pallas_call | solution.py:216
  (15 shorter events, 0.2 us)
Async XLA Ops:
  0.0 10.8 %collective-permute-start.1 = (bf16[16,4096]{1,0:T(8,128)(2,1)}, bf16[16,4096]{1,0:T(8,128)(2,1)S(1)}, u32[]{:S(2)}, u32[]{:S(2)}) collective-permute-start(bf16[16,4096]{1,0:T(8,128)(2,1)} %tokens.1), channel_id=1, source_target_pairs={{0,8},{1,13},{2,10},{3,15},{4,12},{5,9},{6,14},{7,11},{8,0},{9,5},... | collective-permute-start | bytes 393224 | tf_op jit(solution)/shard_map/ppermute | solution.py:157
  5.0 7.2 %copy-start = (bf16[1,384,4096]{2,1,0:T(8,128)(2,1)S(1)}, bf16[1,384,4096]{2,1,0:T(8,128)(2,1)}, u32[]{:S(2)}) copy-start(bf16[1,384,4096]{2,1,0:T(8,128)(2,1)} %w_down.1) | copy-start | bytes 9437188
  5.0 7.2 %copy-start.1 = (bf16[1,384,4096]{2,1,0:T(8,128)(2,1)S(1)}, bf16[1,384,4096]{2,1,0:T(8,128)(2,1)}, u32[]{:S(2)}) copy-start(bf16[1,384,4096]{2,1,0:T(8,128)(2,1)} %refs_2_.1) | copy-start | bytes 9437188
  5.0 7.2 %copy-start.2 = (bf16[1,384,4096]{2,1,0:T(8,128)(2,1)S(1)}, bf16[1,384,4096]{2,1,0:T(8,128)(2,1)}, u32[]{:S(2)}) copy-start(bf16[1,384,4096]{2,1,0:T(8,128)(2,1)} %refs_3_.1) | copy-start | bytes 9437188
  5.1 7.1 %collective-permute-start = (bf16[16,4096]{1,0:T(8,128)(2,1)S(1)}, bf16[16,4096]{1,0:T(8,128)(2,1)S(1)}, u32[]{:S(2)}, u32[]{:S(2)}) collective-permute-start(bf16[16,4096]{1,0:T(8,128)(2,1)S(1)} %fetch.1.own), channel_id=1, source_target_pairs={{0,4},{4,0},{8,12},{12,8},{1,5},{5,1},{9,13},{13,9},{2,6},{6,2},{1... | collective-permute-start | bytes 393224 | tf_op jit(solution)/shard_map/ppermute | solution.py:158
  10.8 1.4 %collective-permute-start.2 = (bf16[16,4096]{1,0:T(8,128)(2,1)S(1)}, bf16[16,4096]{1,0:T(8,128)(2,1)S(1)}, u32[]{:S(2)}, u32[]{:S(2)}) collective-permute-start(bf16[16,4096]{1,0:T(8,128)(2,1)S(1)} %collective-permute-done.1.refs_0_), channel_id=1, source_target_pairs={{0,1},{1,0},{2,3},{3,2},{4,5},{5,4},{6,7},{7,6},{8,9},{9,8},{10,11... | collective-permute-start | bytes 393224 | tf_op jit(solution)/shard_map/ppermute | solution.py:159
  14.8 13.6 %copy-start.3 = (s32[16,2]{0,1:T(2,128)S(1)}, s32[16,2]{0,1:T(2,128)}, u32[]{:S(2)}) copy-start(s32[16,2]{0,1:T(2,128)} %param.7) | copy-start | bytes 388
  14.8 13.6 %copy-start.4 = (f32[4,2]{0,1:T(2,128)S(1)}, f32[4,2]{0,1:T(2,128)}, u32[]{:S(2)}) copy-start(f32[4,2]{0,1:T(2,128)} %param.8) | copy-start | bytes 100
  14.8 1.4 %collective-permute-start.6 = (bf16[16,4096]{1,0:T(8,128)(2,1)S(1)}, bf16[16,4096]{1,0:T(8,128)(2,1)S(1)}, u32[]{:S(2)}, u32[]{:S(2)}) collective-permute-start(bf16[16,4096]{1,0:T(8,128)(2,1)S(1)} %get-tuple-element.30), channel_id=1, source_target_pairs={{0,1},{1,0},{2,3},{3,2},{4,5},{5,4},{6,7},{7,6},{8,9},{9,8},{10,11... | collective-permute-start | bytes 393224 | tf_op jit(solution)/shard_map/ppermute | solution.py:187
  15.6 2.4 %collective-permute-start.3 = (bf16[16,4096]{1,0:T(8,128)(2,1)S(1)}, bf16[16,4096]{1,0:T(8,128)(2,1)S(1)}, u32[]{:S(2)}, u32[]{:S(2)}) collective-permute-start(bf16[16,4096]{1,0:T(8,128)(2,1)S(1)} %get-tuple-element.24), channel_id=1, source_target_pairs={{0,1},{1,0},{2,3},{3,2},{4,5},{5,4},{6,7},{7,6},{8,9},{9,8},{10,11... | collective-permute-start | bytes 393224 | tf_op jit(solution)/shard_map/ppermute | solution.py:187
  16.2 4.4 %collective-permute-start.7 = (bf16[8,4096]{1,0:T(8,128)(2,1)S(1)}, bf16[8,4096]{1,0:T(8,128)(2,1)S(1)}, u32[]{:S(2)}, u32[]{:S(2)}) collective-permute-start(bf16[8,4096]{1,0:T(8,128)(2,1)S(1)} %get-tuple-element.32), channel_id=1, source_target_pairs={{0,2},{1,3},{2,0},{3,1},{4,6},{5,7},{6,4},{7,5},{8,10},{9,11},{10,... | collective-permute-start | bytes 196616 | tf_op jit(solution)/shard_map/ppermute | solution.py:200
  18.0 6.4 %collective-permute-start.4 = (bf16[8,4096]{1,0:T(8,128)(2,1)S(1)}, bf16[8,4096]{1,0:T(8,128)(2,1)S(1)}, u32[]{:S(2)}, u32[]{:S(2)}) collective-permute-start(bf16[8,4096]{1,0:T(8,128)(2,1)S(1)} %get-tuple-element.26), channel_id=1, source_target_pairs={{0,2},{1,3},{2,0},{3,1},{4,6},{5,7},{6,4},{7,5},{8,10},{9,11},{10,... | collective-permute-start | bytes 196616 | tf_op jit(solution)/shard_map/ppermute | solution.py:200
  20.7 4.9 %collective-permute-start.8 = (bf16[8,2048]{1,0:T(8,128)(2,1)S(1)}, bf16[8,2048]{1,0:T(8,128)(2,1)S(1)}, u32[]{:S(2)}, u32[]{:S(2)}) collective-permute-start(bf16[8,2048]{1,0:T(8,128)(2,1)S(1)} %get-tuple-element.33), channel_id=1, source_target_pairs={{0,8},{4,12},{8,0},{12,4},{1,9},{5,13},{9,1},{13,5},{2,10},{6,14},... | collective-permute-start | bytes 98312 | tf_op jit(solution)/shard_map/ppermute | solution.py:213
  21.6 5.7 %collective-permute-start.9 = (bf16[8,2048]{1,0:T(8,128)(2,1)S(1)}, bf16[8,2048]{1,0:T(8,128)(2,1)S(1)}, u32[]{:S(2)}, u32[]{:S(2)}) collective-permute-start(bf16[8,2048]{1,0:T(8,128)(2,1)S(1)} %get-tuple-element.34), channel_id=1, source_target_pairs={{0,12},{4,8},{8,4},{12,0},{1,13},{5,9},{9,5},{13,1},{2,14},{6,10},... | collective-permute-start | bytes 98312 | tf_op jit(solution)/shard_map/ppermute | solution.py:213
  24.4 4.0 %collective-permute-start.5 = (bf16[8,2048]{1,0:T(8,128)(2,1)S(1)}, bf16[8,2048]{1,0:T(8,128)(2,1)S(1)}, u32[]{:S(2)}, u32[]{:S(2)}) collective-permute-start(bf16[8,2048]{1,0:T(8,128)(2,1)S(1)} %get-tuple-element.28), channel_id=1, source_target_pairs={{0,4},{4,0},{8,12},{12,8},{1,5},{5,1},{9,13},{13,9},{2,6},{6,2},{1... | collective-permute-start | bytes 98312 | tf_op jit(solution)/shard_map/ppermute | solution.py:213

commit v15 on v13

--- a/solution.py
+++ b/solution.py
@@ -48,10 +48,10 @@
         for block, k in ((far[i], i + 2 + core), (far[i + 1], i + 3 - core)):
             x[pl.ds(pl.multiple_of(k * tok, tok), tok), :] = block[...]
     contract = (((1,), (1,)), ((), ()))
-    gate = lax.dot_general(w_gate[0], x[...], contract, preferred_element_type=jnp.float32)
-    upper = lax.dot_general(w_up[0], x[...], contract, preferred_element_type=jnp.float32)
+    gate = lax.dot_general(x[...], w_gate[0], contract, preferred_element_type=jnp.float32)
+    upper = lax.dot_general(x[...], w_up[0], contract, preferred_element_type=jnp.float32)
     hidden = (gate / (1.0 + jnp.exp(-gate)) * upper).astype(jnp.bfloat16)
-    hidden = lax.dot_general(order[...], hidden, contract, preferred_element_type=jnp.float32)
+    hidden = jnp.dot(order[...], hidden, preferred_element_type=jnp.float32)
     hidden = hidden.astype(jnp.bfloat16)
     now = rest.shape[0]
     rest[...] = hidden[now:]

time: 29.3 us -> 29.6 us (1.010)
  no operation moved by 1% of the time
where the time goes in v15:
time: 29.6 us; the launch traced here: 29.4 us
  starting transfers between devices  12.6 us (43%)
  waiting for transfers between devices  11.5 us (39%)
  Pallas kernels  5.26 us (18%)
    ppermute x1, waiting for transfers between devices, on_device(): far.append(lax.ppermute(tokens, ('expert', 'etp'), route))  4.1 us
    ppermute x1, starting transfers between devices, on_device(): far.append(lax.ppermute(tokens, ('expert', 'etp'), route))  4.04 us
    ppermute x3, waiting for transfers between devices, on_device(): lax.ppermute(pieces[k], 'expert', [(e, e ^ k) for e in range(n_expert)])  3.9 us
    ppermute x3, starting transfers between devices, on_device(): lax.ppermute(pieces[k], 'expert', [(e, e ^ k) for e in range(n_expert)])  3.79 us
    pallas_call x1, Pallas kernels, on_device(): pl.pallas_call(functools.partial(ffn_kernel, n_expert, parts), out_shape=...  2.78 us
    ppermute x2, starting transfers between devices, on_device(): landed.append(lax.ppermute(piece, 'etp', route))  2.5 us
    ppermute x2, waiting for transfers between devices, on_device(): landed.append(lax.ppermute(piece, 'etp', route))  1.89 us
    ppermute x1, starting transfers between devices, on_device(): lax.ppermute(own, 'expert', [(e, e ^ 1) for e in range(n_expert)])  1.64 us
  transfers between devices with their start and end apart: 10, of which 7 were waited for; matrix products, arithmetic and copies ran while one was open for 0% of the time, Pallas kernels for 6%

profile of v15, /device:TPU:0, one launch (start us, length us, event | category | flops | bytes accessed | tf_op | source)
XLA Modules:
  0.0 29.4 jit_solution(15894687353804174157)
XLA Ops:
  0.0 4.0 %collective-permute-start.1 = (bf16[16,4096]{1,0:T(8,128)(2,1)}, bf16[16,4096]{1,0:T(8,128)(2,1)S(1)}, u32[]{:S(2)}, u32[]{:S(2)}) collective-permute-start(bf16[16,4096]{1,0:T(8,128)(2,1)} %tokens.1), channel_id=1, source_target_pairs={{0,8},{1,13},{2,10},{3,15},{4,12},{5,9},{6,14},{7,11},{8,0},{9,5},... | collective-permute-start | bytes 393224 | tf_op jit(solution)/shard_map/ppermute | solution.py:151
  4.0 0.9 %fetch.1.own = bf16[16,4096]{1,0:T(8,128)(2,1)S(1)} custom-call(bf16[16,4096]{1,0:T(8,128)(2,1)} %tokens.1), custom_call_target="tpu_custom_call" | custom-call | tf_op jit(solution)/shard_map/fetch/pallas_call | solution.py:123
  5.0 0.0 copy-start
  5.0 0.0 copy-start.1
  5.0 0.0 copy-start.2
  5.1 1.6 %collective-permute-start = (bf16[16,4096]{1,0:T(8,128)(2,1)S(1)}, bf16[16,4096]{1,0:T(8,128)(2,1)S(1)}, u32[]{:S(2)}, u32[]{:S(2)}) collective-permute-start(bf16[16,4096]{1,0:T(8,128)(2,1)S(1)} %fetch.1.own), channel_id=1, source_target_pairs={{0,4},{4,0},{8,12},{12,8},{1,5},{5,1},{9,13},{13,9},{2,6},{6,2},{1... | collective-permute-start | bytes 393224 | tf_op jit(solution)/shard_map/ppermute | solution.py:152
  6.7 4.1 %collective-permute-done.1.refs_0_ = bf16[16,4096]{1,0:T(8,128)(2,1)S(1)} collective-permute-done((bf16[16,4096]{1,0:T(8,128)(2,1)}, bf16[16,4096]{1,0:T(8,128)(2,1)S(1)}, u32[]{:S(2)}, u32[]{:S(2)}) %collective-permute-start.1) | collective-permute-done | bytes 131104 | tf_op jit(solution)/shard_map/ppermute | solution.py:151
  10.8 1.4 %collective-permute-done.next_block = bf16[16,4096]{1,0:T(8,128)(2,1)S(1)} collective-permute-done((bf16[16,4096]{1,0:T(8,128)(2,1)S(1)}, bf16[16,4096]{1,0:T(8,128)(2,1)S(1)}, u32[]{:S(2)}, u32[]{:S(2)}) %collective-permute-start) | collective-permute-done | bytes 131104 | tf_op jit(solution)/shard_map/ppermute | solution.py:152
  12.3 2.8 %ffn.1 = (f32[16,4096]{1,0:T(8,128)S(1)}, bf16[16,4096]{1,0:T(8,128)(2,1)S(1)}, bf16[32,384]{1,0:T(8,128)(2,1)S(1)}) custom-call(bf16[16,4096]{1,0:T(8,128)(2,1)S(1)} %fetch.1.own, bf16[16,4096]{1,0:T(8,128)(2,1)S(1)} %collective-permute-done.next_block, bf16[64,64]{1,0:T(8,128)(2,1)S(1)} %order.1, bf16[16,4096]{1,0:T(8,128)(2,1)S(1)} %collective-permute-done.1.refs_0_, ...), custom_call_target="tpu_custom_call" | custom-call | tf_op jit(solution)/shard_map/ffn/pallas_call | solution.py:160
  15.0 0.0 copy-start.4
  15.1 0.1 collective-permute-start.6
  15.2 0.6 %down.1 = (f32[16,4096]{1,0:T(8,128)S(1)}, bf16[16,4096]{1,0:T(8,128)(2,1)S(1)}) custom-call(bf16[32,384]{1,0:T(8,128)(2,1)S(1)} %get-tuple-element.22.hidden, bf16[1,384,4096]{2,1,0:T(8,128)(2,1)S(1)} %copy-done), custom_call_target="tpu_custom_call" | custom-call | tf_op jit(solution)/shard_map/down/pallas_call | solution.py:169
  15.8 0.5 %collective-permute-start.3 = (bf16[16,4096]{1,0:T(8,128)(2,1)S(1)}, bf16[16,4096]{1,0:T(8,128)(2,1)S(1)}, u32[]{:S(2)}, u32[]{:S(2)}) collective-permute-start(bf16[16,4096]{1,0:T(8,128)(2,1)S(1)} %get-tuple-element.24), channel_id=1, source_target_pairs={{0,1},{1,0},{2,3},{3,2},{4,5},{5,4},{6,7},{7,6},{8,9},{9,8},{10,11... | collective-permute-start | bytes 393224 | tf_op jit(solution)/shard_map/ppermute | solution.py:181
  16.3 0.2 collective-permute-done.6.arrived
  16.5 1.7 %collective-permute-start.7 = (bf16[8,4096]{1,0:T(8,128)(2,1)S(1)}, bf16[8,4096]{1,0:T(8,128)(2,1)S(1)}, u32[]{:S(2)}, u32[]{:S(2)}) collective-permute-start(bf16[8,4096]{1,0:T(8,128)(2,1)S(1)} %get-tuple-element.32), channel_id=1, source_target_pairs={{0,2},{1,3},{2,0},{3,1},{4,6},{5,7},{6,4},{7,5},{8,10},{9,11},{10,... | collective-permute-start | bytes 196616 | tf_op jit(solution)/shard_map/ppermute | solution.py:194
  18.2 0.8 %collective-permute-start.4 = (bf16[8,4096]{1,0:T(8,128)(2,1)S(1)}, bf16[8,4096]{1,0:T(8,128)(2,1)S(1)}, u32[]{:S(2)}, u32[]{:S(2)}) collective-permute-start(bf16[8,4096]{1,0:T(8,128)(2,1)S(1)} %get-tuple-element.26), channel_id=1, source_target_pairs={{0,2},{1,3},{2,0},{3,1},{4,6},{5,7},{6,4},{7,5},{8,10},{9,11},{10,... | collective-permute-start | bytes 196616 | tf_op jit(solution)/shard_map/ppermute | solution.py:194
  19.0 1.9 %collective-permute-done.7.refs_0_ = bf16[8,4096]{1,0:T(8,128)(2,1)S(1)} collective-permute-done((bf16[8,4096]{1,0:T(8,128)(2,1)S(1)}, bf16[8,4096]{1,0:T(8,128)(2,1)S(1)}, u32[]{:S(2)}, u32[]{:S(2)}) %collective-permute-start.7) | collective-permute-done | bytes 65568 | tf_op jit(solution)/shard_map/ppermute | solution.py:194
  21.0 0.9 %collective-permute-start.8 = (bf16[4,4096]{1,0:T(4,128)(2,1)S(1)}, bf16[4,4096]{1,0:T(4,128)(2,1)S(1)}, u32[]{:S(2)}, u32[]{:S(2)}) collective-permute-start(bf16[4,4096]{1,0:T(4,128)(2,1)S(1)} %get-tuple-element.33), channel_id=1, source_target_pairs={{0,8},{4,12},{8,0},{12,4},{1,9},{5,13},{9,1},{13,5},{2,10},{6,14},... | collective-permute-start | bytes 98312 | tf_op jit(solution)/shard_map/ppermute | solution.py:206
  21.9 2.8 %collective-permute-start.9 = (bf16[4,4096]{1,0:T(4,128)(2,1)S(1)}, bf16[4,4096]{1,0:T(4,128)(2,1)S(1)}, u32[]{:S(2)}, u32[]{:S(2)}) collective-permute-start(bf16[4,4096]{1,0:T(4,128)(2,1)S(1)} %get-tuple-element.34), channel_id=1, source_target_pairs={{0,12},{4,8},{8,4},{12,0},{1,13},{5,9},{9,5},{13,1},{2,14},{6,10},... | collective-permute-start | bytes 98312 | tf_op jit(solution)/shard_map/ppermute | solution.py:206
  24.7 0.1 collective-permute-start.5
  24.8 1.1 %collective-permute-done.8.refs_2_ = bf16[4,4096]{1,0:T(4,128)(2,1)S(1)} collective-permute-done((bf16[4,4096]{1,0:T(4,128)(2,1)S(1)}, bf16[4,4096]{1,0:T(4,128)(2,1)S(1)}, u32[]{:S(2)}, u32[]{:S(2)}) %collective-permute-start.8) | collective-permute-done | bytes 32800 | tf_op jit(solution)/shard_map/ppermute | solution.py:206
  25.9 1.7 %collective-permute-done.9.refs_3_ = bf16[4,4096]{1,0:T(4,128)(2,1)S(1)} collective-permute-done((bf16[4,4096]{1,0:T(4,128)(2,1)S(1)}, bf16[4,4096]{1,0:T(4,128)(2,1)S(1)}, u32[]{:S(2)}, u32[]{:S(2)}) %collective-permute-start.9) | collective-permute-done | bytes 32800 | tf_op jit(solution)/shard_map/ppermute | solution.py:206
  27.6 1.1 %collective-permute-done.5.refs_1_ = bf16[4,4096]{1,0:T(4,128)(2,1)S(1)} collective-permute-done((bf16[4,4096]{1,0:T(4,128)(2,1)S(1)}, bf16[4,4096]{1,0:T(4,128)(2,1)S(1)}, u32[]{:S(2)}, u32[]{:S(2)}) %collective-permute-start.5) | collective-permute-done | bytes 32800 | tf_op jit(solution)/shard_map/ppermute | solution.py:206
  28.7 0.7 %mix.1 = bf16[4,4096]{1,0:T(4,128)(2,1)} custom-call(s32[2,16]{1,0:T(2,128)S(1)} %bitcast.2, f32[2,4]{1,0:T(2,128)S(1)} %bitcast.3, bf16[4,4096]{1,0:T(4,128)(2,1)S(1)} %get-tuple-element.27.refs_0_, bf16[4,4096]{1,0:T(4,128)(2,1)S(1)} %collective-permute-done.5.refs_1_, bf16[4,4096]{1,0:T(4,128)(2,1)S(1)} %collective-permute-done.8.refs_2_, ...), custom_call_target="tpu_custom_call" | custom-call | tf_op jit(solution)/shard_map/mix/pallas_call | solution.py:209
  (15 shorter events, 0.2 us)
Async XLA Ops:
  0.0 10.8 %collective-permute-start.1 = (bf16[16,4096]{1,0:T(8,128)(2,1)}, bf16[16,4096]{1,0:T(8,128)(2,1)S(1)}, u32[]{:S(2)}, u32[]{:S(2)}) collective-permute-start(bf16[16,4096]{1,0:T(8,128)(2,1)} %tokens.1), channel_id=1, source_target_pairs={{0,8},{1,13},{2,10},{3,15},{4,12},{5,9},{6,14},{7,11},{8,0},{9,5},... | collective-permute-start | bytes 393224 | tf_op jit(solution)/shard_map/ppermute | solution.py:151
  5.0 7.2 %copy-start = (bf16[1,384,4096]{2,1,0:T(8,128)(2,1)S(1)}, bf16[1,384,4096]{2,1,0:T(8,128)(2,1)}, u32[]{:S(2)}) copy-start(bf16[1,384,4096]{2,1,0:T(8,128)(2,1)} %w_down.1) | copy-start | bytes 9437188
  5.0 7.2 %copy-start.1 = (bf16[1,384,4096]{2,1,0:T(8,128)(2,1)S(1)}, bf16[1,384,4096]{2,1,0:T(8,128)(2,1)}, u32[]{:S(2)}) copy-start(bf16[1,384,4096]{2,1,0:T(8,128)(2,1)} %refs_2_.1) | copy-start | bytes 9437188
  5.0 7.2 %copy-start.2 = (bf16[1,384,4096]{2,1,0:T(8,128)(2,1)S(1)}, bf16[1,384,4096]{2,1,0:T(8,128)(2,1)}, u32[]{:S(2)}) copy-start(bf16[1,384,4096]{2,1,0:T(8,128)(2,1)} %refs_3_.1) | copy-start | bytes 9437188
  5.1 7.1 %collective-permute-start = (bf16[16,4096]{1,0:T(8,128)(2,1)S(1)}, bf16[16,4096]{1,0:T(8,128)(2,1)S(1)}, u32[]{:S(2)}, u32[]{:S(2)}) collective-permute-start(bf16[16,4096]{1,0:T(8,128)(2,1)S(1)} %fetch.1.own), channel_id=1, source_target_pairs={{0,4},{4,0},{8,12},{12,8},{1,5},{5,1},{9,13},{13,9},{2,6},{6,2},{1... | collective-permute-start | bytes 393224 | tf_op jit(solution)/shard_map/ppermute | solution.py:152
  10.8 1.4 %collective-permute-start.2 = (bf16[16,4096]{1,0:T(8,128)(2,1)S(1)}, bf16[16,4096]{1,0:T(8,128)(2,1)S(1)}, u32[]{:S(2)}, u32[]{:S(2)}) collective-permute-start(bf16[16,4096]{1,0:T(8,128)(2,1)S(1)} %collective-permute-done.1.refs_0_), channel_id=1, source_target_pairs={{0,1},{1,0},{2,3},{3,2},{4,5},{5,4},{6,7},{7,6},{8,9},{9,8},{10,11... | collective-permute-start | bytes 393224 | tf_op jit(solution)/shard_map/ppermute | solution.py:153
  15.0 13.6 %copy-start.3 = (s32[16,2]{0,1:T(2,128)S(1)}, s32[16,2]{0,1:T(2,128)}, u32[]{:S(2)}) copy-start(s32[16,2]{0,1:T(2,128)} %param.7) | copy-start | bytes 388
  15.0 13.6 %copy-start.4 = (f32[4,2]{0,1:T(2,128)S(1)}, f32[4,2]{0,1:T(2,128)}, u32[]{:S(2)}) copy-start(f32[4,2]{0,1:T(2,128)} %param.8) | copy-start | bytes 100
  15.1 1.4 %collective-permute-start.6 = (bf16[16,4096]{1,0:T(8,128)(2,1)S(1)}, bf16[16,4096]{1,0:T(8,128)(2,1)S(1)}, u32[]{:S(2)}, u32[]{:S(2)}) collective-permute-start(bf16[16,4096]{1,0:T(8,128)(2,1)S(1)} %get-tuple-element.30), channel_id=1, source_target_pairs={{0,1},{1,0},{2,3},{3,2},{4,5},{5,4},{6,7},{7,6},{8,9},{9,8},{10,11... | collective-permute-start | bytes 393224 | tf_op jit(solution)/shard_map/ppermute | solution.py:181
  15.8 2.4 %collective-permute-start.3 = (bf16[16,4096]{1,0:T(8,128)(2,1)S(1)}, bf16[16,4096]{1,0:T(8,128)(2,1)S(1)}, u32[]{:S(2)}, u32[]{:S(2)}) collective-permute-start(bf16[16,4096]{1,0:T(8,128)(2,1)S(1)} %get-tuple-element.24), channel_id=1, source_target_pairs={{0,1},{1,0},{2,3},{3,2},{4,5},{5,4},{6,7},{7,6},{8,9},{9,8},{10,11... | collective-permute-start | bytes 393224 | tf_op jit(solution)/shard_map/ppermute | solution.py:181
  16.5 4.4 %collective-permute-start.7 = (bf16[8,4096]{1,0:T(8,128)(2,1)S(1)}, bf16[8,4096]{1,0:T(8,128)(2,1)S(1)}, u32[]{:S(2)}, u32[]{:S(2)}) collective-permute-start(bf16[8,4096]{1,0:T(8,128)(2,1)S(1)} %get-tuple-element.32), channel_id=1, source_target_pairs={{0,2},{1,3},{2,0},{3,1},{4,6},{5,7},{6,4},{7,5},{8,10},{9,11},{10,... | collective-permute-start | bytes 196616 | tf_op jit(solution)/shard_map/ppermute | solution.py:194
  18.2 6.4 %collective-permute-start.4 = (bf16[8,4096]{1,0:T(8,128)(2,1)S(1)}, bf16[8,4096]{1,0:T(8,128)(2,1)S(1)}, u32[]{:S(2)}, u32[]{:S(2)}) collective-permute-start(bf16[8,4096]{1,0:T(8,128)(2,1)S(1)} %get-tuple-element.26), channel_id=1, source_target_pairs={{0,2},{1,3},{2,0},{3,1},{4,6},{5,7},{6,4},{7,5},{8,10},{9,11},{10,... | collective-permute-start | bytes 196616 | tf_op jit(solution)/shard_map/ppermute | solution.py:194
  21.0 4.9 %collective-permute-start.8 = (bf16[4,4096]{1,0:T(4,128)(2,1)S(1)}, bf16[4,4096]{1,0:T(4,128)(2,1)S(1)}, u32[]{:S(2)}, u32[]{:S(2)}) collective-permute-start(bf16[4,4096]{1,0:T(4,128)(2,1)S(1)} %get-tuple-element.33), channel_id=1, source_target_pairs={{0,8},{4,12},{8,0},{12,4},{1,9},{5,13},{9,1},{13,5},{2,10},{6,14},... | collective-permute-start | bytes 98312 | tf_op jit(solution)/shard_map/ppermute | solution.py:206
  21.9 5.7 %collective-permute-start.9 = (bf16[4,4096]{1,0:T(4,128)(2,1)S(1)}, bf16[4,4096]{1,0:T(4,128)(2,1)S(1)}, u32[]{:S(2)}, u32[]{:S(2)}) collective-permute-start(bf16[4,4096]{1,0:T(4,128)(2,1)S(1)} %get-tuple-element.34), channel_id=1, source_target_pairs={{0,12},{4,8},{8,4},{12,0},{1,13},{5,9},{9,5},{13,1},{2,14},{6,10},... | collective-permute-start | bytes 98312 | tf_op jit(solution)/shard_map/ppermute | solution.py:206
  24.7 4.0 %collective-permute-start.5 = (bf16[4,4096]{1,0:T(4,128)(2,1)S(1)}, bf16[4,4096]{1,0:T(4,128)(2,1)S(1)}, u32[]{:S(2)}, u32[]{:S(2)}) collective-permute-start(bf16[4,4096]{1,0:T(4,128)(2,1)S(1)} %get-tuple-element.28), channel_id=1, source_target_pairs={{0,4},{4,0},{8,12},{12,8},{1,5},{5,1},{9,13},{13,9},{2,6},{6,2},{1... | collective-permute-start | bytes 98312 | tf_op jit(solution)/shard_map/ppermute | solution.py:206

commit v16 on v13

--- a/solution.py
+++ b/solution.py
@@ -138,7 +138,6 @@
         compiler_params=GRANT,
         name="order",
     )(own)
-    own, order = lax.optimization_barrier((own, order))
 
     swap = [(t, t ^ 1) for t in range(n_etp)]
     far = []
@@ -149,7 +148,7 @@
             for t in range(n_etp)
         ]
         far.append(lax.ppermute(tokens, ("expert", "etp"), route))
-    next_block = lax.ppermute(own, "expert", [(e, e ^ 1) for e in range(n_expert)])
+    next_block = lax.ppermute(tokens, "expert", [(e, e ^ 1) for e in range(n_expert)])
     far = [b for block in far for b in (block, lax.ppermute(block, "etp", swap))]
 
     parts = 4

time: 29.3 us -> 29.3 us (level)
  starting transfers between devices: 12.6 us -> 12.2 us
  waiting for transfers between devices: 11.5 us -> 11.8 us
    ppermute x1, waiting for transfers between devices: 1.41 us -> 0.74 us  [on_device(): lax.ppermute(tokens, 'expert', [(e, e ^ 1) for e in range(n_expert)])]
    ppermute x1, waiting for transfers between devices: 0.01 us -> 0.56 us  [on_device(): lax.ppermute(block, 'etp', swap)]
    ppermute x2, waiting for transfers between devices: 1.89 us -> 2.21 us  [on_device(): landed.append(lax.ppermute(piece, 'etp', route))]
  transfers between devices with their start and end apart: 10 -> 10, of which waited for: 7 -> 8; matrix products, arithmetic and copies ran while one was open for 0% -> 0% of each run, Pallas kernels for 6% -> 6%
where the time goes in v16:
time: 29.3 us; the launch traced here: 29.2 us
  starting transfers between devices  12.2 us (42%)
  waiting for transfers between devices  11.8 us (40%)
  Pallas kernels  5.01 us (17%)
    ppermute x1, waiting for transfers between devices, on_device(): far.append(lax.ppermute(tokens, ('expert', 'etp'), route))  4.22 us
    ppermute x1, starting transfers between devices, on_device(): far.append(lax.ppermute(tokens, ('expert', 'etp'), route))  4.04 us
    ppermute x3, waiting for transfers between devices, on_device(): lax.ppermute(pieces[k], 'expert', [(e, e ^ k) for e in range(n_expert)])  3.9 us
    ppermute x3, starting transfers between devices, on_device(): lax.ppermute(pieces[k], 'expert', [(e, e ^ k) for e in range(n_expert)])  3.68 us
    pallas_call x1, Pallas kernels, on_device(): pl.pallas_call(functools.partial(ffn_kernel, n_expert, parts), out_shape=...  2.53 us
    ppermute x2, starting transfers between devices, on_device(): landed.append(lax.ppermute(piece, 'etp', route))  2.35 us
    ppermute x2, waiting for transfers between devices, on_device(): landed.append(lax.ppermute(piece, 'etp', route))  2.21 us
    ppermute x1, starting transfers between devices, on_device(): lax.ppermute(tokens, 'expert', [(e, e ^ 1) for e in range(n_expert)])  1.58 us
  transfers between devices with their start and end apart: 10, of which 8 were waited for; matrix products, arithmetic and copies ran while one was open for 0% of the time, Pallas kernels for 6%

profile of v16, /device:TPU:0, one launch (start us, length us, event | category | flops | bytes accessed | tf_op | source)
XLA Modules:
  0.0 29.2 jit_solution(5608389273446553621)
XLA Ops:
  0.0 4.0 %collective-permute-start.1 = (bf16[16,4096]{1,0:T(8,128)(2,1)}, bf16[16,4096]{1,0:T(8,128)(2,1)S(1)}, u32[]{:S(2)}, u32[]{:S(2)}) collective-permute-start(bf16[16,4096]{1,0:T(8,128)(2,1)} %tokens.1), channel_id=1, source_target_pairs={{0,8},{1,13},{2,10},{3,15},{4,12},{5,9},{6,14},{7,11},{8,0},{9,5},... | collective-permute-start | bytes 393224 | tf_op jit(solution)/shard_map/ppermute | solution.py:150
  4.0 1.6 %collective-permute-start = (bf16[16,4096]{1,0:T(8,128)(2,1)}, bf16[16,4096]{1,0:T(8,128)(2,1)S(1)}, u32[]{:S(2)}, u32[]{:S(2)}) collective-permute-start(bf16[16,4096]{1,0:T(8,128)(2,1)} %tokens.1), channel_id=1, source_target_pairs={{0,4},{4,0},{8,12},{12,8},{1,5},{5,1},{9,13},{13,9},{2,6},{6,2},{1... | collective-permute-start | bytes 393224 | tf_op jit(solution)/shard_map/ppermute | solution.py:151
  5.6 0.9 %fetch.1.own = bf16[16,4096]{1,0:T(8,128)(2,1)S(1)} custom-call(bf16[16,4096]{1,0:T(8,128)(2,1)} %tokens.1), custom_call_target="tpu_custom_call" | custom-call | tf_op jit(solution)/shard_map/fetch/pallas_call | solution.py:123
  6.6 0.0 copy-start
  6.6 0.0 copy-start.1
  6.6 4.2 %collective-permute-done.1.refs_0_ = bf16[16,4096]{1,0:T(8,128)(2,1)S(1)} collective-permute-done((bf16[16,4096]{1,0:T(8,128)(2,1)}, bf16[16,4096]{1,0:T(8,128)(2,1)S(1)}, u32[]{:S(2)}, u32[]{:S(2)}) %collective-permute-start.1) | collective-permute-done | bytes 131104 | tf_op jit(solution)/shard_map/ppermute | solution.py:150
  10.9 0.7 %collective-permute-done.next_block = bf16[16,4096]{1,0:T(8,128)(2,1)S(1)} collective-permute-done((bf16[16,4096]{1,0:T(8,128)(2,1)}, bf16[16,4096]{1,0:T(8,128)(2,1)S(1)}, u32[]{:S(2)}, u32[]{:S(2)}) %collective-permute-start) | collective-permute-done | bytes 131104 | tf_op jit(solution)/shard_map/ppermute | solution.py:151
  11.6 0.6 %collective-permute-done.2.refs_1_ = bf16[16,4096]{1,0:T(8,128)(2,1)S(1)} collective-permute-done((bf16[16,4096]{1,0:T(8,128)(2,1)S(1)}, bf16[16,4096]{1,0:T(8,128)(2,1)S(1)}, u32[]{:S(2)}, u32[]{:S(2)}) %collective-permute-start.2) | collective-permute-done | bytes 131104 | tf_op jit(solution)/shard_map/ppermute | solution.py:152
  12.2 2.5 %ffn.1 = (f32[16,4096]{1,0:T(8,128)S(1)}, bf16[16,4096]{1,0:T(8,128)(2,1)S(1)}, bf16[32,384]{1,0:T(8,128)(2,1)S(1)}) custom-call(bf16[16,4096]{1,0:T(8,128)(2,1)S(1)} %fetch.1.own, bf16[16,4096]{1,0:T(8,128)(2,1)S(1)} %collective-permute-done.next_block, bf16[64,64]{1,0:T(8,128)(2,1)S(1)} %order.1, bf16[16,4096]{1,0:T(8,128)(2,1)S(1)} %collective-permute-done.1.refs_0_, ...), custom_call_target="tpu_custom_call" | custom-call | tf_op jit(solution)/shard_map/ffn/pallas_call | solution.py:159
  14.7 0.0 copy-start.4
  14.7 0.2 collective-permute-start.6
  14.9 0.6 %down.1 = (f32[16,4096]{1,0:T(8,128)S(1)}, bf16[16,4096]{1,0:T(8,128)(2,1)S(1)}) custom-call(bf16[32,384]{1,0:T(8,128)(2,1)S(1)} %get-tuple-element.18.hidden, bf16[1,384,4096]{2,1,0:T(8,128)(2,1)S(1)} %copy-done), custom_call_target="tpu_custom_call" | custom-call | tf_op jit(solution)/shard_map/down/pallas_call | solution.py:168
  15.6 0.4 %collective-permute-start.3 = (bf16[16,4096]{1,0:T(8,128)(2,1)S(1)}, bf16[16,4096]{1,0:T(8,128)(2,1)S(1)}, u32[]{:S(2)}, u32[]{:S(2)}) collective-permute-start(bf16[16,4096]{1,0:T(8,128)(2,1)S(1)} %get-tuple-element.20), channel_id=1, source_target_pairs={{0,1},{1,0},{2,3},{3,2},{4,5},{5,4},{6,7},{7,6},{8,9},{9,8},{10,11... | collective-permute-start | bytes 393224 | tf_op jit(solution)/shard_map/ppermute | solution.py:180
  16.0 0.2 collective-permute-done.6.arrived
  16.2 1.6 %collective-permute-start.7 = (bf16[8,4096]{1,0:T(8,128)(2,1)S(1)}, bf16[8,4096]{1,0:T(8,128)(2,1)S(1)}, u32[]{:S(2)}, u32[]{:S(2)}) collective-permute-start(bf16[8,4096]{1,0:T(8,128)(2,1)S(1)} %get-tuple-element.28), channel_id=1, source_target_pairs={{0,2},{1,3},{2,0},{3,1},{4,6},{5,7},{6,4},{7,5},{8,10},{9,11},{10,... | collective-permute-start | bytes 196616 | tf_op jit(solution)/shard_map/ppermute | solution.py:193
  17.8 0.8 %collective-permute-start.4 = (bf16[8,4096]{1,0:T(8,128)(2,1)S(1)}, bf16[8,4096]{1,0:T(8,128)(2,1)S(1)}, u32[]{:S(2)}, u32[]{:S(2)}) collective-permute-start(bf16[8,4096]{1,0:T(8,128)(2,1)S(1)} %get-tuple-element.22), channel_id=1, source_target_pairs={{0,2},{1,3},{2,0},{3,1},{4,6},{5,7},{6,4},{7,5},{8,10},{9,11},{10,... | collective-permute-start | bytes 196616 | tf_op jit(solution)/shard_map/ppermute | solution.py:193
  18.6 2.2 %collective-permute-done.7.refs_0_ = bf16[8,4096]{1,0:T(8,128)(2,1)S(1)} collective-permute-done((bf16[8,4096]{1,0:T(8,128)(2,1)S(1)}, bf16[8,4096]{1,0:T(8,128)(2,1)S(1)}, u32[]{:S(2)}, u32[]{:S(2)}) %collective-permute-start.7) | collective-permute-done | bytes 65568 | tf_op jit(solution)/shard_map/ppermute | solution.py:193
  20.8 0.8 %collective-permute-start.8 = (bf16[4,4096]{1,0:T(4,128)(2,1)S(1)}, bf16[4,4096]{1,0:T(4,128)(2,1)S(1)}, u32[]{:S(2)}, u32[]{:S(2)}) collective-permute-start(bf16[4,4096]{1,0:T(4,128)(2,1)S(1)} %get-tuple-element.29), channel_id=1, source_target_pairs={{0,8},{4,12},{8,0},{12,4},{1,9},{5,13},{9,1},{13,5},{2,10},{6,14},... | collective-permute-start | bytes 98312 | tf_op jit(solution)/shard_map/ppermute | solution.py:205
  21.6 2.8 %collective-permute-start.9 = (bf16[4,4096]{1,0:T(4,128)(2,1)S(1)}, bf16[4,4096]{1,0:T(4,128)(2,1)S(1)}, u32[]{:S(2)}, u32[]{:S(2)}) collective-permute-start(bf16[4,4096]{1,0:T(4,128)(2,1)S(1)} %get-tuple-element.30), channel_id=1, source_target_pairs={{0,12},{4,8},{8,4},{12,0},{1,13},{5,9},{9,5},{13,1},{2,14},{6,10},... | collective-permute-start | bytes 98312 | tf_op jit(solution)/shard_map/ppermute | solution.py:205
  24.4 0.1 collective-permute-start.5
  24.5 1.3 %collective-permute-done.8.refs_2_ = bf16[4,4096]{1,0:T(4,128)(2,1)S(1)} collective-permute-done((bf16[4,4096]{1,0:T(4,128)(2,1)S(1)}, bf16[4,4096]{1,0:T(4,128)(2,1)S(1)}, u32[]{:S(2)}, u32[]{:S(2)}) %collective-permute-start.8) | collective-permute-done | bytes 32800 | tf_op jit(solution)/shard_map/ppermute | solution.py:205
  25.8 1.5 %collective-permute-done.9.refs_3_ = bf16[4,4096]{1,0:T(4,128)(2,1)S(1)} collective-permute-done((bf16[4,4096]{1,0:T(4,128)(2,1)S(1)}, bf16[4,4096]{1,0:T(4,128)(2,1)S(1)}, u32[]{:S(2)}, u32[]{:S(2)}) %collective-permute-start.9) | collective-permute-done | bytes 32800 | tf_op jit(solution)/shard_map/ppermute | solution.py:205
  27.3 1.1 %collective-permute-done.5.refs_1_ = bf16[4,4096]{1,0:T(4,128)(2,1)S(1)} collective-permute-done((bf16[4,4096]{1,0:T(4,128)(2,1)S(1)}, bf16[4,4096]{1,0:T(4,128)(2,1)S(1)}, u32[]{:S(2)}, u32[]{:S(2)}) %collective-permute-start.5) | collective-permute-done | bytes 32800 | tf_op jit(solution)/shard_map/ppermute | solution.py:205
  28.4 0.7 %mix.1 = bf16[4,4096]{1,0:T(4,128)(2,1)} custom-call(s32[2,16]{1,0:T(2,128)S(1)} %bitcast.2, f32[2,4]{1,0:T(2,128)S(1)} %bitcast.3, bf16[4,4096]{1,0:T(4,128)(2,1)S(1)} %get-tuple-element.23.refs_0_, bf16[4,4096]{1,0:T(4,128)(2,1)S(1)} %collective-permute-done.5.refs_1_, bf16[4,4096]{1,0:T(4,128)(2,1)S(1)} %collective-permute-done.8.refs_2_, ...), custom_call_target="tpu_custom_call" | custom-call | tf_op jit(solution)/shard_map/mix/pallas_call | solution.py:208
  (15 shorter events, 0.2 us)
Async XLA Ops:
  0.0 10.8 %collective-permute-start.1 = (bf16[16,4096]{1,0:T(8,128)(2,1)}, bf16[16,4096]{1,0:T(8,128)(2,1)S(1)}, u32[]{:S(2)}, u32[]{:S(2)}) collective-permute-start(bf16[16,4096]{1,0:T(8,128)(2,1)} %tokens.1), channel_id=1, source_target_pairs={{0,8},{1,13},{2,10},{3,15},{4,12},{5,9},{6,14},{7,11},{8,0},{9,5},... | collective-permute-start | bytes 393224 | tf_op jit(solution)/shard_map/ppermute | solution.py:150
  4.0 7.6 %collective-permute-start = (bf16[16,4096]{1,0:T(8,128)(2,1)}, bf16[16,4096]{1,0:T(8,128)(2,1)S(1)}, u32[]{:S(2)}, u32[]{:S(2)}) collective-permute-start(bf16[16,4096]{1,0:T(8,128)(2,1)} %tokens.1), channel_id=1, source_target_pairs={{0,4},{4,0},{8,12},{12,8},{1,5},{5,1},{9,13},{13,9},{2,6},{6,2},{1... | collective-permute-start | bytes 393224 | tf_op jit(solution)/shard_map/ppermute | solution.py:151
  6.6 5.6 %copy-start = (bf16[1,384,4096]{2,1,0:T(8,128)(2,1)S(1)}, bf16[1,384,4096]{2,1,0:T(8,128)(2,1)}, u32[]{:S(2)}) copy-start(bf16[1,384,4096]{2,1,0:T(8,128)(2,1)} %w_down.1) | copy-start | bytes 9437188
  6.6 5.6 %copy-start.1 = (bf16[1,384,4096]{2,1,0:T(8,128)(2,1)S(1)}, bf16[1,384,4096]{2,1,0:T(8,128)(2,1)}, u32[]{:S(2)}) copy-start(bf16[1,384,4096]{2,1,0:T(8,128)(2,1)} %refs_2_.1) | copy-start | bytes 9437188
  6.6 5.6 %copy-start.2 = (bf16[1,384,4096]{2,1,0:T(8,128)(2,1)S(1)}, bf16[1,384,4096]{2,1,0:T(8,128)(2,1)}, u32[]{:S(2)}) copy-start(bf16[1,384,4096]{2,1,0:T(8,128)(2,1)} %refs_3_.1) | copy-start | bytes 9437188
  10.8 1.3 %collective-permute-start.2 = (bf16[16,4096]{1,0:T(8,128)(2,1)S(1)}, bf16[16,4096]{1,0:T(8,128)(2,1)S(1)}, u32[]{:S(2)}, u32[]{:S(2)}) collective-permute-start(bf16[16,4096]{1,0:T(8,128)(2,1)S(1)} %collective-permute-done.1.refs_0_), channel_id=1, source_target_pairs={{0,1},{1,0},{2,3},{3,2},{4,5},{5,4},{6,7},{7,6},{8,9},{9,8},{10,11... | collective-permute-start | bytes 393224 | tf_op jit(solution)/shard_map/ppermute | solution.py:152
  14.7 13.7 %copy-start.3 = (s32[16,2]{0,1:T(2,128)S(1)}, s32[16,2]{0,1:T(2,128)}, u32[]{:S(2)}) copy-start(s32[16,2]{0,1:T(2,128)} %param.7) | copy-start | bytes 388
  14.7 13.7 %copy-start.4 = (f32[4,2]{0,1:T(2,128)S(1)}, f32[4,2]{0,1:T(2,128)}, u32[]{:S(2)}) copy-start(f32[4,2]{0,1:T(2,128)} %param.8) | copy-start | bytes 100
  14.7 1.4 %collective-permute-start.6 = (bf16[16,4096]{1,0:T(8,128)(2,1)S(1)}, bf16[16,4096]{1,0:T(8,128)(2,1)S(1)}, u32[]{:S(2)}, u32[]{:S(2)}) collective-permute-start(bf16[16,4096]{1,0:T(8,128)(2,1)S(1)} %get-tuple-element.26), channel_id=1, source_target_pairs={{0,1},{1,0},{2,3},{3,2},{4,5},{5,4},{6,7},{7,6},{8,9},{9,8},{10,11... | collective-permute-start | bytes 393224 | tf_op jit(solution)/shard_map/ppermute | solution.py:180
  15.6 2.1 %collective-permute-start.3 = (bf16[16,4096]{1,0:T(8,128)(2,1)S(1)}, bf16[16,4096]{1,0:T(8,128)(2,1)S(1)}, u32[]{:S(2)}, u32[]{:S(2)}) collective-permute-start(bf16[16,4096]{1,0:T(8,128)(2,1)S(1)} %get-tuple-element.20), channel_id=1, source_target_pairs={{0,1},{1,0},{2,3},{3,2},{4,5},{5,4},{6,7},{7,6},{8,9},{9,8},{10,11... | collective-permute-start | bytes 393224 | tf_op jit(solution)/shard_map/ppermute | solution.py:180
  16.2 4.6 %collective-permute-start.7 = (bf16[8,4096]{1,0:T(8,128)(2,1)S(1)}, bf16[8,4096]{1,0:T(8,128)(2,1)S(1)}, u32[]{:S(2)}, u32[]{:S(2)}) collective-permute-start(bf16[8,4096]{1,0:T(8,128)(2,1)S(1)} %get-tuple-element.28), channel_id=1, source_target_pairs={{0,2},{1,3},{2,0},{3,1},{4,6},{5,7},{6,4},{7,5},{8,10},{9,11},{10,... | collective-permute-start | bytes 196616 | tf_op jit(solution)/shard_map/ppermute | solution.py:193
  17.8 6.6 %collective-permute-start.4 = (bf16[8,4096]{1,0:T(8,128)(2,1)S(1)}, bf16[8,4096]{1,0:T(8,128)(2,1)S(1)}, u32[]{:S(2)}, u32[]{:S(2)}) collective-permute-start(bf16[8,4096]{1,0:T(8,128)(2,1)S(1)} %get-tuple-element.22), channel_id=1, source_target_pairs={{0,2},{1,3},{2,0},{3,1},{4,6},{5,7},{6,4},{7,5},{8,10},{9,11},{10,... | collective-permute-start | bytes 196616 | tf_op jit(solution)/shard_map/ppermute | solution.py:193
  20.8 5.0 %collective-permute-start.8 = (bf16[4,4096]{1,0:T(4,128)(2,1)S(1)}, bf16[4,4096]{1,0:T(4,128)(2,1)S(1)}, u32[]{:S(2)}, u32[]{:S(2)}) collective-permute-start(bf16[4,4096]{1,0:T(4,128)(2,1)S(1)} %get-tuple-element.29), channel_id=1, source_target_pairs={{0,8},{4,12},{8,0},{12,4},{1,9},{5,13},{9,1},{13,5},{2,10},{6,14},... | collective-permute-start | bytes 98312 | tf_op jit(solution)/shard_map/ppermute | solution.py:205
  21.6 5.7 %collective-permute-start.9 = (bf16[4,4096]{1,0:T(4,128)(2,1)S(1)}, bf16[4,4096]{1,0:T(4,128)(2,1)S(1)}, u32[]{:S(2)}, u32[]{:S(2)}) collective-permute-start(bf16[4,4096]{1,0:T(4,128)(2,1)S(1)} %get-tuple-element.30), channel_id=1, source_target_pairs={{0,12},{4,8},{8,4},{12,0},{1,13},{5,9},{9,5},{13,1},{2,14},{6,10},... | collective-permute-start | bytes 98312 | tf_op jit(solution)/shard_map/ppermute | solution.py:205
  24.4 4.0 %collective-permute-start.5 = (bf16[4,4096]{1,0:T(4,128)(2,1)S(1)}, bf16[4,4096]{1,0:T(4,128)(2,1)S(1)}, u32[]{:S(2)}, u32[]{:S(2)}) collective-permute-start(bf16[4,4096]{1,0:T(4,128)(2,1)S(1)} %get-tuple-element.24), channel_id=1, source_target_pairs={{0,4},{4,0},{8,12},{12,8},{1,5},{5,1},{9,13},{13,9},{2,6},{6,2},{1... | collective-permute-start | bytes 98312 | tf_op jit(solution)/shard_map/ppermute | solution.py:205

commit v17 on v16

--- a/solution.py
+++ b/solution.py
@@ -48,8 +48,16 @@
         for block, k in ((far[i], i + 2 + core), (far[i + 1], i + 3 - core)):
             x[pl.ds(pl.multiple_of(k * tok, tok), tok), :] = block[...]
     contract = (((1,), (1,)), ((), ()))
-    gate = lax.dot_general(w_gate[0], x[...], contract, preferred_element_type=jnp.float32)
-    upper = lax.dot_general(w_up[0], x[...], contract, preferred_element_type=jnp.float32)
+    step = x.shape[1] // parts
+    sums = [None, None]
+    for c in range(parts):
+        cols = slice(c * step, (c + 1) * step)
+        for i, w in enumerate((w_gate, w_up)):
+            part = lax.dot_general(
+                w[0, :, cols], x[:, cols], contract, preferred_element_type=jnp.float32
+            )
+            sums[i] = part if c == 0 else sums[i] + part
+    gate, upper = sums
     hidden = (gate / (1.0 + jnp.exp(-gate)) * upper).astype(jnp.bfloat16)
     hidden = lax.dot_general(order[...], hidden, contract, preferred_element_type=jnp.float32)
     hidden = hidden.astype(jnp.bfloat16)

time: 29.3 us -> 29.3 us (level)
  no operation moved by 1% of the time
where the time goes in v17:
time: 29.3 us; the launch traced here: 29.2 us
  starting transfers between devices  12.2 us (42%)
  waiting for transfers between devices  11.8 us (40%)
  Pallas kernels  5.01 us (17%)
    ppermute x1, waiting for transfers between devices, on_device(): far.append(lax.ppermute(tokens, ('expert', 'etp'), route))  4.22 us
    ppermute x1, starting transfers between devices, on_device(): far.append(lax.ppermute(tokens, ('expert', 'etp'), route))  4.04 us
    ppermute x3, waiting for transfers between devices, on_device(): lax.ppermute(pieces[k], 'expert', [(e, e ^ k) for e in range(n_expert)])  3.9 us
    ppermute x3, starting transfers between devices, on_device(): lax.ppermute(pieces[k], 'expert', [(e, e ^ k) for e in range(n_expert)])  3.68 us
    pallas_call x1, Pallas kernels, on_device(): pl.pallas_call(functools.partial(ffn_kernel, n_expert, parts), out_shape=...  2.53 us
    ppermute x2, starting transfers between devices, on_device(): landed.append(lax.ppermute(piece, 'etp', route))  2.35 us
    ppermute x2, waiting for transfers between devices, on_device(): landed.append(lax.ppermute(piece, 'etp', route))  2.21 us
    ppermute x1, starting transfers between devices, on_device(): lax.ppermute(tokens, 'expert', [(e, e ^ 1) for e in range(n_expert)])  1.58 us
  transfers between devices with their start and end apart: 10, of which 8 were waited for; matrix products, arithmetic and copies ran while one was open for 0% of the time, Pallas kernels for 6%

profile of v17, /device:TPU:0, one launch (start us, length us, event | category | flops | bytes accessed | tf_op | source)
XLA Modules:
  0.0 29.2 jit_solution(12374537867102877731)
XLA Ops:
  0.0 4.0 %collective-permute-start.1 = (bf16[16,4096]{1,0:T(8,128)(2,1)}, bf16[16,4096]{1,0:T(8,128)(2,1)S(1)}, u32[]{:S(2)}, u32[]{:S(2)}) collective-permute-start(bf16[16,4096]{1,0:T(8,128)(2,1)} %tokens.1), channel_id=1, source_target_pairs={{0,8},{1,13},{2,10},{3,15},{4,12},{5,9},{6,14},{7,11},{8,0},{9,5},... | collective-permute-start | bytes 393224 | tf_op jit(solution)/shard_map/ppermute | solution.py:158
  4.0 1.6 %collective-permute-start = (bf16[16,4096]{1,0:T(8,128)(2,1)}, bf16[16,4096]{1,0:T(8,128)(2,1)S(1)}, u32[]{:S(2)}, u32[]{:S(2)}) collective-permute-start(bf16[16,4096]{1,0:T(8,128)(2,1)} %tokens.1), channel_id=1, source_target_pairs={{0,4},{4,0},{8,12},{12,8},{1,5},{5,1},{9,13},{13,9},{2,6},{6,2},{1... | collective-permute-start | bytes 393224 | tf_op jit(solution)/shard_map/ppermute | solution.py:159
  5.6 0.9 %fetch.1.own = bf16[16,4096]{1,0:T(8,128)(2,1)S(1)} custom-call(bf16[16,4096]{1,0:T(8,128)(2,1)} %tokens.1), custom_call_target="tpu_custom_call" | custom-call | tf_op jit(solution)/shard_map/fetch/pallas_call | solution.py:131
  6.6 0.0 copy-start
  6.6 0.0 copy-start.1
  6.6 4.2 %collective-permute-done.1.refs_0_ = bf16[16,4096]{1,0:T(8,128)(2,1)S(1)} collective-permute-done((bf16[16,4096]{1,0:T(8,128)(2,1)}, bf16[16,4096]{1,0:T(8,128)(2,1)S(1)}, u32[]{:S(2)}, u32[]{:S(2)}) %collective-permute-start.1) | collective-permute-done | bytes 131104 | tf_op jit(solution)/shard_map/ppermute | solution.py:158
  10.9 0.7 %collective-permute-done.next_block = bf16[16,4096]{1,0:T(8,128)(2,1)S(1)} collective-permute-done((bf16[16,4096]{1,0:T(8,128)(2,1)}, bf16[16,4096]{1,0:T(8,128)(2,1)S(1)}, u32[]{:S(2)}, u32[]{:S(2)}) %collective-permute-start) | collective-permute-done | bytes 131104 | tf_op jit(solution)/shard_map/ppermute | solution.py:159
  11.6 0.6 %collective-permute-done.2.refs_1_ = bf16[16,4096]{1,0:T(8,128)(2,1)S(1)} collective-permute-done((bf16[16,4096]{1,0:T(8,128)(2,1)S(1)}, bf16[16,4096]{1,0:T(8,128)(2,1)S(1)}, u32[]{:S(2)}, u32[]{:S(2)}) %collective-permute-start.2) | collective-permute-done | bytes 131104 | tf_op jit(solution)/shard_map/ppermute | solution.py:160
  12.2 2.5 %ffn.1 = (f32[16,4096]{1,0:T(8,128)S(1)}, bf16[16,4096]{1,0:T(8,128)(2,1)S(1)}, bf16[32,384]{1,0:T(8,128)(2,1)S(1)}) custom-call(bf16[16,4096]{1,0:T(8,128)(2,1)S(1)} %fetch.1.own, bf16[16,4096]{1,0:T(8,128)(2,1)S(1)} %collective-permute-done.next_block, bf16[64,64]{1,0:T(8,128)(2,1)S(1)} %order.1, bf16[16,4096]{1,0:T(8,128)(2,1)S(1)} %collective-permute-done.1.refs_0_, ...), custom_call_target="tpu_custom_call" | custom-call | tf_op jit(solution)/shard_map/ffn/pallas_call | solution.py:167
  14.7 0.0 copy-start.4
  14.7 0.2 collective-permute-start.6
  14.9 0.6 %down.1 = (f32[16,4096]{1,0:T(8,128)S(1)}, bf16[16,4096]{1,0:T(8,128)(2,1)S(1)}) custom-call(bf16[32,384]{1,0:T(8,128)(2,1)S(1)} %get-tuple-element.18.hidden, bf16[1,384,4096]{2,1,0:T(8,128)(2,1)S(1)} %copy-done), custom_call_target="tpu_custom_call" | custom-call | tf_op jit(solution)/shard_map/down/pallas_call | solution.py:176
  15.6 0.4 %collective-permute-start.3 = (bf16[16,4096]{1,0:T(8,128)(2,1)S(1)}, bf16[16,4096]{1,0:T(8,128)(2,1)S(1)}, u32[]{:S(2)}, u32[]{:S(2)}) collective-permute-start(bf16[16,4096]{1,0:T(8,128)(2,1)S(1)} %get-tuple-element.20), channel_id=1, source_target_pairs={{0,1},{1,0},{2,3},{3,2},{4,5},{5,4},{6,7},{7,6},{8,9},{9,8},{10,11... | collective-permute-start | bytes 393224 | tf_op jit(solution)/shard_map/ppermute | solution.py:188
  16.0 0.2 collective-permute-done.6.arrived
  16.2 1.6 %collective-permute-start.7 = (bf16[8,4096]{1,0:T(8,128)(2,1)S(1)}, bf16[8,4096]{1,0:T(8,128)(2,1)S(1)}, u32[]{:S(2)}, u32[]{:S(2)}) collective-permute-start(bf16[8,4096]{1,0:T(8,128)(2,1)S(1)} %get-tuple-element.28), channel_id=1, source_target_pairs={{0,2},{1,3},{2,0},{3,1},{4,6},{5,7},{6,4},{7,5},{8,10},{9,11},{10,... | collective-permute-start | bytes 196616 | tf_op jit(solution)/shard_map/ppermute | solution.py:201
  17.8 0.8 %collective-permute-start.4 = (bf16[8,4096]{1,0:T(8,128)(2,1)S(1)}, bf16[8,4096]{1,0:T(8,128)(2,1)S(1)}, u32[]{:S(2)}, u32[]{:S(2)}) collective-permute-start(bf16[8,4096]{1,0:T(8,128)(2,1)S(1)} %get-tuple-element.22), channel_id=1, source_target_pairs={{0,2},{1,3},{2,0},{3,1},{4,6},{5,7},{6,4},{7,5},{8,10},{9,11},{10,... | collective-permute-start | bytes 196616 | tf_op jit(solution)/shard_map/ppermute | solution.py:201
  18.6 2.2 %collective-permute-done.7.refs_0_ = bf16[8,4096]{1,0:T(8,128)(2,1)S(1)} collective-permute-done((bf16[8,4096]{1,0:T(8,128)(2,1)S(1)}, bf16[8,4096]{1,0:T(8,128)(2,1)S(1)}, u32[]{:S(2)}, u32[]{:S(2)}) %collective-permute-start.7) | collective-permute-done | bytes 65568 | tf_op jit(solution)/shard_map/ppermute | solution.py:201
  20.8 0.8 %collective-permute-start.8 = (bf16[4,4096]{1,0:T(4,128)(2,1)S(1)}, bf16[4,4096]{1,0:T(4,128)(2,1)S(1)}, u32[]{:S(2)}, u32[]{:S(2)}) collective-permute-start(bf16[4,4096]{1,0:T(4,128)(2,1)S(1)} %get-tuple-element.29), channel_id=1, source_target_pairs={{0,8},{4,12},{8,0},{12,4},{1,9},{5,13},{9,1},{13,5},{2,10},{6,14},... | collective-permute-start | bytes 98312 | tf_op jit(solution)/shard_map/ppermute | solution.py:213
  21.6 2.8 %collective-permute-start.9 = (bf16[4,4096]{1,0:T(4,128)(2,1)S(1)}, bf16[4,4096]{1,0:T(4,128)(2,1)S(1)}, u32[]{:S(2)}, u32[]{:S(2)}) collective-permute-start(bf16[4,4096]{1,0:T(4,128)(2,1)S(1)} %get-tuple-element.30), channel_id=1, source_target_pairs={{0,12},{4,8},{8,4},{12,0},{1,13},{5,9},{9,5},{13,1},{2,14},{6,10},... | collective-permute-start | bytes 98312 | tf_op jit(solution)/shard_map/ppermute | solution.py:213
  24.4 0.1 collective-permute-start.5
  24.5 1.3 %collective-permute-done.8.refs_2_ = bf16[4,4096]{1,0:T(4,128)(2,1)S(1)} collective-permute-done((bf16[4,4096]{1,0:T(4,128)(2,1)S(1)}, bf16[4,4096]{1,0:T(4,128)(2,1)S(1)}, u32[]{:S(2)}, u32[]{:S(2)}) %collective-permute-start.8) | collective-permute-done | bytes 32800 | tf_op jit(solution)/shard_map/ppermute | solution.py:213
  25.8 1.5 %collective-permute-done.9.refs_3_ = bf16[4,4096]{1,0:T(4,128)(2,1)S(1)} collective-permute-done((bf16[4,4096]{1,0:T(4,128)(2,1)S(1)}, bf16[4,4096]{1,0:T(4,128)(2,1)S(1)}, u32[]{:S(2)}, u32[]{:S(2)}) %collective-permute-start.9) | collective-permute-done | bytes 32800 | tf_op jit(solution)/shard_map/ppermute | solution.py:213
  27.3 1.1 %collective-permute-done.5.refs_1_ = bf16[4,4096]{1,0:T(4,128)(2,1)S(1)} collective-permute-done((bf16[4,4096]{1,0:T(4,128)(2,1)S(1)}, bf16[4,4096]{1,0:T(4,128)(2,1)S(1)}, u32[]{:S(2)}, u32[]{:S(2)}) %collective-permute-start.5) | collective-permute-done | bytes 32800 | tf_op jit(solution)/shard_map/ppermute | solution.py:213
  28.4 0.7 %mix.1 = bf16[4,4096]{1,0:T(4,128)(2,1)} custom-call(s32[2,16]{1,0:T(2,128)S(1)} %bitcast.2, f32[2,4]{1,0:T(2,128)S(1)} %bitcast.3, bf16[4,4096]{1,0:T(4,128)(2,1)S(1)} %get-tuple-element.23.refs_0_, bf16[4,4096]{1,0:T(4,128)(2,1)S(1)} %collective-permute-done.5.refs_1_, bf16[4,4096]{1,0:T(4,128)(2,1)S(1)} %collective-permute-done.8.refs_2_, ...), custom_call_target="tpu_custom_call" | custom-call | tf_op jit(solution)/shard_map/mix/pallas_call | solution.py:216
  (15 shorter events, 0.2 us)
Async XLA Ops:
  0.0 10.8 %collective-permute-start.1 = (bf16[16,4096]{1,0:T(8,128)(2,1)}, bf16[16,4096]{1,0:T(8,128)(2,1)S(1)}, u32[]{:S(2)}, u32[]{:S(2)}) collective-permute-start(bf16[16,4096]{1,0:T(8,128)(2,1)} %tokens.1), channel_id=1, source_target_pairs={{0,8},{1,13},{2,10},{3,15},{4,12},{5,9},{6,14},{7,11},{8,0},{9,5},... | collective-permute-start | bytes 393224 | tf_op jit(solution)/shard_map/ppermute | solution.py:158
  4.0 7.6 %collective-permute-start = (bf16[16,4096]{1,0:T(8,128)(2,1)}, bf16[16,4096]{1,0:T(8,128)(2,1)S(1)}, u32[]{:S(2)}, u32[]{:S(2)}) collective-permute-start(bf16[16,4096]{1,0:T(8,128)(2,1)} %tokens.1), channel_id=1, source_target_pairs={{0,4},{4,0},{8,12},{12,8},{1,5},{5,1},{9,13},{13,9},{2,6},{6,2},{1... | collective-permute-start | bytes 393224 | tf_op jit(solution)/shard_map/ppermute | solution.py:159
  6.6 5.6 %copy-start = (bf16[1,384,4096]{2,1,0:T(8,128)(2,1)S(1)}, bf16[1,384,4096]{2,1,0:T(8,128)(2,1)}, u32[]{:S(2)}) copy-start(bf16[1,384,4096]{2,1,0:T(8,128)(2,1)} %w_down.1) | copy-start | bytes 9437188
  6.6 5.6 %copy-start.1 = (bf16[1,384,4096]{2,1,0:T(8,128)(2,1)S(1)}, bf16[1,384,4096]{2,1,0:T(8,128)(2,1)}, u32[]{:S(2)}) copy-start(bf16[1,384,4096]{2,1,0:T(8,128)(2,1)} %refs_2_.1) | copy-start | bytes 9437188
  6.6 5.6 %copy-start.2 = (bf16[1,384,4096]{2,1,0:T(8,128)(2,1)S(1)}, bf16[1,384,4096]{2,1,0:T(8,128)(2,1)}, u32[]{:S(2)}) copy-start(bf16[1,384,4096]{2,1,0:T(8,128)(2,1)} %refs_3_.1) | copy-start | bytes 9437188
  10.8 1.3 %collective-permute-start.2 = (bf16[16,4096]{1,0:T(8,128)(2,1)S(1)}, bf16[16,4096]{1,0:T(8,128)(2,1)S(1)}, u32[]{:S(2)}, u32[]{:S(2)}) collective-permute-start(bf16[16,4096]{1,0:T(8,128)(2,1)S(1)} %collective-permute-done.1.refs_0_), channel_id=1, source_target_pairs={{0,1},{1,0},{2,3},{3,2},{4,5},{5,4},{6,7},{7,6},{8,9},{9,8},{10,11... | collective-permute-start | bytes 393224 | tf_op jit(solution)/shard_map/ppermute | solution.py:160
  14.7 13.7 %copy-start.3 = (s32[16,2]{0,1:T(2,128)S(1)}, s32[16,2]{0,1:T(2,128)}, u32[]{:S(2)}) copy-start(s32[16,2]{0,1:T(2,128)} %param.7) | copy-start | bytes 388
  14.7 13.7 %copy-start.4 = (f32[4,2]{0,1:T(2,128)S(1)}, f32[4,2]{0,1:T(2,128)}, u32[]{:S(2)}) copy-start(f32[4,2]{0,1:T(2,128)} %param.8) | copy-start | bytes 100
  14.7 1.4 %collective-permute-start.6 = (bf16[16,4096]{1,0:T(8,128)(2,1)S(1)}, bf16[16,4096]{1,0:T(8,128)(2,1)S(1)}, u32[]{:S(2)}, u32[]{:S(2)}) collective-permute-start(bf16[16,4096]{1,0:T(8,128)(2,1)S(1)} %get-tuple-element.26), channel_id=1, source_target_pairs={{0,1},{1,0},{2,3},{3,2},{4,5},{5,4},{6,7},{7,6},{8,9},{9,8},{10,11... | collective-permute-start | bytes 393224 | tf_op jit(solution)/shard_map/ppermute | solution.py:188
  15.6 2.1 %collective-permute-start.3 = (bf16[16,4096]{1,0:T(8,128)(2,1)S(1)}, bf16[16,4096]{1,0:T(8,128)(2,1)S(1)}, u32[]{:S(2)}, u32[]{:S(2)}) collective-permute-start(bf16[16,4096]{1,0:T(8,128)(2,1)S(1)} %get-tuple-element.20), channel_id=1, source_target_pairs={{0,1},{1,0},{2,3},{3,2},{4,5},{5,4},{6,7},{7,6},{8,9},{9,8},{10,11... | collective-permute-start | bytes 393224 | tf_op jit(solution)/shard_map/ppermute | solution.py:188
  16.2 4.6 %collective-permute-start.7 = (bf16[8,4096]{1,0:T(8,128)(2,1)S(1)}, bf16[8,4096]{1,0:T(8,128)(2,1)S(1)}, u32[]{:S(2)}, u32[]{:S(2)}) collective-permute-start(bf16[8,4096]{1,0:T(8,128)(2,1)S(1)} %get-tuple-element.28), channel_id=1, source_target_pairs={{0,2},{1,3},{2,0},{3,1},{4,6},{5,7},{6,4},{7,5},{8,10},{9,11},{10,... | collective-permute-start | bytes 196616 | tf_op jit(solution)/shard_map/ppermute | solution.py:201
  17.8 6.6 %collective-permute-start.4 = (bf16[8,4096]{1,0:T(8,128)(2,1)S(1)}, bf16[8,4096]{1,0:T(8,128)(2,1)S(1)}, u32[]{:S(2)}, u32[]{:S(2)}) collective-permute-start(bf16[8,4096]{1,0:T(8,128)(2,1)S(1)} %get-tuple-element.22), channel_id=1, source_target_pairs={{0,2},{1,3},{2,0},{3,1},{4,6},{5,7},{6,4},{7,5},{8,10},{9,11},{10,... | collective-permute-start | bytes 196616 | tf_op jit(solution)/shard_map/ppermute | solution.py:201
  20.8 5.0 %collective-permute-start.8 = (bf16[4,4096]{1,0:T(4,128)(2,1)S(1)}, bf16[4,4096]{1,0:T(4,128)(2,1)S(1)}, u32[]{:S(2)}, u32[]{:S(2)}) collective-permute-start(bf16[4,4096]{1,0:T(4,128)(2,1)S(1)} %get-tuple-element.29), channel_id=1, source_target_pairs={{0,8},{4,12},{8,0},{12,4},{1,9},{5,13},{9,1},{13,5},{2,10},{6,14},... | collective-permute-start | bytes 98312 | tf_op jit(solution)/shard_map/ppermute | solution.py:213
  21.6 5.7 %collective-permute-start.9 = (bf16[4,4096]{1,0:T(4,128)(2,1)S(1)}, bf16[4,4096]{1,0:T(4,128)(2,1)S(1)}, u32[]{:S(2)}, u32[]{:S(2)}) collective-permute-start(bf16[4,4096]{1,0:T(4,128)(2,1)S(1)} %get-tuple-element.30), channel_id=1, source_target_pairs={{0,12},{4,8},{8,4},{12,0},{1,13},{5,9},{9,5},{13,1},{2,14},{6,10},... | collective-permute-start | bytes 98312 | tf_op jit(solution)/shard_map/ppermute | solution.py:213
  24.4 4.0 %collective-permute-start.5 = (bf16[4,4096]{1,0:T(4,128)(2,1)S(1)}, bf16[4,4096]{1,0:T(4,128)(2,1)S(1)}, u32[]{:S(2)}, u32[]{:S(2)}) collective-permute-start(bf16[4,4096]{1,0:T(4,128)(2,1)S(1)} %get-tuple-element.24), channel_id=1, source_target_pairs={{0,4},{4,0},{8,12},{12,8},{1,5},{5,1},{9,13},{13,9},{2,6},{6,2},{1... | collective-permute-start | bytes 98312 | tf_op jit(solution)/shard_map/ppermute | solution.py:213

commit v18 on v16

--- a/solution.py
+++ b/solution.py
@@ -31,7 +31,10 @@
     k = lax.rem(lax.div(place, rows), half)
     h = lax.rem(lax.div(place, rows * half), pairs)
     sent = lax.rem(lax.div(place, rows * half * pairs), 2)
-    k = k + half * (1 - lax.div(place, rows * half * pairs * 2))
+    second = lax.div(place, rows * half * pairs * 2)
+    shift = jnp.where(second == 0, k + 1, jnp.where(k == 0, 0, k + half))
+    expert = lax.axis_index("expert")
+    k = lax.bitwise_xor(expert, lax.rem(expert + shift, n_expert))
     block = 2 * lax.rem(pair + h, pairs) + lax.rem(core + sent, 2)
     wanted = (k * pairs * 2 + block) * rows + row
     out[...] = jnp.where(source == wanted, 1.0, 0.0).astype(jnp.bfloat16)
@@ -107,7 +110,7 @@
     scale = sum(own_weights)
     total = None
     for k in range(n_expert):
-        owner = lax.bitwise_xor(expert, k)
+        owner = lax.rem(expert - k + n_expert, n_expert)
         factor = sum(jnp.where(own_ids[i] == owner, own_weights[i], 0.0) for i in range(top)) / scale
         term = pieces[k][...].astype(jnp.float32) * factor
         total = term if total is None else total + term
@@ -199,11 +202,13 @@
             compiler_params=GRANT,
             name="fold",
         )(own, *landed)
-        pieces = list(folded) + pieces
-    landed = []
-    for k in range(n_expert - 1, 0, -1):
-        landed.insert(0, lax.ppermute(pieces[k], "expert", [(e, e ^ k) for e in range(n_expert)]))
-    landed.insert(0, pieces[0])
+        pieces.append(list(folded))
+    half = n_expert // 2
+    pieces = pieces[1][:1] + pieces[0] + pieces[1][1:]
+    landed = pieces[:1]
+    for k in range(1, n_expert):
+        route = [(e, (e + k) % n_expert) for e in range(n_expert)]
+        landed.append(lax.ppermute(pieces[k], "expert", route))
 
     return pl.pallas_call(
         functools.partial(mix_kernel, n_expert),

time: 29.3 us -> 29.2 us (level)
  waiting for transfers between devices: 11.8 us -> 11.1 us
  starting transfers between devices: 12.2 us -> 12.8 us
    ppermute x3, waiting for transfers between devices: 3.9 us -> 3.22 us  [on_device(): landed.append(lax.ppermute(pieces[k], 'expert', route))]
    ppermute x3, starting transfers between devices: 3.68 us -> 4.23 us  [on_device(): landed.append(lax.ppermute(pieces[k], 'expert', route))]
where the time goes in v18:
time: 29.2 us; the launch traced here: 29 us
  starting transfers between devices  12.8 us (44%)
  waiting for transfers between devices  11.1 us (38%)
  Pallas kernels  5.01 us (17%)
    ppermute x3, starting transfers between devices, on_device(): landed.append(lax.ppermute(pieces[k], 'expert', route))  4.23 us
    ppermute x1, waiting for transfers between devices, on_device(): far.append(lax.ppermute(tokens, ('expert', 'etp'), route))  4.22 us
    ppermute x1, starting transfers between devices, on_device(): far.append(lax.ppermute(tokens, ('expert', 'etp'), route))  4.04 us
    ppermute x3, waiting for transfers between devices, on_device(): landed.append(lax.ppermute(pieces[k], 'expert', route))  3.22 us
    pallas_call x1, Pallas kernels, on_device(): pl.pallas_call(functools.partial(ffn_kernel, n_expert, parts), out_shape=...  2.53 us
    ppermute x2, starting transfers between devices, on_device(): landed.append(lax.ppermute(piece, 'etp', route))  2.35 us
    ppermute x2, waiting for transfers between devices, on_device(): landed.append(lax.ppermute(piece, 'etp', route))  2.21 us
    ppermute x1, starting transfers between devices, on_device(): lax.ppermute(tokens, 'expert', [(e, e ^ 1) for e in range(n_expert)])  1.58 us
  transfers between devices with their start and end apart: 10, of which 8 were waited for; matrix products, arithmetic and copies ran while one was open for 0% of the time, Pallas kernels for 6%

profile of v18, /device:TPU:0, one launch (start us, length us, event | category | flops | bytes accessed | tf_op | source)
XLA Modules:
  0.0 29.0 jit_solution(7553043508053479851)
XLA Ops:
  0.0 4.0 %collective-permute-start.1 = (bf16[16,4096]{1,0:T(8,128)(2,1)}, bf16[16,4096]{1,0:T(8,128)(2,1)S(1)}, u32[]{:S(2)}, u32[]{:S(2)}) collective-permute-start(bf16[16,4096]{1,0:T(8,128)(2,1)} %tokens.1), channel_id=1, source_target_pairs={{0,8},{1,13},{2,10},{3,15},{4,12},{5,9},{6,14},{7,11},{8,0},{9,5},... | collective-permute-start | bytes 393224 | tf_op jit(solution)/shard_map/ppermute | solution.py:153
  4.0 1.6 %collective-permute-start = (bf16[16,4096]{1,0:T(8,128)(2,1)}, bf16[16,4096]{1,0:T(8,128)(2,1)S(1)}, u32[]{:S(2)}, u32[]{:S(2)}) collective-permute-start(bf16[16,4096]{1,0:T(8,128)(2,1)} %tokens.1), channel_id=1, source_target_pairs={{0,4},{4,0},{8,12},{12,8},{1,5},{5,1},{9,13},{13,9},{2,6},{6,2},{1... | collective-permute-start | bytes 393224 | tf_op jit(solution)/shard_map/ppermute | solution.py:154
  5.6 0.9 %fetch.1.own = bf16[16,4096]{1,0:T(8,128)(2,1)S(1)} custom-call(bf16[16,4096]{1,0:T(8,128)(2,1)} %tokens.1), custom_call_target="tpu_custom_call" | custom-call | tf_op jit(solution)/shard_map/fetch/pallas_call | solution.py:126
  6.6 0.0 copy-start
  6.6 4.2 %collective-permute-done.1.refs_0_ = bf16[16,4096]{1,0:T(8,128)(2,1)S(1)} collective-permute-done((bf16[16,4096]{1,0:T(8,128)(2,1)}, bf16[16,4096]{1,0:T(8,128)(2,1)S(1)}, u32[]{:S(2)}, u32[]{:S(2)}) %collective-permute-start.1) | collective-permute-done | bytes 131104 | tf_op jit(solution)/shard_map/ppermute | solution.py:153
  10.8 0.1 order.1
  10.9 0.7 %collective-permute-done.next_block = bf16[16,4096]{1,0:T(8,128)(2,1)S(1)} collective-permute-done((bf16[16,4096]{1,0:T(8,128)(2,1)}, bf16[16,4096]{1,0:T(8,128)(2,1)S(1)}, u32[]{:S(2)}, u32[]{:S(2)}) %collective-permute-start) | collective-permute-done | bytes 131104 | tf_op jit(solution)/shard_map/ppermute | solution.py:154
  11.6 0.6 %collective-permute-done.2.refs_1_ = bf16[16,4096]{1,0:T(8,128)(2,1)S(1)} collective-permute-done((bf16[16,4096]{1,0:T(8,128)(2,1)S(1)}, bf16[16,4096]{1,0:T(8,128)(2,1)S(1)}, u32[]{:S(2)}, u32[]{:S(2)}) %collective-permute-start.2) | collective-permute-done | bytes 131104 | tf_op jit(solution)/shard_map/ppermute | solution.py:155
  12.2 2.5 %ffn.1 = (f32[16,4096]{1,0:T(8,128)S(1)}, bf16[16,4096]{1,0:T(8,128)(2,1)S(1)}, bf16[32,384]{1,0:T(8,128)(2,1)S(1)}) custom-call(bf16[16,4096]{1,0:T(8,128)(2,1)S(1)} %fetch.1.own, bf16[16,4096]{1,0:T(8,128)(2,1)S(1)} %collective-permute-done.next_block, bf16[64,64]{1,0:T(8,128)(2,1)S(1)} %order.1, bf16[16,4096]{1,0:T(8,128)(2,1)S(1)} %collective-permute-done.1.refs_0_, ...), custom_call_target="tpu_custom_call" | custom-call | tf_op jit(solution)/shard_map/ffn/pallas_call | solution.py:162
  14.7 0.0 copy-start.4
  14.7 0.2 collective-permute-start.5
  14.9 0.6 %down.1 = (f32[16,4096]{1,0:T(8,128)S(1)}, bf16[16,4096]{1,0:T(8,128)(2,1)S(1)}) custom-call(bf16[32,384]{1,0:T(8,128)(2,1)S(1)} %get-tuple-element.18.hidden, bf16[1,384,4096]{2,1,0:T(8,128)(2,1)S(1)} %copy-done), custom_call_target="tpu_custom_call" | custom-call | tf_op jit(solution)/shard_map/down/pallas_call | solution.py:171
  15.6 0.4 %collective-permute-start.3 = (bf16[16,4096]{1,0:T(8,128)(2,1)S(1)}, bf16[16,4096]{1,0:T(8,128)(2,1)S(1)}, u32[]{:S(2)}, u32[]{:S(2)}) collective-permute-start(bf16[16,4096]{1,0:T(8,128)(2,1)S(1)} %get-tuple-element.20), channel_id=1, source_target_pairs={{0,1},{1,0},{2,3},{3,2},{4,5},{5,4},{6,7},{7,6},{8,9},{9,8},{10,11... | collective-permute-start | bytes 393224 | tf_op jit(solution)/shard_map/ppermute | solution.py:183
  16.0 0.2 collective-permute-done.5.arrived
  16.2 1.6 %collective-permute-start.6 = (bf16[8,4096]{1,0:T(8,128)(2,1)S(1)}, bf16[8,4096]{1,0:T(8,128)(2,1)S(1)}, u32[]{:S(2)}, u32[]{:S(2)}) collective-permute-start(bf16[8,4096]{1,0:T(8,128)(2,1)S(1)} %get-tuple-element.27), channel_id=1, source_target_pairs={{0,2},{1,3},{2,0},{3,1},{4,6},{5,7},{6,4},{7,5},{8,10},{9,11},{10,... | collective-permute-start | bytes 196616 | tf_op jit(solution)/shard_map/ppermute | solution.py:196
  17.8 0.8 %collective-permute-start.4 = (bf16[8,4096]{1,0:T(8,128)(2,1)S(1)}, bf16[8,4096]{1,0:T(8,128)(2,1)S(1)}, u32[]{:S(2)}, u32[]{:S(2)}) collective-permute-start(bf16[8,4096]{1,0:T(8,128)(2,1)S(1)} %get-tuple-element.22), channel_id=1, source_target_pairs={{0,2},{1,3},{2,0},{3,1},{4,6},{5,7},{6,4},{7,5},{8,10},{9,11},{10,... | collective-permute-start | bytes 196616 | tf_op jit(solution)/shard_map/ppermute | solution.py:196
  18.6 2.2 %collective-permute-done.6.refs_0_ = bf16[8,4096]{1,0:T(8,128)(2,1)S(1)} collective-permute-done((bf16[8,4096]{1,0:T(8,128)(2,1)S(1)}, bf16[8,4096]{1,0:T(8,128)(2,1)S(1)}, u32[]{:S(2)}, u32[]{:S(2)}) %collective-permute-start.6) | collective-permute-done | bytes 65568 | tf_op jit(solution)/shard_map/ppermute | solution.py:196
  20.8 1.2 %collective-permute-start.7 = (bf16[4,4096]{1,0:T(4,128)(2,1)S(1)}, bf16[4,4096]{1,0:T(4,128)(2,1)S(1)}, u32[]{:S(2)}, u32[]{:S(2)}) collective-permute-start(bf16[4,4096]{1,0:T(4,128)(2,1)S(1)} %get-tuple-element.28), channel_id=1, source_target_pairs={{0,4},{4,8},{8,12},{12,0},{1,5},{5,9},{9,13},{13,1},{2,6},{6,10},{... | collective-permute-start | bytes 98312 | tf_op jit(solution)/shard_map/ppermute | solution.py:211
  22.0 2.3 %collective-permute-start.8 = (bf16[4,4096]{1,0:T(4,128)(2,1)S(1)}, bf16[4,4096]{1,0:T(4,128)(2,1)S(1)}, u32[]{:S(2)}, u32[]{:S(2)}) collective-permute-start(bf16[4,4096]{1,0:T(4,128)(2,1)S(1)} %get-tuple-element.29), channel_id=1, source_target_pairs={{0,8},{4,12},{8,0},{12,4},{1,9},{5,13},{9,1},{13,5},{2,10},{6,14},... | collective-permute-start | bytes 98312 | tf_op jit(solution)/shard_map/ppermute | solution.py:211
  24.3 0.7 %collective-permute-start.9 = (bf16[4,4096]{1,0:T(4,128)(2,1)S(1)}, bf16[4,4096]{1,0:T(4,128)(2,1)S(1)}, u32[]{:S(2)}, u32[]{:S(2)}) collective-permute-start(bf16[4,4096]{1,0:T(4,128)(2,1)S(1)} %get-tuple-element.30), channel_id=1, source_target_pairs={{0,12},{4,0},{8,4},{12,8},{1,13},{5,1},{9,5},{13,9},{2,14},{6,2},{... | collective-permute-start | bytes 98312 | tf_op jit(solution)/shard_map/ppermute | solution.py:211
  25.0 1.5 %collective-permute-done.7.refs_1_ = bf16[4,4096]{1,0:T(4,128)(2,1)S(1)} collective-permute-done((bf16[4,4096]{1,0:T(4,128)(2,1)S(1)}, bf16[4,4096]{1,0:T(4,128)(2,1)S(1)}, u32[]{:S(2)}, u32[]{:S(2)}) %collective-permute-start.7) | collective-permute-done | bytes 32800 | tf_op jit(solution)/shard_map/ppermute | solution.py:211
  26.6 0.7 %collective-permute-done.8.refs_2_ = bf16[4,4096]{1,0:T(4,128)(2,1)S(1)} collective-permute-done((bf16[4,4096]{1,0:T(4,128)(2,1)S(1)}, bf16[4,4096]{1,0:T(4,128)(2,1)S(1)}, u32[]{:S(2)}, u32[]{:S(2)}) %collective-permute-start.8) | collective-permute-done | bytes 32800 | tf_op jit(solution)/shard_map/ppermute | solution.py:211
  27.3 1.0 %collective-permute-done.9.refs_3_ = bf16[4,4096]{1,0:T(4,128)(2,1)S(1)} collective-permute-done((bf16[4,4096]{1,0:T(4,128)(2,1)S(1)}, bf16[4,4096]{1,0:T(4,128)(2,1)S(1)}, u32[]{:S(2)}, u32[]{:S(2)}) %collective-permute-start.9) | collective-permute-done | bytes 32800 | tf_op jit(solution)/shard_map/ppermute | solution.py:211
  28.3 0.7 %mix.1 = bf16[4,4096]{1,0:T(4,128)(2,1)} custom-call(s32[2,16]{1,0:T(2,128)S(1)} %bitcast.2, f32[2,4]{1,0:T(2,128)S(1)} %bitcast.3, bf16[4,4096]{1,0:T(4,128)(2,1)S(1)} %get-tuple-element.23.refs_0_, bf16[4,4096]{1,0:T(4,128)(2,1)S(1)} %collective-permute-done.7.refs_1_, bf16[4,4096]{1,0:T(4,128)(2,1)S(1)} %collective-permute-done.8.refs_2_, ...), custom_call_target="tpu_custom_call" | custom-call | tf_op jit(solution)/shard_map/mix/pallas_call | solution.py:213
  (15 shorter events, 0.1 us)
Async XLA Ops:
  0.0 10.8 %collective-permute-start.1 = (bf16[16,4096]{1,0:T(8,128)(2,1)}, bf16[16,4096]{1,0:T(8,128)(2,1)S(1)}, u32[]{:S(2)}, u32[]{:S(2)}) collective-permute-start(bf16[16,4096]{1,0:T(8,128)(2,1)} %tokens.1), channel_id=1, source_target_pairs={{0,8},{1,13},{2,10},{3,15},{4,12},{5,9},{6,14},{7,11},{8,0},{9,5},... | collective-permute-start | bytes 393224 | tf_op jit(solution)/shard_map/ppermute | solution.py:153
  4.0 7.6 %collective-permute-start = (bf16[16,4096]{1,0:T(8,128)(2,1)}, bf16[16,4096]{1,0:T(8,128)(2,1)S(1)}, u32[]{:S(2)}, u32[]{:S(2)}) collective-permute-start(bf16[16,4096]{1,0:T(8,128)(2,1)} %tokens.1), channel_id=1, source_target_pairs={{0,4},{4,0},{8,12},{12,8},{1,5},{5,1},{9,13},{13,9},{2,6},{6,2},{1... | collective-permute-start | bytes 393224 | tf_op jit(solution)/shard_map/ppermute | solution.py:154
  6.6 5.6 %copy-start = (bf16[1,384,4096]{2,1,0:T(8,128)(2,1)S(1)}, bf16[1,384,4096]{2,1,0:T(8,128)(2,1)}, u32[]{:S(2)}) copy-start(bf16[1,384,4096]{2,1,0:T(8,128)(2,1)} %w_down.1) | copy-start | bytes 9437188
  6.6 5.6 %copy-start.1 = (bf16[1,384,4096]{2,1,0:T(8,128)(2,1)S(1)}, bf16[1,384,4096]{2,1,0:T(8,128)(2,1)}, u32[]{:S(2)}) copy-start(bf16[1,384,4096]{2,1,0:T(8,128)(2,1)} %refs_2_.1) | copy-start | bytes 9437188
  6.6 5.6 %copy-start.2 = (bf16[1,384,4096]{2,1,0:T(8,128)(2,1)S(1)}, bf16[1,384,4096]{2,1,0:T(8,128)(2,1)}, u32[]{:S(2)}) copy-start(bf16[1,384,4096]{2,1,0:T(8,128)(2,1)} %refs_3_.1) | copy-start | bytes 9437188
  10.8 1.3 %collective-permute-start.2 = (bf16[16,4096]{1,0:T(8,128)(2,1)S(1)}, bf16[16,4096]{1,0:T(8,128)(2,1)S(1)}, u32[]{:S(2)}, u32[]{:S(2)}) collective-permute-start(bf16[16,4096]{1,0:T(8,128)(2,1)S(1)} %collective-permute-done.1.refs_0_), channel_id=1, source_target_pairs={{0,1},{1,0},{2,3},{3,2},{4,5},{5,4},{6,7},{7,6},{8,9},{9,8},{10,11... | collective-permute-start | bytes 393224 | tf_op jit(solution)/shard_map/ppermute | solution.py:155
  14.7 13.6 %copy-start.3 = (s32[16,2]{0,1:T(2,128)S(1)}, s32[16,2]{0,1:T(2,128)}, u32[]{:S(2)}) copy-start(s32[16,2]{0,1:T(2,128)} %param.7) | copy-start | bytes 388
  14.7 13.6 %copy-start.4 = (f32[4,2]{0,1:T(2,128)S(1)}, f32[4,2]{0,1:T(2,128)}, u32[]{:S(2)}) copy-start(f32[4,2]{0,1:T(2,128)} %param.8) | copy-start | bytes 100
  14.7 1.4 %collective-permute-start.5 = (bf16[16,4096]{1,0:T(8,128)(2,1)S(1)}, bf16[16,4096]{1,0:T(8,128)(2,1)S(1)}, u32[]{:S(2)}, u32[]{:S(2)}) collective-permute-start(bf16[16,4096]{1,0:T(8,128)(2,1)S(1)} %get-tuple-element.25), channel_id=1, source_target_pairs={{0,1},{1,0},{2,3},{3,2},{4,5},{5,4},{6,7},{7,6},{8,9},{9,8},{10,11... | collective-permute-start | bytes 393224 | tf_op jit(solution)/shard_map/ppermute | solution.py:183
  15.6 2.1 %collective-permute-start.3 = (bf16[16,4096]{1,0:T(8,128)(2,1)S(1)}, bf16[16,4096]{1,0:T(8,128)(2,1)S(1)}, u32[]{:S(2)}, u32[]{:S(2)}) collective-permute-start(bf16[16,4096]{1,0:T(8,128)(2,1)S(1)} %get-tuple-element.20), channel_id=1, source_target_pairs={{0,1},{1,0},{2,3},{3,2},{4,5},{5,4},{6,7},{7,6},{8,9},{9,8},{10,11... | collective-permute-start | bytes 393224 | tf_op jit(solution)/shard_map/ppermute | solution.py:183
  16.2 4.6 %collective-permute-start.6 = (bf16[8,4096]{1,0:T(8,128)(2,1)S(1)}, bf16[8,4096]{1,0:T(8,128)(2,1)S(1)}, u32[]{:S(2)}, u32[]{:S(2)}) collective-permute-start(bf16[8,4096]{1,0:T(8,128)(2,1)S(1)} %get-tuple-element.27), channel_id=1, source_target_pairs={{0,2},{1,3},{2,0},{3,1},{4,6},{5,7},{6,4},{7,5},{8,10},{9,11},{10,... | collective-permute-start | bytes 196616 | tf_op jit(solution)/shard_map/ppermute | solution.py:196
  17.8 6.5 %collective-permute-start.4 = (bf16[8,4096]{1,0:T(8,128)(2,1)S(1)}, bf16[8,4096]{1,0:T(8,128)(2,1)S(1)}, u32[]{:S(2)}, u32[]{:S(2)}) collective-permute-start(bf16[8,4096]{1,0:T(8,128)(2,1)S(1)} %get-tuple-element.22), channel_id=1, source_target_pairs={{0,2},{1,3},{2,0},{3,1},{4,6},{5,7},{6,4},{7,5},{8,10},{9,11},{10,... | collective-permute-start | bytes 196616 | tf_op jit(solution)/shard_map/ppermute | solution.py:196
  20.8 5.8 %collective-permute-start.7 = (bf16[4,4096]{1,0:T(4,128)(2,1)S(1)}, bf16[4,4096]{1,0:T(4,128)(2,1)S(1)}, u32[]{:S(2)}, u32[]{:S(2)}) collective-permute-start(bf16[4,4096]{1,0:T(4,128)(2,1)S(1)} %get-tuple-element.28), channel_id=1, source_target_pairs={{0,4},{4,8},{8,12},{12,0},{1,5},{5,9},{9,13},{13,1},{2,6},{6,10},{... | collective-permute-start | bytes 98312 | tf_op jit(solution)/shard_map/ppermute | solution.py:211
  22.0 5.2 %collective-permute-start.8 = (bf16[4,4096]{1,0:T(4,128)(2,1)S(1)}, bf16[4,4096]{1,0:T(4,128)(2,1)S(1)}, u32[]{:S(2)}, u32[]{:S(2)}) collective-permute-start(bf16[4,4096]{1,0:T(4,128)(2,1)S(1)} %get-tuple-element.29), channel_id=1, source_target_pairs={{0,8},{4,12},{8,0},{12,4},{1,9},{5,13},{9,1},{13,5},{2,10},{6,14},... | collective-permute-start | bytes 98312 | tf_op jit(solution)/shard_map/ppermute | solution.py:211
  24.3 4.0 %collective-permute-start.9 = (bf16[4,4096]{1,0:T(4,128)(2,1)S(1)}, bf16[4,4096]{1,0:T(4,128)(2,1)S(1)}, u32[]{:S(2)}, u32[]{:S(2)}) collective-permute-start(bf16[4,4096]{1,0:T(4,128)(2,1)S(1)} %get-tuple-element.30), channel_id=1, source_target_pairs={{0,12},{4,0},{8,4},{12,8},{1,13},{5,1},{9,5},{13,9},{2,14},{6,2},{... | collective-permute-start | bytes 98312 | tf_op jit(solution)/shard_map/ppermute | solution.py:211

commit v19 on v18

--- a/solution.py
+++ b/solution.py
@@ -75,12 +75,13 @@
     down(parts, hidden[...], w_down, kept, sent)
 
 
-def add_kernel(kept, arrived, own, *pieces):
-    span = own.shape[0]
-    own[...] = kept[:span, :] + arrived[:span, :].astype(jnp.float32)
-    for i, piece in enumerate(pieces):
-        at = slice((i + 1) * span, (i + 2) * span)
-        piece[...] = (kept[at, :] + arrived[at, :].astype(jnp.float32)).astype(jnp.bfloat16)
+def add_kernel(pairs, kept, arrived, *refs):
+    start = 0
+    for h in range(pairs):
+        for out in refs[h::pairs]:
+            at = slice(start, start + out.shape[0])
+            out[...] = (kept[at, :] + arrived[at, :].astype(jnp.float32)).astype(out.dtype)
+            start += out.shape[0]
 
 
 def fold_kernel(pairs, own, *refs):
@@ -94,7 +95,7 @@
 
 
 def mix_kernel(n_expert, ids, weights, *refs):
-    pieces, out = refs[:-1], refs[-1]
+    pieces, (out, own_factor) = refs[:-2], refs[-2:]
     rows = out.shape[0]
     me, expert = lax.axis_index("etp"), lax.axis_index("expert")
     top, tok = ids.shape
@@ -112,9 +113,18 @@
     for k in range(n_expert):
         owner = lax.rem(expert - k + n_expert, n_expert)
         factor = sum(jnp.where(own_ids[i] == owner, own_weights[i], 0.0) for i in range(top)) / scale
-        term = pieces[k][...].astype(jnp.float32) * factor
-        total = term if total is None else total + term
-    out[...] = total.astype(out.dtype)
+        if k == 0:
+            own_factor[...] = jnp.broadcast_to(factor, own_factor.shape)
+        else:
+            term = pieces[k - 1][...].astype(jnp.float32) * factor
+            total = term if total is None else total + term
+    out[...] = total
+
+
+def finish_kernel(partial, own_factor, *refs):
+    own, out = refs[:-1], refs[-1]
+    total = sum(block[...].astype(jnp.float32) for block in own)
+    out[...] = (partial[...] + total * own_factor[:, :1]).astype(out.dtype)
 
 
 def on_device(n_expert, n_etp, tokens, expert_ids, route_weights, w_gate, w_up, w_down):
@@ -177,47 +187,73 @@
         name="down",
     )(rest, w_down)
 
-    block = n_expert // 2 * rows
-    pieces = []
-    for kept, sent in ((far_kept, far_sent), (near_kept, near_sent)):
-        arrived = lax.ppermute(sent, "etp", swap)
-        own, *others = pl.pallas_call(
-            add_kernel,
-            out_shape=[jax.ShapeDtypeStruct((block, width), jnp.float32)]
-            + [jax.ShapeDtypeStruct((block, width), jnp.bfloat16)] * (pairs - 1),
+    turns = [
+        [(t, 2 * ((t // 2 + h) % pairs) + t % 2) for t in range(n_etp)] for h in range(1, pairs)
+    ]
+
+    def add(kept, sent, counts):
+        shapes = [
+            jax.ShapeDtypeStruct((count * rows, width), jnp.bfloat16 if h else jnp.float32)
+            for count in counts
+            for h in range(pairs)
+        ]
+        sums = pl.pallas_call(
+            functools.partial(add_kernel, pairs),
+            out_shape=shapes,
             in_specs=[VMEM] * 2,
-            out_specs=[VMEM] * pairs,
+            out_specs=[VMEM] * len(shapes),
             compiler_params=GRANT,
             name="add",
-        )(kept, arrived)
-        landed = []
-        for h, piece in enumerate(others, 1):
-            route = [(t, 2 * ((t // 2 + h) % pairs) + t % 2) for t in range(n_etp)]
-            landed.append(lax.ppermute(piece, "etp", route))
-        folded = pl.pallas_call(
-            functools.partial(fold_kernel, pairs),
-            out_shape=[jax.ShapeDtypeStruct((rows, width), jnp.bfloat16)] * (n_expert // 2),
-            in_specs=[VMEM] * pairs,
-            out_specs=[VMEM] * (n_expert // 2),
-            compiler_params=GRANT,
-            name="fold",
-        )(own, *landed)
-        pieces.append(list(folded))
+        )(kept, lax.ppermute(sent, "etp", swap))
+        return [sums[i * pairs : (i + 1) * pairs] for i in range(len(counts))]
+
+    def over_pairs(own, *others):
+        take = own.shape[0] // rows
+        landed = [lax.ppermute(piece, "etp", turn) for piece, turn in zip(others, turns)]
+        return list(
+            pl.pallas_call(
+                functools.partial(fold_kernel, pairs),
+                out_shape=[jax.ShapeDtypeStruct((rows, width), jnp.bfloat16)] * take,
+                in_specs=[VMEM] * pairs,
+                out_specs=[VMEM] * take,
+                compiler_params=GRANT,
+                name="fold",
+            )(own, *landed)
+        )
+
     half = n_expert // 2
-    pieces = pieces[1][:1] + pieces[0] + pieces[1][1:]
-    landed = pieces[:1]
-    for k in range(1, n_expert):
+    first, second = add(far_kept, far_sent, (half // 2, half - half // 2))
+    pieces = over_pairs(*first) + over_pairs(*second)
+    own, last = add(near_kept, near_sent, (1, half - 1))
+    last = over_pairs(*last)
+    pieces += last
+    own, *others = own
+    others, _ = lax.optimization_barrier((others, last))
+    landed = []
+    for k, piece in enumerate(pieces, 1):
         route = [(e, (e + k) % n_expert) for e in range(n_expert)]
-        landed.append(lax.ppermute(pieces[k], "expert", route))
-
-    return pl.pallas_call(
+        landed.append(lax.ppermute(piece, "expert", route))
+    own = [own] + [lax.ppermute(piece, "etp", turn) for piece, turn in zip(others, turns)]
+
+    partial, own_factor = pl.pallas_call(
         functools.partial(mix_kernel, n_expert),
-        out_shape=jax.ShapeDtypeStruct((rows, width), jnp.bfloat16),
-        in_specs=[VMEM] * (2 + n_expert),
-        out_specs=VMEM,
+        out_shape=[
+            jax.ShapeDtypeStruct((rows, width), jnp.float32),
+            jax.ShapeDtypeStruct((rows, 128), jnp.float32),
+        ],
+        in_specs=[VMEM] * (1 + n_expert),
+        out_specs=[VMEM] * 2,
         compiler_params=GRANT,
         name="mix",
     )(expert_ids.T, route_weights.T, *landed)
+    return pl.pallas_call(
+        finish_kernel,
+        out_shape=jax.ShapeDtypeStruct((rows, width), jnp.bfloat16),
+        in_specs=[VMEM] * (2 + pairs),
+        out_specs=VMEM,
+        compiler_params=GRANT,
+        name="finish",
+    )(partial, own_factor, *own)
 
 
 def solution(mesh):

time: 29.2 us -> 30.1 us (1.031)
  starting transfers between devices: 12.8 us -> 16.2 us
  waiting for transfers between devices: 11.1 us -> 8.55 us
    ppermute x7 -> x9, starting transfers between devices: 7.18 us -> 10.6 us  [the longest x3 4.91 us: on_device(): landed.append(lax.ppermute(piece, 'expert', route))]
    ppermute x7 -> x9, waiting for transfers between devices: 5.6 us -> 3.05 us  [the longest x1 1.4 us: on_device(): lax.ppermute(piece, 'etp', turn)]
    pallas_call x5 -> x7, Pallas kernels: 0.84 us -> 0.98 us  [the longest x1 0.7 us: on_device(): pl.pallas_call(finish_kernel, out_shape=jax.ShapeDtypeStruct((rows, width...]
  transfers between devices with their start and end apart: 10 -> 12, of which waited for: 8 -> 8; matrix products, arithmetic and copies ran while one was open for 0% -> 0% of each run, Pallas kernels for 6% -> 6%
where the time goes in v19:
time: 30.1 us; the launch traced here: 30 us
  starting transfers between devices  16.2 us (54%)
  waiting for transfers between devices  8.55 us (28%)
  Pallas kernels  5.15 us (17%)
    ppermute x3, starting transfers between devices, on_device(): landed.append(lax.ppermute(piece, 'expert', route))  4.91 us
    ppermute x1, waiting for transfers between devices, on_device(): far.append(lax.ppermute(tokens, ('expert', 'etp'), route))  4.22 us
    ppermute x1, starting transfers between devices, on_device(): far.append(lax.ppermute(tokens, ('expert', 'etp'), route))  4.04 us
    ppermute x3, starting transfers between devices, over_pairs(): lax.ppermute(piece, 'etp', turn)  3.65 us
    pallas_call x1, Pallas kernels, on_device(): pl.pallas_call(functools.partial(ffn_kernel, n_expert, parts), out_shape=...  2.53 us
    ppermute x1, starting transfers between devices, on_device(): lax.ppermute(tokens, 'expert', [(e, e ^ 1) for e in range(n_expert)])  1.58 us
    ppermute x1, waiting for transfers between devices, on_device(): lax.ppermute(piece, 'etp', turn)  1.4 us
    ppermute x1, starting transfers between devices, on_device(): lax.ppermute(piece, 'etp', turn)  1.4 us
  transfers between devices with their start and end apart: 12, of which 8 were waited for; matrix products, arithmetic and copies ran while one was open for 0% of the time, Pallas kernels for 6%

profile of v19, /device:TPU:0, one launch (start us, length us, event | category | flops | bytes accessed | tf_op | source)
XLA Modules:
  0.0 30.0 jit_solution(12998966198705154503)
XLA Ops:
  0.0 4.0 %collective-permute-start.1 = (bf16[16,4096]{1,0:T(8,128)(2,1)}, bf16[16,4096]{1,0:T(8,128)(2,1)S(1)}, u32[]{:S(2)}, u32[]{:S(2)}) collective-permute-start(bf16[16,4096]{1,0:T(8,128)(2,1)} %tokens.1), channel_id=1, source_target_pairs={{0,8},{1,13},{2,10},{3,15},{4,12},{5,9},{6,14},{7,11},{8,0},{9,5},... | collective-permute-start | bytes 393224 | tf_op jit(solution)/shard_map/ppermute | solution.py:163
  4.0 1.6 %collective-permute-start = (bf16[16,4096]{1,0:T(8,128)(2,1)}, bf16[16,4096]{1,0:T(8,128)(2,1)S(1)}, u32[]{:S(2)}, u32[]{:S(2)}) collective-permute-start(bf16[16,4096]{1,0:T(8,128)(2,1)} %tokens.1), channel_id=1, source_target_pairs={{0,4},{4,0},{8,12},{12,8},{1,5},{5,1},{9,13},{13,9},{2,6},{6,2},{1... | collective-permute-start | bytes 393224 | tf_op jit(solution)/shard_map/ppermute | solution.py:164
  5.6 0.9 %fetch.1.own = bf16[16,4096]{1,0:T(8,128)(2,1)S(1)} custom-call(bf16[16,4096]{1,0:T(8,128)(2,1)} %tokens.1), custom_call_target="tpu_custom_call" | custom-call | tf_op jit(solution)/shard_map/fetch/pallas_call | solution.py:136
  6.6 4.2 %collective-permute-done.1.refs_0_ = bf16[16,4096]{1,0:T(8,128)(2,1)S(1)} collective-permute-done((bf16[16,4096]{1,0:T(8,128)(2,1)}, bf16[16,4096]{1,0:T(8,128)(2,1)S(1)}, u32[]{:S(2)}, u32[]{:S(2)}) %collective-permute-start.1) | collective-permute-done | bytes 131104 | tf_op jit(solution)/shard_map/ppermute | solution.py:163
  10.9 0.7 %collective-permute-done.next_block = bf16[16,4096]{1,0:T(8,128)(2,1)S(1)} collective-permute-done((bf16[16,4096]{1,0:T(8,128)(2,1)}, bf16[16,4096]{1,0:T(8,128)(2,1)S(1)}, u32[]{:S(2)}, u32[]{:S(2)}) %collective-permute-start) | collective-permute-done | bytes 131104 | tf_op jit(solution)/shard_map/ppermute | solution.py:164
  11.6 0.6 %collective-permute-done.2.refs_1_ = bf16[16,4096]{1,0:T(8,128)(2,1)S(1)} collective-permute-done((bf16[16,4096]{1,0:T(8,128)(2,1)S(1)}, bf16[16,4096]{1,0:T(8,128)(2,1)S(1)}, u32[]{:S(2)}, u32[]{:S(2)}) %collective-permute-start.2) | collective-permute-done | bytes 131104 | tf_op jit(solution)/shard_map/ppermute | solution.py:165
  12.2 2.5 %ffn.1 = (f32[16,4096]{1,0:T(8,128)S(1)}, bf16[16,4096]{1,0:T(8,128)(2,1)S(1)}, bf16[32,384]{1,0:T(8,128)(2,1)S(1)}) custom-call(bf16[16,4096]{1,0:T(8,128)(2,1)S(1)} %fetch.1.own, bf16[16,4096]{1,0:T(8,128)(2,1)S(1)} %collective-permute-done.next_block, bf16[64,64]{1,0:T(8,128)(2,1)S(1)} %order.1, bf16[16,4096]{1,0:T(8,128)(2,1)S(1)} %collective-permute-done.1.refs_0_, ...), custom_call_target="tpu_custom_call" | custom-call | tf_op jit(solution)/shard_map/ffn/pallas_call | solution.py:172
  14.7 0.2 collective-permute-start.3
  14.9 0.6 %down.1 = (f32[16,4096]{1,0:T(8,128)S(1)}, bf16[16,4096]{1,0:T(8,128)(2,1)S(1)}) custom-call(bf16[32,384]{1,0:T(8,128)(2,1)S(1)} %get-tuple-element.27.hidden, bf16[1,384,4096]{2,1,0:T(8,128)(2,1)S(1)} %copy-done), custom_call_target="tpu_custom_call" | custom-call | tf_op jit(solution)/shard_map/down/pallas_call | solution.py:181
  15.6 0.4 %collective-permute-start.8 = (bf16[16,4096]{1,0:T(8,128)(2,1)S(1)}, bf16[16,4096]{1,0:T(8,128)(2,1)S(1)}, u32[]{:S(2)}, u32[]{:S(2)}) collective-permute-start(bf16[16,4096]{1,0:T(8,128)(2,1)S(1)} %get-tuple-element.29), channel_id=1, source_target_pairs={{0,1},{1,0},{2,3},{3,2},{4,5},{5,4},{6,7},{7,6},{8,9},{9,8},{10,11... | collective-permute-start | bytes 393224 | tf_op jit(solution)/shard_map/ppermute | solution.py:207
  16.0 0.2 collective-permute-done.3.arrived
  16.2 1.6 %collective-permute-start.4 = (bf16[4,4096]{1,0:T(4,128)(2,1)S(1)}, bf16[4,4096]{1,0:T(4,128)(2,1)S(1)}, u32[]{:S(2)}, u32[]{:S(2)}) collective-permute-start(bf16[4,4096]{1,0:T(4,128)(2,1)S(1)} %get-tuple-element.24), channel_id=1, source_target_pairs={{0,2},{1,3},{2,0},{3,1},{4,6},{5,7},{6,4},{7,5},{8,10},{9,11},{10,... | collective-permute-start | bytes 98312 | tf_op jit(solution)/shard_map/ppermute | solution.py:212
  17.8 0.5 %collective-permute-start.6 = (bf16[4,4096]{1,0:T(4,128)(2,1)S(1)}, bf16[4,4096]{1,0:T(4,128)(2,1)S(1)}, u32[]{:S(2)}, u32[]{:S(2)}) collective-permute-start(bf16[4,4096]{1,0:T(4,128)(2,1)S(1)} %get-tuple-element.26), channel_id=1, source_target_pairs={{0,2},{1,3},{2,0},{3,1},{4,6},{5,7},{6,4},{7,5},{8,10},{9,11},{10,... | collective-permute-start | bytes 98312 | tf_op jit(solution)/shard_map/ppermute | solution.py:212
  18.4 1.6 %collective-permute-start.9 = (bf16[4,4096]{1,0:T(4,128)(2,1)S(1)}, bf16[4,4096]{1,0:T(4,128)(2,1)S(1)}, u32[]{:S(2)}, u32[]{:S(2)}) collective-permute-start(bf16[4,4096]{1,0:T(4,128)(2,1)S(1)} %get-tuple-element.31), channel_id=1, source_target_pairs={{0,2},{1,3},{2,0},{3,1},{4,6},{5,7},{6,4},{7,5},{8,10},{9,11},{10,... | collective-permute-start | bytes 98312 | tf_op jit(solution)/shard_map/ppermute | solution.py:212
  19.9 0.3 collective-permute-done.4.refs_0_
  20.2 1.2 %collective-permute-start.5 = (bf16[4,4096]{1,0:T(4,128)(2,1)S(1)}, bf16[4,4096]{1,0:T(4,128)(2,1)S(1)}, u32[]{:S(2)}, u32[]{:S(2)}) collective-permute-start(bf16[4,4096]{1,0:T(4,128)(2,1)S(1)} %fold.3), channel_id=1, source_target_pairs={{0,4},{4,8},{8,12},{12,0},{1,5},{5,9},{9,13},{13,1},{2,6},{6,10},{... | collective-permute-start | bytes 98312 | tf_op jit(solution)/shard_map/ppermute | solution.py:235
  21.4 0.2 collective-permute-done.6.refs_0_
  21.7 2.1 %collective-permute-start.7 = (bf16[4,4096]{1,0:T(4,128)(2,1)S(1)}, bf16[4,4096]{1,0:T(4,128)(2,1)S(1)}, u32[]{:S(2)}, u32[]{:S(2)}) collective-permute-start(bf16[4,4096]{1,0:T(4,128)(2,1)S(1)} %fold.4), channel_id=1, source_target_pairs={{0,8},{4,12},{8,0},{12,4},{1,9},{5,13},{9,1},{13,5},{2,10},{6,14},... | collective-permute-start | bytes 98312 | tf_op jit(solution)/shard_map/ppermute | solution.py:235
  23.8 1.6 %collective-permute-start.10 = (bf16[4,4096]{1,0:T(4,128)(2,1)S(1)}, bf16[4,4096]{1,0:T(4,128)(2,1)S(1)}, u32[]{:S(2)}, u32[]{:S(2)}) collective-permute-start(bf16[4,4096]{1,0:T(4,128)(2,1)S(1)} %fold.5), channel_id=1, source_target_pairs={{0,12},{4,0},{8,4},{12,8},{1,13},{5,1},{9,5},{13,9},{2,14},{6,2},{... | collective-permute-start | bytes 98312 | tf_op jit(solution)/shard_map/ppermute | solution.py:235
  25.4 1.4 %collective-permute-start.11 = (bf16[4,4096]{1,0:T(4,128)(2,1)S(1)}, bf16[4,4096]{1,0:T(4,128)(2,1)S(1)}, u32[]{:S(2)}, u32[]{:S(2)}) collective-permute-start(bf16[4,4096]{1,0:T(4,128)(2,1)S(1)} %get-tuple-element.36), channel_id=1, source_target_pairs={{0,2},{1,3},{2,0},{3,1},{4,6},{5,7},{6,4},{7,5},{8,10},{9,11},{10,... | collective-permute-start | bytes 98312 | tf_op jit(solution)/shard_map/ppermute | solution.py:236
  26.8 1.0 %collective-permute-done.10.refs_2_ = bf16[4,4096]{1,0:T(4,128)(2,1)S(1)} collective-permute-done((bf16[4,4096]{1,0:T(4,128)(2,1)S(1)}, bf16[4,4096]{1,0:T(4,128)(2,1)S(1)}, u32[]{:S(2)}, u32[]{:S(2)}) %collective-permute-start.10) | collective-permute-done | bytes 32800 | tf_op jit(solution)/shard_map/ppermute | solution.py:235
  27.8 0.1 mix.1
  27.9 1.4 %collective-permute-done.11.refs_1_ = bf16[4,4096]{1,0:T(4,128)(2,1)S(1)} collective-permute-done((bf16[4,4096]{1,0:T(4,128)(2,1)S(1)}, bf16[4,4096]{1,0:T(4,128)(2,1)S(1)}, u32[]{:S(2)}, u32[]{:S(2)}) %collective-permute-start.11) | collective-permute-done | bytes 32800 | tf_op jit(solution)/shard_map/ppermute | solution.py:236
  29.3 0.7 %finish.1 = bf16[4,4096]{1,0:T(4,128)(2,1)} custom-call(f32[4,4096]{1,0:T(4,128)S(1)} %get-tuple-element.32.partial, f32[4,128]{1,0:T(4,128)S(1)} %get-tuple-element.33.own_factor, f32[4,4096]{1,0:T(4,128)S(1)} %get-tuple-element.34.refs_0_, bf16[4,4096]{1,0:T(4,128)(2,1)S(1)} %collective-permute-done.11.refs_1_), custom_call_target="tpu_custom_call" | custom-call | tf_op jit(solution)/shard_map/finish/pallas_call | solution.py:249
  (21 shorter events, 0.3 us)
Async XLA Ops:
  0.0 10.8 %collective-permute-start.1 = (bf16[16,4096]{1,0:T(8,128)(2,1)}, bf16[16,4096]{1,0:T(8,128)(2,1)S(1)}, u32[]{:S(2)}, u32[]{:S(2)}) collective-permute-start(bf16[16,4096]{1,0:T(8,128)(2,1)} %tokens.1), channel_id=1, source_target_pairs={{0,8},{1,13},{2,10},{3,15},{4,12},{5,9},{6,14},{7,11},{8,0},{9,5},... | collective-permute-start | bytes 393224 | tf_op jit(solution)/shard_map/ppermute | solution.py:163
  4.0 7.6 %collective-permute-start = (bf16[16,4096]{1,0:T(8,128)(2,1)}, bf16[16,4096]{1,0:T(8,128)(2,1)S(1)}, u32[]{:S(2)}, u32[]{:S(2)}) collective-permute-start(bf16[16,4096]{1,0:T(8,128)(2,1)} %tokens.1), channel_id=1, source_target_pairs={{0,4},{4,0},{8,12},{12,8},{1,5},{5,1},{9,13},{13,9},{2,6},{6,2},{1... | collective-permute-start | bytes 393224 | tf_op jit(solution)/shard_map/ppermute | solution.py:164
  6.6 5.6 %copy-start = (bf16[1,384,4096]{2,1,0:T(8,128)(2,1)S(1)}, bf16[1,384,4096]{2,1,0:T(8,128)(2,1)}, u32[]{:S(2)}) copy-start(bf16[1,384,4096]{2,1,0:T(8,128)(2,1)} %w_down.1) | copy-start | bytes 9437188
  6.6 5.6 %copy-start.1 = (bf16[1,384,4096]{2,1,0:T(8,128)(2,1)S(1)}, bf16[1,384,4096]{2,1,0:T(8,128)(2,1)}, u32[]{:S(2)}) copy-start(bf16[1,384,4096]{2,1,0:T(8,128)(2,1)} %refs_2_.1) | copy-start | bytes 9437188
  6.6 5.6 %copy-start.2 = (bf16[1,384,4096]{2,1,0:T(8,128)(2,1)S(1)}, bf16[1,384,4096]{2,1,0:T(8,128)(2,1)}, u32[]{:S(2)}) copy-start(bf16[1,384,4096]{2,1,0:T(8,128)(2,1)} %refs_3_.1) | copy-start | bytes 9437188
  10.8 1.3 %collective-permute-start.2 = (bf16[16,4096]{1,0:T(8,128)(2,1)S(1)}, bf16[16,4096]{1,0:T(8,128)(2,1)S(1)}, u32[]{:S(2)}, u32[]{:S(2)}) collective-permute-start(bf16[16,4096]{1,0:T(8,128)(2,1)S(1)} %collective-permute-done.1.refs_0_), channel_id=1, source_target_pairs={{0,1},{1,0},{2,3},{3,2},{4,5},{5,4},{6,7},{7,6},{8,9},{9,8},{10,11... | collective-permute-start | bytes 393224 | tf_op jit(solution)/shard_map/ppermute | solution.py:165
  14.7 13.1 %copy-start.3 = (s32[16,2]{0,1:T(2,128)S(1)}, s32[16,2]{0,1:T(2,128)}, u32[]{:S(2)}) copy-start(s32[16,2]{0,1:T(2,128)} %param.7) | copy-start | bytes 388
  14.7 13.1 %copy-start.4 = (f32[4,2]{0,1:T(2,128)S(1)}, f32[4,2]{0,1:T(2,128)}, u32[]{:S(2)}) copy-start(f32[4,2]{0,1:T(2,128)} %param.8) | copy-start | bytes 100
  14.7 1.4 %collective-permute-start.3 = (bf16[16,4096]{1,0:T(8,128)(2,1)S(1)}, bf16[16,4096]{1,0:T(8,128)(2,1)S(1)}, u32[]{:S(2)}, u32[]{:S(2)}) collective-permute-start(bf16[16,4096]{1,0:T(8,128)(2,1)S(1)} %get-tuple-element.22), channel_id=1, source_target_pairs={{0,1},{1,0},{2,3},{3,2},{4,5},{5,4},{6,7},{7,6},{8,9},{9,8},{10,11... | collective-permute-start | bytes 393224 | tf_op jit(solution)/shard_map/ppermute | solution.py:207
  15.6 2.7 %collective-permute-start.8 = (bf16[16,4096]{1,0:T(8,128)(2,1)S(1)}, bf16[16,4096]{1,0:T(8,128)(2,1)S(1)}, u32[]{:S(2)}, u32[]{:S(2)}) collective-permute-start(bf16[16,4096]{1,0:T(8,128)(2,1)S(1)} %get-tuple-element.29), channel_id=1, source_target_pairs={{0,1},{1,0},{2,3},{3,2},{4,5},{5,4},{6,7},{7,6},{8,9},{9,8},{10,11... | collective-permute-start | bytes 393224 | tf_op jit(solution)/shard_map/ppermute | solution.py:207
  16.2 4.0 %collective-permute-start.4 = (bf16[4,4096]{1,0:T(4,128)(2,1)S(1)}, bf16[4,4096]{1,0:T(4,128)(2,1)S(1)}, u32[]{:S(2)}, u32[]{:S(2)}) collective-permute-start(bf16[4,4096]{1,0:T(4,128)(2,1)S(1)} %get-tuple-element.24), channel_id=1, source_target_pairs={{0,2},{1,3},{2,0},{3,1},{4,6},{5,7},{6,4},{7,5},{8,10},{9,11},{10,... | collective-permute-start | bytes 98312 | tf_op jit(solution)/shard_map/ppermute | solution.py:212
  17.8 3.9 %collective-permute-start.6 = (bf16[4,4096]{1,0:T(4,128)(2,1)S(1)}, bf16[4,4096]{1,0:T(4,128)(2,1)S(1)}, u32[]{:S(2)}, u32[]{:S(2)}) collective-permute-start(bf16[4,4096]{1,0:T(4,128)(2,1)S(1)} %get-tuple-element.26), channel_id=1, source_target_pairs={{0,2},{1,3},{2,0},{3,1},{4,6},{5,7},{6,4},{7,5},{8,10},{9,11},{10,... | collective-permute-start | bytes 98312 | tf_op jit(solution)/shard_map/ppermute | solution.py:212
  18.4 5.4 %collective-permute-start.9 = (bf16[4,4096]{1,0:T(4,128)(2,1)S(1)}, bf16[4,4096]{1,0:T(4,128)(2,1)S(1)}, u32[]{:S(2)}, u32[]{:S(2)}) collective-permute-start(bf16[4,4096]{1,0:T(4,128)(2,1)S(1)} %get-tuple-element.31), channel_id=1, source_target_pairs={{0,2},{1,3},{2,0},{3,1},{4,6},{5,7},{6,4},{7,5},{8,10},{9,11},{10,... | collective-permute-start | bytes 98312 | tf_op jit(solution)/shard_map/ppermute | solution.py:212
  20.2 6.6 %collective-permute-start.5 = (bf16[4,4096]{1,0:T(4,128)(2,1)S(1)}, bf16[4,4096]{1,0:T(4,128)(2,1)S(1)}, u32[]{:S(2)}, u32[]{:S(2)}) collective-permute-start(bf16[4,4096]{1,0:T(4,128)(2,1)S(1)} %fold.3), channel_id=1, source_target_pairs={{0,4},{4,8},{8,12},{12,0},{1,5},{5,9},{9,13},{13,1},{2,6},{6,10},{... | collective-permute-start | bytes 98312 | tf_op jit(solution)/shard_map/ppermute | solution.py:235
  21.7 5.1 %collective-permute-start.7 = (bf16[4,4096]{1,0:T(4,128)(2,1)S(1)}, bf16[4,4096]{1,0:T(4,128)(2,1)S(1)}, u32[]{:S(2)}, u32[]{:S(2)}) collective-permute-start(bf16[4,4096]{1,0:T(4,128)(2,1)S(1)} %fold.4), channel_id=1, source_target_pairs={{0,8},{4,12},{8,0},{12,4},{1,9},{5,13},{9,1},{13,5},{2,10},{6,14},... | collective-permute-start | bytes 98312 | tf_op jit(solution)/shard_map/ppermute | solution.py:235
  23.8 4.0 %collective-permute-start.10 = (bf16[4,4096]{1,0:T(4,128)(2,1)S(1)}, bf16[4,4096]{1,0:T(4,128)(2,1)S(1)}, u32[]{:S(2)}, u32[]{:S(2)}) collective-permute-start(bf16[4,4096]{1,0:T(4,128)(2,1)S(1)} %fold.5), channel_id=1, source_target_pairs={{0,12},{4,0},{8,4},{12,8},{1,13},{5,1},{9,5},{13,9},{2,14},{6,2},{... | collective-permute-start | bytes 98312 | tf_op jit(solution)/shard_map/ppermute | solution.py:235
  25.4 3.9 %collective-permute-start.11 = (bf16[4,4096]{1,0:T(4,128)(2,1)S(1)}, bf16[4,4096]{1,0:T(4,128)(2,1)S(1)}, u32[]{:S(2)}, u32[]{:S(2)}) collective-permute-start(bf16[4,4096]{1,0:T(4,128)(2,1)S(1)} %get-tuple-element.36), channel_id=1, source_target_pairs={{0,2},{1,3},{2,0},{3,1},{4,6},{5,7},{6,4},{7,5},{8,10},{9,11},{10,... | collective-permute-start | bytes 98312 | tf_op jit(solution)/shard_map/ppermute | solution.py:236

commit v20 on v19

--- a/solution.py
+++ b/solution.py
@@ -94,8 +94,8 @@
         piece[...] = total[k * rows : (k + 1) * rows].astype(piece.dtype)
 
 
-def mix_kernel(n_expert, ids, weights, *refs):
-    pieces, (out, own_factor) = refs[:-2], refs[-2:]
+def mix_kernel(n_expert, pairs, ids, weights, *refs):
+    own, pieces, out = refs[:pairs], refs[pairs:-1], refs[-1]
     rows = out.shape[0]
     me, expert = lax.axis_index("etp"), lax.axis_index("expert")
     top, tok = ids.shape
@@ -109,22 +109,14 @@
     own_ids = [column(ids, me * rows, i) for i in range(top)]
     own_weights = [column(weights, 0, i) for i in range(top)]
     scale = sum(own_weights)
-    total = None
     for k in range(n_expert):
         owner = lax.rem(expert - k + n_expert, n_expert)
         factor = sum(jnp.where(own_ids[i] == owner, own_weights[i], 0.0) for i in range(top)) / scale
         if k == 0:
-            own_factor[...] = jnp.broadcast_to(factor, own_factor.shape)
+            total = sum(block[...].astype(jnp.float32) for block in own) * factor
         else:
-            term = pieces[k - 1][...].astype(jnp.float32) * factor
-            total = term if total is None else total + term
-    out[...] = total
-
-
-def finish_kernel(partial, own_factor, *refs):
-    own, out = refs[:-1], refs[-1]
-    total = sum(block[...].astype(jnp.float32) for block in own)
-    out[...] = (partial[...] + total * own_factor[:, :1]).astype(out.dtype)
+            total = total + pieces[k - 1][...].astype(jnp.float32) * factor
+    out[...] = total.astype(out.dtype)
 
 
 def on_device(n_expert, n_etp, tokens, expert_ids, route_weights, w_gate, w_up, w_down):
@@ -228,32 +220,20 @@
     last = over_pairs(*last)
     pieces += last
     own, *others = own
-    others, _ = lax.optimization_barrier((others, last))
+    own = [own] + [lax.ppermute(piece, "etp", turn) for piece, turn in zip(others, turns)]
     landed = []
     for k, piece in enumerate(pieces, 1):
         route = [(e, (e + k) % n_expert) for e in range(n_expert)]
         landed.append(lax.ppermute(piece, "expert", route))
-    own = [own] + [lax.ppermute(piece, "etp", turn) for piece, turn in zip(others, turns)]
-
-    partial, own_factor = pl.pallas_call(
-        functools.partial(mix_kernel, n_expert),
-        out_shape=[
-            jax.ShapeDtypeStruct((rows, width), jnp.float32),
-            jax.ShapeDtypeStruct((rows, 128), jnp.float32),
-        ],
-        in_specs=[VMEM] * (1 + n_expert),
-        out_specs=[VMEM] * 2,
+
+    return pl.pallas_call(
+        functools.partial(mix_kernel, n_expert, pairs),
+        out_shape=jax.ShapeDtypeStruct((rows, width), jnp.bfloat16),
+        in_specs=[VMEM] * (1 + n_expert + pairs),
+        out_specs=VMEM,
         compiler_params=GRANT,
         name="mix",
-    )(expert_ids.T, route_weights.T, *landed)
-    return pl.pallas_call(
-        finish_kernel,
-        out_shape=jax.ShapeDtypeStruct((rows, width), jnp.bfloat16),
-        in_specs=[VMEM] * (2 + pairs),
-        out_specs=VMEM,
-        compiler_params=GRANT,
-        name="finish",
-    )(partial, own_factor, *own)
+    )(expert_ids.T, route_weights.T, *own, *landed)
 
 
 def solution(mesh):

time: 30.1 us -> 28.9 us (0.960)
  starting transfers between devices: 16.2 us -> 15.3 us
    ppermute x3, waiting for transfers between devices: 0.98 us -> 2.57 us  [on_device(): landed.append(lax.ppermute(piece, 'expert', route))]
    ppermute x1, waiting for transfers between devices: 1.4 us -> 0.01 us  [on_device(): lax.ppermute(piece, 'etp', turn)]
    ppermute x1, starting transfers between devices: 1.4 us -> 0.53 us  [on_device(): lax.ppermute(piece, 'etp', turn)]
    ppermute x3, waiting for transfers between devices: 0.49 us -> 0.01 us  [over_pairs(): lax.ppermute(piece, 'etp', turn)]
    pallas_call x2 -> x1, Pallas kernels: 0.81 us -> 0.75 us  [on_device(): pl.pallas_call(functools.partial(mix_kernel, n_expert, pairs), out_shape=...]
  transfers between devices with their start and end apart: 12 -> 12, of which waited for: 8 -> 7; matrix products, arithmetic and copies ran while one was open for 0% -> 0% of each run, Pallas kernels for 6% -> 6%
where the time goes in v20:
time: 28.9 us; the launch traced here: 28.8 us
  starting transfers between devices  15.3 us (53%)
  waiting for transfers between devices  8.26 us (29%)
  Pallas kernels  5.09 us (18%)
    ppermute x3, starting transfers between devices, on_device(): landed.append(lax.ppermute(piece, 'expert', route))  4.95 us
    ppermute x1, waiting for transfers between devices, on_device(): far.append(lax.ppermute(tokens, ('expert', 'etp'), route))  4.22 us
    ppermute x1, starting transfers between devices, on_device(): far.append(lax.ppermute(tokens, ('expert', 'etp'), route))  4.04 us
    ppermute x3, starting transfers between devices, over_pairs(): lax.ppermute(piece, 'etp', turn)  3.65 us
    ppermute x3, waiting for transfers between devices, on_device(): landed.append(lax.ppermute(piece, 'expert', route))  2.57 us
    pallas_call x1, Pallas kernels, on_device(): pl.pallas_call(functools.partial(ffn_kernel, n_expert, parts), out_shape=...  2.53 us
    ppermute x1, starting transfers between devices, on_device(): lax.ppermute(tokens, 'expert', [(e, e ^ 1) for e in range(n_expert)])  1.58 us
    pallas_call x1, Pallas kernels, on_device(): pl.pallas_call(fetch_kernel, out_shape=jax.ShapeDtypeStruct((tok, width),...  0.95 us
  transfers between devices with their start and end apart: 12, of which 7 were waited for; matrix products, arithmetic and copies ran while one was open for 0% of the time, Pallas kernels for 6%

profile of v20, /device:TPU:0, one launch (start us, length us, event | category | flops | bytes accessed | tf_op | source)
XLA Modules:
  0.0 28.8 jit_solution(15337430809913318686)
XLA Ops:
  0.0 4.0 %collective-permute-start.1 = (bf16[16,4096]{1,0:T(8,128)(2,1)}, bf16[16,4096]{1,0:T(8,128)(2,1)S(1)}, u32[]{:S(2)}, u32[]{:S(2)}) collective-permute-start(bf16[16,4096]{1,0:T(8,128)(2,1)} %tokens.1), channel_id=1, source_target_pairs={{0,8},{1,13},{2,10},{3,15},{4,12},{5,9},{6,14},{7,11},{8,0},{9,5},... | collective-permute-start | bytes 393224 | tf_op jit(solution)/shard_map/ppermute | solution.py:155
  4.0 1.6 %collective-permute-start = (bf16[16,4096]{1,0:T(8,128)(2,1)}, bf16[16,4096]{1,0:T(8,128)(2,1)S(1)}, u32[]{:S(2)}, u32[]{:S(2)}) collective-permute-start(bf16[16,4096]{1,0:T(8,128)(2,1)} %tokens.1), channel_id=1, source_target_pairs={{0,4},{4,0},{8,12},{12,8},{1,5},{5,1},{9,13},{13,9},{2,6},{6,2},{1... | collective-permute-start | bytes 393224 | tf_op jit(solution)/shard_map/ppermute | solution.py:156
  5.6 0.9 %fetch.1.own = bf16[16,4096]{1,0:T(8,128)(2,1)S(1)} custom-call(bf16[16,4096]{1,0:T(8,128)(2,1)} %tokens.1), custom_call_target="tpu_custom_call" | custom-call | tf_op jit(solution)/shard_map/fetch/pallas_call | solution.py:128
  6.6 4.2 %collective-permute-done.1.refs_0_ = bf16[16,4096]{1,0:T(8,128)(2,1)S(1)} collective-permute-done((bf16[16,4096]{1,0:T(8,128)(2,1)}, bf16[16,4096]{1,0:T(8,128)(2,1)S(1)}, u32[]{:S(2)}, u32[]{:S(2)}) %collective-permute-start.1) | collective-permute-done | bytes 131104 | tf_op jit(solution)/shard_map/ppermute | solution.py:155
  10.8 0.1 order.1
  10.9 0.7 %collective-permute-done.next_block = bf16[16,4096]{1,0:T(8,128)(2,1)S(1)} collective-permute-done((bf16[16,4096]{1,0:T(8,128)(2,1)}, bf16[16,4096]{1,0:T(8,128)(2,1)S(1)}, u32[]{:S(2)}, u32[]{:S(2)}) %collective-permute-start) | collective-permute-done | bytes 131104 | tf_op jit(solution)/shard_map/ppermute | solution.py:156
  11.6 0.6 %collective-permute-done.2.refs_1_ = bf16[16,4096]{1,0:T(8,128)(2,1)S(1)} collective-permute-done((bf16[16,4096]{1,0:T(8,128)(2,1)S(1)}, bf16[16,4096]{1,0:T(8,128)(2,1)S(1)}, u32[]{:S(2)}, u32[]{:S(2)}) %collective-permute-start.2) | collective-permute-done | bytes 131104 | tf_op jit(solution)/shard_map/ppermute | solution.py:157
  12.2 2.5 %ffn.1 = (f32[16,4096]{1,0:T(8,128)S(1)}, bf16[16,4096]{1,0:T(8,128)(2,1)S(1)}, bf16[32,384]{1,0:T(8,128)(2,1)S(1)}) custom-call(bf16[16,4096]{1,0:T(8,128)(2,1)S(1)} %fetch.1.own, bf16[16,4096]{1,0:T(8,128)(2,1)S(1)} %collective-permute-done.next_block, bf16[64,64]{1,0:T(8,128)(2,1)S(1)} %order.1, bf16[16,4096]{1,0:T(8,128)(2,1)S(1)} %collective-permute-done.1.refs_0_, ...), custom_call_target="tpu_custom_call" | custom-call | tf_op jit(solution)/shard_map/ffn/pallas_call | solution.py:164
  14.7 0.2 collective-permute-start.5
  14.9 0.6 %down.1 = (f32[16,4096]{1,0:T(8,128)S(1)}, bf16[16,4096]{1,0:T(8,128)(2,1)S(1)}) custom-call(bf16[32,384]{1,0:T(8,128)(2,1)S(1)} %get-tuple-element.18.hidden, bf16[1,384,4096]{2,1,0:T(8,128)(2,1)S(1)} %copy-done), custom_call_target="tpu_custom_call" | custom-call | tf_op jit(solution)/shard_map/down/pallas_call | solution.py:173
  15.6 0.4 %collective-permute-start.3 = (bf16[16,4096]{1,0:T(8,128)(2,1)S(1)}, bf16[16,4096]{1,0:T(8,128)(2,1)S(1)}, u32[]{:S(2)}, u32[]{:S(2)}) collective-permute-start(bf16[16,4096]{1,0:T(8,128)(2,1)S(1)} %get-tuple-element.20), channel_id=1, source_target_pairs={{0,1},{1,0},{2,3},{3,2},{4,5},{5,4},{6,7},{7,6},{8,9},{9,8},{10,11... | collective-permute-start | bytes 393224 | tf_op jit(solution)/shard_map/ppermute | solution.py:199
  16.0 0.2 collective-permute-done.5.arrived
  16.2 1.6 %collective-permute-start.6 = (bf16[4,4096]{1,0:T(4,128)(2,1)S(1)}, bf16[4,4096]{1,0:T(4,128)(2,1)S(1)}, u32[]{:S(2)}, u32[]{:S(2)}) collective-permute-start(bf16[4,4096]{1,0:T(4,128)(2,1)S(1)} %get-tuple-element.26), channel_id=1, source_target_pairs={{0,2},{1,3},{2,0},{3,1},{4,6},{5,7},{6,4},{7,5},{8,10},{9,11},{10,... | collective-permute-start | bytes 98312 | tf_op jit(solution)/shard_map/ppermute | solution.py:204
  17.8 0.5 %collective-permute-start.8 = (bf16[4,4096]{1,0:T(4,128)(2,1)S(1)}, bf16[4,4096]{1,0:T(4,128)(2,1)S(1)}, u32[]{:S(2)}, u32[]{:S(2)}) collective-permute-start(bf16[4,4096]{1,0:T(4,128)(2,1)S(1)} %get-tuple-element.28), channel_id=1, source_target_pairs={{0,2},{1,3},{2,0},{3,1},{4,6},{5,7},{6,4},{7,5},{8,10},{9,11},{10,... | collective-permute-start | bytes 98312 | tf_op jit(solution)/shard_map/ppermute | solution.py:204
  18.3 0.1 add.2
  18.4 1.6 %collective-permute-start.10 = (bf16[4,4096]{1,0:T(4,128)(2,1)S(1)}, bf16[4,4096]{1,0:T(4,128)(2,1)S(1)}, u32[]{:S(2)}, u32[]{:S(2)}) collective-permute-start(bf16[4,4096]{1,0:T(4,128)(2,1)S(1)} %get-tuple-element.30), channel_id=1, source_target_pairs={{0,2},{1,3},{2,0},{3,1},{4,6},{5,7},{6,4},{7,5},{8,10},{9,11},{10,... | collective-permute-start | bytes 98312 | tf_op jit(solution)/shard_map/ppermute | solution.py:204
  19.9 0.5 %collective-permute-start.4 = (bf16[4,4096]{1,0:T(4,128)(2,1)S(1)}, bf16[4,4096]{1,0:T(4,128)(2,1)S(1)}, u32[]{:S(2)}, u32[]{:S(2)}) collective-permute-start(bf16[4,4096]{1,0:T(4,128)(2,1)S(1)} %get-tuple-element.22), channel_id=1, source_target_pairs={{0,2},{1,3},{2,0},{3,1},{4,6},{5,7},{6,4},{7,5},{8,10},{9,11},{10,... | collective-permute-start | bytes 98312 | tf_op jit(solution)/shard_map/ppermute | solution.py:223
  20.5 1.2 %collective-permute-start.7 = (bf16[4,4096]{1,0:T(4,128)(2,1)S(1)}, bf16[4,4096]{1,0:T(4,128)(2,1)S(1)}, u32[]{:S(2)}, u32[]{:S(2)}) collective-permute-start(bf16[4,4096]{1,0:T(4,128)(2,1)S(1)} %fold.3), channel_id=1, source_target_pairs={{0,4},{4,8},{8,12},{12,0},{1,5},{5,9},{9,13},{13,1},{2,6},{6,10},{... | collective-permute-start | bytes 98312 | tf_op jit(solution)/shard_map/ppermute | solution.py:227
  21.7 2.3 %collective-permute-start.9 = (bf16[4,4096]{1,0:T(4,128)(2,1)S(1)}, bf16[4,4096]{1,0:T(4,128)(2,1)S(1)}, u32[]{:S(2)}, u32[]{:S(2)}) collective-permute-start(bf16[4,4096]{1,0:T(4,128)(2,1)S(1)} %fold.4), channel_id=1, source_target_pairs={{0,8},{4,12},{8,0},{12,4},{1,9},{5,13},{9,1},{13,5},{2,10},{6,14},... | collective-permute-start | bytes 98312 | tf_op jit(solution)/shard_map/ppermute | solution.py:227
  24.1 1.4 %collective-permute-start.11 = (bf16[4,4096]{1,0:T(4,128)(2,1)S(1)}, bf16[4,4096]{1,0:T(4,128)(2,1)S(1)}, u32[]{:S(2)}, u32[]{:S(2)}) collective-permute-start(bf16[4,4096]{1,0:T(4,128)(2,1)S(1)} %fold.5), channel_id=1, source_target_pairs={{0,12},{4,0},{8,4},{12,8},{1,13},{5,1},{9,5},{13,9},{2,14},{6,2},{... | collective-permute-start | bytes 98312 | tf_op jit(solution)/shard_map/ppermute | solution.py:227
  25.5 0.9 %collective-permute-done.7.refs_2_ = bf16[4,4096]{1,0:T(4,128)(2,1)S(1)} collective-permute-done((bf16[4,4096]{1,0:T(4,128)(2,1)S(1)}, bf16[4,4096]{1,0:T(4,128)(2,1)S(1)}, u32[]{:S(2)}, u32[]{:S(2)}) %collective-permute-start.7) | collective-permute-done | bytes 32800 | tf_op jit(solution)/shard_map/ppermute | solution.py:227
  26.3 0.4 %collective-permute-done.9.refs_3_ = bf16[4,4096]{1,0:T(4,128)(2,1)S(1)} collective-permute-done((bf16[4,4096]{1,0:T(4,128)(2,1)S(1)}, bf16[4,4096]{1,0:T(4,128)(2,1)S(1)}, u32[]{:S(2)}, u32[]{:S(2)}) %collective-permute-start.9) | collective-permute-done | bytes 32800 | tf_op jit(solution)/shard_map/ppermute | solution.py:227
  26.8 1.3 %collective-permute-done.11.refs_4_ = bf16[4,4096]{1,0:T(4,128)(2,1)S(1)} collective-permute-done((bf16[4,4096]{1,0:T(4,128)(2,1)S(1)}, bf16[4,4096]{1,0:T(4,128)(2,1)S(1)}, u32[]{:S(2)}, u32[]{:S(2)}) %collective-permute-start.11) | collective-permute-done | bytes 32800 | tf_op jit(solution)/shard_map/ppermute | solution.py:227
  28.1 0.7 %mix.1 = bf16[4,4096]{1,0:T(4,128)(2,1)} custom-call(s32[2,16]{1,0:T(2,128)S(1)} %bitcast.2, f32[2,4]{1,0:T(2,128)S(1)} %bitcast.3, f32[4,4096]{1,0:T(4,128)S(1)} %get-tuple-element.21.refs_0_, bf16[4,4096]{1,0:T(4,128)(2,1)S(1)} %collective-permute-done.4.refs_1_, bf16[4,4096]{1,0:T(4,128)(2,1)S(1)} %collective-permute-done.7.refs_2_, ...), custom_call_target="tpu_custom_call" | custom-call | tf_op jit(solution)/shard_map/mix/pallas_call | solution.py:229
  (20 shorter events, 0.2 us)
Async XLA Ops:
  0.0 10.8 %collective-permute-start.1 = (bf16[16,4096]{1,0:T(8,128)(2,1)}, bf16[16,4096]{1,0:T(8,128)(2,1)S(1)}, u32[]{:S(2)}, u32[]{:S(2)}) collective-permute-start(bf16[16,4096]{1,0:T(8,128)(2,1)} %tokens.1), channel_id=1, source_target_pairs={{0,8},{1,13},{2,10},{3,15},{4,12},{5,9},{6,14},{7,11},{8,0},{9,5},... | collective-permute-start | bytes 393224 | tf_op jit(solution)/shard_map/ppermute | solution.py:155
  4.0 7.6 %collective-permute-start = (bf16[16,4096]{1,0:T(8,128)(2,1)}, bf16[16,4096]{1,0:T(8,128)(2,1)S(1)}, u32[]{:S(2)}, u32[]{:S(2)}) collective-permute-start(bf16[16,4096]{1,0:T(8,128)(2,1)} %tokens.1), channel_id=1, source_target_pairs={{0,4},{4,0},{8,12},{12,8},{1,5},{5,1},{9,13},{13,9},{2,6},{6,2},{1... | collective-permute-start | bytes 393224 | tf_op jit(solution)/shard_map/ppermute | solution.py:156
  6.6 5.6 %copy-start = (bf16[1,384,4096]{2,1,0:T(8,128)(2,1)S(1)}, bf16[1,384,4096]{2,1,0:T(8,128)(2,1)}, u32[]{:S(2)}) copy-start(bf16[1,384,4096]{2,1,0:T(8,128)(2,1)} %w_down.1) | copy-start | bytes 9437188
  6.6 5.6 %copy-start.1 = (bf16[1,384,4096]{2,1,0:T(8,128)(2,1)S(1)}, bf16[1,384,4096]{2,1,0:T(8,128)(2,1)}, u32[]{:S(2)}) copy-start(bf16[1,384,4096]{2,1,0:T(8,128)(2,1)} %refs_2_.1) | copy-start | bytes 9437188
  6.6 5.6 %copy-start.2 = (bf16[1,384,4096]{2,1,0:T(8,128)(2,1)S(1)}, bf16[1,384,4096]{2,1,0:T(8,128)(2,1)}, u32[]{:S(2)}) copy-start(bf16[1,384,4096]{2,1,0:T(8,128)(2,1)} %refs_3_.1) | copy-start | bytes 9437188
  10.8 1.3 %collective-permute-start.2 = (bf16[16,4096]{1,0:T(8,128)(2,1)S(1)}, bf16[16,4096]{1,0:T(8,128)(2,1)S(1)}, u32[]{:S(2)}, u32[]{:S(2)}) collective-permute-start(bf16[16,4096]{1,0:T(8,128)(2,1)S(1)} %collective-permute-done.1.refs_0_), channel_id=1, source_target_pairs={{0,1},{1,0},{2,3},{3,2},{4,5},{5,4},{6,7},{7,6},{8,9},{9,8},{10,11... | collective-permute-start | bytes 393224 | tf_op jit(solution)/shard_map/ppermute | solution.py:157
  14.7 13.3 %copy-start.3 = (s32[16,2]{0,1:T(2,128)S(1)}, s32[16,2]{0,1:T(2,128)}, u32[]{:S(2)}) copy-start(s32[16,2]{0,1:T(2,128)} %param.7) | copy-start | bytes 388
  14.7 13.3 %copy-start.4 = (f32[4,2]{0,1:T(2,128)S(1)}, f32[4,2]{0,1:T(2,128)}, u32[]{:S(2)}) copy-start(f32[4,2]{0,1:T(2,128)} %param.8) | copy-start | bytes 100
  14.7 1.4 %collective-permute-start.5 = (bf16[16,4096]{1,0:T(8,128)(2,1)S(1)}, bf16[16,4096]{1,0:T(8,128)(2,1)S(1)}, u32[]{:S(2)}, u32[]{:S(2)}) collective-permute-start(bf16[16,4096]{1,0:T(8,128)(2,1)S(1)} %get-tuple-element.24), channel_id=1, source_target_pairs={{0,1},{1,0},{2,3},{3,2},{4,5},{5,4},{6,7},{7,6},{8,9},{9,8},{10,11... | collective-permute-start | bytes 393224 | tf_op jit(solution)/shard_map/ppermute | solution.py:199
  15.6 2.7 %collective-permute-start.3 = (bf16[16,4096]{1,0:T(8,128)(2,1)S(1)}, bf16[16,4096]{1,0:T(8,128)(2,1)S(1)}, u32[]{:S(2)}, u32[]{:S(2)}) collective-permute-start(bf16[16,4096]{1,0:T(8,128)(2,1)S(1)} %get-tuple-element.20), channel_id=1, source_target_pairs={{0,1},{1,0},{2,3},{3,2},{4,5},{5,4},{6,7},{7,6},{8,9},{9,8},{10,11... | collective-permute-start | bytes 393224 | tf_op jit(solution)/shard_map/ppermute | solution.py:199
  16.2 4.3 %collective-permute-start.6 = (bf16[4,4096]{1,0:T(4,128)(2,1)S(1)}, bf16[4,4096]{1,0:T(4,128)(2,1)S(1)}, u32[]{:S(2)}, u32[]{:S(2)}) collective-permute-start(bf16[4,4096]{1,0:T(4,128)(2,1)S(1)} %get-tuple-element.26), channel_id=1, source_target_pairs={{0,2},{1,3},{2,0},{3,1},{4,6},{5,7},{6,4},{7,5},{8,10},{9,11},{10,... | collective-permute-start | bytes 98312 | tf_op jit(solution)/shard_map/ppermute | solution.py:204
  17.8 4.0 %collective-permute-start.8 = (bf16[4,4096]{1,0:T(4,128)(2,1)S(1)}, bf16[4,4096]{1,0:T(4,128)(2,1)S(1)}, u32[]{:S(2)}, u32[]{:S(2)}) collective-permute-start(bf16[4,4096]{1,0:T(4,128)(2,1)S(1)} %get-tuple-element.28), channel_id=1, source_target_pairs={{0,2},{1,3},{2,0},{3,1},{4,6},{5,7},{6,4},{7,5},{8,10},{9,11},{10,... | collective-permute-start | bytes 98312 | tf_op jit(solution)/shard_map/ppermute | solution.py:204
  18.4 5.7 %collective-permute-start.10 = (bf16[4,4096]{1,0:T(4,128)(2,1)S(1)}, bf16[4,4096]{1,0:T(4,128)(2,1)S(1)}, u32[]{:S(2)}, u32[]{:S(2)}) collective-permute-start(bf16[4,4096]{1,0:T(4,128)(2,1)S(1)} %get-tuple-element.30), channel_id=1, source_target_pairs={{0,2},{1,3},{2,0},{3,1},{4,6},{5,7},{6,4},{7,5},{8,10},{9,11},{10,... | collective-permute-start | bytes 98312 | tf_op jit(solution)/shard_map/ppermute | solution.py:204
  19.9 5.6 %collective-permute-start.4 = (bf16[4,4096]{1,0:T(4,128)(2,1)S(1)}, bf16[4,4096]{1,0:T(4,128)(2,1)S(1)}, u32[]{:S(2)}, u32[]{:S(2)}) collective-permute-start(bf16[4,4096]{1,0:T(4,128)(2,1)S(1)} %get-tuple-element.22), channel_id=1, source_target_pairs={{0,2},{1,3},{2,0},{3,1},{4,6},{5,7},{6,4},{7,5},{8,10},{9,11},{10,... | collective-permute-start | bytes 98312 | tf_op jit(solution)/shard_map/ppermute | solution.py:223
  20.5 5.9 %collective-permute-start.7 = (bf16[4,4096]{1,0:T(4,128)(2,1)S(1)}, bf16[4,4096]{1,0:T(4,128)(2,1)S(1)}, u32[]{:S(2)}, u32[]{:S(2)}) collective-permute-start(bf16[4,4096]{1,0:T(4,128)(2,1)S(1)} %fold.3), channel_id=1, source_target_pairs={{0,4},{4,8},{8,12},{12,0},{1,5},{5,9},{9,13},{13,1},{2,6},{6,10},{... | collective-permute-start | bytes 98312 | tf_op jit(solution)/shard_map/ppermute | solution.py:227
  21.7 5.1 %collective-permute-start.9 = (bf16[4,4096]{1,0:T(4,128)(2,1)S(1)}, bf16[4,4096]{1,0:T(4,128)(2,1)S(1)}, u32[]{:S(2)}, u32[]{:S(2)}) collective-permute-start(bf16[4,4096]{1,0:T(4,128)(2,1)S(1)} %fold.4), channel_id=1, source_target_pairs={{0,8},{4,12},{8,0},{12,4},{1,9},{5,13},{9,1},{13,5},{2,10},{6,14},... | collective-permute-start | bytes 98312 | tf_op jit(solution)/shard_map/ppermute | solution.py:227
  24.1 4.0 %collective-permute-start.11 = (bf16[4,4096]{1,0:T(4,128)(2,1)S(1)}, bf16[4,4096]{1,0:T(4,128)(2,1)S(1)}, u32[]{:S(2)}, u32[]{:S(2)}) collective-permute-start(bf16[4,4096]{1,0:T(4,128)(2,1)S(1)} %fold.5), channel_id=1, source_target_pairs={{0,12},{4,0},{8,4},{12,8},{1,13},{5,1},{9,5},{13,9},{2,14},{6,2},{... | collective-permute-start | bytes 98312 | tf_op jit(solution)/shard_map/ppermute | solution.py:227

commit v21 on v20

--- a/solution.py
+++ b/solution.py
@@ -11,6 +11,19 @@
 GRANT = pltpu.CompilerParams(vmem_limit_bytes=16 * 1024 * 1024)
 AHEAD = pl.CostEstimate(flops=10**10, bytes_accessed=0, transcendentals=0)
 HBM = pl.BlockSpec(memory_space=pltpu.HBM)
+
+
+def ring(place, n_expert):
+    place = (place + n_expert) % n_expert if isinstance(place, int) else lax.rem(place + n_expert, n_expert)
+    return place ^ (place >> 1)
+
+
+def ring_place(n_expert):
+    expert = lax.axis_index("expert")
+    place = expert
+    for shift in range(1, n_expert.bit_length() - 1):
+        place = place ^ (expert >> shift)
+    return place
 
 
 def fetch_kernel(tokens, own, sem):
@@ -34,7 +47,7 @@
     second = lax.div(place, rows * half * pairs * 2)
     shift = jnp.where(second == 0, k + 1, jnp.where(k == 0, 0, k + half))
     expert = lax.axis_index("expert")
-    k = lax.bitwise_xor(expert, lax.rem(expert + shift, n_expert))
+    k = lax.bitwise_xor(expert, ring(ring_place(n_expert) + shift, n_expert))
     block = 2 * lax.rem(pair + h, pairs) + lax.rem(core + sent, 2)
     wanted = (k * pairs * 2 + block) * rows + row
     out[...] = jnp.where(source == wanted, 1.0, 0.0).astype(jnp.bfloat16)
@@ -97,7 +110,7 @@
 def mix_kernel(n_expert, pairs, ids, weights, *refs):
     own, pieces, out = refs[:pairs], refs[pairs:-1], refs[-1]
     rows = out.shape[0]
-    me, expert = lax.axis_index("etp"), lax.axis_index("expert")
+    me, place = lax.axis_index("etp"), ring_place(n_expert)
     top, tok = ids.shape
 
     def column(ref, start, i):
@@ -110,7 +123,7 @@
     own_weights = [column(weights, 0, i) for i in range(top)]
     scale = sum(own_weights)
     for k in range(n_expert):
-        owner = lax.rem(expert - k + n_expert, n_expert)
+        owner = ring(place - k, n_expert)
         factor = sum(jnp.where(own_ids[i] == owner, own_weights[i], 0.0) for i in range(top)) / scale
         if k == 0:
             total = sum(block[...].astype(jnp.float32) for block in own) * factor
@@ -223,7 +236,7 @@
     own = [own] + [lax.ppermute(piece, "etp", turn) for piece, turn in zip(others, turns)]
     landed = []
     for k, piece in enumerate(pieces, 1):
-        route = [(e, (e + k) % n_expert) for e in range(n_expert)]
+        route = [(ring(i, n_expert), ring(i + k, n_expert)) for i in range(n_expert)]
         landed.append(lax.ppermute(piece, "expert", route))
 
     return pl.pallas_call(

time: 28.9 us -> 29.5 us (1.021)
  waiting for transfers between devices: 8.26 us -> 8.7 us
    ppermute x3, waiting for transfers between devices: 2.57 us -> 3.02 us  [on_device(): landed.append(lax.ppermute(piece, 'expert', route))]
where the time goes in v21:
time: 29.5 us; the launch traced here: 29.4 us
  starting transfers between devices  15.5 us (53%)
  waiting for transfers between devices  8.7 us (29%)
  Pallas kernels  5.1 us (17%)
    ppermute x3, starting transfers between devices, on_device(): landed.append(lax.ppermute(piece, 'expert', route))  5.07 us
    ppermute x1, waiting for transfers between devices, on_device(): far.append(lax.ppermute(tokens, ('expert', 'etp'), route))  4.22 us
    ppermute x1, starting transfers between devices, on_device(): far.append(lax.ppermute(tokens, ('expert', 'etp'), route))  4.04 us
    ppermute x3, starting transfers between devices, over_pairs(): lax.ppermute(piece, 'etp', turn)  3.65 us
    ppermute x3, waiting for transfers between devices, on_device(): landed.append(lax.ppermute(piece, 'expert', route))  3.02 us
    pallas_call x1, Pallas kernels, on_device(): pl.pallas_call(functools.partial(ffn_kernel, n_expert, parts), out_shape=...  2.53 us
    ppermute x1, starting transfers between devices, on_device(): lax.ppermute(tokens, 'expert', [(e, e ^ 1) for e in range(n_expert)])  1.58 us
    pallas_call x1, Pallas kernels, on_device(): pl.pallas_call(fetch_kernel, out_shape=jax.ShapeDtypeStruct((tok, width),...  0.95 us
  transfers between devices with their start and end apart: 12, of which 7 were waited for; matrix products, arithmetic and copies ran while one was open for 0% of the time, Pallas kernels for 6%

profile of v21, /device:TPU:0, one launch (start us, length us, event | category | flops | bytes accessed | tf_op | source)
XLA Modules:
  0.0 29.4 jit_solution(16053818715409431057)
XLA Ops:
  0.0 4.0 %collective-permute-start.1 = (bf16[16,4096]{1,0:T(8,128)(2,1)}, bf16[16,4096]{1,0:T(8,128)(2,1)S(1)}, u32[]{:S(2)}, u32[]{:S(2)}) collective-permute-start(bf16[16,4096]{1,0:T(8,128)(2,1)} %tokens.1), channel_id=1, source_target_pairs={{0,8},{1,13},{2,10},{3,15},{4,12},{5,9},{6,14},{7,11},{8,0},{9,5},... | collective-permute-start | bytes 393224 | tf_op jit(solution)/shard_map/ppermute | solution.py:168
  4.0 1.6 %collective-permute-start = (bf16[16,4096]{1,0:T(8,128)(2,1)}, bf16[16,4096]{1,0:T(8,128)(2,1)S(1)}, u32[]{:S(2)}, u32[]{:S(2)}) collective-permute-start(bf16[16,4096]{1,0:T(8,128)(2,1)} %tokens.1), channel_id=1, source_target_pairs={{0,4},{4,0},{8,12},{12,8},{1,5},{5,1},{9,13},{13,9},{2,6},{6,2},{1... | collective-permute-start | bytes 393224 | tf_op jit(solution)/shard_map/ppermute | solution.py:169
  5.6 0.9 %fetch.1.own = bf16[16,4096]{1,0:T(8,128)(2,1)S(1)} custom-call(bf16[16,4096]{1,0:T(8,128)(2,1)} %tokens.1), custom_call_target="tpu_custom_call" | custom-call | tf_op jit(solution)/shard_map/fetch/pallas_call | solution.py:141
  6.6 4.2 %collective-permute-done.1.refs_0_ = bf16[16,4096]{1,0:T(8,128)(2,1)S(1)} collective-permute-done((bf16[16,4096]{1,0:T(8,128)(2,1)}, bf16[16,4096]{1,0:T(8,128)(2,1)S(1)}, u32[]{:S(2)}, u32[]{:S(2)}) %collective-permute-start.1) | collective-permute-done | bytes 131104 | tf_op jit(solution)/shard_map/ppermute | solution.py:168
  10.8 0.1 order.1
  10.9 0.7 %collective-permute-done.next_block = bf16[16,4096]{1,0:T(8,128)(2,1)S(1)} collective-permute-done((bf16[16,4096]{1,0:T(8,128)(2,1)}, bf16[16,4096]{1,0:T(8,128)(2,1)S(1)}, u32[]{:S(2)}, u32[]{:S(2)}) %collective-permute-start) | collective-permute-done | bytes 131104 | tf_op jit(solution)/shard_map/ppermute | solution.py:169
  11.6 0.6 %collective-permute-done.2.refs_1_ = bf16[16,4096]{1,0:T(8,128)(2,1)S(1)} collective-permute-done((bf16[16,4096]{1,0:T(8,128)(2,1)S(1)}, bf16[16,4096]{1,0:T(8,128)(2,1)S(1)}, u32[]{:S(2)}, u32[]{:S(2)}) %collective-permute-start.2) | collective-permute-done | bytes 131104 | tf_op jit(solution)/shard_map/ppermute | solution.py:170
  12.2 2.5 %ffn.1 = (f32[16,4096]{1,0:T(8,128)S(1)}, bf16[16,4096]{1,0:T(8,128)(2,1)S(1)}, bf16[32,384]{1,0:T(8,128)(2,1)S(1)}) custom-call(bf16[16,4096]{1,0:T(8,128)(2,1)S(1)} %fetch.1.own, bf16[16,4096]{1,0:T(8,128)(2,1)S(1)} %collective-permute-done.next_block, bf16[64,64]{1,0:T(8,128)(2,1)S(1)} %order.1, bf16[16,4096]{1,0:T(8,128)(2,1)S(1)} %collective-permute-done.1.refs_0_, ...), custom_call_target="tpu_custom_call" | custom-call | tf_op jit(solution)/shard_map/ffn/pallas_call | solution.py:177
  14.7 0.2 collective-permute-start.5
  14.9 0.6 %down.1 = (f32[16,4096]{1,0:T(8,128)S(1)}, bf16[16,4096]{1,0:T(8,128)(2,1)S(1)}) custom-call(bf16[32,384]{1,0:T(8,128)(2,1)S(1)} %get-tuple-element.18.hidden, bf16[1,384,4096]{2,1,0:T(8,128)(2,1)S(1)} %copy-done), custom_call_target="tpu_custom_call" | custom-call | tf_op jit(solution)/shard_map/down/pallas_call | solution.py:186
  15.6 0.4 %collective-permute-start.3 = (bf16[16,4096]{1,0:T(8,128)(2,1)S(1)}, bf16[16,4096]{1,0:T(8,128)(2,1)S(1)}, u32[]{:S(2)}, u32[]{:S(2)}) collective-permute-start(bf16[16,4096]{1,0:T(8,128)(2,1)S(1)} %get-tuple-element.20), channel_id=1, source_target_pairs={{0,1},{1,0},{2,3},{3,2},{4,5},{5,4},{6,7},{7,6},{8,9},{9,8},{10,11... | collective-permute-start | bytes 393224 | tf_op jit(solution)/shard_map/ppermute | solution.py:212
  16.0 0.2 collective-permute-done.5.arrived
  16.2 1.6 %collective-permute-start.6 = (bf16[4,4096]{1,0:T(4,128)(2,1)S(1)}, bf16[4,4096]{1,0:T(4,128)(2,1)S(1)}, u32[]{:S(2)}, u32[]{:S(2)}) collective-permute-start(bf16[4,4096]{1,0:T(4,128)(2,1)S(1)} %get-tuple-element.26), channel_id=1, source_target_pairs={{0,2},{1,3},{2,0},{3,1},{4,6},{5,7},{6,4},{7,5},{8,10},{9,11},{10,... | collective-permute-start | bytes 98312 | tf_op jit(solution)/shard_map/ppermute | solution.py:217
  17.8 0.5 %collective-permute-start.8 = (bf16[4,4096]{1,0:T(4,128)(2,1)S(1)}, bf16[4,4096]{1,0:T(4,128)(2,1)S(1)}, u32[]{:S(2)}, u32[]{:S(2)}) collective-permute-start(bf16[4,4096]{1,0:T(4,128)(2,1)S(1)} %get-tuple-element.28), channel_id=1, source_target_pairs={{0,2},{1,3},{2,0},{3,1},{4,6},{5,7},{6,4},{7,5},{8,10},{9,11},{10,... | collective-permute-start | bytes 98312 | tf_op jit(solution)/shard_map/ppermute | solution.py:217
  18.3 0.1 add.2
  18.4 1.6 %collective-permute-start.10 = (bf16[4,4096]{1,0:T(4,128)(2,1)S(1)}, bf16[4,4096]{1,0:T(4,128)(2,1)S(1)}, u32[]{:S(2)}, u32[]{:S(2)}) collective-permute-start(bf16[4,4096]{1,0:T(4,128)(2,1)S(1)} %get-tuple-element.30), channel_id=1, source_target_pairs={{0,2},{1,3},{2,0},{3,1},{4,6},{5,7},{6,4},{7,5},{8,10},{9,11},{10,... | collective-permute-start | bytes 98312 | tf_op jit(solution)/shard_map/ppermute | solution.py:217
  19.9 0.5 %collective-permute-start.4 = (bf16[4,4096]{1,0:T(4,128)(2,1)S(1)}, bf16[4,4096]{1,0:T(4,128)(2,1)S(1)}, u32[]{:S(2)}, u32[]{:S(2)}) collective-permute-start(bf16[4,4096]{1,0:T(4,128)(2,1)S(1)} %get-tuple-element.22), channel_id=1, source_target_pairs={{0,2},{1,3},{2,0},{3,1},{4,6},{5,7},{6,4},{7,5},{8,10},{9,11},{10,... | collective-permute-start | bytes 98312 | tf_op jit(solution)/shard_map/ppermute | solution.py:236
  20.5 1.2 %collective-permute-start.7 = (bf16[4,4096]{1,0:T(4,128)(2,1)S(1)}, bf16[4,4096]{1,0:T(4,128)(2,1)S(1)}, u32[]{:S(2)}, u32[]{:S(2)}) collective-permute-start(bf16[4,4096]{1,0:T(4,128)(2,1)S(1)} %fold.3), channel_id=1, source_target_pairs={{0,4},{4,12},{12,8},{8,0},{1,5},{5,13},{13,9},{9,1},{2,6},{6,14},{... | collective-permute-start | bytes 98312 | tf_op jit(solution)/shard_map/ppermute | solution.py:240
  21.7 2.9 %collective-permute-start.9 = (bf16[4,4096]{1,0:T(4,128)(2,1)S(1)}, bf16[4,4096]{1,0:T(4,128)(2,1)S(1)}, u32[]{:S(2)}, u32[]{:S(2)}) collective-permute-start(bf16[4,4096]{1,0:T(4,128)(2,1)S(1)} %fold.4), channel_id=1, source_target_pairs={{0,12},{4,8},{12,0},{8,4},{1,13},{5,9},{13,1},{9,5},{2,14},{6,10},... | collective-permute-start | bytes 98312 | tf_op jit(solution)/shard_map/ppermute | solution.py:240
  24.7 0.9 %collective-permute-start.11 = (bf16[4,4096]{1,0:T(4,128)(2,1)S(1)}, bf16[4,4096]{1,0:T(4,128)(2,1)S(1)}, u32[]{:S(2)}, u32[]{:S(2)}) collective-permute-start(bf16[4,4096]{1,0:T(4,128)(2,1)S(1)} %fold.5), channel_id=1, source_target_pairs={{0,8},{4,0},{12,4},{8,12},{1,9},{5,1},{13,5},{9,13},{2,10},{6,2},{... | collective-permute-start | bytes 98312 | tf_op jit(solution)/shard_map/ppermute | solution.py:240
  25.6 0.7 %collective-permute-done.7.refs_2_ = bf16[4,4096]{1,0:T(4,128)(2,1)S(1)} collective-permute-done((bf16[4,4096]{1,0:T(4,128)(2,1)S(1)}, bf16[4,4096]{1,0:T(4,128)(2,1)S(1)}, u32[]{:S(2)}, u32[]{:S(2)}) %collective-permute-start.7) | collective-permute-done | bytes 32800 | tf_op jit(solution)/shard_map/ppermute | solution.py:240
  26.3 1.4 %collective-permute-done.9.refs_3_ = bf16[4,4096]{1,0:T(4,128)(2,1)S(1)} collective-permute-done((bf16[4,4096]{1,0:T(4,128)(2,1)S(1)}, bf16[4,4096]{1,0:T(4,128)(2,1)S(1)}, u32[]{:S(2)}, u32[]{:S(2)}) %collective-permute-start.9) | collective-permute-done | bytes 32800 | tf_op jit(solution)/shard_map/ppermute | solution.py:240
  27.6 1.0 %collective-permute-done.11.refs_4_ = bf16[4,4096]{1,0:T(4,128)(2,1)S(1)} collective-permute-done((bf16[4,4096]{1,0:T(4,128)(2,1)S(1)}, bf16[4,4096]{1,0:T(4,128)(2,1)S(1)}, u32[]{:S(2)}, u32[]{:S(2)}) %collective-permute-start.11) | collective-permute-done | bytes 32800 | tf_op jit(solution)/shard_map/ppermute | solution.py:240
  28.6 0.7 %mix.1 = bf16[4,4096]{1,0:T(4,128)(2,1)} custom-call(s32[2,16]{1,0:T(2,128)S(1)} %bitcast.2, f32[2,4]{1,0:T(2,128)S(1)} %bitcast.3, f32[4,4096]{1,0:T(4,128)S(1)} %get-tuple-element.21.refs_0_, bf16[4,4096]{1,0:T(4,128)(2,1)S(1)} %collective-permute-done.4.refs_1_, bf16[4,4096]{1,0:T(4,128)(2,1)S(1)} %collective-permute-done.7.refs_2_, ...), custom_call_target="tpu_custom_call" | custom-call | tf_op jit(solution)/shard_map/mix/pallas_call | solution.py:242
  (20 shorter events, 0.2 us)
Async XLA Ops:
  0.0 10.8 %collective-permute-start.1 = (bf16[16,4096]{1,0:T(8,128)(2,1)}, bf16[16,4096]{1,0:T(8,128)(2,1)S(1)}, u32[]{:S(2)}, u32[]{:S(2)}) collective-permute-start(bf16[16,4096]{1,0:T(8,128)(2,1)} %tokens.1), channel_id=1, source_target_pairs={{0,8},{1,13},{2,10},{3,15},{4,12},{5,9},{6,14},{7,11},{8,0},{9,5},... | collective-permute-start | bytes 393224 | tf_op jit(solution)/shard_map/ppermute | solution.py:168
  4.0 7.6 %collective-permute-start = (bf16[16,4096]{1,0:T(8,128)(2,1)}, bf16[16,4096]{1,0:T(8,128)(2,1)S(1)}, u32[]{:S(2)}, u32[]{:S(2)}) collective-permute-start(bf16[16,4096]{1,0:T(8,128)(2,1)} %tokens.1), channel_id=1, source_target_pairs={{0,4},{4,0},{8,12},{12,8},{1,5},{5,1},{9,13},{13,9},{2,6},{6,2},{1... | collective-permute-start | bytes 393224 | tf_op jit(solution)/shard_map/ppermute | solution.py:169
  6.6 5.6 %copy-start = (bf16[1,384,4096]{2,1,0:T(8,128)(2,1)S(1)}, bf16[1,384,4096]{2,1,0:T(8,128)(2,1)}, u32[]{:S(2)}) copy-start(bf16[1,384,4096]{2,1,0:T(8,128)(2,1)} %w_down.1) | copy-start | bytes 9437188
  6.6 5.6 %copy-start.1 = (bf16[1,384,4096]{2,1,0:T(8,128)(2,1)S(1)}, bf16[1,384,4096]{2,1,0:T(8,128)(2,1)}, u32[]{:S(2)}) copy-start(bf16[1,384,4096]{2,1,0:T(8,128)(2,1)} %refs_2_.1) | copy-start | bytes 9437188
  6.6 5.6 %copy-start.2 = (bf16[1,384,4096]{2,1,0:T(8,128)(2,1)S(1)}, bf16[1,384,4096]{2,1,0:T(8,128)(2,1)}, u32[]{:S(2)}) copy-start(bf16[1,384,4096]{2,1,0:T(8,128)(2,1)} %refs_3_.1) | copy-start | bytes 9437188
  10.8 1.3 %collective-permute-start.2 = (bf16[16,4096]{1,0:T(8,128)(2,1)S(1)}, bf16[16,4096]{1,0:T(8,128)(2,1)S(1)}, u32[]{:S(2)}, u32[]{:S(2)}) collective-permute-start(bf16[16,4096]{1,0:T(8,128)(2,1)S(1)} %collective-permute-done.1.refs_0_), channel_id=1, source_target_pairs={{0,1},{1,0},{2,3},{3,2},{4,5},{5,4},{6,7},{7,6},{8,9},{9,8},{10,11... | collective-permute-start | bytes 393224 | tf_op jit(solution)/shard_map/ppermute | solution.py:170
  14.7 13.9 %copy-start.3 = (s32[16,2]{0,1:T(2,128)S(1)}, s32[16,2]{0,1:T(2,128)}, u32[]{:S(2)}) copy-start(s32[16,2]{0,1:T(2,128)} %param.7) | copy-start | bytes 388
  14.7 13.9 %copy-start.4 = (f32[4,2]{0,1:T(2,128)S(1)}, f32[4,2]{0,1:T(2,128)}, u32[]{:S(2)}) copy-start(f32[4,2]{0,1:T(2,128)} %param.8) | copy-start | bytes 100
  14.7 1.4 %collective-permute-start.5 = (bf16[16,4096]{1,0:T(8,128)(2,1)S(1)}, bf16[16,4096]{1,0:T(8,128)(2,1)S(1)}, u32[]{:S(2)}, u32[]{:S(2)}) collective-permute-start(bf16[16,4096]{1,0:T(8,128)(2,1)S(1)} %get-tuple-element.24), channel_id=1, source_target_pairs={{0,1},{1,0},{2,3},{3,2},{4,5},{5,4},{6,7},{7,6},{8,9},{9,8},{10,11... | collective-permute-start | bytes 393224 | tf_op jit(solution)/shard_map/ppermute | solution.py:212
  15.6 2.7 %collective-permute-start.3 = (bf16[16,4096]{1,0:T(8,128)(2,1)S(1)}, bf16[16,4096]{1,0:T(8,128)(2,1)S(1)}, u32[]{:S(2)}, u32[]{:S(2)}) collective-permute-start(bf16[16,4096]{1,0:T(8,128)(2,1)S(1)} %get-tuple-element.20), channel_id=1, source_target_pairs={{0,1},{1,0},{2,3},{3,2},{4,5},{5,4},{6,7},{7,6},{8,9},{9,8},{10,11... | collective-permute-start | bytes 393224 | tf_op jit(solution)/shard_map/ppermute | solution.py:212
  16.2 4.3 %collective-permute-start.6 = (bf16[4,4096]{1,0:T(4,128)(2,1)S(1)}, bf16[4,4096]{1,0:T(4,128)(2,1)S(1)}, u32[]{:S(2)}, u32[]{:S(2)}) collective-permute-start(bf16[4,4096]{1,0:T(4,128)(2,1)S(1)} %get-tuple-element.26), channel_id=1, source_target_pairs={{0,2},{1,3},{2,0},{3,1},{4,6},{5,7},{6,4},{7,5},{8,10},{9,11},{10,... | collective-permute-start | bytes 98312 | tf_op jit(solution)/shard_map/ppermute | solution.py:217
  17.8 4.0 %collective-permute-start.8 = (bf16[4,4096]{1,0:T(4,128)(2,1)S(1)}, bf16[4,4096]{1,0:T(4,128)(2,1)S(1)}, u32[]{:S(2)}, u32[]{:S(2)}) collective-permute-start(bf16[4,4096]{1,0:T(4,128)(2,1)S(1)} %get-tuple-element.28), channel_id=1, source_target_pairs={{0,2},{1,3},{2,0},{3,1},{4,6},{5,7},{6,4},{7,5},{8,10},{9,11},{10,... | collective-permute-start | bytes 98312 | tf_op jit(solution)/shard_map/ppermute | solution.py:217
  18.4 6.3 %collective-permute-start.10 = (bf16[4,4096]{1,0:T(4,128)(2,1)S(1)}, bf16[4,4096]{1,0:T(4,128)(2,1)S(1)}, u32[]{:S(2)}, u32[]{:S(2)}) collective-permute-start(bf16[4,4096]{1,0:T(4,128)(2,1)S(1)} %get-tuple-element.30), channel_id=1, source_target_pairs={{0,2},{1,3},{2,0},{3,1},{4,6},{5,7},{6,4},{7,5},{8,10},{9,11},{10,... | collective-permute-start | bytes 98312 | tf_op jit(solution)/shard_map/ppermute | solution.py:217
  19.9 5.7 %collective-permute-start.4 = (bf16[4,4096]{1,0:T(4,128)(2,1)S(1)}, bf16[4,4096]{1,0:T(4,128)(2,1)S(1)}, u32[]{:S(2)}, u32[]{:S(2)}) collective-permute-start(bf16[4,4096]{1,0:T(4,128)(2,1)S(1)} %get-tuple-element.22), channel_id=1, source_target_pairs={{0,2},{1,3},{2,0},{3,1},{4,6},{5,7},{6,4},{7,5},{8,10},{9,11},{10,... | collective-permute-start | bytes 98312 | tf_op jit(solution)/shard_map/ppermute | solution.py:236
  20.5 5.8 %collective-permute-start.7 = (bf16[4,4096]{1,0:T(4,128)(2,1)S(1)}, bf16[4,4096]{1,0:T(4,128)(2,1)S(1)}, u32[]{:S(2)}, u32[]{:S(2)}) collective-permute-start(bf16[4,4096]{1,0:T(4,128)(2,1)S(1)} %fold.3), channel_id=1, source_target_pairs={{0,4},{4,12},{12,8},{8,0},{1,5},{5,13},{13,9},{9,1},{2,6},{6,14},{... | collective-permute-start | bytes 98312 | tf_op jit(solution)/shard_map/ppermute | solution.py:240
  21.7 5.9 %collective-permute-start.9 = (bf16[4,4096]{1,0:T(4,128)(2,1)S(1)}, bf16[4,4096]{1,0:T(4,128)(2,1)S(1)}, u32[]{:S(2)}, u32[]{:S(2)}) collective-permute-start(bf16[4,4096]{1,0:T(4,128)(2,1)S(1)} %fold.4), channel_id=1, source_target_pairs={{0,12},{4,8},{12,0},{8,4},{1,13},{5,9},{13,1},{9,5},{2,14},{6,10},... | collective-permute-start | bytes 98312 | tf_op jit(solution)/shard_map/ppermute | solution.py:240
  24.7 4.0 %collective-permute-start.11 = (bf16[4,4096]{1,0:T(4,128)(2,1)S(1)}, bf16[4,4096]{1,0:T(4,128)(2,1)S(1)}, u32[]{:S(2)}, u32[]{:S(2)}) collective-permute-start(bf16[4,4096]{1,0:T(4,128)(2,1)S(1)} %fold.5), channel_id=1, source_target_pairs={{0,8},{4,0},{12,4},{8,12},{1,9},{5,1},{13,5},{9,13},{2,10},{6,2},{... | collective-permute-start | bytes 98312 | tf_op jit(solution)/shard_map/ppermute | solution.py:240

commit v22 on v20

--- a/solution.py
+++ b/solution.py
@@ -40,9 +40,59 @@
     out[...] = jnp.where(source == wanted, 1.0, 0.0).astype(jnp.bfloat16)
 
 
-def ffn_kernel(n_expert, parts, own, next_block, order, *refs):
+TILE = 256
+
+
+def tiles_of(unit, count):
+    return [t for t in range(count) if 2 * t + 1 == count or (2 * t < count) == (unit == 0)]
+
+
+def staged(unit, x, weights, accs):
+    hidden, width = weights[0].shape[1:]
+    count = len(weights) * hidden // TILE
+
+    def rows_of(tile, cols):
+        parts, start = [], tile * TILE
+        while start < (tile + 1) * TILE:
+            i, at = divmod(start, hidden)
+            size = min(hidden - at, (tile + 1) * TILE - start)
+            parts.append(weights[i][0, at : at + size, cols])
+            start += size
+        return parts[0] if len(parts) == 1 else jnp.concatenate(parts, axis=0)
+
+    steps = []
+    for slot, tile in enumerate(tiles_of(unit, count)):
+        shared = 2 * tile + 1 == count
+        for i in range(width // TILE):
+            if not shared or i % 2 == unit:
+                steps.append((slot, tile, slice(i * TILE, (i + 1) * TILE)))
+    for i, (slot, tile, cols) in enumerate(steps):
+        pltpu.matmul_push_rhs(rows_of(tile, cols), i % 2, unit, transpose=True)
+        yield
+        if i:
+            last, _, before = steps[i - 1]
+            pltpu.matmul_acc_lhs(accs[last], x[:, before], load_staged_rhs=(i - 1) % 2)
+        yield
+    last, _, before = steps[-1]
+    pltpu.matmul_acc_lhs(accs[last], x[:, before], load_staged_rhs=(len(steps) - 1) % 2)
+
+
+def stacked_product(x, weights, accs):
+    count = len(weights) * weights[0].shape[1] // TILE
+    running = [staged(unit, x, weights, accs[unit]) for unit in range(2)]
+    while running:
+        running = [steps for steps in running if next(steps, running) is None]
+    columns = [None] * count
+    for unit in range(2):
+        for slot, tile in enumerate(tiles_of(unit, count)):
+            part = pltpu.matmul_pop(accs[unit][slot])
+            columns[tile] = part if columns[tile] is None else columns[tile] + part
+    return jnp.concatenate(columns, axis=1)
+
+
+def hidden_kernel(n_expert, own, next_block, *refs):
     far = refs[: n_expert - 2]
-    w_gate, w_up, w_down, kept, sent, rest, x = refs[n_expert - 2 :]
+    w_gate, w_up, out, x = refs[n_expert - 2 :]
     core = lax.rem(lax.axis_index("etp"), 2)
     tok = own.shape[0]
     x[0:tok, :] = own[...]
@@ -50,11 +100,28 @@
     for i in range(0, n_expert - 2, 2):
         for block, k in ((far[i], i + 2 + core), (far[i + 1], i + 3 - core)):
             x[pl.ds(pl.multiple_of(k * tok, tok), tok), :] = block[...]
-    contract = (((1,), (1,)), ((), ()))
-    gate = lax.dot_general(w_gate[0], x[...], contract, preferred_element_type=jnp.float32)
-    upper = lax.dot_general(w_up[0], x[...], contract, preferred_element_type=jnp.float32)
-    hidden = (gate / (1.0 + jnp.exp(-gate)) * upper).astype(jnp.bfloat16)
-    hidden = lax.dot_general(order[...], hidden, contract, preferred_element_type=jnp.float32)
+    size = w_gate.shape[1]
+    if x.shape[0] <= TILE and 2 * size % TILE == 0 and size % 128 == 0:
+        columns = 2 * size // TILE
+        first = len(tiles_of(0, columns))
+        both = pl.run_scoped(
+            lambda *accs: stacked_product(x, (w_gate, w_up), (accs[:first], accs[first:])),
+            *(
+                pltpu.ACC(unit)((x.shape[0], TILE), jnp.float32)
+                for unit in range(2)
+                for _ in tiles_of(unit, columns)
+            ),
+        )
+        gate, upper = both[:, :size], both[:, size:]
+    else:
+        contract = (((1,), (1,)), ((), ()))
+        gate = lax.dot_general(x[...], w_gate[0], contract, preferred_element_type=jnp.float32)
+        upper = lax.dot_general(x[...], w_up[0], contract, preferred_element_type=jnp.float32)
+    out[...] = (gate / (1.0 + jnp.exp(-gate)) * upper).astype(out.dtype)
+
+
+def ffn_kernel(parts, order, hidden, w_down, kept, sent, rest):
+    hidden = jnp.dot(order[...], hidden[...], preferred_element_type=jnp.float32)
     hidden = hidden.astype(jnp.bfloat16)
     now = rest.shape[0]
     rest[...] = hidden[now:]
@@ -161,15 +228,23 @@
         jax.ShapeDtypeStruct((side // 2, width), jnp.float32),
         jax.ShapeDtypeStruct((side // 2, width), jnp.bfloat16),
     ]
+    hidden = pl.pallas_call(
+        functools.partial(hidden_kernel, n_expert),
+        out_shape=jax.ShapeDtypeStruct((n_expert * tok, w_gate.shape[1]), jnp.bfloat16),
+        in_specs=[VMEM] * (n_expert + 2),
+        out_specs=VMEM,
+        scratch_shapes=[pltpu.VMEM((n_expert * tok, width), jnp.bfloat16)],
+        compiler_params=GRANT,
+        name="hidden",
+    )(own, next_block, *far, w_gate, w_up)
     far_kept, far_sent, rest = pl.pallas_call(
-        functools.partial(ffn_kernel, n_expert, parts),
+        functools.partial(ffn_kernel, parts),
         out_shape=halves + [jax.ShapeDtypeStruct((side, w_gate.shape[1]), jnp.bfloat16)],
-        in_specs=[VMEM] * (n_expert + 4),
+        in_specs=[VMEM] * 3,
         out_specs=[VMEM] * 3,
-        scratch_shapes=[pltpu.VMEM((n_expert * tok, width), jnp.bfloat16)],
         compiler_params=GRANT,
         name="ffn",
-    )(own, next_block, order, *far, w_gate, w_up, w_down)
+    )(order, hidden, w_down)
     near_kept, near_sent = pl.pallas_call(
         functools.partial(down_kernel, parts),
         out_shape=halves,

time: 28.9 us -> 29 us (level)
    pallas_call x1 -> x2, Pallas kernels: 2.53 us -> 2.64 us  [the longest x1 1.88 us: on_device(): pl.pallas_call(functools.partial(hidden_kernel, n_expert), out_shape=jax....]
where the time goes in v22:
time: 29 us; the launch traced here: 28.9 us
  starting transfers between devices  15.3 us (53%)
  waiting for transfers between devices  8.27 us (29%)
  Pallas kernels  5.2 us (18%)
    ppermute x3, starting transfers between devices, on_device(): landed.append(lax.ppermute(piece, 'expert', route))  4.95 us
    ppermute x1, waiting for transfers between devices, on_device(): far.append(lax.ppermute(tokens, ('expert', 'etp'), route))  4.23 us
    ppermute x1, starting transfers between devices, on_device(): far.append(lax.ppermute(tokens, ('expert', 'etp'), route))  4.04 us
    ppermute x3, starting transfers between devices, over_pairs(): lax.ppermute(piece, 'etp', turn)  3.65 us
    ppermute x3, waiting for transfers between devices, on_device(): landed.append(lax.ppermute(piece, 'expert', route))  2.58 us
    pallas_call x1, Pallas kernels, on_device(): pl.pallas_call(functools.partial(hidden_kernel, n_expert), out_shape=jax....  1.88 us
    ppermute x1, starting transfers between devices, on_device(): lax.ppermute(tokens, 'expert', [(e, e ^ 1) for e in range(n_expert)])  1.58 us
    pallas_call x1, Pallas kernels, on_device(): pl.pallas_call(fetch_kernel, out_shape=jax.ShapeDtypeStruct((tok, width),...  0.95 us
  transfers between devices with their start and end apart: 12, of which 7 were waited for; matrix products, arithmetic and copies ran while one was open for 0% of the time, Pallas kernels for 6%

profile of v22, /device:TPU:0, one launch (start us, length us, event | category | flops | bytes accessed | tf_op | source)
XLA Modules:
  0.0 28.9 jit_solution(7372426650444991258)
XLA Ops:
  0.0 4.0 %collective-permute-start.1 = (bf16[16,4096]{1,0:T(8,128)(2,1)}, bf16[16,4096]{1,0:T(8,128)(2,1)S(1)}, u32[]{:S(2)}, u32[]{:S(2)}) collective-permute-start(bf16[16,4096]{1,0:T(8,128)(2,1)} %tokens.1), channel_id=1, source_target_pairs={{0,8},{1,13},{2,10},{3,15},{4,12},{5,9},{6,14},{7,11},{8,0},{9,5},... | collective-permute-start | bytes 393224 | tf_op jit(solution)/shard_map/ppermute | solution.py:222
  4.0 1.6 %collective-permute-start = (bf16[16,4096]{1,0:T(8,128)(2,1)}, bf16[16,4096]{1,0:T(8,128)(2,1)S(1)}, u32[]{:S(2)}, u32[]{:S(2)}) collective-permute-start(bf16[16,4096]{1,0:T(8,128)(2,1)} %tokens.1), channel_id=1, source_target_pairs={{0,4},{4,0},{8,12},{12,8},{1,5},{5,1},{9,13},{13,9},{2,6},{6,2},{1... | collective-permute-start | bytes 393224 | tf_op jit(solution)/shard_map/ppermute | solution.py:223
  5.6 0.9 %fetch.1.own = bf16[16,4096]{1,0:T(8,128)(2,1)S(1)} custom-call(bf16[16,4096]{1,0:T(8,128)(2,1)} %tokens.1), custom_call_target="tpu_custom_call" | custom-call | tf_op jit(solution)/shard_map/fetch/pallas_call | solution.py:195
  6.6 4.2 %collective-permute-done.1.refs_0_ = bf16[16,4096]{1,0:T(8,128)(2,1)S(1)} collective-permute-done((bf16[16,4096]{1,0:T(8,128)(2,1)}, bf16[16,4096]{1,0:T(8,128)(2,1)S(1)}, u32[]{:S(2)}, u32[]{:S(2)}) %collective-permute-start.1) | collective-permute-done | bytes 131104 | tf_op jit(solution)/shard_map/ppermute | solution.py:222
  10.9 0.7 %collective-permute-done.next_block = bf16[16,4096]{1,0:T(8,128)(2,1)S(1)} collective-permute-done((bf16[16,4096]{1,0:T(8,128)(2,1)}, bf16[16,4096]{1,0:T(8,128)(2,1)S(1)}, u32[]{:S(2)}, u32[]{:S(2)}) %collective-permute-start) | collective-permute-done | bytes 131104 | tf_op jit(solution)/shard_map/ppermute | solution.py:223
  11.6 0.6 %collective-permute-done.2.refs_1_ = bf16[16,4096]{1,0:T(8,128)(2,1)S(1)} collective-permute-done((bf16[16,4096]{1,0:T(8,128)(2,1)S(1)}, bf16[16,4096]{1,0:T(8,128)(2,1)S(1)}, u32[]{:S(2)}, u32[]{:S(2)}) %collective-permute-start.2) | collective-permute-done | bytes 131104 | tf_op jit(solution)/shard_map/ppermute | solution.py:224
  12.2 1.9 %hidden.1 = bf16[64,384]{1,0:T(8,128)(2,1)S(1)} custom-call(bf16[16,4096]{1,0:T(8,128)(2,1)S(1)} %fetch.1.own, bf16[16,4096]{1,0:T(8,128)(2,1)S(1)} %collective-permute-done.next_block, bf16[16,4096]{1,0:T(8,128)(2,1)S(1)} %collective-permute-done.1.refs_0_, bf16[16,4096]{1,0:T(8,128)(2,1)S(1)} %collective-permute-done.2.refs_1_, ...), custom_call_target="tpu_custom_call" | custom-call | tf_op jit(solution)/shard_map/hidden/pallas_call | solution.py:231
  14.1 0.8 %ffn.1 = (f32[16,4096]{1,0:T(8,128)S(1)}, bf16[16,4096]{1,0:T(8,128)(2,1)S(1)}, bf16[32,384]{1,0:T(8,128)(2,1)S(1)}) custom-call(bf16[64,64]{1,0:T(8,128)(2,1)S(1)} %order.1, bf16[64,384]{1,0:T(8,128)(2,1)S(1)} %hidden.1, bf16[1,384,4096]{2,1,0:T(8,128)(2,1)S(1)} %copy-done), custom_call_target="tpu_custom_call" | custom-call | tf_op jit(solution)/shard_map/ffn/pallas_call | solution.py:240
  14.9 0.2 collective-permute-start.5
  15.0 0.6 %down.1 = (f32[16,4096]{1,0:T(8,128)S(1)}, bf16[16,4096]{1,0:T(8,128)(2,1)S(1)}) custom-call(bf16[32,384]{1,0:T(8,128)(2,1)S(1)} %get-tuple-element.18.hidden, bf16[1,384,4096]{2,1,0:T(8,128)(2,1)S(1)} %copy-done), custom_call_target="tpu_custom_call" | custom-call | tf_op jit(solution)/shard_map/down/pallas_call | solution.py:248
  15.7 0.4 %collective-permute-start.3 = (bf16[16,4096]{1,0:T(8,128)(2,1)S(1)}, bf16[16,4096]{1,0:T(8,128)(2,1)S(1)}, u32[]{:S(2)}, u32[]{:S(2)}) collective-permute-start(bf16[16,4096]{1,0:T(8,128)(2,1)S(1)} %get-tuple-element.20), channel_id=1, source_target_pairs={{0,1},{1,0},{2,3},{3,2},{4,5},{5,4},{6,7},{7,6},{8,9},{9,8},{10,11... | collective-permute-start | bytes 393224 | tf_op jit(solution)/shard_map/ppermute | solution.py:274
  16.0 0.2 collective-permute-done.5.arrived
  16.3 1.6 %collective-permute-start.6 = (bf16[4,4096]{1,0:T(4,128)(2,1)S(1)}, bf16[4,4096]{1,0:T(4,128)(2,1)S(1)}, u32[]{:S(2)}, u32[]{:S(2)}) collective-permute-start(bf16[4,4096]{1,0:T(4,128)(2,1)S(1)} %get-tuple-element.26), channel_id=1, source_target_pairs={{0,2},{1,3},{2,0},{3,1},{4,6},{5,7},{6,4},{7,5},{8,10},{9,11},{10,... | collective-permute-start | bytes 98312 | tf_op jit(solution)/shard_map/ppermute | solution.py:279
  17.8 0.5 %collective-permute-start.8 = (bf16[4,4096]{1,0:T(4,128)(2,1)S(1)}, bf16[4,4096]{1,0:T(4,128)(2,1)S(1)}, u32[]{:S(2)}, u32[]{:S(2)}) collective-permute-start(bf16[4,4096]{1,0:T(4,128)(2,1)S(1)} %get-tuple-element.28), channel_id=1, source_target_pairs={{0,2},{1,3},{2,0},{3,1},{4,6},{5,7},{6,4},{7,5},{8,10},{9,11},{10,... | collective-permute-start | bytes 98312 | tf_op jit(solution)/shard_map/ppermute | solution.py:279
  18.4 0.1 add.2
  18.4 1.6 %collective-permute-start.10 = (bf16[4,4096]{1,0:T(4,128)(2,1)S(1)}, bf16[4,4096]{1,0:T(4,128)(2,1)S(1)}, u32[]{:S(2)}, u32[]{:S(2)}) collective-permute-start(bf16[4,4096]{1,0:T(4,128)(2,1)S(1)} %get-tuple-element.30), channel_id=1, source_target_pairs={{0,2},{1,3},{2,0},{3,1},{4,6},{5,7},{6,4},{7,5},{8,10},{9,11},{10,... | collective-permute-start | bytes 98312 | tf_op jit(solution)/shard_map/ppermute | solution.py:279
  20.0 0.5 %collective-permute-start.4 = (bf16[4,4096]{1,0:T(4,128)(2,1)S(1)}, bf16[4,4096]{1,0:T(4,128)(2,1)S(1)}, u32[]{:S(2)}, u32[]{:S(2)}) collective-permute-start(bf16[4,4096]{1,0:T(4,128)(2,1)S(1)} %get-tuple-element.22), channel_id=1, source_target_pairs={{0,2},{1,3},{2,0},{3,1},{4,6},{5,7},{6,4},{7,5},{8,10},{9,11},{10,... | collective-permute-start | bytes 98312 | tf_op jit(solution)/shard_map/ppermute | solution.py:298
  20.6 1.2 %collective-permute-start.7 = (bf16[4,4096]{1,0:T(4,128)(2,1)S(1)}, bf16[4,4096]{1,0:T(4,128)(2,1)S(1)}, u32[]{:S(2)}, u32[]{:S(2)}) collective-permute-start(bf16[4,4096]{1,0:T(4,128)(2,1)S(1)} %fold.3), channel_id=1, source_target_pairs={{0,4},{4,8},{8,12},{12,0},{1,5},{5,9},{9,13},{13,1},{2,6},{6,10},{... | collective-permute-start | bytes 98312 | tf_op jit(solution)/shard_map/ppermute | solution.py:302
  21.8 2.3 %collective-permute-start.9 = (bf16[4,4096]{1,0:T(4,128)(2,1)S(1)}, bf16[4,4096]{1,0:T(4,128)(2,1)S(1)}, u32[]{:S(2)}, u32[]{:S(2)}) collective-permute-start(bf16[4,4096]{1,0:T(4,128)(2,1)S(1)} %fold.4), channel_id=1, source_target_pairs={{0,8},{4,12},{8,0},{12,4},{1,9},{5,13},{9,1},{13,5},{2,10},{6,14},... | collective-permute-start | bytes 98312 | tf_op jit(solution)/shard_map/ppermute | solution.py:302
  24.2 1.4 %collective-permute-start.11 = (bf16[4,4096]{1,0:T(4,128)(2,1)S(1)}, bf16[4,4096]{1,0:T(4,128)(2,1)S(1)}, u32[]{:S(2)}, u32[]{:S(2)}) collective-permute-start(bf16[4,4096]{1,0:T(4,128)(2,1)S(1)} %fold.5), channel_id=1, source_target_pairs={{0,12},{4,0},{8,4},{12,8},{1,13},{5,1},{9,5},{13,9},{2,14},{6,2},{... | collective-permute-start | bytes 98312 | tf_op jit(solution)/shard_map/ppermute | solution.py:302
  25.6 0.9 %collective-permute-done.7.refs_2_ = bf16[4,4096]{1,0:T(4,128)(2,1)S(1)} collective-permute-done((bf16[4,4096]{1,0:T(4,128)(2,1)S(1)}, bf16[4,4096]{1,0:T(4,128)(2,1)S(1)}, u32[]{:S(2)}, u32[]{:S(2)}) %collective-permute-start.7) | collective-permute-done | bytes 32800 | tf_op jit(solution)/shard_map/ppermute | solution.py:302
  26.4 0.4 %collective-permute-done.9.refs_3_ = bf16[4,4096]{1,0:T(4,128)(2,1)S(1)} collective-permute-done((bf16[4,4096]{1,0:T(4,128)(2,1)S(1)}, bf16[4,4096]{1,0:T(4,128)(2,1)S(1)}, u32[]{:S(2)}, u32[]{:S(2)}) %collective-permute-start.9) | collective-permute-done | bytes 32800 | tf_op jit(solution)/shard_map/ppermute | solution.py:302
  26.9 1.3 %collective-permute-done.11.refs_4_ = bf16[4,4096]{1,0:T(4,128)(2,1)S(1)} collective-permute-done((bf16[4,4096]{1,0:T(4,128)(2,1)S(1)}, bf16[4,4096]{1,0:T(4,128)(2,1)S(1)}, u32[]{:S(2)}, u32[]{:S(2)}) %collective-permute-start.11) | collective-permute-done | bytes 32800 | tf_op jit(solution)/shard_map/ppermute | solution.py:302
  28.1 0.7 %mix.1 = bf16[4,4096]{1,0:T(4,128)(2,1)} custom-call(s32[2,16]{1,0:T(2,128)S(1)} %bitcast.2, f32[2,4]{1,0:T(2,128)S(1)} %bitcast.3, f32[4,4096]{1,0:T(4,128)S(1)} %get-tuple-element.21.refs_0_, bf16[4,4096]{1,0:T(4,128)(2,1)S(1)} %collective-permute-done.4.refs_1_, bf16[4,4096]{1,0:T(4,128)(2,1)S(1)} %collective-permute-done.7.refs_2_, ...), custom_call_target="tpu_custom_call" | custom-call | tf_op jit(solution)/shard_map/mix/pallas_call | solution.py:304
  (21 shorter events, 0.2 us)
Async XLA Ops:
  0.0 10.8 %collective-permute-start.1 = (bf16[16,4096]{1,0:T(8,128)(2,1)}, bf16[16,4096]{1,0:T(8,128)(2,1)S(1)}, u32[]{:S(2)}, u32[]{:S(2)}) collective-permute-start(bf16[16,4096]{1,0:T(8,128)(2,1)} %tokens.1), channel_id=1, source_target_pairs={{0,8},{1,13},{2,10},{3,15},{4,12},{5,9},{6,14},{7,11},{8,0},{9,5},... | collective-permute-start | bytes 393224 | tf_op jit(solution)/shard_map/ppermute | solution.py:222
  4.0 7.6 %collective-permute-start = (bf16[16,4096]{1,0:T(8,128)(2,1)}, bf16[16,4096]{1,0:T(8,128)(2,1)S(1)}, u32[]{:S(2)}, u32[]{:S(2)}) collective-permute-start(bf16[16,4096]{1,0:T(8,128)(2,1)} %tokens.1), channel_id=1, source_target_pairs={{0,4},{4,0},{8,12},{12,8},{1,5},{5,1},{9,13},{13,9},{2,6},{6,2},{1... | collective-permute-start | bytes 393224 | tf_op jit(solution)/shard_map/ppermute | solution.py:223
  6.6 5.6 %copy-start.1 = (bf16[1,384,4096]{2,1,0:T(8,128)(2,1)S(1)}, bf16[1,384,4096]{2,1,0:T(8,128)(2,1)}, u32[]{:S(2)}) copy-start(bf16[1,384,4096]{2,1,0:T(8,128)(2,1)} %refs_2_.1) | copy-start | bytes 9437188
  6.6 5.6 %copy-start.2 = (bf16[1,384,4096]{2,1,0:T(8,128)(2,1)S(1)}, bf16[1,384,4096]{2,1,0:T(8,128)(2,1)}, u32[]{:S(2)}) copy-start(bf16[1,384,4096]{2,1,0:T(8,128)(2,1)} %refs_3_.1) | copy-start | bytes 9437188
  10.8 1.3 %collective-permute-start.2 = (bf16[16,4096]{1,0:T(8,128)(2,1)S(1)}, bf16[16,4096]{1,0:T(8,128)(2,1)S(1)}, u32[]{:S(2)}, u32[]{:S(2)}) collective-permute-start(bf16[16,4096]{1,0:T(8,128)(2,1)S(1)} %collective-permute-done.1.refs_0_), channel_id=1, source_target_pairs={{0,1},{1,0},{2,3},{3,2},{4,5},{5,4},{6,7},{7,6},{8,9},{9,8},{10,11... | collective-permute-start | bytes 393224 | tf_op jit(solution)/shard_map/ppermute | solution.py:224
  10.9 3.2 %copy-start = (bf16[1,384,4096]{2,1,0:T(8,128)(2,1)S(1)}, bf16[1,384,4096]{2,1,0:T(8,128)(2,1)}, u32[]{:S(2)}) copy-start(bf16[1,384,4096]{2,1,0:T(8,128)(2,1)} %w_down.3) | copy-start | bytes 9437188
  14.1 14.1 %copy-start.3 = (s32[16,2]{0,1:T(2,128)S(1)}, s32[16,2]{0,1:T(2,128)}, u32[]{:S(2)}) copy-start(s32[16,2]{0,1:T(2,128)} %param.7) | copy-start | bytes 388
  14.1 14.1 %copy-start.4 = (f32[4,2]{0,1:T(2,128)S(1)}, f32[4,2]{0,1:T(2,128)}, u32[]{:S(2)}) copy-start(f32[4,2]{0,1:T(2,128)} %param.8) | copy-start | bytes 100
  14.9 1.4 %collective-permute-start.5 = (bf16[16,4096]{1,0:T(8,128)(2,1)S(1)}, bf16[16,4096]{1,0:T(8,128)(2,1)S(1)}, u32[]{:S(2)}, u32[]{:S(2)}) collective-permute-start(bf16[16,4096]{1,0:T(8,128)(2,1)S(1)} %get-tuple-element.24), channel_id=1, source_target_pairs={{0,1},{1,0},{2,3},{3,2},{4,5},{5,4},{6,7},{7,6},{8,9},{9,8},{10,11... | collective-permute-start | bytes 393224 | tf_op jit(solution)/shard_map/ppermute | solution.py:274
  15.7 2.7 %collective-permute-start.3 = (bf16[16,4096]{1,0:T(8,128)(2,1)S(1)}, bf16[16,4096]{1,0:T(8,128)(2,1)S(1)}, u32[]{:S(2)}, u32[]{:S(2)}) collective-permute-start(bf16[16,4096]{1,0:T(8,128)(2,1)S(1)} %get-tuple-element.20), channel_id=1, source_target_pairs={{0,1},{1,0},{2,3},{3,2},{4,5},{5,4},{6,7},{7,6},{8,9},{9,8},{10,11... | collective-permute-start | bytes 393224 | tf_op jit(solution)/shard_map/ppermute | solution.py:274
  16.3 4.3 %collective-permute-start.6 = (bf16[4,4096]{1,0:T(4,128)(2,1)S(1)}, bf16[4,4096]{1,0:T(4,128)(2,1)S(1)}, u32[]{:S(2)}, u32[]{:S(2)}) collective-permute-start(bf16[4,4096]{1,0:T(4,128)(2,1)S(1)} %get-tuple-element.26), channel_id=1, source_target_pairs={{0,2},{1,3},{2,0},{3,1},{4,6},{5,7},{6,4},{7,5},{8,10},{9,11},{10,... | collective-permute-start | bytes 98312 | tf_op jit(solution)/shard_map/ppermute | solution.py:279
  17.8 4.0 %collective-permute-start.8 = (bf16[4,4096]{1,0:T(4,128)(2,1)S(1)}, bf16[4,4096]{1,0:T(4,128)(2,1)S(1)}, u32[]{:S(2)}, u32[]{:S(2)}) collective-permute-start(bf16[4,4096]{1,0:T(4,128)(2,1)S(1)} %get-tuple-element.28), channel_id=1, source_target_pairs={{0,2},{1,3},{2,0},{3,1},{4,6},{5,7},{6,4},{7,5},{8,10},{9,11},{10,... | collective-permute-start | bytes 98312 | tf_op jit(solution)/shard_map/ppermute | solution.py:279
  18.4 5.7 %collective-permute-start.10 = (bf16[4,4096]{1,0:T(4,128)(2,1)S(1)}, bf16[4,4096]{1,0:T(4,128)(2,1)S(1)}, u32[]{:S(2)}, u32[]{:S(2)}) collective-permute-start(bf16[4,4096]{1,0:T(4,128)(2,1)S(1)} %get-tuple-element.30), channel_id=1, source_target_pairs={{0,2},{1,3},{2,0},{3,1},{4,6},{5,7},{6,4},{7,5},{8,10},{9,11},{10,... | collective-permute-start | bytes 98312 | tf_op jit(solution)/shard_map/ppermute | solution.py:279
  20.0 5.6 %collective-permute-start.4 = (bf16[4,4096]{1,0:T(4,128)(2,1)S(1)}, bf16[4,4096]{1,0:T(4,128)(2,1)S(1)}, u32[]{:S(2)}, u32[]{:S(2)}) collective-permute-start(bf16[4,4096]{1,0:T(4,128)(2,1)S(1)} %get-tuple-element.22), channel_id=1, source_target_pairs={{0,2},{1,3},{2,0},{3,1},{4,6},{5,7},{6,4},{7,5},{8,10},{9,11},{10,... | collective-permute-start | bytes 98312 | tf_op jit(solution)/shard_map/ppermute | solution.py:298
  20.6 5.9 %collective-permute-start.7 = (bf16[4,4096]{1,0:T(4,128)(2,1)S(1)}, bf16[4,4096]{1,0:T(4,128)(2,1)S(1)}, u32[]{:S(2)}, u32[]{:S(2)}) collective-permute-start(bf16[4,4096]{1,0:T(4,128)(2,1)S(1)} %fold.3), channel_id=1, source_target_pairs={{0,4},{4,8},{8,12},{12,0},{1,5},{5,9},{9,13},{13,1},{2,6},{6,10},{... | collective-permute-start | bytes 98312 | tf_op jit(solution)/shard_map/ppermute | solution.py:302
  21.8 5.0 %collective-permute-start.9 = (bf16[4,4096]{1,0:T(4,128)(2,1)S(1)}, bf16[4,4096]{1,0:T(4,128)(2,1)S(1)}, u32[]{:S(2)}, u32[]{:S(2)}) collective-permute-start(bf16[4,4096]{1,0:T(4,128)(2,1)S(1)} %fold.4), channel_id=1, source_target_pairs={{0,8},{4,12},{8,0},{12,4},{1,9},{5,13},{9,1},{13,5},{2,10},{6,14},... | collective-permute-start | bytes 98312 | tf_op jit(solution)/shard_map/ppermute | solution.py:302
  24.2 4.0 %collective-permute-start.11 = (bf16[4,4096]{1,0:T(4,128)(2,1)S(1)}, bf16[4,4096]{1,0:T(4,128)(2,1)S(1)}, u32[]{:S(2)}, u32[]{:S(2)}) collective-permute-start(bf16[4,4096]{1,0:T(4,128)(2,1)S(1)} %fold.5), channel_id=1, source_target_pairs={{0,12},{4,0},{8,4},{12,8},{1,13},{5,1},{9,5},{13,9},{2,14},{6,2},{... | collective-permute-start | bytes 98312 | tf_op jit(solution)/shard_map/ppermute | solution.py:302

commit v23 on v20

--- a/solution.py
+++ b/solution.py
@@ -40,9 +40,36 @@
     out[...] = jnp.where(source == wanted, 1.0, 0.0).astype(jnp.bfloat16)
 
 
-def ffn_kernel(n_expert, parts, own, next_block, order, *refs):
+TILE = 256
+
+
+CHUNK = 128
+
+
+def streamed_products(x, weights, accs):
+    columns = x.shape[1] // TILE
+
+    def stage(i):
+        rows = x[:, i * TILE : (i + 1) * TILE]
+        for unit in range(len(weights)):
+            pltpu.matmul_push_rhs(rows, i % 2, unit, transpose=True)
+
+    stage(0)
+    for i in range(columns):
+        cols = slice(i * TILE, (i + 1) * TILE)
+        for c in range(len(accs[0])):
+            span = slice(c * CHUNK, (c + 1) * CHUNK)
+            for unit, w in enumerate(weights):
+                pltpu.matmul_acc_lhs(
+                    accs[unit][c], w[0, span, cols], load_staged_rhs=None if c else i % 2
+                )
+            if c == 0 and i + 1 < columns:
+                stage(i + 1)
+
+
+def hidden_kernel(n_expert, own, next_block, *refs):
     far = refs[: n_expert - 2]
-    w_gate, w_up, w_down, kept, sent, rest, x = refs[n_expert - 2 :]
+    w_gate, w_up, out, x = refs[n_expert - 2 :]
     core = lax.rem(lax.axis_index("etp"), 2)
     tok = own.shape[0]
     x[0:tok, :] = own[...]
@@ -50,11 +77,33 @@
     for i in range(0, n_expert - 2, 2):
         for block, k in ((far[i], i + 2 + core), (far[i + 1], i + 3 - core)):
             x[pl.ds(pl.multiple_of(k * tok, tok), tok), :] = block[...]
+    size, count = out.shape
+
+    def silu(gate, upper):
+        return (gate / (1.0 + jnp.exp(-gate)) * upper).astype(out.dtype)
+
+    def by_units(*accs):
+        half = len(accs) // 2
+        streamed_products(x, (w_gate, w_up), (accs[:half], accs[half:]))
+        for c in range(half):
+            gate, upper = pltpu.matmul_pop(accs[c]), pltpu.matmul_pop(accs[half + c])
+            out[c * CHUNK : (c + 1) * CHUNK] = silu(gate[:, :count], upper[:, :count])
+
+    if x.shape[0] == TILE:
+        chunk = [pltpu.ACC(unit)((CHUNK, TILE), jnp.float32) for unit in range(2)]
+        pl.run_scoped(by_units, *([chunk[0]] * (size // CHUNK) + [chunk[1]] * (size // CHUNK)))
+    else:
+        contract = (((1,), (1,)), ((), ()))
+        gate = lax.dot_general(w_gate[0], x[...], contract, preferred_element_type=jnp.float32)
+        upper = lax.dot_general(w_up[0], x[...], contract, preferred_element_type=jnp.float32)
+        out[...] = silu(gate, upper)
+
+
+def ffn_kernel(parts, order, hidden, w_down, kept, sent, rest):
     contract = (((1,), (1,)), ((), ()))
-    gate = lax.dot_general(w_gate[0], x[...], contract, preferred_element_type=jnp.float32)
-    upper = lax.dot_general(w_up[0], x[...], contract, preferred_element_type=jnp.float32)
-    hidden = (gate / (1.0 + jnp.exp(-gate)) * upper).astype(jnp.bfloat16)
-    hidden = lax.dot_general(order[...], hidden, contract, preferred_element_type=jnp.float32)
+    hidden = lax.dot_general(
+        order[...], hidden[...], contract, preferred_element_type=jnp.float32
+    )
     hidden = hidden.astype(jnp.bfloat16)
     now = rest.shape[0]
     rest[...] = hidden[now:]
@@ -161,15 +210,26 @@
         jax.ShapeDtypeStruct((side // 2, width), jnp.float32),
         jax.ShapeDtypeStruct((side // 2, width), jnp.bfloat16),
     ]
+    by_units = n_expert * tok <= TILE and w_gate.shape[1] % CHUNK == 0 and width % TILE == 0
+    hidden = pl.pallas_call(
+        functools.partial(hidden_kernel, n_expert),
+        out_shape=jax.ShapeDtypeStruct((w_gate.shape[1], n_expert * tok), jnp.bfloat16),
+        in_specs=[VMEM] * (n_expert + 2),
+        out_specs=VMEM,
+        scratch_shapes=[
+            pltpu.VMEM((TILE if by_units else n_expert * tok, width), jnp.bfloat16)
+        ],
+        compiler_params=GRANT,
+        name="hidden",
+    )(own, next_block, *far, w_gate, w_up)
     far_kept, far_sent, rest = pl.pallas_call(
-        functools.partial(ffn_kernel, n_expert, parts),
+        functools.partial(ffn_kernel, parts),
         out_shape=halves + [jax.ShapeDtypeStruct((side, w_gate.shape[1]), jnp.bfloat16)],
-        in_specs=[VMEM] * (n_expert + 4),
+        in_specs=[VMEM] * 3,
         out_specs=[VMEM] * 3,
-        scratch_shapes=[pltpu.VMEM((n_expert * tok, width), jnp.bfloat16)],
         compiler_params=GRANT,
         name="ffn",
-    )(own, next_block, order, *far, w_gate, w_up, w_down)
+    )(order, hidden, w_down)
     near_kept, near_sent = pl.pallas_call(
         functools.partial(down_kernel, parts),
         out_shape=halves,

time: 28.9 us -> 29 us (level)
    pallas_call x1 -> x2, Pallas kernels: 2.53 us -> 2.66 us  [the longest x1 1.88 us: on_device(): pl.pallas_call(functools.partial(hidden_kernel, n_expert), out_shape=jax....]
where the time goes in v23:
time: 29 us; the launch traced here: 28.9 us
  starting transfers between devices  15.3 us (53%)
  waiting for transfers between devices  8.25 us (28%)
  Pallas kernels  5.23 us (18%)
    ppermute x3, starting transfers between devices, on_device(): landed.append(lax.ppermute(piece, 'expert', route))  4.95 us
    ppermute x1, waiting for transfers between devices, on_device(): far.append(lax.ppermute(tokens, ('expert', 'etp'), route))  4.23 us
    ppermute x1, starting transfers between devices, on_device(): far.append(lax.ppermute(tokens, ('expert', 'etp'), route))  4.04 us
    ppermute x3, starting transfers between devices, over_pairs(): lax.ppermute(piece, 'etp', turn)  3.64 us
    ppermute x3, waiting for transfers between devices, on_device(): landed.append(lax.ppermute(piece, 'expert', route))  2.57 us
    pallas_call x1, Pallas kernels, on_device(): pl.pallas_call(functools.partial(hidden_kernel, n_expert), out_shape=jax....  1.88 us
    ppermute x1, starting transfers between devices, on_device(): lax.ppermute(tokens, 'expert', [(e, e ^ 1) for e in range(n_expert)])  1.58 us
    pallas_call x1, Pallas kernels, on_device(): pl.pallas_call(fetch_kernel, out_shape=jax.ShapeDtypeStruct((tok, width),...  0.95 us
  transfers between devices with their start and end apart: 12, of which 7 were waited for; matrix products, arithmetic and copies ran while one was open for 0% of the time, Pallas kernels for 6%

profile of v23, /device:TPU:0, one launch (start us, length us, event | category | flops | bytes accessed | tf_op | source)
XLA Modules:
  0.0 28.9 jit_solution(18203870413251864860)
XLA Ops:
  0.0 4.0 %collective-permute-start.1 = (bf16[16,4096]{1,0:T(8,128)(2,1)}, bf16[16,4096]{1,0:T(8,128)(2,1)S(1)}, u32[]{:S(2)}, u32[]{:S(2)}) collective-permute-start(bf16[16,4096]{1,0:T(8,128)(2,1)} %tokens.1), channel_id=1, source_target_pairs={{0,8},{1,13},{2,10},{3,15},{4,12},{5,9},{6,14},{7,11},{8,0},{9,5},... | collective-permute-start | bytes 393224 | tf_op jit(solution)/shard_map/ppermute | solution.py:204
  4.0 1.6 %collective-permute-start = (bf16[16,4096]{1,0:T(8,128)(2,1)}, bf16[16,4096]{1,0:T(8,128)(2,1)S(1)}, u32[]{:S(2)}, u32[]{:S(2)}) collective-permute-start(bf16[16,4096]{1,0:T(8,128)(2,1)} %tokens.1), channel_id=1, source_target_pairs={{0,4},{4,0},{8,12},{12,8},{1,5},{5,1},{9,13},{13,9},{2,6},{6,2},{1... | collective-permute-start | bytes 393224 | tf_op jit(solution)/shard_map/ppermute | solution.py:205
  5.6 0.9 %fetch.1.own = bf16[16,4096]{1,0:T(8,128)(2,1)S(1)} custom-call(bf16[16,4096]{1,0:T(8,128)(2,1)} %tokens.1), custom_call_target="tpu_custom_call" | custom-call | tf_op jit(solution)/shard_map/fetch/pallas_call | solution.py:177
  6.6 4.2 %collective-permute-done.1.refs_0_ = bf16[16,4096]{1,0:T(8,128)(2,1)S(1)} collective-permute-done((bf16[16,4096]{1,0:T(8,128)(2,1)}, bf16[16,4096]{1,0:T(8,128)(2,1)S(1)}, u32[]{:S(2)}, u32[]{:S(2)}) %collective-permute-start.1) | collective-permute-done | bytes 131104 | tf_op jit(solution)/shard_map/ppermute | solution.py:204
  10.9 0.7 %collective-permute-done.next_block = bf16[16,4096]{1,0:T(8,128)(2,1)S(1)} collective-permute-done((bf16[16,4096]{1,0:T(8,128)(2,1)}, bf16[16,4096]{1,0:T(8,128)(2,1)S(1)}, u32[]{:S(2)}, u32[]{:S(2)}) %collective-permute-start) | collective-permute-done | bytes 131104 | tf_op jit(solution)/shard_map/ppermute | solution.py:205
  11.6 0.6 %collective-permute-done.2.refs_1_ = bf16[16,4096]{1,0:T(8,128)(2,1)S(1)} collective-permute-done((bf16[16,4096]{1,0:T(8,128)(2,1)S(1)}, bf16[16,4096]{1,0:T(8,128)(2,1)S(1)}, u32[]{:S(2)}, u32[]{:S(2)}) %collective-permute-start.2) | collective-permute-done | bytes 131104 | tf_op jit(solution)/shard_map/ppermute | solution.py:206
  12.2 1.9 %hidden.1 = bf16[384,64]{1,0:T(8,128)(2,1)S(1)} custom-call(bf16[16,4096]{1,0:T(8,128)(2,1)S(1)} %fetch.1.own, bf16[16,4096]{1,0:T(8,128)(2,1)S(1)} %collective-permute-done.next_block, bf16[16,4096]{1,0:T(8,128)(2,1)S(1)} %collective-permute-done.1.refs_0_, bf16[16,4096]{1,0:T(8,128)(2,1)S(1)} %collective-permute-done.2.refs_1_, ...), custom_call_target="tpu_custom_call" | custom-call | tf_op jit(solution)/shard_map/hidden/pallas_call | solution.py:214
  14.1 0.8 %ffn.1 = (f32[16,4096]{1,0:T(8,128)S(1)}, bf16[16,4096]{1,0:T(8,128)(2,1)S(1)}, bf16[32,384]{1,0:T(8,128)(2,1)S(1)}) custom-call(bf16[64,64]{1,0:T(8,128)(2,1)S(1)} %order.1, bf16[384,64]{1,0:T(8,128)(2,1)S(1)} %hidden.1, bf16[1,384,4096]{2,1,0:T(8,128)(2,1)S(1)} %copy-done), custom_call_target="tpu_custom_call" | custom-call | tf_op jit(solution)/shard_map/ffn/pallas_call | solution.py:225
  14.9 0.2 collective-permute-start.5
  15.0 0.6 %down.1 = (f32[16,4096]{1,0:T(8,128)S(1)}, bf16[16,4096]{1,0:T(8,128)(2,1)S(1)}) custom-call(bf16[32,384]{1,0:T(8,128)(2,1)S(1)} %get-tuple-element.18.hidden, bf16[1,384,4096]{2,1,0:T(8,128)(2,1)S(1)} %copy-done), custom_call_target="tpu_custom_call" | custom-call | tf_op jit(solution)/shard_map/down/pallas_call | solution.py:233
  15.7 0.4 %collective-permute-start.3 = (bf16[16,4096]{1,0:T(8,128)(2,1)S(1)}, bf16[16,4096]{1,0:T(8,128)(2,1)S(1)}, u32[]{:S(2)}, u32[]{:S(2)}) collective-permute-start(bf16[16,4096]{1,0:T(8,128)(2,1)S(1)} %get-tuple-element.20), channel_id=1, source_target_pairs={{0,1},{1,0},{2,3},{3,2},{4,5},{5,4},{6,7},{7,6},{8,9},{9,8},{10,11... | collective-permute-start | bytes 393224 | tf_op jit(solution)/shard_map/ppermute | solution.py:259
  16.1 0.2 collective-permute-done.5.arrived
  16.3 1.6 %collective-permute-start.6 = (bf16[4,4096]{1,0:T(4,128)(2,1)S(1)}, bf16[4,4096]{1,0:T(4,128)(2,1)S(1)}, u32[]{:S(2)}, u32[]{:S(2)}) collective-permute-start(bf16[4,4096]{1,0:T(4,128)(2,1)S(1)} %get-tuple-element.26), channel_id=1, source_target_pairs={{0,2},{1,3},{2,0},{3,1},{4,6},{5,7},{6,4},{7,5},{8,10},{9,11},{10,... | collective-permute-start | bytes 98312 | tf_op jit(solution)/shard_map/ppermute | solution.py:264
  17.8 0.5 %collective-permute-start.8 = (bf16[4,4096]{1,0:T(4,128)(2,1)S(1)}, bf16[4,4096]{1,0:T(4,128)(2,1)S(1)}, u32[]{:S(2)}, u32[]{:S(2)}) collective-permute-start(bf16[4,4096]{1,0:T(4,128)(2,1)S(1)} %get-tuple-element.28), channel_id=1, source_target_pairs={{0,2},{1,3},{2,0},{3,1},{4,6},{5,7},{6,4},{7,5},{8,10},{9,11},{10,... | collective-permute-start | bytes 98312 | tf_op jit(solution)/shard_map/ppermute | solution.py:264
  18.4 0.1 add.2
  18.5 1.6 %collective-permute-start.10 = (bf16[4,4096]{1,0:T(4,128)(2,1)S(1)}, bf16[4,4096]{1,0:T(4,128)(2,1)S(1)}, u32[]{:S(2)}, u32[]{:S(2)}) collective-permute-start(bf16[4,4096]{1,0:T(4,128)(2,1)S(1)} %get-tuple-element.30), channel_id=1, source_target_pairs={{0,2},{1,3},{2,0},{3,1},{4,6},{5,7},{6,4},{7,5},{8,10},{9,11},{10,... | collective-permute-start | bytes 98312 | tf_op jit(solution)/shard_map/ppermute | solution.py:264
  20.0 0.5 %collective-permute-start.4 = (bf16[4,4096]{1,0:T(4,128)(2,1)S(1)}, bf16[4,4096]{1,0:T(4,128)(2,1)S(1)}, u32[]{:S(2)}, u32[]{:S(2)}) collective-permute-start(bf16[4,4096]{1,0:T(4,128)(2,1)S(1)} %get-tuple-element.22), channel_id=1, source_target_pairs={{0,2},{1,3},{2,0},{3,1},{4,6},{5,7},{6,4},{7,5},{8,10},{9,11},{10,... | collective-permute-start | bytes 98312 | tf_op jit(solution)/shard_map/ppermute | solution.py:283
  20.6 1.2 %collective-permute-start.7 = (bf16[4,4096]{1,0:T(4,128)(2,1)S(1)}, bf16[4,4096]{1,0:T(4,128)(2,1)S(1)}, u32[]{:S(2)}, u32[]{:S(2)}) collective-permute-start(bf16[4,4096]{1,0:T(4,128)(2,1)S(1)} %fold.3), channel_id=1, source_target_pairs={{0,4},{4,8},{8,12},{12,0},{1,5},{5,9},{9,13},{13,1},{2,6},{6,10},{... | collective-permute-start | bytes 98312 | tf_op jit(solution)/shard_map/ppermute | solution.py:287
  21.8 2.3 %collective-permute-start.9 = (bf16[4,4096]{1,0:T(4,128)(2,1)S(1)}, bf16[4,4096]{1,0:T(4,128)(2,1)S(1)}, u32[]{:S(2)}, u32[]{:S(2)}) collective-permute-start(bf16[4,4096]{1,0:T(4,128)(2,1)S(1)} %fold.4), channel_id=1, source_target_pairs={{0,8},{4,12},{8,0},{12,4},{1,9},{5,13},{9,1},{13,5},{2,10},{6,14},... | collective-permute-start | bytes 98312 | tf_op jit(solution)/shard_map/ppermute | solution.py:287
  24.2 1.4 %collective-permute-start.11 = (bf16[4,4096]{1,0:T(4,128)(2,1)S(1)}, bf16[4,4096]{1,0:T(4,128)(2,1)S(1)}, u32[]{:S(2)}, u32[]{:S(2)}) collective-permute-start(bf16[4,4096]{1,0:T(4,128)(2,1)S(1)} %fold.5), channel_id=1, source_target_pairs={{0,12},{4,0},{8,4},{12,8},{1,13},{5,1},{9,5},{13,9},{2,14},{6,2},{... | collective-permute-start | bytes 98312 | tf_op jit(solution)/shard_map/ppermute | solution.py:287
  25.6 0.9 %collective-permute-done.7.refs_2_ = bf16[4,4096]{1,0:T(4,128)(2,1)S(1)} collective-permute-done((bf16[4,4096]{1,0:T(4,128)(2,1)S(1)}, bf16[4,4096]{1,0:T(4,128)(2,1)S(1)}, u32[]{:S(2)}, u32[]{:S(2)}) %collective-permute-start.7) | collective-permute-done | bytes 32800 | tf_op jit(solution)/shard_map/ppermute | solution.py:287
  26.4 0.4 %collective-permute-done.9.refs_3_ = bf16[4,4096]{1,0:T(4,128)(2,1)S(1)} collective-permute-done((bf16[4,4096]{1,0:T(4,128)(2,1)S(1)}, bf16[4,4096]{1,0:T(4,128)(2,1)S(1)}, u32[]{:S(2)}, u32[]{:S(2)}) %collective-permute-start.9) | collective-permute-done | bytes 32800 | tf_op jit(solution)/shard_map/ppermute | solution.py:287
  26.9 1.3 %collective-permute-done.11.refs_4_ = bf16[4,4096]{1,0:T(4,128)(2,1)S(1)} collective-permute-done((bf16[4,4096]{1,0:T(4,128)(2,1)S(1)}, bf16[4,4096]{1,0:T(4,128)(2,1)S(1)}, u32[]{:S(2)}, u32[]{:S(2)}) %collective-permute-start.11) | collective-permute-done | bytes 32800 | tf_op jit(solution)/shard_map/ppermute | solution.py:287
  28.1 0.7 %mix.1 = bf16[4,4096]{1,0:T(4,128)(2,1)} custom-call(s32[2,16]{1,0:T(2,128)S(1)} %bitcast.2, f32[2,4]{1,0:T(2,128)S(1)} %bitcast.3, f32[4,4096]{1,0:T(4,128)S(1)} %get-tuple-element.21.refs_0_, bf16[4,4096]{1,0:T(4,128)(2,1)S(1)} %collective-permute-done.4.refs_1_, bf16[4,4096]{1,0:T(4,128)(2,1)S(1)} %collective-permute-done.7.refs_2_, ...), custom_call_target="tpu_custom_call" | custom-call | tf_op jit(solution)/shard_map/mix/pallas_call | solution.py:289
  (21 shorter events, 0.2 us)
Async XLA Ops:
  0.0 10.8 %collective-permute-start.1 = (bf16[16,4096]{1,0:T(8,128)(2,1)}, bf16[16,4096]{1,0:T(8,128)(2,1)S(1)}, u32[]{:S(2)}, u32[]{:S(2)}) collective-permute-start(bf16[16,4096]{1,0:T(8,128)(2,1)} %tokens.1), channel_id=1, source_target_pairs={{0,8},{1,13},{2,10},{3,15},{4,12},{5,9},{6,14},{7,11},{8,0},{9,5},... | collective-permute-start | bytes 393224 | tf_op jit(solution)/shard_map/ppermute | solution.py:204
  4.0 7.6 %collective-permute-start = (bf16[16,4096]{1,0:T(8,128)(2,1)}, bf16[16,4096]{1,0:T(8,128)(2,1)S(1)}, u32[]{:S(2)}, u32[]{:S(2)}) collective-permute-start(bf16[16,4096]{1,0:T(8,128)(2,1)} %tokens.1), channel_id=1, source_target_pairs={{0,4},{4,0},{8,12},{12,8},{1,5},{5,1},{9,13},{13,9},{2,6},{6,2},{1... | collective-permute-start | bytes 393224 | tf_op jit(solution)/shard_map/ppermute | solution.py:205
  6.6 5.6 %copy-start.1 = (bf16[1,384,4096]{2,1,0:T(8,128)(2,1)S(1)}, bf16[1,384,4096]{2,1,0:T(8,128)(2,1)}, u32[]{:S(2)}) copy-start(bf16[1,384,4096]{2,1,0:T(8,128)(2,1)} %refs_2_.1) | copy-start | bytes 9437188
  6.6 5.6 %copy-start.2 = (bf16[1,384,4096]{2,1,0:T(8,128)(2,1)S(1)}, bf16[1,384,4096]{2,1,0:T(8,128)(2,1)}, u32[]{:S(2)}) copy-start(bf16[1,384,4096]{2,1,0:T(8,128)(2,1)} %refs_3_.1) | copy-start | bytes 9437188
  10.8 1.3 %collective-permute-start.2 = (bf16[16,4096]{1,0:T(8,128)(2,1)S(1)}, bf16[16,4096]{1,0:T(8,128)(2,1)S(1)}, u32[]{:S(2)}, u32[]{:S(2)}) collective-permute-start(bf16[16,4096]{1,0:T(8,128)(2,1)S(1)} %collective-permute-done.1.refs_0_), channel_id=1, source_target_pairs={{0,1},{1,0},{2,3},{3,2},{4,5},{5,4},{6,7},{7,6},{8,9},{9,8},{10,11... | collective-permute-start | bytes 393224 | tf_op jit(solution)/shard_map/ppermute | solution.py:206
  10.9 3.2 %copy-start = (bf16[1,384,4096]{2,1,0:T(8,128)(2,1)S(1)}, bf16[1,384,4096]{2,1,0:T(8,128)(2,1)}, u32[]{:S(2)}) copy-start(bf16[1,384,4096]{2,1,0:T(8,128)(2,1)} %w_down.3) | copy-start | bytes 9437188
  14.1 14.1 %copy-start.3 = (s32[16,2]{0,1:T(2,128)S(1)}, s32[16,2]{0,1:T(2,128)}, u32[]{:S(2)}) copy-start(s32[16,2]{0,1:T(2,128)} %param.7) | copy-start | bytes 388
  14.1 14.1 %copy-start.4 = (f32[4,2]{0,1:T(2,128)S(1)}, f32[4,2]{0,1:T(2,128)}, u32[]{:S(2)}) copy-start(f32[4,2]{0,1:T(2,128)} %param.8) | copy-start | bytes 100
  14.9 1.4 %collective-permute-start.5 = (bf16[16,4096]{1,0:T(8,128)(2,1)S(1)}, bf16[16,4096]{1,0:T(8,128)(2,1)S(1)}, u32[]{:S(2)}, u32[]{:S(2)}) collective-permute-start(bf16[16,4096]{1,0:T(8,128)(2,1)S(1)} %get-tuple-element.24), channel_id=1, source_target_pairs={{0,1},{1,0},{2,3},{3,2},{4,5},{5,4},{6,7},{7,6},{8,9},{9,8},{10,11... | collective-permute-start | bytes 393224 | tf_op jit(solution)/shard_map/ppermute | solution.py:259
  15.7 2.7 %collective-permute-start.3 = (bf16[16,4096]{1,0:T(8,128)(2,1)S(1)}, bf16[16,4096]{1,0:T(8,128)(2,1)S(1)}, u32[]{:S(2)}, u32[]{:S(2)}) collective-permute-start(bf16[16,4096]{1,0:T(8,128)(2,1)S(1)} %get-tuple-element.20), channel_id=1, source_target_pairs={{0,1},{1,0},{2,3},{3,2},{4,5},{5,4},{6,7},{7,6},{8,9},{9,8},{10,11... | collective-permute-start | bytes 393224 | tf_op jit(solution)/shard_map/ppermute | solution.py:259
  16.3 4.3 %collective-permute-start.6 = (bf16[4,4096]{1,0:T(4,128)(2,1)S(1)}, bf16[4,4096]{1,0:T(4,128)(2,1)S(1)}, u32[]{:S(2)}, u32[]{:S(2)}) collective-permute-start(bf16[4,4096]{1,0:T(4,128)(2,1)S(1)} %get-tuple-element.26), channel_id=1, source_target_pairs={{0,2},{1,3},{2,0},{3,1},{4,6},{5,7},{6,4},{7,5},{8,10},{9,11},{10,... | collective-permute-start | bytes 98312 | tf_op jit(solution)/shard_map/ppermute | solution.py:264
  17.8 4.0 %collective-permute-start.8 = (bf16[4,4096]{1,0:T(4,128)(2,1)S(1)}, bf16[4,4096]{1,0:T(4,128)(2,1)S(1)}, u32[]{:S(2)}, u32[]{:S(2)}) collective-permute-start(bf16[4,4096]{1,0:T(4,128)(2,1)S(1)} %get-tuple-element.28), channel_id=1, source_target_pairs={{0,2},{1,3},{2,0},{3,1},{4,6},{5,7},{6,4},{7,5},{8,10},{9,11},{10,... | collective-permute-start | bytes 98312 | tf_op jit(solution)/shard_map/ppermute | solution.py:264
  18.5 5.7 %collective-permute-start.10 = (bf16[4,4096]{1,0:T(4,128)(2,1)S(1)}, bf16[4,4096]{1,0:T(4,128)(2,1)S(1)}, u32[]{:S(2)}, u32[]{:S(2)}) collective-permute-start(bf16[4,4096]{1,0:T(4,128)(2,1)S(1)} %get-tuple-element.30), channel_id=1, source_target_pairs={{0,2},{1,3},{2,0},{3,1},{4,6},{5,7},{6,4},{7,5},{8,10},{9,11},{10,... | collective-permute-start | bytes 98312 | tf_op jit(solution)/shard_map/ppermute | solution.py:264
  20.0 5.6 %collective-permute-start.4 = (bf16[4,4096]{1,0:T(4,128)(2,1)S(1)}, bf16[4,4096]{1,0:T(4,128)(2,1)S(1)}, u32[]{:S(2)}, u32[]{:S(2)}) collective-permute-start(bf16[4,4096]{1,0:T(4,128)(2,1)S(1)} %get-tuple-element.22), channel_id=1, source_target_pairs={{0,2},{1,3},{2,0},{3,1},{4,6},{5,7},{6,4},{7,5},{8,10},{9,11},{10,... | collective-permute-start | bytes 98312 | tf_op jit(solution)/shard_map/ppermute | solution.py:283
  20.6 5.9 %collective-permute-start.7 = (bf16[4,4096]{1,0:T(4,128)(2,1)S(1)}, bf16[4,4096]{1,0:T(4,128)(2,1)S(1)}, u32[]{:S(2)}, u32[]{:S(2)}) collective-permute-start(bf16[4,4096]{1,0:T(4,128)(2,1)S(1)} %fold.3), channel_id=1, source_target_pairs={{0,4},{4,8},{8,12},{12,0},{1,5},{5,9},{9,13},{13,1},{2,6},{6,10},{... | collective-permute-start | bytes 98312 | tf_op jit(solution)/shard_map/ppermute | solution.py:287
  21.8 5.0 %collective-permute-start.9 = (bf16[4,4096]{1,0:T(4,128)(2,1)S(1)}, bf16[4,4096]{1,0:T(4,128)(2,1)S(1)}, u32[]{:S(2)}, u32[]{:S(2)}) collective-permute-start(bf16[4,4096]{1,0:T(4,128)(2,1)S(1)} %fold.4), channel_id=1, source_target_pairs={{0,8},{4,12},{8,0},{12,4},{1,9},{5,13},{9,1},{13,5},{2,10},{6,14},... | collective-permute-start | bytes 98312 | tf_op jit(solution)/shard_map/ppermute | solution.py:287
  24.2 4.0 %collective-permute-start.11 = (bf16[4,4096]{1,0:T(4,128)(2,1)S(1)}, bf16[4,4096]{1,0:T(4,128)(2,1)S(1)}, u32[]{:S(2)}, u32[]{:S(2)}) collective-permute-start(bf16[4,4096]{1,0:T(4,128)(2,1)S(1)} %fold.5), channel_id=1, source_target_pairs={{0,12},{4,0},{8,4},{12,8},{1,13},{5,1},{9,5},{13,9},{2,14},{6,2},{... | collective-permute-start | bytes 98312 | tf_op jit(solution)/shard_map/ppermute | solution.py:287

commit v24 on v20

--- a/solution.py
+++ b/solution.py
@@ -76,11 +76,11 @@
 
 
 def add_kernel(pairs, kept, arrived, *refs):
+    total = kept[...] + arrived[...].astype(jnp.float32)
     start = 0
     for h in range(pairs):
         for out in refs[h::pairs]:
-            at = slice(start, start + out.shape[0])
-            out[...] = (kept[at, :] + arrived[at, :].astype(jnp.float32)).astype(out.dtype)
+            out[...] = total[start : start + out.shape[0]].astype(out.dtype)
             start += out.shape[0]
 
 

time: 28.9 us -> 28.9 us (level)
  no operation moved by 1% of the time
where the time goes in v24:
time: 28.9 us; the launch traced here: 28.8 us
  starting transfers between devices  15.3 us (53%)
  waiting for transfers between devices  8.26 us (29%)
  Pallas kernels  5.04 us (17%)
    ppermute x3, starting transfers between devices, on_device(): landed.append(lax.ppermute(piece, 'expert', route))  4.95 us
    ppermute x1, waiting for transfers between devices, on_device(): far.append(lax.ppermute(tokens, ('expert', 'etp'), route))  4.22 us
    ppermute x1, starting transfers between devices, on_device(): far.append(lax.ppermute(tokens, ('expert', 'etp'), route))  4.04 us
    ppermute x3, starting transfers between devices, over_pairs(): lax.ppermute(piece, 'etp', turn)  3.65 us
    ppermute x3, waiting for transfers between devices, on_device(): landed.append(lax.ppermute(piece, 'expert', route))  2.57 us
    pallas_call x1, Pallas kernels, on_device(): pl.pallas_call(functools.partial(ffn_kernel, n_expert, parts), out_shape=...  2.53 us
    ppermute x1, starting transfers between devices, on_device(): lax.ppermute(tokens, 'expert', [(e, e ^ 1) for e in range(n_expert)])  1.58 us
    pallas_call x1, Pallas kernels, on_device(): pl.pallas_call(fetch_kernel, out_shape=jax.ShapeDtypeStruct((tok, width),...  0.95 us
  transfers between devices with their start and end apart: 12, of which 7 were waited for; matrix products, arithmetic and copies ran while one was open for 0% of the time, Pallas kernels for 6%

profile of v24, /device:TPU:0, one launch (start us, length us, event | category | flops | bytes accessed | tf_op | source)
XLA Modules:
  0.0 28.8 jit_solution(7944820539281021303)
XLA Ops:
  0.0 4.0 %collective-permute-start.1 = (bf16[16,4096]{1,0:T(8,128)(2,1)}, bf16[16,4096]{1,0:T(8,128)(2,1)S(1)}, u32[]{:S(2)}, u32[]{:S(2)}) collective-permute-start(bf16[16,4096]{1,0:T(8,128)(2,1)} %tokens.1), channel_id=1, source_target_pairs={{0,8},{1,13},{2,10},{3,15},{4,12},{5,9},{6,14},{7,11},{8,0},{9,5},... | collective-permute-start | bytes 393224 | tf_op jit(solution)/shard_map/ppermute | solution.py:155
  4.0 1.6 %collective-permute-start = (bf16[16,4096]{1,0:T(8,128)(2,1)}, bf16[16,4096]{1,0:T(8,128)(2,1)S(1)}, u32[]{:S(2)}, u32[]{:S(2)}) collective-permute-start(bf16[16,4096]{1,0:T(8,128)(2,1)} %tokens.1), channel_id=1, source_target_pairs={{0,4},{4,0},{8,12},{12,8},{1,5},{5,1},{9,13},{13,9},{2,6},{6,2},{1... | collective-permute-start | bytes 393224 | tf_op jit(solution)/shard_map/ppermute | solution.py:156
  5.6 0.9 %fetch.1.own = bf16[16,4096]{1,0:T(8,128)(2,1)S(1)} custom-call(bf16[16,4096]{1,0:T(8,128)(2,1)} %tokens.1), custom_call_target="tpu_custom_call" | custom-call | tf_op jit(solution)/shard_map/fetch/pallas_call | solution.py:128
  6.6 4.2 %collective-permute-done.1.refs_0_ = bf16[16,4096]{1,0:T(8,128)(2,1)S(1)} collective-permute-done((bf16[16,4096]{1,0:T(8,128)(2,1)}, bf16[16,4096]{1,0:T(8,128)(2,1)S(1)}, u32[]{:S(2)}, u32[]{:S(2)}) %collective-permute-start.1) | collective-permute-done | bytes 131104 | tf_op jit(solution)/shard_map/ppermute | solution.py:155
  10.8 0.1 order.1
  10.9 0.7 %collective-permute-done.next_block = bf16[16,4096]{1,0:T(8,128)(2,1)S(1)} collective-permute-done((bf16[16,4096]{1,0:T(8,128)(2,1)}, bf16[16,4096]{1,0:T(8,128)(2,1)S(1)}, u32[]{:S(2)}, u32[]{:S(2)}) %collective-permute-start) | collective-permute-done | bytes 131104 | tf_op jit(solution)/shard_map/ppermute | solution.py:156
  11.6 0.6 %collective-permute-done.2.refs_1_ = bf16[16,4096]{1,0:T(8,128)(2,1)S(1)} collective-permute-done((bf16[16,4096]{1,0:T(8,128)(2,1)S(1)}, bf16[16,4096]{1,0:T(8,128)(2,1)S(1)}, u32[]{:S(2)}, u32[]{:S(2)}) %collective-permute-start.2) | collective-permute-done | bytes 131104 | tf_op jit(solution)/shard_map/ppermute | solution.py:157
  12.2 2.5 %ffn.1 = (f32[16,4096]{1,0:T(8,128)S(1)}, bf16[16,4096]{1,0:T(8,128)(2,1)S(1)}, bf16[32,384]{1,0:T(8,128)(2,1)S(1)}) custom-call(bf16[16,4096]{1,0:T(8,128)(2,1)S(1)} %fetch.1.own, bf16[16,4096]{1,0:T(8,128)(2,1)S(1)} %collective-permute-done.next_block, bf16[64,64]{1,0:T(8,128)(2,1)S(1)} %order.1, bf16[16,4096]{1,0:T(8,128)(2,1)S(1)} %collective-permute-done.1.refs_0_, ...), custom_call_target="tpu_custom_call" | custom-call | tf_op jit(solution)/shard_map/ffn/pallas_call | solution.py:164
  14.7 0.0 copy-start.4
  14.7 0.2 collective-permute-start.5
  14.9 0.6 %down.1 = (f32[16,4096]{1,0:T(8,128)S(1)}, bf16[16,4096]{1,0:T(8,128)(2,1)S(1)}) custom-call(bf16[32,384]{1,0:T(8,128)(2,1)S(1)} %get-tuple-element.18.hidden, bf16[1,384,4096]{2,1,0:T(8,128)(2,1)S(1)} %copy-done), custom_call_target="tpu_custom_call" | custom-call | tf_op jit(solution)/shard_map/down/pallas_call | solution.py:173
  15.6 0.4 %collective-permute-start.3 = (bf16[16,4096]{1,0:T(8,128)(2,1)S(1)}, bf16[16,4096]{1,0:T(8,128)(2,1)S(1)}, u32[]{:S(2)}, u32[]{:S(2)}) collective-permute-start(bf16[16,4096]{1,0:T(8,128)(2,1)S(1)} %get-tuple-element.20), channel_id=1, source_target_pairs={{0,1},{1,0},{2,3},{3,2},{4,5},{5,4},{6,7},{7,6},{8,9},{9,8},{10,11... | collective-permute-start | bytes 393224 | tf_op jit(solution)/shard_map/ppermute | solution.py:199
  16.0 0.2 collective-permute-done.5.arrived
  16.2 1.6 %collective-permute-start.6 = (bf16[4,4096]{1,0:T(4,128)(2,1)S(1)}, bf16[4,4096]{1,0:T(4,128)(2,1)S(1)}, u32[]{:S(2)}, u32[]{:S(2)}) collective-permute-start(bf16[4,4096]{1,0:T(4,128)(2,1)S(1)} %get-tuple-element.26), channel_id=1, source_target_pairs={{0,2},{1,3},{2,0},{3,1},{4,6},{5,7},{6,4},{7,5},{8,10},{9,11},{10,... | collective-permute-start | bytes 98312 | tf_op jit(solution)/shard_map/ppermute | solution.py:204
  17.7 0.5 %collective-permute-start.8 = (bf16[4,4096]{1,0:T(4,128)(2,1)S(1)}, bf16[4,4096]{1,0:T(4,128)(2,1)S(1)}, u32[]{:S(2)}, u32[]{:S(2)}) collective-permute-start(bf16[4,4096]{1,0:T(4,128)(2,1)S(1)} %get-tuple-element.28), channel_id=1, source_target_pairs={{0,2},{1,3},{2,0},{3,1},{4,6},{5,7},{6,4},{7,5},{8,10},{9,11},{10,... | collective-permute-start | bytes 98312 | tf_op jit(solution)/shard_map/ppermute | solution.py:204
  18.3 1.6 %collective-permute-start.10 = (bf16[4,4096]{1,0:T(4,128)(2,1)S(1)}, bf16[4,4096]{1,0:T(4,128)(2,1)S(1)}, u32[]{:S(2)}, u32[]{:S(2)}) collective-permute-start(bf16[4,4096]{1,0:T(4,128)(2,1)S(1)} %get-tuple-element.30), channel_id=1, source_target_pairs={{0,2},{1,3},{2,0},{3,1},{4,6},{5,7},{6,4},{7,5},{8,10},{9,11},{10,... | collective-permute-start | bytes 98312 | tf_op jit(solution)/shard_map/ppermute | solution.py:204
  19.9 0.5 %collective-permute-start.4 = (bf16[4,4096]{1,0:T(4,128)(2,1)S(1)}, bf16[4,4096]{1,0:T(4,128)(2,1)S(1)}, u32[]{:S(2)}, u32[]{:S(2)}) collective-permute-start(bf16[4,4096]{1,0:T(4,128)(2,1)S(1)} %get-tuple-element.22), channel_id=1, source_target_pairs={{0,2},{1,3},{2,0},{3,1},{4,6},{5,7},{6,4},{7,5},{8,10},{9,11},{10,... | collective-permute-start | bytes 98312 | tf_op jit(solution)/shard_map/ppermute | solution.py:223
  20.4 1.2 %collective-permute-start.7 = (bf16[4,4096]{1,0:T(4,128)(2,1)S(1)}, bf16[4,4096]{1,0:T(4,128)(2,1)S(1)}, u32[]{:S(2)}, u32[]{:S(2)}) collective-permute-start(bf16[4,4096]{1,0:T(4,128)(2,1)S(1)} %fold.3), channel_id=1, source_target_pairs={{0,4},{4,8},{8,12},{12,0},{1,5},{5,9},{9,13},{13,1},{2,6},{6,10},{... | collective-permute-start | bytes 98312 | tf_op jit(solution)/shard_map/ppermute | solution.py:227
  21.7 2.3 %collective-permute-start.9 = (bf16[4,4096]{1,0:T(4,128)(2,1)S(1)}, bf16[4,4096]{1,0:T(4,128)(2,1)S(1)}, u32[]{:S(2)}, u32[]{:S(2)}) collective-permute-start(bf16[4,4096]{1,0:T(4,128)(2,1)S(1)} %fold.4), channel_id=1, source_target_pairs={{0,8},{4,12},{8,0},{12,4},{1,9},{5,13},{9,1},{13,5},{2,10},{6,14},... | collective-permute-start | bytes 98312 | tf_op jit(solution)/shard_map/ppermute | solution.py:227
  24.0 1.4 %collective-permute-start.11 = (bf16[4,4096]{1,0:T(4,128)(2,1)S(1)}, bf16[4,4096]{1,0:T(4,128)(2,1)S(1)}, u32[]{:S(2)}, u32[]{:S(2)}) collective-permute-start(bf16[4,4096]{1,0:T(4,128)(2,1)S(1)} %fold.5), channel_id=1, source_target_pairs={{0,12},{4,0},{8,4},{12,8},{1,13},{5,1},{9,5},{13,9},{2,14},{6,2},{... | collective-permute-start | bytes 98312 | tf_op jit(solution)/shard_map/ppermute | solution.py:227
  25.4 0.9 %collective-permute-done.7.refs_2_ = bf16[4,4096]{1,0:T(4,128)(2,1)S(1)} collective-permute-done((bf16[4,4096]{1,0:T(4,128)(2,1)S(1)}, bf16[4,4096]{1,0:T(4,128)(2,1)S(1)}, u32[]{:S(2)}, u32[]{:S(2)}) %collective-permute-start.7) | collective-permute-done | bytes 32800 | tf_op jit(solution)/shard_map/ppermute | solution.py:227
  26.3 0.5 %collective-permute-done.9.refs_3_ = bf16[4,4096]{1,0:T(4,128)(2,1)S(1)} collective-permute-done((bf16[4,4096]{1,0:T(4,128)(2,1)S(1)}, bf16[4,4096]{1,0:T(4,128)(2,1)S(1)}, u32[]{:S(2)}, u32[]{:S(2)}) %collective-permute-start.9) | collective-permute-done | bytes 32800 | tf_op jit(solution)/shard_map/ppermute | solution.py:227
  26.8 1.2 %collective-permute-done.11.refs_4_ = bf16[4,4096]{1,0:T(4,128)(2,1)S(1)} collective-permute-done((bf16[4,4096]{1,0:T(4,128)(2,1)S(1)}, bf16[4,4096]{1,0:T(4,128)(2,1)S(1)}, u32[]{:S(2)}, u32[]{:S(2)}) %collective-permute-start.11) | collective-permute-done | bytes 32800 | tf_op jit(solution)/shard_map/ppermute | solution.py:227
  28.0 0.7 %mix.1 = bf16[4,4096]{1,0:T(4,128)(2,1)} custom-call(s32[2,16]{1,0:T(2,128)S(1)} %bitcast.2, f32[2,4]{1,0:T(2,128)S(1)} %bitcast.3, f32[4,4096]{1,0:T(4,128)S(1)} %get-tuple-element.21.refs_0_, bf16[4,4096]{1,0:T(4,128)(2,1)S(1)} %collective-permute-done.4.refs_1_, bf16[4,4096]{1,0:T(4,128)(2,1)S(1)} %collective-permute-done.7.refs_2_, ...), custom_call_target="tpu_custom_call" | custom-call | tf_op jit(solution)/shard_map/mix/pallas_call | solution.py:229
  (20 shorter events, 0.2 us)
Async XLA Ops:
  0.0 10.8 %collective-permute-start.1 = (bf16[16,4096]{1,0:T(8,128)(2,1)}, bf16[16,4096]{1,0:T(8,128)(2,1)S(1)}, u32[]{:S(2)}, u32[]{:S(2)}) collective-permute-start(bf16[16,4096]{1,0:T(8,128)(2,1)} %tokens.1), channel_id=1, source_target_pairs={{0,8},{1,13},{2,10},{3,15},{4,12},{5,9},{6,14},{7,11},{8,0},{9,5},... | collective-permute-start | bytes 393224 | tf_op jit(solution)/shard_map/ppermute | solution.py:155
  4.0 7.6 %collective-permute-start = (bf16[16,4096]{1,0:T(8,128)(2,1)}, bf16[16,4096]{1,0:T(8,128)(2,1)S(1)}, u32[]{:S(2)}, u32[]{:S(2)}) collective-permute-start(bf16[16,4096]{1,0:T(8,128)(2,1)} %tokens.1), channel_id=1, source_target_pairs={{0,4},{4,0},{8,12},{12,8},{1,5},{5,1},{9,13},{13,9},{2,6},{6,2},{1... | collective-permute-start | bytes 393224 | tf_op jit(solution)/shard_map/ppermute | solution.py:156
  6.6 5.6 %copy-start = (bf16[1,384,4096]{2,1,0:T(8,128)(2,1)S(1)}, bf16[1,384,4096]{2,1,0:T(8,128)(2,1)}, u32[]{:S(2)}) copy-start(bf16[1,384,4096]{2,1,0:T(8,128)(2,1)} %w_down.1) | copy-start | bytes 9437188
  6.6 5.6 %copy-start.1 = (bf16[1,384,4096]{2,1,0:T(8,128)(2,1)S(1)}, bf16[1,384,4096]{2,1,0:T(8,128)(2,1)}, u32[]{:S(2)}) copy-start(bf16[1,384,4096]{2,1,0:T(8,128)(2,1)} %refs_2_.1) | copy-start | bytes 9437188
  6.6 5.6 %copy-start.2 = (bf16[1,384,4096]{2,1,0:T(8,128)(2,1)S(1)}, bf16[1,384,4096]{2,1,0:T(8,128)(2,1)}, u32[]{:S(2)}) copy-start(bf16[1,384,4096]{2,1,0:T(8,128)(2,1)} %refs_3_.1) | copy-start | bytes 9437188
  10.8 1.3 %collective-permute-start.2 = (bf16[16,4096]{1,0:T(8,128)(2,1)S(1)}, bf16[16,4096]{1,0:T(8,128)(2,1)S(1)}, u32[]{:S(2)}, u32[]{:S(2)}) collective-permute-start(bf16[16,4096]{1,0:T(8,128)(2,1)S(1)} %collective-permute-done.1.refs_0_), channel_id=1, source_target_pairs={{0,1},{1,0},{2,3},{3,2},{4,5},{5,4},{6,7},{7,6},{8,9},{9,8},{10,11... | collective-permute-start | bytes 393224 | tf_op jit(solution)/shard_map/ppermute | solution.py:157
  14.7 13.3 %copy-start.3 = (s32[16,2]{0,1:T(2,128)S(1)}, s32[16,2]{0,1:T(2,128)}, u32[]{:S(2)}) copy-start(s32[16,2]{0,1:T(2,128)} %param.7) | copy-start | bytes 388
  14.7 13.3 %copy-start.4 = (f32[4,2]{0,1:T(2,128)S(1)}, f32[4,2]{0,1:T(2,128)}, u32[]{:S(2)}) copy-start(f32[4,2]{0,1:T(2,128)} %param.8) | copy-start | bytes 100
  14.7 1.4 %collective-permute-start.5 = (bf16[16,4096]{1,0:T(8,128)(2,1)S(1)}, bf16[16,4096]{1,0:T(8,128)(2,1)S(1)}, u32[]{:S(2)}, u32[]{:S(2)}) collective-permute-start(bf16[16,4096]{1,0:T(8,128)(2,1)S(1)} %get-tuple-element.24), channel_id=1, source_target_pairs={{0,1},{1,0},{2,3},{3,2},{4,5},{5,4},{6,7},{7,6},{8,9},{9,8},{10,11... | collective-permute-start | bytes 393224 | tf_op jit(solution)/shard_map/ppermute | solution.py:199
  15.6 2.7 %collective-permute-start.3 = (bf16[16,4096]{1,0:T(8,128)(2,1)S(1)}, bf16[16,4096]{1,0:T(8,128)(2,1)S(1)}, u32[]{:S(2)}, u32[]{:S(2)}) collective-permute-start(bf16[16,4096]{1,0:T(8,128)(2,1)S(1)} %get-tuple-element.20), channel_id=1, source_target_pairs={{0,1},{1,0},{2,3},{3,2},{4,5},{5,4},{6,7},{7,6},{8,9},{9,8},{10,11... | collective-permute-start | bytes 393224 | tf_op jit(solution)/shard_map/ppermute | solution.py:199
  16.2 4.2 %collective-permute-start.6 = (bf16[4,4096]{1,0:T(4,128)(2,1)S(1)}, bf16[4,4096]{1,0:T(4,128)(2,1)S(1)}, u32[]{:S(2)}, u32[]{:S(2)}) collective-permute-start(bf16[4,4096]{1,0:T(4,128)(2,1)S(1)} %get-tuple-element.26), channel_id=1, source_target_pairs={{0,2},{1,3},{2,0},{3,1},{4,6},{5,7},{6,4},{7,5},{8,10},{9,11},{10,... | collective-permute-start | bytes 98312 | tf_op jit(solution)/shard_map/ppermute | solution.py:204
  17.7 3.9 %collective-permute-start.8 = (bf16[4,4096]{1,0:T(4,128)(2,1)S(1)}, bf16[4,4096]{1,0:T(4,128)(2,1)S(1)}, u32[]{:S(2)}, u32[]{:S(2)}) collective-permute-start(bf16[4,4096]{1,0:T(4,128)(2,1)S(1)} %get-tuple-element.28), channel_id=1, source_target_pairs={{0,2},{1,3},{2,0},{3,1},{4,6},{5,7},{6,4},{7,5},{8,10},{9,11},{10,... | collective-permute-start | bytes 98312 | tf_op jit(solution)/shard_map/ppermute | solution.py:204
  18.3 5.7 %collective-permute-start.10 = (bf16[4,4096]{1,0:T(4,128)(2,1)S(1)}, bf16[4,4096]{1,0:T(4,128)(2,1)S(1)}, u32[]{:S(2)}, u32[]{:S(2)}) collective-permute-start(bf16[4,4096]{1,0:T(4,128)(2,1)S(1)} %get-tuple-element.30), channel_id=1, source_target_pairs={{0,2},{1,3},{2,0},{3,1},{4,6},{5,7},{6,4},{7,5},{8,10},{9,11},{10,... | collective-permute-start | bytes 98312 | tf_op jit(solution)/shard_map/ppermute | solution.py:204
  19.9 5.6 %collective-permute-start.4 = (bf16[4,4096]{1,0:T(4,128)(2,1)S(1)}, bf16[4,4096]{1,0:T(4,128)(2,1)S(1)}, u32[]{:S(2)}, u32[]{:S(2)}) collective-permute-start(bf16[4,4096]{1,0:T(4,128)(2,1)S(1)} %get-tuple-element.22), channel_id=1, source_target_pairs={{0,2},{1,3},{2,0},{3,1},{4,6},{5,7},{6,4},{7,5},{8,10},{9,11},{10,... | collective-permute-start | bytes 98312 | tf_op jit(solution)/shard_map/ppermute | solution.py:223
  20.4 5.9 %collective-permute-start.7 = (bf16[4,4096]{1,0:T(4,128)(2,1)S(1)}, bf16[4,4096]{1,0:T(4,128)(2,1)S(1)}, u32[]{:S(2)}, u32[]{:S(2)}) collective-permute-start(bf16[4,4096]{1,0:T(4,128)(2,1)S(1)} %fold.3), channel_id=1, source_target_pairs={{0,4},{4,8},{8,12},{12,0},{1,5},{5,9},{9,13},{13,1},{2,6},{6,10},{... | collective-permute-start | bytes 98312 | tf_op jit(solution)/shard_map/ppermute | solution.py:227
  21.7 5.1 %collective-permute-start.9 = (bf16[4,4096]{1,0:T(4,128)(2,1)S(1)}, bf16[4,4096]{1,0:T(4,128)(2,1)S(1)}, u32[]{:S(2)}, u32[]{:S(2)}) collective-permute-start(bf16[4,4096]{1,0:T(4,128)(2,1)S(1)} %fold.4), channel_id=1, source_target_pairs={{0,8},{4,12},{8,0},{12,4},{1,9},{5,13},{9,1},{13,5},{2,10},{6,14},... | collective-permute-start | bytes 98312 | tf_op jit(solution)/shard_map/ppermute | solution.py:227
  24.0 4.0 %collective-permute-start.11 = (bf16[4,4096]{1,0:T(4,128)(2,1)S(1)}, bf16[4,4096]{1,0:T(4,128)(2,1)S(1)}, u32[]{:S(2)}, u32[]{:S(2)}) collective-permute-start(bf16[4,4096]{1,0:T(4,128)(2,1)S(1)} %fold.5), channel_id=1, source_target_pairs={{0,12},{4,0},{8,4},{12,8},{1,13},{5,1},{9,5},{13,9},{2,14},{6,2},{... | collective-permute-start | bytes 98312 | tf_op jit(solution)/shard_map/ppermute | solution.py:227

commit v25 on v24

--- a/solution.py
+++ b/solution.py
@@ -42,7 +42,7 @@
 
 def ffn_kernel(n_expert, parts, own, next_block, order, *refs):
     far = refs[: n_expert - 2]
-    w_gate, w_up, w_down, kept, sent, rest, x = refs[n_expert - 2 :]
+    w_gate, w_up, w_down, *outs, x = refs[n_expert - 2 :]
     core = lax.rem(lax.axis_index("etp"), 2)
     tok = own.shape[0]
     x[0:tok, :] = own[...]
@@ -56,23 +56,13 @@
     hidden = (gate / (1.0 + jnp.exp(-gate)) * upper).astype(jnp.bfloat16)
     hidden = lax.dot_general(order[...], hidden, contract, preferred_element_type=jnp.float32)
     hidden = hidden.astype(jnp.bfloat16)
-    now = rest.shape[0]
-    rest[...] = hidden[now:]
-    down(parts, hidden[:now], w_down, kept, sent)
-
-
-def down(parts, hidden, w_down, kept, sent):
-    side, width = kept.shape
+    side, width = outs[0].shape
     step = width // parts
     for c in range(parts):
         cols = slice(c * step, (c + 1) * step)
-        out = jnp.dot(hidden, w_down[0, :, cols], preferred_element_type=jnp.float32)
-        kept[:, cols] = out[:side]
-        sent[:, cols] = out[side:].astype(jnp.bfloat16)
-
-
-def down_kernel(parts, hidden, w_down, kept, sent):
-    down(parts, hidden[...], w_down, kept, sent)
+        rows = jnp.dot(hidden, w_down[0, :, cols], preferred_element_type=jnp.float32)
+        for i, out in enumerate(outs):
+            out[:, cols] = rows[i * side : (i + 1) * side].astype(out.dtype)
 
 
 def add_kernel(pairs, kept, arrived, *refs):
@@ -161,23 +151,15 @@
         jax.ShapeDtypeStruct((side // 2, width), jnp.float32),
         jax.ShapeDtypeStruct((side // 2, width), jnp.bfloat16),
     ]
-    far_kept, far_sent, rest = pl.pallas_call(
+    far_kept, far_sent, near_kept, near_sent = pl.pallas_call(
         functools.partial(ffn_kernel, n_expert, parts),
-        out_shape=halves + [jax.ShapeDtypeStruct((side, w_gate.shape[1]), jnp.bfloat16)],
+        out_shape=halves * 2,
         in_specs=[VMEM] * (n_expert + 4),
-        out_specs=[VMEM] * 3,
+        out_specs=[VMEM] * 4,
         scratch_shapes=[pltpu.VMEM((n_expert * tok, width), jnp.bfloat16)],
         compiler_params=GRANT,
         name="ffn",
     )(own, next_block, order, *far, w_gate, w_up, w_down)
-    near_kept, near_sent = pl.pallas_call(
-        functools.partial(down_kernel, parts),
-        out_shape=halves,
-        in_specs=[VMEM] * 2,
-        out_specs=[VMEM] * 2,
-        compiler_params=GRANT,
-        name="down",
-    )(rest, w_down)
 
     turns = [
         [(t, 2 * ((t // 2 + h) % pairs) + t % 2) for t in range(n_etp)] for h in range(1, pairs)
@@ -215,6 +197,7 @@
 
     half = n_expert // 2
     first, second = add(far_kept, far_sent, (half // 2, half - half // 2))
+    near_kept, first, second = lax.optimization_barrier((near_kept, first, second))
     pieces = over_pairs(*first) + over_pairs(*second)
     own, last = add(near_kept, near_sent, (1, half - 1))
     last = over_pairs(*last)

time: 28.9 us -> 28.9 us (level)
  waiting for transfers between devices: 8.26 us -> 8.9 us
  Pallas kernels: 5.04 us -> 4.41 us
    ppermute x2, waiting for transfers between devices: 0.17 us -> 0.84 us  [add(): lax.ppermute(sent, 'etp', swap)]
    pallas_call x1 -> x0, Pallas kernels: 0.64 us -> none  [on_device(): pl.pallas_call(functools.partial(down_kernel, parts), out_shape=halves, i...]
  transfers between devices with their start and end apart: 12 -> 12, of which waited for: 7 -> 7; matrix products, arithmetic and copies ran while one was open for 0% -> 0% of each run, Pallas kernels for 6% -> 4%
where the time goes in v25:
time: 28.9 us; the launch traced here: 28.8 us
  starting transfers between devices  15.3 us (53%)
  waiting for transfers between devices  8.9 us (31%)
  Pallas kernels  4.41 us (15%)
    ppermute x3, starting transfers between devices, on_device(): landed.append(lax.ppermute(piece, 'expert', route))  4.94 us
    ppermute x1, waiting for transfers between devices, on_device(): far.append(lax.ppermute(tokens, ('expert', 'etp'), route))  4.22 us
    ppermute x1, starting transfers between devices, on_device(): far.append(lax.ppermute(tokens, ('expert', 'etp'), route))  4.04 us
    ppermute x3, starting transfers between devices, over_pairs(): lax.ppermute(piece, 'etp', turn)  3.65 us
    ppermute x3, waiting for transfers between devices, on_device(): landed.append(lax.ppermute(piece, 'expert', route))  2.57 us
    pallas_call x1, Pallas kernels, on_device(): pl.pallas_call(functools.partial(ffn_kernel, n_expert, parts), out_shape=...  2.54 us
    ppermute x1, starting transfers between devices, on_device(): lax.ppermute(tokens, 'expert', [(e, e ^ 1) for e in range(n_expert)])  1.58 us
    pallas_call x1, Pallas kernels, on_device(): pl.pallas_call(fetch_kernel, out_shape=jax.ShapeDtypeStruct((tok, width),...  0.95 us
  transfers between devices with their start and end apart: 12, of which 7 were waited for; matrix products, arithmetic and copies ran while one was open for 0% of the time, Pallas kernels for 4%

profile of v25, /device:TPU:0, one launch (start us, length us, event | category | flops | bytes accessed | tf_op | source)
XLA Modules:
  0.0 28.8 jit_solution(15460896455446258405)
XLA Ops:
  0.0 4.0 %collective-permute-start.1 = (bf16[16,4096]{1,0:T(8,128)(2,1)}, bf16[16,4096]{1,0:T(8,128)(2,1)S(1)}, u32[]{:S(2)}, u32[]{:S(2)}) collective-permute-start(bf16[16,4096]{1,0:T(8,128)(2,1)} %tokens.1), channel_id=1, source_target_pairs={{0,8},{1,13},{2,10},{3,15},{4,12},{5,9},{6,14},{7,11},{8,0},{9,5},... | collective-permute-start | bytes 393224 | tf_op jit(solution)/shard_map/ppermute | solution.py:145
  4.0 1.6 %collective-permute-start = (bf16[16,4096]{1,0:T(8,128)(2,1)}, bf16[16,4096]{1,0:T(8,128)(2,1)S(1)}, u32[]{:S(2)}, u32[]{:S(2)}) collective-permute-start(bf16[16,4096]{1,0:T(8,128)(2,1)} %tokens.1), channel_id=1, source_target_pairs={{0,4},{4,0},{8,12},{12,8},{1,5},{5,1},{9,13},{13,9},{2,6},{6,2},{1... | collective-permute-start | bytes 393224 | tf_op jit(solution)/shard_map/ppermute | solution.py:146
  5.6 0.9 %fetch.1.own = bf16[16,4096]{1,0:T(8,128)(2,1)S(1)} custom-call(bf16[16,4096]{1,0:T(8,128)(2,1)} %tokens.1), custom_call_target="tpu_custom_call" | custom-call | tf_op jit(solution)/shard_map/fetch/pallas_call | solution.py:118
  6.6 0.0 copy-start.2
  6.6 4.2 %collective-permute-done.1.refs_0_ = bf16[16,4096]{1,0:T(8,128)(2,1)S(1)} collective-permute-done((bf16[16,4096]{1,0:T(8,128)(2,1)}, bf16[16,4096]{1,0:T(8,128)(2,1)S(1)}, u32[]{:S(2)}, u32[]{:S(2)}) %collective-permute-start.1) | collective-permute-done | bytes 131104 | tf_op jit(solution)/shard_map/ppermute | solution.py:145
  10.8 0.1 order.1
  10.9 0.0 copy-start.3
  10.9 0.7 %collective-permute-done.next_block = bf16[16,4096]{1,0:T(8,128)(2,1)S(1)} collective-permute-done((bf16[16,4096]{1,0:T(8,128)(2,1)}, bf16[16,4096]{1,0:T(8,128)(2,1)S(1)}, u32[]{:S(2)}, u32[]{:S(2)}) %collective-permute-start) | collective-permute-done | bytes 131104 | tf_op jit(solution)/shard_map/ppermute | solution.py:146
  11.6 0.6 %collective-permute-done.2.refs_1_ = bf16[16,4096]{1,0:T(8,128)(2,1)S(1)} collective-permute-done((bf16[16,4096]{1,0:T(8,128)(2,1)S(1)}, bf16[16,4096]{1,0:T(8,128)(2,1)S(1)}, u32[]{:S(2)}, u32[]{:S(2)}) %collective-permute-start.2) | collective-permute-done | bytes 131104 | tf_op jit(solution)/shard_map/ppermute | solution.py:147
  12.2 2.5 %ffn.1 = (f32[16,4096]{1,0:T(8,128)S(1)}, bf16[16,4096]{1,0:T(8,128)(2,1)S(1)}, f32[16,4096]{1,0:T(8,128)S(1)}, bf16[16,4096]{1,0:T(8,128)(2,1)S(1)}) custom-call(bf16[16,4096]{1,0:T(8,128)(2,1)S(1)} %fetch.1.own, bf16[16,4096]{1,0:T(8,128)(2,1)S(1)} %collective-permute-done.next_block, bf16[64,64]{1,0:T(8,128)(2,1)S(1)} %order.1, ...), custom_call_target="tpu_custom_call" | custom-call | tf_op jit(solution)/shard_map/ffn/pallas_call | solution.py:154
  14.7 0.2 collective-permute-start.3
  14.9 0.4 %collective-permute-start.4 = (bf16[16,4096]{1,0:T(8,128)(2,1)S(1)}, bf16[16,4096]{1,0:T(8,128)(2,1)S(1)}, u32[]{:S(2)}, u32[]{:S(2)}) collective-permute-start(bf16[16,4096]{1,0:T(8,128)(2,1)S(1)} %get-tuple-element.30), channel_id=1, source_target_pairs={{0,1},{1,0},{2,3},{3,2},{4,5},{5,4},{6,7},{7,6},{8,9},{9,8},{10,11... | collective-permute-start | bytes 393224 | tf_op jit(solution)/shard_map/ppermute | solution.py:181
  15.3 0.8 %collective-permute-done.3.arrived = bf16[16,4096]{1,0:T(8,128)(2,1)S(1)} collective-permute-done((bf16[16,4096]{1,0:T(8,128)(2,1)S(1)}, bf16[16,4096]{1,0:T(8,128)(2,1)S(1)}, u32[]{:S(2)}, u32[]{:S(2)}) %collective-permute-start.3) | collective-permute-done | bytes 131104 | tf_op jit(solution)/shard_map/ppermute | solution.py:181
  16.2 1.6 %collective-permute-start.6 = (bf16[4,4096]{1,0:T(4,128)(2,1)S(1)}, bf16[4,4096]{1,0:T(4,128)(2,1)S(1)}, u32[]{:S(2)}, u32[]{:S(2)}) collective-permute-start(bf16[4,4096]{1,0:T(4,128)(2,1)S(1)} %get-tuple-element.34), channel_id=1, source_target_pairs={{0,2},{1,3},{2,0},{3,1},{4,6},{5,7},{6,4},{7,5},{8,10},{9,11},{10,... | collective-permute-start | bytes 98312 | tf_op jit(solution)/shard_map/ppermute | solution.py:186
  17.7 0.5 %collective-permute-start.8 = (bf16[4,4096]{1,0:T(4,128)(2,1)S(1)}, bf16[4,4096]{1,0:T(4,128)(2,1)S(1)}, u32[]{:S(2)}, u32[]{:S(2)}) collective-permute-start(bf16[4,4096]{1,0:T(4,128)(2,1)S(1)} %get-tuple-element.36), channel_id=1, source_target_pairs={{0,2},{1,3},{2,0},{3,1},{4,6},{5,7},{6,4},{7,5},{8,10},{9,11},{10,... | collective-permute-start | bytes 98312 | tf_op jit(solution)/shard_map/ppermute | solution.py:186
  18.3 1.6 %collective-permute-start.10 = (bf16[4,4096]{1,0:T(4,128)(2,1)S(1)}, bf16[4,4096]{1,0:T(4,128)(2,1)S(1)}, u32[]{:S(2)}, u32[]{:S(2)}) collective-permute-start(bf16[4,4096]{1,0:T(4,128)(2,1)S(1)} %get-tuple-element.38), channel_id=1, source_target_pairs={{0,2},{1,3},{2,0},{3,1},{4,6},{5,7},{6,4},{7,5},{8,10},{9,11},{10,... | collective-permute-start | bytes 98312 | tf_op jit(solution)/shard_map/ppermute | solution.py:186
  19.9 0.5 %collective-permute-start.5 = (bf16[4,4096]{1,0:T(4,128)(2,1)S(1)}, bf16[4,4096]{1,0:T(4,128)(2,1)S(1)}, u32[]{:S(2)}, u32[]{:S(2)}) collective-permute-start(bf16[4,4096]{1,0:T(4,128)(2,1)S(1)} %get-tuple-element.32), channel_id=1, source_target_pairs={{0,2},{1,3},{2,0},{3,1},{4,6},{5,7},{6,4},{7,5},{8,10},{9,11},{10,... | collective-permute-start | bytes 98312 | tf_op jit(solution)/shard_map/ppermute | solution.py:206
  20.4 1.2 %collective-permute-start.7 = (bf16[4,4096]{1,0:T(4,128)(2,1)S(1)}, bf16[4,4096]{1,0:T(4,128)(2,1)S(1)}, u32[]{:S(2)}, u32[]{:S(2)}) collective-permute-start(bf16[4,4096]{1,0:T(4,128)(2,1)S(1)} %fold.3), channel_id=1, source_target_pairs={{0,4},{4,8},{8,12},{12,0},{1,5},{5,9},{9,13},{13,1},{2,6},{6,10},{... | collective-permute-start | bytes 98312 | tf_op jit(solution)/shard_map/ppermute | solution.py:210
  21.7 2.3 %collective-permute-start.9 = (bf16[4,4096]{1,0:T(4,128)(2,1)S(1)}, bf16[4,4096]{1,0:T(4,128)(2,1)S(1)}, u32[]{:S(2)}, u32[]{:S(2)}) collective-permute-start(bf16[4,4096]{1,0:T(4,128)(2,1)S(1)} %fold.4), channel_id=1, source_target_pairs={{0,8},{4,12},{8,0},{12,4},{1,9},{5,13},{9,1},{13,5},{2,10},{6,14},... | collective-permute-start | bytes 98312 | tf_op jit(solution)/shard_map/ppermute | solution.py:210
  24.0 1.4 %collective-permute-start.11 = (bf16[4,4096]{1,0:T(4,128)(2,1)S(1)}, bf16[4,4096]{1,0:T(4,128)(2,1)S(1)}, u32[]{:S(2)}, u32[]{:S(2)}) collective-permute-start(bf16[4,4096]{1,0:T(4,128)(2,1)S(1)} %fold.5), channel_id=1, source_target_pairs={{0,12},{4,0},{8,4},{12,8},{1,13},{5,1},{9,5},{13,9},{2,14},{6,2},{... | collective-permute-start | bytes 98312 | tf_op jit(solution)/shard_map/ppermute | solution.py:210
  25.4 0.9 %collective-permute-done.7.refs_2_ = bf16[4,4096]{1,0:T(4,128)(2,1)S(1)} collective-permute-done((bf16[4,4096]{1,0:T(4,128)(2,1)S(1)}, bf16[4,4096]{1,0:T(4,128)(2,1)S(1)}, u32[]{:S(2)}, u32[]{:S(2)}) %collective-permute-start.7) | collective-permute-done | bytes 32800 | tf_op jit(solution)/shard_map/ppermute | solution.py:210
  26.3 0.5 %collective-permute-done.9.refs_3_ = bf16[4,4096]{1,0:T(4,128)(2,1)S(1)} collective-permute-done((bf16[4,4096]{1,0:T(4,128)(2,1)S(1)}, bf16[4,4096]{1,0:T(4,128)(2,1)S(1)}, u32[]{:S(2)}, u32[]{:S(2)}) %collective-permute-start.9) | collective-permute-done | bytes 32800 | tf_op jit(solution)/shard_map/ppermute | solution.py:210
  26.8 1.2 %collective-permute-done.11.refs_4_ = bf16[4,4096]{1,0:T(4,128)(2,1)S(1)} collective-permute-done((bf16[4,4096]{1,0:T(4,128)(2,1)S(1)}, bf16[4,4096]{1,0:T(4,128)(2,1)S(1)}, u32[]{:S(2)}, u32[]{:S(2)}) %collective-permute-start.11) | collective-permute-done | bytes 32800 | tf_op jit(solution)/shard_map/ppermute | solution.py:210
  28.0 0.7 %mix.1 = bf16[4,4096]{1,0:T(4,128)(2,1)} custom-call(s32[2,16]{1,0:T(2,128)S(1)} %bitcast.2, f32[2,4]{1,0:T(2,128)S(1)} %bitcast.3, f32[4,4096]{1,0:T(4,128)S(1)} %get-tuple-element.31.refs_0_, bf16[4,4096]{1,0:T(4,128)(2,1)S(1)} %collective-permute-done.5.refs_1_, bf16[4,4096]{1,0:T(4,128)(2,1)S(1)} %collective-permute-done.7.refs_2_, ...), custom_call_target="tpu_custom_call" | custom-call | tf_op jit(solution)/shard_map/mix/pallas_call | solution.py:212
  (19 shorter events, 0.2 us)
Async XLA Ops:
  0.0 10.8 %collective-permute-start.1 = (bf16[16,4096]{1,0:T(8,128)(2,1)}, bf16[16,4096]{1,0:T(8,128)(2,1)S(1)}, u32[]{:S(2)}, u32[]{:S(2)}) collective-permute-start(bf16[16,4096]{1,0:T(8,128)(2,1)} %tokens.1), channel_id=1, source_target_pairs={{0,8},{1,13},{2,10},{3,15},{4,12},{5,9},{6,14},{7,11},{8,0},{9,5},... | collective-permute-start | bytes 393224 | tf_op jit(solution)/shard_map/ppermute | solution.py:145
  4.0 7.6 %collective-permute-start = (bf16[16,4096]{1,0:T(8,128)(2,1)}, bf16[16,4096]{1,0:T(8,128)(2,1)S(1)}, u32[]{:S(2)}, u32[]{:S(2)}) collective-permute-start(bf16[16,4096]{1,0:T(8,128)(2,1)} %tokens.1), channel_id=1, source_target_pairs={{0,4},{4,0},{8,12},{12,8},{1,5},{5,1},{9,13},{13,9},{2,6},{6,2},{1... | collective-permute-start | bytes 393224 | tf_op jit(solution)/shard_map/ppermute | solution.py:146
  6.6 5.6 %copy-start = (bf16[1,384,4096]{2,1,0:T(8,128)(2,1)S(1)}, bf16[1,384,4096]{2,1,0:T(8,128)(2,1)}, u32[]{:S(2)}) copy-start(bf16[1,384,4096]{2,1,0:T(8,128)(2,1)} %refs_2_.1) | copy-start | bytes 9437188
  6.6 5.6 %copy-start.1 = (bf16[1,384,4096]{2,1,0:T(8,128)(2,1)S(1)}, bf16[1,384,4096]{2,1,0:T(8,128)(2,1)}, u32[]{:S(2)}) copy-start(bf16[1,384,4096]{2,1,0:T(8,128)(2,1)} %refs_3_.1) | copy-start | bytes 9437188
  6.6 5.6 %copy-start.2 = (bf16[1,384,4096]{2,1,0:T(8,128)(2,1)S(1)}, bf16[1,384,4096]{2,1,0:T(8,128)(2,1)}, u32[]{:S(2)}) copy-start(bf16[1,384,4096]{2,1,0:T(8,128)(2,1)} %refs_4_.1) | copy-start | bytes 9437188
  10.8 1.3 %collective-permute-start.2 = (bf16[16,4096]{1,0:T(8,128)(2,1)S(1)}, bf16[16,4096]{1,0:T(8,128)(2,1)S(1)}, u32[]{:S(2)}, u32[]{:S(2)}) collective-permute-start(bf16[16,4096]{1,0:T(8,128)(2,1)S(1)} %collective-permute-done.1.refs_0_), channel_id=1, source_target_pairs={{0,1},{1,0},{2,3},{3,2},{4,5},{5,4},{6,7},{7,6},{8,9},{9,8},{10,11... | collective-permute-start | bytes 393224 | tf_op jit(solution)/shard_map/ppermute | solution.py:147
  10.9 17.1 %copy-start.3 = (s32[16,2]{0,1:T(2,128)S(1)}, s32[16,2]{0,1:T(2,128)}, u32[]{:S(2)}) copy-start(s32[16,2]{0,1:T(2,128)} %param.7) | copy-start | bytes 388
  10.9 17.1 %copy-start.4 = (f32[4,2]{0,1:T(2,128)S(1)}, f32[4,2]{0,1:T(2,128)}, u32[]{:S(2)}) copy-start(f32[4,2]{0,1:T(2,128)} %param.8) | copy-start | bytes 100
  14.7 1.4 %collective-permute-start.3 = (bf16[16,4096]{1,0:T(8,128)(2,1)S(1)}, bf16[16,4096]{1,0:T(8,128)(2,1)S(1)}, u32[]{:S(2)}, u32[]{:S(2)}) collective-permute-start(bf16[16,4096]{1,0:T(8,128)(2,1)S(1)} %get-tuple-element.24), channel_id=1, source_target_pairs={{0,1},{1,0},{2,3},{3,2},{4,5},{5,4},{6,7},{7,6},{8,9},{9,8},{10,11... | collective-permute-start | bytes 393224 | tf_op jit(solution)/shard_map/ppermute | solution.py:181
  14.9 3.3 %collective-permute-start.4 = (bf16[16,4096]{1,0:T(8,128)(2,1)S(1)}, bf16[16,4096]{1,0:T(8,128)(2,1)S(1)}, u32[]{:S(2)}, u32[]{:S(2)}) collective-permute-start(bf16[16,4096]{1,0:T(8,128)(2,1)S(1)} %get-tuple-element.30), channel_id=1, source_target_pairs={{0,1},{1,0},{2,3},{3,2},{4,5},{5,4},{6,7},{7,6},{8,9},{9,8},{10,11... | collective-permute-start | bytes 393224 | tf_op jit(solution)/shard_map/ppermute | solution.py:181
  16.2 4.2 %collective-permute-start.6 = (bf16[4,4096]{1,0:T(4,128)(2,1)S(1)}, bf16[4,4096]{1,0:T(4,128)(2,1)S(1)}, u32[]{:S(2)}, u32[]{:S(2)}) collective-permute-start(bf16[4,4096]{1,0:T(4,128)(2,1)S(1)} %get-tuple-element.34), channel_id=1, source_target_pairs={{0,2},{1,3},{2,0},{3,1},{4,6},{5,7},{6,4},{7,5},{8,10},{9,11},{10,... | collective-permute-start | bytes 98312 | tf_op jit(solution)/shard_map/ppermute | solution.py:186
  17.7 3.9 %collective-permute-start.8 = (bf16[4,4096]{1,0:T(4,128)(2,1)S(1)}, bf16[4,4096]{1,0:T(4,128)(2,1)S(1)}, u32[]{:S(2)}, u32[]{:S(2)}) collective-permute-start(bf16[4,4096]{1,0:T(4,128)(2,1)S(1)} %get-tuple-element.36), channel_id=1, source_target_pairs={{0,2},{1,3},{2,0},{3,1},{4,6},{5,7},{6,4},{7,5},{8,10},{9,11},{10,... | collective-permute-start | bytes 98312 | tf_op jit(solution)/shard_map/ppermute | solution.py:186
  18.3 5.7 %collective-permute-start.10 = (bf16[4,4096]{1,0:T(4,128)(2,1)S(1)}, bf16[4,4096]{1,0:T(4,128)(2,1)S(1)}, u32[]{:S(2)}, u32[]{:S(2)}) collective-permute-start(bf16[4,4096]{1,0:T(4,128)(2,1)S(1)} %get-tuple-element.38), channel_id=1, source_target_pairs={{0,2},{1,3},{2,0},{3,1},{4,6},{5,7},{6,4},{7,5},{8,10},{9,11},{10,... | collective-permute-start | bytes 98312 | tf_op jit(solution)/shard_map/ppermute | solution.py:186
  19.9 5.6 %collective-permute-start.5 = (bf16[4,4096]{1,0:T(4,128)(2,1)S(1)}, bf16[4,4096]{1,0:T(4,128)(2,1)S(1)}, u32[]{:S(2)}, u32[]{:S(2)}) collective-permute-start(bf16[4,4096]{1,0:T(4,128)(2,1)S(1)} %get-tuple-element.32), channel_id=1, source_target_pairs={{0,2},{1,3},{2,0},{3,1},{4,6},{5,7},{6,4},{7,5},{8,10},{9,11},{10,... | collective-permute-start | bytes 98312 | tf_op jit(solution)/shard_map/ppermute | solution.py:206
  20.4 5.9 %collective-permute-start.7 = (bf16[4,4096]{1,0:T(4,128)(2,1)S(1)}, bf16[4,4096]{1,0:T(4,128)(2,1)S(1)}, u32[]{:S(2)}, u32[]{:S(2)}) collective-permute-start(bf16[4,4096]{1,0:T(4,128)(2,1)S(1)} %fold.3), channel_id=1, source_target_pairs={{0,4},{4,8},{8,12},{12,0},{1,5},{5,9},{9,13},{13,1},{2,6},{6,10},{... | collective-permute-start | bytes 98312 | tf_op jit(solution)/shard_map/ppermute | solution.py:210
  21.7 5.1 %collective-permute-start.9 = (bf16[4,4096]{1,0:T(4,128)(2,1)S(1)}, bf16[4,4096]{1,0:T(4,128)(2,1)S(1)}, u32[]{:S(2)}, u32[]{:S(2)}) collective-permute-start(bf16[4,4096]{1,0:T(4,128)(2,1)S(1)} %fold.4), channel_id=1, source_target_pairs={{0,8},{4,12},{8,0},{12,4},{1,9},{5,13},{9,1},{13,5},{2,10},{6,14},... | collective-permute-start | bytes 98312 | tf_op jit(solution)/shard_map/ppermute | solution.py:210
  24.0 4.0 %collective-permute-start.11 = (bf16[4,4096]{1,0:T(4,128)(2,1)S(1)}, bf16[4,4096]{1,0:T(4,128)(2,1)S(1)}, u32[]{:S(2)}, u32[]{:S(2)}) collective-permute-start(bf16[4,4096]{1,0:T(4,128)(2,1)S(1)} %fold.5), channel_id=1, source_target_pairs={{0,12},{4,0},{8,4},{12,8},{1,13},{5,1},{9,5},{13,9},{2,14},{6,2},{... | collective-permute-start | bytes 98312 | tf_op jit(solution)/shard_map/ppermute | solution.py:210

commit v26 on v12

--- a/solution.py
+++ b/solution.py
@@ -13,22 +13,14 @@
 HBM = pl.BlockSpec(memory_space=pltpu.HBM)
 
 
-def fetch_kernel(tokens, own, mine, sems):
-    half = mine.shape[1]
-    core = lax.rem(lax.axis_index("etp"), 2)
-    cols = pl.ds(pl.multiple_of(core * half, half), half)
-    copies = [
-        pltpu.make_async_copy(tokens.at[:, cols], mine, sems.at[0]),
-        pltpu.make_async_copy(tokens, own, sems.at[1]),
-    ]
-    for copy in copies:
-        copy.start()
-    for copy in copies:
-        copy.wait()
-
-
-def order_kernel(n_expert, pairs, rows, mine, out):
-    del mine
+def fetch_kernel(tokens, own, sem):
+    copy = pltpu.make_async_copy(tokens, own, sem)
+    copy.start()
+    copy.wait()
+
+
+def order_kernel(n_expert, pairs, rows, own, out):
+    del own
     total = out.shape[0]
     me = lax.axis_index("etp")
     core, pair = lax.rem(me, 2), lax.div(me, 2)
@@ -49,15 +41,13 @@
     out[...] = jnp.where(source == wanted, 1.0, 0.0).astype(jnp.bfloat16)
 
 
-def ffn_kernel(n_expert, parts, own, next_block, next_swapped, order, *refs):
+def ffn_kernel(n_expert, parts, own, next_block, order, *refs):
     far = refs[: n_expert - 2]
     w_gate, w_up, w_down, kept, sent, rest, x = refs[n_expert - 2 :]
     core = lax.rem(lax.axis_index("etp"), 2)
     tok = own.shape[0]
     x[0:tok, :] = own[...]
-    half = next_block.shape[1]
-    for block, side in ((next_block, core), (next_swapped, 1 - core)):
-        x[tok : 2 * tok, pl.ds(pl.multiple_of(side * half, half), half)] = block[...]
+    x[tok : 2 * tok, :] = next_block[...]
     for i in range(0, n_expert - 2, 2):
         for block, k in ((far[i], i + 2 + core), (far[i + 1], i + 3 - core)):
             x[pl.ds(pl.multiple_of(k * tok, tok), tok), :] = block[...]
@@ -104,16 +94,15 @@
         piece[...] = total[k * rows : (k + 1) * rows].astype(piece.dtype)
 
 
-def pack_kernel(near_kept, near_landed, *refs):
+def pack_kernel(near_landed, *refs):
     far, out = refs[:-1], refs[-1]
-    rows = near_kept.shape[0] // 2
-    core = lax.rem(lax.axis_index("etp"), 2)
-    out[:rows] = jnp.where(core == 0, near_kept[rows:], near_landed[rows:])
+    rows = near_landed.shape[0] // 2
+    out[:rows] = near_landed[rows:]
     for i, piece in enumerate(far, 1):
         out[i * rows : (i + 1) * rows] = piece[rows:]
 
 
-def mix_kernel(ids, weights, swapped, near_kept, near_landed, *refs):
+def mix_kernel(ids, weights, swapped, near_landed, *refs):
     far, out = refs[:-1], refs[-1]
     rows = out.shape[0]
     me, expert = lax.axis_index("etp"), lax.axis_index("expert")
@@ -132,7 +121,7 @@
     total = None
     for i in range(len(far) + 1):
         if i == 0:
-            mine = jnp.where(core == 0, near_kept[:rows], near_landed[:rows])
+            mine = near_landed[:rows]
         else:
             mine = far[i - 1][:rows]
         for part, k in ((mine, 2 * i + core), (swapped[i * rows : (i + 1) * rows], 2 * i + 1 - core)):
@@ -151,15 +140,12 @@
     pairs = n_etp // 2
     side = n_expert * tok // 2
 
-    own, mine = pl.pallas_call(
+    own = pl.pallas_call(
         fetch_kernel,
-        out_shape=[
-            jax.ShapeDtypeStruct((tok, width), tokens.dtype),
-            jax.ShapeDtypeStruct((tok, width // 2), tokens.dtype),
-        ],
+        out_shape=jax.ShapeDtypeStruct((tok, width), tokens.dtype),
         in_specs=[HBM],
-        out_specs=[VMEM] * 2,
-        scratch_shapes=[pltpu.SemaphoreType.DMA((2,))],
+        out_specs=VMEM,
+        scratch_shapes=[pltpu.SemaphoreType.DMA],
         compiler_params=GRANT,
         name="fetch",
     )(pltpu.with_memory_space_constraint(tokens, pltpu.HBM))
@@ -171,8 +157,7 @@
         cost_estimate=AHEAD,
         compiler_params=GRANT,
         name="order",
-    )(mine)
-    mine, order = lax.optimization_barrier((mine, order))
+    )(own)
 
     swap = [(t, t ^ 1) for t in range(n_etp)]
     routes = [
@@ -184,8 +169,7 @@
         for k in range(2, n_expert, 2)
     ]
     far = [lax.ppermute(tokens, ("expert", "etp"), route) for route in routes]
-    next_block = lax.ppermute(mine, "expert", [(e, e ^ 1) for e in range(n_expert)])
-    near = [next_block, lax.ppermute(next_block, "etp", swap)]
+    next_block = lax.ppermute(tokens, "expert", [(e, e ^ 1) for e in range(n_expert)])
     far = [b for block in far for b in (block, lax.ppermute(block, "etp", swap))]
 
     parts = 4
@@ -197,12 +181,12 @@
         functools.partial(ffn_kernel, n_expert, parts),
         out_shape=halves(n_expert - 2)
         + [jax.ShapeDtypeStruct((2 * tok, w_gate.shape[1]), jnp.bfloat16)],
-        in_specs=[VMEM] * (n_expert + 5),
+        in_specs=[VMEM] * (n_expert + 4),
         out_specs=[VMEM] * 3,
         scratch_shapes=[pltpu.VMEM((n_expert * tok, width), jnp.bfloat16)],
         compiler_params=GRANT,
         name="ffn",
-    )(own, *near, order, *far, w_gate, w_up, w_down)
+    )(own, next_block, order, *far, w_gate, w_up, w_down)
     near_kept, near_sent = pl.pallas_call(
         functools.partial(down_kernel, parts),
         out_shape=halves(2),
@@ -244,27 +228,27 @@
     ]
     (near_kept,) = over_etp(near_kept, near_sent, 1)
     odd = [
-        (e * n_etp + t, (e ^ 1) * n_etp + t) for e in range(n_expert) for t in range(1, n_etp, 2)
+        (e * n_etp + t, (e ^ t % 2) * n_etp + t) for e in range(n_expert) for t in range(n_etp)
     ]
     near_landed = lax.ppermute(near_kept, ("expert", "etp"), odd)
     packed = pl.pallas_call(
         pack_kernel,
         out_shape=jax.ShapeDtypeStruct((twos * rows, width), jnp.bfloat16),
-        in_specs=[VMEM] * (twos + 1),
+        in_specs=[VMEM] * twos,
         out_specs=VMEM,
         compiler_params=GRANT,
         name="pack",
-    )(near_kept, near_landed, *far)
+    )(near_landed, *far)
     swapped = lax.ppermute(packed, "etp", swap)
 
     return pl.pallas_call(
         mix_kernel,
         out_shape=jax.ShapeDtypeStruct((rows, width), jnp.bfloat16),
-        in_specs=[VMEM] * (twos + 4),
+        in_specs=[VMEM] * (twos + 3),
         out_specs=VMEM,
         compiler_params=GRANT,
         name="mix",
-    )(expert_ids.T, route_weights.T, swapped, near_kept, near_landed, *far)
+    )(expert_ids.T, route_weights.T, swapped, near_landed, *far)
 
 
 def solution(mesh):

time: 29.8 us -> 29.1 us (0.977)
  starting transfers between devices: 12 us -> 11.3 us
    ppermute x1, waiting for transfers between devices: 3.87 us -> 3.24 us  [on_device(): lax.ppermute(piece, ('expert', 'etp'), route)]
    ppermute x1, waiting for transfers between devices: 0.01 us -> 0.56 us  [on_device(): lax.ppermute(block, 'etp', swap)]
    ppermute x2 -> x1, starting transfers between devices: 2.12 us -> 1.58 us  [on_device(): lax.ppermute(tokens, 'expert', [(e, e ^ 1) for e in range(n_expert)])]
    ppermute x2 -> x1, waiting for transfers between devices: 0.96 us -> 0.74 us  [on_device(): lax.ppermute(tokens, 'expert', [(e, e ^ 1) for e in range(n_expert)])]
  transfers between devices with their start and end apart: 11 -> 10, of which waited for: 7 -> 8; matrix products, arithmetic and copies ran while one was open for 0% -> 0% of each run, Pallas kernels for 6% -> 6%
where the time goes in v26:
time: 29.1 us; the launch traced here: 29 us
  waiting for transfers between devices  12.5 us (43%)
  starting transfers between devices  11.3 us (39%)
  Pallas kernels  5.03 us (17%)
    ppermute x1, waiting for transfers between devices, on_device(): far = [lax.ppermute(tokens, ('expert', 'etp'), route) for route in routes]  4.22 us
    ppermute x1, starting transfers between devices, on_device(): far = [lax.ppermute(tokens, ('expert', 'etp'), route) for route in routes]  4.04 us
    ppermute x1, waiting for transfers between devices, on_device(): lax.ppermute(piece, ('expert', 'etp'), route)  3.24 us
    ppermute x2, waiting for transfers between devices, over_etp(): lax.ppermute(piece, 'etp', turn)  2.7 us
    pallas_call x1, Pallas kernels, on_device(): pl.pallas_call(functools.partial(ffn_kernel, n_expert, parts), out_shape=...  2.53 us
    ppermute x2, starting transfers between devices, over_etp(): lax.ppermute(piece, 'etp', turn)  2.35 us
    ppermute x1, starting transfers between devices, on_device(): lax.ppermute(tokens, 'expert', [(e, e ^ 1) for e in range(n_expert)])  1.58 us
    ppermute x1, starting transfers between devices, on_device(): swapped = lax.ppermute(packed, 'etp', swap)  1.24 us
  transfers between devices with their start and end apart: 10, of which 8 were waited for; matrix products, arithmetic and copies ran while one was open for 0% of the time, Pallas kernels for 6%

profile of v26, /device:TPU:0, one launch (start us, length us, event | category | flops | bytes accessed | tf_op | source)
XLA Modules:
  0.0 29.0 jit_solution(10745919974317752395)
XLA Ops:
  0.0 4.0 %collective-permute-start.1 = (bf16[16,4096]{1,0:T(8,128)(2,1)}, bf16[16,4096]{1,0:T(8,128)(2,1)S(1)}, u32[]{:S(2)}, u32[]{:S(2)}) collective-permute-start(bf16[16,4096]{1,0:T(8,128)(2,1)} %tokens.1), channel_id=1, source_target_pairs={{0,8},{1,13},{2,10},{3,15},{4,12},{5,9},{6,14},{7,11},{8,0},{9,5},... | collective-permute-start | bytes 393224 | tf_op jit(solution)/shard_map/ppermute | solution.py:171
  4.0 1.6 %collective-permute-start = (bf16[16,4096]{1,0:T(8,128)(2,1)}, bf16[16,4096]{1,0:T(8,128)(2,1)S(1)}, u32[]{:S(2)}, u32[]{:S(2)}) collective-permute-start(bf16[16,4096]{1,0:T(8,128)(2,1)} %tokens.1), channel_id=1, source_target_pairs={{0,4},{4,0},{8,12},{12,8},{1,5},{5,1},{9,13},{13,9},{2,6},{6,2},{1... | collective-permute-start | bytes 393224 | tf_op jit(solution)/shard_map/ppermute | solution.py:172
  5.6 0.9 %fetch.1.own = bf16[16,4096]{1,0:T(8,128)(2,1)S(1)} custom-call(bf16[16,4096]{1,0:T(8,128)(2,1)} %tokens.1), custom_call_target="tpu_custom_call" | custom-call | tf_op jit(solution)/shard_map/fetch/pallas_call | solution.py:143
  6.6 0.0 copy-start.1
  6.6 0.0 copy-start.2
  6.6 4.2 %collective-permute-done.1.refs_0_ = bf16[16,4096]{1,0:T(8,128)(2,1)S(1)} collective-permute-done((bf16[16,4096]{1,0:T(8,128)(2,1)}, bf16[16,4096]{1,0:T(8,128)(2,1)S(1)}, u32[]{:S(2)}, u32[]{:S(2)}) %collective-permute-start.1) | collective-permute-done | bytes 131104 | tf_op jit(solution)/shard_map/ppermute | solution.py:171
  10.9 0.7 %collective-permute-done.next_block = bf16[16,4096]{1,0:T(8,128)(2,1)S(1)} collective-permute-done((bf16[16,4096]{1,0:T(8,128)(2,1)}, bf16[16,4096]{1,0:T(8,128)(2,1)S(1)}, u32[]{:S(2)}, u32[]{:S(2)}) %collective-permute-start) | collective-permute-done | bytes 131104 | tf_op jit(solution)/shard_map/ppermute | solution.py:172
  11.6 0.6 %collective-permute-done.2.refs_1_ = bf16[16,4096]{1,0:T(8,128)(2,1)S(1)} collective-permute-done((bf16[16,4096]{1,0:T(8,128)(2,1)S(1)}, bf16[16,4096]{1,0:T(8,128)(2,1)S(1)}, u32[]{:S(2)}, u32[]{:S(2)}) %collective-permute-start.2) | collective-permute-done | bytes 131104 | tf_op jit(solution)/shard_map/ppermute | solution.py:173
  12.2 2.5 %ffn.1 = (f32[16,4096]{1,0:T(8,128)S(1)}, bf16[16,4096]{1,0:T(8,128)(2,1)S(1)}, bf16[32,384]{1,0:T(8,128)(2,1)S(1)}) custom-call(bf16[16,4096]{1,0:T(8,128)(2,1)S(1)} %fetch.1.own, bf16[16,4096]{1,0:T(8,128)(2,1)S(1)} %collective-permute-done.next_block, bf16[64,64]{1,0:T(8,128)(2,1)S(1)} %order.1, bf16[16,4096]{1,0:T(8,128)(2,1)S(1)} %collective-permute-done.1.refs_0_, ...), custom_call_target="tpu_custom_call" | custom-call | tf_op jit(solution)/shard_map/ffn/pallas_call | solution.py:180
  14.7 0.0 copy-start.4
  14.7 0.2 collective-permute-start.6
  14.9 0.6 %down.1 = (f32[16,4096]{1,0:T(8,128)S(1)}, bf16[16,4096]{1,0:T(8,128)(2,1)S(1)}) custom-call(bf16[32,384]{1,0:T(8,128)(2,1)S(1)} %get-tuple-element.14.hidden, bf16[1,384,4096]{2,1,0:T(8,128)(2,1)S(1)} %copy-done), custom_call_target="tpu_custom_call" | custom-call | tf_op jit(solution)/shard_map/down/pallas_call | solution.py:190
  15.6 0.4 %collective-permute-start.3 = (bf16[16,4096]{1,0:T(8,128)(2,1)S(1)}, bf16[16,4096]{1,0:T(8,128)(2,1)S(1)}, u32[]{:S(2)}, u32[]{:S(2)}) collective-permute-start(bf16[16,4096]{1,0:T(8,128)(2,1)S(1)} %get-tuple-element.16), channel_id=1, source_target_pairs={{0,1},{1,0},{2,3},{3,2},{4,5},{5,4},{6,7},{7,6},{8,9},{9,8},{10,11... | collective-permute-start | bytes 393224 | tf_op jit(solution)/shard_map/ppermute | solution.py:213
  16.0 0.2 collective-permute-done.6.arrived
  16.2 1.6 %collective-permute-start.7 = (bf16[8,4096]{1,0:T(8,128)(2,1)S(1)}, bf16[8,4096]{1,0:T(8,128)(2,1)S(1)}, u32[]{:S(2)}, u32[]{:S(2)}) collective-permute-start(bf16[8,4096]{1,0:T(8,128)(2,1)S(1)} %get-tuple-element.22), channel_id=1, source_target_pairs={{0,2},{1,3},{2,0},{3,1},{4,6},{5,7},{6,4},{7,5},{8,10},{9,11},{10,... | collective-permute-start | bytes 196616 | tf_op jit(solution)/shard_map/ppermute | solution.py:214
  17.8 0.8 %collective-permute-start.4 = (bf16[8,4096]{1,0:T(8,128)(2,1)S(1)}, bf16[8,4096]{1,0:T(8,128)(2,1)S(1)}, u32[]{:S(2)}, u32[]{:S(2)}) collective-permute-start(bf16[8,4096]{1,0:T(8,128)(2,1)S(1)} %get-tuple-element.18), channel_id=1, source_target_pairs={{0,2},{1,3},{2,0},{3,1},{4,6},{5,7},{6,4},{7,5},{8,10},{9,11},{10,... | collective-permute-start | bytes 196616 | tf_op jit(solution)/shard_map/ppermute | solution.py:214
  18.6 2.2 %collective-permute-done.7.refs_0_ = bf16[8,4096]{1,0:T(8,128)(2,1)S(1)} collective-permute-done((bf16[8,4096]{1,0:T(8,128)(2,1)S(1)}, bf16[8,4096]{1,0:T(8,128)(2,1)S(1)}, u32[]{:S(2)}, u32[]{:S(2)}) %collective-permute-start.7) | collective-permute-done | bytes 65568 | tf_op jit(solution)/shard_map/ppermute | solution.py:214
  20.8 0.8 %collective-permute-start.8 = (bf16[8,4096]{1,0:T(8,128)(2,1)S(1)}, bf16[8,4096]{1,0:T(8,128)(2,1)S(1)}, u32[]{:S(2)}, u32[]{:S(2)}) collective-permute-start(bf16[8,4096]{1,0:T(8,128)(2,1)S(1)} %fold.3), channel_id=1, source_target_pairs={{0,8},{1,13},{2,10},{3,15},{4,12},{5,9},{6,14},{7,11},{8,0},{9,5},... | collective-permute-start | bytes 196616 | tf_op jit(solution)/shard_map/ppermute | solution.py:226
  21.6 0.5 %collective-permute-done.4.refs_0_ = bf16[8,4096]{1,0:T(8,128)(2,1)S(1)} collective-permute-done((bf16[8,4096]{1,0:T(8,128)(2,1)S(1)}, bf16[8,4096]{1,0:T(8,128)(2,1)S(1)}, u32[]{:S(2)}, u32[]{:S(2)}) %collective-permute-start.4) | collective-permute-done | bytes 65568 | tf_op jit(solution)/shard_map/ppermute | solution.py:214
  22.1 0.7 %collective-permute-start.5 = (bf16[8,4096]{1,0:T(8,128)(2,1)S(1)}, bf16[8,4096]{1,0:T(8,128)(2,1)S(1)}, u32[]{:S(2)}, u32[]{:S(2)}) collective-permute-start(bf16[8,4096]{1,0:T(8,128)(2,1)S(1)} %fold.2), channel_id=1, source_target_pairs={{0,0},{1,5},{2,2},{3,7},{4,4},{5,1},{6,6},{7,3},{8,8},{9,13},{10,1... | collective-permute-start | bytes 196616 | tf_op jit(solution)/shard_map/ppermute | solution.py:233
  22.8 3.2 %collective-permute-done.8.refs_0_ = bf16[8,4096]{1,0:T(8,128)(2,1)S(1)} collective-permute-done((bf16[8,4096]{1,0:T(8,128)(2,1)S(1)}, bf16[8,4096]{1,0:T(8,128)(2,1)S(1)}, u32[]{:S(2)}, u32[]{:S(2)}) %collective-permute-start.8) | collective-permute-done | bytes 65568 | tf_op jit(solution)/shard_map/ppermute | solution.py:226
  26.1 1.2 %collective-permute-start.9 = (bf16[8,4096]{1,0:T(8,128)(2,1)S(1)}, bf16[8,4096]{1,0:T(8,128)(2,1)S(1)}, u32[]{:S(2)}, u32[]{:S(2)}) collective-permute-start(bf16[8,4096]{1,0:T(8,128)(2,1)S(1)} %pack.1), channel_id=1, source_target_pairs={{0,1},{1,0},{2,3},{3,2},{4,5},{5,4},{6,7},{7,6},{8,9},{9,8},{10,11... | collective-permute-start | bytes 196616 | tf_op jit(solution)/shard_map/ppermute | solution.py:242
  27.3 0.9 %collective-permute-done.9.swapped = bf16[8,4096]{1,0:T(8,128)(2,1)S(1)} collective-permute-done((bf16[8,4096]{1,0:T(8,128)(2,1)S(1)}, bf16[8,4096]{1,0:T(8,128)(2,1)S(1)}, u32[]{:S(2)}, u32[]{:S(2)}) %collective-permute-start.9) | collective-permute-done | bytes 65568 | tf_op jit(solution)/shard_map/ppermute | solution.py:242
  28.2 0.8 %mix.1 = bf16[4,4096]{1,0:T(4,128)(2,1)} custom-call(s32[2,16]{1,0:T(2,128)S(1)} %bitcast.2, f32[2,4]{1,0:T(2,128)S(1)} %bitcast.3, bf16[8,4096]{1,0:T(8,128)(2,1)S(1)} %collective-permute-done.9.swapped, bf16[8,4096]{1,0:T(8,128)(2,1)S(1)} %collective-permute-done.5.near_landed, bf16[8,4096]{1,0:T(8,128)(2,1)S(1)} %collective-permute-done.8.refs_0_), custom_call_target="tpu_custom_call" | custom-call | tf_op jit(solution)/shard_map/mix/pallas_call | solution.py:244
  (16 shorter events, 0.2 us)
Async XLA Ops:
  0.0 10.8 %collective-permute-start.1 = (bf16[16,4096]{1,0:T(8,128)(2,1)}, bf16[16,4096]{1,0:T(8,128)(2,1)S(1)}, u32[]{:S(2)}, u32[]{:S(2)}) collective-permute-start(bf16[16,4096]{1,0:T(8,128)(2,1)} %tokens.1), channel_id=1, source_target_pairs={{0,8},{1,13},{2,10},{3,15},{4,12},{5,9},{6,14},{7,11},{8,0},{9,5},... | collective-permute-start | bytes 393224 | tf_op jit(solution)/shard_map/ppermute | solution.py:171
  4.0 7.6 %collective-permute-start = (bf16[16,4096]{1,0:T(8,128)(2,1)}, bf16[16,4096]{1,0:T(8,128)(2,1)S(1)}, u32[]{:S(2)}, u32[]{:S(2)}) collective-permute-start(bf16[16,4096]{1,0:T(8,128)(2,1)} %tokens.1), channel_id=1, source_target_pairs={{0,4},{4,0},{8,12},{12,8},{1,5},{5,1},{9,13},{13,9},{2,6},{6,2},{1... | collective-permute-start | bytes 393224 | tf_op jit(solution)/shard_map/ppermute | solution.py:172
  6.6 5.6 %copy-start = (bf16[1,384,4096]{2,1,0:T(8,128)(2,1)S(1)}, bf16[1,384,4096]{2,1,0:T(8,128)(2,1)}, u32[]{:S(2)}) copy-start(bf16[1,384,4096]{2,1,0:T(8,128)(2,1)} %w_down.1) | copy-start | bytes 9437188
  6.6 5.6 %copy-start.1 = (bf16[1,384,4096]{2,1,0:T(8,128)(2,1)S(1)}, bf16[1,384,4096]{2,1,0:T(8,128)(2,1)}, u32[]{:S(2)}) copy-start(bf16[1,384,4096]{2,1,0:T(8,128)(2,1)} %refs_2_.1) | copy-start | bytes 9437188
  6.6 5.6 %copy-start.2 = (bf16[1,384,4096]{2,1,0:T(8,128)(2,1)S(1)}, bf16[1,384,4096]{2,1,0:T(8,128)(2,1)}, u32[]{:S(2)}) copy-start(bf16[1,384,4096]{2,1,0:T(8,128)(2,1)} %refs_3_.1) | copy-start | bytes 9437188
  10.8 1.3 %collective-permute-start.2 = (bf16[16,4096]{1,0:T(8,128)(2,1)S(1)}, bf16[16,4096]{1,0:T(8,128)(2,1)S(1)}, u32[]{:S(2)}, u32[]{:S(2)}) collective-permute-start(bf16[16,4096]{1,0:T(8,128)(2,1)S(1)} %collective-permute-done.1.refs_0_), channel_id=1, source_target_pairs={{0,1},{1,0},{2,3},{3,2},{4,5},{5,4},{6,7},{7,6},{8,9},{9,8},{10,11... | collective-permute-start | bytes 393224 | tf_op jit(solution)/shard_map/ppermute | solution.py:173
  14.7 13.5 %copy-start.3 = (s32[16,2]{0,1:T(2,128)S(1)}, s32[16,2]{0,1:T(2,128)}, u32[]{:S(2)}) copy-start(s32[16,2]{0,1:T(2,128)} %param.7) | copy-start | bytes 388
  14.7 13.5 %copy-start.4 = (f32[4,2]{0,1:T(2,128)S(1)}, f32[4,2]{0,1:T(2,128)}, u32[]{:S(2)}) copy-start(f32[4,2]{0,1:T(2,128)} %param.8) | copy-start | bytes 100
  14.7 1.4 %collective-permute-start.6 = (bf16[16,4096]{1,0:T(8,128)(2,1)S(1)}, bf16[16,4096]{1,0:T(8,128)(2,1)S(1)}, u32[]{:S(2)}, u32[]{:S(2)}) collective-permute-start(bf16[16,4096]{1,0:T(8,128)(2,1)S(1)} %get-tuple-element.20), channel_id=1, source_target_pairs={{0,1},{1,0},{2,3},{3,2},{4,5},{5,4},{6,7},{7,6},{8,9},{9,8},{10,11... | collective-permute-start | bytes 393224 | tf_op jit(solution)/shard_map/ppermute | solution.py:213
  15.6 2.1 %collective-permute-start.3 = (bf16[16,4096]{1,0:T(8,128)(2,1)S(1)}, bf16[16,4096]{1,0:T(8,128)(2,1)S(1)}, u32[]{:S(2)}, u32[]{:S(2)}) collective-permute-start(bf16[16,4096]{1,0:T(8,128)(2,1)S(1)} %get-tuple-element.16), channel_id=1, source_target_pairs={{0,1},{1,0},{2,3},{3,2},{4,5},{5,4},{6,7},{7,6},{8,9},{9,8},{10,11... | collective-permute-start | bytes 393224 | tf_op jit(solution)/shard_map/ppermute | solution.py:213
  16.2 4.6 %collective-permute-start.7 = (bf16[8,4096]{1,0:T(8,128)(2,1)S(1)}, bf16[8,4096]{1,0:T(8,128)(2,1)S(1)}, u32[]{:S(2)}, u32[]{:S(2)}) collective-permute-start(bf16[8,4096]{1,0:T(8,128)(2,1)S(1)} %get-tuple-element.22), channel_id=1, source_target_pairs={{0,2},{1,3},{2,0},{3,1},{4,6},{5,7},{6,4},{7,5},{8,10},{9,11},{10,... | collective-permute-start | bytes 196616 | tf_op jit(solution)/shard_map/ppermute | solution.py:214
  17.8 4.3 %collective-permute-start.4 = (bf16[8,4096]{1,0:T(8,128)(2,1)S(1)}, bf16[8,4096]{1,0:T(8,128)(2,1)S(1)}, u32[]{:S(2)}, u32[]{:S(2)}) collective-permute-start(bf16[8,4096]{1,0:T(8,128)(2,1)S(1)} %get-tuple-element.18), channel_id=1, source_target_pairs={{0,2},{1,3},{2,0},{3,1},{4,6},{5,7},{6,4},{7,5},{8,10},{9,11},{10,... | collective-permute-start | bytes 196616 | tf_op jit(solution)/shard_map/ppermute | solution.py:214
  20.8 5.2 %collective-permute-start.8 = (bf16[8,4096]{1,0:T(8,128)(2,1)S(1)}, bf16[8,4096]{1,0:T(8,128)(2,1)S(1)}, u32[]{:S(2)}, u32[]{:S(2)}) collective-permute-start(bf16[8,4096]{1,0:T(8,128)(2,1)S(1)} %fold.3), channel_id=1, source_target_pairs={{0,8},{1,13},{2,10},{3,15},{4,12},{5,9},{6,14},{7,11},{8,0},{9,5},... | collective-permute-start | bytes 196616 | tf_op jit(solution)/shard_map/ppermute | solution.py:226
  22.1 3.9 %collective-permute-start.5 = (bf16[8,4096]{1,0:T(8,128)(2,1)S(1)}, bf16[8,4096]{1,0:T(8,128)(2,1)S(1)}, u32[]{:S(2)}, u32[]{:S(2)}) collective-permute-start(bf16[8,4096]{1,0:T(8,128)(2,1)S(1)} %fold.2), channel_id=1, source_target_pairs={{0,0},{1,5},{2,2},{3,7},{4,4},{5,1},{6,6},{7,3},{8,8},{9,13},{10,1... | collective-permute-start | bytes 196616 | tf_op jit(solution)/shard_map/ppermute | solution.py:233
  26.1 2.1 %collective-permute-start.9 = (bf16[8,4096]{1,0:T(8,128)(2,1)S(1)}, bf16[8,4096]{1,0:T(8,128)(2,1)S(1)}, u32[]{:S(2)}, u32[]{:S(2)}) collective-permute-start(bf16[8,4096]{1,0:T(8,128)(2,1)S(1)} %pack.1), channel_id=1, source_target_pairs={{0,1},{1,0},{2,3},{3,2},{4,5},{5,4},{6,7},{7,6},{8,9},{9,8},{10,11... | collective-permute-start | bytes 196616 | tf_op jit(solution)/shard_map/ppermute | solution.py:242

commit v27 on v24

--- a/solution.py
+++ b/solution.py
@@ -94,8 +94,8 @@
         piece[...] = total[k * rows : (k + 1) * rows].astype(piece.dtype)
 
 
-def mix_kernel(n_expert, pairs, ids, weights, *refs):
-    own, pieces, out = refs[:pairs], refs[pairs:-1], refs[-1]
+def weigh_kernel(n_expert, pairs, ids, weights, *refs):
+    own, pieces, (out, last_factor) = refs[:pairs], refs[pairs:-2], refs[-2:]
     rows = out.shape[0]
     me, expert = lax.axis_index("etp"), lax.axis_index("expert")
     top, tok = ids.shape
@@ -114,8 +114,15 @@
         factor = sum(jnp.where(own_ids[i] == owner, own_weights[i], 0.0) for i in range(top)) / scale
         if k == 0:
             total = sum(block[...].astype(jnp.float32) for block in own) * factor
+        elif k < n_expert - 1:
+            total = total + pieces[k - 1][...].astype(jnp.float32) * factor
         else:
-            total = total + pieces[k - 1][...].astype(jnp.float32) * factor
+            last_factor[...] = jnp.broadcast_to(factor, last_factor.shape)
+    out[...] = total
+
+
+def finish_kernel(partial, factor, piece, out):
+    total = partial[...] + piece[...].astype(jnp.float32) * factor[:, :1]
     out[...] = total.astype(out.dtype)
 
 
@@ -226,14 +233,25 @@
         route = [(e, (e + k) % n_expert) for e in range(n_expert)]
         landed.append(lax.ppermute(piece, "expert", route))
 
+    partial, factor = pl.pallas_call(
+        functools.partial(weigh_kernel, n_expert, pairs),
+        out_shape=[
+            jax.ShapeDtypeStruct((rows, width), jnp.float32),
+            jax.ShapeDtypeStruct((rows, 128), jnp.float32),
+        ],
+        in_specs=[VMEM] * (n_expert + pairs),
+        out_specs=[VMEM] * 2,
+        compiler_params=GRANT,
+        name="weigh",
+    )(expert_ids.T, route_weights.T, *own, *landed[:-1])
     return pl.pallas_call(
-        functools.partial(mix_kernel, n_expert, pairs),
+        finish_kernel,
         out_shape=jax.ShapeDtypeStruct((rows, width), jnp.bfloat16),
-        in_specs=[VMEM] * (1 + n_expert + pairs),
+        in_specs=[VMEM] * 3,
         out_specs=VMEM,
         compiler_params=GRANT,
-        name="mix",
-    )(expert_ids.T, route_weights.T, *own, *landed)
+        name="finish",
+    )(partial, factor, landed[-1])
 
 
 def solution(mesh):

time: 28.9 us -> 28.8 us (level)
    pallas_call x1 -> x2, Pallas kernels: 0.75 us -> 0.81 us  [the longest x1 0.7 us: on_device(): pl.pallas_call(finish_kernel, out_shape=jax.ShapeDtypeStruct((rows, width...]
  transfers between devices with their start and end apart: 12 -> 12, of which waited for: 7 -> 7; matrix products, arithmetic and copies ran while one was open for 0% -> 0% of each run, Pallas kernels for 6% -> 7%
where the time goes in v27:
time: 28.8 us; the launch traced here: 28.7 us
  starting transfers between devices  15.3 us (53%)
  waiting for transfers between devices  8.13 us (28%)
  Pallas kernels  5.1 us (18%)
    ppermute x3, starting transfers between devices, on_device(): landed.append(lax.ppermute(piece, 'expert', route))  4.95 us
    ppermute x1, waiting for transfers between devices, on_device(): far.append(lax.ppermute(tokens, ('expert', 'etp'), route))  4.22 us
    ppermute x1, starting transfers between devices, on_device(): far.append(lax.ppermute(tokens, ('expert', 'etp'), route))  4.04 us
    ppermute x3, starting transfers between devices, over_pairs(): lax.ppermute(piece, 'etp', turn)  3.65 us
    pallas_call x1, Pallas kernels, on_device(): pl.pallas_call(functools.partial(ffn_kernel, n_expert, parts), out_shape=...  2.53 us
    ppermute x3, waiting for transfers between devices, on_device(): landed.append(lax.ppermute(piece, 'expert', route))  2.45 us
    ppermute x1, starting transfers between devices, on_device(): lax.ppermute(tokens, 'expert', [(e, e ^ 1) for e in range(n_expert)])  1.58 us
    pallas_call x1, Pallas kernels, on_device(): pl.pallas_call(fetch_kernel, out_shape=jax.ShapeDtypeStruct((tok, width),...  0.95 us
  transfers between devices with their start and end apart: 12, of which 7 were waited for; matrix products, arithmetic and copies ran while one was open for 0% of the time, Pallas kernels for 7%

profile of v27, /device:TPU:0, one launch (start us, length us, event | category | flops | bytes accessed | tf_op | source)
XLA Modules:
  0.0 28.7 jit_solution(13858881989788569772)
XLA Ops:
  0.0 4.0 %collective-permute-start.1 = (bf16[16,4096]{1,0:T(8,128)(2,1)}, bf16[16,4096]{1,0:T(8,128)(2,1)S(1)}, u32[]{:S(2)}, u32[]{:S(2)}) collective-permute-start(bf16[16,4096]{1,0:T(8,128)(2,1)} %tokens.1), channel_id=1, source_target_pairs={{0,8},{1,13},{2,10},{3,15},{4,12},{5,9},{6,14},{7,11},{8,0},{9,5},... | collective-permute-start | bytes 393224 | tf_op jit(solution)/shard_map/ppermute | solution.py:162
  4.0 1.6 %collective-permute-start = (bf16[16,4096]{1,0:T(8,128)(2,1)}, bf16[16,4096]{1,0:T(8,128)(2,1)S(1)}, u32[]{:S(2)}, u32[]{:S(2)}) collective-permute-start(bf16[16,4096]{1,0:T(8,128)(2,1)} %tokens.1), channel_id=1, source_target_pairs={{0,4},{4,0},{8,12},{12,8},{1,5},{5,1},{9,13},{13,9},{2,6},{6,2},{1... | collective-permute-start | bytes 393224 | tf_op jit(solution)/shard_map/ppermute | solution.py:163
  5.6 0.9 %fetch.1.own = bf16[16,4096]{1,0:T(8,128)(2,1)S(1)} custom-call(bf16[16,4096]{1,0:T(8,128)(2,1)} %tokens.1), custom_call_target="tpu_custom_call" | custom-call | tf_op jit(solution)/shard_map/fetch/pallas_call | solution.py:135
  6.6 4.2 %collective-permute-done.1.refs_0_ = bf16[16,4096]{1,0:T(8,128)(2,1)S(1)} collective-permute-done((bf16[16,4096]{1,0:T(8,128)(2,1)}, bf16[16,4096]{1,0:T(8,128)(2,1)S(1)}, u32[]{:S(2)}, u32[]{:S(2)}) %collective-permute-start.1) | collective-permute-done | bytes 131104 | tf_op jit(solution)/shard_map/ppermute | solution.py:162
  10.8 0.1 order.1
  10.9 0.7 %collective-permute-done.next_block = bf16[16,4096]{1,0:T(8,128)(2,1)S(1)} collective-permute-done((bf16[16,4096]{1,0:T(8,128)(2,1)}, bf16[16,4096]{1,0:T(8,128)(2,1)S(1)}, u32[]{:S(2)}, u32[]{:S(2)}) %collective-permute-start) | collective-permute-done | bytes 131104 | tf_op jit(solution)/shard_map/ppermute | solution.py:163
  11.6 0.6 %collective-permute-done.2.refs_1_ = bf16[16,4096]{1,0:T(8,128)(2,1)S(1)} collective-permute-done((bf16[16,4096]{1,0:T(8,128)(2,1)S(1)}, bf16[16,4096]{1,0:T(8,128)(2,1)S(1)}, u32[]{:S(2)}, u32[]{:S(2)}) %collective-permute-start.2) | collective-permute-done | bytes 131104 | tf_op jit(solution)/shard_map/ppermute | solution.py:164
  12.2 2.5 %ffn.1 = (f32[16,4096]{1,0:T(8,128)S(1)}, bf16[16,4096]{1,0:T(8,128)(2,1)S(1)}, bf16[32,384]{1,0:T(8,128)(2,1)S(1)}) custom-call(bf16[16,4096]{1,0:T(8,128)(2,1)S(1)} %fetch.1.own, bf16[16,4096]{1,0:T(8,128)(2,1)S(1)} %collective-permute-done.next_block, bf16[64,64]{1,0:T(8,128)(2,1)S(1)} %order.1, bf16[16,4096]{1,0:T(8,128)(2,1)S(1)} %collective-permute-done.1.refs_0_, ...), custom_call_target="tpu_custom_call" | custom-call | tf_op jit(solution)/shard_map/ffn/pallas_call | solution.py:171
  14.7 0.2 collective-permute-start.5
  14.9 0.6 %down.1 = (f32[16,4096]{1,0:T(8,128)S(1)}, bf16[16,4096]{1,0:T(8,128)(2,1)S(1)}) custom-call(bf16[32,384]{1,0:T(8,128)(2,1)S(1)} %get-tuple-element.20.hidden, bf16[1,384,4096]{2,1,0:T(8,128)(2,1)S(1)} %copy-done), custom_call_target="tpu_custom_call" | custom-call | tf_op jit(solution)/shard_map/down/pallas_call | solution.py:180
  15.6 0.4 %collective-permute-start.3 = (bf16[16,4096]{1,0:T(8,128)(2,1)S(1)}, bf16[16,4096]{1,0:T(8,128)(2,1)S(1)}, u32[]{:S(2)}, u32[]{:S(2)}) collective-permute-start(bf16[16,4096]{1,0:T(8,128)(2,1)S(1)} %get-tuple-element.22), channel_id=1, source_target_pairs={{0,1},{1,0},{2,3},{3,2},{4,5},{5,4},{6,7},{7,6},{8,9},{9,8},{10,11... | collective-permute-start | bytes 393224 | tf_op jit(solution)/shard_map/ppermute | solution.py:206
  16.0 0.2 collective-permute-done.5.arrived
  16.2 1.6 %collective-permute-start.6 = (bf16[4,4096]{1,0:T(4,128)(2,1)S(1)}, bf16[4,4096]{1,0:T(4,128)(2,1)S(1)}, u32[]{:S(2)}, u32[]{:S(2)}) collective-permute-start(bf16[4,4096]{1,0:T(4,128)(2,1)S(1)} %get-tuple-element.28), channel_id=1, source_target_pairs={{0,2},{1,3},{2,0},{3,1},{4,6},{5,7},{6,4},{7,5},{8,10},{9,11},{10,... | collective-permute-start | bytes 98312 | tf_op jit(solution)/shard_map/ppermute | solution.py:211
  17.7 0.5 %collective-permute-start.8 = (bf16[4,4096]{1,0:T(4,128)(2,1)S(1)}, bf16[4,4096]{1,0:T(4,128)(2,1)S(1)}, u32[]{:S(2)}, u32[]{:S(2)}) collective-permute-start(bf16[4,4096]{1,0:T(4,128)(2,1)S(1)} %get-tuple-element.30), channel_id=1, source_target_pairs={{0,2},{1,3},{2,0},{3,1},{4,6},{5,7},{6,4},{7,5},{8,10},{9,11},{10,... | collective-permute-start | bytes 98312 | tf_op jit(solution)/shard_map/ppermute | solution.py:211
  18.3 1.6 %collective-permute-start.10 = (bf16[4,4096]{1,0:T(4,128)(2,1)S(1)}, bf16[4,4096]{1,0:T(4,128)(2,1)S(1)}, u32[]{:S(2)}, u32[]{:S(2)}) collective-permute-start(bf16[4,4096]{1,0:T(4,128)(2,1)S(1)} %get-tuple-element.34), channel_id=1, source_target_pairs={{0,2},{1,3},{2,0},{3,1},{4,6},{5,7},{6,4},{7,5},{8,10},{9,11},{10,... | collective-permute-start | bytes 98312 | tf_op jit(solution)/shard_map/ppermute | solution.py:211
  19.9 0.5 %collective-permute-start.4 = (bf16[4,4096]{1,0:T(4,128)(2,1)S(1)}, bf16[4,4096]{1,0:T(4,128)(2,1)S(1)}, u32[]{:S(2)}, u32[]{:S(2)}) collective-permute-start(bf16[4,4096]{1,0:T(4,128)(2,1)S(1)} %get-tuple-element.24), channel_id=1, source_target_pairs={{0,2},{1,3},{2,0},{3,1},{4,6},{5,7},{6,4},{7,5},{8,10},{9,11},{10,... | collective-permute-start | bytes 98312 | tf_op jit(solution)/shard_map/ppermute | solution.py:230
  20.4 1.2 %collective-permute-start.7 = (bf16[4,4096]{1,0:T(4,128)(2,1)S(1)}, bf16[4,4096]{1,0:T(4,128)(2,1)S(1)}, u32[]{:S(2)}, u32[]{:S(2)}) collective-permute-start(bf16[4,4096]{1,0:T(4,128)(2,1)S(1)} %fold.3), channel_id=1, source_target_pairs={{0,4},{4,8},{8,12},{12,0},{1,5},{5,9},{9,13},{13,1},{2,6},{6,10},{... | collective-permute-start | bytes 98312 | tf_op jit(solution)/shard_map/ppermute | solution.py:234
  21.7 2.3 %collective-permute-start.9 = (bf16[4,4096]{1,0:T(4,128)(2,1)S(1)}, bf16[4,4096]{1,0:T(4,128)(2,1)S(1)}, u32[]{:S(2)}, u32[]{:S(2)}) collective-permute-start(bf16[4,4096]{1,0:T(4,128)(2,1)S(1)} %fold.4), channel_id=1, source_target_pairs={{0,8},{4,12},{8,0},{12,4},{1,9},{5,13},{9,1},{13,5},{2,10},{6,14},... | collective-permute-start | bytes 98312 | tf_op jit(solution)/shard_map/ppermute | solution.py:234
  24.0 1.4 %collective-permute-start.11 = (bf16[4,4096]{1,0:T(4,128)(2,1)S(1)}, bf16[4,4096]{1,0:T(4,128)(2,1)S(1)}, u32[]{:S(2)}, u32[]{:S(2)}) collective-permute-start(bf16[4,4096]{1,0:T(4,128)(2,1)S(1)} %fold.5), channel_id=1, source_target_pairs={{0,12},{4,0},{8,4},{12,8},{1,13},{5,1},{9,5},{13,9},{2,14},{6,2},{... | collective-permute-start | bytes 98312 | tf_op jit(solution)/shard_map/ppermute | solution.py:234
  25.4 0.9 %collective-permute-done.7.refs_2_ = bf16[4,4096]{1,0:T(4,128)(2,1)S(1)} collective-permute-done((bf16[4,4096]{1,0:T(4,128)(2,1)S(1)}, bf16[4,4096]{1,0:T(4,128)(2,1)S(1)}, u32[]{:S(2)}, u32[]{:S(2)}) %collective-permute-start.7) | collective-permute-done | bytes 32800 | tf_op jit(solution)/shard_map/ppermute | solution.py:234
  26.3 0.5 %collective-permute-done.9.refs_3_ = bf16[4,4096]{1,0:T(4,128)(2,1)S(1)} collective-permute-done((bf16[4,4096]{1,0:T(4,128)(2,1)S(1)}, bf16[4,4096]{1,0:T(4,128)(2,1)S(1)}, u32[]{:S(2)}, u32[]{:S(2)}) %collective-permute-start.9) | collective-permute-done | bytes 32800 | tf_op jit(solution)/shard_map/ppermute | solution.py:234
  26.8 0.1 weigh.1
  26.9 1.1 %collective-permute-done.11.piece = bf16[4,4096]{1,0:T(4,128)(2,1)S(1)} collective-permute-done((bf16[4,4096]{1,0:T(4,128)(2,1)S(1)}, bf16[4,4096]{1,0:T(4,128)(2,1)S(1)}, u32[]{:S(2)}, u32[]{:S(2)}) %collective-permute-start.11) | collective-permute-done | bytes 32800 | tf_op jit(solution)/shard_map/ppermute | solution.py:234
  28.0 0.7 %finish.1 = bf16[4,4096]{1,0:T(4,128)(2,1)} custom-call(f32[4,4096]{1,0:T(4,128)S(1)} %get-tuple-element.31.partial, f32[4,128]{1,0:T(4,128)S(1)} %get-tuple-element.32.factor, bf16[4,4096]{1,0:T(4,128)(2,1)S(1)} %collective-permute-done.11.piece), custom_call_target="tpu_custom_call" | custom-call | tf_op jit(solution)/shard_map/finish/pallas_call | solution.py:247
  (21 shorter events, 0.2 us)
Async XLA Ops:
  0.0 10.8 %collective-permute-start.1 = (bf16[16,4096]{1,0:T(8,128)(2,1)}, bf16[16,4096]{1,0:T(8,128)(2,1)S(1)}, u32[]{:S(2)}, u32[]{:S(2)}) collective-permute-start(bf16[16,4096]{1,0:T(8,128)(2,1)} %tokens.1), channel_id=1, source_target_pairs={{0,8},{1,13},{2,10},{3,15},{4,12},{5,9},{6,14},{7,11},{8,0},{9,5},... | collective-permute-start | bytes 393224 | tf_op jit(solution)/shard_map/ppermute | solution.py:162
  4.0 7.6 %collective-permute-start = (bf16[16,4096]{1,0:T(8,128)(2,1)}, bf16[16,4096]{1,0:T(8,128)(2,1)S(1)}, u32[]{:S(2)}, u32[]{:S(2)}) collective-permute-start(bf16[16,4096]{1,0:T(8,128)(2,1)} %tokens.1), channel_id=1, source_target_pairs={{0,4},{4,0},{8,12},{12,8},{1,5},{5,1},{9,13},{13,9},{2,6},{6,2},{1... | collective-permute-start | bytes 393224 | tf_op jit(solution)/shard_map/ppermute | solution.py:163
  6.6 5.6 %copy-start = (bf16[1,384,4096]{2,1,0:T(8,128)(2,1)S(1)}, bf16[1,384,4096]{2,1,0:T(8,128)(2,1)}, u32[]{:S(2)}) copy-start(bf16[1,384,4096]{2,1,0:T(8,128)(2,1)} %w_down.1) | copy-start | bytes 9437188
  6.6 5.6 %copy-start.1 = (bf16[1,384,4096]{2,1,0:T(8,128)(2,1)S(1)}, bf16[1,384,4096]{2,1,0:T(8,128)(2,1)}, u32[]{:S(2)}) copy-start(bf16[1,384,4096]{2,1,0:T(8,128)(2,1)} %refs_2_.1) | copy-start | bytes 9437188
  6.6 5.6 %copy-start.2 = (bf16[1,384,4096]{2,1,0:T(8,128)(2,1)S(1)}, bf16[1,384,4096]{2,1,0:T(8,128)(2,1)}, u32[]{:S(2)}) copy-start(bf16[1,384,4096]{2,1,0:T(8,128)(2,1)} %refs_3_.1) | copy-start | bytes 9437188
  10.8 1.3 %collective-permute-start.2 = (bf16[16,4096]{1,0:T(8,128)(2,1)S(1)}, bf16[16,4096]{1,0:T(8,128)(2,1)S(1)}, u32[]{:S(2)}, u32[]{:S(2)}) collective-permute-start(bf16[16,4096]{1,0:T(8,128)(2,1)S(1)} %collective-permute-done.1.refs_0_), channel_id=1, source_target_pairs={{0,1},{1,0},{2,3},{3,2},{4,5},{5,4},{6,7},{7,6},{8,9},{9,8},{10,11... | collective-permute-start | bytes 393224 | tf_op jit(solution)/shard_map/ppermute | solution.py:164
  14.7 12.1 %copy-start.3 = (s32[16,2]{0,1:T(2,128)S(1)}, s32[16,2]{0,1:T(2,128)}, u32[]{:S(2)}) copy-start(s32[16,2]{0,1:T(2,128)} %param.7) | copy-start | bytes 388
  14.7 12.1 %copy-start.4 = (f32[4,2]{0,1:T(2,128)S(1)}, f32[4,2]{0,1:T(2,128)}, u32[]{:S(2)}) copy-start(f32[4,2]{0,1:T(2,128)} %param.8) | copy-start | bytes 100
  14.7 1.4 %collective-permute-start.5 = (bf16[16,4096]{1,0:T(8,128)(2,1)S(1)}, bf16[16,4096]{1,0:T(8,128)(2,1)S(1)}, u32[]{:S(2)}, u32[]{:S(2)}) collective-permute-start(bf16[16,4096]{1,0:T(8,128)(2,1)S(1)} %get-tuple-element.26), channel_id=1, source_target_pairs={{0,1},{1,0},{2,3},{3,2},{4,5},{5,4},{6,7},{7,6},{8,9},{9,8},{10,11... | collective-permute-start | bytes 393224 | tf_op jit(solution)/shard_map/ppermute | solution.py:206
  15.6 2.7 %collective-permute-start.3 = (bf16[16,4096]{1,0:T(8,128)(2,1)S(1)}, bf16[16,4096]{1,0:T(8,128)(2,1)S(1)}, u32[]{:S(2)}, u32[]{:S(2)}) collective-permute-start(bf16[16,4096]{1,0:T(8,128)(2,1)S(1)} %get-tuple-element.22), channel_id=1, source_target_pairs={{0,1},{1,0},{2,3},{3,2},{4,5},{5,4},{6,7},{7,6},{8,9},{9,8},{10,11... | collective-permute-start | bytes 393224 | tf_op jit(solution)/shard_map/ppermute | solution.py:206
  16.2 4.2 %collective-permute-start.6 = (bf16[4,4096]{1,0:T(4,128)(2,1)S(1)}, bf16[4,4096]{1,0:T(4,128)(2,1)S(1)}, u32[]{:S(2)}, u32[]{:S(2)}) collective-permute-start(bf16[4,4096]{1,0:T(4,128)(2,1)S(1)} %get-tuple-element.28), channel_id=1, source_target_pairs={{0,2},{1,3},{2,0},{3,1},{4,6},{5,7},{6,4},{7,5},{8,10},{9,11},{10,... | collective-permute-start | bytes 98312 | tf_op jit(solution)/shard_map/ppermute | solution.py:211
  17.7 3.9 %collective-permute-start.8 = (bf16[4,4096]{1,0:T(4,128)(2,1)S(1)}, bf16[4,4096]{1,0:T(4,128)(2,1)S(1)}, u32[]{:S(2)}, u32[]{:S(2)}) collective-permute-start(bf16[4,4096]{1,0:T(4,128)(2,1)S(1)} %get-tuple-element.30), channel_id=1, source_target_pairs={{0,2},{1,3},{2,0},{3,1},{4,6},{5,7},{6,4},{7,5},{8,10},{9,11},{10,... | collective-permute-start | bytes 98312 | tf_op jit(solution)/shard_map/ppermute | solution.py:211
  18.3 5.7 %collective-permute-start.10 = (bf16[4,4096]{1,0:T(4,128)(2,1)S(1)}, bf16[4,4096]{1,0:T(4,128)(2,1)S(1)}, u32[]{:S(2)}, u32[]{:S(2)}) collective-permute-start(bf16[4,4096]{1,0:T(4,128)(2,1)S(1)} %get-tuple-element.34), channel_id=1, source_target_pairs={{0,2},{1,3},{2,0},{3,1},{4,6},{5,7},{6,4},{7,5},{8,10},{9,11},{10,... | collective-permute-start | bytes 98312 | tf_op jit(solution)/shard_map/ppermute | solution.py:211
  19.9 5.6 %collective-permute-start.4 = (bf16[4,4096]{1,0:T(4,128)(2,1)S(1)}, bf16[4,4096]{1,0:T(4,128)(2,1)S(1)}, u32[]{:S(2)}, u32[]{:S(2)}) collective-permute-start(bf16[4,4096]{1,0:T(4,128)(2,1)S(1)} %get-tuple-element.24), channel_id=1, source_target_pairs={{0,2},{1,3},{2,0},{3,1},{4,6},{5,7},{6,4},{7,5},{8,10},{9,11},{10,... | collective-permute-start | bytes 98312 | tf_op jit(solution)/shard_map/ppermute | solution.py:230
  20.4 5.9 %collective-permute-start.7 = (bf16[4,4096]{1,0:T(4,128)(2,1)S(1)}, bf16[4,4096]{1,0:T(4,128)(2,1)S(1)}, u32[]{:S(2)}, u32[]{:S(2)}) collective-permute-start(bf16[4,4096]{1,0:T(4,128)(2,1)S(1)} %fold.3), channel_id=1, source_target_pairs={{0,4},{4,8},{8,12},{12,0},{1,5},{5,9},{9,13},{13,1},{2,6},{6,10},{... | collective-permute-start | bytes 98312 | tf_op jit(solution)/shard_map/ppermute | solution.py:234
  21.7 5.1 %collective-permute-start.9 = (bf16[4,4096]{1,0:T(4,128)(2,1)S(1)}, bf16[4,4096]{1,0:T(4,128)(2,1)S(1)}, u32[]{:S(2)}, u32[]{:S(2)}) collective-permute-start(bf16[4,4096]{1,0:T(4,128)(2,1)S(1)} %fold.4), channel_id=1, source_target_pairs={{0,8},{4,12},{8,0},{12,4},{1,9},{5,13},{9,1},{13,5},{2,10},{6,14},... | collective-permute-start | bytes 98312 | tf_op jit(solution)/shard_map/ppermute | solution.py:234
  24.0 4.0 %collective-permute-start.11 = (bf16[4,4096]{1,0:T(4,128)(2,1)S(1)}, bf16[4,4096]{1,0:T(4,128)(2,1)S(1)}, u32[]{:S(2)}, u32[]{:S(2)}) collective-permute-start(bf16[4,4096]{1,0:T(4,128)(2,1)S(1)} %fold.5), channel_id=1, source_target_pairs={{0,12},{4,0},{8,4},{12,8},{1,13},{5,1},{9,5},{13,9},{2,14},{6,2},{... | collective-permute-start | bytes 98312 | tf_op jit(solution)/shard_map/ppermute | solution.py:234

commit v28 on v27

--- a/solution.py
+++ b/solution.py
@@ -32,7 +32,8 @@
     h = lax.rem(lax.div(place, rows * half), pairs)
     sent = lax.rem(lax.div(place, rows * half * pairs), 2)
     second = lax.div(place, rows * half * pairs * 2)
-    shift = jnp.where(second == 0, k + 1, jnp.where(k == 0, 0, k + half))
+    first = jnp.where(lax.rem(core + sent, 2) == 0, k + 1, half - k)
+    shift = jnp.where(second == 0, first, jnp.where(k == 0, 0, k + half))
     expert = lax.axis_index("expert")
     k = lax.bitwise_xor(expert, lax.rem(expert + shift, n_expert))
     block = 2 * lax.rem(pair + h, pairs) + lax.rem(core + sent, 2)
@@ -110,7 +111,9 @@
     own_weights = [column(weights, 0, i) for i in range(top)]
     scale = sum(own_weights)
     for k in range(n_expert):
-        owner = lax.rem(expert - k + n_expert, n_expert)
+        half = n_expert // 2
+        shift = jnp.where(lax.rem(me, 2) == 0, k, half + 1 - k) if 0 < k <= half else k
+        owner = lax.rem(expert - shift + n_expert, n_expert)
         factor = sum(jnp.where(own_ids[i] == owner, own_weights[i], 0.0) for i in range(top)) / scale
         if k == 0:
             total = sum(block[...].astype(jnp.float32) for block in own) * factor
@@ -230,8 +233,12 @@
     own = [own] + [lax.ppermute(piece, "etp", turn) for piece, turn in zip(others, turns)]
     landed = []
     for k, piece in enumerate(pieces, 1):
-        route = [(e, (e + k) % n_expert) for e in range(n_expert)]
-        landed.append(lax.ppermute(piece, "expert", route))
+        route = [
+            (e * n_etp + t, (e + (half + 1 - k if t % 2 and k <= half else k)) % n_expert * n_etp + t)
+            for e in range(n_expert)
+            for t in range(n_etp)
+        ]
+        landed.append(lax.ppermute(piece, ("expert", "etp"), route))
 
     partial, factor = pl.pallas_call(
         functools.partial(weigh_kernel, n_expert, pairs),

time: 28.8 us -> 28.8 us (level)
  no operation moved by 1% of the time
where the time goes in v28:
time: 28.8 us; the launch traced here: 28.7 us
  starting transfers between devices  15.3 us (53%)
  waiting for transfers between devices  8.11 us (28%)
  Pallas kernels  5.11 us (18%)
    ppermute x3, starting transfers between devices, on_device(): landed.append(lax.ppermute(piece, ('expert', 'etp'), route))  4.95 us
    ppermute x1, waiting for transfers between devices, on_device(): far.append(lax.ppermute(tokens, ('expert', 'etp'), route))  4.22 us
    ppermute x1, starting transfers between devices, on_device(): far.append(lax.ppermute(tokens, ('expert', 'etp'), route))  4.04 us
    ppermute x3, starting transfers between devices, over_pairs(): lax.ppermute(piece, 'etp', turn)  3.65 us
    pallas_call x1, Pallas kernels, on_device(): pl.pallas_call(functools.partial(ffn_kernel, n_expert, parts), out_shape=...  2.53 us
    ppermute x3, waiting for transfers between devices, on_device(): landed.append(lax.ppermute(piece, ('expert', 'etp'), route))  2.43 us
    ppermute x1, starting transfers between devices, on_device(): lax.ppermute(tokens, 'expert', [(e, e ^ 1) for e in range(n_expert)])  1.58 us
    pallas_call x1, Pallas kernels, on_device(): pl.pallas_call(fetch_kernel, out_shape=jax.ShapeDtypeStruct((tok, width),...  0.95 us
  transfers between devices with their start and end apart: 12, of which 7 were waited for; matrix products, arithmetic and copies ran while one was open for 0% of the time, Pallas kernels for 7%

profile of v28, /device:TPU:0, one launch (start us, length us, event | category | flops | bytes accessed | tf_op | source)
XLA Modules:
  0.0 28.7 jit_solution(9018744760284013061)
XLA Ops:
  0.0 4.0 %collective-permute-start.1 = (bf16[16,4096]{1,0:T(8,128)(2,1)}, bf16[16,4096]{1,0:T(8,128)(2,1)S(1)}, u32[]{:S(2)}, u32[]{:S(2)}) collective-permute-start(bf16[16,4096]{1,0:T(8,128)(2,1)} %tokens.1), channel_id=1, source_target_pairs={{0,8},{1,13},{2,10},{3,15},{4,12},{5,9},{6,14},{7,11},{8,0},{9,5},... | collective-permute-start | bytes 393224 | tf_op jit(solution)/shard_map/ppermute | solution.py:165
  4.0 1.6 %collective-permute-start = (bf16[16,4096]{1,0:T(8,128)(2,1)}, bf16[16,4096]{1,0:T(8,128)(2,1)S(1)}, u32[]{:S(2)}, u32[]{:S(2)}) collective-permute-start(bf16[16,4096]{1,0:T(8,128)(2,1)} %tokens.1), channel_id=1, source_target_pairs={{0,4},{4,0},{8,12},{12,8},{1,5},{5,1},{9,13},{13,9},{2,6},{6,2},{1... | collective-permute-start | bytes 393224 | tf_op jit(solution)/shard_map/ppermute | solution.py:166
  5.6 0.9 %fetch.1.own = bf16[16,4096]{1,0:T(8,128)(2,1)S(1)} custom-call(bf16[16,4096]{1,0:T(8,128)(2,1)} %tokens.1), custom_call_target="tpu_custom_call" | custom-call | tf_op jit(solution)/shard_map/fetch/pallas_call | solution.py:138
  6.6 4.2 %collective-permute-done.1.refs_0_ = bf16[16,4096]{1,0:T(8,128)(2,1)S(1)} collective-permute-done((bf16[16,4096]{1,0:T(8,128)(2,1)}, bf16[16,4096]{1,0:T(8,128)(2,1)S(1)}, u32[]{:S(2)}, u32[]{:S(2)}) %collective-permute-start.1) | collective-permute-done | bytes 131104 | tf_op jit(solution)/shard_map/ppermute | solution.py:165
  10.8 0.1 order.1
  10.9 0.7 %collective-permute-done.next_block = bf16[16,4096]{1,0:T(8,128)(2,1)S(1)} collective-permute-done((bf16[16,4096]{1,0:T(8,128)(2,1)}, bf16[16,4096]{1,0:T(8,128)(2,1)S(1)}, u32[]{:S(2)}, u32[]{:S(2)}) %collective-permute-start) | collective-permute-done | bytes 131104 | tf_op jit(solution)/shard_map/ppermute | solution.py:166
  11.6 0.6 %collective-permute-done.2.refs_1_ = bf16[16,4096]{1,0:T(8,128)(2,1)S(1)} collective-permute-done((bf16[16,4096]{1,0:T(8,128)(2,1)S(1)}, bf16[16,4096]{1,0:T(8,128)(2,1)S(1)}, u32[]{:S(2)}, u32[]{:S(2)}) %collective-permute-start.2) | collective-permute-done | bytes 131104 | tf_op jit(solution)/shard_map/ppermute | solution.py:167
  12.2 2.5 %ffn.1 = (f32[16,4096]{1,0:T(8,128)S(1)}, bf16[16,4096]{1,0:T(8,128)(2,1)S(1)}, bf16[32,384]{1,0:T(8,128)(2,1)S(1)}) custom-call(bf16[16,4096]{1,0:T(8,128)(2,1)S(1)} %fetch.1.own, bf16[16,4096]{1,0:T(8,128)(2,1)S(1)} %collective-permute-done.next_block, bf16[64,64]{1,0:T(8,128)(2,1)S(1)} %order.1, bf16[16,4096]{1,0:T(8,128)(2,1)S(1)} %collective-permute-done.1.refs_0_, ...), custom_call_target="tpu_custom_call" | custom-call | tf_op jit(solution)/shard_map/ffn/pallas_call | solution.py:174
  14.7 0.2 collective-permute-start.5
  14.9 0.6 %down.1 = (f32[16,4096]{1,0:T(8,128)S(1)}, bf16[16,4096]{1,0:T(8,128)(2,1)S(1)}) custom-call(bf16[32,384]{1,0:T(8,128)(2,1)S(1)} %get-tuple-element.20.hidden, bf16[1,384,4096]{2,1,0:T(8,128)(2,1)S(1)} %copy-done), custom_call_target="tpu_custom_call" | custom-call | tf_op jit(solution)/shard_map/down/pallas_call | solution.py:183
  15.6 0.4 %collective-permute-start.3 = (bf16[16,4096]{1,0:T(8,128)(2,1)S(1)}, bf16[16,4096]{1,0:T(8,128)(2,1)S(1)}, u32[]{:S(2)}, u32[]{:S(2)}) collective-permute-start(bf16[16,4096]{1,0:T(8,128)(2,1)S(1)} %get-tuple-element.22), channel_id=1, source_target_pairs={{0,1},{1,0},{2,3},{3,2},{4,5},{5,4},{6,7},{7,6},{8,9},{9,8},{10,11... | collective-permute-start | bytes 393224 | tf_op jit(solution)/shard_map/ppermute | solution.py:209
  16.0 0.2 collective-permute-done.5.arrived
  16.2 1.6 %collective-permute-start.6 = (bf16[4,4096]{1,0:T(4,128)(2,1)S(1)}, bf16[4,4096]{1,0:T(4,128)(2,1)S(1)}, u32[]{:S(2)}, u32[]{:S(2)}) collective-permute-start(bf16[4,4096]{1,0:T(4,128)(2,1)S(1)} %get-tuple-element.28), channel_id=1, source_target_pairs={{0,2},{1,3},{2,0},{3,1},{4,6},{5,7},{6,4},{7,5},{8,10},{9,11},{10,... | collective-permute-start | bytes 98312 | tf_op jit(solution)/shard_map/ppermute | solution.py:214
  17.7 0.5 %collective-permute-start.8 = (bf16[4,4096]{1,0:T(4,128)(2,1)S(1)}, bf16[4,4096]{1,0:T(4,128)(2,1)S(1)}, u32[]{:S(2)}, u32[]{:S(2)}) collective-permute-start(bf16[4,4096]{1,0:T(4,128)(2,1)S(1)} %get-tuple-element.30), channel_id=1, source_target_pairs={{0,2},{1,3},{2,0},{3,1},{4,6},{5,7},{6,4},{7,5},{8,10},{9,11},{10,... | collective-permute-start | bytes 98312 | tf_op jit(solution)/shard_map/ppermute | solution.py:214
  18.3 1.6 %collective-permute-start.10 = (bf16[4,4096]{1,0:T(4,128)(2,1)S(1)}, bf16[4,4096]{1,0:T(4,128)(2,1)S(1)}, u32[]{:S(2)}, u32[]{:S(2)}) collective-permute-start(bf16[4,4096]{1,0:T(4,128)(2,1)S(1)} %get-tuple-element.34), channel_id=1, source_target_pairs={{0,2},{1,3},{2,0},{3,1},{4,6},{5,7},{6,4},{7,5},{8,10},{9,11},{10,... | collective-permute-start | bytes 98312 | tf_op jit(solution)/shard_map/ppermute | solution.py:214
  19.9 0.5 %collective-permute-start.4 = (bf16[4,4096]{1,0:T(4,128)(2,1)S(1)}, bf16[4,4096]{1,0:T(4,128)(2,1)S(1)}, u32[]{:S(2)}, u32[]{:S(2)}) collective-permute-start(bf16[4,4096]{1,0:T(4,128)(2,1)S(1)} %get-tuple-element.24), channel_id=1, source_target_pairs={{0,2},{1,3},{2,0},{3,1},{4,6},{5,7},{6,4},{7,5},{8,10},{9,11},{10,... | collective-permute-start | bytes 98312 | tf_op jit(solution)/shard_map/ppermute | solution.py:233
  20.4 1.2 %collective-permute-start.7 = (bf16[4,4096]{1,0:T(4,128)(2,1)S(1)}, bf16[4,4096]{1,0:T(4,128)(2,1)S(1)}, u32[]{:S(2)}, u32[]{:S(2)}) collective-permute-start(bf16[4,4096]{1,0:T(4,128)(2,1)S(1)} %fold.3), channel_id=1, source_target_pairs={{0,4},{1,9},{2,6},{3,11},{4,8},{5,13},{6,10},{7,15},{8,12},{9,1},{... | collective-permute-start | bytes 98312 | tf_op jit(solution)/shard_map/ppermute | solution.py:241
  21.7 2.3 %collective-permute-start.9 = (bf16[4,4096]{1,0:T(4,128)(2,1)S(1)}, bf16[4,4096]{1,0:T(4,128)(2,1)S(1)}, u32[]{:S(2)}, u32[]{:S(2)}) collective-permute-start(bf16[4,4096]{1,0:T(4,128)(2,1)S(1)} %fold.4), channel_id=1, source_target_pairs={{0,8},{1,5},{2,10},{3,7},{4,12},{5,9},{6,14},{7,11},{8,0},{9,13},{... | collective-permute-start | bytes 98312 | tf_op jit(solution)/shard_map/ppermute | solution.py:241
  24.0 1.4 %collective-permute-start.11 = (bf16[4,4096]{1,0:T(4,128)(2,1)S(1)}, bf16[4,4096]{1,0:T(4,128)(2,1)S(1)}, u32[]{:S(2)}, u32[]{:S(2)}) collective-permute-start(bf16[4,4096]{1,0:T(4,128)(2,1)S(1)} %fold.5), channel_id=1, source_target_pairs={{0,12},{1,13},{2,14},{3,15},{4,0},{5,1},{6,2},{7,3},{8,4},{9,5},{1... | collective-permute-start | bytes 98312 | tf_op jit(solution)/shard_map/ppermute | solution.py:241
  25.4 1.1 %collective-permute-done.7.refs_2_ = bf16[4,4096]{1,0:T(4,128)(2,1)S(1)} collective-permute-done((bf16[4,4096]{1,0:T(4,128)(2,1)S(1)}, bf16[4,4096]{1,0:T(4,128)(2,1)S(1)}, u32[]{:S(2)}, u32[]{:S(2)}) %collective-permute-start.7) | collective-permute-done | bytes 32800 | tf_op jit(solution)/shard_map/ppermute | solution.py:241
  26.5 0.2 collective-permute-done.9.refs_3_
  26.7 0.1 weigh.1
  26.9 1.1 %collective-permute-done.11.piece = bf16[4,4096]{1,0:T(4,128)(2,1)S(1)} collective-permute-done((bf16[4,4096]{1,0:T(4,128)(2,1)S(1)}, bf16[4,4096]{1,0:T(4,128)(2,1)S(1)}, u32[]{:S(2)}, u32[]{:S(2)}) %collective-permute-start.11) | collective-permute-done | bytes 32800 | tf_op jit(solution)/shard_map/ppermute | solution.py:241
  28.0 0.7 %finish.1 = bf16[4,4096]{1,0:T(4,128)(2,1)} custom-call(f32[4,4096]{1,0:T(4,128)S(1)} %get-tuple-element.31.partial, f32[4,128]{1,0:T(4,128)S(1)} %get-tuple-element.32.factor, bf16[4,4096]{1,0:T(4,128)(2,1)S(1)} %collective-permute-done.11.piece), custom_call_target="tpu_custom_call" | custom-call | tf_op jit(solution)/shard_map/finish/pallas_call | solution.py:254
  (21 shorter events, 0.2 us)
Async XLA Ops:
  0.0 10.8 %collective-permute-start.1 = (bf16[16,4096]{1,0:T(8,128)(2,1)}, bf16[16,4096]{1,0:T(8,128)(2,1)S(1)}, u32[]{:S(2)}, u32[]{:S(2)}) collective-permute-start(bf16[16,4096]{1,0:T(8,128)(2,1)} %tokens.1), channel_id=1, source_target_pairs={{0,8},{1,13},{2,10},{3,15},{4,12},{5,9},{6,14},{7,11},{8,0},{9,5},... | collective-permute-start | bytes 393224 | tf_op jit(solution)/shard_map/ppermute | solution.py:165
  4.0 7.6 %collective-permute-start = (bf16[16,4096]{1,0:T(8,128)(2,1)}, bf16[16,4096]{1,0:T(8,128)(2,1)S(1)}, u32[]{:S(2)}, u32[]{:S(2)}) collective-permute-start(bf16[16,4096]{1,0:T(8,128)(2,1)} %tokens.1), channel_id=1, source_target_pairs={{0,4},{4,0},{8,12},{12,8},{1,5},{5,1},{9,13},{13,9},{2,6},{6,2},{1... | collective-permute-start | bytes 393224 | tf_op jit(solution)/shard_map/ppermute | solution.py:166
  6.6 5.6 %copy-start = (bf16[1,384,4096]{2,1,0:T(8,128)(2,1)S(1)}, bf16[1,384,4096]{2,1,0:T(8,128)(2,1)}, u32[]{:S(2)}) copy-start(bf16[1,384,4096]{2,1,0:T(8,128)(2,1)} %w_down.1) | copy-start | bytes 9437188
  6.6 5.6 %copy-start.1 = (bf16[1,384,4096]{2,1,0:T(8,128)(2,1)S(1)}, bf16[1,384,4096]{2,1,0:T(8,128)(2,1)}, u32[]{:S(2)}) copy-start(bf16[1,384,4096]{2,1,0:T(8,128)(2,1)} %refs_2_.1) | copy-start | bytes 9437188
  6.6 5.6 %copy-start.2 = (bf16[1,384,4096]{2,1,0:T(8,128)(2,1)S(1)}, bf16[1,384,4096]{2,1,0:T(8,128)(2,1)}, u32[]{:S(2)}) copy-start(bf16[1,384,4096]{2,1,0:T(8,128)(2,1)} %refs_3_.1) | copy-start | bytes 9437188
  10.8 1.3 %collective-permute-start.2 = (bf16[16,4096]{1,0:T(8,128)(2,1)S(1)}, bf16[16,4096]{1,0:T(8,128)(2,1)S(1)}, u32[]{:S(2)}, u32[]{:S(2)}) collective-permute-start(bf16[16,4096]{1,0:T(8,128)(2,1)S(1)} %collective-permute-done.1.refs_0_), channel_id=1, source_target_pairs={{0,1},{1,0},{2,3},{3,2},{4,5},{5,4},{6,7},{7,6},{8,9},{9,8},{10,11... | collective-permute-start | bytes 393224 | tf_op jit(solution)/shard_map/ppermute | solution.py:167
  14.7 12.0 %copy-start.3 = (s32[16,2]{0,1:T(2,128)S(1)}, s32[16,2]{0,1:T(2,128)}, u32[]{:S(2)}) copy-start(s32[16,2]{0,1:T(2,128)} %param.7) | copy-start | bytes 388
  14.7 12.0 %copy-start.4 = (f32[4,2]{0,1:T(2,128)S(1)}, f32[4,2]{0,1:T(2,128)}, u32[]{:S(2)}) copy-start(f32[4,2]{0,1:T(2,128)} %param.8) | copy-start | bytes 100
  14.7 1.4 %collective-permute-start.5 = (bf16[16,4096]{1,0:T(8,128)(2,1)S(1)}, bf16[16,4096]{1,0:T(8,128)(2,1)S(1)}, u32[]{:S(2)}, u32[]{:S(2)}) collective-permute-start(bf16[16,4096]{1,0:T(8,128)(2,1)S(1)} %get-tuple-element.26), channel_id=1, source_target_pairs={{0,1},{1,0},{2,3},{3,2},{4,5},{5,4},{6,7},{7,6},{8,9},{9,8},{10,11... | collective-permute-start | bytes 393224 | tf_op jit(solution)/shard_map/ppermute | solution.py:209
  15.6 2.7 %collective-permute-start.3 = (bf16[16,4096]{1,0:T(8,128)(2,1)S(1)}, bf16[16,4096]{1,0:T(8,128)(2,1)S(1)}, u32[]{:S(2)}, u32[]{:S(2)}) collective-permute-start(bf16[16,4096]{1,0:T(8,128)(2,1)S(1)} %get-tuple-element.22), channel_id=1, source_target_pairs={{0,1},{1,0},{2,3},{3,2},{4,5},{5,4},{6,7},{7,6},{8,9},{9,8},{10,11... | collective-permute-start | bytes 393224 | tf_op jit(solution)/shard_map/ppermute | solution.py:209
  16.2 4.2 %collective-permute-start.6 = (bf16[4,4096]{1,0:T(4,128)(2,1)S(1)}, bf16[4,4096]{1,0:T(4,128)(2,1)S(1)}, u32[]{:S(2)}, u32[]{:S(2)}) collective-permute-start(bf16[4,4096]{1,0:T(4,128)(2,1)S(1)} %get-tuple-element.28), channel_id=1, source_target_pairs={{0,2},{1,3},{2,0},{3,1},{4,6},{5,7},{6,4},{7,5},{8,10},{9,11},{10,... | collective-permute-start | bytes 98312 | tf_op jit(solution)/shard_map/ppermute | solution.py:214
  17.7 3.9 %collective-permute-start.8 = (bf16[4,4096]{1,0:T(4,128)(2,1)S(1)}, bf16[4,4096]{1,0:T(4,128)(2,1)S(1)}, u32[]{:S(2)}, u32[]{:S(2)}) collective-permute-start(bf16[4,4096]{1,0:T(4,128)(2,1)S(1)} %get-tuple-element.30), channel_id=1, source_target_pairs={{0,2},{1,3},{2,0},{3,1},{4,6},{5,7},{6,4},{7,5},{8,10},{9,11},{10,... | collective-permute-start | bytes 98312 | tf_op jit(solution)/shard_map/ppermute | solution.py:214
  18.3 5.7 %collective-permute-start.10 = (bf16[4,4096]{1,0:T(4,128)(2,1)S(1)}, bf16[4,4096]{1,0:T(4,128)(2,1)S(1)}, u32[]{:S(2)}, u32[]{:S(2)}) collective-permute-start(bf16[4,4096]{1,0:T(4,128)(2,1)S(1)} %get-tuple-element.34), channel_id=1, source_target_pairs={{0,2},{1,3},{2,0},{3,1},{4,6},{5,7},{6,4},{7,5},{8,10},{9,11},{10,... | collective-permute-start | bytes 98312 | tf_op jit(solution)/shard_map/ppermute | solution.py:214
  19.9 5.6 %collective-permute-start.4 = (bf16[4,4096]{1,0:T(4,128)(2,1)S(1)}, bf16[4,4096]{1,0:T(4,128)(2,1)S(1)}, u32[]{:S(2)}, u32[]{:S(2)}) collective-permute-start(bf16[4,4096]{1,0:T(4,128)(2,1)S(1)} %get-tuple-element.24), channel_id=1, source_target_pairs={{0,2},{1,3},{2,0},{3,1},{4,6},{5,7},{6,4},{7,5},{8,10},{9,11},{10,... | collective-permute-start | bytes 98312 | tf_op jit(solution)/shard_map/ppermute | solution.py:233
  20.4 6.1 %collective-permute-start.7 = (bf16[4,4096]{1,0:T(4,128)(2,1)S(1)}, bf16[4,4096]{1,0:T(4,128)(2,1)S(1)}, u32[]{:S(2)}, u32[]{:S(2)}) collective-permute-start(bf16[4,4096]{1,0:T(4,128)(2,1)S(1)} %fold.3), channel_id=1, source_target_pairs={{0,4},{1,9},{2,6},{3,11},{4,8},{5,13},{6,10},{7,15},{8,12},{9,1},{... | collective-permute-start | bytes 98312 | tf_op jit(solution)/shard_map/ppermute | solution.py:241
  21.7 5.0 %collective-permute-start.9 = (bf16[4,4096]{1,0:T(4,128)(2,1)S(1)}, bf16[4,4096]{1,0:T(4,128)(2,1)S(1)}, u32[]{:S(2)}, u32[]{:S(2)}) collective-permute-start(bf16[4,4096]{1,0:T(4,128)(2,1)S(1)} %fold.4), channel_id=1, source_target_pairs={{0,8},{1,5},{2,10},{3,7},{4,12},{5,9},{6,14},{7,11},{8,0},{9,13},{... | collective-permute-start | bytes 98312 | tf_op jit(solution)/shard_map/ppermute | solution.py:241
  24.0 4.0 %collective-permute-start.11 = (bf16[4,4096]{1,0:T(4,128)(2,1)S(1)}, bf16[4,4096]{1,0:T(4,128)(2,1)S(1)}, u32[]{:S(2)}, u32[]{:S(2)}) collective-permute-start(bf16[4,4096]{1,0:T(4,128)(2,1)S(1)} %fold.5), channel_id=1, source_target_pairs={{0,12},{1,13},{2,14},{3,15},{4,0},{5,1},{6,2},{7,3},{8,4},{9,5},{1... | collective-permute-start | bytes 98312 | tf_op jit(solution)/shard_map/ppermute | solution.py:241

commit v29 on v27

--- a/solution.py
+++ b/solution.py
@@ -163,7 +163,7 @@
     next_block = lax.ppermute(tokens, "expert", [(e, e ^ 1) for e in range(n_expert)])
     far = [b for block in far for b in (block, lax.ppermute(block, "etp", swap))]
 
-    parts = 4
+    parts = 8
     halves = [
         jax.ShapeDtypeStruct((side // 2, width), jnp.float32),
         jax.ShapeDtypeStruct((side // 2, width), jnp.bfloat16),

time: 28.8 us -> 28.8 us (level)
  no operation moved by 1% of the time
where the time goes in v29:
time: 28.8 us; the launch traced here: 28.7 us
  starting transfers between devices  15.3 us (53%)
  waiting for transfers between devices  8.13 us (28%)
  Pallas kernels  5.1 us (18%)
    ppermute x3, starting transfers between devices, on_device(): landed.append(lax.ppermute(piece, 'expert', route))  4.95 us
    ppermute x1, waiting for transfers between devices, on_device(): far.append(lax.ppermute(tokens, ('expert', 'etp'), route))  4.22 us
    ppermute x1, starting transfers between devices, on_device(): far.append(lax.ppermute(tokens, ('expert', 'etp'), route))  4.04 us
    ppermute x3, starting transfers between devices, over_pairs(): lax.ppermute(piece, 'etp', turn)  3.65 us
    pallas_call x1, Pallas kernels, on_device(): pl.pallas_call(functools.partial(ffn_kernel, n_expert, parts), out_shape=...  2.53 us
    ppermute x3, waiting for transfers between devices, on_device(): landed.append(lax.ppermute(piece, 'expert', route))  2.45 us
    ppermute x1, starting transfers between devices, on_device(): lax.ppermute(tokens, 'expert', [(e, e ^ 1) for e in range(n_expert)])  1.58 us
    pallas_call x1, Pallas kernels, on_device(): pl.pallas_call(fetch_kernel, out_shape=jax.ShapeDtypeStruct((tok, width),...  0.95 us
  transfers between devices with their start and end apart: 12, of which 7 were waited for; matrix products, arithmetic and copies ran while one was open for 0% of the time, Pallas kernels for 7%

profile of v29, /device:TPU:0, one launch (start us, length us, event | category | flops | bytes accessed | tf_op | source)
XLA Modules:
  0.0 28.7 jit_solution(13858881989788569772)
XLA Ops:
  0.0 4.0 %collective-permute-start.1 = (bf16[16,4096]{1,0:T(8,128)(2,1)}, bf16[16,4096]{1,0:T(8,128)(2,1)S(1)}, u32[]{:S(2)}, u32[]{:S(2)}) collective-permute-start(bf16[16,4096]{1,0:T(8,128)(2,1)} %tokens.1), channel_id=1, source_target_pairs={{0,8},{1,13},{2,10},{3,15},{4,12},{5,9},{6,14},{7,11},{8,0},{9,5},... | collective-permute-start | bytes 393224 | tf_op jit(solution)/shard_map/ppermute | solution.py:162
  4.0 1.6 %collective-permute-start = (bf16[16,4096]{1,0:T(8,128)(2,1)}, bf16[16,4096]{1,0:T(8,128)(2,1)S(1)}, u32[]{:S(2)}, u32[]{:S(2)}) collective-permute-start(bf16[16,4096]{1,0:T(8,128)(2,1)} %tokens.1), channel_id=1, source_target_pairs={{0,4},{4,0},{8,12},{12,8},{1,5},{5,1},{9,13},{13,9},{2,6},{6,2},{1... | collective-permute-start | bytes 393224 | tf_op jit(solution)/shard_map/ppermute | solution.py:163
  5.6 0.9 %fetch.1.own = bf16[16,4096]{1,0:T(8,128)(2,1)S(1)} custom-call(bf16[16,4096]{1,0:T(8,128)(2,1)} %tokens.1), custom_call_target="tpu_custom_call" | custom-call | tf_op jit(solution)/shard_map/fetch/pallas_call | solution.py:135
  6.6 4.2 %collective-permute-done.1.refs_0_ = bf16[16,4096]{1,0:T(8,128)(2,1)S(1)} collective-permute-done((bf16[16,4096]{1,0:T(8,128)(2,1)}, bf16[16,4096]{1,0:T(8,128)(2,1)S(1)}, u32[]{:S(2)}, u32[]{:S(2)}) %collective-permute-start.1) | collective-permute-done | bytes 131104 | tf_op jit(solution)/shard_map/ppermute | solution.py:162
  10.8 0.1 order.1
  10.9 0.7 %collective-permute-done.next_block = bf16[16,4096]{1,0:T(8,128)(2,1)S(1)} collective-permute-done((bf16[16,4096]{1,0:T(8,128)(2,1)}, bf16[16,4096]{1,0:T(8,128)(2,1)S(1)}, u32[]{:S(2)}, u32[]{:S(2)}) %collective-permute-start) | collective-permute-done | bytes 131104 | tf_op jit(solution)/shard_map/ppermute | solution.py:163
  11.6 0.6 %collective-permute-done.2.refs_1_ = bf16[16,4096]{1,0:T(8,128)(2,1)S(1)} collective-permute-done((bf16[16,4096]{1,0:T(8,128)(2,1)S(1)}, bf16[16,4096]{1,0:T(8,128)(2,1)S(1)}, u32[]{:S(2)}, u32[]{:S(2)}) %collective-permute-start.2) | collective-permute-done | bytes 131104 | tf_op jit(solution)/shard_map/ppermute | solution.py:164
  12.2 2.5 %ffn.1 = (f32[16,4096]{1,0:T(8,128)S(1)}, bf16[16,4096]{1,0:T(8,128)(2,1)S(1)}, bf16[32,384]{1,0:T(8,128)(2,1)S(1)}) custom-call(bf16[16,4096]{1,0:T(8,128)(2,1)S(1)} %fetch.1.own, bf16[16,4096]{1,0:T(8,128)(2,1)S(1)} %collective-permute-done.next_block, bf16[64,64]{1,0:T(8,128)(2,1)S(1)} %order.1, bf16[16,4096]{1,0:T(8,128)(2,1)S(1)} %collective-permute-done.1.refs_0_, ...), custom_call_target="tpu_custom_call" | custom-call | tf_op jit(solution)/shard_map/ffn/pallas_call | solution.py:171
  14.7 0.2 collective-permute-start.5
  14.9 0.6 %down.1 = (f32[16,4096]{1,0:T(8,128)S(1)}, bf16[16,4096]{1,0:T(8,128)(2,1)S(1)}) custom-call(bf16[32,384]{1,0:T(8,128)(2,1)S(1)} %get-tuple-element.20.hidden, bf16[1,384,4096]{2,1,0:T(8,128)(2,1)S(1)} %copy-done), custom_call_target="tpu_custom_call" | custom-call | tf_op jit(solution)/shard_map/down/pallas_call | solution.py:180
  15.6 0.4 %collective-permute-start.3 = (bf16[16,4096]{1,0:T(8,128)(2,1)S(1)}, bf16[16,4096]{1,0:T(8,128)(2,1)S(1)}, u32[]{:S(2)}, u32[]{:S(2)}) collective-permute-start(bf16[16,4096]{1,0:T(8,128)(2,1)S(1)} %get-tuple-element.22), channel_id=1, source_target_pairs={{0,1},{1,0},{2,3},{3,2},{4,5},{5,4},{6,7},{7,6},{8,9},{9,8},{10,11... | collective-permute-start | bytes 393224 | tf_op jit(solution)/shard_map/ppermute | solution.py:206
  16.0 0.2 collective-permute-done.5.arrived
  16.2 1.6 %collective-permute-start.6 = (bf16[4,4096]{1,0:T(4,128)(2,1)S(1)}, bf16[4,4096]{1,0:T(4,128)(2,1)S(1)}, u32[]{:S(2)}, u32[]{:S(2)}) collective-permute-start(bf16[4,4096]{1,0:T(4,128)(2,1)S(1)} %get-tuple-element.28), channel_id=1, source_target_pairs={{0,2},{1,3},{2,0},{3,1},{4,6},{5,7},{6,4},{7,5},{8,10},{9,11},{10,... | collective-permute-start | bytes 98312 | tf_op jit(solution)/shard_map/ppermute | solution.py:211
  17.7 0.5 %collective-permute-start.8 = (bf16[4,4096]{1,0:T(4,128)(2,1)S(1)}, bf16[4,4096]{1,0:T(4,128)(2,1)S(1)}, u32[]{:S(2)}, u32[]{:S(2)}) collective-permute-start(bf16[4,4096]{1,0:T(4,128)(2,1)S(1)} %get-tuple-element.30), channel_id=1, source_target_pairs={{0,2},{1,3},{2,0},{3,1},{4,6},{5,7},{6,4},{7,5},{8,10},{9,11},{10,... | collective-permute-start | bytes 98312 | tf_op jit(solution)/shard_map/ppermute | solution.py:211
  18.3 1.6 %collective-permute-start.10 = (bf16[4,4096]{1,0:T(4,128)(2,1)S(1)}, bf16[4,4096]{1,0:T(4,128)(2,1)S(1)}, u32[]{:S(2)}, u32[]{:S(2)}) collective-permute-start(bf16[4,4096]{1,0:T(4,128)(2,1)S(1)} %get-tuple-element.34), channel_id=1, source_target_pairs={{0,2},{1,3},{2,0},{3,1},{4,6},{5,7},{6,4},{7,5},{8,10},{9,11},{10,... | collective-permute-start | bytes 98312 | tf_op jit(solution)/shard_map/ppermute | solution.py:211
  19.9 0.5 %collective-permute-start.4 = (bf16[4,4096]{1,0:T(4,128)(2,1)S(1)}, bf16[4,4096]{1,0:T(4,128)(2,1)S(1)}, u32[]{:S(2)}, u32[]{:S(2)}) collective-permute-start(bf16[4,4096]{1,0:T(4,128)(2,1)S(1)} %get-tuple-element.24), channel_id=1, source_target_pairs={{0,2},{1,3},{2,0},{3,1},{4,6},{5,7},{6,4},{7,5},{8,10},{9,11},{10,... | collective-permute-start | bytes 98312 | tf_op jit(solution)/shard_map/ppermute | solution.py:230
  20.4 1.2 %collective-permute-start.7 = (bf16[4,4096]{1,0:T(4,128)(2,1)S(1)}, bf16[4,4096]{1,0:T(4,128)(2,1)S(1)}, u32[]{:S(2)}, u32[]{:S(2)}) collective-permute-start(bf16[4,4096]{1,0:T(4,128)(2,1)S(1)} %fold.3), channel_id=1, source_target_pairs={{0,4},{4,8},{8,12},{12,0},{1,5},{5,9},{9,13},{13,1},{2,6},{6,10},{... | collective-permute-start | bytes 98312 | tf_op jit(solution)/shard_map/ppermute | solution.py:234
  21.7 2.3 %collective-permute-start.9 = (bf16[4,4096]{1,0:T(4,128)(2,1)S(1)}, bf16[4,4096]{1,0:T(4,128)(2,1)S(1)}, u32[]{:S(2)}, u32[]{:S(2)}) collective-permute-start(bf16[4,4096]{1,0:T(4,128)(2,1)S(1)} %fold.4), channel_id=1, source_target_pairs={{0,8},{4,12},{8,0},{12,4},{1,9},{5,13},{9,1},{13,5},{2,10},{6,14},... | collective-permute-start | bytes 98312 | tf_op jit(solution)/shard_map/ppermute | solution.py:234
  24.0 1.4 %collective-permute-start.11 = (bf16[4,4096]{1,0:T(4,128)(2,1)S(1)}, bf16[4,4096]{1,0:T(4,128)(2,1)S(1)}, u32[]{:S(2)}, u32[]{:S(2)}) collective-permute-start(bf16[4,4096]{1,0:T(4,128)(2,1)S(1)} %fold.5), channel_id=1, source_target_pairs={{0,12},{4,0},{8,4},{12,8},{1,13},{5,1},{9,5},{13,9},{2,14},{6,2},{... | collective-permute-start | bytes 98312 | tf_op jit(solution)/shard_map/ppermute | solution.py:234
  25.4 0.9 %collective-permute-done.7.refs_2_ = bf16[4,4096]{1,0:T(4,128)(2,1)S(1)} collective-permute-done((bf16[4,4096]{1,0:T(4,128)(2,1)S(1)}, bf16[4,4096]{1,0:T(4,128)(2,1)S(1)}, u32[]{:S(2)}, u32[]{:S(2)}) %collective-permute-start.7) | collective-permute-done | bytes 32800 | tf_op jit(solution)/shard_map/ppermute | solution.py:234
  26.3 0.5 %collective-permute-done.9.refs_3_ = bf16[4,4096]{1,0:T(4,128)(2,1)S(1)} collective-permute-done((bf16[4,4096]{1,0:T(4,128)(2,1)S(1)}, bf16[4,4096]{1,0:T(4,128)(2,1)S(1)}, u32[]{:S(2)}, u32[]{:S(2)}) %collective-permute-start.9) | collective-permute-done | bytes 32800 | tf_op jit(solution)/shard_map/ppermute | solution.py:234
  26.8 0.1 weigh.1
  26.9 1.1 %collective-permute-done.11.piece = bf16[4,4096]{1,0:T(4,128)(2,1)S(1)} collective-permute-done((bf16[4,4096]{1,0:T(4,128)(2,1)S(1)}, bf16[4,4096]{1,0:T(4,128)(2,1)S(1)}, u32[]{:S(2)}, u32[]{:S(2)}) %collective-permute-start.11) | collective-permute-done | bytes 32800 | tf_op jit(solution)/shard_map/ppermute | solution.py:234
  28.0 0.7 %finish.1 = bf16[4,4096]{1,0:T(4,128)(2,1)} custom-call(f32[4,4096]{1,0:T(4,128)S(1)} %get-tuple-element.31.partial, f32[4,128]{1,0:T(4,128)S(1)} %get-tuple-element.32.factor, bf16[4,4096]{1,0:T(4,128)(2,1)S(1)} %collective-permute-done.11.piece), custom_call_target="tpu_custom_call" | custom-call | tf_op jit(solution)/shard_map/finish/pallas_call | solution.py:247
  (21 shorter events, 0.2 us)
Async XLA Ops:
  0.0 10.8 %collective-permute-start.1 = (bf16[16,4096]{1,0:T(8,128)(2,1)}, bf16[16,4096]{1,0:T(8,128)(2,1)S(1)}, u32[]{:S(2)}, u32[]{:S(2)}) collective-permute-start(bf16[16,4096]{1,0:T(8,128)(2,1)} %tokens.1), channel_id=1, source_target_pairs={{0,8},{1,13},{2,10},{3,15},{4,12},{5,9},{6,14},{7,11},{8,0},{9,5},... | collective-permute-start | bytes 393224 | tf_op jit(solution)/shard_map/ppermute | solution.py:162
  4.0 7.6 %collective-permute-start = (bf16[16,4096]{1,0:T(8,128)(2,1)}, bf16[16,4096]{1,0:T(8,128)(2,1)S(1)}, u32[]{:S(2)}, u32[]{:S(2)}) collective-permute-start(bf16[16,4096]{1,0:T(8,128)(2,1)} %tokens.1), channel_id=1, source_target_pairs={{0,4},{4,0},{8,12},{12,8},{1,5},{5,1},{9,13},{13,9},{2,6},{6,2},{1... | collective-permute-start | bytes 393224 | tf_op jit(solution)/shard_map/ppermute | solution.py:163
  6.6 5.6 %copy-start = (bf16[1,384,4096]{2,1,0:T(8,128)(2,1)S(1)}, bf16[1,384,4096]{2,1,0:T(8,128)(2,1)}, u32[]{:S(2)}) copy-start(bf16[1,384,4096]{2,1,0:T(8,128)(2,1)} %w_down.1) | copy-start | bytes 9437188
  6.6 5.6 %copy-start.1 = (bf16[1,384,4096]{2,1,0:T(8,128)(2,1)S(1)}, bf16[1,384,4096]{2,1,0:T(8,128)(2,1)}, u32[]{:S(2)}) copy-start(bf16[1,384,4096]{2,1,0:T(8,128)(2,1)} %refs_2_.1) | copy-start | bytes 9437188
  6.6 5.6 %copy-start.2 = (bf16[1,384,4096]{2,1,0:T(8,128)(2,1)S(1)}, bf16[1,384,4096]{2,1,0:T(8,128)(2,1)}, u32[]{:S(2)}) copy-start(bf16[1,384,4096]{2,1,0:T(8,128)(2,1)} %refs_3_.1) | copy-start | bytes 9437188
  10.8 1.3 %collective-permute-start.2 = (bf16[16,4096]{1,0:T(8,128)(2,1)S(1)}, bf16[16,4096]{1,0:T(8,128)(2,1)S(1)}, u32[]{:S(2)}, u32[]{:S(2)}) collective-permute-start(bf16[16,4096]{1,0:T(8,128)(2,1)S(1)} %collective-permute-done.1.refs_0_), channel_id=1, source_target_pairs={{0,1},{1,0},{2,3},{3,2},{4,5},{5,4},{6,7},{7,6},{8,9},{9,8},{10,11... | collective-permute-start | bytes 393224 | tf_op jit(solution)/shard_map/ppermute | solution.py:164
  14.7 12.1 %copy-start.3 = (s32[16,2]{0,1:T(2,128)S(1)}, s32[16,2]{0,1:T(2,128)}, u32[]{:S(2)}) copy-start(s32[16,2]{0,1:T(2,128)} %param.7) | copy-start | bytes 388
  14.7 12.1 %copy-start.4 = (f32[4,2]{0,1:T(2,128)S(1)}, f32[4,2]{0,1:T(2,128)}, u32[]{:S(2)}) copy-start(f32[4,2]{0,1:T(2,128)} %param.8) | copy-start | bytes 100
  14.7 1.4 %collective-permute-start.5 = (bf16[16,4096]{1,0:T(8,128)(2,1)S(1)}, bf16[16,4096]{1,0:T(8,128)(2,1)S(1)}, u32[]{:S(2)}, u32[]{:S(2)}) collective-permute-start(bf16[16,4096]{1,0:T(8,128)(2,1)S(1)} %get-tuple-element.26), channel_id=1, source_target_pairs={{0,1},{1,0},{2,3},{3,2},{4,5},{5,4},{6,7},{7,6},{8,9},{9,8},{10,11... | collective-permute-start | bytes 393224 | tf_op jit(solution)/shard_map/ppermute | solution.py:206
  15.6 2.7 %collective-permute-start.3 = (bf16[16,4096]{1,0:T(8,128)(2,1)S(1)}, bf16[16,4096]{1,0:T(8,128)(2,1)S(1)}, u32[]{:S(2)}, u32[]{:S(2)}) collective-permute-start(bf16[16,4096]{1,0:T(8,128)(2,1)S(1)} %get-tuple-element.22), channel_id=1, source_target_pairs={{0,1},{1,0},{2,3},{3,2},{4,5},{5,4},{6,7},{7,6},{8,9},{9,8},{10,11... | collective-permute-start | bytes 393224 | tf_op jit(solution)/shard_map/ppermute | solution.py:206
  16.2 4.2 %collective-permute-start.6 = (bf16[4,4096]{1,0:T(4,128)(2,1)S(1)}, bf16[4,4096]{1,0:T(4,128)(2,1)S(1)}, u32[]{:S(2)}, u32[]{:S(2)}) collective-permute-start(bf16[4,4096]{1,0:T(4,128)(2,1)S(1)} %get-tuple-element.28), channel_id=1, source_target_pairs={{0,2},{1,3},{2,0},{3,1},{4,6},{5,7},{6,4},{7,5},{8,10},{9,11},{10,... | collective-permute-start | bytes 98312 | tf_op jit(solution)/shard_map/ppermute | solution.py:211
  17.7 3.9 %collective-permute-start.8 = (bf16[4,4096]{1,0:T(4,128)(2,1)S(1)}, bf16[4,4096]{1,0:T(4,128)(2,1)S(1)}, u32[]{:S(2)}, u32[]{:S(2)}) collective-permute-start(bf16[4,4096]{1,0:T(4,128)(2,1)S(1)} %get-tuple-element.30), channel_id=1, source_target_pairs={{0,2},{1,3},{2,0},{3,1},{4,6},{5,7},{6,4},{7,5},{8,10},{9,11},{10,... | collective-permute-start | bytes 98312 | tf_op jit(solution)/shard_map/ppermute | solution.py:211
  18.3 5.7 %collective-permute-start.10 = (bf16[4,4096]{1,0:T(4,128)(2,1)S(1)}, bf16[4,4096]{1,0:T(4,128)(2,1)S(1)}, u32[]{:S(2)}, u32[]{:S(2)}) collective-permute-start(bf16[4,4096]{1,0:T(4,128)(2,1)S(1)} %get-tuple-element.34), channel_id=1, source_target_pairs={{0,2},{1,3},{2,0},{3,1},{4,6},{5,7},{6,4},{7,5},{8,10},{9,11},{10,... | collective-permute-start | bytes 98312 | tf_op jit(solution)/shard_map/ppermute | solution.py:211
  19.9 5.6 %collective-permute-start.4 = (bf16[4,4096]{1,0:T(4,128)(2,1)S(1)}, bf16[4,4096]{1,0:T(4,128)(2,1)S(1)}, u32[]{:S(2)}, u32[]{:S(2)}) collective-permute-start(bf16[4,4096]{1,0:T(4,128)(2,1)S(1)} %get-tuple-element.24), channel_id=1, source_target_pairs={{0,2},{1,3},{2,0},{3,1},{4,6},{5,7},{6,4},{7,5},{8,10},{9,11},{10,... | collective-permute-start | bytes 98312 | tf_op jit(solution)/shard_map/ppermute | solution.py:230
  20.4 5.9 %collective-permute-start.7 = (bf16[4,4096]{1,0:T(4,128)(2,1)S(1)}, bf16[4,4096]{1,0:T(4,128)(2,1)S(1)}, u32[]{:S(2)}, u32[]{:S(2)}) collective-permute-start(bf16[4,4096]{1,0:T(4,128)(2,1)S(1)} %fold.3), channel_id=1, source_target_pairs={{0,4},{4,8},{8,12},{12,0},{1,5},{5,9},{9,13},{13,1},{2,6},{6,10},{... | collective-permute-start | bytes 98312 | tf_op jit(solution)/shard_map/ppermute | solution.py:234
  21.7 5.1 %collective-permute-start.9 = (bf16[4,4096]{1,0:T(4,128)(2,1)S(1)}, bf16[4,4096]{1,0:T(4,128)(2,1)S(1)}, u32[]{:S(2)}, u32[]{:S(2)}) collective-permute-start(bf16[4,4096]{1,0:T(4,128)(2,1)S(1)} %fold.4), channel_id=1, source_target_pairs={{0,8},{4,12},{8,0},{12,4},{1,9},{5,13},{9,1},{13,5},{2,10},{6,14},... | collective-permute-start | bytes 98312 | tf_op jit(solution)/shard_map/ppermute | solution.py:234
  24.0 4.0 %collective-permute-start.11 = (bf16[4,4096]{1,0:T(4,128)(2,1)S(1)}, bf16[4,4096]{1,0:T(4,128)(2,1)S(1)}, u32[]{:S(2)}, u32[]{:S(2)}) collective-permute-start(bf16[4,4096]{1,0:T(4,128)(2,1)S(1)} %fold.5), channel_id=1, source_target_pairs={{0,12},{4,0},{8,4},{12,8},{1,13},{5,1},{9,5},{13,9},{2,14},{6,2},{... | collective-permute-start | bytes 98312 | tf_op jit(solution)/shard_map/ppermute | solution.py:234
